TPU v7x, 32 devices: a whole 2x2x4 slice. The times are simulated.
32 devices in a mesh: band: 16 (over z, y, core), head: 2 (over x).
Axes of the slice: x: 2, y: 2, z: 4, core: 2. Of those that a mesh axis runs over, the one named last changes fastest.
Arguments:
- block_input: bfloat16 [4096, 1024], P('band'), may hold values from -6 to 6
- out_grad: bfloat16 [4096, 1024], P('band'), may hold values from -6 to 6
- segments: int32 [4096], P('band'), may hold values from 0 to 31, as said below
- lead_steps: int32 [32], replicated, may hold values from 1 to 12
- gain_attn: float32 [1024], replicated, may hold values from 0.1 to 1.9
- shift_attn: float32 [1024], replicated, may hold values from -3 to 3
- lead_weight: float32 [1024], replicated, may hold values from -4 to 4
- query_weight: bfloat16 [1024, 1024], P(None, 'head'), may hold values from -0.1875 to 0.1875
- key_weight: bfloat16 [1024, 1024], P(None, 'head'), may hold values from -0.1875 to 0.1875
- value_weight: bfloat16 [1024, 1024], P(None, 'head'), may hold values from -0.1875 to 0.1875
- output_weight: bfloat16 [1024, 1024], P('head'), may hold values from -0.75 to 0.75
- output_bias: float32 [1024], replicated, may hold values from -3 to 3
- gain_mlp: float32 [1024], replicated, may hold values from 0.1 to 1.9
- shift_mlp: float32 [1024], replicated, may hold values from -3 to 3
- up_weight: bfloat16 [1024, 4096], P(None, 'head'), may hold values from -0.1875 to 0.1875
- up_bias: float32 [4096], P('head'), may hold values from -3 to 3
- down_weight: bfloat16 [4096, 1024], P('head'), may hold values from -0.09375 to 0.09375
- down_bias: float32 [1024], replicated, may hold values from -3 to 3
Outputs:
- block_output: bfloat16 [4096, 1024], P('band')
- input_grad: bfloat16 [4096, 1024], P('band')
- dgain_attn: float32 [1024], replicated
- dshift_attn: float32 [1024], replicated
- dlead_weight: float32 [1024], replicated
- dquery_weight: float32 [1024, 1024], P(None, 'head')
- dkey_weight: float32 [1024, 1024], P(None, 'head')
- dvalue_weight: float32 [1024, 1024], P(None, 'head')
- doutput_weight: float32 [1024, 1024], P('head')
- doutput_bias: float32 [1024], replicated
- dgain_mlp: float32 [1024], replicated
- dshift_mlp: float32 [1024], replicated
- dup_weight: float32 [1024, 4096], P(None, 'head')
- dup_bias: float32 [4096], P('head')
- ddown_weight: float32 [4096, 1024], P('head')
- ddown_bias: float32 [1024], replicated
Inputs may be any that keep to these rules, and one draw needn't show every extreme that they name: `segments`: the patches of one crop lie in a run of consecutive latitude bands of 256 patches each; at least one crop covers every band; every crop number occurs.
All inputs are finite; a program needn't handle non-finite values.
Results may differ from a plain program's by a relative error of at most 0.025.
Values may be sent and summed in bfloat16 or wider, within the bound.
No kernel may reach another device: no remote copies, remote signals or barrier semaphores. Data moves between devices by JAX's collectives and lax.ppermute only.
A program may use at most 128 MiB of HBM per device.

v0:
```python
from functools import partial
import math

import jax
import jax.numpy as jnp
from jax import lax
from jax.sharding import PartitionSpec as P

HD = 64


eps = 1e-05
masked_value = -1e30
highest = lax.Precision.HIGHEST


def normalize(values):
    centred = values - jnp.mean(values, axis=-1, keepdims=True)
    inverse = lax.rsqrt(jnp.mean(centred * centred, axis=-1, keepdims=True) + eps)
    return (centred * inverse, inverse)


def normalize_back(grad_unit, unit, inverse):
    return inverse * (
        grad_unit
        - jnp.mean(grad_unit, axis=-1, keepdims=True)
        - unit * jnp.mean(grad_unit * unit, axis=-1, keepdims=True)
    )


def left_product(first, second):
    return lax.dot_general(
        first, second, (((0,), (0,)), ((), ())), preferred_element_type=jnp.float32
    )


def right_product(first, second):
    return lax.dot_general(
        first, second, (((1,), (1,)), ((), ())), preferred_element_type=jnp.float32
    )


def exact_gelu(values):
    return jax.nn.gelu(values, approximate=False)


def split_blocks(arrays, count):
    stride = math.gcd(count, 1024)
    return (
        stride,
        tuple((array.reshape((count // stride, stride) + array.shape[1:]) for array in arrays)),
    )


def forward_fold(query3, seg_query, carry, piece):
    keys, values, seg_keys = piece
    count = keys.shape[0]
    heads = query3.shape[1]
    stride, blocks = split_blocks((keys, values, seg_keys), count)

    def forward_step(state, block):
        top, total, accum = state
        key_block, value_block, seg_block = block
        key3 = key_block.reshape(stride, heads, HD)
        value3 = value_block.reshape(stride, heads, HD)
        scores = (
            jnp.einsum("qhd,khd->qhk", query3, key3, preferred_element_type=jnp.float32) * 0.125
        )
        allowed = (seg_query[:, None] == seg_block.astype(jnp.float32)[None, :])[:, None, :]
        masked = jnp.where(allowed, scores, masked_value)
        new_top = jnp.maximum(top, jnp.max(masked, axis=-1))
        weights = jnp.where(allowed, jnp.exp(masked - new_top[..., None]), 0.0)
        factor = jnp.exp(top - new_top)
        total = total * factor + jnp.sum(weights, axis=-1)
        accum = accum * factor[..., None] + jnp.einsum(
            "qhk,khd->qhd", weights.astype(jnp.bfloat16), value3, preferred_element_type=jnp.float32
        )
        return ((new_top, total, accum), None)

    return lax.scan(forward_step, carry, blocks)[0]


def backward_fold(query3, grad3, seg_query, logsum, delta, with_keys, carry, piece, start):
    keys, values, seg_keys = piece
    count = keys.shape[0]
    heads = query3.shape[1]
    stride, blocks = split_blocks((keys, values, seg_keys), count)
    offsets = jnp.arange(count // stride, dtype=jnp.int32) * stride

    def backward_step(state, block):
        key_block, value_block, seg_block, offset = block
        key3 = key_block.reshape(stride, heads, HD)
        value3 = value_block.reshape(stride, heads, HD)
        scores = (
            jnp.einsum("qhd,khd->qhk", query3, key3, preferred_element_type=jnp.float32) * 0.125
        )
        allowed = (seg_query[:, None] == seg_block.astype(jnp.float32)[None, :])[:, None, :]
        probs = jnp.where(allowed, jnp.exp(scores - logsum[..., None]), 0.0)
        dprobs = jnp.einsum("qhd,khd->qhk", grad3, value3, preferred_element_type=jnp.float32)
        dscores = (probs * (dprobs - delta[..., None])).astype(jnp.bfloat16)
        dquery = (
            state[0]
            + jnp.einsum("qhk,khd->qhd", dscores, key3, preferred_element_type=jnp.float32) * 0.125
        )
        dkey = (
            jnp.einsum("qhk,qhd->khd", dscores, query3, preferred_element_type=jnp.float32) * 0.125
        )
        dvalue = jnp.einsum(
            "qhk,qhd->khd", probs.astype(jnp.bfloat16), grad3, preferred_element_type=jnp.float32
        )
        block_rows = jnp.concatenate(
            [dkey.reshape(stride, heads * HD), dvalue.reshape(stride, heads * HD)], axis=1
        )
        buffer = lax.dynamic_update_slice(state[1], block_rows, (offset, 0))
        return ((dquery, buffer), None)

    return lax.scan(backward_step, carry, blocks + (offsets,))[0]


def local(
    block_input,
    out_grad,
    segments,
    lead_steps,
    gain_attn,
    shift_attn,
    lead_weight,
    query_weight,
    key_weight,
    value_weight,
    output_weight,
    output_bias,
    gain_mlp,
    shift_mlp,
    up_weight,
    up_bias,
    down_weight,
    down_bias,
):
    rows = block_input.shape[0]
    heads = query_weight.shape[1] // HD
    width_local = heads * HD
    total_rows = rows * lax.axis_size("band")
    inputs = block_input.astype(jnp.float32)
    unit_attn, inverse_attn = normalize(inputs)
    crops = lead_steps.shape[0]
    onehot = (segments[:, None] == jnp.arange(crops, dtype=jnp.int32)[None, :]).astype(jnp.float32)
    lead = jnp.dot(onehot, lead_steps.astype(jnp.float32), precision=highest) / 12.0
    attn_in = (unit_attn * gain_attn + shift_attn + lead[:, None] * lead_weight).astype(
        jnp.bfloat16
    )
    query = jnp.dot(attn_in, query_weight, preferred_element_type=jnp.float32).astype(jnp.bfloat16)
    key_low = jnp.dot(attn_in, key_weight, preferred_element_type=jnp.float32).astype(jnp.bfloat16)
    value_low = jnp.dot(attn_in, value_weight, preferred_element_type=jnp.float32).astype(
        jnp.bfloat16
    )
    seg_low = segments.astype(jnp.bfloat16)
    seg_query = segments.astype(jnp.float32)
    query3 = query.reshape(rows, heads, HD)
    start_state = (
        jnp.full((rows, heads), masked_value, jnp.float32),
        jnp.zeros((rows, heads), jnp.float32),
        jnp.zeros((rows, heads, HD), jnp.float32),
    )
    top, total, accum = forward_fold(
        query3,
        seg_query,
        start_state,
        (
            lax.all_gather(key_low, "band", axis=0, tiled=True),
            lax.all_gather(value_low, "band", axis=0, tiled=True),
            lax.all_gather(seg_low, "band", axis=0, tiled=True),
        ),
    )
    logsum = top + jnp.log(total)
    attn_raw = accum / total[..., None]
    attn_out = attn_raw.reshape(rows, width_local).astype(jnp.bfloat16)
    branch = lax.psum(
        jnp.dot(attn_out, output_weight, preferred_element_type=jnp.float32).astype(jnp.bfloat16),
        "head",
    ).astype(jnp.float32)
    hidden = inputs + branch + output_bias
    unit_mlp, inverse_mlp = normalize(hidden)
    mlp_in = (unit_mlp * gain_mlp + shift_mlp).astype(jnp.bfloat16)
    upper = jnp.dot(mlp_in, up_weight, preferred_element_type=jnp.float32) + up_bias
    active, gelu_back = jax.vjp(exact_gelu, upper)
    active_low = active.astype(jnp.bfloat16)
    mlp_out = lax.psum(
        jnp.dot(active_low, down_weight, preferred_element_type=jnp.float32).astype(jnp.bfloat16),
        "head",
    ).astype(jnp.float32)
    block_output = (hidden + mlp_out + down_bias).astype(jnp.bfloat16)
    grad_out = out_grad.astype(jnp.float32)
    ddown_bias = jnp.sum(grad_out, axis=0)
    ddown_weight = left_product(active_low, out_grad)
    d_active = right_product(out_grad, down_weight)
    d_upper = gelu_back(d_active)[0].astype(jnp.bfloat16)
    dup_bias = jnp.sum(d_upper.astype(jnp.float32), axis=0)
    dup_weight = left_product(mlp_in, d_upper)
    d_mlp = lax.psum(right_product(d_upper, up_weight).astype(jnp.bfloat16), "head").astype(
        jnp.float32
    )
    dgain_mlp = jnp.sum(d_mlp * unit_mlp, axis=0)
    dshift_mlp = jnp.sum(d_mlp, axis=0)
    d_hidden = grad_out + normalize_back(d_mlp * gain_mlp, unit_mlp, inverse_mlp)
    doutput_bias = jnp.sum(d_hidden, axis=0)
    d_branch = d_hidden.astype(jnp.bfloat16)
    doutput_weight = left_product(attn_out, d_branch)
    d_attn = right_product(d_branch, output_weight).astype(jnp.bfloat16)
    grad3 = d_attn.reshape(rows, heads, HD)
    delta = jnp.sum(grad3.astype(jnp.float32) * attn_raw, axis=-1)
    dquery_zero = jnp.zeros((rows, heads, HD), jnp.float32)
    back_start = (dquery_zero, jnp.zeros((total_rows, 2 * width_local), jnp.float32))
    back_step = partial(backward_fold, query3, grad3, seg_query, logsum, delta, True)
    folded = back_step(
        back_start,
        (
            lax.all_gather(key_low, "band", axis=0, tiled=True),
            lax.all_gather(value_low, "band", axis=0, tiled=True),
            lax.all_gather(seg_low, "band", axis=0, tiled=True),
        ),
        jnp.int32(0),
    )
    key_value_grad = lax.psum_scatter(
        folded[1].astype(jnp.bfloat16), "band", scatter_dimension=0, tiled=True
    ).astype(jnp.float32)
    dquery_low = folded[0].reshape(rows, width_local).astype(jnp.bfloat16)
    dkey_low = key_value_grad[:, :width_local].astype(jnp.bfloat16)
    dvalue_low = key_value_grad[:, width_local:].astype(jnp.bfloat16)
    dquery_weight = left_product(attn_in, dquery_low)
    dkey_weight = left_product(attn_in, dkey_low)
    dvalue_weight = left_product(attn_in, dvalue_low)
    d_part = (
        right_product(dquery_low, query_weight)
        + right_product(dkey_low, key_weight)
        + right_product(dvalue_low, value_weight)
    )
    d_in = lax.psum(d_part.astype(jnp.bfloat16), "head").astype(jnp.float32)
    dlead_weight = jnp.sum(lead[:, None] * d_in, axis=0)
    dgain_attn = jnp.sum(d_in * unit_attn, axis=0)
    dshift_attn = jnp.sum(d_in, axis=0)
    input_grad = (d_hidden + normalize_back(d_in * gain_attn, unit_attn, inverse_attn)).astype(
        jnp.bfloat16
    )
    summed = (
        lax.psum(dgain_attn.astype(jnp.bfloat16), "band").astype(jnp.float32),
        lax.psum(dshift_attn.astype(jnp.bfloat16), "band").astype(jnp.float32),
        lax.psum(dlead_weight.astype(jnp.bfloat16), "band").astype(jnp.float32),
        lax.psum(dquery_weight.astype(jnp.bfloat16), "band").astype(jnp.float32),
        lax.psum(dkey_weight.astype(jnp.bfloat16), "band").astype(jnp.float32),
        lax.psum(dvalue_weight.astype(jnp.bfloat16), "band").astype(jnp.float32),
        lax.psum(doutput_weight.astype(jnp.bfloat16), "band").astype(jnp.float32),
        lax.psum(doutput_bias.astype(jnp.bfloat16), "band").astype(jnp.float32),
        lax.psum(dgain_mlp.astype(jnp.bfloat16), "band").astype(jnp.float32),
        lax.psum(dshift_mlp.astype(jnp.bfloat16), "band").astype(jnp.float32),
        lax.psum(dup_weight.astype(jnp.bfloat16), "band").astype(jnp.float32),
        lax.psum(dup_bias.astype(jnp.bfloat16), "band").astype(jnp.float32),
        lax.psum(ddown_weight.astype(jnp.bfloat16), "band").astype(jnp.float32),
        lax.psum(ddown_bias.astype(jnp.bfloat16), "band").astype(jnp.float32),
    )
    return (block_output, input_grad) + tuple(summed)


def solution(mesh):
    placed = (
        P("band", None),
        P("band", None),
        P("band"),
        P(),
        P(),
        P(),
        P(),
        P(None, "head"),
        P(None, "head"),
        P(None, "head"),
        P("head", None),
        P(),
        P(),
        P(),
        P(None, "head"),
        P("head"),
        P("head", None),
        P(),
    )
    return jax.shard_map(
        local,
        mesh=mesh,
        in_specs=placed,
        out_specs=(
            P("band", None),
            P("band", None),
            P(),
            P(),
            P(),
            P(None, "head"),
            P(None, "head"),
            P(None, "head"),
            P("head", None),
            P(),
            P(),
            P(),
            P(None, "head"),
            P("head"),
            P("head", None),
            P(),
        ),
        check_vma=False,
    )
```

profile of v0, /device:TPU:0, one launch (start us, length us, event | category | flops | bytes accessed | tf_op | source)
XLA Modules:
  0.0 849.6 jit_solution(3842084930848138585)
XLA Ops:
  13.6 2.4 convolution_convert_fusion.10
  16.1 23.1 %all-gather = bf16[16,1,256]{2,1,0:T(2,128)(2,1)S(1)} all-gather(bf16[1,1,256]{2,1,0:T(2,128)(2,1)S(1)} %reshape.188), channel_id=1, replica_groups=mesh['band'=16,'head'=2] {'band'}, dimensions={0}, use_global_device_ids=true | all-gather | bytes 8704 | tf_op jit(solution)/shard_map/all_gather | solution.py:172
  39.9 27.1 %all-gather.4.cloned.1.call-done = bf16[4096,512]{1,0:T(8,128)(2,1)} async-done(((bf16[256,512]{1,0:T(8,128)(2,1)}), bf16[4096,512]{1,0:T(8,128)(2,1)}) %all-gather.4.cloned.1.call-update) | async-done | bytes 4194320 | tf_op jit(solution)/shard_map/all_gather | solution.py:170
  67.0 6.3 copy.71
  73.3 45.5 %all-gather.6.cloned.1.call-done = bf16[4096,512]{1,0:T(8,128)(2,1)} async-done(((bf16[256,512]{1,0:T(8,128)(2,1)}), bf16[4096,512]{1,0:T(8,128)(2,1)}) %all-gather.6.cloned.1.call-update) | async-done | bytes 4194320 | tf_op jit(solution)/shard_map/all_gather | solution.py:171
  118.8 6.3 copy.72
  125.1 59.5 %while.28 = (s32[]{:T(128)}, f32[256,8]{0,1:T(8,128)S(1)}, f32[256,8]{0,1:T(8,128)S(1)}, f32[256,8,64]{0,2,1:T(8,128)S(1)}, f32[256]{0:T(256)S(1)}, /*index=5*/b...) while((s32[]{:T(128)}, f32[256,8]{0,1:T(8,128)S(1)}, ...), condition=%wide.region_5.6_spmd.clone, body=%wide.region_2.5_spmd.clone.sunk | while | flops 564800512 | bytes 67513512 | solution.py:80
  125.4 1.7 constant_dynamic-slice_fusion.6
  127.1 4.9 fusion.147
  132.0 4.6 fusion.148
  137.8 2.1 fusion.150
  140.2 1.7 constant_dynamic-slice_fusion.6
  142.0 4.9 fusion.147
  146.9 4.6 fusion.148
  152.7 2.1 fusion.150
  155.1 1.7 constant_dynamic-slice_fusion.6
  156.8 4.9 fusion.147
  161.8 4.6 fusion.148
  167.6 2.1 fusion.150
  170.0 1.7 constant_dynamic-slice_fusion.6
  171.7 4.9 fusion.147
  176.7 4.6 fusion.148
  182.5 2.1 fusion.150
  187.0 27.0 %all-reduce.8.cloned.1.call-done = bf16[256,1024]{1,0:T(8,128)(2,1)} async-done(((bf16[256,1024]{1,0:T(8,128)(2,1)}), bf16[256,1024]{1,0:T(8,128)(2,1)}) %all-reduce.8.cloned.1.call-update) | async-done | bytes 524304 | tf_op jit(solution)/shard_map/psum | solution.py:178
  216.8 3.7 convolution_add_fusion
  220.6 7.1 fusion.74
  228.7 2.1 convolution_convert_fusion.7
  230.9 28.7 %all-reduce.10.cloned.1.call-done = bf16[256,1024]{1,0:T(8,128)(2,1)} async-done(((bf16[256,1024]{1,0:T(8,128)(2,1)}), bf16[256,1024]{1,0:T(8,128)(2,1)}) %all-reduce.10.cloned.1.call-update) | async-done | bytes 524304 | tf_op jit(solution)/shard_map/psum | solution.py:200
  266.2 4.4 broadcast_in_dim.39
  270.7 161.8 %while.29 = (s32[]{:T(128)}, f32[256,8,64]{0,2,1:T(8,128)}, bf16[4096,1024]{0,1:T(8,128)(2,1)}, bf16[4,1024,512]{1,2,0:T(8,128)(2,1)}, f32[256]{0:T(256)S(1)}, /...) while((s32[]{:T(128)}, f32[256,8,64]{0,2,1:T(8,128)}, ...), condition=%wide.region_15.16_spmd.clone, body=%wide.region_14.15_spmd.clone.sunk | while | flops 1369048064 | bytes 108825856 | solution.py:117
  270.7 1.7 constant_dynamic-slice_fusion.7
  274.0 5.4 fusion.162
  279.4 3.8 fusion.163
  283.2 5.3 fusion.164
  292.6 18.8 %dynamic_update_slice.5 = bf16[4096,1024]{0,1:T(8,128)(2,1)} dynamic-update-slice(bf16[4096,1024]{0,1:T(8,128)(2,1)} %get-tuple-element.564, bf16[1024,1024]{0,1:T(8,128)(2,1)S(1)} %pad_maximum_fusion.2, s32[]{:T(128)S(6)} %select_n.62, s32[]{:T(128)} %constant.27.clone.1..sunk.1) | dynamic-update-slice | bytes 4194308 | tf_op jit(solution)/shard_map/while/body/eval_jaxpr/dynamic_update_slice | solution.py:114
  311.4 1.7 constant_dynamic-slice_fusion.7
  314.6 5.4 fusion.162
  320.0 3.9 fusion.163
  324.0 5.3 fusion.164
  333.4 18.8 %dynamic_update_slice.5 = bf16[4096,1024]{0,1:T(8,128)(2,1)} dynamic-update-slice(bf16[4096,1024]{0,1:T(8,128)(2,1)} %get-tuple-element.564, bf16[1024,1024]{0,1:T(8,128)(2,1)S(1)} %pad_maximum_fusion.2, s32[]{:T(128)S(6)} %select_n.62, s32[]{:T(128)} %constant.27.clone.1..sunk.1) | dynamic-update-slice | bytes 4194308 | tf_op jit(solution)/shard_map/while/body/eval_jaxpr/dynamic_update_slice | solution.py:114
  352.1 1.7 constant_dynamic-slice_fusion.7
  355.4 5.4 fusion.162
  360.8 3.9 fusion.163
  364.7 5.3 fusion.164
  374.1 18.8 %dynamic_update_slice.5 = bf16[4096,1024]{0,1:T(8,128)(2,1)} dynamic-update-slice(bf16[4096,1024]{0,1:T(8,128)(2,1)} %get-tuple-element.564, bf16[1024,1024]{0,1:T(8,128)(2,1)S(1)} %pad_maximum_fusion.2, s32[]{:T(128)S(6)} %select_n.62, s32[]{:T(128)} %constant.27.clone.1..sunk.1) | dynamic-update-slice | bytes 4194308 | tf_op jit(solution)/shard_map/while/body/eval_jaxpr/dynamic_update_slice | solution.py:114
  392.9 1.7 constant_dynamic-slice_fusion.7
  396.2 5.4 fusion.162
  401.6 3.9 fusion.163
  405.5 5.3 fusion.164
  414.9 17.6 %dynamic_update_slice.5 = bf16[4096,1024]{0,1:T(8,128)(2,1)} dynamic-update-slice(bf16[4096,1024]{0,1:T(8,128)(2,1)} %get-tuple-element.564, bf16[1024,1024]{0,1:T(8,128)(2,1)S(1)} %pad_maximum_fusion.2, s32[]{:T(128)S(6)} %select_n.62, s32[]{:T(128)} %constant.27.clone.1..sunk.1) | dynamic-update-slice | bytes 4194308 | tf_op jit(solution)/shard_map/while/body/eval_jaxpr/dynamic_update_slice | solution.py:114
  432.8 2.6 multiply_convert_fusion
  435.5 3.3 convolution_convert_fusion
  438.8 3.4 convolution_convert_fusion.1
  442.2 2.1 convolution_convert_fusion.8
  446.9 90.7 %reduce-scatter.2.cloned.1.call-done = bf16[256,1024]{0,1:T(8,128)(2,1)} async-done(((bf16[4096,1024]{0,1:T(8,128)(2,1)}), bf16[256,1024]{0,1:T(8,128)(2,1)}) %reduce-scatter.2.cloned.1.call-update) | async-done | bytes 524304 | tf_op jit(solution)/shard_map/reduce_scatter | solution.py:224
  537.5 2.2 convolution_add_fusion.2
  541.1 2.5 convolution_convert_fusion.5
  549.1 32.1 %all-reduce.14.cloned.1.call-done = (bf16[256,1024]{1,0:T(8,128)(2,1)}, bf16[256,1024]{1,0:T(8,128)(2,1)}) async-done(((bf16[256,1024]{1,0:T(8,128)(2,1)}, bf16[256,1024]{1,0:T(8,128)(2,1)}), (bf16[256,1024]{1,0:T(8,128)(2,1)}, bf16[256,1024]{1,0:T(8,128)(2,1)})) %all-reduce.14.cloned.1.call-update) | async-done | bytes 1048592 | tf_op jit(solution)/shard_map/psum | solution.py:188
  584.0 64.3 %all-reduce = (bf16[1024]{0:T(1024)(128)(2,1)S(1)}, bf16[1024]{0:T(1024)(128)(2,1)S(1)}, bf16[1024]{0:T(1024)(128)(2,1)S(1)}, bf16[1024]{0:T(1024)(128)(2,1)S(1)...) all-reduce(bf16[1024]{0:T(1024)(128)(2,1)S(1)} %get-tuple-element.2, ...), channel_id=1, replica_groups=mesh['band'=16,'head'=2] {'band'}, use_global_device_ids=true, to_apply=%region_21.22 | all-reduce | flops 9216 | bytes 36864 | tf_op jit(solution)/shard_map/psum | solution.py:246
  653.1 2.7 fusion.51
  655.8 169.5 %all-reduce.12.cloned.1.call-done = (bf16[1024,512]{1,0:T(8,128)(2,1)}, bf16[1024,512]{1,0:T(8,128)(2,1)}, bf16[1024,512]{1,0:T(8,128)(2,1)}, bf16[512,1024]{1,0...) async-done(((bf16[1024,512]{1,0:T(8,128)(2,1)}, bf16[1024,512]{1,0:T(8,128)(2,1)}, bf16[1024,512]{1,0:T(8,128)(2,1)}, bf16[512,1024]{1,0:T(8,128)(2,1)}, ...) | async-done | bytes 12582928 | tf_op jit(solution)/shard_map/psum | solution.py:249
  825.3 2.9 convert_element_type.220
  833.8 4.4 convert_element_type.233
  838.3 4.4 convert_element_type.236
  (229 shorter events, 63.1 us)
Async XLA Ops:
  7.2 178.3 %copy-start = (bf16[512,1024]{1,0:T(8,128)(2,1)S(1)}, bf16[512,1024]{1,0:T(8,128)(2,1)}, u32[]{:S(2)}) copy-start(bf16[512,1024]{1,0:T(8,128)(2,1)} %param.32) | copy-start | bytes 3145732
  7.2 59.8 %all-gather.4.cloned.1.call-start = ((), (), s32[]{:S(2)}) async-start(), calls=%async_computation.1 | async-start | bytes 4456448 | tf_op jit(solution)/shard_map/all_gather | solution.py:170
  7.2 5.1 copy-start.20
  8.6 2.3 copy-start.37
  10.9 1.4 copy-start.39
  10.9 1.4 copy-start.41
  12.3 26.9 %copy-start.7 = (bf16[256,1024]{1,0:T(8,128)(2,1)}, bf16[256,1024]{1,0:T(8,128)(2,1)S(1)}, u32[]{:S(2)}) copy-start(bf16[256,1024]{1,0:T(8,128)(2,1)S(1)} %fusion.47) | copy-start | bytes 1572868
  12.4 3.7 copy-start.44
  12.4 26.9 %copy-start.18 = (bf16[1024,512]{1,0:T(8,128)(2,1)S(1)}, bf16[1024,512]{1,0:T(8,128)(2,1)}, u32[]{:S(2)}) copy-start(bf16[1024,512]{1,0:T(8,128)(2,1)} %param.29) | copy-start | bytes 3145732
  13.5 105.3 %all-gather.6.cloned.1.call-start = ((), (), s32[]{:S(2)}) async-start(), calls=%async_computation.2 | async-start | bytes 4456448 | tf_op jit(solution)/shard_map/all_gather | solution.py:171
  16.0 198.0 %all-reduce.8.cloned.1.call-start = ((), (), s32[]{:S(2)}) async-start(), calls=%async_computation.3 | async-start | bytes 1048576 | tf_op jit(solution)/shard_map/psum | solution.py:178
  132.0 5.8 copy-start.2
  146.9 5.8 copy-start.2
  161.8 5.8 copy-start.2
  176.7 5.8 copy-start.2
  184.7 29.3 %copy-start.5 = (bf16[256,1024]{1,0:T(8,128)(2,1)S(1)}, bf16[256,1024]{1,0:T(8,128)(2,1)}, u32[]{:S(2)}) copy-start(bf16[256,1024]{1,0:T(8,128)(2,1)} %param.22) | copy-start | bytes 1572868
  184.7 29.3 %copy-start.33 = (f32[1024]{0:T(1024)S(1)}, f32[1024]{0:T(1024)}, u32[]{:S(2)}) copy-start(f32[1024]{0:T(1024)} %param.33) | copy-start | bytes 12292
  185.4 31.3 %copy-start.34 = (f32[1024]{0:T(1024)S(1)}, f32[1024]{0:T(1024)}, u32[]{:S(2)}) copy-start(f32[1024]{0:T(1024)} %param.34) | copy-start | bytes 12292
  185.4 31.3 %copy-start.35 = (f32[1024]{0:T(1024)S(1)}, f32[1024]{0:T(1024)}, u32[]{:S(2)}) copy-start(f32[1024]{0:T(1024)} %param.35) | copy-start | bytes 12292
  185.4 31.3 %copy-start.48 = (f32[2048]{0:T(1024)S(1)}, f32[2048]{0:T(1024)}, u32[]{:S(2)}) copy-start(f32[2048]{0:T(1024)} %param.37) | copy-start | bytes 24580
  186.7 72.8 %all-reduce.10.cloned.1.call-start = ((), (), s32[]{:S(2)}) async-start(), calls=%async_computation.4 | async-start | bytes 1048576 | tf_op jit(solution)/shard_map/psum | solution.py:200
  214.0 2.8 copy-start.9
  216.8 3.8 copy-start.13
  216.8 3.8 copy-start.46
  220.6 7.2 copy-start.25
  220.6 8.1 copy-start.45
  227.7 1.0 copy-start.31
  230.8 306.7 %reduce-scatter.2.cloned.1.call-start = ((), (), s32[]{:S(2)}) async-start(), calls=%async_computation.5 | async-start | bytes 8912896 | tf_op jit(solution)/shard_map/reduce_scatter | solution.py:224
  262.9 1.0 copy-start.11
  273.7 5.7 copy-start.4
  283.2 5.3 copy-start.3
  314.4 5.7 copy-start.4
  324.0 5.3 copy-start.3
  355.2 5.7 copy-start.4
  364.7 5.3 copy-start.3
  395.9 5.7 copy-start.4
  405.5 5.3 copy-start.3
  432.5 148.7 %all-reduce.14.cloned.1.call-start = ((), (), s32[]{:S(2)}) async-start(), calls=%async_computation.7 | async-start | bytes 2097152 | tf_op jit(solution)/shard_map/psum | solution.py:188
  432.8 2.7 copy-start.14
  435.4 3.3 copy-start.6
  435.5 3.3 copy-start.10
  435.5 3.3 copy-start.32
  438.7 3.5 copy-start.47
  442.2 3.2 copy-start.19
  445.4 92.1 %copy-start.24 = (bf16[256,8,64]{0,2,1:T(8,128)(2,1)}, bf16[256,8,64]{0,2,1:T(8,128)(2,1)S(1)}, u32[]{:S(2)}) copy-start(bf16[256,8,64]{0,2,1:T(8,128)(2,1)S(1)} %convert_element_type.208) | copy-start | bytes 786436
  446.9 92.8 %copy-start.21 = (bf16[1024,512]{1,0:T(8,128)(2,1)S(1)}, bf16[1024,512]{1,0:T(8,128)(2,1)}, u32[]{:S(2)}) copy-start(bf16[1024,512]{1,0:T(8,128)(2,1)} %param.31) | copy-start | bytes 3145732
  537.5 2.2 copy-start.26
  539.7 1.4 copy-start.8
  541.0 2.6 copy-start.12
  541.0 2.6 copy-start.23
  541.0 284.2 %all-reduce.12.cloned.1.call-start = ((), (), s32[]{:S(2)}) async-start(), calls=%async_computation.6 | async-start | bytes 25165824 | tf_op jit(solution)/shard_map/psum | solution.py:249
  541.1 4.0 copy-start.27
  548.0 1.0 copy-start.15
  548.0 34.3 %copy-start.36 = (f32[1024]{0:T(1024)S(1)}, f32[1024]{0:T(1024)}, u32[]{:S(2)}) copy-start(f32[1024]{0:T(1024)} %param.26) | copy-start | bytes 12292
  548.0 34.3 %copy-start.38 = (f32[256]{0:T(256)S(1)}, f32[256]{0:T(256)}, u32[]{:S(2)}) copy-start(f32[256]{0:T(256)} %copy-done.37) | copy-start | bytes 3076
  548.0 34.3 %copy-start.40 = (f32[256]{0:T(256)S(1)}, f32[256]{0:T(256)}, u32[]{:S(2)}) copy-start(f32[256]{0:T(256)} %copy-done.39) | copy-start | bytes 3076
  548.0 34.4 %copy-start.42 = (f32[256]{0:T(256)S(1)}, f32[256]{0:T(256)}, u32[]{:S(2)}) copy-start(f32[256]{0:T(256)} %copy-done.41) | copy-start | bytes 3076
  548.0 105.0 %copy-start.43 = (f32[1024]{0:T(1024)S(1)}, f32[1024]{0:T(1024)}, u32[]{:S(2)}) copy-start(f32[1024]{0:T(1024)} %param.39) | copy-start | bytes 12292
  825.3 2.9 copy-start.30
  828.2 1.6 copy-start.29
  829.8 1.6 copy-start.28
  829.8 4.0 copy-start.17
  833.8 4.5 copy-start.16
  838.3 4.4 copy-start.1
  (1 other events, 0.7 us)
Sparse Core Ops, SparseCore 0:
  13.7 53.2 all-gather.3
  69.7 49.0 all-gather.5
  186.9 27.0 all-reduce.7
  230.9 28.5 all-reduce.9
  432.6 104.8 reduce-scatter.1
  541.2 39.9 all-reduce.13
  588.3 236.9 all-reduce.11
where the time goes:
time: 853 us; the launch traced here: 850 us
  waiting for transfers between devices  421 us (49%)
  matrix products  137 us (16%)
  local copies, waits for them, and re-layouts  117 us (14%)
  blocking collectives  87.4 us (10%)
  other arithmetic  63 us (7%)
  between operations  14.7 us (2%)
    psum x1, waiting for transfers between devices, local(): lax.psum(dquery_weight.astype(jnp.bfloat16), 'band').astype(jnp.float32)  169 us
    reduce_scatter x1, waiting for transfers between devices, local(): lax.psum_scatter(folded[1].astype(jnp.bfloat16), 'band', scatter_dimensio...  90.7 us
    dynamic_update_slice x4, local copies, waits for them, and re-layouts, backward_step(): buffer = lax.dynamic_update_slice(state[1], block_rows, (offset, 0))  73.9 us
    psum x1, blocking collectives, local(): lax.psum(dgain_attn.astype(jnp.bfloat16), 'band').astype(jnp.float32)  64.3 us
    all_gather x1, waiting for transfers between devices, local(): lax.all_gather(value_low, 'band', axis=0, tiled=True)  45.5 us
    psum x1, waiting for transfers between devices, local(): lax.psum(jnp.dot(active_low, down_weight, preferred_element_type=jnp.floa...  32.1 us
    psum x1, waiting for transfers between devices, local(): lax.psum(right_product(d_upper, up_weight).astype(jnp.bfloat16), 'head')  28.7 us
    all_gather x1, waiting for transfers between devices, local(): lax.all_gather(key_low, 'band', axis=0, tiled=True)  27.1 us
  transfers between devices with their start and end apart: 7, of which 7 were waited for; matrix products, arithmetic and copies ran while one was open for 5% of the time, Pallas kernels for 0%

commit v1 on v0

v1 whole, which is shorter than its diff:
```python
import functools

import jax
import jax.numpy as jnp
from jax import lax
from jax.experimental import pallas as pl
from jax.experimental.pallas import tpu as pltpu
from jax.sharding import Mesh, PartitionSpec as P

HD = 64
F32 = jnp.float32
BF16 = jnp.bfloat16
eps = 1e-05
masked_value = -1e30
seg_row = 3 * HD
payload_rows = 3 * HD + 16
vmem_limit = 48 * 2**20


def normalize(values):
    centred = values - jnp.mean(values, axis=-1, keepdims=True)
    inverse = lax.rsqrt(jnp.mean(centred * centred, axis=-1, keepdims=True) + eps)
    return (centred * inverse, inverse)


def normalize_back(grad_unit, unit, inverse):
    return inverse * (
        grad_unit
        - jnp.mean(grad_unit, axis=-1, keepdims=True)
        - unit * jnp.mean(grad_unit * unit, axis=-1, keepdims=True)
    )


def product(first, second, first_axis=1, second_axis=0):
    return lax.dot_general(
        first,
        second,
        (((first_axis,), (second_axis,)), ((), ())),
        preferred_element_type=jnp.float32,
    )


def exact_gelu(values):
    return jax.nn.gelu(values, approximate=False)


def load_keys(pieces, crops, keys, key_t, value_t, value_n):
    start = 0
    for piece in pieces:
        chips, _, patches = piece.shape
        for chip in range(chips):
            crop = lax.broadcasted_iota(jnp.int32, (HD, patches), 0)
            segment = piece[chip, pl.ds(seg_row, 16), :].astype(F32)[:1].astype(jnp.int32)
            mask = jnp.where((crop != segment) & (crop < crops), masked_value, 0.0)
            key = piece[chip, pl.ds(HD, HD), :]
            value = piece[chip, pl.ds(2 * HD, HD), :]
            place = pl.ds(start, patches)
            keys[place, :] = jnp.concatenate([key.astype(F32), mask], axis=0).T.astype(BF16)
            if key_t is not None:
                key_t[:, place] = key
            if value_t is not None:
                value_t[pl.ds(0, HD), place] = value
                value_t[pl.ds(HD, 16), place] = jnp.ones((16, patches), BF16)
            if value_n is not None:
                value_n[place, :] = value.astype(F32).T.astype(BF16)
            start += patches


def masked_query(query_ref):
    query = query_ref[0, pl.ds(0, HD), :].astype(F32) * 0.125
    segment = query_ref[0, pl.ds(seg_row, 16), :].astype(F32)[:1].astype(jnp.int32)
    crop = lax.broadcasted_iota(jnp.int32, query.shape, 0)
    onehot = jnp.where(crop == segment, 1.0, 0.0)
    return jnp.concatenate([query, onehot], axis=0).astype(BF16)


def forward_kernel(crops, step, query_ref, own, other, raw_ref, out_ref, logsum_ref, keys, value_t):
    @pl.when(pl.program_id(0) == 0)
    def _():
        load_keys((own, other), crops, keys, None, value_t, None)

    query = masked_query(query_ref)
    count = query.shape[1]
    top = jnp.full((1, count), masked_value, F32)
    accum = jnp.zeros((HD + 16, count), F32)
    for start in range(0, keys.shape[0], step):
        scores = product(keys[pl.ds(start, step), :], query)
        new_top = jnp.maximum(top, jnp.max(scores, axis=0, keepdims=True))
        weights = jnp.exp(scores - new_top).astype(BF16)
        accum = accum * jnp.exp(top - new_top) + product(value_t[:, pl.ds(start, step)], weights)
        top = new_top
    total = accum[HD : HD + 1]
    raw = accum[:HD] / total
    raw_ref[0] = raw
    out_ref[0] = raw.astype(BF16)
    logsum_ref[0] = top + jnp.log(total)


def backward_kernel(
    crops,
    step,
    query_ref,
    grad_ref,
    raw_ref,
    logsum_ref,
    own,
    other,
    dquery_ref,
    own_ref,
    other_ref,
    keys,
    key_t,
    value_n,
    sums,
):
    group = pl.program_id(0)

    @pl.when(group == 0)
    def _():
        load_keys((own, other), crops, keys, key_t, None, value_n)
        sums[...] = jnp.zeros_like(sums)

    query = masked_query(query_ref)
    grad = grad_ref[0]
    grad_wide = grad.astype(F32)
    delta = jnp.sum(grad_wide * raw_ref[0], axis=0, keepdims=True)
    logsum = logsum_ref[0]
    scaled = query_ref[0, pl.ds(0, HD), :].astype(F32) * 0.125
    zero = jnp.zeros_like(scaled)
    query_side = jnp.concatenate([scaled, zero], axis=0).T.astype(BF16)
    grad_side = jnp.concatenate([zero, grad_wide], axis=0).T.astype(BF16)
    dquery = jnp.zeros_like(scaled)
    for start in range(0, keys.shape[0], step):
        place = pl.ds(start, step)
        probs = jnp.exp(product(keys[place, :], query) - logsum)
        dprobs = product(value_n[place, :], grad)
        dscores = (probs * (dprobs - delta)).astype(BF16)
        sums[place, :] += product(dscores, query_side) + product(probs.astype(BF16), grad_side)
        dquery += product(key_t[:, place], dscores)
    dquery_ref[0] = (dquery * 0.125).astype(BF16)

    @pl.when(group == pl.num_programs(0) - 1)
    def _():
        start = 0
        for target in (own_ref, other_ref):
            chips, _, patches = target.shape
            for chip in range(chips):
                target[chip] = sums[pl.ds(start, patches), :].T.astype(target.dtype)
                start += patches


def key_step(count):
    return 1024 if count % 1024 == 0 else 256


def query_spec(rows, patches):
    return pl.BlockSpec((1, rows, patches), lambda group: (group, 0, 0))


def whole_spec(shape):
    return pl.BlockSpec(shape, lambda group: (0,) * len(shape))


def attention_forward(queries, own, other, crops):
    groups, _, patches = queries.shape
    count = 2 * own.shape[0] * own.shape[2]
    return pl.pallas_call(
        functools.partial(forward_kernel, crops, key_step(count)),
        grid=(groups,),
        in_specs=[
            query_spec(payload_rows, patches),
            whole_spec(own.shape),
            whole_spec(other.shape),
        ],
        out_specs=[query_spec(HD, patches), query_spec(HD, patches), query_spec(1, patches)],
        out_shape=[
            jax.ShapeDtypeStruct((groups, HD, patches), F32),
            jax.ShapeDtypeStruct((groups, HD, patches), BF16),
            jax.ShapeDtypeStruct((groups, 1, patches), F32),
        ],
        scratch_shapes=[pltpu.VMEM((count, 2 * HD), BF16), pltpu.VMEM((HD + 16, count), BF16)],
        compiler_params=pltpu.CompilerParams(vmem_limit_bytes=vmem_limit),
        name="attention_forward",
    )(queries, own, other)


def attention_backward(queries, grads, raw, logsum, own, other, crops):
    groups, _, patches = queries.shape
    count = 2 * own.shape[0] * own.shape[2]
    sums_shape = (own.shape[0], 2 * HD, own.shape[2])
    return pl.pallas_call(
        functools.partial(backward_kernel, crops, key_step(count)),
        grid=(groups,),
        in_specs=[
            query_spec(payload_rows, patches),
            query_spec(HD, patches),
            query_spec(HD, patches),
            query_spec(1, patches),
            whole_spec(own.shape),
            whole_spec(other.shape),
        ],
        out_specs=[query_spec(HD, patches), whole_spec(sums_shape), whole_spec(sums_shape)],
        out_shape=[
            jax.ShapeDtypeStruct((groups, HD, patches), BF16),
            jax.ShapeDtypeStruct(sums_shape, F32),
            jax.ShapeDtypeStruct(sums_shape, BF16),
        ],
        scratch_shapes=[
            pltpu.VMEM((count, 2 * HD), BF16),
            pltpu.VMEM((HD, count), BF16),
            pltpu.VMEM((count, HD), BF16),
            pltpu.VMEM((count, 2 * HD), F32),
        ],
        compiler_params=pltpu.CompilerParams(vmem_limit_bytes=vmem_limit),
        name="attention_backward",
    )(queries, grads, raw, logsum, own, other)


def swap_cores(values):
    return lax.ppermute(values, "core", [(0, 1), (1, 0)])


def to_heads(blocks):
    return lax.all_to_all(blocks, "chip", 0, 0, tiled=True)


def scatter_queries(values, heads, split):
    rows, patches = values.shape[0] // heads, values.shape[1]
    if split == 1:
        return to_heads(values.reshape(heads, rows, patches))
    part = patches // split
    blocks = values.reshape(heads, rows, split, part).transpose(0, 2, 1, 3)
    moved = to_heads(blocks.reshape(heads * split, rows, part))
    width = min(256, moved.shape[0] * part)
    joined = moved.transpose(1, 0, 2).reshape(rows, -1, width)
    return joined.transpose(1, 0, 2)


def gather_queries(values, heads, split, patches):
    rows = values.shape[1]
    if split == 1:
        return to_heads(values).reshape(heads * rows, patches)
    part = patches // split
    joined = values.transpose(1, 0, 2).reshape(rows, heads * split, part)
    moved = to_heads(joined.transpose(1, 0, 2)).reshape(heads, split, rows, part)
    return moved.transpose(0, 2, 1, 3).reshape(heads * rows, patches)


def head_sum(values):
    low = values.astype(BF16)
    if lax.axis_size("head") == 2:
        return low.astype(F32) + lax.ppermute(low, "head", [(0, 1), (1, 0)]).astype(F32)
    return lax.psum(low, "head").astype(F32)


def band_sum(values):
    values = values + swap_cores(values)
    chips, reach = lax.axis_size("chip"), 1
    while reach < chips:
        pairs = [(chip, chip ^ reach) for chip in range(chips)]
        values = values + lax.ppermute(values, "chip", pairs)
        reach *= 2
    return values


def local(
    block_input,
    out_grad,
    segments,
    lead_steps,
    gain_attn,
    shift_attn,
    lead_weight,
    query_weight,
    key_weight,
    value_weight,
    output_weight,
    output_bias,
    gain_mlp,
    shift_mlp,
    up_weight,
    up_bias,
    down_weight,
    down_bias,
):
    rows = block_input.shape[0]
    heads = query_weight.shape[1] // HD
    width = heads * HD
    chips = lax.axis_size("chip")
    split = chips // heads
    crops = lead_steps.shape[0]
    inputs = block_input.astype(F32)
    unit_attn, inverse_attn = normalize(inputs)
    onehot = (segments[:, None] == jnp.arange(crops, dtype=jnp.int32)[None, :]).astype(F32)
    lead = jnp.sum(onehot * lead_steps.astype(F32)[None, :], axis=1) / 12.0
    attn_in = (unit_attn * gain_attn + shift_attn + lead[:, None] * lead_weight).astype(BF16)
    query, key, value = (
        product(weight, attn_in, 0, 1).astype(BF16).reshape(heads, HD, rows)
        for weight in (query_weight, key_weight, value_weight)
    )
    crop_rows = jnp.broadcast_to(segments.astype(BF16), (heads, 16, rows))
    payload = jnp.concatenate([query, key, value, crop_rows], axis=1)
    if split == 1:
        own = to_heads(payload)
        queries = own
    else:
        queries = scatter_queries(payload.reshape(-1, rows), heads, split)
        own = to_heads(jnp.repeat(payload, split, axis=0))
    other = swap_cores(own)
    raw, out, logsum = attention_forward(queries, own, other, crops)
    attn_out = gather_queries(out, heads, split, rows)
    branch = head_sum(product(attn_out, output_weight, 0, 0))
    hidden = inputs + branch + output_bias
    unit_mlp, inverse_mlp = normalize(hidden)
    mlp_in = (unit_mlp * gain_mlp + shift_mlp).astype(BF16)
    upper = product(mlp_in, up_weight) + up_bias
    active, gelu_back = jax.vjp(exact_gelu, upper)
    active_low = active.astype(BF16)
    d_active = product(out_grad, down_weight, 1, 1)
    d_upper = gelu_back(d_active)[0].astype(BF16)
    d_mlp = head_sum(product(d_upper, up_weight, 1, 1))
    mlp_out = head_sum(product(active_low, down_weight))
    block_output = (hidden + mlp_out + down_bias).astype(BF16)
    grad_out = out_grad.astype(F32)
    ddown_weight = product(active_low, out_grad, 0, 0)
    dup_weight = product(mlp_in, d_upper, 0, 0)
    d_hidden = grad_out + normalize_back(d_mlp * gain_mlp, unit_mlp, inverse_mlp)
    d_branch = d_hidden.astype(BF16)
    doutput_weight = product(attn_out, d_branch)
    d_attn = product(output_weight, d_branch, 1, 1).astype(BF16)
    grads = scatter_queries(d_attn, heads, split)
    dquery, own_sums, other_sums = attention_backward(
        queries, grads, raw, logsum, own, other, crops
    )
    key_value = (own_sums + swap_cores(other_sums).astype(F32)).astype(BF16)
    if split == 1:
        moved = to_heads(jnp.concatenate([dquery, key_value], axis=1))
        dquery, dkey, dvalue = (
            moved[:, at * HD : at * HD + HD].reshape(width, rows) for at in range(3)
        )
    else:
        dquery = gather_queries(dquery, heads, split, rows)
        moved = to_heads(key_value).reshape(heads, split, 2 * HD, rows).astype(F32)
        moved = jnp.sum(moved, axis=1).astype(BF16)
        dkey, dvalue = (moved[:, at * HD : at * HD + HD].reshape(width, rows) for at in range(2))
    dquery_weight, dkey_weight, dvalue_weight = (
        product(attn_in, grad, 0, 1) for grad in (dquery, dkey, dvalue)
    )
    d_in = head_sum(
        product(dquery, query_weight, 0, 1)
        + product(dkey, key_weight, 0, 1)
        + product(dvalue, value_weight, 0, 1)
    )
    input_grad = (d_hidden + normalize_back(d_in * gain_attn, unit_attn, inverse_attn)).astype(
        BF16
    )
    small = band_sum(
        jnp.stack(
            [
                jnp.sum(d_in * unit_attn, axis=0),
                jnp.sum(d_in, axis=0),
                jnp.sum(lead[:, None] * d_in, axis=0),
                jnp.sum(d_hidden, axis=0),
                jnp.sum(d_mlp * unit_mlp, axis=0),
                jnp.sum(d_mlp, axis=0),
                jnp.sum(grad_out, axis=0),
            ]
        )
    )
    dup_bias = band_sum(jnp.sum(d_upper.astype(F32), axis=0))
    large = [
        lax.psum(grad.astype(BF16), ("chip", "core")).astype(F32)
        for grad in (
            dquery_weight,
            dkey_weight,
            dvalue_weight,
            doutput_weight,
            dup_weight,
            ddown_weight,
        )
    ]
    return (
        block_output,
        input_grad,
        small[0],
        small[1],
        small[2],
        large[0],
        large[1],
        large[2],
        large[3],
        small[3],
        small[4],
        small[5],
        large[4],
        dup_bias,
        large[5],
        small[6],
    )


def solution(mesh):
    bands, halves = mesh.shape["band"], mesh.shape["head"]
    inner = Mesh(mesh.devices.reshape(bands // 2, 2, halves), ("chip", "core", "head"))
    band = ("chip", "core")
    rows, columns, split_rows = P(band, None), P(None, "head"), P("head", None)
    return jax.shard_map(
        local,
        mesh=inner,
        in_specs=(
            rows,
            rows,
            P(band),
            P(),
            P(),
            P(),
            P(),
            columns,
            columns,
            columns,
            split_rows,
            P(),
            P(),
            P(),
            columns,
            P("head"),
            split_rows,
            P(),
        ),
        out_specs=(
            rows,
            rows,
            P(),
            P(),
            P(),
            columns,
            columns,
            columns,
            split_rows,
            P(),
            P(),
            P(),
            columns,
            P("head"),
            split_rows,
            P(),
        ),
        check_vma=False,
    )
```

time: 853 us -> 469 us (0.55)
  waiting for transfers between devices: 421 us -> 268 us
  local copies, waits for them, and re-layouts: 117 us -> 8.16 us
  matrix products: 137 us -> 29.5 us
  Pallas kernels: 0 us -> 46.1 us
  blocking collectives: 87.4 us -> 55.4 us
  other arithmetic: 63 us -> 31.9 us
  starting transfers between devices: 0.69 us -> 15 us
    dot_general x47 -> x18, matrix products: 137 us -> 29.5 us  [product(): lax.dot_general(first, second, (((first_axis,), (second_axis,)), ((), ())...]
    reduce_scatter x1 -> x0, waiting for transfers between devices: 90.7 us -> none  [local(): lax.psum_scatter(folded[1].astype(jnp.bfloat16), 'band', scatter_dimensio...]
    dynamic_update_slice x4 -> x0, local copies, waits for them, and re-layouts: 73.9 us -> none  [backward_step(): buffer = lax.dynamic_update_slice(state[1], block_rows, (offset, 0))]
    all_gather x2 -> x0, waiting for transfers between devices: 72.6 us -> none  [the longest x1 45.5 us: local(): lax.all_gather(value_low, 'band', axis=0, tiled=True)]
    psum x4 -> x1, waiting for transfers between devices: 257 us -> 190 us  [local(): lax.psum(grad.astype(BF16), ('chip', 'core')).astype(F32)]
    ppermute x0 -> x14, waiting for transfers between devices: none -> 65 us  [the longest x4 39.8 us: head_sum(): lax.ppermute(low, 'head', [(0, 1), (1, 0)]).astype(F32)]
    psum x1 -> x0, blocking collectives: 64.3 us -> none  [local(): lax.psum(dgain_attn.astype(jnp.bfloat16), 'band').astype(jnp.float32)]
    all_to_all x0 -> x3, blocking collectives: none -> 55.4 us  [to_heads(): return lax.all_to_all(blocks, 'chip', 0, 0, tiled=True)]
  transfers between devices with their start and end apart: 7 -> 16, of which waited for: 7 -> 14; matrix products, arithmetic and copies ran while one was open for 5% -> 3% of each run, Pallas kernels for 0% -> 0%
where the time goes in v1:
time: 469 us; the launch traced here: 468 us
  waiting for transfers between devices  268 us (57%)
  blocking collectives  55.4 us (12%)
  Pallas kernels  46.1 us (10%)
  other arithmetic  31.9 us (7%)
  matrix products  29.5 us (6%)
  starting transfers between devices  15 us (3%)
  between operations  14.8 us (3%)
  local copies, waits for them, and re-layouts  8.16 us (2%)
    psum x1, waiting for transfers between devices, local(): lax.psum(grad.astype(BF16), ('chip', 'core')).astype(F32)  190 us
    all_to_all x3, blocking collectives, to_heads(): return lax.all_to_all(blocks, 'chip', 0, 0, tiled=True)  55.4 us
    ppermute x4, waiting for transfers between devices, head_sum(): lax.ppermute(low, 'head', [(0, 1), (1, 0)]).astype(F32)  39.8 us
    dot_general x18, matrix products, product(): lax.dot_general(first, second, (((first_axis,), (second_axis,)), ((), ())...  29.5 us
    pallas_call x1, Pallas kernels, attention_forward(): pl.pallas_call(functools.partial(forward_kernel, crops, key_step(count)),...  23.5 us
    pallas_call x1, Pallas kernels, attention_backward(): pl.pallas_call(functools.partial(backward_kernel, crops, key_step(count))...  22.6 us
    ppermute x6, waiting for transfers between devices, band_sum(): values = values + lax.ppermute(values, 'chip', pairs)  20.9 us
    convert_element_type x6, other arithmetic, local(): lax.psum(grad.astype(BF16), ('chip', 'core')).astype(F32)  17.6 us
  transfers between devices with their start and end apart: 16, of which 14 were waited for; matrix products, arithmetic and copies ran while one was open for 3% of the time, Pallas kernels for 0%

profile of v1, /device:TPU:0, one launch (start us, length us, event | category | flops | bytes accessed | tf_op | source)
XLA Modules:
  0.0 468.4 jit_solution(3069642675704702828)
XLA Ops:
  7.2 1.3 convert_reduce_fusion.1
  8.6 1.4 fusion.26
  10.0 0.7 convert_element_type.140
  10.6 0.7 convert_element_type.148
  11.3 0.8 select_reduce_fusion
  12.1 1.4 fusion.19
  14.8 1.7 fusion.15
  16.6 29.3 %all_to_all.20.query_ref.own = bf16[8,208,256]{2,1,0:T(8,128)(2,1)S(1)} all-to-all(bf16[8,208,256]{2,1,0:T(8,128)(2,1)S(1)} %pad_maximum_fusion), channel_id=1, replica_groups=mesh['chip'=8,'core'=2,'head'=2] {'chip'}, dimensions={0} | all-to-all | bytes 1703936 | tf_op jit(solution)/shard_map/all_to_all | solution.py:224
  45.9 2.4 collective-permute-done.other
  48.3 23.5 %attention_forward.1 = (f32[8,64,256]{2,1,0:T(8,128)S(1)}, bf16[8,64,256]{2,1,0:T(8,128)(2,1)S(1)}, f32[8,1,256]{2,1,0:T(1,128)S(1)}) custom-call(bf16[8,208,256]{2,1,0:T(8,128)(2,1)S(1)} %all_to_all.20.query_ref.own, bf16[8,208,256]{2,1,0:T(8,128)(2,1)S(1)} %all_to_all.20.query_ref.own, bf16[8,208,256]{2,1,0:T(8,128)(2,1)S(1)} %collective-permute-done.other), custom_call_target="tpu_custom_call" | custom-call | tf_op jit(solution)/shard_map/attention_forward/pallas_call | solution.py:167
  71.8 12.0 %all_to_all.21 = bf16[8,64,256]{2,1,0:T(8,128)(2,1)S(1)} all-to-all(bf16[8,64,256]{2,1,0:T(8,128)(2,1)S(1)} %get-tuple-element.22), channel_id=1, replica_groups=mesh['chip'=8,'core'=2,'head'=2] {'chip'}, dimensions={0} | all-to-all | bytes 524288 | tf_op jit(solution)/shard_map/all_to_all | solution.py:224
  84.3 1.6 collective-permute-start.1
  85.8 10.7 %collective-permute-done.1 = bf16[256,1024]{1,0:T(8,128)(2,1)S(1)} collective-permute-done((bf16[256,1024]{1,0:T(8,128)(2,1)S(1)}, bf16[256,1024]{1,0:T(8,128)(2,1)S(1)}, u32[]{:S(2)}, u32[]{:S(2)}) %collective-permute-start.1) | collective-permute-done | bytes 524320 | tf_op jit(solution)/shard_map/ppermute | solution.py:252
  97.2 1.4 convolution_add_fusion
  98.6 1.0 copy-done.47
  99.6 7.3 %convert_reduce_fusion = (f32[2048]{0:T(1024)}, bf16[256,2048]{1,0:T(8,128)(2,1)S(1)}, f32[256,2048]{1,0:T(8,128)S(1)}) fusion(f32[256,2048]{1,0:T(8,128)S(1)} %convolution_add_fusion, bf16[256,1024]{1,0:T(8,128)(2,1)S(1)} %copy-done.18, bf16[2048,1024]{1,0:T(8,128)(2,1)S(1)} %copy-done.47), kind=kOutput, calls=%fused_computation.5 | convolution fusion | flops 1112537088 | bytes 9969664 | tf_op jit(solution)/shard_map/dot_general | solution.py:35
  106.9 1.3 convolution_convert_fusion.7
  108.2 1.5 collective-permute-start.3
  110.1 1.3 convolution_convert_fusion.8
  111.4 0.6 collective-permute-start.2
  112.1 11.1 %collective-permute-done.3 = bf16[256,1024]{1,0:T(8,128)(2,1)S(1)} collective-permute-done((bf16[256,1024]{1,0:T(8,128)(2,1)S(1)}, bf16[256,1024]{1,0:T(8,128)(2,1)S(1)}, u32[]{:S(2)}, u32[]{:S(2)}) %collective-permute-start.3) | collective-permute-done | bytes 524320 | tf_op jit(solution)/shard_map/ppermute | solution.py:252
  123.1 1.1 multiply_reduce_fusion
  124.3 6.5 %collective-permute-done.2 = bf16[256,1024]{1,0:T(8,128)(2,1)S(1)} collective-permute-done((bf16[256,1024]{1,0:T(8,128)(2,1)S(1)}, bf16[256,1024]{1,0:T(8,128)(2,1)S(1)}, u32[]{:S(2)}, u32[]{:S(2)}) %collective-permute-start.2) | collective-permute-done | bytes 524320 | tf_op jit(solution)/shard_map/ppermute | solution.py:252
  130.8 2.1 fusion.35
  132.9 1.0 copy-done.8
  133.9 1.2 fusion.16
  135.1 1.1 copy.41
  136.2 14.2 %all_to_all.22.grad_ref = bf16[8,64,256]{2,1,0:T(8,128)(2,1)S(1)} all-to-all(bf16[8,64,256]{2,1,0:T(8,128)(2,1)S(1)} %bitcast.70), channel_id=1, replica_groups=mesh['chip'=8,'core'=2,'head'=2] {'chip'}, dimensions={0} | all-to-all | bytes 524288 | tf_op jit(solution)/shard_map/all_to_all | solution.py:224
  150.3 22.6 %attention_backward.1 = (bf16[8,64,256]{2,1,0:T(8,128)(2,1)S(1)}, f32[8,128,256]{2,1,0:T(8,128)S(1)}, bf16[8,128,256]{2,1,0:T(8,128)(2,1)S(1)}) custom-call(bf16[8,208,256]{2,1,0:T(8,128)(2,1)S(1)} %all_to_all.20.query_ref.own, bf16[8,64,256]{2,1,0:T(8,128)(2,1)S(1)} %all_to_all.22.grad_ref, f32[8,64,256]{2,1,0:T(8,128)S(1)} %get-tuple-element.23.raw_ref, ...), custom_call_target="tpu_custom_call" | custom-call | tf_op jit(solution)/shard_map/attention_backward/pallas_call | solution.py:191
  173.0 1.9 collective-permute-done.4
  175.1 1.0 pad_maximum_fusion.1
  176.1 4.2 all-to-all-start.3
  180.6 3.3 convolution_convert_fusion
  183.9 3.5 convolution_convert_fusion.1
  187.4 1.4 convolution_convert_fusion.2
  188.8 12.2 %all-to-all-done.3 = bf16[8,192,256]{2,1,0:T(8,128)(2,1)} async-done(((bf16[8,192,256]{2,1,0:T(8,128)(2,1)}), bf16[8,192,256]{2,1,0:T(8,128)(2,1)}, u32[]{:S(2)}, u32[]{:S(2)}) %all-to-all-start.3) | async-done | bytes 786464 | tf_op jit(solution)/shard_map/all_to_all | solution.py:224
  201.0 1.2 fusion.38
  202.2 1.5 convolution_convert_fusion.3
  203.6 1.5 convolution_convert_fusion.4
  205.1 1.5 convolution_convert_fusion.5
  206.6 1.2 copy-done.14
  208.3 0.7 copy-done.16
  209.5 0.7 copy-done.17
  210.8 1.6 collective-permute-start.5
  212.4 11.6 %collective-permute-done.5 = bf16[256,1024]{1,0:T(8,128)(2,1)S(1)} collective-permute-done((bf16[256,1024]{1,0:T(8,128)(2,1)S(1)}, bf16[256,1024]{1,0:T(8,128)(2,1)S(1)}, u32[]{:S(2)}, u32[]{:S(2)}) %collective-permute-start.5) | collective-permute-done | bytes 524320 | tf_op jit(solution)/shard_map/ppermute | solution.py:252
  224.0 0.7 fusion.25
  224.9 1.5 collective-permute-start.11
  226.4 2.2 collective-permute-done.11
  228.7 4.0 collective-permute-done.12
  232.7 0.9 collective-permute-start.13
  233.6 4.0 collective-permute-done.13
  238.2 1.5 collective-permute-start.7
  239.7 2.4 collective-permute-done.7
  242.2 4.8 %collective-permute-done.8 = f32[7,1024]{1,0:T(8,128)S(1)} collective-permute-done((f32[7,1024]{1,0:T(8,128)S(1)}, f32[7,1024]{1,0:T(8,128)S(1)}, u32[]{:S(2)}, u32[]{:S(2)}) %collective-permute-start.8) | collective-permute-done | bytes 28704 | tf_op jit(solution)/shard_map/ppermute | solution.py:261
  246.9 1.2 collective-permute-start.9
  248.1 1.3 fusion.24
  249.4 3.5 collective-permute-done.9
  253.5 190.4 %all-reduce.3.cloned.1.call-done = (bf16[1024,512]{1,0:T(8,128)(2,1)}, bf16[1024,512]{1,0:T(8,128)(2,1)}, bf16[1024,512]{1,0:T(8,128)(2,1)}, bf16[512,1024]{1,0:...) async-done(((bf16[1024,512]{1,0:T(8,128)(2,1)}, bf16[1024,512]{1,0:T(8,128)(2,1)}, bf16[1024,512]{1,0:T(8,128)(2,1)}, bf16[512,1024]{1,0:T(8,128)(2,1)}, ...) | async-done | bytes 12582928 | tf_op jit(solution)/shard_map/psum | solution.py:372
  443.9 6.8 %convert_element_type.181 = f32[1024,2048]{1,0:T(8,128)} convert(bf16[1024,2048]{1,0:T(8,128)(2,1)} %get-tuple-element.41) | non-fusion elementwise | flops 2097152 | bytes 12582912 | tf_op jit(solution)/shard_map/convert_element_type | solution.py:372
  450.7 4.4 convert_element_type.184
  455.2 1.6 convert_element_type.173
  456.8 1.6 convert_element_type.175
  458.4 1.6 convert_element_type.177
  460.0 1.6 convert_element_type.179
  (136 shorter events, 6.3 us)
Async XLA Ops:
  7.2 76.6 %copy-start = (bf16[512,1024]{1,0:T(8,128)(2,1)S(1)}, bf16[512,1024]{1,0:T(8,128)(2,1)}, u32[]{:S(2)}) copy-start(bf16[512,1024]{1,0:T(8,128)(2,1)} %param.28) | copy-start | bytes 3145732
  7.2 6.4 %copy-start.13 = (bf16[1024,512]{1,0:T(8,128)(2,1)S(1)}, bf16[1024,512]{1,0:T(8,128)(2,1)}, u32[]{:S(2)}) copy-start(bf16[1024,512]{1,0:T(8,128)(2,1)} %param.25) | copy-start | bytes 3145732
  8.5 5.6 %copy-start.15 = (bf16[1024,512]{1,0:T(8,128)(2,1)S(1)}, bf16[1024,512]{1,0:T(8,128)(2,1)}, u32[]{:S(2)}) copy-start(bf16[1024,512]{1,0:T(8,128)(2,1)} %param.26) | copy-start | bytes 3145732
  8.6 5.0 %copy-start.31 = (f32[256]{0:T(256)}, f32[256]{0:T(256)S(1)}, u32[]{:S(2)}) copy-start(f32[256]{0:T(256)S(1)} %broadcast_multiply_fusion.6) | copy-start | bytes 3076
  12.1 1.4 copy-start.37
  12.1 1.4 copy-start.41
  13.6 1.2 copy-start.4
  45.9 50.6 %copy-start.6 = (bf16[256,1024]{1,0:T(8,128)(2,1)S(1)}, bf16[256,1024]{1,0:T(8,128)(2,1)}, u32[]{:S(2)}) copy-start(bf16[256,1024]{1,0:T(8,128)(2,1)} %param.18) | copy-start | bytes 1572868
  45.9 50.6 %copy-start.44 = (f32[1024]{0:T(1024)S(1)}, f32[1024]{0:T(1024)}, u32[]{:S(2)}) copy-start(f32[1024]{0:T(1024)} %param.29) | copy-start | bytes 12292
  45.9 2.4 collective-permute-start
  83.8 13.4 %copy-start.46 = (bf16[1024,2048]{1,0:T(8,128)(2,1)S(1)}, bf16[1024,2048]{1,0:T(8,128)(2,1)}, u32[]{:S(2)}) copy-start(bf16[1024,2048]{1,0:T(8,128)(2,1)} %param.32) | copy-start | bytes 12582916
  84.2 12.9 %copy-start.26 = (f32[1024]{0:T(1024)S(1)}, f32[1024]{0:T(1024)}, u32[]{:S(2)}) copy-start(f32[1024]{0:T(1024)} %param.30) | copy-start | bytes 12292
  84.3 12.9 %copy-start.27 = (f32[1024]{0:T(1024)S(1)}, f32[1024]{0:T(1024)}, u32[]{:S(2)}) copy-start(f32[1024]{0:T(1024)} %param.31) | copy-start | bytes 12292
  84.3 12.9 %copy-start.48 = (f32[2048]{0:T(1024)S(1)}, f32[2048]{0:T(1024)}, u32[]{:S(2)}) copy-start(f32[2048]{0:T(1024)} %param.33) | copy-start | bytes 24580
  84.3 12.2 %collective-permute-start.1 = (bf16[256,1024]{1,0:T(8,128)(2,1)S(1)}, bf16[256,1024]{1,0:T(8,128)(2,1)S(1)}, u32[]{:S(2)}, u32[]{:S(2)}) collective-permute-start(bf16[256,1024]{1,0:T(8,128)(2,1)S(1)} %convolution_convert_fusion.6), channel_id=1, source_target_pairs={{0,1},{1,0},{2,3},{3,2},{4,5},{5,4},{6,7},{7,6},{8,9},{9,8},{10,11... | collective-permute-start | bytes 1572872 | tf_op jit(solution)/shard_map/ppermute | solution.py:252
  96.8 33.9 %copy-start.2 = (f32[256,1024]{1,0:T(8,128)}, f32[256,1024]{1,0:T(8,128)S(1)}, u32[]{:S(2)}) copy-start(f32[256,1024]{1,0:T(8,128)S(1)} %get-tuple-element.49) | copy-start | bytes 3145732
  96.9 33.9 %copy-start.29 = (f32[256]{0:T(256)}, f32[256]{0:T(256)S(1)}, u32[]{:S(2)}) copy-start(f32[256]{0:T(256)S(1)} %broadcast_multiply_fusion.5) | copy-start | bytes 3076
  97.2 33.6 %copy-start.33 = (f32[256]{0:T(256)}, f32[256]{0:T(256)S(1)}, u32[]{:S(2)}) copy-start(f32[256]{0:T(256)S(1)} %add_rsqrt_fusion) | copy-start | bytes 3076
  97.2 1.4 copy-start.18
  97.2 2.4 copy-start.47
  106.9 1.3 copy-start.24
  108.2 14.9 %collective-permute-start.3 = (bf16[256,1024]{1,0:T(8,128)(2,1)S(1)}, bf16[256,1024]{1,0:T(8,128)(2,1)S(1)}, u32[]{:S(2)}, u32[]{:S(2)}) collective-permute-start(bf16[256,1024]{1,0:T(8,128)(2,1)S(1)} %convolution_convert_fusion.7), channel_id=1, source_target_pairs={{0,1},{1,0},{2,3},{3,2},{4,5},{5,4},{6,7},{7,6},{8,9},{9,8},{10,11... | collective-permute-start | bytes 1572872 | tf_op jit(solution)/shard_map/ppermute | solution.py:252
  110.1 1.3 copy-start.10
  111.4 19.3 %copy-start.45 = (f32[1024]{0:T(1024)S(1)}, f32[1024]{0:T(1024)}, u32[]{:S(2)}) copy-start(f32[1024]{0:T(1024)} %param.35) | copy-start | bytes 12292
  111.4 19.3 %collective-permute-start.2 = (bf16[256,1024]{1,0:T(8,128)(2,1)S(1)}, bf16[256,1024]{1,0:T(8,128)(2,1)S(1)}, u32[]{:S(2)}, u32[]{:S(2)}) collective-permute-start(bf16[256,1024]{1,0:T(8,128)(2,1)S(1)} %convolution_convert_fusion.8), channel_id=1, source_target_pairs={{0,1},{1,0},{2,3},{3,2},{4,5},{5,4},{6,7},{7,6},{8,9},{9,8},{10,11... | collective-permute-start | bytes 1572872 | tf_op jit(solution)/shard_map/ppermute | solution.py:252
  172.9 2.0 collective-permute-start.4
  175.0 5.5 %copy-start.11 = (bf16[256,2048]{1,0:T(8,128)(2,1)S(1)}, bf16[256,2048]{1,0:T(8,128)(2,1)}, u32[]{:S(2)}) copy-start(bf16[256,2048]{1,0:T(8,128)(2,1)} %copy-done.10) | copy-start | bytes 3145732
  175.0 5.5 %copy-start.19 = (bf16[256,1024]{1,0:T(8,128)(2,1)S(1)}, bf16[256,1024]{1,0:T(8,128)(2,1)}, u32[]{:S(2)}) copy-start(bf16[256,1024]{1,0:T(8,128)(2,1)} %param.19) | copy-start | bytes 1572868
  176.1 24.9 %all-to-all-start.3 = ((bf16[8,192,256]{2,1,0:T(8,128)(2,1)}), bf16[8,192,256]{2,1,0:T(8,128)(2,1)}, u32[]{:S(2)}, u32[]{:S(2)}) async-start(bf16[8,192,256]{2,1,0:T(8,128)(2,1)} %pad_maximum_fusion.1), calls=%async_computation.3 | async-start | bytes 1572864 | tf_op jit(solution)/shard_map/all_to_all | solution.py:224
  180.3 3.6 copy-start.3
  180.3 3.6 copy-start.30
  180.3 3.6 copy-start.34
  180.3 263.6 %all-reduce.3.cloned.1.call-start = ((), (), s32[]{:S(2)}) async-start(), calls=%async_computation.4 | async-start | bytes 25165824 | tf_op jit(solution)/shard_map/psum | solution.py:372
  180.6 3.3 copy-start.25
  183.9 3.5 copy-start.9
  187.4 14.8 %copy-start.5 = (bf16[256,1024]{1,0:T(8,128)(2,1)S(1)}, bf16[256,1024]{1,0:T(8,128)(2,1)}, u32[]{:S(2)}) copy-start(bf16[256,1024]{1,0:T(8,128)(2,1)} %copy-done.4) | copy-start | bytes 1572868
  206.6 1.2 copy-start.14
  207.8 1.2 copy-start.16
  209.0 1.2 copy-start.17
  210.2 2.1 copy-start.43
  210.2 13.8 %copy-start.7 = (bf16[256,1024]{1,0:T(8,128)(2,1)S(1)}, bf16[256,1024]{1,0:T(8,128)(2,1)}, u32[]{:S(2)}) copy-start(bf16[256,1024]{1,0:T(8,128)(2,1)} %param.18) | copy-start | bytes 1572868
  210.2 13.8 %copy-start.28 = (f32[1024]{0:T(1024)S(1)}, f32[1024]{0:T(1024)}, u32[]{:S(2)}) copy-start(f32[1024]{0:T(1024)} %param.22) | copy-start | bytes 12292
  210.2 13.8 %copy-start.32 = (f32[256]{0:T(256)S(1)}, f32[256]{0:T(256)}, u32[]{:S(2)}) copy-start(f32[256]{0:T(256)} %copy-done.31) | copy-start | bytes 3076
  210.2 13.8 %copy-start.38 = (f32[256]{0:T(256)S(1)}, f32[256]{0:T(256)}, u32[]{:S(2)}) copy-start(f32[256]{0:T(256)} %copy-done.37) | copy-start | bytes 3076
  210.3 13.8 %copy-start.42 = (f32[256]{0:T(256)S(1)}, f32[256]{0:T(256)}, u32[]{:S(2)}) copy-start(f32[256]{0:T(256)} %copy-done.41) | copy-start | bytes 3076
  210.3 14.5 %copy-start.35 = (f32[1024]{0:T(1024)S(1)}, f32[1024]{0:T(1024)}, u32[]{:S(2)}) copy-start(f32[1024]{0:T(1024)} %get-tuple-element.28) | copy-start | bytes 12292
  210.3 14.5 %copy-start.36 = (f32[1024]{0:T(1024)S(1)}, f32[1024]{0:T(1024)}, u32[]{:S(2)}) copy-start(f32[1024]{0:T(1024)} %get-tuple-element.34) | copy-start | bytes 12292
  210.3 14.5 %copy-start.39 = (f32[1024]{0:T(1024)S(1)}, f32[1024]{0:T(1024)}, u32[]{:S(2)}) copy-start(f32[1024]{0:T(1024)} %get-tuple-element.46) | copy-start | bytes 12292
  210.3 14.5 %copy-start.40 = (f32[1024]{0:T(1024)S(1)}, f32[1024]{0:T(1024)}, u32[]{:S(2)}) copy-start(f32[1024]{0:T(1024)} %get-tuple-element.54) | copy-start | bytes 12292
  210.8 13.2 %collective-permute-start.5 = (bf16[256,1024]{1,0:T(8,128)(2,1)S(1)}, bf16[256,1024]{1,0:T(8,128)(2,1)S(1)}, u32[]{:S(2)}, u32[]{:S(2)}) collective-permute-start(bf16[256,1024]{1,0:T(8,128)(2,1)S(1)} %fusion.6), channel_id=1, source_target_pairs={{0,1},{1,0},{2,3},{3,2},{4,5},{5,4},{6,7},{7,6},{8,9},{9,8},{10,11... | collective-permute-start | bytes 1572872 | tf_op jit(solution)/shard_map/ppermute | solution.py:252
  212.4 12.6 %collective-permute-start.10 = (f32[2048]{0:T(1024)S(1)}, f32[2048]{0:T(1024)S(1)}, u32[]{:S(2)}, u32[]{:S(2)}) collective-permute-start(f32[2048]{0:T(1024)S(1)} %copy-done.43), channel_id=1, source_target_pairs={{0,2},{2,0},{1,3},{3,1},{4,6},{6,4},{5,7},{7,5},{8,10},{10,8},{9,1... | collective-permute-start | bytes 24584 | tf_op jit(solution)/shard_map/ppermute | solution.py:220
  224.8 13.3 %collective-permute-start.6 = (f32[7,1024]{1,0:T(8,128)S(1)}, f32[7,1024]{1,0:T(8,128)S(1)}, u32[]{:S(2)}, u32[]{:S(2)}) collective-permute-start(f32[7,1024]{1,0:T(8,128)S(1)} %stack.31), channel_id=1, source_target_pairs={{0,2},{2,0},{1,3},{3,1},{4,6},{6,4},{5,7},{7,5},{8,10},{10,8},{9,1... | collective-permute-start | bytes 86024 | tf_op jit(solution)/shard_map/ppermute | solution.py:220
  224.9 3.7 collective-permute-start.11
  228.7 4.0 collective-permute-start.12
  232.7 4.9 %collective-permute-start.13 = (f32[2048]{0:T(1024)S(1)}, f32[2048]{0:T(1024)S(1)}, u32[]{:S(2)}, u32[]{:S(2)}) collective-permute-start(f32[2048]{0:T(1024)S(1)} %add.158), channel_id=1, source_target_pairs={{0,16},{4,20},{8,24},{12,28},{16,0},{20,4},{24,8},{28,12},{1,17},{... | collective-permute-start | bytes 24584 | tf_op jit(solution)/shard_map/ppermute | solution.py:261
  238.2 4.0 collective-permute-start.7
  242.2 4.8 %collective-permute-start.8 = (f32[7,1024]{1,0:T(8,128)S(1)}, f32[7,1024]{1,0:T(8,128)S(1)}, u32[]{:S(2)}, u32[]{:S(2)}) collective-permute-start(f32[7,1024]{1,0:T(8,128)S(1)} %add.153), channel_id=1, source_target_pairs={{0,8},{4,12},{8,0},{12,4},{16,24},{20,28},{24,16},{28,20},{1,9},{5... | collective-permute-start | bytes 86024 | tf_op jit(solution)/shard_map/ppermute | solution.py:261
  246.9 5.9 %collective-permute-start.9 = (f32[7,1024]{1,0:T(8,128)S(1)}, f32[7,1024]{1,0:T(8,128)S(1)}, u32[]{:S(2)}, u32[]{:S(2)}) collective-permute-start(f32[7,1024]{1,0:T(8,128)S(1)} %add.154), channel_id=1, source_target_pairs={{0,16},{4,20},{8,24},{12,28},{16,0},{20,4},{24,8},{28,12},{1,17},{... | collective-permute-start | bytes 86024 | tf_op jit(solution)/shard_map/ppermute | solution.py:261
  443.9 6.8 %copy-start.12 = (bf16[2048,1024]{1,0:T(8,128)(2,1)S(1)}, bf16[2048,1024]{1,0:T(8,128)(2,1)}, u32[]{:S(2)}) copy-start(bf16[2048,1024]{1,0:T(8,128)(2,1)} %get-tuple-element.42) | copy-start | bytes 12582916
  450.7 4.4 copy-start.23
  455.2 1.6 copy-start.22
  456.8 1.6 copy-start.21
  458.4 1.6 copy-start.20
  458.4 3.2 copy-start.1
  (1 other events, 1.0 us)
Sparse Core Ops, SparseCore 0:
  206.7 237.1 all-reduce.2

commit v2 on v1

--- a/solution.py
+++ b/solution.py
@@ -98,16 +98,14 @@
 
 def backward_kernel(
     crops,
-    step,
     query_ref,
     grad_ref,
     raw_ref,
     logsum_ref,
-    own,
-    other,
+    before_ref,
+    piece,
     dquery_ref,
-    own_ref,
-    other_ref,
+    sums_ref,
     keys,
     key_t,
     value_n,
@@ -117,36 +115,31 @@
 
     @pl.when(group == 0)
     def _():
-        load_keys((own, other), crops, keys, key_t, None, value_n)
+        load_keys((piece,), crops, keys, key_t, None, value_n)
         sums[...] = jnp.zeros_like(sums)
 
     query = masked_query(query_ref)
     grad = grad_ref[0]
     grad_wide = grad.astype(F32)
     delta = jnp.sum(grad_wide * raw_ref[0], axis=0, keepdims=True)
-    logsum = logsum_ref[0]
     scaled = query_ref[0, pl.ds(0, HD), :].astype(F32) * 0.125
     zero = jnp.zeros_like(scaled)
     query_side = jnp.concatenate([scaled, zero], axis=0).T.astype(BF16)
     grad_side = jnp.concatenate([zero, grad_wide], axis=0).T.astype(BF16)
-    dquery = jnp.zeros_like(scaled)
-    for start in range(0, keys.shape[0], step):
-        place = pl.ds(start, step)
-        probs = jnp.exp(product(keys[place, :], query) - logsum)
-        dprobs = product(value_n[place, :], grad)
-        dscores = (probs * (dprobs - delta)).astype(BF16)
-        sums[place, :] += product(dscores, query_side) + product(probs.astype(BF16), grad_side)
-        dquery += product(key_t[:, place], dscores)
-    dquery_ref[0] = (dquery * 0.125).astype(BF16)
+    probs = jnp.exp(product(keys[...], query) - logsum_ref[0])
+    dprobs = product(value_n[...], grad)
+    dscores = (probs * (dprobs - delta)).astype(BF16)
+    sums[...] += product(dscores, query_side) + product(probs.astype(BF16), grad_side)
+    dquery = product(key_t[...], dscores) * 0.125
+    if before_ref is not None:
+        dquery = before_ref[0] + dquery
+    dquery_ref[0] = dquery.astype(dquery_ref.dtype)
 
     @pl.when(group == pl.num_programs(0) - 1)
     def _():
-        start = 0
-        for target in (own_ref, other_ref):
-            chips, _, patches = target.shape
-            for chip in range(chips):
-                target[chip] = sums[pl.ds(start, patches), :].T.astype(target.dtype)
-                start += patches
+        chips, _, patches = sums_ref.shape
+        for chip in range(chips):
+            sums_ref[chip] = sums[pl.ds(chip * patches, patches), :].T.astype(sums_ref.dtype)
 
 
 def key_step(count):
@@ -180,30 +173,39 @@
         ],
         scratch_shapes=[pltpu.VMEM((count, 2 * HD), BF16), pltpu.VMEM((HD + 16, count), BF16)],
         compiler_params=pltpu.CompilerParams(vmem_limit_bytes=vmem_limit),
+        cost_estimate=pl.CostEstimate(
+            flops=groups * patches * count * 2 * 1024,
+            bytes_accessed=4 * 2**20,
+            transcendentals=groups * patches * count,
+        ),
         name="attention_forward",
     )(queries, own, other)
 
 
-def attention_backward(queries, grads, raw, logsum, own, other, crops):
+def backward_piece(queries, grads, raw, logsum, before, keys, index, pieces, crops, sums_type, last):
     groups, _, patches = queries.shape
-    count = 2 * own.shape[0] * own.shape[2]
-    sums_shape = (own.shape[0], 2 * HD, own.shape[2])
+    chips = keys.shape[0] // pieces
+    count = chips * keys.shape[2]
+    sums_shape = (chips, 2 * HD, keys.shape[2])
+    earlier = [] if before is None else [before]
+    body = functools.partial(backward_kernel, crops)
+    if before is None:
+        body = lambda *refs: backward_kernel(crops, *refs[:4], None, *refs[4:])
     return pl.pallas_call(
-        functools.partial(backward_kernel, crops, key_step(count)),
+        body,
         grid=(groups,),
         in_specs=[
             query_spec(payload_rows, patches),
             query_spec(HD, patches),
             query_spec(HD, patches),
             query_spec(1, patches),
-            whole_spec(own.shape),
-            whole_spec(other.shape),
-        ],
-        out_specs=[query_spec(HD, patches), whole_spec(sums_shape), whole_spec(sums_shape)],
+        ]
+        + [query_spec(HD, patches)] * len(earlier)
+        + [pl.BlockSpec((chips,) + keys.shape[1:], lambda group: (index, 0, 0))],
+        out_specs=[query_spec(HD, patches), whole_spec(sums_shape)],
         out_shape=[
-            jax.ShapeDtypeStruct((groups, HD, patches), BF16),
-            jax.ShapeDtypeStruct(sums_shape, F32),
-            jax.ShapeDtypeStruct(sums_shape, BF16),
+            jax.ShapeDtypeStruct((groups, HD, patches), BF16 if last else F32),
+            jax.ShapeDtypeStruct(sums_shape, sums_type),
         ],
         scratch_shapes=[
             pltpu.VMEM((count, 2 * HD), BF16),
@@ -212,8 +214,13 @@
             pltpu.VMEM((count, 2 * HD), F32),
         ],
         compiler_params=pltpu.CompilerParams(vmem_limit_bytes=vmem_limit),
+        cost_estimate=pl.CostEstimate(
+            flops=groups * patches * count * 2 * 2048,
+            bytes_accessed=4 * 2**20,
+            transcendentals=groups * patches * count,
+        ),
         name="attention_backward",
-    )(queries, grads, raw, logsum, own, other)
+    )(queries, grads, raw, logsum, *earlier, keys)
 
 
 def swap_cores(values):
@@ -246,11 +253,104 @@
     return moved.transpose(0, 2, 1, 3).reshape(heads * rows, patches)
 
 
+def ring_position():
+    chips, chip = lax.axis_size("chip"), lax.axis_index("chip")
+    return jnp.where(chip % 2 == 0, chip // 2, chips - 1 - chip // 2)
+
+
+def ring_pairs(direction):
+    chips = lax.axis_size("chip")
+    order = list(range(0, chips, 2)) + list(range(chips - 1, 0, -2))
+    return [(order[at], order[(at + direction) % chips]) for at in range(chips)]
+
+
+def ring_sum(partial, direction):
+    chips, place, pairs = lax.axis_size("chip"), ring_position(), ring_pairs(direction)
+    rows = partial.shape[0] // chips
+
+    def block(step):
+        index = lax.rem(place + (chips - direction * step) % chips, chips)
+        return lax.dynamic_slice_in_dim(partial, index * rows, rows, 0)
+
+    travel = block(1).astype(BF16)
+    for step in range(2, chips + 1):
+        travel = (lax.ppermute(travel, "chip", pairs).astype(F32) + block(step)).astype(BF16)
+    blocks = [travel]
+    for _ in range(chips - 1):
+        blocks.append(lax.ppermute(blocks[-1], "chip", pairs))
+    return blocks
+
+
+def assemble_kernel(cuts, _, *refs):
+    inputs, outputs = refs[: -len(cuts)], refs[-len(cuts) :]
+    for at, block in enumerate(inputs):
+
+        @pl.when(pl.program_id(0) == at)
+        def _(block=block):
+            for output, cut in zip(outputs, cuts):
+                output[...] = block[:, cut].astype(F32)
+
+
+def assemble(blocks, direction, axis, count=1):
+    chips, place, core = lax.axis_size("chip"), ring_position(), lax.axis_index("core")
+    steps = jnp.arange(chips, dtype=jnp.int32)
+    index = lax.rem(place + (chips - direction * steps) % chips, chips)
+    index = jnp.concatenate([index, index])
+    side = jnp.concatenate([jnp.full((chips,), core), jnp.full((chips,), 1 - core)])
+    if axis == 0:
+        order = jnp.stack([side * chips + index, jnp.zeros_like(index)])
+    else:
+        order = jnp.stack([index, side])
+    rows, columns = blocks[0].shape
+    columns //= count
+    shape = (2 * chips * rows, columns) if axis == 0 else (chips * rows, 2 * columns)
+    cuts = [slice(at * columns, at * columns + columns) for at in range(count)]
+    blocks = blocks + [swap_cores(block) for block in blocks]
+    if rows % 8 or columns % 128:
+        outputs = [jnp.zeros(shape, F32)] * count
+        for at, block in enumerate(blocks):
+            start = (order[0, at] * rows, order[1, at] * columns)
+            outputs = [
+                lax.dynamic_update_slice(output, block[:, cut].astype(F32), start)
+                for output, cut in zip(outputs, cuts)
+            ]
+        return outputs
+    return pl.pallas_call(
+        functools.partial(assemble_kernel, cuts),
+        grid_spec=pltpu.PrefetchScalarGridSpec(
+            num_scalar_prefetch=1,
+            grid=(2 * chips,),
+            in_specs=[pl.BlockSpec(blocks[0].shape, lambda at, order: (0, 0))] * (2 * chips),
+            out_specs=[pl.BlockSpec((rows, columns), lambda at, order: (order[0, at], order[1, at]))]
+            * count,
+        ),
+        out_shape=[jax.ShapeDtypeStruct(shape, F32)] * count,
+        compiler_params=pltpu.CompilerParams(vmem_limit_bytes=vmem_limit),
+        name="assemble",
+    )(order.astype(jnp.int32), *blocks)
+
+
+def core_half(values, axis, side):
+    size = values.shape[axis] // 2
+    return lax.dynamic_slice_in_dim(values, side * size, size, axis)
+
+
+def share_halves(values, axis):
+    core = lax.axis_index("core")
+    return core_half(values, axis, core), swap_cores(core_half(values, axis, 1 - core))
+
+
 def head_sum(values):
     low = values.astype(BF16)
     if lax.axis_size("head") == 2:
         return low.astype(F32) + lax.ppermute(low, "head", [(0, 1), (1, 0)]).astype(F32)
     return lax.psum(low, "head").astype(F32)
+
+
+def whole_head_sum(values):
+    if lax.axis_size("head") == 2:
+        return values + lax.ppermute(values, "head", [(0, 1), (1, 0)])
+    return lax.psum(values, "head")
 
 
 def band_sum(values):
@@ -319,20 +419,39 @@
     d_active = product(out_grad, down_weight, 1, 1)
     d_upper = gelu_back(d_active)[0].astype(BF16)
     d_mlp = head_sum(product(d_upper, up_weight, 1, 1))
-    mlp_out = head_sum(product(active_low, down_weight))
+    mlp_part, d_mlp = lax.optimization_barrier(
+        (product(active_low, down_weight).astype(BF16), d_mlp)
+    )
+    mlp_out = head_sum(mlp_part)
     block_output = (hidden + mlp_out + down_bias).astype(BF16)
     grad_out = out_grad.astype(F32)
-    ddown_weight = product(active_low, out_grad, 0, 0)
-    dup_weight = product(mlp_in, d_upper, 0, 0)
+    grad_far, mlp_in_far, attn_in_far = (swap_cores(v) for v in (out_grad, mlp_in, attn_in))
+    active_near, active_far = share_halves(active_low, 1)
+    upper_near, upper_far = share_halves(d_upper, 1)
+    ddown = ring_sum(product(active_near, out_grad, 0, 0) + product(active_far, grad_far, 0, 0), 1)
+    dup = ring_sum(product(mlp_in, upper_near, 0, 0) + product(mlp_in_far, upper_far, 0, 0), -1)
     d_hidden = grad_out + normalize_back(d_mlp * gain_mlp, unit_mlp, inverse_mlp)
     d_branch = d_hidden.astype(BF16)
-    doutput_weight = product(attn_out, d_branch)
+    out_near, out_far = share_halves(attn_out, 0)
+    doutput = ring_sum(product(out_near, d_branch) + product(out_far, swap_cores(d_branch)), -1)
     d_attn = product(output_weight, d_branch, 1, 1).astype(BF16)
     grads = scatter_queries(d_attn, heads, split)
-    dquery, own_sums, other_sums = attention_backward(
-        queries, grads, raw, logsum, own, other, crops
-    )
-    key_value = (own_sums + swap_cores(other_sums).astype(F32)).astype(BF16)
+    pieces = 2
+    dquery = None
+    far_sums, near_sums = [], []
+    for keys, sums, sums_type in ((other, far_sums, BF16), (own, near_sums, F32)):
+        for index in range(pieces):
+            last = keys is own and index == pieces - 1
+            dquery, piece = backward_piece(
+                queries, grads, raw, logsum, dquery, keys, index, pieces, crops, sums_type, last
+            )
+            sums.append(piece)
+    key_value = jnp.concatenate(
+        [
+            (near + swap_cores(far).astype(F32)).astype(BF16)
+            for near, far in zip(near_sums, far_sums)
+        ]
+    )
     if split == 1:
         moved = to_heads(jnp.concatenate([dquery, key_value], axis=1))
         dquery, dkey, dvalue = (
@@ -343,23 +462,36 @@
         moved = to_heads(key_value).reshape(heads, split, 2 * HD, rows).astype(F32)
         moved = jnp.sum(moved, axis=1).astype(BF16)
         dkey, dvalue = (moved[:, at * HD : at * HD + HD].reshape(width, rows) for at in range(2))
-    dquery_weight, dkey_weight, dvalue_weight = (
-        product(attn_in, grad, 0, 1) for grad in (dquery, dkey, dvalue)
-    )
-    d_in = head_sum(
+    d_part = (
         product(dquery, query_weight, 0, 1)
         + product(dkey, key_weight, 0, 1)
         + product(dvalue, value_weight, 0, 1)
     )
+    near, far = zip(*(share_halves(grad, 0) for grad in (dquery, dkey, dvalue)))
+    dquery_weight, dkey_weight, dvalue_weight = (
+        product(attn_in, one, 0, 1) + product(attn_in_far, two, 0, 1)
+        for one, two in zip(near, far)
+    )
+    dquery_key = ring_sum(jnp.concatenate([dquery_weight, dkey_weight], axis=1), 1)
+    dvalue_blocks = ring_sum(dvalue_weight, -1)
+    d_in = head_sum(d_part)
     input_grad = (d_hidden + normalize_back(d_in * gain_attn, unit_attn, inverse_attn)).astype(
         BF16
+    )
+    ends = band_sum(
+        whole_head_sum(
+            jnp.stack(
+                [
+                    jnp.sum(d_part * unit_attn, axis=0),
+                    jnp.sum(d_part, axis=0),
+                    jnp.sum(lead[:, None] * d_part, axis=0),
+                ]
+            )
+        )
     )
     small = band_sum(
         jnp.stack(
             [
-                jnp.sum(d_in * unit_attn, axis=0),
-                jnp.sum(d_in, axis=0),
-                jnp.sum(lead[:, None] * d_in, axis=0),
                 jnp.sum(d_hidden, axis=0),
                 jnp.sum(d_mlp * unit_mlp, axis=0),
                 jnp.sum(d_mlp, axis=0),
@@ -368,34 +500,28 @@
         )
     )
     dup_bias = band_sum(jnp.sum(d_upper.astype(F32), axis=0))
-    large = [
-        lax.psum(grad.astype(BF16), ("chip", "core")).astype(F32)
-        for grad in (
-            dquery_weight,
-            dkey_weight,
-            dvalue_weight,
-            doutput_weight,
-            dup_weight,
-            ddown_weight,
-        )
-    ]
+    (ddown_weight,) = assemble(ddown, 1, 0)
+    (dup_weight,) = assemble(dup, -1, 1)
+    (doutput_weight,) = assemble(doutput, -1, 0)
+    dquery_weight, dkey_weight = assemble(dquery_key, 1, 1, 2)
+    (dvalue_weight,) = assemble(dvalue_blocks, -1, 1)
     return (
         block_output,
         input_grad,
+        ends[0],
+        ends[1],
+        ends[2],
+        dquery_weight,
+        dkey_weight,
+        dvalue_weight,
+        doutput_weight,
         small[0],
         small[1],
         small[2],
-        large[0],
-        large[1],
-        large[2],
-        large[3],
+        dup_weight,
+        dup_bias,
+        ddown_weight,
         small[3],
-        small[4],
-        small[5],
-        large[4],
-        dup_bias,
-        large[5],
-        small[6],
     )
 
 

time: 469 us -> 482 us (1.028); the launches traced: 468 us -> 476 us
  waiting for transfers between devices: 268 us -> 144 us
  starting transfers between devices: 15 us -> 123 us
  Pallas kernels: 46.1 us -> 87.2 us
  blocking collectives: 55.4 us -> 41.3 us
  between operations: 14.8 us -> 2.2 us
  other arithmetic: 31.9 us -> 42.4 us
    psum x1 -> x0, waiting for transfers between devices: 190 us -> none  [local(): lax.psum(grad.astype(BF16), ('chip', 'core')).astype(F32)]
    ppermute x0 -> x71, waiting for transfers between devices: none -> 101 us  [the longest x35 70 us: ring_sum(): lax.ppermute(travel, 'chip', pairs).astype(F32) + block(step)]
    ppermute x0 -> x71, starting transfers between devices: none -> 90.5 us  [the longest x35 50.4 us: ring_sum(): lax.ppermute(travel, 'chip', pairs).astype(F32) + block(step)]
    pallas_call x1 -> x9, Pallas kernels: 22.6 us -> 63.7 us  [the longest x5 35.1 us: assemble(): pl.pallas_call(functools.partial(assemble_kernel, cuts), grid_spec=pltpu....]
    ppermute x4, waiting for transfers between devices: 39.8 us -> 25.1 us  [head_sum(): lax.ppermute(low, 'head', [(0, 1), (1, 0)]).astype(F32)]
    all_to_all x3 -> x2, blocking collectives: 55.4 us -> 41.3 us  [to_heads(): return lax.all_to_all(blocks, 'chip', 0, 0, tiled=True)]
    all_to_all x1 -> x2, waiting for transfers between devices: 12.2 us -> 0.01 us  [to_heads(): return lax.all_to_all(blocks, 'chip', 0, 0, tiled=True)]
    ppermute x4 -> x56, starting transfers between devices: 0.15 us -> 8.02 us  [swap_cores(): return lax.ppermute(values, 'core', [(0, 1), (1, 0)])]
  transfers between devices with their start and end apart: 16 -> 142, of which waited for: 14 -> 43; matrix products, arithmetic and copies ran while one was open for 3% -> 14% of each run, Pallas kernels for 0% -> 12%
where the time goes in v2:
time: 482 us; the launch traced here: 476 us
  waiting for transfers between devices  144 us (30%)
  starting transfers between devices  123 us (26%)
  Pallas kernels  87.2 us (18%)
  other arithmetic  42.4 us (9%)
  blocking collectives  41.3 us (9%)
  matrix products  28.2 us (6%)
  local copies, waits for them, and re-layouts  7.89 us (2%)
    ppermute x35, waiting for transfers between devices, ring_sum(): lax.ppermute(travel, 'chip', pairs).astype(F32) + block(step)  70 us
    ppermute x35, starting transfers between devices, ring_sum(): lax.ppermute(travel, 'chip', pairs).astype(F32) + block(step)  50.4 us
    all_to_all x2, blocking collectives, to_heads(): return lax.all_to_all(blocks, 'chip', 0, 0, tiled=True)  41.3 us
    ppermute x35, starting transfers between devices, ring_sum(): blocks.append(lax.ppermute(blocks[-1], 'chip', pairs))  39.5 us
    pallas_call x5, Pallas kernels, assemble(): pl.pallas_call(functools.partial(assemble_kernel, cuts), grid_spec=pltpu....  35.1 us
    ppermute x35, waiting for transfers between devices, ring_sum(): blocks.append(lax.ppermute(blocks[-1], 'chip', pairs))  31.3 us
    pallas_call x4, Pallas kernels, backward_piece(): pl.pallas_call(body, grid=(groups,), in_specs=[query_spec(payload_rows, p...  28.6 us
    dot_general x24, matrix products, product(): lax.dot_general(first, second, (((first_axis,), (second_axis,)), ((), ())...  28.2 us
  transfers between devices with their start and end apart: 142, of which 43 were waited for; matrix products, arithmetic and copies ran while one was open for 14% of the time, Pallas kernels for 12%

profile of v2, /device:TPU:0, one launch (start us, length us, event | category | flops | bytes accessed | tf_op | source)
XLA Modules:
  0.0 476.4 jit_solution(2570640408035250614)
XLA Ops:
  8.9 29.3 %all_to_all.20.query_ref.own.refs_0_.piece = bf16[8,208,256]{2,1,0:T(8,128)(2,1)S(1)} all-to-all(bf16[8,208,256]{2,1,0:T(8,128)(2,1)S(1)} %pad_maximum_fusion), channel_id=1, replica_groups=mesh['chip'=8,'core'=2,'head'=2] {'chip'}, dimensions={0} | all-to-all | bytes 1703936 | tf_op jit(solution)/shard_map/all_to_all | solution.py:231
  38.2 2.4 collective-permute-done.other.refs_4_.piece
  40.5 23.5 %attention_forward.1 = (f32[8,64,256]{2,1,0:T(8,128)S(1)}, bf16[8,64,256]{2,1,0:T(8,128)(2,1)S(1)}, f32[8,1,256]{2,1,0:T(1,128)S(1)}) custom-call(bf16[8,208,256]{2,1,0:T(8,128)(2,1)S(1)} %all_to_all.20.query_ref.own.refs_0_.piece, bf16[8,208,256]{2,1,0:T(8,128)(2,1)S(1)} %all_to_all.20.query_ref.own.refs_0_.piece, ...), custom_call_target="tpu_custom_call" | custom-call | flops 17179869184 | bytes 4194304 | tf_op jit(solution)/shard_map/attention_forward/pallas_call | solution.py:160
  64.1 12.0 %all_to_all.21 = bf16[8,64,256]{2,1,0:T(8,128)(2,1)S(1)} all-to-all(bf16[8,64,256]{2,1,0:T(8,128)(2,1)S(1)} %get-tuple-element.31), channel_id=1, replica_groups=mesh['chip'=8,'core'=2,'head'=2] {'chip'}, dimensions={0} | all-to-all | bytes 524288 | tf_op jit(solution)/shard_map/all_to_all | solution.py:231
  80.0 9.9 %collective-permute-done.1 = bf16[256,1024]{1,0:T(8,128)(2,1)} collective-permute-done((bf16[256,1024]{1,0:T(8,128)(2,1)}, bf16[256,1024]{1,0:T(8,128)(2,1)}, u32[]{:S(2)}, u32[]{:S(2)}) %collective-permute-start.1) | collective-permute-done | bytes 524320 | tf_op jit(solution)/shard_map/ppermute | solution.py:346
  94.3 7.0 %convert_reduce_fusion = (f32[2048]{0:T(1024)S(1)}, bf16[256,2048]{1,0:T(8,128)(2,1)S(1)}, f32[256,2048]{1,0:T(8,128)S(1)}) fusion(f32[256,2048]{1,0:T(8,128)S(1)} %convolution_add_fusion, bf16[256,1024]{1,0:T(8,128)(2,1)} %param.19, bf16[2048,1024]{1,0:T(8,128)(2,1)S(1)} %copy-done.34), kind=kOutput, calls=%fused_computation.21 | convolution fusion | flops 1112537088 | bytes 9969664 | tf_op jit(solution)/shard_map/dot_general | solution.py:35
  115.4 7.3 %collective-permute-done.2 = bf16[256,1024]{1,0:T(8,128)(2,1)S(1)} collective-permute-done((bf16[256,1024]{1,0:T(8,128)(2,1)S(1)}, bf16[256,1024]{1,0:T(8,128)(2,1)S(1)}, u32[]{:S(2)}, u32[]{:S(2)}) %collective-permute-start.2) | collective-permute-done | bytes 524320 | tf_op jit(solution)/shard_map/ppermute | solution.py:346
  128.6 7.9 %collective-permute-done.3 = bf16[256,1024]{1,0:T(8,128)(2,1)S(1)} collective-permute-done((bf16[256,1024]{1,0:T(8,128)(2,1)S(1)}, bf16[256,1024]{1,0:T(8,128)(2,1)S(1)}, u32[]{:S(2)}, u32[]{:S(2)}) %collective-permute-start.3) | collective-permute-done | bytes 524320 | tf_op jit(solution)/shard_map/ppermute | solution.py:346
  136.5 3.2 fusion.80
  141.5 2.2 fusion.15
  143.7 2.3 fusion.55
  147.8 4.7 all-to-all-start.2
  153.7 2.1 collective-permute-start.120
  157.7 6.7 %collective-permute-done.120 = bf16[128,1024]{1,0:T(8,128)(2,1)S(1)} collective-permute-done((bf16[128,1024]{1,0:T(8,128)(2,1)S(1)}, bf16[128,1024]{1,0:T(8,128)(2,1)S(1)}, u32[]{:S(2)}, u32[]{:S(2)}) %collective-permute-start.120) | collective-permute-done | bytes 262176 | tf_op jit(solution)/shard_map/ppermute | solution.py:277
  166.3 2.0 collective-permute-start.121
  170.1 7.1 %attention_backward.4 = (f32[8,64,256]{2,1,0:T(8,128)S(1)}, bf16[4,128,256]{2,1,0:T(8,128)(2,1)S(1)}) custom-call(bf16[8,208,256]{2,1,0:T(8,128)(2,1)S(1)} %all_to_all.20.query_ref.own.refs_0_.piece, bf16[8,64,256]{2,1,0:T(8,128)(2,1)S(1)} %all-to-all-done.2.refs_1_.grad_ref, f32[8,64,256]{2,1,0:T(8,128)S(1)} %get-tuple-element.34.refs_2_.raw_ref, ...), custom_call_target="tpu_custom_call" | custom-call | flops 8589934592 | bytes 4194304 | tf_op jit(solution)/shard_map/attention_backward/pallas_call | solution.py:194
  177.2 7.1 %attention_backward.5 = (f32[8,64,256]{2,1,0:T(8,128)S(1)}, bf16[4,128,256]{2,1,0:T(8,128)(2,1)S(1)}) custom-call(bf16[8,208,256]{2,1,0:T(8,128)(2,1)S(1)} %all_to_all.20.query_ref.own.refs_0_.piece, bf16[8,64,256]{2,1,0:T(8,128)(2,1)S(1)} %all-to-all-done.2.refs_1_.grad_ref, f32[8,64,256]{2,1,0:T(8,128)S(1)} %get-tuple-element.34.refs_2_.raw_ref, ...), custom_call_target="tpu_custom_call" | custom-call | flops 8589934592 | bytes 4194304 | tf_op jit(solution)/shard_map/attention_backward/pallas_call | solution.py:194
  184.3 7.2 %attention_backward.6 = (f32[8,64,256]{2,1,0:T(8,128)S(1)}, f32[4,128,256]{2,1,0:T(8,128)S(1)}) custom-call(bf16[8,208,256]{2,1,0:T(8,128)(2,1)S(1)} %all_to_all.20.query_ref.own.refs_0_.piece, bf16[8,64,256]{2,1,0:T(8,128)(2,1)S(1)} %all-to-all-done.2.refs_1_.grad_ref, f32[8,64,256]{2,1,0:T(8,128)S(1)} %get-tuple-element.34.refs_2_.raw_ref, ...), custom_call_target="tpu_custom_call" | custom-call | flops 8589934592 | bytes 4194304 | tf_op jit(solution)/shard_map/attention_backward/pallas_call | solution.py:194
  193.5 2.9 collective-permute-start.62
  196.4 7.2 %attention_backward.7 = (bf16[8,64,256]{2,1,0:T(8,128)(2,1)S(1)}, f32[4,128,256]{2,1,0:T(8,128)S(1)}) custom-call(bf16[8,208,256]{2,1,0:T(8,128)(2,1)S(1)} %all_to_all.20.query_ref.own.refs_0_.piece, bf16[8,64,256]{2,1,0:T(8,128)(2,1)S(1)} %all-to-all-done.2.refs_1_.grad_ref, f32[8,64,256]{2,1,0:T(8,128)S(1)} %get-tuple-element.34.refs_2_.raw_ref, ...), custom_call_target="tpu_custom_call" | custom-call | flops 8589934592 | bytes 4194304 | tf_op jit(solution)/shard_map/attention_backward/pallas_call | solution.py:194
  203.7 2.1 collective-permute-start.63
  208.3 2.1 collective-permute-start.64
  212.9 2.1 collective-permute-start.94
  215.0 2.5 collective-permute-start.65
  217.6 4.7 collective-permute-done.65
  222.3 2.1 collective-permute-start.66
  225.3 4.3 all-to-all-start.3
  230.6 1.9 collective-permute-start.67
  233.8 7.3 %collective-permute-done.67 = bf16[32,1024]{1,0:T(8,128)(2,1)S(1)} collective-permute-done((bf16[32,1024]{1,0:T(8,128)(2,1)S(1)}, bf16[32,1024]{1,0:T(8,128)(2,1)S(1)}, u32[]{:S(2)}, u32[]{:S(2)}) %collective-permute-start.67) | collective-permute-done | bytes 65568 | tf_op jit(solution)/shard_map/ppermute | solution.py:277
  242.0 3.5 collective-permute-start.68
  246.6 5.6 %collective-permute-start.95 = (bf16[128,1024]{1,0:T(8,128)(2,1)S(1)}, bf16[128,1024]{1,0:T(8,128)(2,1)S(1)}, u32[]{:S(2)}, u32[]{:S(2)}) collective-permute-start(bf16[128,1024]{1,0:T(8,128)(2,1)S(1)} %add_convert_fusion.12), channel_id=1, source_target_pairs={{0,4},{8,0},{16,8},{24,16},{28,24},{20,28},{12,20},{4,12},{1,5},{9... | collective-permute-start | bytes 786440 | tf_op jit(solution)/shard_map/ppermute | solution.py:277
  252.3 2.4 collective-permute-done.68
  257.8 2.1 collective-permute-done.69.refs_1_
  267.0 2.4 collective-permute-start.96
  274.4 3.0 collective-permute-done.114
  281.0 2.0 collective-permute-start.73
  292.3 2.9 collective-permute-done.38
  298.1 2.9 collective-permute-done.39
  302.1 3.3 collective-permute-done.40
  305.5 4.9 %collective-permute-done.15 = bf16[128,512]{1,0:T(8,128)(2,1)S(1)} collective-permute-done((bf16[128,512]{1,0:T(8,128)(2,1)S(1)}, bf16[128,512]{1,0:T(8,128)(2,1)S(1)}, u32[]{:S(2)}, u32[]{:S(2)}) %collective-permute-start.15) | collective-permute-done | bytes 131104 | tf_op jit(solution)/shard_map/ppermute | solution.py:277
  311.4 3.3 collective-permute-done.41
  314.8 2.0 collective-permute-start.74
  316.8 2.8 collective-permute-done.16
  321.3 2.6 collective-permute-done.42
  325.5 2.6 collective-permute-done.75.refs_7_
  331.2 3.2 collective-permute-done.17
  335.4 4.3 collective-permute-done.43
  343.7 2.4 collective-permute-done.18
  346.7 3.7 collective-permute-done.126.refs_2_
  354.3 6.0 %collective-permute-done.19 = bf16[128,512]{1,0:T(8,128)(2,1)S(1)} collective-permute-done((bf16[128,512]{1,0:T(8,128)(2,1)S(1)}, bf16[128,512]{1,0:T(8,128)(2,1)S(1)}, u32[]{:S(2)}, u32[]{:S(2)}) %collective-permute-start.19) | collective-permute-done | bytes 131104 | tf_op jit(solution)/shard_map/ppermute | solution.py:277
  364.2 7.6 %collective-permute-done.20 = bf16[128,512]{1,0:T(8,128)(2,1)S(1)} collective-permute-done((bf16[128,512]{1,0:T(8,128)(2,1)S(1)}, bf16[128,512]{1,0:T(8,128)(2,1)S(1)}, u32[]{:S(2)}, u32[]{:S(2)}) %collective-permute-start.20) | collective-permute-done | bytes 131104 | tf_op jit(solution)/shard_map/ppermute | solution.py:277
  378.3 4.8 %collective-permute-done.9 = f32[3,1024]{1,0:T(4,128)S(1)} collective-permute-done((f32[3,1024]{1,0:T(4,128)S(1)}, f32[3,1024]{1,0:T(4,128)S(1)}, u32[]{:S(2)}, u32[]{:S(2)}) %collective-permute-start.9) | collective-permute-done | bytes 12320 | tf_op jit(solution)/shard_map/ppermute | solution.py:361
  385.4 2.0 collective-permute-done.45.refs_1_
  389.3 2.5 collective-permute-done.10
  391.8 2.5 collective-permute-start.22
  395.0 4.0 collective-permute-done.11
  400.4 3.1 collective-permute-done.47.refs_3_
  406.1 6.8 %collective-permute-done.48.refs_4_ = bf16[128,256]{1,0:T(8,128)(2,1)S(1)} collective-permute-done((bf16[128,256]{1,0:T(8,128)(2,1)S(1)}, bf16[128,256]{1,0:T(8,128)(2,1)S(1)}, u32[]{:S(2)}, u32[]{:S(2)}) %collective-permute-start.48) | collective-permute-done | bytes 65568 | tf_op jit(solution)/shard_map/ppermute | solution.py:280
  424.2 6.4 %assemble.7 = f32[512,1024]{1,0:T(8,128)} custom-call(s32[2,16]{1,0:T(2,128)S(1)} %stack.68._, bf16[32,1024]{1,0:T(8,128)(2,1)S(1)} %add_convert_fusion.19.refs_0_, bf16[32,1024]{1,0:T(8,128)(2,1)S(1)} %collective-permute-done.69.refs_1_, bf16[32,1024]{1,0:T(8,128)(2,1)S(1)} %collective-permute-done.70.refs_2_, ...), custom_call_target="tpu_custom_call" | custom-call | tf_op jit(solution)/shard_map/assemble/pallas_call | solution.py:318
  433.3 3.6 collective-permute-done.26.refs_5_
  447.4 6.4 %assemble.6 = f32[1024,512]{1,0:T(8,128)} custom-call(s32[2,16]{1,0:T(2,128)S(1)} %get-tuple-element.81._, bf16[128,256]{1,0:T(8,128)(2,1)S(1)} %add_convert_fusion.26.refs_0_, bf16[128,256]{1,0:T(8,128)(2,1)S(1)} %collective-permute-done.45.refs_1_, bf16[128,256]{1,0:T(8,128)(2,1)S(1)} %collective-permute-done.46.refs_2_, ...), custom_call_target="tpu_custom_call" | custom-call | tf_op jit(solution)/shard_map/assemble/pallas_call | solution.py:318
  453.8 7.7 %assemble.8 = f32[1024,2048]{1,0:T(8,128)} custom-call(s32[2,16]{1,0:T(2,128)S(1)} %get-tuple-element.81._, bf16[128,1024]{1,0:T(8,128)(2,1)S(1)} %add_convert_fusion.10.refs_0_, bf16[128,1024]{1,0:T(8,128)(2,1)S(1)} %collective-permute-done.97.refs_1_, bf16[128,1024]{1,0:T(8,128)(2,1)S(1)} %collective-permute-done.98.refs_2_, ...), custom_call_target="tpu_custom_call" | custom-call | tf_op jit(solution)/shard_map/assemble/pallas_call | solution.py:318
  461.6 7.7 %assemble.9 = f32[2048,1024]{1,0:T(8,128)} custom-call(s32[2,16]{1,0:T(2,128)S(1)} %stack.75._, bf16[128,1024]{1,0:T(8,128)(2,1)S(1)} %add_convert_fusion.3.refs_0_, bf16[128,1024]{1,0:T(8,128)(2,1)S(1)} %collective-permute-done.125.refs_1_, bf16[128,1024]{1,0:T(8,128)(2,1)S(1)} %collective-permute-done.126.refs_2_, ...), custom_call_target="tpu_custom_call" | custom-call | tf_op jit(solution)/shard_map/assemble/pallas_call | solution.py:318
  469.3 6.9 %assemble.5 = (f32[1024,512]{1,0:T(8,128)}, f32[1024,512]{1,0:T(8,128)}) custom-call(s32[2,16]{1,0:T(2,128)S(1)} %get-tuple-element.82._, bf16[128,512]{1,0:T(8,128)(2,1)S(1)} %fusion.34.refs_0_, bf16[128,512]{1,0:T(8,128)(2,1)S(1)} %collective-permute-done.22.refs_1_, bf16[128,512]{1,0:T(8,128)(2,1)S(1)} %collective-permute-done.23.refs_2_, ...), custom_call_target="tpu_custom_call" | custom-call | tf_op jit(solution)/shard_map/assemble/pallas_call | solution.py:318
  (432 shorter events, 151.4 us)
Async XLA Ops:
  77.3 12.5 %collective-permute-start.1 = (bf16[256,1024]{1,0:T(8,128)(2,1)}, bf16[256,1024]{1,0:T(8,128)(2,1)}, u32[]{:S(2)}, u32[]{:S(2)}) collective-permute-start(bf16[256,1024]{1,0:T(8,128)(2,1)} %convolution_convert_fusion), channel_id=1, source_target_pairs={{0,1},{1,0},{2,3},{3,2},{4,5},{5,4},{6,7},{7,6},{8,9},{9,8},{10,11... | collective-permute-start | bytes 1572872 | tf_op jit(solution)/shard_map/ppermute | solution.py:346
  78.8 29.6 %collective-permute-start.117 = (bf16[256,1024]{1,0:T(8,128)(2,1)}, bf16[256,1024]{1,0:T(8,128)(2,1)}, u32[]{:S(2)}, u32[]{:S(2)}) collective-permute-start(bf16[256,1024]{1,0:T(8,128)(2,1)} %param.19), channel_id=1, source_target_pairs={{0,2},{2,0},{1,3},{3,1},{4,6},{6,4},{5,7},{7,5},{8,10},{10,8},{9,1... | collective-permute-start | bytes 1572872 | tf_op jit(solution)/shard_map/ppermute | solution.py:227
  79.5 112.0 %collective-permute-start.60 = (bf16[256,256]{1,0:T(8,128)(2,1)}, bf16[256,256]{1,0:T(8,128)(2,1)}, u32[]{:S(2)}, u32[]{:S(2)}) collective-permute-start(bf16[256,256]{1,0:T(8,128)(2,1)} %constant_dynamic-slice_fusion.2), channel_id=1, source_target_pairs={{0,2},{2,0},{1,3},{3,1},{4,6},{6,4},{5,7},{7,5},{8,10},{10,8},{9,1... | collective-permute-start | bytes 393224 | tf_op jit(solution)/shard_map/ppermute | solution.py:227
  92.1 21.6 %collective-permute-start.88 = (bf16[256,1024]{1,0:T(8,128)(2,1)S(1)}, bf16[256,1024]{1,0:T(8,128)(2,1)S(1)}, u32[]{:S(2)}, u32[]{:S(2)}) collective-permute-start(bf16[256,1024]{1,0:T(8,128)(2,1)S(1)} %add_convert_fusion.2), channel_id=1, source_target_pairs={{0,2},{2,0},{1,3},{3,1},{4,6},{6,4},{5,7},{7,5},{8,10},{10,8},{9,1... | collective-permute-start | bytes 1572872 | tf_op jit(solution)/shard_map/ppermute | solution.py:227
  108.5 14.3 %collective-permute-start.2 = (bf16[256,1024]{1,0:T(8,128)(2,1)S(1)}, bf16[256,1024]{1,0:T(8,128)(2,1)S(1)}, u32[]{:S(2)}, u32[]{:S(2)}) collective-permute-start(bf16[256,1024]{1,0:T(8,128)(2,1)S(1)} %convolution_convert_fusion.1), channel_id=1, source_target_pairs={{0,1},{1,0},{2,3},{3,2},{4,5},{5,4},{6,7},{7,6},{8,9},{9,8},{10,11... | collective-permute-start | bytes 1572872 | tf_op jit(solution)/shard_map/ppermute | solution.py:346
  109.9 163.1 %collective-permute-start.113 = (f32[2048]{0:T(1024)}, f32[2048]{0:T(1024)}, u32[]{:S(2)}, u32[]{:S(2)}) collective-permute-start(f32[2048]{0:T(1024)} %add.557), channel_id=1, source_target_pairs={{0,4},{4,0},{8,12},{12,8},{16,20},{20,16},{24,28},{28,24},{1,5},{5... | collective-permute-start | bytes 24584 | tf_op jit(solution)/shard_map/ppermute | solution.py:361
  112.4 12.6 %collective-permute-start.118 = (bf16[128,1024]{1,0:T(8,128)(2,1)S(1)}, bf16[128,1024]{1,0:T(8,128)(2,1)S(1)}, u32[]{:S(2)}, u32[]{:S(2)}) collective-permute-start(bf16[128,1024]{1,0:T(8,128)(2,1)S(1)} %dynamic-slice_convert_fusion), channel_id=1, source_target_pairs={{0,8},{8,16},{16,24},{24,28},{28,20},{20,12},{12,4},{4,0},{1,9},{9... | collective-permute-start | bytes 786440 | tf_op jit(solution)/shard_map/ppermute | solution.py:277
  114.5 11.8 %collective-permute-start.90 = (bf16[128,1024]{1,0:T(8,128)(2,1)S(1)}, bf16[128,1024]{1,0:T(8,128)(2,1)S(1)}, u32[]{:S(2)}, u32[]{:S(2)}) collective-permute-start(bf16[128,1024]{1,0:T(8,128)(2,1)S(1)} %dynamic-slice_convert_fusion.1), channel_id=1, source_target_pairs={{0,4},{8,0},{16,8},{24,16},{28,24},{20,28},{12,20},{4,12},{1,5},{9... | collective-permute-start | bytes 786440 | tf_op jit(solution)/shard_map/ppermute | solution.py:277
  122.9 13.6 %collective-permute-start.3 = (bf16[256,1024]{1,0:T(8,128)(2,1)S(1)}, bf16[256,1024]{1,0:T(8,128)(2,1)S(1)}, u32[]{:S(2)}, u32[]{:S(2)}) collective-permute-start(bf16[256,1024]{1,0:T(8,128)(2,1)S(1)} %convolution_convert_fusion.2), channel_id=1, source_target_pairs={{0,1},{1,0},{2,3},{3,2},{4,5},{5,4},{6,7},{7,6},{8,9},{9,8},{10,11... | collective-permute-start | bytes 1572872 | tf_op jit(solution)/shard_map/ppermute | solution.py:346
  125.8 26.8 %collective-permute-start.119 = (bf16[128,1024]{1,0:T(8,128)(2,1)}, bf16[128,1024]{1,0:T(8,128)(2,1)}, u32[]{:S(2)}, u32[]{:S(2)}) collective-permute-start(bf16[128,1024]{1,0:T(8,128)(2,1)} %add_convert_fusion.9), channel_id=1, source_target_pairs={{0,8},{8,16},{16,24},{24,28},{28,20},{20,12},{12,4},{4,0},{1,9},{9... | collective-permute-start | bytes 786440 | tf_op jit(solution)/shard_map/ppermute | solution.py:277
  127.1 28.8 %collective-permute-start.91 = (bf16[128,1024]{1,0:T(8,128)(2,1)}, bf16[128,1024]{1,0:T(8,128)(2,1)}, u32[]{:S(2)}, u32[]{:S(2)}) collective-permute-start(bf16[128,1024]{1,0:T(8,128)(2,1)} %add_convert_fusion.16), channel_id=1, source_target_pairs={{0,4},{8,0},{16,8},{24,16},{28,24},{20,28},{12,20},{4,12},{1,5},{9... | collective-permute-start | bytes 786440 | tf_op jit(solution)/shard_map/ppermute | solution.py:277
  141.5 50.6 %collective-permute-start.61 = (bf16[256,1024]{1,0:T(8,128)(2,1)}, bf16[256,1024]{1,0:T(8,128)(2,1)}, u32[]{:S(2)}, u32[]{:S(2)}) collective-permute-start(bf16[256,1024]{1,0:T(8,128)(2,1)} %convert_element_type.358), channel_id=1, source_target_pairs={{0,2},{2,0},{1,3},{3,1},{4,6},{6,4},{5,7},{7,5},{8,10},{10,8},{9,1... | collective-permute-start | bytes 1572872 | tf_op jit(solution)/shard_map/ppermute | solution.py:227
  147.8 22.2 %all-to-all-start.2 = ((bf16[8,64,256]{2,1,0:T(8,128)(2,1)}), bf16[8,64,256]{2,1,0:T(8,128)(2,1)S(1)}, u32[]{:S(2)}, u32[]{:S(2)}) async-start(bf16[8,64,256]{2,1,0:T(8,128)(2,1)} %bitcast.94), calls=%async_computation.2 | async-start | bytes 524288 | tf_op jit(solution)/shard_map/all_to_all | solution.py:231
  153.7 10.6 %collective-permute-start.120 = (bf16[128,1024]{1,0:T(8,128)(2,1)S(1)}, bf16[128,1024]{1,0:T(8,128)(2,1)S(1)}, u32[]{:S(2)}, u32[]{:S(2)}) collective-permute-start(bf16[128,1024]{1,0:T(8,128)(2,1)S(1)} %add_convert_fusion.8), channel_id=1, source_target_pairs={{0,8},{8,16},{16,24},{24,28},{28,20},{20,12},{12,4},{4,0},{1,9},{9... | collective-permute-start | bytes 786440 | tf_op jit(solution)/shard_map/ppermute | solution.py:277
  164.4 91.4 %collective-permute-start.84 = (f32[4,1024]{1,0:T(4,128)}, f32[4,1024]{1,0:T(4,128)}, u32[]{:S(2)}, u32[]{:S(2)}) collective-permute-start(f32[4,1024]{1,0:T(4,128)} %pad_maximum_fusion.2), channel_id=1, source_target_pairs={{0,2},{2,0},{1,3},{3,1},{4,6},{6,4},{5,7},{7,5},{8,10},{10,8},{9,1... | collective-permute-start | bytes 49160 | tf_op jit(solution)/shard_map/ppermute | solution.py:227
  166.3 37.4 %collective-permute-start.121 = (bf16[128,1024]{1,0:T(8,128)(2,1)}, bf16[128,1024]{1,0:T(8,128)(2,1)}, u32[]{:S(2)}, u32[]{:S(2)}) collective-permute-start(bf16[128,1024]{1,0:T(8,128)(2,1)} %add_convert_fusion.7), channel_id=1, source_target_pairs={{0,8},{8,16},{16,24},{24,28},{28,20},{20,12},{12,4},{4,0},{1,9},{9... | collective-permute-start | bytes 786440 | tf_op jit(solution)/shard_map/ppermute | solution.py:277
  191.5 16.7 %collective-permute-start.93 = (bf16[128,1024]{1,0:T(8,128)(2,1)S(1)}, bf16[128,1024]{1,0:T(8,128)(2,1)S(1)}, u32[]{:S(2)}, u32[]{:S(2)}) collective-permute-start(bf16[128,1024]{1,0:T(8,128)(2,1)S(1)} %copy-done.16), channel_id=1, source_target_pairs={{0,4},{8,0},{16,8},{24,16},{28,24},{20,28},{12,20},{4,12},{1,5},{9... | collective-permute-start | bytes 786440 | tf_op jit(solution)/shard_map/ppermute | solution.py:277
  193.5 10.0 %collective-permute-start.62 = (bf16[32,1024]{1,0:T(8,128)(2,1)S(1)}, bf16[32,1024]{1,0:T(8,128)(2,1)S(1)}, u32[]{:S(2)}, u32[]{:S(2)}) collective-permute-start(bf16[32,1024]{1,0:T(8,128)(2,1)S(1)} %dynamic-slice_convert_fusion.2), channel_id=1, source_target_pairs={{0,4},{8,0},{16,8},{24,16},{28,24},{20,28},{12,20},{4,12},{1,5},{9... | collective-permute-start | bytes 196616 | tf_op jit(solution)/shard_map/ppermute | solution.py:277
  212.8 19.7 %collective-permute-start.122 = (bf16[128,1024]{1,0:T(8,128)(2,1)S(1)}, bf16[128,1024]{1,0:T(8,128)(2,1)S(1)}, u32[]{:S(2)}, u32[]{:S(2)}) collective-permute-start(bf16[128,1024]{1,0:T(8,128)(2,1)S(1)} %add_convert_fusion.6), channel_id=1, source_target_pairs={{0,8},{8,16},{16,24},{24,28},{28,20},{20,12},{12,4},{4,0},{1,9},{9... | collective-permute-start | bytes 786440 | tf_op jit(solution)/shard_map/ppermute | solution.py:277
  212.9 32.7 %collective-permute-start.94 = (bf16[128,1024]{1,0:T(8,128)(2,1)S(1)}, bf16[128,1024]{1,0:T(8,128)(2,1)S(1)}, u32[]{:S(2)}, u32[]{:S(2)}) collective-permute-start(bf16[128,1024]{1,0:T(8,128)(2,1)S(1)} %add_convert_fusion.13), channel_id=1, source_target_pairs={{0,4},{8,0},{16,8},{24,16},{28,24},{20,28},{12,20},{4,12},{1,5},{9... | collective-permute-start | bytes 786440 | tf_op jit(solution)/shard_map/ppermute | solution.py:277
  225.3 60.0 %all-to-all-start.3 = ((bf16[8,192,256]{2,1,0:T(8,128)(2,1)}), bf16[8,192,256]{2,1,0:T(8,128)(2,1)}, u32[]{:S(2)}, u32[]{:S(2)}) async-start(bf16[8,192,256]{2,1,0:T(8,128)(2,1)} %maximum_maximum_fusion), calls=%async_computation.3 | async-start | bytes 1572864 | tf_op jit(solution)/shard_map/all_to_all | solution.py:231
  230.6 10.5 %collective-permute-start.67 = (bf16[32,1024]{1,0:T(8,128)(2,1)S(1)}, bf16[32,1024]{1,0:T(8,128)(2,1)S(1)}, u32[]{:S(2)}, u32[]{:S(2)}) collective-permute-start(bf16[32,1024]{1,0:T(8,128)(2,1)S(1)} %add_convert_fusion.21), channel_id=1, source_target_pairs={{0,4},{8,0},{16,8},{24,16},{28,24},{20,28},{12,20},{4,12},{1,5},{9... | collective-permute-start | bytes 196616 | tf_op jit(solution)/shard_map/ppermute | solution.py:277
  233.6 28.0 %collective-permute-start.123 = (bf16[128,1024]{1,0:T(8,128)(2,1)S(1)}, bf16[128,1024]{1,0:T(8,128)(2,1)S(1)}, u32[]{:S(2)}, u32[]{:S(2)}) collective-permute-start(bf16[128,1024]{1,0:T(8,128)(2,1)S(1)} %add_convert_fusion.5), channel_id=1, source_target_pairs={{0,8},{8,16},{16,24},{24,28},{28,20},{20,12},{12,4},{4,0},{1,9},{9... | collective-permute-start | bytes 786440 | tf_op jit(solution)/shard_map/ppermute | solution.py:277
  242.0 12.7 %collective-permute-start.68 = (bf16[32,1024]{1,0:T(8,128)(2,1)S(1)}, bf16[32,1024]{1,0:T(8,128)(2,1)S(1)}, u32[]{:S(2)}, u32[]{:S(2)}) collective-permute-start(bf16[32,1024]{1,0:T(8,128)(2,1)S(1)} %add_convert_fusion.20), channel_id=1, source_target_pairs={{0,4},{8,0},{16,8},{24,16},{28,24},{20,28},{12,20},{4,12},{1,5},{9... | collective-permute-start | bytes 196616 | tf_op jit(solution)/shard_map/ppermute | solution.py:277
  246.6 19.3 %collective-permute-start.95 = (bf16[128,1024]{1,0:T(8,128)(2,1)S(1)}, bf16[128,1024]{1,0:T(8,128)(2,1)S(1)}, u32[]{:S(2)}, u32[]{:S(2)}) collective-permute-start(bf16[128,1024]{1,0:T(8,128)(2,1)S(1)} %add_convert_fusion.12), channel_id=1, source_target_pairs={{0,4},{8,0},{16,8},{24,16},{28,24},{20,28},{12,20},{4,12},{1,5},{9... | collective-permute-start | bytes 786440 | tf_op jit(solution)/shard_map/ppermute | solution.py:277
  256.5 14.4 %collective-permute-start.85 = (f32[4,1024]{1,0:T(4,128)S(1)}, f32[4,1024]{1,0:T(4,128)S(1)}, u32[]{:S(2)}, u32[]{:S(2)}) collective-permute-start(f32[4,1024]{1,0:T(4,128)S(1)} %fusion.78), channel_id=1, source_target_pairs={{0,4},{4,0},{8,12},{12,8},{16,20},{20,16},{24,28},{28,24},{1,5},{5... | collective-permute-start | bytes 49160 | tf_op jit(solution)/shard_map/ppermute | solution.py:361
  262.7 18.3 %collective-permute-start.124 = (bf16[128,1024]{1,0:T(8,128)(2,1)S(1)}, bf16[128,1024]{1,0:T(8,128)(2,1)S(1)}, u32[]{:S(2)}, u32[]{:S(2)}) collective-permute-start(bf16[128,1024]{1,0:T(8,128)(2,1)S(1)} %add_convert_fusion.4), channel_id=1, source_target_pairs={{0,8},{8,16},{16,24},{24,28},{28,20},{20,12},{12,4},{4,0},{1,9},{9... | collective-permute-start | bytes 786440 | tf_op jit(solution)/shard_map/ppermute | solution.py:277
  267.0 17.1 %collective-permute-start.96 = (bf16[128,1024]{1,0:T(8,128)(2,1)S(1)}, bf16[128,1024]{1,0:T(8,128)(2,1)S(1)}, u32[]{:S(2)}, u32[]{:S(2)}) collective-permute-start(bf16[128,1024]{1,0:T(8,128)(2,1)S(1)} %add_convert_fusion.11), channel_id=1, source_target_pairs={{0,4},{8,0},{16,8},{24,16},{28,24},{20,28},{12,20},{4,12},{1,5},{9... | collective-permute-start | bytes 786440 | tf_op jit(solution)/shard_map/ppermute | solution.py:277
  277.4 12.1 %collective-permute-start.12 = (bf16[256,1024]{1,0:T(8,128)(2,1)S(1)}, bf16[256,1024]{1,0:T(8,128)(2,1)S(1)}, u32[]{:S(2)}, u32[]{:S(2)}) collective-permute-start(bf16[256,1024]{1,0:T(8,128)(2,1)S(1)} %copy-done.2), channel_id=1, source_target_pairs={{0,2},{2,0},{1,3},{3,1},{4,6},{6,4},{5,7},{7,5},{8,10},{10,8},{9,1... | collective-permute-start | bytes 1572872 | tf_op jit(solution)/shard_map/ppermute | solution.py:227
  278.0 36.7 %collective-permute-start.115 = (f32[2048]{0:T(1024)}, f32[2048]{0:T(1024)}, u32[]{:S(2)}, u32[]{:S(2)}) collective-permute-start(f32[2048]{0:T(1024)} %add.559), channel_id=1, source_target_pairs={{0,16},{4,20},{8,24},{12,28},{16,0},{20,4},{24,8},{28,12},{1,17},{... | collective-permute-start | bytes 24584 | tf_op jit(solution)/shard_map/ppermute | solution.py:361
  279.7 40.9 %collective-permute-start.87 = (f32[4,1024]{1,0:T(4,128)S(1)}, f32[4,1024]{1,0:T(4,128)}, u32[]{:S(2)}, u32[]{:S(2)}) collective-permute-start(f32[4,1024]{1,0:T(4,128)S(1)} %add.545), channel_id=1, source_target_pairs={{0,16},{4,20},{8,24},{12,28},{16,0},{20,4},{24,8},{28,12},{1,17},{... | collective-permute-start | bytes 49160 | tf_op jit(solution)/shard_map/ppermute | solution.py:361
  281.0 33.7 %collective-permute-start.73 = (bf16[32,1024]{1,0:T(8,128)(2,1)S(1)}, bf16[32,1024]{1,0:T(8,128)(2,1)S(1)}, u32[]{:S(2)}, u32[]{:S(2)}) collective-permute-start(bf16[32,1024]{1,0:T(8,128)(2,1)S(1)} %collective-permute-done.72.refs_4_), channel_id=1, source_target_pairs={{0,4},{8,0},{16,8},{24,16},{28,24},{20,28},{12,20},{4,12},{1,5},{9... | collective-permute-start | bytes 196616 | tf_op jit(solution)/shard_map/ppermute | solution.py:280
  295.2 32.9 %collective-permute-start.6 = (bf16[256,1024]{1,0:T(8,128)(2,1)S(1)}, bf16[256,1024]{1,0:T(8,128)(2,1)S(1)}, u32[]{:S(2)}, u32[]{:S(2)}) collective-permute-start(bf16[256,1024]{1,0:T(8,128)(2,1)S(1)} %get-tuple-element.83), channel_id=1, source_target_pairs={{0,1},{1,0},{2,3},{3,2},{4,5},{5,4},{6,7},{7,6},{8,9},{9,8},{10,11... | collective-permute-start | bytes 1572872 | tf_op jit(solution)/shard_map/ppermute | solution.py:346
  328.8 12.5 %collective-permute-start.125 = (bf16[128,1024]{1,0:T(8,128)(2,1)S(1)}, bf16[128,1024]{1,0:T(8,128)(2,1)S(1)}, u32[]{:S(2)}, u32[]{:S(2)}) collective-permute-start(bf16[128,1024]{1,0:T(8,128)(2,1)S(1)} %add_convert_fusion.3.refs_0_), channel_id=1, source_target_pairs={{0,8},{8,16},{16,24},{24,28},{28,20},{20,12},{12,4},{4,0},{1,9},{9... | collective-permute-start | bytes 786440 | tf_op jit(solution)/shard_map/ppermute | solution.py:280
  329.6 12.4 %collective-permute-start.132 = (bf16[128,1024]{1,0:T(8,128)(2,1)S(1)}, bf16[128,1024]{1,0:T(8,128)(2,1)S(1)}, u32[]{:S(2)}, u32[]{:S(2)}) collective-permute-start(bf16[128,1024]{1,0:T(8,128)(2,1)S(1)} %add_convert_fusion.3.refs_0_), channel_id=1, source_target_pairs={{0,2},{2,0},{1,3},{3,1},{4,6},{6,4},{5,7},{7,5},{8,10},{10,8},{9,1... | collective-permute-start | bytes 786440 | tf_op jit(solution)/shard_map/ppermute | solution.py:227
  329.6 12.4 %collective-permute-start.97 = (bf16[128,1024]{1,0:T(8,128)(2,1)S(1)}, bf16[128,1024]{1,0:T(8,128)(2,1)S(1)}, u32[]{:S(2)}, u32[]{:S(2)}) collective-permute-start(bf16[128,1024]{1,0:T(8,128)(2,1)S(1)} %add_convert_fusion.10.refs_0_), channel_id=1, source_target_pairs={{0,4},{8,0},{16,8},{24,16},{28,24},{20,28},{12,20},{4,12},{1,5},{9... | collective-permute-start | bytes 786440 | tf_op jit(solution)/shard_map/ppermute | solution.py:280
  331.2 12.3 %collective-permute-start.104 = (bf16[128,1024]{1,0:T(8,128)(2,1)S(1)}, bf16[128,1024]{1,0:T(8,128)(2,1)S(1)}, u32[]{:S(2)}, u32[]{:S(2)}) collective-permute-start(bf16[128,1024]{1,0:T(8,128)(2,1)S(1)} %add_convert_fusion.10.refs_0_), channel_id=1, source_target_pairs={{0,2},{2,0},{1,3},{3,1},{4,6},{6,4},{5,7},{7,5},{8,10},{10,8},{9,1... | collective-permute-start | bytes 786440 | tf_op jit(solution)/shard_map/ppermute | solution.py:227
  342.0 10.0 %collective-permute-start.133 = (bf16[128,1024]{1,0:T(8,128)(2,1)S(1)}, bf16[128,1024]{1,0:T(8,128)(2,1)S(1)}, u32[]{:S(2)}, u32[]{:S(2)}) collective-permute-start(bf16[128,1024]{1,0:T(8,128)(2,1)S(1)} %collective-permute-done.125.refs_1_), channel_id=1, source_target_pairs={{0,2},{2,0},{1,3},{3,1},{4,6},{6,4},{5,7},{7,5},{8,10},{10,8},{9,1... | collective-permute-start | bytes 786440 | tf_op jit(solution)/shard_map/ppermute | solution.py:227
  342.0 10.0 %collective-permute-start.98 = (bf16[128,1024]{1,0:T(8,128)(2,1)S(1)}, bf16[128,1024]{1,0:T(8,128)(2,1)S(1)}, u32[]{:S(2)}, u32[]{:S(2)}) collective-permute-start(bf16[128,1024]{1,0:T(8,128)(2,1)S(1)} %collective-permute-done.97.refs_1_), channel_id=1, source_target_pairs={{0,4},{8,0},{16,8},{24,16},{28,24},{20,28},{12,20},{4,12},{1,5},{9... | collective-permute-start | bytes 786440 | tf_op jit(solution)/shard_map/ppermute | solution.py:280
  350.4 9.9 %collective-permute-start.127 = (bf16[128,1024]{1,0:T(8,128)(2,1)S(1)}, bf16[128,1024]{1,0:T(8,128)(2,1)S(1)}, u32[]{:S(2)}, u32[]{:S(2)}) collective-permute-start(bf16[128,1024]{1,0:T(8,128)(2,1)S(1)} %collective-permute-done.126.refs_2_), channel_id=1, source_target_pairs={{0,8},{8,16},{16,24},{24,28},{28,20},{20,12},{12,4},{4,0},{1,9},{9... | collective-permute-start | bytes 786440 | tf_op jit(solution)/shard_map/ppermute | solution.py:280
  352.0 10.1 %collective-permute-start.99 = (bf16[128,1024]{1,0:T(8,128)(2,1)S(1)}, bf16[128,1024]{1,0:T(8,128)(2,1)S(1)}, u32[]{:S(2)}, u32[]{:S(2)}) collective-permute-start(bf16[128,1024]{1,0:T(8,128)(2,1)S(1)} %collective-permute-done.98.refs_2_), channel_id=1, source_target_pairs={{0,4},{8,0},{16,8},{24,16},{28,24},{20,28},{12,20},{4,12},{1,5},{9... | collective-permute-start | bytes 786440 | tf_op jit(solution)/shard_map/ppermute | solution.py:280
  352.5 10.2 %collective-permute-start.106 = (bf16[128,1024]{1,0:T(8,128)(2,1)S(1)}, bf16[128,1024]{1,0:T(8,128)(2,1)S(1)}, u32[]{:S(2)}, u32[]{:S(2)}) collective-permute-start(bf16[128,1024]{1,0:T(8,128)(2,1)S(1)} %collective-permute-done.98.refs_2_), channel_id=1, source_target_pairs={{0,2},{2,0},{1,3},{3,1},{4,6},{6,4},{5,7},{7,5},{8,10},{10,8},{9,1... | collective-permute-start | bytes 786440 | tf_op jit(solution)/shard_map/ppermute | solution.py:227
  360.3 13.4 %collective-permute-start.128 = (bf16[128,1024]{1,0:T(8,128)(2,1)S(1)}, bf16[128,1024]{1,0:T(8,128)(2,1)S(1)}, u32[]{:S(2)}, u32[]{:S(2)}) collective-permute-start(bf16[128,1024]{1,0:T(8,128)(2,1)S(1)} %collective-permute-done.127.refs_3_), channel_id=1, source_target_pairs={{0,8},{8,16},{16,24},{24,28},{28,20},{20,12},{12,4},{4,0},{1,9},{9... | collective-permute-start | bytes 786440 | tf_op jit(solution)/shard_map/ppermute | solution.py:280
  361.9 12.1 %collective-permute-start.135 = (bf16[128,1024]{1,0:T(8,128)(2,1)S(1)}, bf16[128,1024]{1,0:T(8,128)(2,1)S(1)}, u32[]{:S(2)}, u32[]{:S(2)}) collective-permute-start(bf16[128,1024]{1,0:T(8,128)(2,1)S(1)} %collective-permute-done.127.refs_3_), channel_id=1, source_target_pairs={{0,2},{2,0},{1,3},{3,1},{4,6},{6,4},{5,7},{7,5},{8,10},{10,8},{9,1... | collective-permute-start | bytes 786440 | tf_op jit(solution)/shard_map/ppermute | solution.py:227
  362.1 11.9 %collective-permute-start.100 = (bf16[128,1024]{1,0:T(8,128)(2,1)S(1)}, bf16[128,1024]{1,0:T(8,128)(2,1)S(1)}, u32[]{:S(2)}, u32[]{:S(2)}) collective-permute-start(bf16[128,1024]{1,0:T(8,128)(2,1)S(1)} %collective-permute-done.99.refs_3_), channel_id=1, source_target_pairs={{0,4},{8,0},{16,8},{24,16},{28,24},{20,28},{12,20},{4,12},{1,5},{9... | collective-permute-start | bytes 786440 | tf_op jit(solution)/shard_map/ppermute | solution.py:280
  362.7 13.1 %collective-permute-start.107 = (bf16[128,1024]{1,0:T(8,128)(2,1)S(1)}, bf16[128,1024]{1,0:T(8,128)(2,1)S(1)}, u32[]{:S(2)}, u32[]{:S(2)}) collective-permute-start(bf16[128,1024]{1,0:T(8,128)(2,1)S(1)} %collective-permute-done.99.refs_3_), channel_id=1, source_target_pairs={{0,2},{2,0},{1,3},{3,1},{4,6},{6,4},{5,7},{7,5},{8,10},{10,8},{9,1... | collective-permute-start | bytes 786440 | tf_op jit(solution)/shard_map/ppermute | solution.py:227
  373.7 11.2 %collective-permute-start.129 = (bf16[128,1024]{1,0:T(8,128)(2,1)S(1)}, bf16[128,1024]{1,0:T(8,128)(2,1)S(1)}, u32[]{:S(2)}, u32[]{:S(2)}) collective-permute-start(bf16[128,1024]{1,0:T(8,128)(2,1)S(1)} %collective-permute-done.128.refs_4_), channel_id=1, source_target_pairs={{0,8},{8,16},{16,24},{24,28},{28,20},{20,12},{12,4},{4,0},{1,9},{9... | collective-permute-start | bytes 786440 | tf_op jit(solution)/shard_map/ppermute | solution.py:280
  374.0 10.9 %collective-permute-start.136 = (bf16[128,1024]{1,0:T(8,128)(2,1)S(1)}, bf16[128,1024]{1,0:T(8,128)(2,1)S(1)}, u32[]{:S(2)}, u32[]{:S(2)}) collective-permute-start(bf16[128,1024]{1,0:T(8,128)(2,1)S(1)} %collective-permute-done.128.refs_4_), channel_id=1, source_target_pairs={{0,2},{2,0},{1,3},{3,1},{4,6},{6,4},{5,7},{7,5},{8,10},{10,8},{9,1... | collective-permute-start | bytes 786440 | tf_op jit(solution)/shard_map/ppermute | solution.py:227
  374.0 11.3 %collective-permute-start.101 = (bf16[128,1024]{1,0:T(8,128)(2,1)S(1)}, bf16[128,1024]{1,0:T(8,128)(2,1)S(1)}, u32[]{:S(2)}, u32[]{:S(2)}) collective-permute-start(bf16[128,1024]{1,0:T(8,128)(2,1)S(1)} %collective-permute-done.100.refs_4_), channel_id=1, source_target_pairs={{0,4},{8,0},{16,8},{24,16},{28,24},{20,28},{12,20},{4,12},{1,5},{9... | collective-permute-start | bytes 786440 | tf_op jit(solution)/shard_map/ppermute | solution.py:280
  377.3 10.1 %collective-permute-start.21 = (bf16[128,512]{1,0:T(8,128)(2,1)S(1)}, bf16[128,512]{1,0:T(8,128)(2,1)S(1)}, u32[]{:S(2)}, u32[]{:S(2)}) collective-permute-start(bf16[128,512]{1,0:T(8,128)(2,1)S(1)} %fusion.54), channel_id=1, source_target_pairs={{0,8},{8,16},{16,24},{24,28},{28,20},{20,12},{12,4},{4,0},{1,9},{9... | collective-permute-start | bytes 393224 | tf_op jit(solution)/shard_map/ppermute | solution.py:277
  384.9 20.7 %collective-permute-start.130 = (bf16[128,1024]{1,0:T(8,128)(2,1)S(1)}, bf16[128,1024]{1,0:T(8,128)(2,1)S(1)}, u32[]{:S(2)}, u32[]{:S(2)}) collective-permute-start(bf16[128,1024]{1,0:T(8,128)(2,1)S(1)} %collective-permute-done.129.refs_5_), channel_id=1, source_target_pairs={{0,8},{8,16},{16,24},{24,28},{28,20},{20,12},{12,4},{4,0},{1,9},{9... | collective-permute-start | bytes 786440 | tf_op jit(solution)/shard_map/ppermute | solution.py:280
  387.4 11.8 %collective-permute-start.52 = (bf16[128,256]{1,0:T(8,128)(2,1)S(1)}, bf16[128,256]{1,0:T(8,128)(2,1)S(1)}, u32[]{:S(2)}, u32[]{:S(2)}) collective-permute-start(bf16[128,256]{1,0:T(8,128)(2,1)S(1)} %add_convert_fusion.26.refs_0_), channel_id=1, source_target_pairs={{0,2},{2,0},{1,3},{3,1},{4,6},{6,4},{5,7},{7,5},{8,10},{10,8},{9,1... | collective-permute-start | bytes 196616 | tf_op jit(solution)/shard_map/ppermute | solution.py:227
  387.4 11.6 %collective-permute-start.46 = (bf16[128,256]{1,0:T(8,128)(2,1)S(1)}, bf16[128,256]{1,0:T(8,128)(2,1)S(1)}, u32[]{:S(2)}, u32[]{:S(2)}) collective-permute-start(bf16[128,256]{1,0:T(8,128)(2,1)S(1)} %collective-permute-done.45.refs_1_), channel_id=1, source_target_pairs={{0,4},{8,0},{16,8},{24,16},{28,24},{20,28},{12,20},{4,12},{1,5},{9... | collective-permute-start | bytes 196616 | tf_op jit(solution)/shard_map/ppermute | solution.py:280
  391.8 12.0 %collective-permute-start.22 = (bf16[128,512]{1,0:T(8,128)(2,1)S(1)}, bf16[128,512]{1,0:T(8,128)(2,1)S(1)}, u32[]{:S(2)}, u32[]{:S(2)}) collective-permute-start(bf16[128,512]{1,0:T(8,128)(2,1)S(1)} %fusion.34.refs_0_), channel_id=1, source_target_pairs={{0,8},{8,16},{16,24},{24,28},{28,20},{20,12},{12,4},{4,0},{1,9},{9... | collective-permute-start | bytes 393224 | tf_op jit(solution)/shard_map/ppermute | solution.py:280
  400.3 14.7 %collective-permute-start.137 = (bf16[128,1024]{1,0:T(8,128)(2,1)S(1)}, bf16[128,1024]{1,0:T(8,128)(2,1)S(1)}, u32[]{:S(2)}, u32[]{:S(2)}) collective-permute-start(bf16[128,1024]{1,0:T(8,128)(2,1)S(1)} %collective-permute-done.129.refs_5_), channel_id=1, source_target_pairs={{0,2},{2,0},{1,3},{3,1},{4,6},{6,4},{5,7},{7,5},{8,10},{10,8},{9,1... | collective-permute-start | bytes 786440 | tf_op jit(solution)/shard_map/ppermute | solution.py:227
  403.5 11.6 %collective-permute-start.102 = (bf16[128,1024]{1,0:T(8,128)(2,1)S(1)}, bf16[128,1024]{1,0:T(8,128)(2,1)S(1)}, u32[]{:S(2)}, u32[]{:S(2)}) collective-permute-start(bf16[128,1024]{1,0:T(8,128)(2,1)S(1)} %collective-permute-done.101.refs_5_), channel_id=1, source_target_pairs={{0,4},{8,0},{16,8},{24,16},{28,24},{20,28},{12,20},{4,12},{1,5},{9... | collective-permute-start | bytes 786440 | tf_op jit(solution)/shard_map/ppermute | solution.py:280
  403.8 13.7 %collective-permute-start.109 = (bf16[128,1024]{1,0:T(8,128)(2,1)S(1)}, bf16[128,1024]{1,0:T(8,128)(2,1)S(1)}, u32[]{:S(2)}, u32[]{:S(2)}) collective-permute-start(bf16[128,1024]{1,0:T(8,128)(2,1)S(1)} %collective-permute-done.101.refs_5_), channel_id=1, source_target_pairs={{0,2},{2,0},{1,3},{3,1},{4,6},{6,4},{5,7},{7,5},{8,10},{10,8},{9,1... | collective-permute-start | bytes 786440 | tf_op jit(solution)/shard_map/ppermute | solution.py:227
  419.6 13.2 %collective-permute-start.131 = (bf16[128,1024]{1,0:T(8,128)(2,1)S(1)}, bf16[128,1024]{1,0:T(8,128)(2,1)S(1)}, u32[]{:S(2)}, u32[]{:S(2)}) collective-permute-start(bf16[128,1024]{1,0:T(8,128)(2,1)S(1)} %collective-permute-done.130.refs_6_), channel_id=1, source_target_pairs={{0,8},{8,16},{16,24},{24,28},{28,20},{20,12},{12,4},{4,0},{1,9},{9... | collective-permute-start | bytes 786440 | tf_op jit(solution)/shard_map/ppermute | solution.py:280
  421.2 11.6 %collective-permute-start.138 = (bf16[128,1024]{1,0:T(8,128)(2,1)S(1)}, bf16[128,1024]{1,0:T(8,128)(2,1)S(1)}, u32[]{:S(2)}, u32[]{:S(2)}) collective-permute-start(bf16[128,1024]{1,0:T(8,128)(2,1)S(1)} %collective-permute-done.130.refs_6_), channel_id=1, source_target_pairs={{0,2},{2,0},{1,3},{3,1},{4,6},{6,4},{5,7},{7,5},{8,10},{10,8},{9,1... | collective-permute-start | bytes 786440 | tf_op jit(solution)/shard_map/ppermute | solution.py:227
  444.8 24.5 %collective-permute-start.32 = (bf16[128,512]{1,0:T(8,128)(2,1)S(1)}, bf16[128,512]{1,0:T(8,128)(2,1)S(1)}, u32[]{:S(2)}, u32[]{:S(2)}) collective-permute-start(bf16[128,512]{1,0:T(8,128)(2,1)S(1)} %collective-permute-done.24.refs_3_), channel_id=1, source_target_pairs={{0,2},{2,0},{1,3},{3,1},{4,6},{6,4},{5,7},{7,5},{8,10},{10,8},{9,1... | collective-permute-start | bytes 393224 | tf_op jit(solution)/shard_map/ppermute | solution.py:227
  444.8 24.4 %collective-permute-start.33 = (bf16[128,512]{1,0:T(8,128)(2,1)S(1)}, bf16[128,512]{1,0:T(8,128)(2,1)S(1)}, u32[]{:S(2)}, u32[]{:S(2)}) collective-permute-start(bf16[128,512]{1,0:T(8,128)(2,1)S(1)} %collective-permute-done.25.refs_4_), channel_id=1, source_target_pairs={{0,2},{2,0},{1,3},{3,1},{4,6},{6,4},{5,7},{7,5},{8,10},{10,8},{9,1... | collective-permute-start | bytes 393224 | tf_op jit(solution)/shard_map/ppermute | solution.py:227
  445.3 24.0 %collective-permute-start.34 = (bf16[128,512]{1,0:T(8,128)(2,1)S(1)}, bf16[128,512]{1,0:T(8,128)(2,1)S(1)}, u32[]{:S(2)}, u32[]{:S(2)}) collective-permute-start(bf16[128,512]{1,0:T(8,128)(2,1)S(1)} %collective-permute-done.26.refs_5_), channel_id=1, source_target_pairs={{0,2},{2,0},{1,3},{3,1},{4,6},{6,4},{5,7},{7,5},{8,10},{10,8},{9,1... | collective-permute-start | bytes 393224 | tf_op jit(solution)/shard_map/ppermute | solution.py:227
  445.4 23.9 %collective-permute-start.35 = (bf16[128,512]{1,0:T(8,128)(2,1)S(1)}, bf16[128,512]{1,0:T(8,128)(2,1)S(1)}, u32[]{:S(2)}, u32[]{:S(2)}) collective-permute-start(bf16[128,512]{1,0:T(8,128)(2,1)S(1)} %collective-permute-done.27.refs_6_), channel_id=1, source_target_pairs={{0,2},{2,0},{1,3},{3,1},{4,6},{6,4},{5,7},{7,5},{8,10},{10,8},{9,1... | collective-permute-start | bytes 393224 | tf_op jit(solution)/shard_map/ppermute | solution.py:227
  446.8 22.5 %collective-permute-start.36 = (bf16[128,512]{1,0:T(8,128)(2,1)S(1)}, bf16[128,512]{1,0:T(8,128)(2,1)S(1)}, u32[]{:S(2)}, u32[]{:S(2)}) collective-permute-start(bf16[128,512]{1,0:T(8,128)(2,1)S(1)} %collective-permute-done.28.refs_7_), channel_id=1, source_target_pairs={{0,2},{2,0},{1,3},{3,1},{4,6},{6,4},{5,7},{7,5},{8,10},{10,8},{9,1... | collective-permute-start | bytes 393224 | tf_op jit(solution)/shard_map/ppermute | solution.py:227
  (114 other events, 979.8 us)

commit v3 on v2

--- a/solution.py
+++ b/solution.py
@@ -264,70 +264,214 @@
     return [(order[at], order[(at + direction) % chips]) for at in range(chips)]
 
 
-def ring_sum(partial, direction):
-    chips, place, pairs = lax.axis_size("chip"), ring_position(), ring_pairs(direction)
-    rows = partial.shape[0] // chips
-
-    def block(step):
-        index = lax.rem(place + (chips - direction * step) % chips, chips)
-        return lax.dynamic_slice_in_dim(partial, index * rows, rows, 0)
-
-    travel = block(1).astype(BF16)
-    for step in range(2, chips + 1):
-        travel = (lax.ppermute(travel, "chip", pairs).astype(F32) + block(step)).astype(BF16)
-    blocks = [travel]
-    for _ in range(chips - 1):
-        blocks.append(lax.ppermute(blocks[-1], "chip", pairs))
-    return blocks
-
-
-def assemble_kernel(cuts, _, *refs):
-    inputs, outputs = refs[: -len(cuts)], refs[-len(cuts) :]
-    for at, block in enumerate(inputs):
-
-        @pl.when(pl.program_id(0) == at)
-        def _(block=block):
-            for output, cut in zip(outputs, cuts):
-                output[...] = block[:, cut].astype(F32)
-
-
-def assemble(blocks, direction, axis, count=1):
-    chips, place, core = lax.axis_size("chip"), ring_position(), lax.axis_index("core")
-    steps = jnp.arange(chips, dtype=jnp.int32)
-    index = lax.rem(place + (chips - direction * steps) % chips, chips)
-    index = jnp.concatenate([index, index])
-    side = jnp.concatenate([jnp.full((chips,), core), jnp.full((chips,), 1 - core)])
-    if axis == 0:
-        order = jnp.stack([side * chips + index, jnp.zeros_like(index)])
-    else:
-        order = jnp.stack([index, side])
-    rows, columns = blocks[0].shape
-    columns //= count
-    shape = (2 * chips * rows, columns) if axis == 0 else (chips * rows, 2 * columns)
-    cuts = [slice(at * columns, at * columns + columns) for at in range(count)]
-    blocks = blocks + [swap_cores(block) for block in blocks]
-    if rows % 8 or columns % 128:
-        outputs = [jnp.zeros(shape, F32)] * count
-        for at, block in enumerate(blocks):
-            start = (order[0, at] * rows, order[1, at] * columns)
-            outputs = [
-                lax.dynamic_update_slice(output, block[:, cut].astype(F32), start)
-                for output, cut in zip(outputs, cuts)
-            ]
-        return outputs
+class Ring:
+    def __init__(self, partial, direction):
+        self.chips = lax.axis_size("chip")
+        self.partial, self.direction = partial, direction
+        self.rows = partial.shape[0] // self.chips
+        self.step, self.near, self.far = 1, [], []
+        self.pending = [self.send(self.block(1).astype(BF16))]
+
+    def index(self, step):
+        ahead = (self.chips - self.direction * step) % self.chips
+        return lax.rem(ring_position() + ahead, self.chips)
+
+    def block(self, step):
+        return lax.dynamic_slice_in_dim(
+            self.partial, self.index(step) * self.rows, self.rows, 0
+        )
+
+    def send(self, block):
+        return lax.ppermute(block, "chip", ring_pairs(self.direction))
+
+    def advance(self, arrived):
+        self.step += 1
+        if len(arrived) > 1 or self.step == 2 * self.chips:
+            self.far.append(arrived[-1])
+        block, self.pending = arrived[0], []
+        if self.step <= self.chips:
+            block = (block.astype(F32) + self.block(self.step)).astype(BF16)
+        if self.step < 2 * self.chips - 1:
+            self.pending.append(self.send(block))
+        if self.chips <= self.step < 2 * self.chips:
+            self.near.append(block)
+            self.pending.append(swap_cores(block))
+
+
+def visit(rings, values):
+    pending, values = lax.optimization_barrier(([ring.pending for ring in rings], values))
+    for ring, arrived in zip(rings, pending):
+        if arrived:
+            ring.advance(arrived)
+    return values
+
+
+def place_kernel(_, *refs):
+    refs = refs[-6:]
+    for side in range(2):
+
+        @pl.when(pl.program_id(0) == side)
+        def _(side=side):
+            refs[4][...] = refs[side][...].astype(F32)
+            refs[5][...] = refs[2 + side][...].astype(F32)
+
+
+def place(outputs, down, up, at):
+    tall, wide = down.near[at].shape, up.near[at].shape
+    chips, core = down.chips, lax.axis_index("core")
+    blocks = [down.near[at], down.far[at], up.near[at], up.far[at]]
+    shapes = [(2 * chips * tall[0], tall[1]), (chips * wide[0], 2 * wide[1])]
+    order = jnp.stack([down.index(at), up.index(at), core]).astype(jnp.int32)
+
+    def side(at, order):
+        return jnp.where(at == 0, order[2], 1 - order[2])
+
     return pl.pallas_call(
-        functools.partial(assemble_kernel, cuts),
+        place_kernel,
         grid_spec=pltpu.PrefetchScalarGridSpec(
             num_scalar_prefetch=1,
-            grid=(2 * chips,),
-            in_specs=[pl.BlockSpec(blocks[0].shape, lambda at, order: (0, 0))] * (2 * chips),
-            out_specs=[pl.BlockSpec((rows, columns), lambda at, order: (order[0, at], order[1, at]))]
-            * count,
+            grid=(2,),
+            in_specs=[pl.BlockSpec(memory_space=pl.ANY)] * len(outputs)
+            + [pl.BlockSpec(block.shape, lambda at, order: (0, 0)) for block in blocks],
+            out_specs=[
+                pl.BlockSpec(tall, lambda at, order: (side(at, order) * chips + order[0], 0)),
+                pl.BlockSpec(wide, lambda at, order: (order[1], side(at, order))),
+            ],
         ),
-        out_shape=[jax.ShapeDtypeStruct(shape, F32)] * count,
+        out_shape=[jax.ShapeDtypeStruct(shape, F32) for shape in shapes],
+        input_output_aliases={1 + at: at for at in range(len(outputs))},
         compiler_params=pltpu.CompilerParams(vmem_limit_bytes=vmem_limit),
-        name="assemble",
-    )(order.astype(jnp.int32), *blocks)
+        name="place",
+    )(order, *outputs, *blocks)
+
+
+def place_all(down, up):
+    outputs = []
+    for at in range(down.chips):
+        outputs = place(outputs, down, up, at)
+    return outputs
+
+
+def core_half(values, axis, side):
+    size = values.shape[axis] // 2
+    return lax.dynamic_slice_in_dim(values, side * size, size, axis)
+
+
+def share_halves(values, axis):
+    core = lax.axis_index("core")
+    return core_half(values, axis, core), swap_cores(core_half(values, axis, 1 - core))
+
+
+def head_sum(values):
+    low = values.astype(BF16)
+    if lax.axis_size("head") == 2:
+        return low.astype(F32) + lax.ppermute(low, "head", [(0, 1), (1, 0)]).astype(F32)
+    return lax.psum(low, "head").astype(F32)
+
+
+def whole_head_sum(values):
+    if lax.axis_size("head") == 2:
+        return values + lax.ppermute(values, "head", [(0, 1), (1, 0)])
+    return lax.psum(values, "head")
+
+
+def ring_position():
+    chips, chip = lax.axis_size("chip"), lax.axis_index("chip")
+    return jnp.where(chip % 2 == 0, chip // 2, chips - 1 - chip // 2)
+
+
+def ring_pairs(direction):
+    chips = lax.axis_size("chip")
+    order = list(range(0, chips, 2)) + list(range(chips - 1, 0, -2))
+    return [(order[at], order[(at + direction) % chips]) for at in range(chips)]
+
+
+class Ring:
+    def __init__(self, partial, direction):
+        self.chips = lax.axis_size("chip")
+        self.partial, self.direction = partial, direction
+        self.rows = partial.shape[0] // self.chips
+        self.step, self.near, self.far = 1, [], []
+        self.pending = [self.send(self.block(1).astype(BF16))]
+
+    def index(self, step):
+        ahead = (self.chips - self.direction * step) % self.chips
+        return lax.rem(ring_position() + ahead, self.chips)
+
+    def block(self, step):
+        return lax.dynamic_slice_in_dim(
+            self.partial, self.index(step) * self.rows, self.rows, 0
+        )
+
+    def send(self, block):
+        return lax.ppermute(block, "chip", ring_pairs(self.direction))
+
+    def advance(self, arrived):
+        self.step += 1
+        if len(arrived) > 1 or self.step == 2 * self.chips:
+            self.far.append(arrived[-1])
+        block, self.pending = arrived[0], []
+        if self.step <= self.chips:
+            block = (block.astype(F32) + self.block(self.step)).astype(BF16)
+        if self.step < 2 * self.chips - 1:
+            self.pending.append(self.send(block))
+        if self.chips <= self.step < 2 * self.chips:
+            self.near.append(block)
+            self.pending.append(swap_cores(block))
+
+
+def visit(rings, values):
+    pending, values = lax.optimization_barrier(([ring.pending for ring in rings], values))
+    for ring, arrived in zip(rings, pending):
+        if arrived:
+            ring.advance(arrived)
+    return values
+
+
+def place_kernel(_, *refs):
+    refs = refs[-6:]
+    for side in range(2):
+
+        @pl.when(pl.program_id(0) == side)
+        def _(side=side):
+            refs[4][...] = refs[side][...].astype(F32)
+            refs[5][...] = refs[2 + side][...].astype(F32)
+
+
+def place(outputs, down, up, at):
+    tall, wide = down.near[at].shape, up.near[at].shape
+    chips, core = down.chips, lax.axis_index("core")
+    blocks = [down.near[at], down.far[at], up.near[at], up.far[at]]
+    shapes = [(2 * chips * tall[0], tall[1]), (chips * wide[0], 2 * wide[1])]
+    order = jnp.stack([down.index(at), up.index(at), core]).astype(jnp.int32)
+
+    def side(at, order):
+        return jnp.where(at == 0, order[2], 1 - order[2])
+
+    return pl.pallas_call(
+        place_kernel,
+        grid_spec=pltpu.PrefetchScalarGridSpec(
+            num_scalar_prefetch=1,
+            grid=(2,),
+            in_specs=[pl.BlockSpec(memory_space=pl.ANY)] * len(outputs)
+            + [pl.BlockSpec(block.shape, lambda at, order: (0, 0)) for block in blocks],
+            out_specs=[
+                pl.BlockSpec(tall, lambda at, order: (side(at, order) * chips + order[0], 0)),
+                pl.BlockSpec(wide, lambda at, order: (order[1], side(at, order))),
+            ],
+        ),
+        out_shape=[jax.ShapeDtypeStruct(shape, F32) for shape in shapes],
+        input_output_aliases={1 + at: at for at in range(len(outputs))},
+        compiler_params=pltpu.CompilerParams(vmem_limit_bytes=vmem_limit),
+        name="place",
+    )(order, *outputs, *blocks)
+
+
+def place_all(down, up):
+    outputs = []
+    for at in range(down.chips):
+        outputs = place(outputs, down, up, at)
+    return outputs
 
 
 def core_half(values, axis, side):
@@ -407,6 +551,9 @@
         queries = scatter_queries(payload.reshape(-1, rows), heads, split)
         own = to_heads(jnp.repeat(payload, split, axis=0))
     other = swap_cores(own)
+    if split == 1:
+        attn_in_all, other = lax.optimization_barrier((attn_in, other))
+        attn_in_all = lax.all_gather(attn_in_all, "chip", axis=0)
     raw, out, logsum = attention_forward(queries, own, other, crops)
     attn_out = gather_queries(out, heads, split, rows)
     branch = head_sum(product(attn_out, output_weight, 0, 0))
@@ -419,28 +566,29 @@
     d_active = product(out_grad, down_weight, 1, 1)
     d_upper = gelu_back(d_active)[0].astype(BF16)
     d_mlp = head_sum(product(d_upper, up_weight, 1, 1))
+    grad_out = out_grad.astype(F32)
+    grad_far, mlp_in_far = swap_cores(out_grad), swap_cores(mlp_in)
+    active_near, active_far = share_halves(active_low, 1)
+    upper_near, upper_far = share_halves(d_upper, 1)
+    down = Ring(product(active_near, out_grad, 0, 0) + product(active_far, grad_far, 0, 0), 1)
+    up = Ring(product(mlp_in, upper_near, 0, 0) + product(mlp_in_far, upper_far, 0, 0), -1)
+    rings = (down, up)
+    d_mlp = visit(rings, d_mlp)
     mlp_part, d_mlp = lax.optimization_barrier(
         (product(active_low, down_weight).astype(BF16), d_mlp)
     )
     mlp_out = head_sum(mlp_part)
-    block_output = (hidden + mlp_out + down_bias).astype(BF16)
-    grad_out = out_grad.astype(F32)
-    grad_far, mlp_in_far, attn_in_far = (swap_cores(v) for v in (out_grad, mlp_in, attn_in))
-    active_near, active_far = share_halves(active_low, 1)
-    upper_near, upper_far = share_halves(d_upper, 1)
-    ddown = ring_sum(product(active_near, out_grad, 0, 0) + product(active_far, grad_far, 0, 0), 1)
-    dup = ring_sum(product(mlp_in, upper_near, 0, 0) + product(mlp_in_far, upper_far, 0, 0), -1)
     d_hidden = grad_out + normalize_back(d_mlp * gain_mlp, unit_mlp, inverse_mlp)
     d_branch = d_hidden.astype(BF16)
-    out_near, out_far = share_halves(attn_out, 0)
-    doutput = ring_sum(product(out_near, d_branch) + product(out_far, swap_cores(d_branch)), -1)
     d_attn = product(output_weight, d_branch, 1, 1).astype(BF16)
+    d_attn = visit(rings, d_attn)
     grads = scatter_queries(d_attn, heads, split)
     pieces = 2
     dquery = None
     far_sums, near_sums = [], []
     for keys, sums, sums_type in ((other, far_sums, BF16), (own, near_sums, F32)):
         for index in range(pieces):
+            grads, dquery = visit(rings, (grads, dquery))
             last = keys is own and index == pieces - 1
             dquery, piece = backward_piece(
                 queries, grads, raw, logsum, dquery, keys, index, pieces, crops, sums_type, last
@@ -452,8 +600,33 @@
             for near, far in zip(near_sums, far_sums)
         ]
     )
+    small = jnp.concatenate(
+        [
+            jnp.stack(
+                [
+                    jnp.sum(d_hidden, axis=0),
+                    jnp.sum(d_mlp * unit_mlp, axis=0),
+                    jnp.sum(d_mlp, axis=0),
+                    jnp.sum(grad_out, axis=0),
+                ]
+            ).reshape(-1),
+            jnp.sum(d_upper.astype(F32), axis=0),
+        ]
+    )
+    lines = -(-small.shape[0] // (16 * d_branch.shape[1])) * 16
+    small = jnp.pad(small, (0, lines * d_branch.shape[1] - small.shape[0])).astype(BF16)
+    later = lax.psum(
+        jnp.concatenate(
+            [product(attn_out, d_branch).astype(BF16), small.reshape(lines, -1)], axis=0
+        ),
+        ("chip", "core"),
+    ).astype(F32)
+    doutput_weight, small = later[:width], later[width:].reshape(-1)
+    model = d_branch.shape[1]
+    dup_bias = small[4 * model : 4 * model + d_upper.shape[1]]
     if split == 1:
-        moved = to_heads(jnp.concatenate([dquery, key_value], axis=1))
+        head_grads = visit(rings, jnp.concatenate([dquery, key_value], axis=1))
+        moved = to_heads(head_grads)
         dquery, dkey, dvalue = (
             moved[:, at * HD : at * HD + HD].reshape(width, rows) for at in range(3)
         )
@@ -462,66 +635,67 @@
         moved = to_heads(key_value).reshape(heads, split, 2 * HD, rows).astype(F32)
         moved = jnp.sum(moved, axis=1).astype(BF16)
         dkey, dvalue = (moved[:, at * HD : at * HD + HD].reshape(width, rows) for at in range(2))
+        dquery, dkey, dvalue = visit(rings, (dquery, dkey, dvalue))
     d_part = (
         product(dquery, query_weight, 0, 1)
         + product(dkey, key_weight, 0, 1)
         + product(dvalue, value_weight, 0, 1)
     )
-    near, far = zip(*(share_halves(grad, 0) for grad in (dquery, dkey, dvalue)))
-    dquery_weight, dkey_weight, dvalue_weight = (
-        product(attn_in, one, 0, 1) + product(attn_in_far, two, 0, 1)
-        for one, two in zip(near, far)
-    )
-    dquery_key = ring_sum(jnp.concatenate([dquery_weight, dkey_weight], axis=1), 1)
-    dvalue_blocks = ring_sum(dvalue_weight, -1)
+    if split == 1:
+        projections = lax.dot_general(
+            head_grads, attn_in_all, (((0, 2), (0, 1)), ((), ())), preferred_element_type=F32
+        ).astype(BF16)
+        near, far = share_halves(projections, 0)
+        projections = (near.astype(F32) + far.astype(F32)).astype(BF16)
+        d_part, projections = visit(rings, (d_part, projections))
+        projections = lax.all_gather(projections, ("chip", "core"), axis=0, tiled=True)
+        projections = projections.reshape(heads, 3, HD, model)
+        projections = [
+            projections[:, at].reshape(width, model).T.astype(F32) for at in range(3)
+        ]
+    else:
+        projections = [
+            lax.psum(product(attn_in, grad, 0, 1).astype(BF16), ("chip", "core")).astype(F32)
+            for grad in (dquery, dkey, dvalue)
+        ]
     d_in = head_sum(d_part)
+    ends = jnp.stack(
+        [
+            jnp.sum(d_part * unit_attn, axis=0),
+            jnp.sum(d_part, axis=0),
+            jnp.sum(lead[:, None] * d_part, axis=0),
+        ]
+    )
+    ends = visit(rings, ends)
+    ends = whole_head_sum(ends)
+    ends = visit(rings, ends)
+    ends = ends + swap_cores(ends)
+    reach = 1
+    while reach < chips:
+        ends = visit(rings, ends)
+        pairs = [(chip, chip ^ reach) for chip in range(chips)]
+        ends = ends + lax.ppermute(ends, "chip", pairs)
+        reach *= 2
     input_grad = (d_hidden + normalize_back(d_in * gain_attn, unit_attn, inverse_attn)).astype(
         BF16
     )
-    ends = band_sum(
-        whole_head_sum(
-            jnp.stack(
-                [
-                    jnp.sum(d_part * unit_attn, axis=0),
-                    jnp.sum(d_part, axis=0),
-                    jnp.sum(lead[:, None] * d_part, axis=0),
-                ]
-            )
-        )
-    )
-    small = band_sum(
-        jnp.stack(
-            [
-                jnp.sum(d_hidden, axis=0),
-                jnp.sum(d_mlp * unit_mlp, axis=0),
-                jnp.sum(d_mlp, axis=0),
-                jnp.sum(grad_out, axis=0),
-            ]
-        )
-    )
-    dup_bias = band_sum(jnp.sum(d_upper.astype(F32), axis=0))
-    (ddown_weight,) = assemble(ddown, 1, 0)
-    (dup_weight,) = assemble(dup, -1, 1)
-    (doutput_weight,) = assemble(doutput, -1, 0)
-    dquery_weight, dkey_weight = assemble(dquery_key, 1, 1, 2)
-    (dvalue_weight,) = assemble(dvalue_blocks, -1, 1)
+    while any(ring.pending for ring in rings):
+        visit(rings, ())
+    ddown_weight, dup_weight = place_all(down, up)
+    block_output = (hidden + mlp_out + down_bias).astype(BF16)
     return (
         block_output,
         input_grad,
         ends[0],
         ends[1],
         ends[2],
-        dquery_weight,
-        dkey_weight,
-        dvalue_weight,
+        *projections,
         doutput_weight,
-        small[0],
-        small[1],
-        small[2],
+        *(small[at * model : at * model + model] for at in range(3)),
         dup_weight,
         dup_bias,
         ddown_weight,
-        small[3],
+        small[3 * model : 4 * model],
     )
 
 

time: 482 us -> 410 us (0.85)
  starting transfers between devices: 123 us -> 56.9 us
  Pallas kernels: 87.2 us -> 70 us
  between operations: 2.2 us -> 17.3 us
  local copies, waits for them, and re-layouts: 7.89 us -> 19.1 us
  waiting for transfers between devices: 144 us -> 134 us
  other arithmetic: 42.4 us -> 37.1 us
    ppermute x79 -> x31, waiting for transfers between devices: 116 us -> 40.7 us  [the longest x28 36.5 us: send(): return lax.ppermute(block, 'chip', ring_pairs(self.direction))]
    ppermute x79 -> x31, starting transfers between devices: 99.3 us -> 38.1 us  [the longest x28 35.2 us: send(): return lax.ppermute(block, 'chip', ring_pairs(self.direction))]
    psum x0 -> x1, waiting for transfers between devices: none -> 29.3 us  [local(): lax.psum(jnp.concatenate([product(attn_out, d_branch).astype(BF16), small...]
    pallas_call x5 -> x8, Pallas kernels: 35.1 us -> 18 us  [place(): pl.pallas_call(place_kernel, grid_spec=pltpu.PrefetchScalarGridSpec(num_s...]
    all_to_all x2, waiting for transfers between devices: 0.01 us -> 16.9 us  [to_heads(): return lax.all_to_all(blocks, 'chip', 0, 0, tiled=True)]
    ppermute x4, waiting for transfers between devices: 25.1 us -> 36.7 us  [head_sum(): lax.ppermute(low, 'head', [(0, 1), (1, 0)]).astype(F32)]
    unnamed x72 -> x100, local copies, waits for them, and re-layouts: 2.25 us -> 10.9 us
    add x12 -> x4, other arithmetic: 5.49 us -> 0.02 us  [the longest x3 0.02 us: local(): ends = ends + lax.ppermute(ends, 'chip', pairs)]
  transfers between devices with their start and end apart: 142 -> 66, of which waited for: 43 -> 21; matrix products, arithmetic and copies ran while one was open for 14% -> 15% of each run, Pallas kernels for 12% -> 11%
where the time goes in v3:
time: 410 us; the launch traced here: 405 us
  waiting for transfers between devices  134 us (33%)
  Pallas kernels  70 us (17%)
  starting transfers between devices  56.9 us (14%)
  blocking collectives  41.2 us (10%)
  other arithmetic  37.1 us (9%)
  matrix products  29 us (7%)
  local copies, waits for them, and re-layouts  19.1 us (5%)
  between operations  17.3 us (4%)
    all_to_all x2, blocking collectives, to_heads(): return lax.all_to_all(blocks, 'chip', 0, 0, tiled=True)  41.2 us
    ppermute x4, waiting for transfers between devices, head_sum(): lax.ppermute(low, 'head', [(0, 1), (1, 0)]).astype(F32)  36.7 us
    ppermute x28, waiting for transfers between devices, send(): return lax.ppermute(block, 'chip', ring_pairs(self.direction))  36.5 us
    ppermute x28, starting transfers between devices, send(): return lax.ppermute(block, 'chip', ring_pairs(self.direction))  35.2 us
    psum x1, waiting for transfers between devices, local(): lax.psum(jnp.concatenate([product(attn_out, d_branch).astype(BF16), small...  29.3 us
    pallas_call x4, Pallas kernels, backward_piece(): pl.pallas_call(body, grid=(groups,), in_specs=[query_spec(payload_rows, p...  28.5 us
    dot_general x17, matrix products, product(): lax.dot_general(first, second, (((first_axis,), (second_axis,)), ((), ())...  25.4 us
    pallas_call x1, Pallas kernels, attention_forward(): pl.pallas_call(functools.partial(forward_kernel, crops, key_step(count)),...  23.5 us
  transfers between devices with their start and end apart: 66, of which 21 were waited for; matrix products, arithmetic and copies ran while one was open for 15% of the time, Pallas kernels for 11%

profile of v3, /device:TPU:0, one launch (start us, length us, event | category | flops | bytes accessed | tf_op | source)
XLA Modules:
  0.0 404.7 jit_solution(13594292369077502562)
XLA Ops:
  14.9 1.7 fusion.14
  17.5 29.3 %all_to_all.20.query_ref.own.refs_0_.piece = bf16[8,208,256]{2,1,0:T(8,128)(2,1)S(1)} all-to-all(bf16[8,208,256]{2,1,0:T(8,128)(2,1)S(1)} %pad_maximum_fusion.1), channel_id=1, replica_groups=mesh['chip'=8,'core'=2,'head'=2] {'chip'}, dimensions={0} | all-to-all | bytes 1703936 | tf_op jit(solution)/shard_map/all_to_all | solution.py:231
  46.7 2.4 collective-permute-done.other.refs_4_.piece
  49.1 23.5 %attention_forward.1 = (f32[8,64,256]{2,1,0:T(8,128)S(1)}, bf16[8,64,256]{2,1,0:T(8,128)(2,1)S(1)}, f32[8,1,256]{2,1,0:T(1,128)S(1)}) custom-call(bf16[8,208,256]{2,1,0:T(8,128)(2,1)S(1)} %all_to_all.20.query_ref.own.refs_0_.piece, bf16[8,208,256]{2,1,0:T(8,128)(2,1)S(1)} %all_to_all.20.query_ref.own.refs_0_.piece, ...), custom_call_target="tpu_custom_call" | custom-call | flops 17179869184 | bytes 4194304 | tf_op jit(solution)/shard_map/attention_forward/pallas_call | solution.py:160
  72.6 12.0 %all_to_all.21 = bf16[8,64,256]{2,1,0:T(8,128)(2,1)S(1)} all-to-all(bf16[8,64,256]{2,1,0:T(8,128)(2,1)S(1)} %get-tuple-element.109), channel_id=1, replica_groups=mesh['chip'=8,'core'=2,'head'=2] {'chip'}, dimensions={0} | all-to-all | bytes 524288 | tf_op jit(solution)/shard_map/all_to_all | solution.py:231
  86.6 1.5 collective-permute-start.1
  88.1 10.9 %collective-permute-done.1 = bf16[256,1024]{1,0:T(8,128)(2,1)} collective-permute-done((bf16[256,1024]{1,0:T(8,128)(2,1)}, bf16[256,1024]{1,0:T(8,128)(2,1)}, u32[]{:S(2)}, u32[]{:S(2)}) %collective-permute-start.1) | collective-permute-done | bytes 524320 | tf_op jit(solution)/shard_map/ppermute | solution.py:490
  99.0 1.7 fusion.43
  103.5 7.6 %fusion.41 = (bf16[2048]{0:T(1024)(128)(2,1)}, bf16[256,2048]{1,0:T(8,128)(2,1)S(1)}, f32[256,2048]{1,0:T(8,128)S(1)}) fusion(f32[256,2048]{1,0:T(8,128)S(1)} %convolution_add_fusion, bf16[256,1024]{1,0:T(8,128)(2,1)} %param.19, bf16[2048,1024]{1,0:T(8,128)(2,1)S(1)} %copy-done.45), kind=kOutput, calls=%fused_computation.133 | convolution fusion | flops 1112012800 | bytes 9965568 | tf_op jit(solution)/shard_map/dot_general | solution.py:35
  113.3 1.6 collective-permute-start.8
  115.2 1.8 fusion.31
  117.3 1.5 convolution_convert_fusion.3
  120.4 2.2 convolution_add_fusion.2
  123.8 3.8 collective-permute-done.8
  127.8 11.7 %collective-permute-done.7 = bf16[128,1024]{1,0:T(8,128)(2,1)S(1)} collective-permute-done((bf16[128,1024]{1,0:T(8,128)(2,1)S(1)}, bf16[128,1024]{1,0:T(8,128)(2,1)S(1)}, u32[]{:S(2)}, u32[]{:S(2)}) %collective-permute-start.7) | collective-permute-done | bytes 262176 | tf_op jit(solution)/shard_map/ppermute | solution.py:407
  139.6 4.6 %collective-permute-start.11 = (bf16[128,1024]{1,0:T(8,128)(2,1)S(1)}, bf16[128,1024]{1,0:T(8,128)(2,1)S(1)}, u32[]{:S(2)}, u32[]{:S(2)}) collective-permute-start(bf16[128,1024]{1,0:T(8,128)(2,1)S(1)} %add_convert_fusion.17), channel_id=1, source_target_pairs={{0,4},{8,0},{16,8},{24,16},{28,24},{20,28},{12,20},{4,12},{1,5},{9... | collective-permute-start | bytes 786440 | tf_op jit(solution)/shard_map/ppermute | solution.py:407
  145.8 11.7 %collective-permute-done.9 = bf16[256,1024]{1,0:T(8,128)(2,1)S(1)} collective-permute-done((bf16[256,1024]{1,0:T(8,128)(2,1)S(1)}, bf16[256,1024]{1,0:T(8,128)(2,1)S(1)}, u32[]{:S(2)}, u32[]{:S(2)}) %collective-permute-start.9) | collective-permute-done | bytes 524320 | tf_op jit(solution)/shard_map/ppermute | solution.py:490
  157.6 3.0 fusion.40
  162.8 3.1 collective-permute-start.13
  166.7 4.1 %all-to-all-start.2 = ((bf16[8,64,256]{2,1,0:T(8,128)(2,1)}), bf16[8,64,256]{2,1,0:T(8,128)(2,1)S(1)}, u32[]{:S(2)}, u32[]{:S(2)}) async-start(bf16[8,64,256]{2,1,0:T(8,128)(2,1)} %bitcast.8), calls=%async_computation.2 | async-start | bytes 524288 | tf_op jit(solution)/shard_map/all_to_all | solution.py:231
  171.9 2.1 collective-permute-start.12
  174.0 5.9 %collective-permute-done.12 = bf16[128,1024]{1,0:T(8,128)(2,1)S(1)} collective-permute-done((bf16[128,1024]{1,0:T(8,128)(2,1)S(1)}, bf16[128,1024]{1,0:T(8,128)(2,1)S(1)}, u32[]{:S(2)}, u32[]{:S(2)}) %collective-permute-start.12) | collective-permute-done | bytes 262176 | tf_op jit(solution)/shard_map/ppermute | solution.py:407
  181.7 2.0 collective-permute-start.15
  184.9 7.1 %attention_backward.4 = (f32[8,64,256]{2,1,0:T(8,128)S(1)}, bf16[4,128,256]{2,1,0:T(8,128)(2,1)S(1)}) custom-call(bf16[8,208,256]{2,1,0:T(8,128)(2,1)S(1)} %all_to_all.20.query_ref.own.refs_0_.piece, bf16[8,64,256]{2,1,0:T(8,128)(2,1)S(1)} %all-to-all-done.2.refs_1_.grad_ref, f32[8,64,256]{2,1,0:T(8,128)S(1)} %get-tuple-element.121.refs_2_.raw_ref, ...), custom_call_target="tpu_custom_call" | custom-call | flops 8589934592 | bytes 4194304 | tf_op jit(solution)/shard_map/attention_backward/pallas_call | solution.py:194
  193.2 2.7 collective-permute-start.17
  197.1 7.1 %attention_backward.5 = (f32[8,64,256]{2,1,0:T(8,128)S(1)}, bf16[4,128,256]{2,1,0:T(8,128)(2,1)S(1)}) custom-call(bf16[8,208,256]{2,1,0:T(8,128)(2,1)S(1)} %all_to_all.20.query_ref.own.refs_0_.piece, bf16[8,64,256]{2,1,0:T(8,128)(2,1)S(1)} %all-to-all-done.2.refs_1_.grad_ref, f32[8,64,256]{2,1,0:T(8,128)S(1)} %get-tuple-element.121.refs_2_.raw_ref, ...), custom_call_target="tpu_custom_call" | custom-call | flops 8589934592 | bytes 4194304 | tf_op jit(solution)/shard_map/attention_backward/pallas_call | solution.py:194
  206.9 1.8 collective-permute-start.19
  210.1 7.2 %attention_backward.6 = (f32[8,64,256]{2,1,0:T(8,128)S(1)}, f32[4,128,256]{2,1,0:T(8,128)S(1)}) custom-call(bf16[8,208,256]{2,1,0:T(8,128)(2,1)S(1)} %all_to_all.20.query_ref.own.refs_0_.piece, bf16[8,64,256]{2,1,0:T(8,128)(2,1)S(1)} %all-to-all-done.2.refs_1_.grad_ref, f32[8,64,256]{2,1,0:T(8,128)S(1)} %get-tuple-element.121.refs_2_.raw_ref, ...), custom_call_target="tpu_custom_call" | custom-call | flops 8589934592 | bytes 4194304 | tf_op jit(solution)/shard_map/attention_backward/pallas_call | solution.py:194
  218.5 1.8 collective-permute-start.21
  221.7 7.1 %attention_backward.7 = (bf16[8,64,256]{2,1,0:T(8,128)(2,1)S(1)}, f32[4,128,256]{2,1,0:T(8,128)S(1)}) custom-call(bf16[8,208,256]{2,1,0:T(8,128)(2,1)S(1)} %all_to_all.20.query_ref.own.refs_0_.piece, bf16[8,64,256]{2,1,0:T(8,128)(2,1)S(1)} %all-to-all-done.2.refs_1_.grad_ref, f32[8,64,256]{2,1,0:T(8,128)S(1)} %get-tuple-element.121.refs_2_.raw_ref, ...), custom_call_target="tpu_custom_call" | custom-call | flops 8589934592 | bytes 4194304 | tf_op jit(solution)/shard_map/attention_backward/pallas_call | solution.py:194
  229.9 3.5 all-to-all-start.3
  238.0 1.9 collective-permute-start.26
  241.7 16.2 %all-to-all-done.3 = bf16[8,192,256]{2,1,0:T(8,128)(2,1)S(1)} async-done(((bf16[8,192,256]{2,1,0:T(8,128)(2,1)}), bf16[8,192,256]{2,1,0:T(8,128)(2,1)S(1)}, u32[]{:S(2)}, u32[]{:S(2)}) %all-to-all-start.3) | async-done | bytes 786464 | tf_op jit(solution)/shard_map/all_to_all | solution.py:231
  260.7 3.6 fusion.6
  268.2 2.0 collective-permute-start.29
  270.4 1.8 collective-permute-start.32
  272.4 10.3 %collective-permute-done.29 = bf16[256,1024]{1,0:T(8,128)(2,1)S(1)} collective-permute-done((bf16[256,1024]{1,0:T(8,128)(2,1)S(1)}, bf16[256,1024]{1,0:T(8,128)(2,1)S(1)}, u32[]{:S(2)}, u32[]{:S(2)}) %collective-permute-start.29) | collective-permute-done | bytes 524320 | tf_op jit(solution)/shard_map/ppermute | solution.py:490
  283.6 1.9 collective-permute-start.36
  285.7 1.7 collective-permute-start.38
  287.5 2.0 collective-permute-done.38
  289.5 2.2 collective-permute-done.34.refs_2_
  292.6 1.7 collective-permute-start.41
  295.9 5.4 %collective-permute-done.39.refs_2_ = bf16[128,1024]{1,0:T(8,128)(2,1)S(1)} collective-permute-done((bf16[128,1024]{1,0:T(8,128)(2,1)S(1)}, bf16[128,1024]{1,0:T(8,128)(2,1)S(1)}, u32[]{:S(2)}, u32[]{:S(2)}) %collective-permute-start.39) | collective-permute-done | bytes 262176 | tf_op jit(solution)/shard_map/ppermute | solution.py:407
  307.0 29.3 %all-reduce.3.cloned.1.call-done = bf16[528,1024]{1,0:T(8,128)(2,1)} async-done(((bf16[528,1024]{1,0:T(8,128)(2,1)}), bf16[528,1024]{1,0:T(8,128)(2,1)}) %all-reduce.3.cloned.1.call-update) | async-done | bytes 1081360 | tf_op jit(solution)/shard_map/psum | solution.py:618
  336.3 1.6 convert_element_type.327
  342.9 1.6 slice.95
  344.5 2.0 place.8
  346.5 4.2 %collective-permute-done.53 = f32[3,1024]{1,0:T(4,128)S(1)} collective-permute-done((f32[3,1024]{1,0:T(4,128)S(1)}, f32[3,1024]{1,0:T(4,128)S(1)}, u32[]{:S(2)}, u32[]{:S(2)}) %collective-permute-start.53) | collective-permute-done | bytes 12320 | tf_op jit(solution)/shard_map/ppermute | solution.py:677
  350.9 2.2 collective-permute-start.57
  353.3 5.7 %collective-permute-done.55.refs_2_ = bf16[128,1024]{1,0:T(8,128)(2,1)S(1)} collective-permute-done((bf16[128,1024]{1,0:T(8,128)(2,1)S(1)}, bf16[128,1024]{1,0:T(8,128)(2,1)S(1)}, u32[]{:S(2)}, u32[]{:S(2)}) %collective-permute-start.55) | collective-permute-done | bytes 262176 | tf_op jit(solution)/shard_map/ppermute | solution.py:407
  359.0 3.3 collective-permute-done.57.refs_4_
  364.1 2.0 place.9
  366.1 2.0 place.10
  368.1 2.0 place.11
  370.0 3.1 place.12
  373.1 3.0 place.13
  376.8 2.0 place.14
  378.7 2.0 place.15
  380.7 5.2 %all-gather.4.cloned.1.call-done = bf16[1536,1024]{1,0:T(8,128)(2,1)} async-done(((bf16[96,1024]{1,0:T(8,128)(2,1)}), bf16[1536,1024]{1,0:T(8,128)(2,1)}) %all-gather.4.cloned.1.call-update) | async-done | bytes 3145744 | tf_op jit(solution)/shard_map/all_gather | solution.py:651
  385.9 3.2 fusion.45
  389.4 1.8 copy.72
  391.6 1.8 copy.73
  393.4 1.5 convert_bitcast_fusion
  394.9 1.8 copy.74
  (286 shorter events, 67.5 us)
Async XLA Ops:
  8.0 252.7 %all-gather.6.cloned.1.call-start = ((), (), s32[]{:S(2)}) async-start(), calls=%async_computation.6 | async-start | bytes 4718592 | tf_op jit(solution)/shard_map/all_gather | solution.py:556
  46.7 2.4 collective-permute-start
  86.6 12.5 %collective-permute-start.1 = (bf16[256,1024]{1,0:T(8,128)(2,1)}, bf16[256,1024]{1,0:T(8,128)(2,1)}, u32[]{:S(2)}, u32[]{:S(2)}) collective-permute-start(bf16[256,1024]{1,0:T(8,128)(2,1)} %convolution_convert_fusion.1), channel_id=1, source_target_pairs={{0,1},{1,0},{2,3},{3,2},{4,5},{5,4},{6,7},{7,6},{8,9},{9,8},{10,11... | collective-permute-start | bytes 1572872 | tf_op jit(solution)/shard_map/ppermute | solution.py:490
  88.1 32.3 %collective-permute-start.3 = (bf16[256,1024]{1,0:T(8,128)(2,1)}, bf16[256,1024]{1,0:T(8,128)(2,1)}, u32[]{:S(2)}, u32[]{:S(2)}) collective-permute-start(bf16[256,1024]{1,0:T(8,128)(2,1)} %param.19), channel_id=1, source_target_pairs={{0,2},{2,0},{1,3},{3,1},{4,6},{6,4},{5,7},{7,5},{8,10},{10,8},{9,1... | collective-permute-start | bytes 1572872 | tf_op jit(solution)/shard_map/ppermute | solution.py:227
  101.3 17.6 %collective-permute-start.5 = (bf16[256,1024]{1,0:T(8,128)(2,1)S(1)}, bf16[256,1024]{1,0:T(8,128)(2,1)S(1)}, u32[]{:S(2)}, u32[]{:S(2)}) collective-permute-start(bf16[256,1024]{1,0:T(8,128)(2,1)S(1)} %add_convert_fusion.2), channel_id=1, source_target_pairs={{0,2},{2,0},{1,3},{3,1},{4,6},{6,4},{5,7},{7,5},{8,10},{10,8},{9,1... | collective-permute-start | bytes 1572872 | tf_op jit(solution)/shard_map/ppermute | solution.py:227
  113.2 5.6 %collective-permute-start.6 = (bf16[256,1024]{1,0:T(8,128)(2,1)S(1)}, bf16[256,1024]{1,0:T(8,128)(2,1)S(1)}, u32[]{:S(2)}, u32[]{:S(2)}) collective-permute-start(bf16[256,1024]{1,0:T(8,128)(2,1)S(1)} %constant_dynamic-slice_fusion.1), channel_id=1, source_target_pairs={{0,2},{2,0},{1,3},{3,1},{4,6},{6,4},{5,7},{7,5},{8,10},{10,8},{9,1... | collective-permute-start | bytes 1572872 | tf_op jit(solution)/shard_map/ppermute | solution.py:227
  113.3 14.3 %collective-permute-start.8 = (bf16[256,1024]{1,0:T(8,128)(2,1)S(1)}, bf16[256,1024]{1,0:T(8,128)(2,1)S(1)}, u32[]{:S(2)}, u32[]{:S(2)}) collective-permute-start(bf16[256,1024]{1,0:T(8,128)(2,1)S(1)} %convolution_convert_fusion.2), channel_id=1, source_target_pairs={{0,1},{1,0},{2,3},{3,2},{4,5},{5,4},{6,7},{7,6},{8,9},{9,8},{10,11... | collective-permute-start | bytes 1572872 | tf_op jit(solution)/shard_map/ppermute | solution.py:490
  117.1 3.3 collective-permute-start.2
  119.7 19.8 %collective-permute-start.7 = (bf16[128,1024]{1,0:T(8,128)(2,1)S(1)}, bf16[128,1024]{1,0:T(8,128)(2,1)S(1)}, u32[]{:S(2)}, u32[]{:S(2)}) collective-permute-start(bf16[128,1024]{1,0:T(8,128)(2,1)S(1)} %dynamic-slice_convert_fusion), channel_id=1, source_target_pairs={{0,4},{8,0},{16,8},{24,16},{28,24},{20,28},{12,20},{4,12},{1,5},{9... | collective-permute-start | bytes 786440 | tf_op jit(solution)/shard_map/ppermute | solution.py:407
  122.7 16.8 %collective-permute-start.4 = (bf16[128,1024]{1,0:T(8,128)(2,1)S(1)}, bf16[128,1024]{1,0:T(8,128)(2,1)S(1)}, u32[]{:S(2)}, u32[]{:S(2)}) collective-permute-start(bf16[128,1024]{1,0:T(8,128)(2,1)S(1)} %dynamic-slice_convert_fusion.1), channel_id=1, source_target_pairs={{0,8},{8,16},{16,24},{24,28},{28,20},{20,12},{12,4},{4,0},{1,9},{9... | collective-permute-start | bytes 786440 | tf_op jit(solution)/shard_map/ppermute | solution.py:407
  139.6 22.5 %collective-permute-start.11 = (bf16[128,1024]{1,0:T(8,128)(2,1)S(1)}, bf16[128,1024]{1,0:T(8,128)(2,1)S(1)}, u32[]{:S(2)}, u32[]{:S(2)}) collective-permute-start(bf16[128,1024]{1,0:T(8,128)(2,1)S(1)} %add_convert_fusion.17), channel_id=1, source_target_pairs={{0,4},{8,0},{16,8},{24,16},{28,24},{20,28},{12,20},{4,12},{1,5},{9... | collective-permute-start | bytes 786440 | tf_op jit(solution)/shard_map/ppermute | solution.py:407
  144.3 17.8 %collective-permute-start.10 = (bf16[128,1024]{1,0:T(8,128)(2,1)S(1)}, bf16[128,1024]{1,0:T(8,128)(2,1)S(1)}, u32[]{:S(2)}, u32[]{:S(2)}) collective-permute-start(bf16[128,1024]{1,0:T(8,128)(2,1)S(1)} %add_convert_fusion.18), channel_id=1, source_target_pairs={{0,8},{8,16},{16,24},{24,28},{28,20},{20,12},{12,4},{4,0},{1,9},{9... | collective-permute-start | bytes 786440 | tf_op jit(solution)/shard_map/ppermute | solution.py:407
  144.4 13.2 %collective-permute-start.9 = (bf16[256,1024]{1,0:T(8,128)(2,1)S(1)}, bf16[256,1024]{1,0:T(8,128)(2,1)S(1)}, u32[]{:S(2)}, u32[]{:S(2)}) collective-permute-start(bf16[256,1024]{1,0:T(8,128)(2,1)S(1)} %convolution_convert_fusion.3), channel_id=1, source_target_pairs={{0,1},{1,0},{2,3},{3,2},{4,5},{5,4},{6,7},{7,6},{8,9},{9,8},{10,11... | collective-permute-start | bytes 1572872 | tf_op jit(solution)/shard_map/ppermute | solution.py:490
  162.8 11.2 %collective-permute-start.13 = (bf16[128,1024]{1,0:T(8,128)(2,1)S(1)}, bf16[128,1024]{1,0:T(8,128)(2,1)S(1)}, u32[]{:S(2)}, u32[]{:S(2)}) collective-permute-start(bf16[128,1024]{1,0:T(8,128)(2,1)S(1)} %add_convert_fusion.15), channel_id=1, source_target_pairs={{0,4},{8,0},{16,8},{24,16},{28,24},{20,28},{12,20},{4,12},{1,5},{9... | collective-permute-start | bytes 786440 | tf_op jit(solution)/shard_map/ppermute | solution.py:407
  166.7 13.9 %all-to-all-start.2 = ((bf16[8,64,256]{2,1,0:T(8,128)(2,1)}), bf16[8,64,256]{2,1,0:T(8,128)(2,1)S(1)}, u32[]{:S(2)}, u32[]{:S(2)}) async-start(bf16[8,64,256]{2,1,0:T(8,128)(2,1)} %bitcast.8), calls=%async_computation.2 | async-start | bytes 524288 | tf_op jit(solution)/shard_map/all_to_all | solution.py:231
  171.9 8.0 %collective-permute-start.12 = (bf16[128,1024]{1,0:T(8,128)(2,1)S(1)}, bf16[128,1024]{1,0:T(8,128)(2,1)S(1)}, u32[]{:S(2)}, u32[]{:S(2)}) collective-permute-start(bf16[128,1024]{1,0:T(8,128)(2,1)S(1)} %add_convert_fusion.16), channel_id=1, source_target_pairs={{0,8},{8,16},{16,24},{24,28},{28,20},{20,12},{12,4},{4,0},{1,9},{9... | collective-permute-start | bytes 786440 | tf_op jit(solution)/shard_map/ppermute | solution.py:407
  181.7 10.4 %collective-permute-start.15 = (bf16[128,1024]{1,0:T(8,128)(2,1)S(1)}, bf16[128,1024]{1,0:T(8,128)(2,1)S(1)}, u32[]{:S(2)}, u32[]{:S(2)}) collective-permute-start(bf16[128,1024]{1,0:T(8,128)(2,1)S(1)} %add_convert_fusion.13), channel_id=1, source_target_pairs={{0,4},{8,0},{16,8},{24,16},{28,24},{20,28},{12,20},{4,12},{1,5},{9... | collective-permute-start | bytes 786440 | tf_op jit(solution)/shard_map/ppermute | solution.py:407
  184.8 7.3 %collective-permute-start.14 = (bf16[128,1024]{1,0:T(8,128)(2,1)S(1)}, bf16[128,1024]{1,0:T(8,128)(2,1)S(1)}, u32[]{:S(2)}, u32[]{:S(2)}) collective-permute-start(bf16[128,1024]{1,0:T(8,128)(2,1)S(1)} %add_convert_fusion.14), channel_id=1, source_target_pairs={{0,8},{8,16},{16,24},{24,28},{28,20},{20,12},{12,4},{4,0},{1,9},{9... | collective-permute-start | bytes 786440 | tf_op jit(solution)/shard_map/ppermute | solution.py:407
  192.0 25.2 %collective-permute-start.22 = (bf16[4,128,256]{2,1,0:T(8,128)(2,1)S(1)}, bf16[4,128,256]{2,1,0:T(8,128)(2,1)S(1)}, u32[]{:S(2)}, u32[]{:S(2)}) collective-permute-start(bf16[4,128,256]{2,1,0:T(8,128)(2,1)S(1)} %get-tuple-element.140), channel_id=1, source_target_pairs={{0,2},{2,0},{1,3},{3,1},{4,6},{6,4},{5,7},{7,5},{8,10},{10,8},{9,1... | collective-permute-start | bytes 786440 | tf_op jit(solution)/shard_map/ppermute | solution.py:227
  193.2 11.2 %collective-permute-start.17 = (bf16[128,1024]{1,0:T(8,128)(2,1)S(1)}, bf16[128,1024]{1,0:T(8,128)(2,1)S(1)}, u32[]{:S(2)}, u32[]{:S(2)}) collective-permute-start(bf16[128,1024]{1,0:T(8,128)(2,1)S(1)} %add_convert_fusion.11), channel_id=1, source_target_pairs={{0,4},{8,0},{16,8},{24,16},{28,24},{20,28},{12,20},{4,12},{1,5},{9... | collective-permute-start | bytes 786440 | tf_op jit(solution)/shard_map/ppermute | solution.py:407
  197.0 8.7 %collective-permute-start.16 = (bf16[128,1024]{1,0:T(8,128)(2,1)S(1)}, bf16[128,1024]{1,0:T(8,128)(2,1)S(1)}, u32[]{:S(2)}, u32[]{:S(2)}) collective-permute-start(bf16[128,1024]{1,0:T(8,128)(2,1)S(1)} %add_convert_fusion.12), channel_id=1, source_target_pairs={{0,8},{8,16},{16,24},{24,28},{28,20},{20,12},{12,4},{4,0},{1,9},{9... | collective-permute-start | bytes 786440 | tf_op jit(solution)/shard_map/ppermute | solution.py:407
  204.2 24.6 %collective-permute-start.23 = (bf16[4,128,256]{2,1,0:T(8,128)(2,1)S(1)}, bf16[4,128,256]{2,1,0:T(8,128)(2,1)S(1)}, u32[]{:S(2)}, u32[]{:S(2)}) collective-permute-start(bf16[4,128,256]{2,1,0:T(8,128)(2,1)S(1)} %get-tuple-element.142), channel_id=1, source_target_pairs={{0,2},{2,0},{1,3},{3,1},{4,6},{6,4},{5,7},{7,5},{8,10},{10,8},{9,1... | collective-permute-start | bytes 786440 | tf_op jit(solution)/shard_map/ppermute | solution.py:227
  206.9 10.5 %collective-permute-start.19 = (bf16[128,1024]{1,0:T(8,128)(2,1)S(1)}, bf16[128,1024]{1,0:T(8,128)(2,1)S(1)}, u32[]{:S(2)}, u32[]{:S(2)}) collective-permute-start(bf16[128,1024]{1,0:T(8,128)(2,1)S(1)} %add_convert_fusion.9), channel_id=1, source_target_pairs={{0,4},{8,0},{16,8},{24,16},{28,24},{20,28},{12,20},{4,12},{1,5},{9... | collective-permute-start | bytes 786440 | tf_op jit(solution)/shard_map/ppermute | solution.py:407
  209.8 7.6 %collective-permute-start.18 = (bf16[128,1024]{1,0:T(8,128)(2,1)S(1)}, bf16[128,1024]{1,0:T(8,128)(2,1)S(1)}, u32[]{:S(2)}, u32[]{:S(2)}) collective-permute-start(bf16[128,1024]{1,0:T(8,128)(2,1)S(1)} %add_convert_fusion.10), channel_id=1, source_target_pairs={{0,8},{8,16},{16,24},{24,28},{28,20},{20,12},{12,4},{4,0},{1,9},{9... | collective-permute-start | bytes 786440 | tf_op jit(solution)/shard_map/ppermute | solution.py:407
  218.5 11.5 %collective-permute-start.21 = (bf16[128,1024]{1,0:T(8,128)(2,1)S(1)}, bf16[128,1024]{1,0:T(8,128)(2,1)}, u32[]{:S(2)}, u32[]{:S(2)}) collective-permute-start(bf16[128,1024]{1,0:T(8,128)(2,1)S(1)} %add_convert_fusion.7), channel_id=1, source_target_pairs={{0,4},{8,0},{16,8},{24,16},{28,24},{20,28},{12,20},{4,12},{1,5},{9... | collective-permute-start | bytes 786440 | tf_op jit(solution)/shard_map/ppermute | solution.py:407
  221.4 8.6 %collective-permute-start.20 = (bf16[128,1024]{1,0:T(8,128)(2,1)S(1)}, bf16[128,1024]{1,0:T(8,128)(2,1)}, u32[]{:S(2)}, u32[]{:S(2)}) collective-permute-start(bf16[128,1024]{1,0:T(8,128)(2,1)S(1)} %add_convert_fusion.8), channel_id=1, source_target_pairs={{0,8},{8,16},{16,24},{24,28},{28,20},{20,12},{12,4},{4,0},{1,9},{9... | collective-permute-start | bytes 786440 | tf_op jit(solution)/shard_map/ppermute | solution.py:407
  229.9 28.0 %all-to-all-start.3 = ((bf16[8,192,256]{2,1,0:T(8,128)(2,1)}), bf16[8,192,256]{2,1,0:T(8,128)(2,1)S(1)}, u32[]{:S(2)}, u32[]{:S(2)}) async-start(bf16[8,192,256]{2,1,0:T(8,128)(2,1)} %maximum_maximum_fusion), calls=%async_computation.3 | async-start | bytes 1572864 | tf_op jit(solution)/shard_map/all_to_all | solution.py:231
  233.5 102.8 %all-reduce.3.cloned.1.call-start = ((), (), s32[]{:S(2)}) async-start(), calls=%async_computation.5 | async-start | bytes 2162688 | tf_op jit(solution)/shard_map/psum | solution.py:618
  236.7 149.2 %all-gather.4.cloned.1.call-start = ((), (), s32[]{:S(2)}) async-start(), calls=%async_computation.4 | async-start | bytes 3342336 | tf_op jit(solution)/shard_map/all_gather | solution.py:651
  238.0 28.6 %collective-permute-start.26 = (bf16[128,1024]{1,0:T(8,128)(2,1)S(1)}, bf16[128,1024]{1,0:T(8,128)(2,1)S(1)}, u32[]{:S(2)}, u32[]{:S(2)}) collective-permute-start(bf16[128,1024]{1,0:T(8,128)(2,1)S(1)} %add_convert_fusion.3.refs_2_), channel_id=1, source_target_pairs={{0,4},{8,0},{16,8},{24,16},{28,24},{20,28},{12,20},{4,12},{1,5},{9... | collective-permute-start | bytes 786440 | tf_op jit(solution)/shard_map/ppermute | solution.py:407
  239.9 26.7 %collective-permute-start.27 = (bf16[128,1024]{1,0:T(8,128)(2,1)S(1)}, bf16[128,1024]{1,0:T(8,128)(2,1)S(1)}, u32[]{:S(2)}, u32[]{:S(2)}) collective-permute-start(bf16[128,1024]{1,0:T(8,128)(2,1)S(1)} %add_convert_fusion.3.refs_2_), channel_id=1, source_target_pairs={{0,2},{2,0},{1,3},{3,1},{4,6},{6,4},{5,7},{7,5},{8,10},{10,8},{9,1... | collective-permute-start | bytes 786440 | tf_op jit(solution)/shard_map/ppermute | solution.py:227
  241.1 25.6 %collective-permute-start.24 = (bf16[128,1024]{1,0:T(8,128)(2,1)S(1)}, bf16[128,1024]{1,0:T(8,128)(2,1)S(1)}, u32[]{:S(2)}, u32[]{:S(2)}) collective-permute-start(bf16[128,1024]{1,0:T(8,128)(2,1)S(1)} %add_convert_fusion.4.refs_0_), channel_id=1, source_target_pairs={{0,8},{8,16},{16,24},{24,28},{28,20},{20,12},{12,4},{4,0},{1,9},{9... | collective-permute-start | bytes 786440 | tf_op jit(solution)/shard_map/ppermute | solution.py:407
  241.3 25.4 %collective-permute-start.25 = (bf16[128,1024]{1,0:T(8,128)(2,1)S(1)}, bf16[128,1024]{1,0:T(8,128)(2,1)S(1)}, u32[]{:S(2)}, u32[]{:S(2)}) collective-permute-start(bf16[128,1024]{1,0:T(8,128)(2,1)S(1)} %add_convert_fusion.4.refs_0_), channel_id=1, source_target_pairs={{0,2},{2,0},{1,3},{3,1},{4,6},{6,4},{5,7},{7,5},{8,10},{10,8},{9,1... | collective-permute-start | bytes 786440 | tf_op jit(solution)/shard_map/ppermute | solution.py:227
  268.2 14.5 %collective-permute-start.29 = (bf16[256,1024]{1,0:T(8,128)(2,1)S(1)}, bf16[256,1024]{1,0:T(8,128)(2,1)S(1)}, u32[]{:S(2)}, u32[]{:S(2)}) collective-permute-start(bf16[256,1024]{1,0:T(8,128)(2,1)S(1)} %convert_element_type.312), channel_id=1, source_target_pairs={{0,1},{1,0},{2,3},{3,2},{4,5},{5,4},{6,7},{7,6},{8,9},{9,8},{10,11... | collective-permute-start | bytes 1572872 | tf_op jit(solution)/shard_map/ppermute | solution.py:490
  270.2 13.2 %collective-permute-start.30 = (bf16[128,1024]{1,0:T(8,128)(2,1)S(1)}, bf16[128,1024]{1,0:T(8,128)(2,1)S(1)}, u32[]{:S(2)}, u32[]{:S(2)}) collective-permute-start(bf16[128,1024]{1,0:T(8,128)(2,1)S(1)} %collective-permute-done.24.refs_2_), channel_id=1, source_target_pairs={{0,8},{8,16},{16,24},{24,28},{28,20},{20,12},{12,4},{4,0},{1,9},{9... | collective-permute-start | bytes 786440 | tf_op jit(solution)/shard_map/ppermute | solution.py:407
  270.2 13.2 %collective-permute-start.31 = (bf16[128,1024]{1,0:T(8,128)(2,1)S(1)}, bf16[128,1024]{1,0:T(8,128)(2,1)S(1)}, u32[]{:S(2)}, u32[]{:S(2)}) collective-permute-start(bf16[128,1024]{1,0:T(8,128)(2,1)S(1)} %collective-permute-done.24.refs_2_), channel_id=1, source_target_pairs={{0,2},{2,0},{1,3},{3,1},{4,6},{6,4},{5,7},{7,5},{8,10},{10,8},{9,1... | collective-permute-start | bytes 786440 | tf_op jit(solution)/shard_map/ppermute | solution.py:227
  270.4 13.0 %collective-permute-start.32 = (bf16[128,1024]{1,0:T(8,128)(2,1)S(1)}, bf16[128,1024]{1,0:T(8,128)(2,1)S(1)}, u32[]{:S(2)}, u32[]{:S(2)}) collective-permute-start(bf16[128,1024]{1,0:T(8,128)(2,1)S(1)} %collective-permute-done.26.refs_4_), channel_id=1, source_target_pairs={{0,4},{8,0},{16,8},{24,16},{28,24},{20,28},{12,20},{4,12},{1,5},{9... | collective-permute-start | bytes 786440 | tf_op jit(solution)/shard_map/ppermute | solution.py:407
  272.2 11.2 %collective-permute-start.33 = (bf16[128,1024]{1,0:T(8,128)(2,1)S(1)}, bf16[128,1024]{1,0:T(8,128)(2,1)S(1)}, u32[]{:S(2)}, u32[]{:S(2)}) collective-permute-start(bf16[128,1024]{1,0:T(8,128)(2,1)S(1)} %collective-permute-done.26.refs_4_), channel_id=1, source_target_pairs={{0,2},{2,0},{1,3},{3,1},{4,6},{6,4},{5,7},{7,5},{8,10},{10,8},{9,1... | collective-permute-start | bytes 786440 | tf_op jit(solution)/shard_map/ppermute | solution.py:227
  283.4 8.2 %collective-permute-start.34 = (bf16[128,1024]{1,0:T(8,128)(2,1)S(1)}, bf16[128,1024]{1,0:T(8,128)(2,1)S(1)}, u32[]{:S(2)}, u32[]{:S(2)}) collective-permute-start(bf16[128,1024]{1,0:T(8,128)(2,1)S(1)} %collective-permute-done.30.refs_2_), channel_id=1, source_target_pairs={{0,8},{8,16},{16,24},{24,28},{28,20},{20,12},{12,4},{4,0},{1,9},{9... | collective-permute-start | bytes 786440 | tf_op jit(solution)/shard_map/ppermute | solution.py:407
  283.5 8.2 %collective-permute-start.35 = (bf16[128,1024]{1,0:T(8,128)(2,1)S(1)}, bf16[128,1024]{1,0:T(8,128)(2,1)S(1)}, u32[]{:S(2)}, u32[]{:S(2)}) collective-permute-start(bf16[128,1024]{1,0:T(8,128)(2,1)S(1)} %collective-permute-done.30.refs_2_), channel_id=1, source_target_pairs={{0,2},{2,0},{1,3},{3,1},{4,6},{6,4},{5,7},{7,5},{8,10},{10,8},{9,1... | collective-permute-start | bytes 786440 | tf_op jit(solution)/shard_map/ppermute | solution.py:227
  283.6 8.8 %collective-permute-start.36 = (bf16[128,1024]{1,0:T(8,128)(2,1)S(1)}, bf16[128,1024]{1,0:T(8,128)(2,1)S(1)}, u32[]{:S(2)}, u32[]{:S(2)}) collective-permute-start(bf16[128,1024]{1,0:T(8,128)(2,1)S(1)} %collective-permute-done.32.refs_4_), channel_id=1, source_target_pairs={{0,4},{8,0},{16,8},{24,16},{28,24},{20,28},{12,20},{4,12},{1,5},{9... | collective-permute-start | bytes 786440 | tf_op jit(solution)/shard_map/ppermute | solution.py:407
  285.5 6.8 %collective-permute-start.37 = (bf16[128,1024]{1,0:T(8,128)(2,1)S(1)}, bf16[128,1024]{1,0:T(8,128)(2,1)S(1)}, u32[]{:S(2)}, u32[]{:S(2)}) collective-permute-start(bf16[128,1024]{1,0:T(8,128)(2,1)S(1)} %collective-permute-done.32.refs_4_), channel_id=1, source_target_pairs={{0,2},{2,0},{1,3},{3,1},{4,6},{6,4},{5,7},{7,5},{8,10},{10,8},{9,1... | collective-permute-start | bytes 786440 | tf_op jit(solution)/shard_map/ppermute | solution.py:227
  285.7 3.7 collective-permute-start.38
  292.3 9.0 %collective-permute-start.39 = (bf16[128,1024]{1,0:T(8,128)(2,1)S(1)}, bf16[128,1024]{1,0:T(8,128)(2,1)S(1)}, u32[]{:S(2)}, u32[]{:S(2)}) collective-permute-start(bf16[128,1024]{1,0:T(8,128)(2,1)S(1)} %collective-permute-done.34.refs_2_), channel_id=1, source_target_pairs={{0,8},{8,16},{16,24},{24,28},{28,20},{20,12},{12,4},{4,0},{1,9},{9... | collective-permute-start | bytes 786440 | tf_op jit(solution)/shard_map/ppermute | solution.py:407
  292.6 8.7 %collective-permute-start.40 = (bf16[128,1024]{1,0:T(8,128)(2,1)S(1)}, bf16[128,1024]{1,0:T(8,128)(2,1)S(1)}, u32[]{:S(2)}, u32[]{:S(2)}) collective-permute-start(bf16[128,1024]{1,0:T(8,128)(2,1)S(1)} %collective-permute-done.34.refs_2_), channel_id=1, source_target_pairs={{0,2},{2,0},{1,3},{3,1},{4,6},{6,4},{5,7},{7,5},{8,10},{10,8},{9,1... | collective-permute-start | bytes 786440 | tf_op jit(solution)/shard_map/ppermute | solution.py:227
  292.6 9.7 %collective-permute-start.41 = (bf16[128,1024]{1,0:T(8,128)(2,1)S(1)}, bf16[128,1024]{1,0:T(8,128)(2,1)}, u32[]{:S(2)}, u32[]{:S(2)}) collective-permute-start(bf16[128,1024]{1,0:T(8,128)(2,1)S(1)} %collective-permute-done.36.refs_4_), channel_id=1, source_target_pairs={{0,4},{8,0},{16,8},{24,16},{28,24},{20,28},{12,20},{4,12},{1,5},{9... | collective-permute-start | bytes 786440 | tf_op jit(solution)/shard_map/ppermute | solution.py:407
  294.3 8.0 %collective-permute-start.42 = (bf16[128,1024]{1,0:T(8,128)(2,1)S(1)}, bf16[128,1024]{1,0:T(8,128)(2,1)S(1)}, u32[]{:S(2)}, u32[]{:S(2)}) collective-permute-start(bf16[128,1024]{1,0:T(8,128)(2,1)S(1)} %collective-permute-done.36.refs_4_), channel_id=1, source_target_pairs={{0,2},{2,0},{1,3},{3,1},{4,6},{6,4},{5,7},{7,5},{8,10},{10,8},{9,1... | collective-permute-start | bytes 786440 | tf_op jit(solution)/shard_map/ppermute | solution.py:227
  303.1 34.8 %collective-permute-start.44 = (bf16[128,1024]{1,0:T(8,128)(2,1)S(1)}, bf16[128,1024]{1,0:T(8,128)(2,1)}, u32[]{:S(2)}, u32[]{:S(2)}) collective-permute-start(bf16[128,1024]{1,0:T(8,128)(2,1)S(1)} %collective-permute-done.39.refs_2_), channel_id=1, source_target_pairs={{0,8},{8,16},{16,24},{24,28},{28,20},{20,12},{12,4},{4,0},{1,9},{9... | collective-permute-start | bytes 786440 | tf_op jit(solution)/shard_map/ppermute | solution.py:407
  303.6 34.3 %collective-permute-start.45 = (bf16[128,1024]{1,0:T(8,128)(2,1)S(1)}, bf16[128,1024]{1,0:T(8,128)(2,1)}, u32[]{:S(2)}, u32[]{:S(2)}) collective-permute-start(bf16[128,1024]{1,0:T(8,128)(2,1)S(1)} %collective-permute-done.39.refs_2_), channel_id=1, source_target_pairs={{0,2},{2,0},{1,3},{3,1},{4,6},{6,4},{5,7},{7,5},{8,10},{10,8},{9,1... | collective-permute-start | bytes 786440 | tf_op jit(solution)/shard_map/ppermute | solution.py:227
  303.6 34.3 %collective-permute-start.46 = (bf16[128,1024]{1,0:T(8,128)(2,1)}, bf16[128,1024]{1,0:T(8,128)(2,1)}, u32[]{:S(2)}, u32[]{:S(2)}) collective-permute-start(bf16[128,1024]{1,0:T(8,128)(2,1)} %collective-permute-done.41.refs_4_), channel_id=1, source_target_pairs={{0,4},{8,0},{16,8},{24,16},{28,24},{20,28},{12,20},{4,12},{1,5},{9... | collective-permute-start | bytes 786440 | tf_op jit(solution)/shard_map/ppermute | solution.py:407
  305.1 32.8 %collective-permute-start.47 = (bf16[128,1024]{1,0:T(8,128)(2,1)}, bf16[128,1024]{1,0:T(8,128)(2,1)}, u32[]{:S(2)}, u32[]{:S(2)}) collective-permute-start(bf16[128,1024]{1,0:T(8,128)(2,1)} %collective-permute-done.41.refs_4_), channel_id=1, source_target_pairs={{0,2},{2,0},{1,3},{3,1},{4,6},{6,4},{5,7},{7,5},{8,10},{10,8},{9,1... | collective-permute-start | bytes 786440 | tf_op jit(solution)/shard_map/ppermute | solution.py:227
  305.5 32.4 %collective-permute-start.48 = (f32[3,1024]{1,0:T(4,128)S(1)}, f32[3,1024]{1,0:T(4,128)S(1)}, u32[]{:S(2)}, u32[]{:S(2)}) collective-permute-start(f32[3,1024]{1,0:T(4,128)S(1)} %add.352), channel_id=1, source_target_pairs={{0,4},{4,0},{8,12},{12,8},{16,20},{20,16},{24,28},{28,24},{1,5},{5... | collective-permute-start | bytes 36872 | tf_op jit(solution)/shard_map/ppermute | solution.py:677
  337.9 12.8 %collective-permute-start.49 = (bf16[128,1024]{1,0:T(8,128)(2,1)}, bf16[128,1024]{1,0:T(8,128)(2,1)S(1)}, u32[]{:S(2)}, u32[]{:S(2)}) collective-permute-start(bf16[128,1024]{1,0:T(8,128)(2,1)} %collective-permute-done.44.refs_2_), channel_id=1, source_target_pairs={{0,8},{8,16},{16,24},{24,28},{28,20},{20,12},{12,4},{4,0},{1,9},{9... | collective-permute-start | bytes 786440 | tf_op jit(solution)/shard_map/ppermute | solution.py:407
  339.4 11.3 %collective-permute-start.50 = (bf16[128,1024]{1,0:T(8,128)(2,1)}, bf16[128,1024]{1,0:T(8,128)(2,1)S(1)}, u32[]{:S(2)}, u32[]{:S(2)}) collective-permute-start(bf16[128,1024]{1,0:T(8,128)(2,1)} %collective-permute-done.44.refs_2_), channel_id=1, source_target_pairs={{0,2},{2,0},{1,3},{3,1},{4,6},{6,4},{5,7},{7,5},{8,10},{10,8},{9,1... | collective-permute-start | bytes 786440 | tf_op jit(solution)/shard_map/ppermute | solution.py:227
  339.4 11.3 %collective-permute-start.51 = (bf16[128,1024]{1,0:T(8,128)(2,1)}, bf16[128,1024]{1,0:T(8,128)(2,1)S(1)}, u32[]{:S(2)}, u32[]{:S(2)}) collective-permute-start(bf16[128,1024]{1,0:T(8,128)(2,1)} %collective-permute-done.46.refs_4_), channel_id=1, source_target_pairs={{0,4},{8,0},{16,8},{24,16},{28,24},{20,28},{12,20},{4,12},{1,5},{9... | collective-permute-start | bytes 786440 | tf_op jit(solution)/shard_map/ppermute | solution.py:407
  340.0 10.7 %collective-permute-start.52 = (bf16[128,1024]{1,0:T(8,128)(2,1)}, bf16[128,1024]{1,0:T(8,128)(2,1)S(1)}, u32[]{:S(2)}, u32[]{:S(2)}) collective-permute-start(bf16[128,1024]{1,0:T(8,128)(2,1)} %collective-permute-done.46.refs_4_), channel_id=1, source_target_pairs={{0,2},{2,0},{1,3},{3,1},{4,6},{6,4},{5,7},{7,5},{8,10},{10,8},{9,1... | collective-permute-start | bytes 786440 | tf_op jit(solution)/shard_map/ppermute | solution.py:227
  340.2 10.4 %collective-permute-start.53 = (f32[3,1024]{1,0:T(4,128)S(1)}, f32[3,1024]{1,0:T(4,128)S(1)}, u32[]{:S(2)}, u32[]{:S(2)}) collective-permute-start(f32[3,1024]{1,0:T(4,128)S(1)} %add.353), channel_id=1, source_target_pairs={{0,8},{4,12},{8,0},{12,4},{16,24},{20,28},{24,16},{28,20},{1,9},{5... | collective-permute-start | bytes 36872 | tf_op jit(solution)/shard_map/ppermute | solution.py:677
  350.7 8.3 %collective-permute-start.55 = (bf16[128,1024]{1,0:T(8,128)(2,1)S(1)}, bf16[128,1024]{1,0:T(8,128)(2,1)S(1)}, u32[]{:S(2)}, u32[]{:S(2)}) collective-permute-start(bf16[128,1024]{1,0:T(8,128)(2,1)S(1)} %collective-permute-done.49.refs_2_), channel_id=1, source_target_pairs={{0,8},{8,16},{16,24},{24,28},{28,20},{20,12},{12,4},{4,0},{1,9},{9... | collective-permute-start | bytes 786440 | tf_op jit(solution)/shard_map/ppermute | solution.py:407
  350.8 8.2 %collective-permute-start.56 = (bf16[128,1024]{1,0:T(8,128)(2,1)S(1)}, bf16[128,1024]{1,0:T(8,128)(2,1)S(1)}, u32[]{:S(2)}, u32[]{:S(2)}) collective-permute-start(bf16[128,1024]{1,0:T(8,128)(2,1)S(1)} %collective-permute-done.49.refs_2_), channel_id=1, source_target_pairs={{0,2},{2,0},{1,3},{3,1},{4,6},{6,4},{5,7},{7,5},{8,10},{10,8},{9,1... | collective-permute-start | bytes 786440 | tf_op jit(solution)/shard_map/ppermute | solution.py:227
  350.9 11.5 %collective-permute-start.57 = (bf16[128,1024]{1,0:T(8,128)(2,1)S(1)}, bf16[128,1024]{1,0:T(8,128)(2,1)S(1)}, u32[]{:S(2)}, u32[]{:S(2)}) collective-permute-start(bf16[128,1024]{1,0:T(8,128)(2,1)S(1)} %collective-permute-done.51.refs_4_), channel_id=1, source_target_pairs={{0,4},{8,0},{16,8},{24,16},{28,24},{20,28},{12,20},{4,12},{1,5},{9... | collective-permute-start | bytes 786440 | tf_op jit(solution)/shard_map/ppermute | solution.py:407
  353.1 9.3 %collective-permute-start.58 = (bf16[128,1024]{1,0:T(8,128)(2,1)S(1)}, bf16[128,1024]{1,0:T(8,128)(2,1)S(1)}, u32[]{:S(2)}, u32[]{:S(2)}) collective-permute-start(bf16[128,1024]{1,0:T(8,128)(2,1)S(1)} %collective-permute-done.51.refs_4_), channel_id=1, source_target_pairs={{0,2},{2,0},{1,3},{3,1},{4,6},{6,4},{5,7},{7,5},{8,10},{10,8},{9,1... | collective-permute-start | bytes 786440 | tf_op jit(solution)/shard_map/ppermute | solution.py:227
  353.3 22.8 %collective-permute-start.54 = (f32[3,1024]{1,0:T(4,128)S(1)}, f32[3,1024]{1,0:T(4,128)S(1)}, u32[]{:S(2)}, u32[]{:S(2)}) collective-permute-start(f32[3,1024]{1,0:T(4,128)S(1)} %add.354), channel_id=1, source_target_pairs={{0,16},{4,20},{8,24},{12,28},{16,0},{20,4},{24,8},{28,12},{1,17},{... | collective-permute-start | bytes 36872 | tf_op jit(solution)/shard_map/ppermute | solution.py:677
  362.3 16.4 %collective-permute-start.59 = (bf16[128,1024]{1,0:T(8,128)(2,1)S(1)}, bf16[128,1024]{1,0:T(8,128)(2,1)S(1)}, u32[]{:S(2)}, u32[]{:S(2)}) collective-permute-start(bf16[128,1024]{1,0:T(8,128)(2,1)S(1)} %collective-permute-done.55.refs_2_), channel_id=1, source_target_pairs={{0,2},{2,0},{1,3},{3,1},{4,6},{6,4},{5,7},{7,5},{8,10},{10,8},{9,1... | collective-permute-start | bytes 786440 | tf_op jit(solution)/shard_map/ppermute | solution.py:227
  362.3 16.4 %collective-permute-start.60 = (bf16[128,1024]{1,0:T(8,128)(2,1)S(1)}, bf16[128,1024]{1,0:T(8,128)(2,1)S(1)}, u32[]{:S(2)}, u32[]{:S(2)}) collective-permute-start(bf16[128,1024]{1,0:T(8,128)(2,1)S(1)} %collective-permute-done.57.refs_4_), channel_id=1, source_target_pairs={{0,2},{2,0},{1,3},{3,1},{4,6},{6,4},{5,7},{7,5},{8,10},{10,8},{9,1... | collective-permute-start | bytes 786440 | tf_op jit(solution)/shard_map/ppermute | solution.py:227
  (49 other events, 538.2 us)
Sparse Core Ops, SparseCore 0:
  88.2 81.2 all-gather.5
Sparse Core Ops, SparseCore 1:
  238.0 98.2 all-reduce.2
  338.4 47.4 all-gather.3

commit v4 on v3

--- a/solution.py
+++ b/solution.py
@@ -264,46 +264,12 @@
     return [(order[at], order[(at + direction) % chips]) for at in range(chips)]
 
 
-class Ring:
-    def __init__(self, partial, direction):
-        self.chips = lax.axis_size("chip")
-        self.partial, self.direction = partial, direction
-        self.rows = partial.shape[0] // self.chips
-        self.step, self.near, self.far = 1, [], []
-        self.pending = [self.send(self.block(1).astype(BF16))]
-
-    def index(self, step):
-        ahead = (self.chips - self.direction * step) % self.chips
-        return lax.rem(ring_position() + ahead, self.chips)
-
-    def block(self, step):
-        return lax.dynamic_slice_in_dim(
-            self.partial, self.index(step) * self.rows, self.rows, 0
-        )
-
-    def send(self, block):
-        return lax.ppermute(block, "chip", ring_pairs(self.direction))
-
-    def advance(self, arrived):
-        self.step += 1
-        if len(arrived) > 1 or self.step == 2 * self.chips:
-            self.far.append(arrived[-1])
-        block, self.pending = arrived[0], []
-        if self.step <= self.chips:
-            block = (block.astype(F32) + self.block(self.step)).astype(BF16)
-        if self.step < 2 * self.chips - 1:
-            self.pending.append(self.send(block))
-        if self.chips <= self.step < 2 * self.chips:
-            self.near.append(block)
-            self.pending.append(swap_cores(block))
-
-
-def visit(rings, values):
-    pending, values = lax.optimization_barrier(([ring.pending for ring in rings], values))
-    for ring, arrived in zip(rings, pending):
-        if arrived:
-            ring.advance(arrived)
-    return values
+def add_kernel(_, *refs):
+    half = len(refs) // 2
+    for partial, arrived, output in zip(refs[:2], refs[2:4], refs[4:]) if half == 3 else ():
+        output[...] = (arrived[...].astype(F32) + partial[...]).astype(BF16)
+    for partial, output in zip(refs[:2], refs[2:]) if half == 2 else ():
+        output[...] = partial[...].astype(BF16)
 
 
 def place_kernel(_, *refs):
@@ -316,40 +282,96 @@
             refs[5][...] = refs[2 + side][...].astype(F32)
 
 
-def place(outputs, down, up, at):
-    tall, wide = down.near[at].shape, up.near[at].shape
-    chips, core = down.chips, lax.axis_index("core")
-    blocks = [down.near[at], down.far[at], up.near[at], up.far[at]]
-    shapes = [(2 * chips * tall[0], tall[1]), (chips * wide[0], 2 * wide[1])]
-    order = jnp.stack([down.index(at), up.index(at), core]).astype(jnp.int32)
-
-    def side(at, order):
-        return jnp.where(at == 0, order[2], 1 - order[2])
-
-    return pl.pallas_call(
-        place_kernel,
-        grid_spec=pltpu.PrefetchScalarGridSpec(
-            num_scalar_prefetch=1,
-            grid=(2,),
-            in_specs=[pl.BlockSpec(memory_space=pl.ANY)] * len(outputs)
-            + [pl.BlockSpec(block.shape, lambda at, order: (0, 0)) for block in blocks],
-            out_specs=[
-                pl.BlockSpec(tall, lambda at, order: (side(at, order) * chips + order[0], 0)),
-                pl.BlockSpec(wide, lambda at, order: (order[1], side(at, order))),
+class Rings:
+    def __init__(self, down, up):
+        self.chips, self.partials, self.directions = lax.axis_size("chip"), (down, up), (1, -1)
+        self.shapes = [(array.shape[0] // self.chips, array.shape[1]) for array in (down, up)]
+        self.step, self.outputs, self.near = 1, [], None
+        self.swapping = []
+        self.pending = self.send(self.add(()))
+
+    def index(self, step):
+        place = ring_position()
+        ahead = [(self.chips - direction * step) % self.chips for direction in self.directions]
+        return jnp.stack([lax.rem(place + steps, self.chips) for steps in ahead]).astype(jnp.int32)
+
+    def add(self, arrived):
+        def local_block(which):
+            return pl.BlockSpec(self.shapes[which], lambda at, order: (order[which], 0))
+
+        whole = [pl.BlockSpec(shape, lambda at, order: (0, 0)) for shape in self.shapes]
+        return pl.pallas_call(
+            add_kernel,
+            grid_spec=pltpu.PrefetchScalarGridSpec(
+                num_scalar_prefetch=1,
+                grid=(1,),
+                in_specs=[local_block(0), local_block(1)] + (whole if arrived else []),
+                out_specs=whole,
+            ),
+            out_shape=[jax.ShapeDtypeStruct(shape, BF16) for shape in self.shapes],
+            compiler_params=pltpu.CompilerParams(vmem_limit_bytes=vmem_limit),
+            name="ring_add",
+        )(self.index(self.step), *self.partials, *arrived)
+
+    def send(self, blocks):
+        return [
+            lax.ppermute(block, "chip", ring_pairs(direction))
+            for block, direction in zip(blocks, self.directions)
+        ]
+
+    def place(self, near, far, step):
+        (tall, columns), (rows, wide) = self.shapes
+        chips, core = self.chips, lax.axis_index("core")
+        order = jnp.concatenate([self.index(step), core[None].astype(jnp.int32)])
+        blocks = [near[0], far[0], near[1], far[1]]
+
+        def side(at, order):
+            return jnp.where(at == 0, order[2], 1 - order[2])
+
+        return pl.pallas_call(
+            place_kernel,
+            grid_spec=pltpu.PrefetchScalarGridSpec(
+                num_scalar_prefetch=1,
+                grid=(2,),
+                in_specs=[pl.BlockSpec(memory_space=pl.ANY)] * len(self.outputs)
+                + [pl.BlockSpec(block.shape, lambda at, order: (0, 0)) for block in blocks],
+                out_specs=[
+                    pl.BlockSpec((tall, columns), lambda at, order: (side(at, order) * chips + order[0], 0)),
+                    pl.BlockSpec((rows, wide), lambda at, order: (order[1], side(at, order))),
+                ],
+            ),
+            out_shape=[
+                jax.ShapeDtypeStruct((2 * chips * tall, columns), F32),
+                jax.ShapeDtypeStruct((chips * rows, 2 * wide), F32),
             ],
-        ),
-        out_shape=[jax.ShapeDtypeStruct(shape, F32) for shape in shapes],
-        input_output_aliases={1 + at: at for at in range(len(outputs))},
-        compiler_params=pltpu.CompilerParams(vmem_limit_bytes=vmem_limit),
-        name="place",
-    )(order, *outputs, *blocks)
-
-
-def place_all(down, up):
-    outputs = []
-    for at in range(down.chips):
-        outputs = place(outputs, down, up, at)
-    return outputs
+            input_output_aliases={1 + at: at for at in range(len(self.outputs))},
+            compiler_params=pltpu.CompilerParams(vmem_limit_bytes=vmem_limit),
+            name="place",
+        )(order, *self.outputs, *blocks)
+
+    def visit(self, values):
+        self.pending, self.swapping, self.outputs, values = lax.optimization_barrier(
+            (self.pending, self.swapping, self.outputs, values)
+        )
+        if self.swapping:
+            self.outputs = self.place(self.near, self.swapping, self.step - self.chips)
+            self.swapping = []
+        if self.pending:
+            self.step += 1
+            blocks, self.pending = self.pending, []
+            if self.step <= self.chips:
+                blocks = self.add(blocks)
+            if self.step < 2 * self.chips - 1:
+                self.pending = self.send(blocks)
+            if self.step >= self.chips:
+                self.near = blocks
+                self.swapping = [swap_cores(block) for block in blocks]
+        return values
+
+    def finish(self):
+        while self.pending or self.swapping:
+            self.visit(())
+        return self.outputs
 
 
 def core_half(values, axis, side):
@@ -570,10 +592,11 @@
     grad_far, mlp_in_far = swap_cores(out_grad), swap_cores(mlp_in)
     active_near, active_far = share_halves(active_low, 1)
     upper_near, upper_far = share_halves(d_upper, 1)
-    down = Ring(product(active_near, out_grad, 0, 0) + product(active_far, grad_far, 0, 0), 1)
-    up = Ring(product(mlp_in, upper_near, 0, 0) + product(mlp_in_far, upper_far, 0, 0), -1)
-    rings = (down, up)
-    d_mlp = visit(rings, d_mlp)
+    rings = Rings(
+        product(active_near, out_grad, 0, 0) + product(active_far, grad_far, 0, 0),
+        product(mlp_in, upper_near, 0, 0) + product(mlp_in_far, upper_far, 0, 0),
+    )
+    d_mlp = rings.visit(d_mlp)
     mlp_part, d_mlp = lax.optimization_barrier(
         (product(active_low, down_weight).astype(BF16), d_mlp)
     )
@@ -581,15 +604,37 @@
     d_hidden = grad_out + normalize_back(d_mlp * gain_mlp, unit_mlp, inverse_mlp)
     d_branch = d_hidden.astype(BF16)
     d_attn = product(output_weight, d_branch, 1, 1).astype(BF16)
-    d_attn = visit(rings, d_attn)
+    d_attn = rings.visit(d_attn)
     grads = scatter_queries(d_attn, heads, split)
+    small = jnp.concatenate(
+        [
+            jnp.sum(d_hidden, axis=0),
+            jnp.sum(d_mlp * unit_mlp, axis=0),
+            jnp.sum(d_mlp, axis=0),
+            jnp.sum(grad_out, axis=0),
+            jnp.sum(d_upper.astype(F32), axis=0),
+        ]
+    )
+    model = d_branch.shape[1]
+    lines = small.shape[0] // chips
+    small = jnp.pad(small.reshape(chips, 1, lines), ((0, 0), (0, 7), (0, model - lines)))
+    out_near, out_far = share_halves(attn_out, 0)
+    doutput = product(out_near, d_branch) + product(out_far, swap_cores(d_branch))
+    doutput = jnp.concatenate([doutput.reshape(chips, -1, model), small], axis=1).astype(BF16)
     pieces = 2
     dquery = None
     far_sums, near_sums = [], []
     for keys, sums, sums_type in ((other, far_sums, BF16), (own, near_sums, F32)):
         for index in range(pieces):
-            grads, dquery = visit(rings, (grads, dquery))
+            if keys is own and index == 0:
+                doutput = to_heads(doutput)
             last = keys is own and index == pieces - 1
+            if not last:
+                grads, dquery, doutput = rings.visit((grads, dquery, doutput))
+            else:
+                grads, dquery, doutput, mlp_out = rings.visit((grads, dquery, doutput, mlp_out))
+                doutput = jnp.sum(doutput.astype(F32), axis=0).astype(BF16)
+                block_output = (hidden + mlp_out + down_bias).astype(BF16)
             dquery, piece = backward_piece(
                 queries, grads, raw, logsum, dquery, keys, index, pieces, crops, sums_type, last
             )
@@ -600,32 +645,8 @@
             for near, far in zip(near_sums, far_sums)
         ]
     )
-    small = jnp.concatenate(
-        [
-            jnp.stack(
-                [
-                    jnp.sum(d_hidden, axis=0),
-                    jnp.sum(d_mlp * unit_mlp, axis=0),
-                    jnp.sum(d_mlp, axis=0),
-                    jnp.sum(grad_out, axis=0),
-                ]
-            ).reshape(-1),
-            jnp.sum(d_upper.astype(F32), axis=0),
-        ]
-    )
-    lines = -(-small.shape[0] // (16 * d_branch.shape[1])) * 16
-    small = jnp.pad(small, (0, lines * d_branch.shape[1] - small.shape[0])).astype(BF16)
-    later = lax.psum(
-        jnp.concatenate(
-            [product(attn_out, d_branch).astype(BF16), small.reshape(lines, -1)], axis=0
-        ),
-        ("chip", "core"),
-    ).astype(F32)
-    doutput_weight, small = later[:width], later[width:].reshape(-1)
-    model = d_branch.shape[1]
-    dup_bias = small[4 * model : 4 * model + d_upper.shape[1]]
     if split == 1:
-        head_grads = visit(rings, jnp.concatenate([dquery, key_value], axis=1))
+        head_grads = rings.visit(jnp.concatenate([dquery, key_value], axis=1))
         moved = to_heads(head_grads)
         dquery, dkey, dvalue = (
             moved[:, at * HD : at * HD + HD].reshape(width, rows) for at in range(3)
@@ -635,7 +656,7 @@
         moved = to_heads(key_value).reshape(heads, split, 2 * HD, rows).astype(F32)
         moved = jnp.sum(moved, axis=1).astype(BF16)
         dkey, dvalue = (moved[:, at * HD : at * HD + HD].reshape(width, rows) for at in range(2))
-        dquery, dkey, dvalue = visit(rings, (dquery, dkey, dvalue))
+        dquery, dkey, dvalue = rings.visit((dquery, dkey, dvalue))
     d_part = (
         product(dquery, query_weight, 0, 1)
         + product(dkey, key_weight, 0, 1)
@@ -647,17 +668,16 @@
         ).astype(BF16)
         near, far = share_halves(projections, 0)
         projections = (near.astype(F32) + far.astype(F32)).astype(BF16)
-        d_part, projections = visit(rings, (d_part, projections))
-        projections = lax.all_gather(projections, ("chip", "core"), axis=0, tiled=True)
-        projections = projections.reshape(heads, 3, HD, model)
-        projections = [
-            projections[:, at].reshape(width, model).T.astype(F32) for at in range(3)
-        ]
+        size = projections.shape[0]
+        blocks = jnp.concatenate([projections, doutput], axis=0)
+        d_part, blocks = rings.visit((d_part, blocks))
     else:
+        size, blocks = 0, doutput
         projections = [
             lax.psum(product(attn_in, grad, 0, 1).astype(BF16), ("chip", "core")).astype(F32)
             for grad in (dquery, dkey, dvalue)
         ]
+    blocks = lax.all_gather(blocks, ("chip", "core"), axis=0)
     d_in = head_sum(d_part)
     ends = jnp.stack(
         [
@@ -666,23 +686,31 @@
             jnp.sum(lead[:, None] * d_part, axis=0),
         ]
     )
-    ends = visit(rings, ends)
     ends = whole_head_sum(ends)
-    ends = visit(rings, ends)
+    ends = rings.visit(ends)
     ends = ends + swap_cores(ends)
     reach = 1
     while reach < chips:
-        ends = visit(rings, ends)
+        ends = rings.visit(ends)
         pairs = [(chip, chip ^ reach) for chip in range(chips)]
         ends = ends + lax.ppermute(ends, "chip", pairs)
         reach *= 2
     input_grad = (d_hidden + normalize_back(d_in * gain_attn, unit_attn, inverse_attn)).astype(
         BF16
     )
-    while any(ring.pending for ring in rings):
-        visit(rings, ())
-    ddown_weight, dup_weight = place_all(down, up)
-    block_output = (hidden + mlp_out + down_bias).astype(BF16)
+    ddown_weight, dup_weight = rings.finish()
+    if split == 1:
+        projections = blocks[:, :size].reshape(heads, 3, HD, model)
+        projections = [
+            projections[:, at].reshape(width, model).T.astype(F32) for at in range(3)
+        ]
+    blocks = blocks.reshape(chips, 2, -1, model)[:, :, size:]
+    doutput_weight = (
+        blocks[:, :, :-8].transpose(1, 0, 2, 3).reshape(width, model).astype(F32)
+    )
+    small = jnp.sum(blocks[:, :, -8, :lines].astype(F32), axis=1).reshape(-1)
+    dup_bias = small[4 * model :]
+    small = [small[at * model : at * model + model] for at in range(4)]
     return (
         block_output,
         input_grad,
@@ -691,11 +719,11 @@
         ends[2],
         *projections,
         doutput_weight,
-        *(small[at * model : at * model + model] for at in range(3)),
+        *small[:3],
         dup_weight,
         dup_bias,
         ddown_weight,
-        small[3 * model : 4 * model],
+        small[3],
     )
 
 

time: 410 us -> 407 us (level)
  waiting for transfers between devices: 134 us -> 106 us
  local copies, waits for them, and re-layouts: 19.1 us -> 33.7 us
  Pallas kernels: 70 us -> 82.2 us
  other arithmetic: 37.1 us -> 31.4 us
    psum x1 -> x0, waiting for transfers between devices: 29.3 us -> none  [local(): lax.psum(jnp.concatenate([product(attn_out, d_branch).astype(BF16), small...]
    ppermute x28, waiting for transfers between devices: 36.5 us -> 54.3 us  [send(): lax.ppermute(block, 'chip', ring_pairs(direction))]
    ppermute x4, waiting for transfers between devices: 36.7 us -> 21.5 us  [head_sum(): lax.ppermute(low, 'head', [(0, 1), (1, 0)]).astype(F32)]
    pallas_call x0 -> x8, Pallas kernels: none -> 13.8 us  [add(): pl.pallas_call(add_kernel, grid_spec=pltpu.PrefetchScalarGridSpec(num_sca...]
    unnamed x100 -> x95, local copies, waits for them, and re-layouts: 10.9 us -> 23 us
    convert_element_type x15 -> x3, other arithmetic: 14.1 us -> 2.53 us  [the longest x1 1.46 us: local(): blocks[:, :, :-8].transpose(1, 0, 2, 3).reshape(width, model).astype(F32)]
    ppermute x3, waiting for transfers between devices: 4.21 us -> 13.8 us  [local(): ends = ends + lax.ppermute(ends, 'chip', pairs)]
    all_to_all x2 -> x3, starting transfers between devices: 7.63 us -> 13.1 us  [to_heads(): return lax.all_to_all(blocks, 'chip', 0, 0, tiled=True)]
  transfers between devices with their start and end apart: 66 -> 68, of which waited for: 21 -> 22; matrix products, arithmetic and copies ran while one was open for 15% -> 12% of each run, Pallas kernels for 11% -> 15%
where the time goes in v4:
time: 407 us; the launch traced here: 402 us
  waiting for transfers between devices  106 us (26%)
  Pallas kernels  82.2 us (20%)
  starting transfers between devices  58.4 us (14%)
  blocking collectives  41.4 us (10%)
  local copies, waits for them, and re-layouts  33.7 us (8%)
  matrix products  32.8 us (8%)
  other arithmetic  31.4 us (8%)
  between operations  15.1 us (4%)
    ppermute x28, waiting for transfers between devices, send(): lax.ppermute(block, 'chip', ring_pairs(direction))  54.3 us
    all_to_all x2, blocking collectives, to_heads(): return lax.all_to_all(blocks, 'chip', 0, 0, tiled=True)  41.4 us
    ppermute x28, starting transfers between devices, send(): lax.ppermute(block, 'chip', ring_pairs(direction))  30.3 us
    dot_general x18, matrix products, product(): lax.dot_general(first, second, (((first_axis,), (second_axis,)), ((), ())...  29.3 us
    pallas_call x4, Pallas kernels, backward_piece(): pl.pallas_call(body, grid=(groups,), in_specs=[query_spec(payload_rows, p...  28.9 us
    pallas_call x1, Pallas kernels, attention_forward(): pl.pallas_call(functools.partial(forward_kernel, crops, key_step(count)),...  23.5 us
    unnamed x95, local copies, waits for them, and re-layouts  23 us
    ppermute x4, waiting for transfers between devices, head_sum(): lax.ppermute(low, 'head', [(0, 1), (1, 0)]).astype(F32)  21.5 us
  transfers between devices with their start and end apart: 68, of which 22 were waited for; matrix products, arithmetic and copies ran while one was open for 12% of the time, Pallas kernels for 15%

profile of v4, /device:TPU:0, one launch (start us, length us, event | category | flops | bytes accessed | tf_op | source)
XLA Modules:
  0.0 401.6 jit_solution(14727800749338093818)
XLA Ops:
  16.6 29.3 %all_to_all.25.query_ref.own.refs_0_.piece = bf16[8,208,256]{2,1,0:T(8,128)(2,1)S(1)} all-to-all(bf16[8,208,256]{2,1,0:T(8,128)(2,1)S(1)} %pad_maximum_fusion), channel_id=1, replica_groups=mesh['chip'=8,'core'=2,'head'=2] {'chip'}, dimensions={0} | all-to-all | bytes 1703936 | tf_op jit(solution)/shard_map/all_to_all | solution.py:231
  45.9 2.4 collective-permute-done.other.refs_4_.piece
  48.3 23.5 %attention_forward.1 = (f32[8,64,256]{2,1,0:T(8,128)S(1)}, bf16[8,64,256]{2,1,0:T(8,128)(2,1)S(1)}, f32[8,1,256]{2,1,0:T(1,128)S(1)}) custom-call(bf16[8,208,256]{2,1,0:T(8,128)(2,1)S(1)} %all_to_all.25.query_ref.own.refs_0_.piece, bf16[8,208,256]{2,1,0:T(8,128)(2,1)S(1)} %all_to_all.25.query_ref.own.refs_0_.piece, ...), custom_call_target="tpu_custom_call" | custom-call | flops 17179869184 | bytes 4194304 | tf_op jit(solution)/shard_map/attention_forward/pallas_call | solution.py:160
  71.8 12.1 %all_to_all.26 = bf16[8,64,256]{2,1,0:T(8,128)(2,1)S(1)} all-to-all(bf16[8,64,256]{2,1,0:T(8,128)(2,1)S(1)} %get-tuple-element.143), channel_id=1, replica_groups=mesh['chip'=8,'core'=2,'head'=2] {'chip'}, dimensions={0} | all-to-all | bytes 524288 | tf_op jit(solution)/shard_map/all_to_all | solution.py:231
  90.9 7.4 %collective-permute-done.1 = bf16[256,1024]{1,0:T(8,128)(2,1)} collective-permute-done((bf16[256,1024]{1,0:T(8,128)(2,1)}, bf16[256,1024]{1,0:T(8,128)(2,1)}, u32[]{:S(2)}, u32[]{:S(2)}) %collective-permute-start.1) | collective-permute-done | bytes 524320 | tf_op jit(solution)/shard_map/ppermute | solution.py:512
  102.7 7.0 %fusion.43 = (bf16[2048]{0:T(1024)(128)(2,1)S(1)}, bf16[256,2048]{1,0:T(8,128)(2,1)S(1)}, f32[256,2048]{1,0:T(8,128)S(1)}) fusion(f32[256,2048]{1,0:T(8,128)S(1)} %convolution_add_fusion, bf16[256,1024]{1,0:T(8,128)(2,1)} %param.19, bf16[2048,1024]{1,0:T(8,128)(2,1)S(1)} %copy-done.42), kind=kOutput, calls=%fused_computation.132 | convolution fusion | flops 1112012800 | bytes 9965568 | tf_op jit(solution)/shard_map/dot_general | solution.py:35
  111.6 2.1 convolution_convert_fusion.1
  115.0 2.0 fusion.34
  118.5 2.8 convolution_add_fusion.1.refs_1_
  121.3 1.9 convolution_add_fusion.2.refs_0_
  123.2 2.0 ring_add.8
  127.3 3.6 collective-permute-done.8
  131.1 8.6 %collective-permute-done.6.refs_2_ = bf16[128,1024]{1,0:T(8,128)(2,1)S(1)} collective-permute-done((bf16[128,1024]{1,0:T(8,128)(2,1)S(1)}, bf16[128,1024]{1,0:T(8,128)(2,1)S(1)}, u32[]{:S(2)}, u32[]{:S(2)}) %collective-permute-start.6) | collective-permute-done | bytes 262176 | tf_op jit(solution)/shard_map/ppermute | solution.py:318
  139.6 6.6 %collective-permute-done.7.refs_3_ = bf16[128,1024]{1,0:T(8,128)(2,1)S(1)} collective-permute-done((bf16[128,1024]{1,0:T(8,128)(2,1)S(1)}, bf16[128,1024]{1,0:T(8,128)(2,1)S(1)}, u32[]{:S(2)}, u32[]{:S(2)}) %collective-permute-start.7) | collective-permute-done | bytes 262176 | tf_op jit(solution)/shard_map/ppermute | solution.py:318
  152.9 1.9 collective-permute-start.9
  154.8 13.1 %collective-permute-done.10.refs_3_ = bf16[128,1024]{1,0:T(8,128)(2,1)S(1)} collective-permute-done((bf16[128,1024]{1,0:T(8,128)(2,1)S(1)}, bf16[128,1024]{1,0:T(8,128)(2,1)S(1)}, u32[]{:S(2)}, u32[]{:S(2)}) %collective-permute-start.10) | collective-permute-done | bytes 262176 | tf_op jit(solution)/shard_map/ppermute | solution.py:318
  168.7 4.6 %all-to-all-start.2 = ((bf16[8,64,256]{2,1,0:T(8,128)(2,1)}), bf16[8,64,256]{2,1,0:T(8,128)(2,1)S(1)}, u32[]{:S(2)}, u32[]{:S(2)}) async-start(bf16[8,64,256]{2,1,0:T(8,128)(2,1)} %bitcast.15), calls=%async_computation.2 | async-start | bytes 524288 | tf_op jit(solution)/shard_map/all_to_all | solution.py:231
  174.8 2.2 copy-done.3
  178.7 2.1 collective-permute-start.11
  183.1 3.7 collective-permute-done.11.refs_2_
  188.0 2.2 copy-done.4
  193.9 7.1 %attention_backward.4 = (f32[8,64,256]{2,1,0:T(8,128)S(1)}, bf16[4,128,256]{2,1,0:T(8,128)(2,1)S(1)}) custom-call(bf16[8,208,256]{2,1,0:T(8,128)(2,1)S(1)} %all_to_all.25.query_ref.own.refs_0_.piece, bf16[8,64,256]{2,1,0:T(8,128)(2,1)S(1)} %all-to-all-done.2.refs_1_.grad_ref, f32[8,64,256]{2,1,0:T(8,128)S(1)} %copy-done.10, ...), custom_call_target="tpu_custom_call" | custom-call | flops 8589934592 | bytes 4194304 | tf_op jit(solution)/shard_map/attention_backward/pallas_call | solution.py:194
  201.8 4.4 %all-to-all-start.3 = ((bf16[8,40,1024]{2,1,0:T(8,128)(2,1)}), bf16[8,40,1024]{2,1,0:T(8,128)(2,1)}, u32[]{:S(2)}, u32[]{:S(2)}) async-start(bf16[8,40,1024]{2,1,0:T(8,128)(2,1)} %fusion.31), calls=%async_computation.3 | async-start | bytes 1310720 | tf_op jit(solution)/shard_map/all_to_all | solution.py:231
  206.4 2.3 convert_add_fusion.1
  208.7 2.2 copy-done.5
  212.6 2.1 collective-permute-start.17
  214.7 7.1 %attention_backward.5 = (f32[8,64,256]{2,1,0:T(8,128)S(1)}, bf16[4,128,256]{2,1,0:T(8,128)(2,1)S(1)}) custom-call(bf16[8,208,256]{2,1,0:T(8,128)(2,1)S(1)} %all_to_all.25.query_ref.own.refs_0_.piece, bf16[8,64,256]{2,1,0:T(8,128)(2,1)S(1)} %all-to-all-done.2.refs_1_.grad_ref, f32[8,64,256]{2,1,0:T(8,128)S(1)} %copy-done.11, ...), custom_call_target="tpu_custom_call" | custom-call | flops 8589934592 | bytes 4194304 | tf_op jit(solution)/shard_map/attention_backward/pallas_call | solution.py:194
  222.9 2.0 collective-permute-done.18.refs_3_
  224.9 2.2 copy-done.6
  228.7 2.9 collective-permute-start.19
  231.6 7.2 %attention_backward.6 = (f32[8,64,256]{2,1,0:T(8,128)S(1)}, f32[4,128,256]{2,1,0:T(8,128)S(1)}) custom-call(bf16[8,208,256]{2,1,0:T(8,128)(2,1)S(1)} %all_to_all.25.query_ref.own.refs_0_.piece, bf16[8,64,256]{2,1,0:T(8,128)(2,1)S(1)} %all-to-all-done.2.refs_1_.grad_ref, f32[8,64,256]{2,1,0:T(8,128)S(1)} %copy-done.12, ...), custom_call_target="tpu_custom_call" | custom-call | flops 8589934592 | bytes 4194304 | tf_op jit(solution)/shard_map/attention_backward/pallas_call | solution.py:194
  241.6 2.0 collective-permute-start.22
  243.6 7.5 %attention_backward.7 = (bf16[8,64,256]{2,1,0:T(8,128)(2,1)S(1)}, f32[4,128,256]{2,1,0:T(8,128)S(1)}) custom-call(bf16[8,208,256]{2,1,0:T(8,128)(2,1)S(1)} %all_to_all.25.query_ref.own.refs_0_.piece, bf16[8,64,256]{2,1,0:T(8,128)(2,1)S(1)} %all-to-all-done.2.refs_1_.grad_ref, f32[8,64,256]{2,1,0:T(8,128)S(1)} %copy-done.12, ...), custom_call_target="tpu_custom_call" | custom-call | flops 8589934592 | bytes 4194304 | tf_op jit(solution)/shard_map/attention_backward/pallas_call | solution.py:194
  252.2 4.1 %all-to-all-start.4 = ((bf16[8,192,256]{2,1,0:T(8,128)(2,1)}), bf16[8,192,256]{2,1,0:T(8,128)(2,1)S(1)}, u32[]{:S(2)}, u32[]{:S(2)}) async-start(bf16[8,192,256]{2,1,0:T(8,128)(2,1)} %maximum_maximum_fusion), calls=%async_computation.4 | async-start | bytes 1572864 | tf_op jit(solution)/shard_map/all_to_all | solution.py:231
  257.6 2.2 copy-done.8
  261.4 2.0 collective-permute-start.26
  264.0 13.0 %all-to-all-done.4 = bf16[8,192,256]{2,1,0:T(8,128)(2,1)S(1)} async-done(((bf16[8,192,256]{2,1,0:T(8,128)(2,1)}), bf16[8,192,256]{2,1,0:T(8,128)(2,1)S(1)}, u32[]{:S(2)}, u32[]{:S(2)}) %all-to-all-start.4) | async-done | bytes 786464 | tf_op jit(solution)/shard_map/all_to_all | solution.py:231
  279.8 3.6 fusion.8
  287.1 2.0 collective-permute-start.33
  289.4 10.5 %collective-permute-done.31 = bf16[256,1024]{1,0:T(8,128)(2,1)S(1)} collective-permute-done((bf16[256,1024]{1,0:T(8,128)(2,1)S(1)}, bf16[256,1024]{1,0:T(8,128)(2,1)S(1)}, u32[]{:S(2)}, u32[]{:S(2)}) %collective-permute-start.31) | collective-permute-done | bytes 524320 | tf_op jit(solution)/shard_map/ppermute | solution.py:512
  301.9 2.0 place.8
  304.5 2.0 collective-permute-start.38
  307.0 2.0 place.9
  309.0 2.3 collective-permute-done.37.refs_2_
  315.9 2.0 place.10
  317.9 7.7 %collective-permute-done.46 = f32[3,1024]{1,0:T(4,128)S(1)} collective-permute-done((f32[3,1024]{1,0:T(4,128)S(1)}, f32[3,1024]{1,0:T(4,128)S(1)}, u32[]{:S(2)}, u32[]{:S(2)}) %collective-permute-start.46) | collective-permute-done | bytes 12320 | tf_op jit(solution)/shard_map/ppermute | solution.py:696
  325.7 5.6 %collective-permute-done.43.refs_4_ = bf16[128,1024]{1,0:T(8,128)(2,1)S(1)} collective-permute-done((bf16[128,1024]{1,0:T(8,128)(2,1)S(1)}, bf16[128,1024]{1,0:T(8,128)(2,1)S(1)}, u32[]{:S(2)}, u32[]{:S(2)}) %collective-permute-start.43) | collective-permute-done | bytes 262176 | tf_op jit(solution)/shard_map/ppermute | solution.py:318
  331.9 1.9 collective-permute-start.48
  334.6 2.0 place.11
  336.6 6.0 %collective-permute-done.51 = f32[3,1024]{1,0:T(4,128)S(1)} collective-permute-done((f32[3,1024]{1,0:T(4,128)S(1)}, f32[3,1024]{1,0:T(4,128)S(1)}, u32[]{:S(2)}, u32[]{:S(2)}) %collective-permute-start.51) | collective-permute-done | bytes 12320 | tf_op jit(solution)/shard_map/ppermute | solution.py:696
  346.0 2.0 place.12
  348.0 2.1 collective-permute-done.53.refs_2_
  350.1 3.6 collective-permute-done.54.refs_4_
  353.7 1.7 collective-permute-start.57
  357.3 2.2 place.13
  359.4 2.5 collective-permute-done.57.refs_2_
  361.9 2.7 collective-permute-done.58.refs_4_
  367.0 2.0 place.14
  368.9 2.0 place.15
  374.6 2.3 slice.77
  379.9 2.9 copy.80
  382.8 2.8 convert_bitcast_fusion.1
  385.6 2.9 copy.81
  390.1 3.0 copy.82
  (285 shorter events, 91.1 us)
Async XLA Ops:
  7.2 272.6 %all-gather.5.cloned.1.call-start = ((), (), s32[]{:S(2)}) async-start(), calls=%async_computation.5 | async-start | bytes 4718592 | tf_op jit(solution)/shard_map/all_gather | solution.py:578
  85.9 12.5 %collective-permute-start.1 = (bf16[256,1024]{1,0:T(8,128)(2,1)}, bf16[256,1024]{1,0:T(8,128)(2,1)}, u32[]{:S(2)}, u32[]{:S(2)}) collective-permute-start(bf16[256,1024]{1,0:T(8,128)(2,1)} %convolution_convert_fusion), channel_id=1, source_target_pairs={{0,1},{1,0},{2,3},{3,2},{4,5},{5,4},{6,7},{7,6},{8,9},{9,8},{10,11... | collective-permute-start | bytes 1572872 | tf_op jit(solution)/shard_map/ppermute | solution.py:512
  87.4 33.9 %collective-permute-start.3 = (bf16[256,1024]{1,0:T(8,128)(2,1)}, bf16[256,1024]{1,0:T(8,128)(2,1)}, u32[]{:S(2)}, u32[]{:S(2)}) collective-permute-start(bf16[256,1024]{1,0:T(8,128)(2,1)} %param.19), channel_id=1, source_target_pairs={{0,2},{2,0},{1,3},{3,1},{4,6},{6,4},{5,7},{7,5},{8,10},{10,8},{9,1... | collective-permute-start | bytes 1572872 | tf_op jit(solution)/shard_map/ppermute | solution.py:227
  90.4 90.4 %collective-permute-start.13 = (bf16[256,256]{1,0:T(8,128)(2,1)}, bf16[256,256]{1,0:T(8,128)(2,1)S(1)}, u32[]{:S(2)}, u32[]{:S(2)}) collective-permute-start(bf16[256,256]{1,0:T(8,128)(2,1)} %constant_dynamic-slice_fusion.1), channel_id=1, source_target_pairs={{0,2},{2,0},{1,3},{3,1},{4,6},{6,4},{5,7},{7,5},{8,10},{10,8},{9,1... | collective-permute-start | bytes 393224 | tf_op jit(solution)/shard_map/ppermute | solution.py:227
  100.5 18.1 %collective-permute-start.4 = (bf16[256,1024]{1,0:T(8,128)(2,1)S(1)}, bf16[256,1024]{1,0:T(8,128)(2,1)S(1)}, u32[]{:S(2)}, u32[]{:S(2)}) collective-permute-start(bf16[256,1024]{1,0:T(8,128)(2,1)S(1)} %add_convert_fusion.2), channel_id=1, source_target_pairs={{0,2},{2,0},{1,3},{3,1},{4,6},{6,4},{5,7},{7,5},{8,10},{10,8},{9,1... | collective-permute-start | bytes 1572872 | tf_op jit(solution)/shard_map/ppermute | solution.py:227
  113.7 7.6 %collective-permute-start.2 = (bf16[256,1024]{1,0:T(8,128)(2,1)S(1)}, bf16[256,1024]{1,0:T(8,128)(2,1)S(1)}, u32[]{:S(2)}, u32[]{:S(2)}) collective-permute-start(bf16[256,1024]{1,0:T(8,128)(2,1)S(1)} %constant_dynamic-slice_fusion.3), channel_id=1, source_target_pairs={{0,2},{2,0},{1,3},{3,1},{4,6},{6,4},{5,7},{7,5},{8,10},{10,8},{9,1... | collective-permute-start | bytes 1572872 | tf_op jit(solution)/shard_map/ppermute | solution.py:227
  117.0 13.9 %collective-permute-start.8 = (bf16[256,1024]{1,0:T(8,128)(2,1)S(1)}, bf16[256,1024]{1,0:T(8,128)(2,1)S(1)}, u32[]{:S(2)}, u32[]{:S(2)}) collective-permute-start(bf16[256,1024]{1,0:T(8,128)(2,1)S(1)} %convolution_convert_fusion.2), channel_id=1, source_target_pairs={{0,1},{1,0},{2,3},{3,2},{4,5},{5,4},{6,7},{7,6},{8,9},{9,8},{10,11... | collective-permute-start | bytes 1572872 | tf_op jit(solution)/shard_map/ppermute | solution.py:512
  125.2 14.4 %collective-permute-start.6 = (bf16[128,1024]{1,0:T(8,128)(2,1)S(1)}, bf16[128,1024]{1,0:T(8,128)(2,1)S(1)}, u32[]{:S(2)}, u32[]{:S(2)}) collective-permute-start(bf16[128,1024]{1,0:T(8,128)(2,1)S(1)} %get-tuple-element.144), channel_id=1, source_target_pairs={{0,8},{8,16},{16,24},{24,28},{28,20},{20,12},{12,4},{4,0},{1,9},{9... | collective-permute-start | bytes 786440 | tf_op jit(solution)/shard_map/ppermute | solution.py:318
  125.8 20.5 %collective-permute-start.7 = (bf16[128,1024]{1,0:T(8,128)(2,1)S(1)}, bf16[128,1024]{1,0:T(8,128)(2,1)S(1)}, u32[]{:S(2)}, u32[]{:S(2)}) collective-permute-start(bf16[128,1024]{1,0:T(8,128)(2,1)S(1)} %get-tuple-element.145), channel_id=1, source_target_pairs={{0,4},{8,0},{16,8},{24,16},{28,24},{20,28},{12,20},{4,12},{1,5},{9... | collective-permute-start | bytes 786440 | tf_op jit(solution)/shard_map/ppermute | solution.py:318
  148.4 32.4 %collective-permute-start.14 = (bf16[256,1024]{1,0:T(8,128)(2,1)S(1)}, bf16[256,1024]{1,0:T(8,128)(2,1)}, u32[]{:S(2)}, u32[]{:S(2)}) collective-permute-start(bf16[256,1024]{1,0:T(8,128)(2,1)S(1)} %convert_element_type.187), channel_id=1, source_target_pairs={{0,2},{2,0},{1,3},{3,1},{4,6},{6,4},{5,7},{7,5},{8,10},{10,8},{9,1... | collective-permute-start | bytes 1572872 | tf_op jit(solution)/shard_map/ppermute | solution.py:227
  152.7 15.2 %collective-permute-start.10 = (bf16[128,1024]{1,0:T(8,128)(2,1)S(1)}, bf16[128,1024]{1,0:T(8,128)(2,1)S(1)}, u32[]{:S(2)}, u32[]{:S(2)}) collective-permute-start(bf16[128,1024]{1,0:T(8,128)(2,1)S(1)} %get-tuple-element.149), channel_id=1, source_target_pairs={{0,4},{8,0},{16,8},{24,16},{28,24},{20,28},{12,20},{4,12},{1,5},{9... | collective-permute-start | bytes 786440 | tf_op jit(solution)/shard_map/ppermute | solution.py:318
  152.9 15.0 %collective-permute-start.9 = (bf16[128,1024]{1,0:T(8,128)(2,1)S(1)}, bf16[128,1024]{1,0:T(8,128)(2,1)S(1)}, u32[]{:S(2)}, u32[]{:S(2)}) collective-permute-start(bf16[128,1024]{1,0:T(8,128)(2,1)S(1)} %get-tuple-element.148), channel_id=1, source_target_pairs={{0,8},{8,16},{16,24},{24,28},{28,20},{20,12},{12,4},{4,0},{1,9},{9... | collective-permute-start | bytes 786440 | tf_op jit(solution)/shard_map/ppermute | solution.py:318
  168.7 19.3 %all-to-all-start.2 = ((bf16[8,64,256]{2,1,0:T(8,128)(2,1)}), bf16[8,64,256]{2,1,0:T(8,128)(2,1)S(1)}, u32[]{:S(2)}, u32[]{:S(2)}) async-start(bf16[8,64,256]{2,1,0:T(8,128)(2,1)} %bitcast.15), calls=%async_computation.2 | async-start | bytes 524288 | tf_op jit(solution)/shard_map/all_to_all | solution.py:231
  173.3 33.1 %collective-permute-start.21 = (bf16[256,1024]{1,0:T(8,128)(2,1)}, bf16[256,1024]{1,0:T(8,128)(2,1)}, u32[]{:S(2)}, u32[]{:S(2)}) collective-permute-start(bf16[256,1024]{1,0:T(8,128)(2,1)} %convolution_convert_fusion.1), channel_id=1, source_target_pairs={{0,1},{1,0},{2,3},{3,2},{4,5},{5,4},{6,7},{7,6},{8,9},{9,8},{10,11... | collective-permute-start | bytes 1572872 | tf_op jit(solution)/shard_map/ppermute | solution.py:512
  178.7 8.1 %collective-permute-start.11 = (bf16[128,1024]{1,0:T(8,128)(2,1)S(1)}, bf16[128,1024]{1,0:T(8,128)(2,1)S(1)}, u32[]{:S(2)}, u32[]{:S(2)}) collective-permute-start(bf16[128,1024]{1,0:T(8,128)(2,1)S(1)} %get-tuple-element.154), channel_id=1, source_target_pairs={{0,8},{8,16},{16,24},{24,28},{28,20},{20,12},{12,4},{4,0},{1,9},{9... | collective-permute-start | bytes 786440 | tf_op jit(solution)/shard_map/ppermute | solution.py:318
  180.8 7.2 %collective-permute-start.12 = (bf16[128,1024]{1,0:T(8,128)(2,1)S(1)}, bf16[128,1024]{1,0:T(8,128)(2,1)S(1)}, u32[]{:S(2)}, u32[]{:S(2)}) collective-permute-start(bf16[128,1024]{1,0:T(8,128)(2,1)S(1)} %get-tuple-element.155), channel_id=1, source_target_pairs={{0,4},{8,0},{16,8},{24,16},{28,24},{20,28},{12,20},{4,12},{1,5},{9... | collective-permute-start | bytes 786440 | tf_op jit(solution)/shard_map/ppermute | solution.py:318
  191.8 10.0 %collective-permute-start.15 = (bf16[128,1024]{1,0:T(8,128)(2,1)S(1)}, bf16[128,1024]{1,0:T(8,128)(2,1)S(1)}, u32[]{:S(2)}, u32[]{:S(2)}) collective-permute-start(bf16[128,1024]{1,0:T(8,128)(2,1)S(1)} %get-tuple-element.159), channel_id=1, source_target_pairs={{0,8},{8,16},{16,24},{24,28},{28,20},{20,12},{12,4},{4,0},{1,9},{9... | collective-permute-start | bytes 786440 | tf_op jit(solution)/shard_map/ppermute | solution.py:318
  193.3 8.6 %collective-permute-start.16 = (bf16[128,1024]{1,0:T(8,128)(2,1)S(1)}, bf16[128,1024]{1,0:T(8,128)(2,1)S(1)}, u32[]{:S(2)}, u32[]{:S(2)}) collective-permute-start(bf16[128,1024]{1,0:T(8,128)(2,1)S(1)} %get-tuple-element.160), channel_id=1, source_target_pairs={{0,4},{8,0},{16,8},{24,16},{28,24},{20,28},{12,20},{4,12},{1,5},{9... | collective-permute-start | bytes 786440 | tf_op jit(solution)/shard_map/ppermute | solution.py:318
  201.8 23.0 %all-to-all-start.3 = ((bf16[8,40,1024]{2,1,0:T(8,128)(2,1)}), bf16[8,40,1024]{2,1,0:T(8,128)(2,1)}, u32[]{:S(2)}, u32[]{:S(2)}) async-start(bf16[8,40,1024]{2,1,0:T(8,128)(2,1)} %fusion.31), calls=%async_computation.3 | async-start | bytes 1310720 | tf_op jit(solution)/shard_map/all_to_all | solution.py:231
  208.7 30.1 %collective-permute-start.24 = (bf16[4,128,256]{2,1,0:T(8,128)(2,1)S(1)}, bf16[4,128,256]{2,1,0:T(8,128)(2,1)}, u32[]{:S(2)}, u32[]{:S(2)}) collective-permute-start(bf16[4,128,256]{2,1,0:T(8,128)(2,1)S(1)} %get-tuple-element.192), channel_id=1, source_target_pairs={{0,2},{2,0},{1,3},{3,1},{4,6},{6,4},{5,7},{7,5},{8,10},{10,8},{9,1... | collective-permute-start | bytes 786440 | tf_op jit(solution)/shard_map/ppermute | solution.py:227
  212.6 10.3 %collective-permute-start.17 = (bf16[128,1024]{1,0:T(8,128)(2,1)S(1)}, bf16[128,1024]{1,0:T(8,128)(2,1)S(1)}, u32[]{:S(2)}, u32[]{:S(2)}) collective-permute-start(bf16[128,1024]{1,0:T(8,128)(2,1)S(1)} %get-tuple-element.168), channel_id=1, source_target_pairs={{0,8},{8,16},{16,24},{24,28},{28,20},{20,12},{12,4},{4,0},{1,9},{9... | collective-permute-start | bytes 786440 | tf_op jit(solution)/shard_map/ppermute | solution.py:318
  214.7 10.2 %collective-permute-start.18 = (bf16[128,1024]{1,0:T(8,128)(2,1)S(1)}, bf16[128,1024]{1,0:T(8,128)(2,1)S(1)}, u32[]{:S(2)}, u32[]{:S(2)}) collective-permute-start(bf16[128,1024]{1,0:T(8,128)(2,1)S(1)} %get-tuple-element.169), channel_id=1, source_target_pairs={{0,4},{8,0},{16,8},{24,16},{28,24},{20,28},{12,20},{4,12},{1,5},{9... | collective-permute-start | bytes 786440 | tf_op jit(solution)/shard_map/ppermute | solution.py:318
  222.6 28.6 %collective-permute-start.25 = (bf16[4,128,256]{2,1,0:T(8,128)(2,1)S(1)}, bf16[4,128,256]{2,1,0:T(8,128)(2,1)S(1)}, u32[]{:S(2)}, u32[]{:S(2)}) collective-permute-start(bf16[4,128,256]{2,1,0:T(8,128)(2,1)S(1)} %get-tuple-element.194), channel_id=1, source_target_pairs={{0,2},{2,0},{1,3},{3,1},{4,6},{6,4},{5,7},{7,5},{8,10},{10,8},{9,1... | collective-permute-start | bytes 786440 | tf_op jit(solution)/shard_map/ppermute | solution.py:227
  228.7 11.1 %collective-permute-start.19 = (bf16[128,1024]{1,0:T(8,128)(2,1)S(1)}, bf16[128,1024]{1,0:T(8,128)(2,1)S(1)}, u32[]{:S(2)}, u32[]{:S(2)}) collective-permute-start(bf16[128,1024]{1,0:T(8,128)(2,1)S(1)} %get-tuple-element.176), channel_id=1, source_target_pairs={{0,8},{8,16},{16,24},{24,28},{28,20},{20,12},{12,4},{4,0},{1,9},{9... | collective-permute-start | bytes 786440 | tf_op jit(solution)/shard_map/ppermute | solution.py:318
  231.6 8.2 %collective-permute-start.20 = (bf16[128,1024]{1,0:T(8,128)(2,1)S(1)}, bf16[128,1024]{1,0:T(8,128)(2,1)S(1)}, u32[]{:S(2)}, u32[]{:S(2)}) collective-permute-start(bf16[128,1024]{1,0:T(8,128)(2,1)S(1)} %get-tuple-element.177), channel_id=1, source_target_pairs={{0,4},{8,0},{16,8},{24,16},{28,24},{20,28},{12,20},{4,12},{1,5},{9... | collective-permute-start | bytes 786440 | tf_op jit(solution)/shard_map/ppermute | solution.py:318
  241.6 10.6 %collective-permute-start.22 = (bf16[128,1024]{1,0:T(8,128)(2,1)S(1)}, bf16[128,1024]{1,0:T(8,128)(2,1)S(1)}, u32[]{:S(2)}, u32[]{:S(2)}) collective-permute-start(bf16[128,1024]{1,0:T(8,128)(2,1)S(1)} %get-tuple-element.186), channel_id=1, source_target_pairs={{0,8},{8,16},{16,24},{24,28},{28,20},{20,12},{12,4},{4,0},{1,9},{9... | collective-permute-start | bytes 786440 | tf_op jit(solution)/shard_map/ppermute | solution.py:318
  243.6 8.6 %collective-permute-start.23 = (bf16[128,1024]{1,0:T(8,128)(2,1)S(1)}, bf16[128,1024]{1,0:T(8,128)(2,1)S(1)}, u32[]{:S(2)}, u32[]{:S(2)}) collective-permute-start(bf16[128,1024]{1,0:T(8,128)(2,1)S(1)} %get-tuple-element.187), channel_id=1, source_target_pairs={{0,4},{8,0},{16,8},{24,16},{28,24},{20,28},{12,20},{4,12},{1,5},{9... | collective-permute-start | bytes 786440 | tf_op jit(solution)/shard_map/ppermute | solution.py:318
  252.2 24.8 %all-to-all-start.4 = ((bf16[8,192,256]{2,1,0:T(8,128)(2,1)}), bf16[8,192,256]{2,1,0:T(8,128)(2,1)S(1)}, u32[]{:S(2)}, u32[]{:S(2)}) async-start(bf16[8,192,256]{2,1,0:T(8,128)(2,1)} %maximum_maximum_fusion), calls=%async_computation.4 | async-start | bytes 1572864 | tf_op jit(solution)/shard_map/all_to_all | solution.py:231
  256.3 114.6 %all-gather.7.cloned.1.call-start = ((), (), s32[]{:S(2)}) async-start(), calls=%async_computation.6 | async-start | bytes 4734976 | tf_op jit(solution)/shard_map/all_gather | solution.py:680
  261.4 24.3 %collective-permute-start.26 = (bf16[128,1024]{1,0:T(8,128)(2,1)S(1)}, bf16[128,1024]{1,0:T(8,128)(2,1)S(1)}, u32[]{:S(2)}, u32[]{:S(2)}) collective-permute-start(bf16[128,1024]{1,0:T(8,128)(2,1)S(1)} %get-tuple-element.197.refs_0_), channel_id=1, source_target_pairs={{0,8},{8,16},{16,24},{24,28},{28,20},{20,12},{12,4},{4,0},{1,9},{9... | collective-permute-start | bytes 786440 | tf_op jit(solution)/shard_map/ppermute | solution.py:318
  263.5 22.3 %collective-permute-start.28 = (bf16[128,1024]{1,0:T(8,128)(2,1)S(1)}, bf16[128,1024]{1,0:T(8,128)(2,1)S(1)}, u32[]{:S(2)}, u32[]{:S(2)}) collective-permute-start(bf16[128,1024]{1,0:T(8,128)(2,1)S(1)} %get-tuple-element.197.refs_0_), channel_id=1, source_target_pairs={{0,2},{2,0},{1,3},{3,1},{4,6},{6,4},{5,7},{7,5},{8,10},{10,8},{9,1... | collective-permute-start | bytes 786440 | tf_op jit(solution)/shard_map/ppermute | solution.py:227
  263.5 22.2 %collective-permute-start.27 = (bf16[128,1024]{1,0:T(8,128)(2,1)S(1)}, bf16[128,1024]{1,0:T(8,128)(2,1)S(1)}, u32[]{:S(2)}, u32[]{:S(2)}) collective-permute-start(bf16[128,1024]{1,0:T(8,128)(2,1)S(1)} %get-tuple-element.198.refs_2_), channel_id=1, source_target_pairs={{0,4},{8,0},{16,8},{24,16},{28,24},{20,28},{12,20},{4,12},{1,5},{9... | collective-permute-start | bytes 786440 | tf_op jit(solution)/shard_map/ppermute | solution.py:318
  263.6 22.1 %collective-permute-start.29 = (bf16[128,1024]{1,0:T(8,128)(2,1)S(1)}, bf16[128,1024]{1,0:T(8,128)(2,1)S(1)}, u32[]{:S(2)}, u32[]{:S(2)}) collective-permute-start(bf16[128,1024]{1,0:T(8,128)(2,1)S(1)} %get-tuple-element.198.refs_2_), channel_id=1, source_target_pairs={{0,2},{2,0},{1,3},{3,1},{4,6},{6,4},{5,7},{7,5},{8,10},{10,8},{9,1... | collective-permute-start | bytes 786440 | tf_op jit(solution)/shard_map/ppermute | solution.py:227
  285.8 14.0 %collective-permute-start.31 = (bf16[256,1024]{1,0:T(8,128)(2,1)S(1)}, bf16[256,1024]{1,0:T(8,128)(2,1)S(1)}, u32[]{:S(2)}, u32[]{:S(2)}) collective-permute-start(bf16[256,1024]{1,0:T(8,128)(2,1)S(1)} %convert_element_type.202), channel_id=1, source_target_pairs={{0,1},{1,0},{2,3},{3,2},{4,5},{5,4},{6,7},{7,6},{8,9},{9,8},{10,11... | collective-permute-start | bytes 1572872 | tf_op jit(solution)/shard_map/ppermute | solution.py:512
  287.1 17.2 %collective-permute-start.32 = (bf16[128,1024]{1,0:T(8,128)(2,1)S(1)}, bf16[128,1024]{1,0:T(8,128)(2,1)S(1)}, u32[]{:S(2)}, u32[]{:S(2)}) collective-permute-start(bf16[128,1024]{1,0:T(8,128)(2,1)S(1)} %collective-permute-done.26.refs_2_), channel_id=1, source_target_pairs={{0,8},{8,16},{16,24},{24,28},{28,20},{20,12},{12,4},{4,0},{1,9},{9... | collective-permute-start | bytes 786440 | tf_op jit(solution)/shard_map/ppermute | solution.py:318
  287.1 17.2 %collective-permute-start.34 = (bf16[128,1024]{1,0:T(8,128)(2,1)S(1)}, bf16[128,1024]{1,0:T(8,128)(2,1)S(1)}, u32[]{:S(2)}, u32[]{:S(2)}) collective-permute-start(bf16[128,1024]{1,0:T(8,128)(2,1)S(1)} %collective-permute-done.26.refs_2_), channel_id=1, source_target_pairs={{0,2},{2,0},{1,3},{3,1},{4,6},{6,4},{5,7},{7,5},{8,10},{10,8},{9,1... | collective-permute-start | bytes 786440 | tf_op jit(solution)/shard_map/ppermute | solution.py:227
  287.1 17.2 %collective-permute-start.33 = (bf16[128,1024]{1,0:T(8,128)(2,1)S(1)}, bf16[128,1024]{1,0:T(8,128)(2,1)S(1)}, u32[]{:S(2)}, u32[]{:S(2)}) collective-permute-start(bf16[128,1024]{1,0:T(8,128)(2,1)S(1)} %collective-permute-done.27.refs_4_), channel_id=1, source_target_pairs={{0,4},{8,0},{16,8},{24,16},{28,24},{20,28},{12,20},{4,12},{1,5},{9... | collective-permute-start | bytes 786440 | tf_op jit(solution)/shard_map/ppermute | solution.py:318
  289.2 15.2 %collective-permute-start.35 = (bf16[128,1024]{1,0:T(8,128)(2,1)S(1)}, bf16[128,1024]{1,0:T(8,128)(2,1)S(1)}, u32[]{:S(2)}, u32[]{:S(2)}) collective-permute-start(bf16[128,1024]{1,0:T(8,128)(2,1)S(1)} %collective-permute-done.27.refs_4_), channel_id=1, source_target_pairs={{0,2},{2,0},{1,3},{3,1},{4,6},{6,4},{5,7},{7,5},{8,10},{10,8},{9,1... | collective-permute-start | bytes 786440 | tf_op jit(solution)/shard_map/ppermute | solution.py:227
  300.5 3.8 collective-permute-start.36
  304.4 6.9 %collective-permute-start.37 = (bf16[128,1024]{1,0:T(8,128)(2,1)S(1)}, bf16[128,1024]{1,0:T(8,128)(2,1)S(1)}, u32[]{:S(2)}, u32[]{:S(2)}) collective-permute-start(bf16[128,1024]{1,0:T(8,128)(2,1)S(1)} %collective-permute-done.32.refs_2_), channel_id=1, source_target_pairs={{0,8},{8,16},{16,24},{24,28},{28,20},{20,12},{12,4},{4,0},{1,9},{9... | collective-permute-start | bytes 786440 | tf_op jit(solution)/shard_map/ppermute | solution.py:318
  304.5 7.1 %collective-permute-start.38 = (bf16[128,1024]{1,0:T(8,128)(2,1)S(1)}, bf16[128,1024]{1,0:T(8,128)(2,1)S(1)}, u32[]{:S(2)}, u32[]{:S(2)}) collective-permute-start(bf16[128,1024]{1,0:T(8,128)(2,1)S(1)} %collective-permute-done.33.refs_4_), channel_id=1, source_target_pairs={{0,4},{8,0},{16,8},{24,16},{28,24},{20,28},{12,20},{4,12},{1,5},{9... | collective-permute-start | bytes 786440 | tf_op jit(solution)/shard_map/ppermute | solution.py:318
  306.5 5.1 %collective-permute-start.39 = (bf16[128,1024]{1,0:T(8,128)(2,1)S(1)}, bf16[128,1024]{1,0:T(8,128)(2,1)S(1)}, u32[]{:S(2)}, u32[]{:S(2)}) collective-permute-start(bf16[128,1024]{1,0:T(8,128)(2,1)S(1)} %collective-permute-done.32.refs_2_), channel_id=1, source_target_pairs={{0,2},{2,0},{1,3},{3,1},{4,6},{6,4},{5,7},{7,5},{8,10},{10,8},{9,1... | collective-permute-start | bytes 786440 | tf_op jit(solution)/shard_map/ppermute | solution.py:227
  306.5 5.1 %collective-permute-start.40 = (bf16[128,1024]{1,0:T(8,128)(2,1)S(1)}, bf16[128,1024]{1,0:T(8,128)(2,1)S(1)}, u32[]{:S(2)}, u32[]{:S(2)}) collective-permute-start(bf16[128,1024]{1,0:T(8,128)(2,1)S(1)} %collective-permute-done.33.refs_4_), channel_id=1, source_target_pairs={{0,2},{2,0},{1,3},{3,1},{4,6},{6,4},{5,7},{7,5},{8,10},{10,8},{9,1... | collective-permute-start | bytes 786440 | tf_op jit(solution)/shard_map/ppermute | solution.py:227
  311.6 14.1 %collective-permute-start.42 = (bf16[128,1024]{1,0:T(8,128)(2,1)S(1)}, bf16[128,1024]{1,0:T(8,128)(2,1)S(1)}, u32[]{:S(2)}, u32[]{:S(2)}) collective-permute-start(bf16[128,1024]{1,0:T(8,128)(2,1)S(1)} %collective-permute-done.37.refs_2_), channel_id=1, source_target_pairs={{0,8},{8,16},{16,24},{24,28},{28,20},{20,12},{12,4},{4,0},{1,9},{9... | collective-permute-start | bytes 786440 | tf_op jit(solution)/shard_map/ppermute | solution.py:318
  312.0 19.3 %collective-permute-start.43 = (bf16[128,1024]{1,0:T(8,128)(2,1)S(1)}, bf16[128,1024]{1,0:T(8,128)(2,1)S(1)}, u32[]{:S(2)}, u32[]{:S(2)}) collective-permute-start(bf16[128,1024]{1,0:T(8,128)(2,1)S(1)} %collective-permute-done.38.refs_4_), channel_id=1, source_target_pairs={{0,4},{8,0},{16,8},{24,16},{28,24},{20,28},{12,20},{4,12},{1,5},{9... | collective-permute-start | bytes 786440 | tf_op jit(solution)/shard_map/ppermute | solution.py:318
  313.6 17.7 %collective-permute-start.44 = (bf16[128,1024]{1,0:T(8,128)(2,1)S(1)}, bf16[128,1024]{1,0:T(8,128)(2,1)S(1)}, u32[]{:S(2)}, u32[]{:S(2)}) collective-permute-start(bf16[128,1024]{1,0:T(8,128)(2,1)S(1)} %collective-permute-done.37.refs_2_), channel_id=1, source_target_pairs={{0,2},{2,0},{1,3},{3,1},{4,6},{6,4},{5,7},{7,5},{8,10},{10,8},{9,1... | collective-permute-start | bytes 786440 | tf_op jit(solution)/shard_map/ppermute | solution.py:227
  313.6 17.7 %collective-permute-start.45 = (bf16[128,1024]{1,0:T(8,128)(2,1)S(1)}, bf16[128,1024]{1,0:T(8,128)(2,1)S(1)}, u32[]{:S(2)}, u32[]{:S(2)}) collective-permute-start(bf16[128,1024]{1,0:T(8,128)(2,1)S(1)} %collective-permute-done.38.refs_4_), channel_id=1, source_target_pairs={{0,2},{2,0},{1,3},{3,1},{4,6},{6,4},{5,7},{7,5},{8,10},{10,8},{9,1... | collective-permute-start | bytes 786440 | tf_op jit(solution)/shard_map/ppermute | solution.py:227
  314.1 11.5 %collective-permute-start.46 = (f32[3,1024]{1,0:T(4,128)S(1)}, f32[3,1024]{1,0:T(4,128)S(1)}, u32[]{:S(2)}, u32[]{:S(2)}) collective-permute-start(f32[3,1024]{1,0:T(4,128)S(1)} %add.250), channel_id=1, source_target_pairs={{0,4},{4,0},{8,12},{12,8},{16,20},{20,16},{24,28},{28,24},{1,5},{5... | collective-permute-start | bytes 36872 | tf_op jit(solution)/shard_map/ppermute | solution.py:696
  331.3 11.3 %collective-permute-start.47 = (bf16[128,1024]{1,0:T(8,128)(2,1)S(1)}, bf16[128,1024]{1,0:T(8,128)(2,1)S(1)}, u32[]{:S(2)}, u32[]{:S(2)}) collective-permute-start(bf16[128,1024]{1,0:T(8,128)(2,1)S(1)} %collective-permute-done.42.refs_2_), channel_id=1, source_target_pairs={{0,8},{8,16},{16,24},{24,28},{28,20},{20,12},{12,4},{4,0},{1,9},{9... | collective-permute-start | bytes 786440 | tf_op jit(solution)/shard_map/ppermute | solution.py:318
  331.9 10.7 %collective-permute-start.48 = (bf16[128,1024]{1,0:T(8,128)(2,1)S(1)}, bf16[128,1024]{1,0:T(8,128)(2,1)S(1)}, u32[]{:S(2)}, u32[]{:S(2)}) collective-permute-start(bf16[128,1024]{1,0:T(8,128)(2,1)S(1)} %collective-permute-done.43.refs_4_), channel_id=1, source_target_pairs={{0,4},{8,0},{16,8},{24,16},{28,24},{20,28},{12,20},{4,12},{1,5},{9... | collective-permute-start | bytes 786440 | tf_op jit(solution)/shard_map/ppermute | solution.py:318
  333.8 8.9 %collective-permute-start.49 = (bf16[128,1024]{1,0:T(8,128)(2,1)S(1)}, bf16[128,1024]{1,0:T(8,128)(2,1)S(1)}, u32[]{:S(2)}, u32[]{:S(2)}) collective-permute-start(bf16[128,1024]{1,0:T(8,128)(2,1)S(1)} %collective-permute-done.42.refs_2_), channel_id=1, source_target_pairs={{0,2},{2,0},{1,3},{3,1},{4,6},{6,4},{5,7},{7,5},{8,10},{10,8},{9,1... | collective-permute-start | bytes 786440 | tf_op jit(solution)/shard_map/ppermute | solution.py:227
  333.8 8.9 %collective-permute-start.50 = (bf16[128,1024]{1,0:T(8,128)(2,1)S(1)}, bf16[128,1024]{1,0:T(8,128)(2,1)S(1)}, u32[]{:S(2)}, u32[]{:S(2)}) collective-permute-start(bf16[128,1024]{1,0:T(8,128)(2,1)S(1)} %collective-permute-done.43.refs_4_), channel_id=1, source_target_pairs={{0,2},{2,0},{1,3},{3,1},{4,6},{6,4},{5,7},{7,5},{8,10},{10,8},{9,1... | collective-permute-start | bytes 786440 | tf_op jit(solution)/shard_map/ppermute | solution.py:227
  334.3 8.3 %collective-permute-start.51 = (f32[3,1024]{1,0:T(4,128)S(1)}, f32[3,1024]{1,0:T(4,128)S(1)}, u32[]{:S(2)}, u32[]{:S(2)}) collective-permute-start(f32[3,1024]{1,0:T(4,128)S(1)} %add.251), channel_id=1, source_target_pairs={{0,8},{4,12},{8,0},{12,4},{16,24},{20,28},{24,16},{28,20},{1,9},{5... | collective-permute-start | bytes 36872 | tf_op jit(solution)/shard_map/ppermute | solution.py:696
  342.7 7.4 %collective-permute-start.53 = (bf16[128,1024]{1,0:T(8,128)(2,1)S(1)}, bf16[128,1024]{1,0:T(8,128)(2,1)S(1)}, u32[]{:S(2)}, u32[]{:S(2)}) collective-permute-start(bf16[128,1024]{1,0:T(8,128)(2,1)S(1)} %collective-permute-done.47.refs_2_), channel_id=1, source_target_pairs={{0,8},{8,16},{16,24},{24,28},{28,20},{20,12},{12,4},{4,0},{1,9},{9... | collective-permute-start | bytes 786440 | tf_op jit(solution)/shard_map/ppermute | solution.py:318
  344.2 9.5 %collective-permute-start.55 = (bf16[128,1024]{1,0:T(8,128)(2,1)S(1)}, bf16[128,1024]{1,0:T(8,128)(2,1)S(1)}, u32[]{:S(2)}, u32[]{:S(2)}) collective-permute-start(bf16[128,1024]{1,0:T(8,128)(2,1)S(1)} %collective-permute-done.47.refs_2_), channel_id=1, source_target_pairs={{0,2},{2,0},{1,3},{3,1},{4,6},{6,4},{5,7},{7,5},{8,10},{10,8},{9,1... | collective-permute-start | bytes 786440 | tf_op jit(solution)/shard_map/ppermute | solution.py:227
  344.2 9.5 %collective-permute-start.54 = (bf16[128,1024]{1,0:T(8,128)(2,1)S(1)}, bf16[128,1024]{1,0:T(8,128)(2,1)S(1)}, u32[]{:S(2)}, u32[]{:S(2)}) collective-permute-start(bf16[128,1024]{1,0:T(8,128)(2,1)S(1)} %collective-permute-done.48.refs_4_), channel_id=1, source_target_pairs={{0,4},{8,0},{16,8},{24,16},{28,24},{20,28},{12,20},{4,12},{1,5},{9... | collective-permute-start | bytes 786440 | tf_op jit(solution)/shard_map/ppermute | solution.py:318
  344.7 9.0 %collective-permute-start.56 = (bf16[128,1024]{1,0:T(8,128)(2,1)S(1)}, bf16[128,1024]{1,0:T(8,128)(2,1)S(1)}, u32[]{:S(2)}, u32[]{:S(2)}) collective-permute-start(bf16[128,1024]{1,0:T(8,128)(2,1)S(1)} %collective-permute-done.48.refs_4_), channel_id=1, source_target_pairs={{0,2},{2,0},{1,3},{3,1},{4,6},{6,4},{5,7},{7,5},{8,10},{10,8},{9,1... | collective-permute-start | bytes 786440 | tf_op jit(solution)/shard_map/ppermute | solution.py:227
  353.7 8.1 %collective-permute-start.57 = (bf16[128,1024]{1,0:T(8,128)(2,1)S(1)}, bf16[128,1024]{1,0:T(8,128)(2,1)S(1)}, u32[]{:S(2)}, u32[]{:S(2)}) collective-permute-start(bf16[128,1024]{1,0:T(8,128)(2,1)S(1)} %collective-permute-done.53.refs_2_), channel_id=1, source_target_pairs={{0,8},{8,16},{16,24},{24,28},{28,20},{20,12},{12,4},{4,0},{1,9},{9... | collective-permute-start | bytes 786440 | tf_op jit(solution)/shard_map/ppermute | solution.py:318
  355.5 9.1 %collective-permute-start.59 = (bf16[128,1024]{1,0:T(8,128)(2,1)S(1)}, bf16[128,1024]{1,0:T(8,128)(2,1)S(1)}, u32[]{:S(2)}, u32[]{:S(2)}) collective-permute-start(bf16[128,1024]{1,0:T(8,128)(2,1)S(1)} %collective-permute-done.53.refs_2_), channel_id=1, source_target_pairs={{0,2},{2,0},{1,3},{3,1},{4,6},{6,4},{5,7},{7,5},{8,10},{10,8},{9,1... | collective-permute-start | bytes 786440 | tf_op jit(solution)/shard_map/ppermute | solution.py:227
  355.5 9.1 %collective-permute-start.58 = (bf16[128,1024]{1,0:T(8,128)(2,1)S(1)}, bf16[128,1024]{1,0:T(8,128)(2,1)S(1)}, u32[]{:S(2)}, u32[]{:S(2)}) collective-permute-start(bf16[128,1024]{1,0:T(8,128)(2,1)S(1)} %collective-permute-done.54.refs_4_), channel_id=1, source_target_pairs={{0,4},{8,0},{16,8},{24,16},{28,24},{20,28},{12,20},{4,12},{1,5},{9... | collective-permute-start | bytes 786440 | tf_op jit(solution)/shard_map/ppermute | solution.py:318
  355.8 8.8 %collective-permute-start.60 = (bf16[128,1024]{1,0:T(8,128)(2,1)S(1)}, bf16[128,1024]{1,0:T(8,128)(2,1)S(1)}, u32[]{:S(2)}, u32[]{:S(2)}) collective-permute-start(bf16[128,1024]{1,0:T(8,128)(2,1)S(1)} %collective-permute-done.54.refs_4_), channel_id=1, source_target_pairs={{0,2},{2,0},{1,3},{3,1},{4,6},{6,4},{5,7},{7,5},{8,10},{10,8},{9,1... | collective-permute-start | bytes 786440 | tf_op jit(solution)/shard_map/ppermute | solution.py:227
  356.0 10.3 %collective-permute-start.52 = (f32[3,1024]{1,0:T(4,128)S(1)}, f32[3,1024]{1,0:T(4,128)S(1)}, u32[]{:S(2)}, u32[]{:S(2)}) collective-permute-start(f32[3,1024]{1,0:T(4,128)S(1)} %add.252), channel_id=1, source_target_pairs={{0,16},{4,20},{8,24},{12,28},{16,0},{20,4},{24,8},{28,12},{1,17},{... | collective-permute-start | bytes 36872 | tf_op jit(solution)/shard_map/ppermute | solution.py:696
  364.6 4.4 %collective-permute-start.61 = (bf16[128,1024]{1,0:T(8,128)(2,1)S(1)}, bf16[128,1024]{1,0:T(8,128)(2,1)S(1)}, u32[]{:S(2)}, u32[]{:S(2)}) collective-permute-start(bf16[128,1024]{1,0:T(8,128)(2,1)S(1)} %collective-permute-done.57.refs_2_), channel_id=1, source_target_pairs={{0,2},{2,0},{1,3},{3,1},{4,6},{6,4},{5,7},{7,5},{8,10},{10,8},{9,1... | collective-permute-start | bytes 786440 | tf_op jit(solution)/shard_map/ppermute | solution.py:227
  364.6 4.4 %collective-permute-start.62 = (bf16[128,1024]{1,0:T(8,128)(2,1)S(1)}, bf16[128,1024]{1,0:T(8,128)(2,1)S(1)}, u32[]{:S(2)}, u32[]{:S(2)}) collective-permute-start(bf16[128,1024]{1,0:T(8,128)(2,1)S(1)} %collective-permute-done.58.refs_4_), channel_id=1, source_target_pairs={{0,2},{2,0},{1,3},{3,1},{4,6},{6,4},{5,7},{7,5},{8,10},{10,8},{9,1... | collective-permute-start | bytes 786440 | tf_op jit(solution)/shard_map/ppermute | solution.py:227
  (48 other events, 453.3 us)
Sparse Core Ops, SparseCore 0:
  88.9 79.7 all-gather.4
  285.9 55.8 all-gather.6

commit v5 on v1

v5 whole, which is shorter than its diff:
```python
import functools
import math

import jax
import jax.numpy as jnp
from jax import lax
from jax.experimental import pallas as pl
from jax.experimental.pallas import tpu as pltpu
from jax.sharding import Mesh, PartitionSpec as P

HD = 64
F32 = jnp.float32
BF16 = jnp.bfloat16
eps = 1e-05
masked_value = -1e30
seg_row = 3 * HD
payload_rows = 3 * HD + 16
small_rows = 8
params = pltpu.CompilerParams(vmem_limit_bytes=56 * 2**20)


def normalize(values):
    centred = values - jnp.mean(values, axis=-1, keepdims=True)
    inverse = lax.rsqrt(jnp.mean(centred * centred, axis=-1, keepdims=True) + eps)
    return (centred * inverse, inverse)


def normalize_back(grad_unit, unit, inverse):
    return inverse * (
        grad_unit
        - jnp.mean(grad_unit, axis=-1, keepdims=True)
        - unit * jnp.mean(grad_unit * unit, axis=-1, keepdims=True)
    )


def product(first, second, first_axis=1, second_axis=0):
    return lax.dot_general(
        first,
        second,
        (((first_axis,), (second_axis,)), ((), ())),
        preferred_element_type=jnp.float32,
    )


def struct(shape, dtype):
    return jax.ShapeDtypeStruct(shape, dtype)


def whole_spec(shape):
    return pl.BlockSpec(shape, lambda *at: (0,) * len(shape))


def cost(flops, size, exps=0):
    return pl.CostEstimate(flops=flops, bytes_accessed=size, transcendentals=exps)


def project_kernel(
    input_ref, segment_ref, steps_ref, gain, shift, lead_weight, *refs
):
    weights, (payload_ref, attn_in_ref) = refs[:3], refs[3:]
    rows = input_ref.shape[0]

    @pl.when(pl.program_id(0) == 0)
    def _():
        unit, _ = normalize(input_ref[...].astype(F32))
        crops = steps_ref.shape[0]
        crop = lax.broadcasted_iota(jnp.int32, (crops, rows), 0)
        onehot = jnp.where(crop == segment_ref[...], 1.0, 0.0)
        lead = product(onehot, steps_ref[...].astype(F32), 0, 0)[:, :1] / 12.0
        attn_in = unit * gain[...] + shift[...] + lead * lead_weight[...]
        attn_in_ref[...] = attn_in.astype(BF16)

    for at, weight in enumerate(weights):
        part = product(attn_in_ref[...], weight[...]).T.astype(BF16)
        for head in range(2):
            payload_ref[head, pl.ds(at * HD, HD), :] = part[head * HD : head * HD + HD]
    segment = jnp.broadcast_to(segment_ref[...].astype(F32), (16, rows)).astype(BF16)
    for head in range(2):
        payload_ref[head, pl.ds(seg_row, 16), :] = segment


def project(block_input, segments, lead_steps, gain, shift, lead_weight, weights):
    rows, model = block_input.shape
    heads = weights[0].shape[1] // HD
    steps = jnp.broadcast_to(lead_steps[:, None], (lead_steps.shape[0], 128))
    line = whole_spec((1, model))
    column = pl.BlockSpec((model, 2 * HD), lambda at: (0, at))
    return pl.pallas_call(
        project_kernel,
        grid=(heads // 2,),
        in_specs=[whole_spec(block_input.shape), whole_spec((1, rows)), whole_spec(steps.shape)]
        + [line] * 3
        + [column] * 3,
        out_specs=[
            pl.BlockSpec((2, payload_rows, rows), lambda at: (at, 0, 0)),
            whole_spec((rows, model)),
        ],
        out_shape=[struct((heads, payload_rows, rows), BF16), struct((rows, model), BF16)],
        compiler_params=params,
        cost_estimate=cost(2 * rows * model * 3 * heads * HD, 8 * 2**20),
        name="project",
    )(block_input, segments[None], steps, gain[None], shift[None], lead_weight[None], *weights)


def mlp_kernel(count, input_ref, grad_ref, *refs):
    branches, refs = refs[:count], refs[count:]
    output_bias, gain, shift, up_weight, up_bias, down_weight = refs[:6]
    wide_ref, mlp_in_ref, hidden_ref, bias_ref, forward_ref, back_ref, forward, back = refs[6:]
    at = pl.program_id(0)

    @pl.when(at == 0)
    def _():
        hidden = input_ref[...].astype(F32) + output_bias[...]
        for branch in branches:
            hidden += branch[...].astype(F32)
        hidden_ref[...] = hidden
        unit, _ = normalize(hidden)
        mlp_in_ref[...] = (unit * gain[...] + shift[...]).astype(BF16)
        forward[...] = jnp.zeros_like(forward)
        back[...] = jnp.zeros_like(back)

    upper = product(mlp_in_ref[...], up_weight[...]) + up_bias[...]
    share = 0.5 + 0.5 * lax.erf(upper * math.sqrt(0.5))
    slope = share + upper * (jnp.exp(upper * upper * -0.5) * (1.0 / math.sqrt(2.0 * math.pi)))
    active = (upper * share).astype(BF16)
    d_active = product(grad_ref[...], down_weight[...], 1, 1)
    d_upper = (d_active * slope).astype(BF16)
    wide_ref[0] = active
    wide_ref[1] = d_upper
    bias_ref[...] = jnp.sum(d_upper.astype(F32), axis=0, keepdims=True)
    forward[...] += product(active, down_weight[...])
    back[...] += product(d_upper, up_weight[...], 1, 1)

    @pl.when(at == pl.num_programs(0) - 1)
    def _():
        forward_ref[...] = forward[...].astype(BF16)
        back_ref[...] = back[...].astype(BF16)


def mlp(block_input, out_grad, branches, output_bias, gain, shift, up_weight, up_bias, down_weight):
    rows, model = block_input.shape
    units = up_weight.shape[1]
    step = math.gcd(units, 512)
    tile, line = whole_spec((rows, model)), whole_spec((1, model))
    return pl.pallas_call(
        functools.partial(mlp_kernel, len(branches)),
        grid=(units // step,),
        in_specs=[tile] * (2 + len(branches))
        + [line] * 3
        + [
            pl.BlockSpec((model, step), lambda at: (0, at)),
            pl.BlockSpec((1, step), lambda at: (0, at)),
            pl.BlockSpec((step, model), lambda at: (at, 0)),
        ],
        out_specs=[
            pl.BlockSpec((2, rows, step), lambda at: (0, 0, at)),
            tile,
            tile,
            pl.BlockSpec((1, step), lambda at: (0, at)),
            tile,
            tile,
        ],
        out_shape=[
            struct((2, rows, units), BF16),
            struct((rows, model), BF16),
            struct((rows, model), F32),
            struct((1, units), F32),
            struct((rows, model), BF16),
            struct((rows, model), BF16),
        ],
        scratch_shapes=[pltpu.VMEM((rows, model), F32)] * 2,
        compiler_params=params,
        cost_estimate=cost(8 * rows * model * units, 16 * 2**20, 2 * rows * units),
        name="mlp",
    )(
        block_input,
        out_grad,
        *branches,
        output_bias[None],
        gain[None],
        shift[None],
        up_weight,
        up_bias[None],
        down_weight,
    )


def middle_kernel(count, hidden_ref, grad_ref, *refs):
    parts, refs = refs[:count], refs[count:]
    gain, output_weight, d_hidden_ref, d_branch_ref, d_attn_ref, sums_ref = refs
    unit, inverse = normalize(hidden_ref[...])
    d_mlp = parts[0][...].astype(F32)
    for part in parts[1:]:
        d_mlp += part[...].astype(F32)
    grad = grad_ref[...].astype(F32)
    d_hidden = grad + normalize_back(d_mlp * gain[...], unit, inverse)
    d_hidden_ref[...] = d_hidden
    d_branch = d_hidden.astype(BF16)
    d_branch_ref[...] = d_branch
    d_attn_ref[...] = product(output_weight[...], d_branch, 1, 1).astype(BF16)
    for at, values in enumerate((d_hidden, d_mlp * unit, d_mlp, grad)):
        sums_ref[pl.ds(at, 1), :] = jnp.sum(values, axis=0, keepdims=True)


def middle(hidden, out_grad, parts, gain, output_weight):
    rows, model = hidden.shape
    width = output_weight.shape[0]
    return pl.pallas_call(
        functools.partial(middle_kernel, len(parts)),
        out_shape=[
            struct((rows, model), F32),
            struct((rows, model), BF16),
            struct((width, rows), BF16),
            struct((4, model), F32),
        ],
        compiler_params=params,
        cost_estimate=cost(2 * rows * model * width, 6 * 2**20),
        name="middle",
    )(hidden, out_grad, *parts, gain[None], output_weight)


def load_keys(pieces, crops, keys, key_t, value_t, value_n):
    start = 0
    for piece in pieces:
        chips, _, patches = piece.shape
        for chip in range(chips):
            crop = lax.broadcasted_iota(jnp.int32, (HD, patches), 0)
            segment = piece[chip, pl.ds(seg_row, 16), :].astype(F32)[:1].astype(jnp.int32)
            mask = jnp.where((crop != segment) & (crop < crops), masked_value, 0.0)
            key = piece[chip, pl.ds(HD, HD), :]
            value = piece[chip, pl.ds(2 * HD, HD), :]
            place = pl.ds(start, patches)
            keys[place, :] = jnp.concatenate([key.astype(F32), mask], axis=0).T.astype(BF16)
            if key_t is not None:
                key_t[:, place] = key
            if value_t is not None:
                value_t[pl.ds(0, HD), place] = value
                value_t[pl.ds(HD, 16), place] = jnp.ones((16, patches), BF16)
            if value_n is not None:
                value_n[place, :] = value.astype(F32).T.astype(BF16)
            start += patches


def masked_query(query_ref):
    query = query_ref[0, pl.ds(0, HD), :].astype(F32) * 0.125
    segment = query_ref[0, pl.ds(seg_row, 16), :].astype(F32)[:1].astype(jnp.int32)
    crop = lax.broadcasted_iota(jnp.int32, query.shape, 0)
    onehot = jnp.where(crop == segment, 1.0, 0.0)
    return jnp.concatenate([query, onehot], axis=0).astype(BF16)


def forward_kernel(crops, step, query_ref, own, other, raw_ref, out_ref, logsum_ref, keys, value_t):
    @pl.when(pl.program_id(0) == 0)
    def _():
        load_keys((own, other), crops, keys, None, value_t, None)

    query = masked_query(query_ref)
    count = query.shape[1]
    top = jnp.full((1, count), masked_value, F32)
    accum = jnp.zeros((HD + 16, count), F32)
    for start in range(0, keys.shape[0], step):
        scores = product(keys[pl.ds(start, step), :], query)
        new_top = jnp.maximum(top, jnp.max(scores, axis=0, keepdims=True))
        weights = jnp.exp(scores - new_top).astype(BF16)
        accum = accum * jnp.exp(top - new_top) + product(value_t[:, pl.ds(start, step)], weights)
        top = new_top
    total = accum[HD : HD + 1]
    raw = accum[:HD] / total
    raw_ref[0] = raw
    out_ref[0] = raw.astype(BF16)
    logsum_ref[0] = top + jnp.log(total)


def backward_kernel(
    crops,
    before,
    query_ref,
    grad_ref,
    raw_ref,
    logsum_ref,
    *refs,
):
    before_refs, (piece, dquery_ref, sums_ref, keys, key_t, value_n, sums) = (
        refs[:before],
        refs[before:],
    )
    group = pl.program_id(0)

    @pl.when(group == 0)
    def _():
        load_keys((piece,), crops, keys, key_t, None, value_n)
        sums[...] = jnp.zeros_like(sums)

    query = masked_query(query_ref)
    grad = grad_ref[0]
    grad_wide = grad.astype(F32)
    delta = jnp.sum(grad_wide * raw_ref[0], axis=0, keepdims=True)
    scaled = query_ref[0, pl.ds(0, HD), :].astype(F32) * 0.125
    zero = jnp.zeros_like(scaled)
    query_side = jnp.concatenate([scaled, zero], axis=0).T.astype(BF16)
    grad_side = jnp.concatenate([zero, grad_wide], axis=0).T.astype(BF16)
    probs = jnp.exp(product(keys[...], query) - logsum_ref[0])
    dprobs = product(value_n[...], grad)
    dscores = (probs * (dprobs - delta)).astype(BF16)
    sums[...] += product(dscores, query_side) + product(probs.astype(BF16), grad_side)
    dquery = product(key_t[...], dscores) * 0.125
    for ref in before_refs:
        dquery = ref[0] + dquery
    dquery_ref[0] = dquery.astype(dquery_ref.dtype)

    @pl.when(group == pl.num_programs(0) - 1)
    def _():
        chips, _, patches = sums_ref.shape
        for chip in range(chips):
            sums_ref[chip] = sums[pl.ds(chip * patches, patches), :].T.astype(sums_ref.dtype)


def key_step(count):
    return 1024 if count % 1024 == 0 else 256


def query_spec(rows, patches):
    return pl.BlockSpec((1, rows, patches), lambda group: (group, 0, 0))


def attention_forward(queries, own, other, crops):
    groups, _, patches = queries.shape
    count = 2 * own.shape[0] * own.shape[2]
    return pl.pallas_call(
        functools.partial(forward_kernel, crops, key_step(count)),
        grid=(groups,),
        in_specs=[
            query_spec(payload_rows, patches),
            whole_spec(own.shape),
            whole_spec(other.shape),
        ],
        out_specs=[query_spec(HD, patches), query_spec(HD, patches), query_spec(1, patches)],
        out_shape=[
            struct((groups, HD, patches), F32),
            struct((groups, HD, patches), BF16),
            struct((groups, 1, patches), F32),
        ],
        scratch_shapes=[pltpu.VMEM((count, 2 * HD), BF16), pltpu.VMEM((HD + 16, count), BF16)],
        compiler_params=params,
        cost_estimate=cost(
            groups * patches * count * 4096, 4 * 2**20, groups * patches * count
        ),
        name="attention_forward",
    )(queries, own, other)


def backward_piece(queries, grads, raw, logsum, before, keys, index, pieces, crops, sums_type, last):
    groups, _, patches = queries.shape
    chips = keys.shape[0] // pieces
    count = chips * keys.shape[2]
    sums_shape = (chips, 2 * HD, keys.shape[2])
    return pl.pallas_call(
        functools.partial(backward_kernel, crops, len(before)),
        grid=(groups,),
        in_specs=[
            query_spec(payload_rows, patches),
            query_spec(HD, patches),
            query_spec(HD, patches),
            query_spec(1, patches),
        ]
        + [query_spec(HD, patches)] * len(before)
        + [pl.BlockSpec((chips,) + keys.shape[1:], lambda group: (index, 0, 0))],
        out_specs=[query_spec(HD, patches), whole_spec(sums_shape)],
        out_shape=[
            struct((groups, HD, patches), BF16 if last else F32),
            struct(sums_shape, sums_type),
        ],
        scratch_shapes=[
            pltpu.VMEM((count, 2 * HD), BF16),
            pltpu.VMEM((HD, count), BF16),
            pltpu.VMEM((count, HD), BF16),
            pltpu.VMEM((count, 2 * HD), F32),
        ],
        compiler_params=params,
        cost_estimate=cost(
            groups * patches * count * 4096, 4 * 2**20, groups * patches * count
        ),
        name="attention_backward",
    )(queries, grads, raw, logsum, *before, keys)


def swap_cores(values):
    return lax.ppermute(values, "core", [(0, 1), (1, 0)])


def to_heads(blocks):
    return lax.all_to_all(blocks, "chip", 0, 0, tiled=True)


def scatter_queries(values, heads, split):
    rows, patches = values.shape[0] // heads, values.shape[1]
    if split == 1:
        return to_heads(values.reshape(heads, rows, patches))
    part = patches // split
    blocks = values.reshape(heads, rows, split, part).transpose(0, 2, 1, 3)
    moved = to_heads(blocks.reshape(heads * split, rows, part))
    width = min(256, moved.shape[0] * part)
    joined = moved.transpose(1, 0, 2).reshape(rows, -1, width)
    return joined.transpose(1, 0, 2)


def gather_queries(values, heads, split, patches):
    rows = values.shape[1]
    if split == 1:
        return to_heads(values).reshape(heads * rows, patches)
    part = patches // split
    joined = values.transpose(1, 0, 2).reshape(rows, heads * split, part)
    moved = to_heads(joined.transpose(1, 0, 2)).reshape(heads, split, rows, part)
    return moved.transpose(0, 2, 1, 3).reshape(heads * rows, patches)


def across_heads(part):
    if lax.axis_size("head") == 2:
        return [part, lax.ppermute(part, "head", [(0, 1), (1, 0)])]
    return [lax.psum(part, "head")]


def ring_position():
    chips, chip = lax.axis_size("chip"), lax.axis_index("chip")
    return jnp.where(chip % 2 == 0, chip // 2, chips - 1 - chip // 2)


def ring_order():
    chips = lax.axis_size("chip")
    return list(range(0, chips, 2)) + list(range(chips - 1, 0, -2))


def ring_pairs(direction):
    order = ring_order()
    return [(order[at], order[(at + direction) % len(order)]) for at in range(len(order))]


def visit(streams, values):
    states, values = lax.optimization_barrier(([stream.state for stream in streams], values))
    for stream, state in zip(streams, states):
        stream.state = state
        stream.advance()
    return values


class Gather:
    def __init__(self, block):
        self.chips = lax.axis_size("chip")
        self.blocks = [(0, block)]
        self.step = 0
        self.state = []
        self.send([block, block])

    def send(self, arrived):
        self.step += 1
        reach = [self.chips // 2, (self.chips - 1) // 2]
        self.state = [
            lax.ppermute(block, "chip", ring_pairs(direction))
            for block, direction, steps in zip(arrived, (1, -1), reach)
            if self.step <= steps
        ]

    def advance(self):
        arrived = self.state
        for block, direction in zip(arrived, (-1, 1)):
            self.blocks.append((direction * self.step, block))
        self.send(arrived)

    def order(self):
        table = jnp.array(ring_order(), jnp.int32)
        steps = jnp.array([step for step, _ in self.blocks], jnp.int32)
        return table[(ring_position() + steps + self.chips) % self.chips]


def partial_kernel(core, grad, mlp_in, wide, grad_far, mlp_in_far, wide_far, out_ref):
    is_down = core[0] == 0

    @pl.when(is_down)
    def _():
        out_ref[...] = (
            product(wide[0], grad[...], 0, 0) + product(wide_far[...], grad_far[...], 0, 0)
        ).astype(BF16)

    @pl.when(jnp.logical_not(is_down))
    def _():
        out_ref[...] = (
            product(mlp_in[...], wide[0], 0, 0) + product(mlp_in_far[...], wide_far[...], 0, 0)
        ).astype(BF16)


def weight_partial(core, grad, mlp_in, wide, grad_far, mlp_in_far, wide_far):
    rows, model = grad.shape
    units = wide.shape[2]
    half = units // 2
    tile = whole_spec((rows, model))
    if model != half:
        down = product(wide[0], grad, 0, 0) + product(wide_far, grad_far, 0, 0)
        down = down.reshape(2, half, model).transpose(1, 0, 2).reshape(model, units)
        up = product(mlp_in, wide[1], 0, 0) + product(mlp_in_far, wide_far, 0, 0)
        return jnp.where(core == 0, down, up).astype(BF16)
    return pl.pallas_call(
        partial_kernel,
        grid_spec=pltpu.PrefetchScalarGridSpec(
            num_scalar_prefetch=1,
            grid=(2,),
            in_specs=[
                tile,
                tile,
                pl.BlockSpec((1, rows, half), lambda at, core: (core[0], 0, at)),
                tile,
                tile,
                pl.BlockSpec((rows, half), lambda at, core: (0, at)),
            ],
            out_specs=pl.BlockSpec((model, half), lambda at, core: (0, at)),
        ),
        out_shape=struct((model, units), BF16),
        compiler_params=params,
        cost_estimate=cost(4 * rows * model * units, 12 * 2**20),
        name="weight_partial",
    )(core[None], grad, mlp_in, wide, grad_far, mlp_in_far, wide_far)


def add_kernel(_, partial, arrived, output):
    output[...] = (arrived[...].astype(F32) + partial[...].astype(F32)).astype(BF16)


def place_kernel(order, *refs):
    near, far, down, up = refs[-4:]
    half = down.shape[2]

    def put(first, second):
        for side in range(2):
            down[side] = first[:, pl.ds(side * half, half)].astype(F32)
        up[...] = second[...].astype(F32)

    pl.when(order[2] == 0)(lambda: put(near, far))
    pl.when(order[2] != 0)(lambda: put(far, near))


class Ring:
    def __init__(self, partial, core):
        self.chips, self.partial, self.core = lax.axis_size("chip"), partial, core
        self.shape = (partial.shape[0] // self.chips, partial.shape[1])
        self.step, self.near = 1, None
        order, count = ring_order(), self.chips
        self.pairs = []
        for at in range(count):
            self.pairs.append((2 * order[at], 2 * order[(at + 1) % count]))
            self.pairs.append((2 * order[at] + 1, 2 * order[(at - 1) % count] + 1))
        block = lax.dynamic_slice_in_dim(partial, self.index() * self.shape[0], self.shape[0], 0)
        self.state = (self.send(block), [], [])

    def index(self, direction=None):
        if direction is None:
            direction = 1 - 2 * self.core
        return lax.rem(ring_position() + self.chips * 2 - direction * self.step, self.chips)

    def send(self, block):
        return [lax.ppermute(block, ("chip", "core"), self.pairs)]

    def add(self, block):
        whole = pl.BlockSpec(self.shape, lambda at, order: (0, 0))
        return pl.pallas_call(
            add_kernel,
            grid_spec=pltpu.PrefetchScalarGridSpec(
                num_scalar_prefetch=1,
                grid=(1,),
                in_specs=[pl.BlockSpec(self.shape, lambda at, order: (order[0], 0)), whole],
                out_specs=whole,
            ),
            out_shape=struct(self.shape, BF16),
            compiler_params=params,
            name="ring_add",
        )(self.index()[None].astype(jnp.int32), self.partial, block)

    def place(self, far, outputs):
        rows, columns = self.shape
        half = columns // 2
        order = jnp.stack([self.index(1), self.index(-1), self.core]).astype(jnp.int32)
        block = pl.BlockSpec(self.shape, lambda at, order: (0, 0))
        return pl.pallas_call(
            place_kernel,
            grid_spec=pltpu.PrefetchScalarGridSpec(
                num_scalar_prefetch=1,
                grid=(1,),
                in_specs=[pl.BlockSpec(memory_space=pl.ANY)] * len(outputs) + [block] * 2,
                out_specs=[
                    pl.BlockSpec((2, rows, half), lambda at, order: (0, order[0], 0)),
                    pl.BlockSpec((rows, columns), lambda at, order: (order[1], 0)),
                ],
            ),
            out_shape=[
                struct((2, self.chips * rows, half), F32),
                struct((self.chips * rows, columns), F32),
            ],
            input_output_aliases={1 + at: at for at in range(len(outputs))},
            compiler_params=params,
            name="place",
        )(order, *outputs, self.near, far)

    def advance(self):
        flying, swapped, outputs = self.state
        if swapped:
            outputs = self.place(swapped[0], outputs)
            swapped = []
        if flying:
            self.step += 1
            block, flying = flying[0], []
            if self.step <= self.chips:
                block = self.add(block)
            if self.step < 2 * self.chips - 1:
                flying = self.send(block)
            if self.step >= self.chips:
                self.near = block
                swapped = [swap_cores(block)]
        self.state = (flying, swapped, outputs)

    def busy(self):
        return bool(self.state[0] or self.state[1])


class Doubling:
    def __init__(self, values):
        chips = lax.axis_size("chip")
        self.moves = [lambda v: swap_cores(v)]
        reach = 1
        while reach < chips:
            pairs = [(chip, chip ^ reach) for chip in range(chips)]
            self.moves.append(functools.partial(lax.ppermute, axis_name="chip", perm=pairs))
            reach *= 2
        parts = across_heads(values)
        self.state = (parts[0], parts[1:])

    def advance(self):
        values, arrived = self.state
        for part in arrived:
            values = values + part
        self.state = (values, [self.moves.pop(0)(values)] if self.moves else [])

    def busy(self):
        return bool(self.state[1])


def head_gradient_kernel(count, order, query_ref, key_value_ref, *refs):
    blocks, (out_ref, accum) = refs[:count], refs[count:]
    at = pl.program_id(0)

    @pl.when(at == 0)
    def _():
        accum[...] = jnp.zeros_like(accum)

    grads = jnp.concatenate([query_ref[0], key_value_ref[0]], axis=0)
    for index, block in enumerate(blocks):

        @pl.when(at == index)
        def _(block=block):
            accum[...] += product(grads, block[...])

    @pl.when(at == count - 1)
    def _():
        out_ref[...] = accum[...].astype(BF16)


def head_gradient(dquery, key_value, inputs):
    count, rows, patches = dquery.shape
    blocks = [block for _, block in inputs.blocks]
    model = blocks[0].shape[1]
    return pl.pallas_call(
        functools.partial(head_gradient_kernel, count),
        grid_spec=pltpu.PrefetchScalarGridSpec(
            num_scalar_prefetch=1,
            grid=(count,),
            in_specs=[
                pl.BlockSpec((1, rows, patches), lambda at, order: (order[at], 0, 0)),
                pl.BlockSpec((1, 2 * rows, patches), lambda at, order: (order[at], 0, 0)),
            ]
            + [pl.BlockSpec((patches, model), lambda at, order: (0, 0))] * count,
            out_specs=pl.BlockSpec((3 * rows, model), lambda at, order: (0, 0)),
            scratch_shapes=[pltpu.VMEM((3 * rows, model), F32)],
        ),
        out_shape=struct((3 * rows, model), BF16),
        compiler_params=params,
        cost_estimate=cost(6 * rows * count * patches * model, 6 * 2**20),
        name="head_gradient",
    )(inputs.order(), dquery, key_value, *blocks)


def layout_kernel(count, size, order, *refs):
    near, far, outputs, (held,) = (
        refs[:count],
        refs[count : 2 * count],
        refs[2 * count : 2 * count + 3],
        refs[2 * count + 3 :],
    )
    at = pl.program_id(0)

    @pl.when(at == 0)
    def _():
        core = order[count]
        for index in range(count):
            head = order[index]
            for side, blocks in ((core, near), (1 - core, far)):
                held[head, side] = blocks[index][pl.ds(0, size), :]

    pair = [
        jnp.concatenate([held[2 * at + head, 0], held[2 * at + head, 1]], axis=0)
        for head in range(2)
    ]
    for index, output in enumerate(outputs):
        rows = [part[index * HD : index * HD + HD] for part in pair]
        output[...] = jnp.concatenate(rows, axis=0).astype(F32).T


def projection_outputs(gathered, far, core, size):
    count = gathered.chips
    blocks = [block for _, block in gathered.blocks]
    rows, model = blocks[0].shape
    order = jnp.concatenate([gathered.order(), core[None].astype(jnp.int32)])
    return pl.pallas_call(
        functools.partial(layout_kernel, count, size),
        grid_spec=pltpu.PrefetchScalarGridSpec(
            num_scalar_prefetch=1,
            grid=(count // 2,),
            in_specs=[pl.BlockSpec((rows, model), lambda at, order: (0, 0))] * (2 * count),
            out_specs=[pl.BlockSpec((model, 2 * HD), lambda at, order: (0, at))] * 3,
            scratch_shapes=[pltpu.VMEM((count, 2, size, model), BF16)],
        ),
        out_shape=[struct((model, count * HD), F32)] * 3,
        compiler_params=params,
        name="projection_outputs",
    )(order, *blocks, *far)


def core_half(values, axis, side):
    size = values.shape[axis] // 2
    return lax.dynamic_slice_in_dim(values, side * size, size, axis)


def share_halves(values, axis):
    core = lax.axis_index("core")
    return core_half(values, axis, core), swap_cores(core_half(values, axis, 1 - core))


def local(
    block_input,
    out_grad,
    segments,
    lead_steps,
    gain_attn,
    shift_attn,
    lead_weight,
    query_weight,
    key_weight,
    value_weight,
    output_weight,
    output_bias,
    gain_mlp,
    shift_mlp,
    up_weight,
    up_bias,
    down_weight,
    down_bias,
):
    rows, model = block_input.shape
    heads = query_weight.shape[1] // HD
    width = heads * HD
    chips, core = lax.axis_size("chip"), lax.axis_index("core")
    split = chips // heads
    crops = lead_steps.shape[0]
    weights = (query_weight, key_weight, value_weight)
    payload, attn_in = project(
        block_input, segments, lead_steps, gain_attn, shift_attn, lead_weight, weights
    )
    if split == 1:
        own = to_heads(payload)
        queries = own
    else:
        queries = scatter_queries(payload.reshape(-1, rows), heads, split)
        own = to_heads(jnp.repeat(payload, split, axis=0))
    own, attn_in = lax.optimization_barrier((own, attn_in))
    inputs = Gather(attn_in)
    grad_far = swap_cores(out_grad)
    raw, out, logsum = attention_forward(queries, own, swap_cores(own), crops)
    other = swap_cores(own)
    attn_out = gather_queries(out, heads, split, rows)
    attn_out = visit([inputs], attn_out)
    branches = across_heads(product(attn_out, output_weight, 0, 0).astype(BF16))
    branches = visit([inputs], branches)
    wide, mlp_in, hidden, dup_bias, mlp_part, d_mlp_part = mlp(
        block_input,
        out_grad,
        branches,
        output_bias,
        gain_mlp,
        shift_mlp,
        up_weight,
        up_bias,
        down_weight,
    )
    wide, mlp_in, d_mlp_part = visit([inputs], (wide, mlp_in, d_mlp_part))
    d_mlp = across_heads(d_mlp_part)
    mlp_in_far = swap_cores(mlp_in)
    wide_far = swap_cores(lax.dynamic_index_in_dim(wide, 1 - core, 0, keepdims=False))
    ring = Ring(
        weight_partial(core, out_grad, mlp_in, wide, grad_far, mlp_in_far, wide_far), core
    )
    d_mlp = visit([ring, inputs], d_mlp)
    mlp_part, d_mlp = lax.optimization_barrier((mlp_part, d_mlp))
    mlp_out = across_heads(mlp_part)
    d_hidden, d_branch, d_attn, sums = middle(hidden, out_grad, d_mlp, gain_mlp, output_weight)
    d_branch_far = swap_cores(d_branch)
    d_attn = visit([ring], d_attn)
    grads = scatter_queries(d_attn, heads, split)
    small = jnp.concatenate([sums.reshape(-1), dup_bias[0]])
    lines = small.shape[0] // chips
    small = jnp.pad(
        small.reshape(chips, 1, lines), ((0, 0), (0, small_rows - 1), (0, model - lines))
    )
    out_near, out_far = share_halves(attn_out, 0)
    doutput = product(out_near, d_branch) + product(out_far, d_branch_far)
    doutput = jnp.concatenate([doutput.reshape(chips, -1, model), small], axis=1).astype(BF16)
    pieces = 2
    dquery = []
    far_sums, near_sums = [], []
    for keys, piece_sums, sums_type in ((other, far_sums, BF16), (own, near_sums, F32)):
        for index in range(pieces):
            if keys is own and index == 0:
                doutput = to_heads(doutput)
            last = keys is own and index == pieces - 1
            if not last:
                grads, dquery, doutput = visit([ring], (grads, dquery, doutput))
            else:
                grads, dquery, doutput, mlp_out = visit([ring], (grads, dquery, doutput, mlp_out))
                doutput = jnp.sum(doutput.astype(F32), axis=0).astype(BF16)
                block_output = hidden + down_bias
                for part in mlp_out:
                    block_output += part.astype(F32)
                block_output = block_output.astype(BF16)
            *dquery, piece = backward_piece(
                queries, grads, raw, logsum, dquery, keys, index, pieces, crops, sums_type, last
            )
            piece_sums.append(piece)
    (dquery,) = dquery
    key_value = jnp.concatenate(
        [
            (near + swap_cores(far).astype(F32)).astype(BF16)
            for near, far in zip(near_sums, far_sums)
        ]
    )
    if split == 1:
        dquery, key_value = visit([ring], (dquery, key_value))
        moved = to_heads(jnp.concatenate([dquery, key_value], axis=1))
        projections = head_gradient(dquery, key_value, inputs)
        near, far = share_halves(projections, 0)
        projections = (near.astype(F32) + far.astype(F32)).astype(BF16)
        size = projections.shape[0]
        blocks = jnp.concatenate([projections, doutput], axis=0)
        dquery, dkey, dvalue = (
            moved[:, at * HD : at * HD + HD].reshape(width, rows) for at in range(3)
        )
    else:
        dquery = gather_queries(dquery, heads, split, rows)
        moved = to_heads(key_value).reshape(heads, split, 2 * HD, rows).astype(F32)
        moved = jnp.sum(moved, axis=1).astype(BF16)
        dkey, dvalue = (moved[:, at * HD : at * HD + HD].reshape(width, rows) for at in range(2))
        size, blocks = 0, doutput
        projections = [
            lax.psum(product(attn_in, grad, 0, 1).astype(BF16), ("chip", "core")).astype(F32)
            for grad in (dquery, dkey, dvalue)
        ]
    dquery, dkey, dvalue, blocks = visit([ring], (dquery, dkey, dvalue, blocks))
    gathered = Gather(blocks)
    d_part = (
        product(dquery, query_weight, 0, 1)
        + product(dkey, key_weight, 0, 1)
        + product(dvalue, value_weight, 0, 1)
    )
    unit_attn, inverse_attn = normalize(block_input.astype(F32))
    onehot = (segments[:, None] == jnp.arange(crops, dtype=jnp.int32)[None, :]).astype(F32)
    lead = jnp.sum(onehot * lead_steps.astype(F32)[None, :], axis=1) / 12.0
    ends = Doubling(
        jnp.stack(
            [
                jnp.sum(d_part * unit_attn, axis=0),
                jnp.sum(d_part, axis=0),
                jnp.sum(lead[:, None] * d_part, axis=0),
            ]
        )
    )
    d_in = across_heads(d_part.astype(BF16))
    d_in = visit([ring, gathered, ends], d_in)
    d_in = functools.reduce(jnp.add, (part.astype(F32) for part in d_in))
    input_grad = (d_hidden + normalize_back(d_in * gain_attn, unit_attn, inverse_attn)).astype(
        BF16
    )
    while ring.busy() or gathered.state or ends.busy():
        visit([ring, gathered, ends], ())
    ddown_weight, dup_weight = ring.state[2]
    ddown_weight = ddown_weight.reshape(-1, model)
    ends = ends.state[0]
    far = [swap_cores(block) for _, block in gathered.blocks]
    if split == 1:
        projections = projection_outputs(gathered, far, core, size)
    position = jnp.argsort(gathered.order())
    blocks = jnp.stack(
        [jnp.stack([block[size:] for _, block in gathered.blocks]), jnp.stack([block[size:] for block in far])]
    )
    blocks = jnp.take(jnp.where(core == 0, blocks, blocks[::-1]), position, axis=1)
    doutput_weight = blocks[:, :, :-small_rows].reshape(width, model).astype(F32)
    small = jnp.sum(blocks[:, :, -small_rows, :lines].astype(F32), axis=0).reshape(-1)
    dup_bias = small[4 * model :]
    small = [small[at * model : at * model + model] for at in range(4)]
    return (
        block_output,
        input_grad,
        ends[0],
        ends[1],
        ends[2],
        *projections,
        doutput_weight,
        *small[:3],
        dup_weight,
        dup_bias,
        ddown_weight,
        small[3],
    )


def solution(mesh):
    bands, halves = mesh.shape["band"], mesh.shape["head"]
    inner = Mesh(mesh.devices.reshape(bands // 2, 2, halves), ("chip", "core", "head"))
    band = ("chip", "core")
    rows, columns, split_rows = P(band, None), P(None, "head"), P("head", None)
    return jax.shard_map(
        local,
        mesh=inner,
        in_specs=(
            rows,
            rows,
            P(band),
            P(),
            P(),
            P(),
            P(),
            columns,
            columns,
            columns,
            split_rows,
            P(),
            P(),
            P(),
            columns,
            P("head"),
            split_rows,
            P(),
        ),
        out_specs=(
            rows,
            rows,
            P(),
            P(),
            P(),
            columns,
            columns,
            columns,
            split_rows,
            P(),
            P(),
            P(),
            columns,
            P("head"),
            split_rows,
            P(),
        ),
        check_vma=False,
    )
```

time: 469 us -> 377 us (0.80)
  waiting for transfers between devices: 268 us -> 98.1 us
  Pallas kernels: 46.1 us -> 147 us
  starting transfers between devices: 15 us -> 65.2 us
  matrix products: 29.5 us -> 2.73 us
  blocking collectives: 55.4 us -> 29.5 us
  other arithmetic: 31.9 us -> 14.1 us
  between operations: 14.8 us -> 1.85 us
  local copies, waits for them, and re-layouts: 8.16 us -> 16 us
    psum x1 -> x0, waiting for transfers between devices: 190 us -> none  [local(): lax.psum(grad.astype(BF16), ('chip', 'core')).astype(F32)]
    pallas_call x1 -> x25, Pallas kernels: 22.6 us -> 121 us  [the longest x4 38.5 us: backward_piece(): pl.pallas_call(functools.partial(backward_kernel, crops, len(before)), gr...]
    ppermute x10 -> x36, starting transfers between devices: 10.4 us -> 44.9 us  [the longest x14 21 us: send(): return [lax.ppermute(block, ('chip', 'core'), self.pairs)]]
    dot_general x18 -> x6, matrix products: 29.5 us -> 2.73 us  [product(): lax.dot_general(first, second, (((first_axis,), (second_axis,)), ((), ())...]
    all_to_all x3 -> x1, blocking collectives: 55.4 us -> 29.5 us  [to_heads(): return lax.all_to_all(blocks, 'chip', 0, 0, tiled=True)]
    convert_element_type x10 -> x5, other arithmetic: 20.2 us -> 3.58 us  [the longest x2 2.24 us: local(): (near + swap_cores(far).astype(F32)).astype(BF16)]
    all_to_all x1 -> x4, starting transfers between devices: 4.21 us -> 16.8 us  [to_heads(): return lax.all_to_all(blocks, 'chip', 0, 0, tiled=True)]
    all_to_all x1 -> x4, waiting for transfers between devices: 12.2 us -> 24.1 us  [to_heads(): return lax.all_to_all(blocks, 'chip', 0, 0, tiled=True)]
  transfers between devices with their start and end apart: 16 -> 66, of which waited for: 14 -> 26; matrix products, arithmetic and copies ran while one was open for 3% -> 6% of each run, Pallas kernels for 0% -> 35%
where the time goes in v5:
time: 377 us; the launch traced here: 374 us
  Pallas kernels  147 us (39%)
  waiting for transfers between devices  98.1 us (26%)
  starting transfers between devices  65.2 us (17%)
  blocking collectives  29.5 us (8%)
  local copies, waits for them, and re-layouts  16 us (4%)
  other arithmetic  14.1 us (4%)
    pallas_call x4, Pallas kernels, backward_piece(): pl.pallas_call(functools.partial(backward_kernel, crops, len(before)), gr...  38.5 us
    all_to_all x1, blocking collectives, to_heads(): return lax.all_to_all(blocks, 'chip', 0, 0, tiled=True)  29.5 us
    pallas_call x8, Pallas kernels, place(): pl.pallas_call(place_kernel, grid_spec=pltpu.PrefetchScalarGridSpec(num_s...  26.6 us
    pallas_call x1, Pallas kernels, attention_forward(): pl.pallas_call(functools.partial(forward_kernel, crops, key_step(count)),...  25.8 us
    all_to_all x4, waiting for transfers between devices, to_heads(): return lax.all_to_all(blocks, 'chip', 0, 0, tiled=True)  24.1 us
    ppermute x5, waiting for transfers between devices, across_heads(): return [part, lax.ppermute(part, 'head', [(0, 1), (1, 0)])]  21.2 us
    ppermute x14, starting transfers between devices, send(): return [lax.ppermute(block, ('chip', 'core'), self.pairs)]  21 us
    ppermute x14, waiting for transfers between devices, send(): return [lax.ppermute(block, ('chip', 'core'), self.pairs)]  18.9 us
  transfers between devices with their start and end apart: 66, of which 26 were waited for; matrix products, arithmetic and copies ran while one was open for 6% of the time, Pallas kernels for 35%

profile of v5, /device:TPU:0, one launch (start us, length us, event | category | flops | bytes accessed | tf_op | source)
XLA Modules:
  0.0 374.2 jit_solution(2940084697934595184)
XLA Ops:
  2.0 5.8 %project.1 = (bf16[8,208,256]{2,1,0:T(8,128)(2,1)}, bf16[256,1024]{1,0:T(8,128)(2,1)}) custom-call(bf16[256,1024]{1,0:T(8,128)(2,1)} %input_ref.3, s32[1,256]{1,0:T(1,128)} %bitcast.134, s32[32,128]{1,0:T(8,128)} %broadcast_in_dim.88.steps_ref, f32[1,1024]{1,0:T(1,128)} %bitcast.127, f32[1,1024]{1,0:T(1,128)} %bitcast.132, f32[1,1024]{1,0:T(1,128)} %bitcast.133, ...), custom_call_target="tpu_custom_call" | custom-call | flops 805306368 | bytes 8388608 | tf_op jit(solution)/shard_map/project/pallas_call | solution.py:88
  7.8 29.5 %all_to_all.25.query_ref.own.refs_1_ = bf16[8,208,256]{2,1,0:T(8,128)(2,1)S(1)} all-to-all(bf16[8,208,256]{2,1,0:T(8,128)(2,1)} %get-tuple-element.156), channel_id=1, replica_groups=mesh['chip'=8,'core'=2,'head'=2] {'chip'}, dimensions={0} | all-to-all | bytes 1703936 | tf_op jit(solution)/shard_map/all_to_all | solution.py:392
  40.6 25.8 %attention_forward.1 = (f32[8,64,256]{2,1,0:T(8,128)}, bf16[8,64,256]{2,1,0:T(8,128)(2,1)}, f32[8,1,256]{2,1,0:T(1,128)}) custom-call(bf16[8,208,256]{2,1,0:T(8,128)(2,1)} %copy-done.14, bf16[8,208,256]{2,1,0:T(8,128)(2,1)} %copy-done.14, bf16[8,208,256]{2,1,0:T(8,128)(2,1)} %copy-done.65), custom_call_target="tpu_custom_call" | custom-call | flops 34359738368 | bytes 4194304 | tf_op jit(solution)/shard_map/attention_forward/pallas_call | solution.py:329
  66.4 3.4 all-to-all-start.1
  69.8 9.4 %all-to-all-done.1 = bf16[8,64,256]{2,1,0:T(8,128)(2,1)S(1)} async-done(((bf16[8,64,256]{2,1,0:T(8,128)(2,1)}), bf16[8,64,256]{2,1,0:T(8,128)(2,1)S(1)}, u32[]{:S(2)}, u32[]{:S(2)}) %all-to-all-start.1) | async-done | bytes 262176 | tf_op jit(solution)/shard_map/all_to_all | solution.py:392
  79.7 1.6 collective-permute-start.5
  83.3 9.1 %collective-permute-done.5.refs_1_ = bf16[256,1024]{1,0:T(8,128)(2,1)S(1)} collective-permute-done((bf16[256,1024]{1,0:T(8,128)(2,1)S(1)}, bf16[256,1024]{1,0:T(8,128)(2,1)S(1)}, u32[]{:S(2)}, u32[]{:S(2)}) %collective-permute-start.5) | collective-permute-done | bytes 524320 | tf_op jit(solution)/shard_map/ppermute | solution.py:419
  94.1 1.7 collective-permute-start.6
  96.2 10.6 %mlp.1 = (bf16[2,256,2048]{2,1,0:T(8,128)(2,1)}, bf16[256,1024]{1,0:T(8,128)(2,1)}, f32[256,1024]{1,0:T(8,128)}, f32[1,2048]{1,0:T(1,128)}, bf16[256,1024]{1,0:T(8,128)(2,1)}, /*index=5*/bf16[256,1024]{1,0:T(8,128)(2,1)}) custom-call(bf16[256,1024]{1,0:T(8,128)(2,1)} %input_ref.3, bf16[256,1024]{1,0:T(8,128)(2,1)} %grad_ref.3, bf16[256,1024]{1,0:T(8,128)(2,1)} %copy-done.32, ...), custom_call_target="tpu_custom_call" | custom-call | flops 4294967296 | bytes 16777216 | tf_op jit(solution)/shard_map/mlp/pallas_call | solution.py:145
  108.1 2.3 dynamic-slice_bitcast_fusion
  117.2 5.8 %weight_partial.1.partial = bf16[1024,2048]{1,0:T(8,128)(2,1)} custom-call(s32[1]{0:T(128)} %bitcast.10.core, bf16[256,1024]{1,0:T(8,128)(2,1)} %grad_ref.3, bf16[256,1024]{1,0:T(8,128)(2,1)} %get-tuple-element.172.mlp_in, bf16[2,256,2048]{2,1,0:T(8,128)(2,1)} %get-tuple-element.173.wide, bf16[256,1024]{1,0:T(8,128)(2,1)} %copy-done.18, ...), custom_call_target="tpu_custom_call" | custom-call | flops 2147483648 | bytes 12582912 | tf_op jit(solution)/shard_map/weight_partial/pallas_call | solution.py:501
  124.1 2.0 collective-permute-start.11
  129.2 4.7 %collective-permute-done.11.arrived = bf16[128,2048]{1,0:T(8,128)(2,1)S(1)} collective-permute-done((bf16[128,2048]{1,0:T(8,128)(2,1)S(1)}, bf16[128,2048]{1,0:T(8,128)(2,1)S(1)}, u32[]{:S(2)}, u32[]{:S(2)}) %collective-permute-start.11) | collective-permute-done | bytes 524320 | tf_op jit(solution)/shard_map/ppermute | solution.py:559
  133.8 4.5 %middle.1 = (f32[256,1024]{1,0:T(8,128)}, bf16[256,1024]{1,0:T(8,128)(2,1)}, bf16[512,256]{1,0:T(8,128)(2,1)}, f32[4,1024]{1,0:T(4,128)}) custom-call(f32[256,1024]{1,0:T(8,128)} %get-tuple-element.166.hidden_ref, bf16[256,1024]{1,0:T(8,128)(2,1)} %grad_ref.3, bf16[256,1024]{1,0:T(8,128)(2,1)} %get-tuple-element.180.refs_0_, ...), custom_call_target="tpu_custom_call" | custom-call | flops 268435456 | bytes 6291456 | tf_op jit(solution)/shard_map/middle/pallas_call | solution.py:208
  138.3 2.1 ring_add.7
  142.1 7.8 %collective-permute-done.14.arrived = bf16[128,2048]{1,0:T(8,128)(2,1)S(1)} collective-permute-done((bf16[128,2048]{1,0:T(8,128)(2,1)}, bf16[128,2048]{1,0:T(8,128)(2,1)S(1)}, u32[]{:S(2)}, u32[]{:S(2)}) %collective-permute-start.14) | collective-permute-done | bytes 524320 | tf_op jit(solution)/shard_map/ppermute | solution.py:559
  150.7 2.1 ring_add.8
  154.2 3.4 all-to-all-start.2
  159.2 8.1 %all-to-all-done.2.grad_ref = bf16[8,64,256]{2,1,0:T(8,128)(2,1)S(1)} async-done(((bf16[8,64,256]{2,1,0:T(8,128)(2,1)}), bf16[8,64,256]{2,1,0:T(8,128)(2,1)S(1)}, u32[]{:S(2)}, u32[]{:S(2)}) %all-to-all-start.2) | async-done | bytes 262176 | tf_op jit(solution)/shard_map/all_to_all | solution.py:392
  168.1 2.1 ring_add.9
  171.2 9.5 %attention_backward.4 = (f32[8,64,256]{2,1,0:T(8,128)}, bf16[4,128,256]{2,1,0:T(8,128)(2,1)}) custom-call(bf16[8,208,256]{2,1,0:T(8,128)(2,1)} %copy-done.14, bf16[8,64,256]{2,1,0:T(8,128)(2,1)} %copy-done.57, f32[8,64,256]{2,1,0:T(8,128)} %get-tuple-element.190.raw_ref, f32[8,1,256]{2,1,0:T(1,128)} %get-tuple-element.191.logsum_ref, ...), custom_call_target="tpu_custom_call" | custom-call | flops 8589934592 | bytes 4194304 | tf_op jit(solution)/shard_map/attention_backward/pallas_call | solution.py:357
  180.8 5.1 %all-to-all-start.3 = ((bf16[8,40,1024]{2,1,0:T(8,128)(2,1)}), bf16[8,40,1024]{2,1,0:T(8,128)(2,1)S(1)}, u32[]{:S(2)}, u32[]{:S(2)}) async-start(bf16[8,40,1024]{2,1,0:T(8,128)(2,1)} %fusion.16), calls=%async_computation.3 | async-start | bytes 1310720 | tf_op jit(solution)/shard_map/all_to_all | solution.py:392
  187.4 2.1 ring_add.10
  189.5 2.0 collective-permute-start.19
  191.5 9.6 %attention_backward.5 = (f32[8,64,256]{2,1,0:T(8,128)}, bf16[4,128,256]{2,1,0:T(8,128)(2,1)}) custom-call(bf16[8,208,256]{2,1,0:T(8,128)(2,1)} %copy-done.14, bf16[8,64,256]{2,1,0:T(8,128)(2,1)} %copy-done.57, f32[8,64,256]{2,1,0:T(8,128)} %get-tuple-element.190.raw_ref, f32[8,1,256]{2,1,0:T(1,128)} %get-tuple-element.191.logsum_ref, ...), custom_call_target="tpu_custom_call" | custom-call | flops 8589934592 | bytes 4194304 | tf_op jit(solution)/shard_map/attention_backward/pallas_call | solution.py:357
  202.6 2.1 ring_add.11
  204.8 2.1 collective-permute-start.20
  206.9 9.8 %attention_backward.6 = (f32[8,64,256]{2,1,0:T(8,128)}, f32[4,128,256]{2,1,0:T(8,128)}) custom-call(bf16[8,208,256]{2,1,0:T(8,128)(2,1)} %copy-done.14, bf16[8,64,256]{2,1,0:T(8,128)(2,1)} %copy-done.57, f32[8,64,256]{2,1,0:T(8,128)} %get-tuple-element.190.raw_ref, f32[8,1,256]{2,1,0:T(1,128)} %get-tuple-element.191.logsum_ref, ...), custom_call_target="tpu_custom_call" | custom-call | flops 8589934592 | bytes 4194304 | tf_op jit(solution)/shard_map/attention_backward/pallas_call | solution.py:357
  218.6 2.1 ring_add.12
  220.7 2.4 collective-permute-start.22
  223.1 9.6 %attention_backward.7 = (bf16[8,64,256]{2,1,0:T(8,128)(2,1)}, f32[4,128,256]{2,1,0:T(8,128)}) custom-call(bf16[8,208,256]{2,1,0:T(8,128)(2,1)} %copy-done.14, bf16[8,64,256]{2,1,0:T(8,128)(2,1)} %copy-done.57, f32[8,64,256]{2,1,0:T(8,128)} %get-tuple-element.190.raw_ref, f32[8,1,256]{2,1,0:T(1,128)} %get-tuple-element.191.logsum_ref, ...), custom_call_target="tpu_custom_call" | custom-call | flops 8589934592 | bytes 4194304 | tf_op jit(solution)/shard_map/attention_backward/pallas_call | solution.py:357
  235.0 4.8 %all-to-all-start.4 = ((bf16[8,192,256]{2,1,0:T(8,128)(2,1)}), bf16[8,192,256]{2,1,0:T(8,128)(2,1)S(1)}, u32[]{:S(2)}, u32[]{:S(2)}) async-start(bf16[8,192,256]{2,1,0:T(8,128)(2,1)} %pad_maximum_fusion.1), calls=%async_computation.4 | async-start | bytes 1572864 | tf_op jit(solution)/shard_map/all_to_all | solution.py:392
  240.8 7.9 %head_gradient.1 = bf16[192,1024]{1,0:T(8,128)(2,1)} custom-call(s32[8]{0:T(128)} %copy-done.63, bf16[8,64,256]{2,1,0:T(8,128)(2,1)} %get-tuple-element.217.query_ref, bf16[8,128,256]{2,1,0:T(8,128)(2,1)} %copy-done.2, bf16[256,1024]{1,0:T(8,128)(2,1)} %get-tuple-element.158.refs_0_, bf16[256,1024]{1,0:T(8,128)(2,1)} %copy-done.33, ...), custom_call_target="tpu_custom_call" | custom-call | flops 805306368 | bytes 6291456 | tf_op jit(solution)/shard_map/head_gradient/pallas_call | solution.py:668
  249.8 2.2 ring_add.13.refs_0_
  252.0 2.0 collective-permute-start.25
  255.0 5.3 %all-to-all-done.4 = bf16[8,192,256]{2,1,0:T(8,128)(2,1)S(1)} async-done(((bf16[8,192,256]{2,1,0:T(8,128)(2,1)}), bf16[8,192,256]{2,1,0:T(8,128)(2,1)S(1)}, u32[]{:S(2)}, u32[]{:S(2)}) %all-to-all-start.4) | async-done | bytes 786464 | tf_op jit(solution)/shard_map/all_to_all | solution.py:392
  261.5 2.0 collective-permute-start.28
  265.7 2.5 collective-permute-start.33
  269.4 11.3 %collective-permute-done.32 = f32[3,1024]{1,0:T(4,128)S(1)} collective-permute-done((f32[3,1024]{1,0:T(4,128)S(1)}, f32[3,1024]{1,0:T(4,128)S(1)}, u32[]{:S(2)}, u32[]{:S(2)}) %collective-permute-start.32) | collective-permute-done | bytes 12320 | tf_op jit(solution)/shard_map/ppermute | solution.py:419
  280.7 1.6 collective-permute-start.30
  282.8 3.3 place.8
  286.1 2.8 collective-permute-done.30.refs_1_
  290.3 1.8 collective-permute-start.34
  295.7 3.3 place.9
  301.1 4.4 %collective-permute-done.36.refs_3_ = bf16[136,1024]{1,0:T(8,128)(2,1)S(1)} collective-permute-done((bf16[136,1024]{1,0:T(8,128)(2,1)S(1)}, bf16[136,1024]{1,0:T(8,128)(2,1)S(1)}, u32[]{:S(2)}, u32[]{:S(2)}) %collective-permute-start.36) | collective-permute-done | bytes 278560 | tf_op jit(solution)/shard_map/ppermute | solution.py:458
  305.5 2.4 collective-permute-done.37.refs_4_
  308.6 1.7 collective-permute-start.41
  310.9 3.3 place.10
  314.7 1.4 collective-permute-start.43
  316.1 7.4 %collective-permute-done.43 = f32[3,1024]{1,0:T(4,128)S(1)} collective-permute-done((f32[3,1024]{1,0:T(4,128)S(1)}, f32[3,1024]{1,0:T(4,128)S(1)}, u32[]{:S(2)}, u32[]{:S(2)}) %collective-permute-start.43) | collective-permute-done | bytes 12320 | tf_op jit(solution)/shard_map/ppermute | solution.py:638
  323.9 1.7 collective-permute-start.46
  326.2 3.3 place.11
  330.0 7.0 %collective-permute-done.47 = f32[3,1024]{1,0:T(4,128)S(1)} collective-permute-done((f32[3,1024]{1,0:T(4,128)S(1)}, f32[3,1024]{1,0:T(4,128)S(1)}, u32[]{:S(2)}, u32[]{:S(2)}) %collective-permute-start.47) | collective-permute-done | bytes 12320 | tf_op jit(solution)/shard_map/ppermute | solution.py:638
  336.9 1.7 collective-permute-done.46.refs_7_
  339.8 1.5 collective-permute-start.50
  341.3 3.3 place.12
  344.8 1.9 collective-permute-done.50
  346.7 1.4 collective-permute-done.48.refs_2_
  350.3 3.3 place.13
  353.6 3.8 %collective-permute-done.51.refs_2_ = bf16[128,2048]{1,0:T(8,128)(2,1)S(1)} collective-permute-done((bf16[128,2048]{1,0:T(8,128)(2,1)}, bf16[128,2048]{1,0:T(8,128)(2,1)S(1)}, u32[]{:S(2)}, u32[]{:S(2)}) %collective-permute-start.51) | collective-permute-done | bytes 524320 | tf_op jit(solution)/shard_map/ppermute | solution.py:559
  357.7 1.5 copy.57
  359.9 6.3 %projection_outputs.1 = (f32[1024,512]{1,0:T(8,128)}, f32[1024,512]{1,0:T(8,128)}, f32[1024,512]{1,0:T(8,128)}) custom-call(s32[9]{0:T(128)} %pad_add_fusion.order, bf16[136,1024]{1,0:T(8,128)(2,1)} %pad_maximum_fusion.3.refs_0_, bf16[136,1024]{1,0:T(8,128)(2,1)} %copy-done.43, bf16[136,1024]{1,0:T(8,128)(2,1)} %copy-done.44, bf16[136,1024]{1,0:T(8,128)(2,1)} %copy-done.45, ...), custom_call_target="tpu_custom_call" | custom-call | tf_op jit(solution)/shard_map/projection_outputs/pallas_call | solution.py:719
  366.8 3.3 place.14
  370.9 3.3 place.15
  (314 shorter events, 59.3 us)
Async XLA Ops:
  37.3 32.5 %collective-permute-start = (bf16[256,1024]{1,0:T(8,128)(2,1)}, bf16[256,1024]{1,0:T(8,128)(2,1)S(1)}, u32[]{:S(2)}, u32[]{:S(2)}) collective-permute-start(bf16[256,1024]{1,0:T(8,128)(2,1)} %get-tuple-element.158.refs_0_), channel_id=1, source_target_pairs={{0,8},{8,16},{16,24},{24,28},{28,20},{20,12},{12,4},{4,0},{1,9},{9... | collective-permute-start | bytes 1572872 | tf_op jit(solution)/shard_map/ppermute | solution.py:458
  38.1 31.8 %collective-permute-start.1 = (bf16[256,1024]{1,0:T(8,128)(2,1)}, bf16[256,1024]{1,0:T(8,128)(2,1)S(1)}, u32[]{:S(2)}, u32[]{:S(2)}) collective-permute-start(bf16[256,1024]{1,0:T(8,128)(2,1)} %get-tuple-element.158.refs_0_), channel_id=1, source_target_pairs={{0,4},{8,0},{16,8},{24,16},{28,24},{20,28},{12,20},{4,12},{1,5},{9... | collective-permute-start | bytes 1572872 | tf_op jit(solution)/shard_map/ppermute | solution.py:458
  66.4 12.9 %all-to-all-start.1 = ((bf16[8,64,256]{2,1,0:T(8,128)(2,1)}), bf16[8,64,256]{2,1,0:T(8,128)(2,1)S(1)}, u32[]{:S(2)}, u32[]{:S(2)}) async-start(bf16[8,64,256]{2,1,0:T(8,128)(2,1)} %get-tuple-element.160), calls=%async_computation.1 | async-start | bytes 524288 | tf_op jit(solution)/shard_map/all_to_all | solution.py:392
  79.7 12.7 %collective-permute-start.5 = (bf16[256,1024]{1,0:T(8,128)(2,1)S(1)}, bf16[256,1024]{1,0:T(8,128)(2,1)S(1)}, u32[]{:S(2)}, u32[]{:S(2)}) collective-permute-start(bf16[256,1024]{1,0:T(8,128)(2,1)S(1)} %convolution_convert_fusion.refs_0_), channel_id=1, source_target_pairs={{0,1},{1,0},{2,3},{3,2},{4,5},{5,4},{6,7},{7,6},{8,9},{9,8},{10,11... | collective-permute-start | bytes 1572872 | tf_op jit(solution)/shard_map/ppermute | solution.py:419
  81.3 12.3 %collective-permute-start.3 = (bf16[256,1024]{1,0:T(8,128)(2,1)S(1)}, bf16[256,1024]{1,0:T(8,128)(2,1)S(1)}, u32[]{:S(2)}, u32[]{:S(2)}) collective-permute-start(bf16[256,1024]{1,0:T(8,128)(2,1)S(1)} %collective-permute-done.refs_1_), channel_id=1, source_target_pairs={{0,8},{8,16},{16,24},{24,28},{28,20},{20,12},{12,4},{4,0},{1,9},{9... | collective-permute-start | bytes 1572872 | tf_op jit(solution)/shard_map/ppermute | solution.py:458
  82.3 11.8 %collective-permute-start.4 = (bf16[256,1024]{1,0:T(8,128)(2,1)S(1)}, bf16[256,1024]{1,0:T(8,128)(2,1)}, u32[]{:S(2)}, u32[]{:S(2)}) collective-permute-start(bf16[256,1024]{1,0:T(8,128)(2,1)S(1)} %collective-permute-done.1.refs_2_), channel_id=1, source_target_pairs={{0,4},{8,0},{16,8},{24,16},{28,24},{20,28},{12,20},{4,12},{1,5},{9... | collective-permute-start | bytes 1572872 | tf_op jit(solution)/shard_map/ppermute | solution.py:458
  94.1 12.7 %collective-permute-start.6 = (bf16[256,1024]{1,0:T(8,128)(2,1)S(1)}, bf16[256,1024]{1,0:T(8,128)(2,1)}, u32[]{:S(2)}, u32[]{:S(2)}) collective-permute-start(bf16[256,1024]{1,0:T(8,128)(2,1)S(1)} %collective-permute-done.3.refs_3_), channel_id=1, source_target_pairs={{0,8},{8,16},{16,24},{24,28},{28,20},{20,12},{12,4},{4,0},{1,9},{9... | collective-permute-start | bytes 1572872 | tf_op jit(solution)/shard_map/ppermute | solution.py:458
  95.9 12.2 %collective-permute-start.7 = (bf16[256,1024]{1,0:T(8,128)(2,1)}, bf16[256,1024]{1,0:T(8,128)(2,1)}, u32[]{:S(2)}, u32[]{:S(2)}) collective-permute-start(bf16[256,1024]{1,0:T(8,128)(2,1)} %collective-permute-done.4.refs_4_), channel_id=1, source_target_pairs={{0,4},{8,0},{16,8},{24,16},{28,24},{20,28},{12,20},{4,12},{1,5},{9... | collective-permute-start | bytes 1572872 | tf_op jit(solution)/shard_map/ppermute | solution.py:458
  110.4 5.0 %collective-permute-start.10 = (bf16[256,2048]{1,0:T(8,128)(2,1)}, bf16[256,2048]{1,0:T(8,128)(2,1)S(1)}, u32[]{:S(2)}, u32[]{:S(2)}) collective-permute-start(bf16[256,2048]{1,0:T(8,128)(2,1)} %dynamic-slice_bitcast_fusion), channel_id=1, source_target_pairs={{0,2},{2,0},{1,3},{3,1},{4,6},{6,4},{5,7},{7,5},{8,10},{10,8},{9,1... | collective-permute-start | bytes 3145736 | tf_op jit(solution)/shard_map/ppermute | solution.py:388
  110.4 5.0 %collective-permute-start.8 = (bf16[256,1024]{1,0:T(8,128)(2,1)S(1)}, bf16[256,1024]{1,0:T(8,128)(2,1)S(1)}, u32[]{:S(2)}, u32[]{:S(2)}) collective-permute-start(bf16[256,1024]{1,0:T(8,128)(2,1)S(1)} %copy-done.8), channel_id=1, source_target_pairs={{0,2},{2,0},{1,3},{3,1},{4,6},{6,4},{5,7},{7,5},{8,10},{10,8},{9,1... | collective-permute-start | bytes 1572872 | tf_op jit(solution)/shard_map/ppermute | solution.py:388
  110.9 4.5 %collective-permute-start.9 = (bf16[256,1024]{1,0:T(8,128)(2,1)S(1)}, bf16[256,1024]{1,0:T(8,128)(2,1)}, u32[]{:S(2)}, u32[]{:S(2)}) collective-permute-start(bf16[256,1024]{1,0:T(8,128)(2,1)S(1)} %copy-done.17), channel_id=1, source_target_pairs={{0,2},{2,0},{1,3},{3,1},{4,6},{6,4},{5,7},{7,5},{8,10},{10,8},{9,1... | collective-permute-start | bytes 1572872 | tf_op jit(solution)/shard_map/ppermute | solution.py:388
  113.7 14.6 %collective-permute-start.12 = (bf16[256,1024]{1,0:T(8,128)(2,1)}, bf16[256,1024]{1,0:T(8,128)(2,1)}, u32[]{:S(2)}, u32[]{:S(2)}) collective-permute-start(bf16[256,1024]{1,0:T(8,128)(2,1)} %collective-permute-done.6.refs_5_), channel_id=1, source_target_pairs={{0,8},{8,16},{16,24},{24,28},{28,20},{20,12},{12,4},{4,0},{1,9},{9... | collective-permute-start | bytes 1572872 | tf_op jit(solution)/shard_map/ppermute | solution.py:458
  114.9 14.3 %collective-permute-start.13 = (bf16[256,1024]{1,0:T(8,128)(2,1)}, bf16[256,1024]{1,0:T(8,128)(2,1)}, u32[]{:S(2)}, u32[]{:S(2)}) collective-permute-start(bf16[256,1024]{1,0:T(8,128)(2,1)} %get-tuple-element.180.refs_0_), channel_id=1, source_target_pairs={{0,1},{1,0},{2,3},{3,2},{4,5},{5,4},{6,7},{7,6},{8,9},{9,8},{10,11... | collective-permute-start | bytes 1572872 | tf_op jit(solution)/shard_map/ppermute | solution.py:419
  124.1 9.8 %collective-permute-start.11 = (bf16[128,2048]{1,0:T(8,128)(2,1)S(1)}, bf16[128,2048]{1,0:T(8,128)(2,1)S(1)}, u32[]{:S(2)}, u32[]{:S(2)}) collective-permute-start(bf16[128,2048]{1,0:T(8,128)(2,1)S(1)} %constant_dynamic-slice_fusion.2), channel_id=1, source_target_pairs={{0,8},{2,6},{8,16},{10,2},{16,24},{18,10},{24,28},{26,18},{28,20},... | collective-permute-start | bytes 1572872 | tf_op jit(solution)/shard_map/ppermute | solution.py:559
  138.3 19.3 %collective-permute-start.17 = (bf16[256,1024]{1,0:T(8,128)(2,1)}, bf16[256,1024]{1,0:T(8,128)(2,1)S(1)}, u32[]{:S(2)}, u32[]{:S(2)}) collective-permute-start(bf16[256,1024]{1,0:T(8,128)(2,1)} %get-tuple-element.185), channel_id=1, source_target_pairs={{0,2},{2,0},{1,3},{3,1},{4,6},{6,4},{5,7},{7,5},{8,10},{10,8},{9,1... | collective-permute-start | bytes 1572872 | tf_op jit(solution)/shard_map/ppermute | solution.py:388
  140.5 9.4 %collective-permute-start.14 = (bf16[128,2048]{1,0:T(8,128)(2,1)}, bf16[128,2048]{1,0:T(8,128)(2,1)S(1)}, u32[]{:S(2)}, u32[]{:S(2)}) collective-permute-start(bf16[128,2048]{1,0:T(8,128)(2,1)} %ring_add.7), channel_id=1, source_target_pairs={{0,8},{2,6},{8,16},{10,2},{16,24},{18,10},{24,28},{26,18},{28,20},... | collective-permute-start | bytes 1572872 | tf_op jit(solution)/shard_map/ppermute | solution.py:559
  141.9 15.7 %collective-permute-start.16 = (bf16[256,256]{1,0:T(8,128)(2,1)S(1)}, bf16[256,256]{1,0:T(8,128)(2,1)S(1)}, u32[]{:S(2)}, u32[]{:S(2)}) collective-permute-start(bf16[256,256]{1,0:T(8,128)(2,1)S(1)} %constant_dynamic-slice_fusion.1), channel_id=1, source_target_pairs={{0,2},{2,0},{1,3},{3,1},{4,6},{6,4},{5,7},{7,5},{8,10},{10,8},{9,1... | collective-permute-start | bytes 393224 | tf_op jit(solution)/shard_map/ppermute | solution.py:388
  152.8 14.5 %collective-permute-start.15 = (bf16[128,2048]{1,0:T(8,128)(2,1)}, bf16[128,2048]{1,0:T(8,128)(2,1)S(1)}, u32[]{:S(2)}, u32[]{:S(2)}) collective-permute-start(bf16[128,2048]{1,0:T(8,128)(2,1)} %ring_add.8), channel_id=1, source_target_pairs={{0,8},{2,6},{8,16},{10,2},{16,24},{18,10},{24,28},{26,18},{28,20},... | collective-permute-start | bytes 1572872 | tf_op jit(solution)/shard_map/ppermute | solution.py:559
  154.2 13.1 %all-to-all-start.2 = ((bf16[8,64,256]{2,1,0:T(8,128)(2,1)}), bf16[8,64,256]{2,1,0:T(8,128)(2,1)S(1)}, u32[]{:S(2)}, u32[]{:S(2)}) async-start(bf16[8,64,256]{2,1,0:T(8,128)(2,1)} %bitcast.16), calls=%async_computation.2 | async-start | bytes 524288 | tf_op jit(solution)/shard_map/all_to_all | solution.py:392
  170.3 10.5 %collective-permute-start.18 = (bf16[128,2048]{1,0:T(8,128)(2,1)}, bf16[128,2048]{1,0:T(8,128)(2,1)S(1)}, u32[]{:S(2)}, u32[]{:S(2)}) collective-permute-start(bf16[128,2048]{1,0:T(8,128)(2,1)} %ring_add.9), channel_id=1, source_target_pairs={{0,8},{2,6},{8,16},{10,2},{16,24},{18,10},{24,28},{26,18},{28,20},... | collective-permute-start | bytes 1572872 | tf_op jit(solution)/shard_map/ppermute | solution.py:559
  180.8 21.9 %all-to-all-start.3 = ((bf16[8,40,1024]{2,1,0:T(8,128)(2,1)}), bf16[8,40,1024]{2,1,0:T(8,128)(2,1)S(1)}, u32[]{:S(2)}, u32[]{:S(2)}) async-start(bf16[8,40,1024]{2,1,0:T(8,128)(2,1)} %fusion.16), calls=%async_computation.3 | async-start | bytes 1310720 | tf_op jit(solution)/shard_map/all_to_all | solution.py:392
  186.6 31.2 %collective-permute-start.21 = (bf16[256,1024]{1,0:T(8,128)(2,1)S(1)}, bf16[256,1024]{1,0:T(8,128)(2,1)S(1)}, u32[]{:S(2)}, u32[]{:S(2)}) collective-permute-start(bf16[256,1024]{1,0:T(8,128)(2,1)S(1)} %copy-done.15), channel_id=1, source_target_pairs={{0,1},{1,0},{2,3},{3,2},{4,5},{5,4},{6,7},{7,6},{8,9},{9,8},{10,11... | collective-permute-start | bytes 1572872 | tf_op jit(solution)/shard_map/ppermute | solution.py:419
  187.3 29.3 %collective-permute-start.23 = (bf16[4,128,256]{2,1,0:T(8,128)(2,1)}, bf16[4,128,256]{2,1,0:T(8,128)(2,1)S(1)}, u32[]{:S(2)}, u32[]{:S(2)}) collective-permute-start(bf16[4,128,256]{2,1,0:T(8,128)(2,1)} %get-tuple-element.213), channel_id=1, source_target_pairs={{0,2},{2,0},{1,3},{3,1},{4,6},{6,4},{5,7},{7,5},{8,10},{10,8},{9,1... | collective-permute-start | bytes 786440 | tf_op jit(solution)/shard_map/ppermute | solution.py:388
  189.5 11.9 %collective-permute-start.19 = (bf16[128,2048]{1,0:T(8,128)(2,1)}, bf16[128,2048]{1,0:T(8,128)(2,1)S(1)}, u32[]{:S(2)}, u32[]{:S(2)}) collective-permute-start(bf16[128,2048]{1,0:T(8,128)(2,1)} %ring_add.10), channel_id=1, source_target_pairs={{0,8},{2,6},{8,16},{10,2},{16,24},{18,10},{24,28},{26,18},{28,20},... | collective-permute-start | bytes 1572872 | tf_op jit(solution)/shard_map/ppermute | solution.py:559
  201.1 31.7 %collective-permute-start.24 = (bf16[4,128,256]{2,1,0:T(8,128)(2,1)}, bf16[4,128,256]{2,1,0:T(8,128)(2,1)S(1)}, u32[]{:S(2)}, u32[]{:S(2)}) collective-permute-start(bf16[4,128,256]{2,1,0:T(8,128)(2,1)} %get-tuple-element.215), channel_id=1, source_target_pairs={{0,2},{2,0},{1,3},{3,1},{4,6},{6,4},{5,7},{7,5},{8,10},{10,8},{9,1... | collective-permute-start | bytes 786440 | tf_op jit(solution)/shard_map/ppermute | solution.py:388
  204.8 13.0 %collective-permute-start.20 = (bf16[128,2048]{1,0:T(8,128)(2,1)}, bf16[128,2048]{1,0:T(8,128)(2,1)S(1)}, u32[]{:S(2)}, u32[]{:S(2)}) collective-permute-start(bf16[128,2048]{1,0:T(8,128)(2,1)} %ring_add.11), channel_id=1, source_target_pairs={{0,8},{2,6},{8,16},{10,2},{16,24},{18,10},{24,28},{26,18},{28,20},... | collective-permute-start | bytes 1572872 | tf_op jit(solution)/shard_map/ppermute | solution.py:559
  220.7 13.2 %collective-permute-start.22 = (bf16[128,2048]{1,0:T(8,128)(2,1)}, bf16[128,2048]{1,0:T(8,128)(2,1)}, u32[]{:S(2)}, u32[]{:S(2)}) collective-permute-start(bf16[128,2048]{1,0:T(8,128)(2,1)} %ring_add.12), channel_id=1, source_target_pairs={{0,8},{2,6},{8,16},{10,2},{16,24},{18,10},{24,28},{26,18},{28,20},... | collective-permute-start | bytes 1572872 | tf_op jit(solution)/shard_map/ppermute | solution.py:559
  235.0 25.3 %all-to-all-start.4 = ((bf16[8,192,256]{2,1,0:T(8,128)(2,1)}), bf16[8,192,256]{2,1,0:T(8,128)(2,1)S(1)}, u32[]{:S(2)}, u32[]{:S(2)}) async-start(bf16[8,192,256]{2,1,0:T(8,128)(2,1)} %pad_maximum_fusion.1), calls=%async_computation.4 | async-start | bytes 1572864 | tf_op jit(solution)/shard_map/all_to_all | solution.py:392
  249.6 4.6 %collective-permute-start.27 = (bf16[96,1024]{1,0:T(8,128)(2,1)S(1)}, bf16[96,1024]{1,0:T(8,128)(2,1)S(1)}, u32[]{:S(2)}, u32[]{:S(2)}) collective-permute-start(bf16[96,1024]{1,0:T(8,128)(2,1)S(1)} %constant_dynamic-slice_fusion), channel_id=1, source_target_pairs={{0,2},{2,0},{1,3},{3,1},{4,6},{6,4},{5,7},{7,5},{8,10},{10,8},{9,1... | collective-permute-start | bytes 589832 | tf_op jit(solution)/shard_map/ppermute | solution.py:388
  252.0 9.5 %collective-permute-start.25 = (bf16[128,2048]{1,0:T(8,128)(2,1)}, bf16[128,2048]{1,0:T(8,128)(2,1)}, u32[]{:S(2)}, u32[]{:S(2)}) collective-permute-start(bf16[128,2048]{1,0:T(8,128)(2,1)} %ring_add.13.refs_0_), channel_id=1, source_target_pairs={{0,8},{2,6},{8,16},{10,2},{16,24},{18,10},{24,28},{26,18},{28,20},... | collective-permute-start | bytes 1572872 | tf_op jit(solution)/shard_map/ppermute | solution.py:559
  254.0 7.5 %collective-permute-start.26 = (bf16[128,2048]{1,0:T(8,128)(2,1)}, bf16[128,2048]{1,0:T(8,128)(2,1)}, u32[]{:S(2)}, u32[]{:S(2)}) collective-permute-start(bf16[128,2048]{1,0:T(8,128)(2,1)} %ring_add.13.refs_0_), channel_id=1, source_target_pairs={{0,2},{2,0},{1,3},{3,1},{4,6},{6,4},{5,7},{7,5},{8,10},{10,8},{9,1... | collective-permute-start | bytes 1572872 | tf_op jit(solution)/shard_map/ppermute | solution.py:388
  261.5 28.7 %collective-permute-start.28 = (bf16[128,2048]{1,0:T(8,128)(2,1)}, bf16[128,2048]{1,0:T(8,128)(2,1)S(1)}, u32[]{:S(2)}, u32[]{:S(2)}) collective-permute-start(bf16[128,2048]{1,0:T(8,128)(2,1)} %collective-permute-done.25.refs_2_), channel_id=1, source_target_pairs={{0,8},{2,6},{8,16},{10,2},{16,24},{18,10},{24,28},{26,18},{28,20},... | collective-permute-start | bytes 1572872 | tf_op jit(solution)/shard_map/ppermute | solution.py:559
  263.5 26.7 %collective-permute-start.29 = (bf16[128,2048]{1,0:T(8,128)(2,1)}, bf16[128,2048]{1,0:T(8,128)(2,1)}, u32[]{:S(2)}, u32[]{:S(2)}) collective-permute-start(bf16[128,2048]{1,0:T(8,128)(2,1)} %collective-permute-done.25.refs_2_), channel_id=1, source_target_pairs={{0,2},{2,0},{1,3},{3,1},{4,6},{6,4},{5,7},{7,5},{8,10},{10,8},{9,1... | collective-permute-start | bytes 1572872 | tf_op jit(solution)/shard_map/ppermute | solution.py:388
  265.7 24.5 %collective-permute-start.33 = (bf16[256,1024]{1,0:T(8,128)(2,1)S(1)}, bf16[256,1024]{1,0:T(8,128)(2,1)S(1)}, u32[]{:S(2)}, u32[]{:S(2)}) collective-permute-start(bf16[256,1024]{1,0:T(8,128)(2,1)S(1)} %get-tuple-element.230), channel_id=1, source_target_pairs={{0,1},{1,0},{2,3},{3,2},{4,5},{5,4},{6,7},{7,6},{8,9},{9,8},{10,11... | collective-permute-start | bytes 1572872 | tf_op jit(solution)/shard_map/ppermute | solution.py:419
  268.2 12.5 %collective-permute-start.32 = (f32[3,1024]{1,0:T(4,128)S(1)}, f32[3,1024]{1,0:T(4,128)S(1)}, u32[]{:S(2)}, u32[]{:S(2)}) collective-permute-start(f32[3,1024]{1,0:T(4,128)S(1)} %pad_maximum_fusion.4), channel_id=1, source_target_pairs={{0,1},{1,0},{2,3},{3,2},{4,5},{5,4},{6,7},{7,6},{8,9},{9,8},{10,11... | collective-permute-start | bytes 36872 | tf_op jit(solution)/shard_map/ppermute | solution.py:419
  268.3 14.0 %collective-permute-start.54 = (bf16[136,1024]{1,0:T(8,128)(2,1)S(1)}, bf16[136,1024]{1,0:T(8,128)(2,1)S(1)}, u32[]{:S(2)}, u32[]{:S(2)}) collective-permute-start(bf16[136,1024]{1,0:T(8,128)(2,1)S(1)} %copy-done.10), channel_id=1, source_target_pairs={{0,2},{2,0},{1,3},{3,1},{4,6},{6,4},{5,7},{7,5},{8,10},{10,8},{9,1... | collective-permute-start | bytes 835592 | tf_op jit(solution)/shard_map/ppermute | solution.py:388
  280.7 8.2 %collective-permute-start.30 = (bf16[136,1024]{1,0:T(8,128)(2,1)S(1)}, bf16[136,1024]{1,0:T(8,128)(2,1)S(1)}, u32[]{:S(2)}, u32[]{:S(2)}) collective-permute-start(bf16[136,1024]{1,0:T(8,128)(2,1)S(1)} %copy-done.10), channel_id=1, source_target_pairs={{0,8},{8,16},{16,24},{24,28},{28,20},{20,12},{12,4},{4,0},{1,9},{9... | collective-permute-start | bytes 835592 | tf_op jit(solution)/shard_map/ppermute | solution.py:458
  282.3 7.9 %collective-permute-start.31 = (bf16[136,1024]{1,0:T(8,128)(2,1)S(1)}, bf16[136,1024]{1,0:T(8,128)(2,1)S(1)}, u32[]{:S(2)}, u32[]{:S(2)}) collective-permute-start(bf16[136,1024]{1,0:T(8,128)(2,1)S(1)} %copy-done.10), channel_id=1, source_target_pairs={{0,4},{8,0},{16,8},{24,16},{28,24},{20,28},{12,20},{4,12},{1,5},{9... | collective-permute-start | bytes 835592 | tf_op jit(solution)/shard_map/ppermute | solution.py:458
  290.3 17.6 %collective-permute-start.34 = (bf16[128,2048]{1,0:T(8,128)(2,1)S(1)}, bf16[128,2048]{1,0:T(8,128)(2,1)S(1)}, u32[]{:S(2)}, u32[]{:S(2)}) collective-permute-start(bf16[128,2048]{1,0:T(8,128)(2,1)S(1)} %collective-permute-done.28.refs_2_), channel_id=1, source_target_pairs={{0,8},{2,6},{8,16},{10,2},{16,24},{18,10},{24,28},{26,18},{28,20},... | collective-permute-start | bytes 1572872 | tf_op jit(solution)/shard_map/ppermute | solution.py:559
  292.1 15.9 %collective-permute-start.35 = (bf16[128,2048]{1,0:T(8,128)(2,1)S(1)}, bf16[128,2048]{1,0:T(8,128)(2,1)S(1)}, u32[]{:S(2)}, u32[]{:S(2)}) collective-permute-start(bf16[128,2048]{1,0:T(8,128)(2,1)S(1)} %collective-permute-done.28.refs_2_), channel_id=1, source_target_pairs={{0,2},{2,0},{1,3},{3,1},{4,6},{6,4},{5,7},{7,5},{8,10},{10,8},{9,1... | collective-permute-start | bytes 1572872 | tf_op jit(solution)/shard_map/ppermute | solution.py:388
  292.1 13.4 %collective-permute-start.36 = (bf16[136,1024]{1,0:T(8,128)(2,1)S(1)}, bf16[136,1024]{1,0:T(8,128)(2,1)S(1)}, u32[]{:S(2)}, u32[]{:S(2)}) collective-permute-start(bf16[136,1024]{1,0:T(8,128)(2,1)S(1)} %collective-permute-done.30.refs_1_), channel_id=1, source_target_pairs={{0,8},{8,16},{16,24},{24,28},{28,20},{20,12},{12,4},{4,0},{1,9},{9... | collective-permute-start | bytes 835592 | tf_op jit(solution)/shard_map/ppermute | solution.py:458
  293.4 5.6 %collective-permute-start.55 = (bf16[136,1024]{1,0:T(8,128)(2,1)S(1)}, bf16[136,1024]{1,0:T(8,128)(2,1)S(1)}, u32[]{:S(2)}, u32[]{:S(2)}) collective-permute-start(bf16[136,1024]{1,0:T(8,128)(2,1)S(1)} %collective-permute-done.30.refs_1_), channel_id=1, source_target_pairs={{0,2},{2,0},{1,3},{3,1},{4,6},{6,4},{5,7},{7,5},{8,10},{10,8},{9,1... | collective-permute-start | bytes 835592 | tf_op jit(solution)/shard_map/ppermute | solution.py:388
  293.7 6.1 %collective-permute-start.56 = (bf16[136,1024]{1,0:T(8,128)(2,1)S(1)}, bf16[136,1024]{1,0:T(8,128)(2,1)S(1)}, u32[]{:S(2)}, u32[]{:S(2)}) collective-permute-start(bf16[136,1024]{1,0:T(8,128)(2,1)S(1)} %collective-permute-done.31.refs_2_), channel_id=1, source_target_pairs={{0,2},{2,0},{1,3},{3,1},{4,6},{6,4},{5,7},{7,5},{8,10},{10,8},{9,1... | collective-permute-start | bytes 835592 | tf_op jit(solution)/shard_map/ppermute | solution.py:388
  299.1 8.8 %collective-permute-start.37 = (bf16[136,1024]{1,0:T(8,128)(2,1)S(1)}, bf16[136,1024]{1,0:T(8,128)(2,1)S(1)}, u32[]{:S(2)}, u32[]{:S(2)}) collective-permute-start(bf16[136,1024]{1,0:T(8,128)(2,1)S(1)} %collective-permute-done.31.refs_2_), channel_id=1, source_target_pairs={{0,4},{8,0},{16,8},{24,16},{28,24},{20,28},{12,20},{4,12},{1,5},{9... | collective-permute-start | bytes 835592 | tf_op jit(solution)/shard_map/ppermute | solution.py:458
  307.9 15.6 %collective-permute-start.39 = (bf16[128,2048]{1,0:T(8,128)(2,1)S(1)}, bf16[128,2048]{1,0:T(8,128)(2,1)S(1)}, u32[]{:S(2)}, u32[]{:S(2)}) collective-permute-start(bf16[128,2048]{1,0:T(8,128)(2,1)S(1)} %collective-permute-done.34.refs_2_), channel_id=1, source_target_pairs={{0,8},{2,6},{8,16},{10,2},{16,24},{18,10},{24,28},{26,18},{28,20},... | collective-permute-start | bytes 1572872 | tf_op jit(solution)/shard_map/ppermute | solution.py:559
  308.6 14.9 %collective-permute-start.40 = (bf16[128,2048]{1,0:T(8,128)(2,1)S(1)}, bf16[128,2048]{1,0:T(8,128)(2,1)S(1)}, u32[]{:S(2)}, u32[]{:S(2)}) collective-permute-start(bf16[128,2048]{1,0:T(8,128)(2,1)S(1)} %collective-permute-done.34.refs_2_), channel_id=1, source_target_pairs={{0,2},{2,0},{1,3},{3,1},{4,6},{6,4},{5,7},{7,5},{8,10},{10,8},{9,1... | collective-permute-start | bytes 1572872 | tf_op jit(solution)/shard_map/ppermute | solution.py:388
  308.6 14.8 %collective-permute-start.41 = (bf16[136,1024]{1,0:T(8,128)(2,1)S(1)}, bf16[136,1024]{1,0:T(8,128)(2,1)S(1)}, u32[]{:S(2)}, u32[]{:S(2)}) collective-permute-start(bf16[136,1024]{1,0:T(8,128)(2,1)S(1)} %collective-permute-done.36.refs_3_), channel_id=1, source_target_pairs={{0,8},{8,16},{16,24},{24,28},{28,20},{20,12},{12,4},{4,0},{1,9},{9... | collective-permute-start | bytes 835592 | tf_op jit(solution)/shard_map/ppermute | solution.py:458
  310.4 3.9 %collective-permute-start.57 = (bf16[136,1024]{1,0:T(8,128)(2,1)S(1)}, bf16[136,1024]{1,0:T(8,128)(2,1)S(1)}, u32[]{:S(2)}, u32[]{:S(2)}) collective-permute-start(bf16[136,1024]{1,0:T(8,128)(2,1)S(1)} %collective-permute-done.36.refs_3_), channel_id=1, source_target_pairs={{0,2},{2,0},{1,3},{3,1},{4,6},{6,4},{5,7},{7,5},{8,10},{10,8},{9,1... | collective-permute-start | bytes 835592 | tf_op jit(solution)/shard_map/ppermute | solution.py:388
  310.6 4.0 %collective-permute-start.58 = (bf16[136,1024]{1,0:T(8,128)(2,1)S(1)}, bf16[136,1024]{1,0:T(8,128)(2,1)S(1)}, u32[]{:S(2)}, u32[]{:S(2)}) collective-permute-start(bf16[136,1024]{1,0:T(8,128)(2,1)S(1)} %collective-permute-done.37.refs_4_), channel_id=1, source_target_pairs={{0,2},{2,0},{1,3},{3,1},{4,6},{6,4},{5,7},{7,5},{8,10},{10,8},{9,1... | collective-permute-start | bytes 835592 | tf_op jit(solution)/shard_map/ppermute | solution.py:388
  314.3 9.2 %collective-permute-start.42 = (bf16[136,1024]{1,0:T(8,128)(2,1)S(1)}, bf16[136,1024]{1,0:T(8,128)(2,1)S(1)}, u32[]{:S(2)}, u32[]{:S(2)}) collective-permute-start(bf16[136,1024]{1,0:T(8,128)(2,1)S(1)} %collective-permute-done.37.refs_4_), channel_id=1, source_target_pairs={{0,4},{8,0},{16,8},{24,16},{28,24},{20,28},{12,20},{4,12},{1,5},{9... | collective-permute-start | bytes 835592 | tf_op jit(solution)/shard_map/ppermute | solution.py:458
  314.7 8.8 %collective-permute-start.43 = (f32[3,1024]{1,0:T(4,128)S(1)}, f32[3,1024]{1,0:T(4,128)S(1)}, u32[]{:S(2)}, u32[]{:S(2)}) collective-permute-start(f32[3,1024]{1,0:T(4,128)S(1)} %add.269), channel_id=1, source_target_pairs={{0,4},{4,0},{8,12},{12,8},{16,20},{20,16},{24,28},{28,24},{1,5},{5... | collective-permute-start | bytes 36872 | tf_op jit(solution)/shard_map/ppermute | solution.py:638
  323.6 15.0 %collective-permute-start.44 = (bf16[128,2048]{1,0:T(8,128)(2,1)S(1)}, bf16[128,2048]{1,0:T(8,128)(2,1)S(1)}, u32[]{:S(2)}, u32[]{:S(2)}) collective-permute-start(bf16[128,2048]{1,0:T(8,128)(2,1)S(1)} %collective-permute-done.39.refs_2_), channel_id=1, source_target_pairs={{0,8},{2,6},{8,16},{10,2},{16,24},{18,10},{24,28},{26,18},{28,20},... | collective-permute-start | bytes 1572872 | tf_op jit(solution)/shard_map/ppermute | solution.py:559
  323.9 14.7 %collective-permute-start.45 = (bf16[128,2048]{1,0:T(8,128)(2,1)S(1)}, bf16[128,2048]{1,0:T(8,128)(2,1)S(1)}, u32[]{:S(2)}, u32[]{:S(2)}) collective-permute-start(bf16[128,2048]{1,0:T(8,128)(2,1)S(1)} %collective-permute-done.39.refs_2_), channel_id=1, source_target_pairs={{0,2},{2,0},{1,3},{3,1},{4,6},{6,4},{5,7},{7,5},{8,10},{10,8},{9,1... | collective-permute-start | bytes 1572872 | tf_op jit(solution)/shard_map/ppermute | solution.py:388
  323.9 14.7 %collective-permute-start.46 = (bf16[136,1024]{1,0:T(8,128)(2,1)S(1)}, bf16[136,1024]{1,0:T(8,128)(2,1)S(1)}, u32[]{:S(2)}, u32[]{:S(2)}) collective-permute-start(bf16[136,1024]{1,0:T(8,128)(2,1)S(1)} %collective-permute-done.41.refs_5_), channel_id=1, source_target_pairs={{0,8},{8,16},{16,24},{24,28},{28,20},{20,12},{12,4},{4,0},{1,9},{9... | collective-permute-start | bytes 835592 | tf_op jit(solution)/shard_map/ppermute | solution.py:458
  325.6 3.9 %collective-permute-start.59 = (bf16[136,1024]{1,0:T(8,128)(2,1)S(1)}, bf16[136,1024]{1,0:T(8,128)(2,1)S(1)}, u32[]{:S(2)}, u32[]{:S(2)}) collective-permute-start(bf16[136,1024]{1,0:T(8,128)(2,1)S(1)} %collective-permute-done.41.refs_5_), channel_id=1, source_target_pairs={{0,2},{2,0},{1,3},{3,1},{4,6},{6,4},{5,7},{7,5},{8,10},{10,8},{9,1... | collective-permute-start | bytes 835592 | tf_op jit(solution)/shard_map/ppermute | solution.py:388
  325.9 12.8 %collective-permute-start.60 = (bf16[136,1024]{1,0:T(8,128)(2,1)S(1)}, bf16[136,1024]{1,0:T(8,128)(2,1)S(1)}, u32[]{:S(2)}, u32[]{:S(2)}) collective-permute-start(bf16[136,1024]{1,0:T(8,128)(2,1)S(1)} %collective-permute-done.42.refs_6_), channel_id=1, source_target_pairs={{0,2},{2,0},{1,3},{3,1},{4,6},{6,4},{5,7},{7,5},{8,10},{10,8},{9,1... | collective-permute-start | bytes 835592 | tf_op jit(solution)/shard_map/ppermute | solution.py:388
  329.6 7.4 %collective-permute-start.47 = (f32[3,1024]{1,0:T(4,128)S(1)}, f32[3,1024]{1,0:T(4,128)S(1)}, u32[]{:S(2)}, u32[]{:S(2)}) collective-permute-start(f32[3,1024]{1,0:T(4,128)S(1)} %add.270), channel_id=1, source_target_pairs={{0,8},{4,12},{8,0},{12,4},{16,24},{20,28},{24,16},{28,20},{1,9},{5... | collective-permute-start | bytes 36872 | tf_op jit(solution)/shard_map/ppermute | solution.py:638
  338.6 6.0 %collective-permute-start.61 = (bf16[136,1024]{1,0:T(8,128)(2,1)S(1)}, bf16[136,1024]{1,0:T(8,128)(2,1)S(1)}, u32[]{:S(2)}, u32[]{:S(2)}) collective-permute-start(bf16[136,1024]{1,0:T(8,128)(2,1)S(1)} %collective-permute-done.46.refs_7_), channel_id=1, source_target_pairs={{0,2},{2,0},{1,3},{3,1},{4,6},{6,4},{5,7},{7,5},{8,10},{10,8},{9,1... | collective-permute-start | bytes 835592 | tf_op jit(solution)/shard_map/ppermute | solution.py:388
  338.7 9.3 %collective-permute-start.48 = (bf16[128,2048]{1,0:T(8,128)(2,1)S(1)}, bf16[128,2048]{1,0:T(8,128)(2,1)}, u32[]{:S(2)}, u32[]{:S(2)}) collective-permute-start(bf16[128,2048]{1,0:T(8,128)(2,1)S(1)} %collective-permute-done.44.refs_2_), channel_id=1, source_target_pairs={{0,8},{2,6},{8,16},{10,2},{16,24},{18,10},{24,28},{26,18},{28,20},... | collective-permute-start | bytes 1572872 | tf_op jit(solution)/shard_map/ppermute | solution.py:559
  339.6 8.5 %collective-permute-start.49 = (bf16[128,2048]{1,0:T(8,128)(2,1)S(1)}, bf16[128,2048]{1,0:T(8,128)(2,1)S(1)}, u32[]{:S(2)}, u32[]{:S(2)}) collective-permute-start(bf16[128,2048]{1,0:T(8,128)(2,1)S(1)} %collective-permute-done.44.refs_2_), channel_id=1, source_target_pairs={{0,2},{2,0},{1,3},{3,1},{4,6},{6,4},{5,7},{7,5},{8,10},{10,8},{9,1... | collective-permute-start | bytes 1572872 | tf_op jit(solution)/shard_map/ppermute | solution.py:388
  339.8 6.8 %collective-permute-start.50 = (f32[3,1024]{1,0:T(4,128)S(1)}, f32[3,1024]{1,0:T(4,128)S(1)}, u32[]{:S(2)}, u32[]{:S(2)}) collective-permute-start(f32[3,1024]{1,0:T(4,128)S(1)} %add.271), channel_id=1, source_target_pairs={{0,16},{4,20},{8,24},{12,28},{16,0},{20,4},{24,8},{28,12},{1,17},{... | collective-permute-start | bytes 36872 | tf_op jit(solution)/shard_map/ppermute | solution.py:638
  348.1 9.4 %collective-permute-start.51 = (bf16[128,2048]{1,0:T(8,128)(2,1)}, bf16[128,2048]{1,0:T(8,128)(2,1)S(1)}, u32[]{:S(2)}, u32[]{:S(2)}) collective-permute-start(bf16[128,2048]{1,0:T(8,128)(2,1)} %collective-permute-done.48.refs_2_), channel_id=1, source_target_pairs={{0,8},{2,6},{8,16},{10,2},{16,24},{18,10},{24,28},{26,18},{28,20},... | collective-permute-start | bytes 1572872 | tf_op jit(solution)/shard_map/ppermute | solution.py:559
  349.1 8.4 %collective-permute-start.52 = (bf16[128,2048]{1,0:T(8,128)(2,1)}, bf16[128,2048]{1,0:T(8,128)(2,1)}, u32[]{:S(2)}, u32[]{:S(2)}) collective-permute-start(bf16[128,2048]{1,0:T(8,128)(2,1)} %collective-permute-done.48.refs_2_), channel_id=1, source_target_pairs={{0,2},{2,0},{1,3},{3,1},{4,6},{6,4},{5,7},{7,5},{8,10},{10,8},{9,1... | collective-permute-start | bytes 1572872 | tf_op jit(solution)/shard_map/ppermute | solution.py:388
  357.5 12.6 %collective-permute-start.53 = (bf16[128,2048]{1,0:T(8,128)(2,1)S(1)}, bf16[128,2048]{1,0:T(8,128)(2,1)S(1)}, u32[]{:S(2)}, u32[]{:S(2)}) collective-permute-start(bf16[128,2048]{1,0:T(8,128)(2,1)S(1)} %collective-permute-done.51.refs_2_), channel_id=1, source_target_pairs={{0,2},{2,0},{1,3},{3,1},{4,6},{6,4},{5,7},{7,5},{8,10},{10,8},{9,1... | collective-permute-start | bytes 1572872 | tf_op jit(solution)/shard_map/ppermute | solution.py:388
  (70 other events, 567.9 us)

commit v6 on v5

--- a/solution.py
+++ b/solution.py
@@ -16,7 +16,8 @@
 seg_row = 3 * HD
 payload_rows = 3 * HD + 16
 small_rows = 8
-params = pltpu.CompilerParams(vmem_limit_bytes=56 * 2**20)
+params = pltpu.CompilerParams(vmem_limit_bytes=32 * 2**20)
+streaming = pltpu.CompilerParams(vmem_limit_bytes=60 * 2**20)
 
 
 def normalize(values):
@@ -280,10 +281,8 @@
     logsum_ref,
     *refs,
 ):
-    before_refs, (piece, dquery_ref, sums_ref, keys, key_t, value_n, sums) = (
-        refs[:before],
-        refs[before:],
-    )
+    before_refs, refs = refs[:before], refs[before:]
+    piece, (dquery_ref, sums_ref, keys, key_t, value_n, sums) = refs[0], refs[-6:]
     group = pl.program_id(0)
 
     @pl.when(group == 0)
@@ -349,7 +348,7 @@
     )(queries, own, other)
 
 
-def backward_piece(queries, grads, raw, logsum, before, keys, index, pieces, crops, sums_type, last):
+def backward_piece(queries, grads, raw, logsum, before, keys, earlier, index, pieces, crops, dtypes):
     groups, _, patches = queries.shape
     chips = keys.shape[0] // pieces
     count = chips * keys.shape[2]
@@ -364,12 +363,17 @@
             query_spec(1, patches),
         ]
         + [query_spec(HD, patches)] * len(before)
-        + [pl.BlockSpec((chips,) + keys.shape[1:], lambda group: (index, 0, 0))],
-        out_specs=[query_spec(HD, patches), whole_spec(sums_shape)],
+        + [pl.BlockSpec((chips,) + keys.shape[1:], lambda group: (index, 0, 0))]
+        + [pl.BlockSpec(memory_space=pl.ANY)] * len(earlier),
+        out_specs=[
+            query_spec(HD, patches),
+            pl.BlockSpec(sums_shape, lambda group: (index, 0, 0)),
+        ],
         out_shape=[
-            struct((groups, HD, patches), BF16 if last else F32),
-            struct(sums_shape, sums_type),
+            struct((groups, HD, patches), dtypes[0]),
+            struct((keys.shape[0],) + sums_shape[1:], dtypes[1]),
         ],
+        input_output_aliases={5 + len(before): 1} if earlier else {},
         scratch_shapes=[
             pltpu.VMEM((count, 2 * HD), BF16),
             pltpu.VMEM((HD, count), BF16),
@@ -381,7 +385,7 @@
             groups * patches * count * 4096, 4 * 2**20, groups * patches * count
         ),
         name="attention_backward",
-    )(queries, grads, raw, logsum, *before, keys)
+    )(queries, grads, raw, logsum, *before, keys, *earlier)
 
 
 def swap_cores(values):
@@ -514,7 +518,7 @@
             out_specs=pl.BlockSpec((model, half), lambda at, core: (0, at)),
         ),
         out_shape=struct((model, units), BF16),
-        compiler_params=params,
+        compiler_params=streaming,
         cost_estimate=cost(4 * rows * model * units, 12 * 2**20),
         name="weight_partial",
     )(core[None], grad, mlp_in, wide, grad_far, mlp_in_far, wide_far)
@@ -569,7 +573,7 @@
                 out_specs=whole,
             ),
             out_shape=struct(self.shape, BF16),
-            compiler_params=params,
+            compiler_params=streaming,
             name="ring_add",
         )(self.index()[None].astype(jnp.int32), self.partial, block)
 
@@ -594,7 +598,7 @@
                 struct((self.chips * rows, columns), F32),
             ],
             input_output_aliases={1 + at: at for at in range(len(outputs))},
-            compiler_params=params,
+            compiler_params=streaming,
             name="place",
         )(order, *outputs, self.near, far)
 
@@ -679,7 +683,7 @@
             scratch_shapes=[pltpu.VMEM((3 * rows, model), F32)],
         ),
         out_shape=struct((3 * rows, model), BF16),
-        compiler_params=params,
+        compiler_params=streaming,
         cost_estimate=cost(6 * rows * count * patches * model, 6 * 2**20),
         name="head_gradient",
     )(inputs.order(), dquery, key_value, *blocks)
@@ -726,7 +730,7 @@
             scratch_shapes=[pltpu.VMEM((count, 2, size, model), BF16)],
         ),
         out_shape=[struct((model, count * HD), F32)] * 3,
-        compiler_params=params,
+        compiler_params=streaming,
         name="projection_outputs",
     )(order, *blocks, *far)
 
@@ -797,8 +801,9 @@
         up_bias,
         down_weight,
     )
-    wide, mlp_in, d_mlp_part = visit([inputs], (wide, mlp_in, d_mlp_part))
     d_mlp = across_heads(d_mlp_part)
+    (wide, mlp_in), d_mlp_part = lax.optimization_barrier(((wide, mlp_in), d_mlp_part))
+    wide, mlp_in = visit([inputs], (wide, mlp_in))
     mlp_in_far = swap_cores(mlp_in)
     wide_far = swap_cores(lax.dynamic_index_in_dim(wide, 1 - core, 0, keepdims=False))
     ring = Ring(
@@ -809,7 +814,6 @@
     mlp_out = across_heads(mlp_part)
     d_hidden, d_branch, d_attn, sums = middle(hidden, out_grad, d_mlp, gain_mlp, output_weight)
     d_branch_far = swap_cores(d_branch)
-    d_attn = visit([ring], d_attn)
     grads = scatter_queries(d_attn, heads, split)
     small = jnp.concatenate([sums.reshape(-1), dup_bias[0]])
     lines = small.shape[0] // chips
@@ -819,16 +823,18 @@
     out_near, out_far = share_halves(attn_out, 0)
     doutput = product(out_near, d_branch) + product(out_far, d_branch_far)
     doutput = jnp.concatenate([doutput.reshape(chips, -1, model), small], axis=1).astype(BF16)
-    pieces = 2
-    dquery = []
-    far_sums, near_sums = [], []
-    for keys, piece_sums, sums_type in ((other, far_sums, BF16), (own, near_sums, F32)):
+    pieces = math.gcd(chips, 4)
+    dquery, sums = [], {}
+    for keys, dtype in ((other, BF16), (own, F32)):
+        piece_sums = []
         for index in range(pieces):
+            last = keys is own and index == pieces - 1
             if keys is own and index == 0:
+                grads, dquery, doutput = visit([ring], (grads, dquery, doutput))
+                far_sums = swap_cores(sums)
                 doutput = to_heads(doutput)
-            last = keys is own and index == pieces - 1
-            if not last:
-                grads, dquery, doutput = visit([ring], (grads, dquery, doutput))
+            elif not last:
+                grads, dquery = visit([ring], (grads, dquery))
             else:
                 grads, dquery, doutput, mlp_out = visit([ring], (grads, dquery, doutput, mlp_out))
                 doutput = jnp.sum(doutput.astype(F32), axis=0).astype(BF16)
@@ -836,17 +842,13 @@
                 for part in mlp_out:
                     block_output += part.astype(F32)
                 block_output = block_output.astype(BF16)
-            *dquery, piece = backward_piece(
-                queries, grads, raw, logsum, dquery, keys, index, pieces, crops, sums_type, last
+            dtypes = (BF16 if last else F32, dtype)
+            *dquery, sums = backward_piece(
+                queries, grads, raw, logsum, dquery, keys, piece_sums, index, pieces, crops, dtypes
             )
-            piece_sums.append(piece)
+            piece_sums = [sums]
     (dquery,) = dquery
-    key_value = jnp.concatenate(
-        [
-            (near + swap_cores(far).astype(F32)).astype(BF16)
-            for near, far in zip(near_sums, far_sums)
-        ]
-    )
+    key_value = (sums + far_sums.astype(F32)).astype(BF16)
     if split == 1:
         dquery, key_value = visit([ring], (dquery, key_value))
         moved = to_heads(jnp.concatenate([dquery, key_value], axis=1))

time: 377 us -> 376 us (level)
  local copies, waits for them, and re-layouts: 16 us -> 56.6 us
  waiting for transfers between devices: 98.1 us -> 59.7 us
  Pallas kernels: 147 us -> 132 us
  starting transfers between devices: 65.2 us -> 71.2 us
  matrix products: 2.73 us -> 6.95 us
    unnamed x151 -> x201, local copies, waits for them, and re-layouts: 5.66 us -> 45.7 us
    ppermute x5, waiting for transfers between devices: 21.2 us -> 9.18 us  [across_heads(): return [part, lax.ppermute(part, 'head', [(0, 1), (1, 0)])]]
    ppermute x3, waiting for transfers between devices: 16.2 us -> 4.85 us  [advance(): self.state = (values, [self.moves.pop(0)(values)] if self.moves else [])]
    ppermute x14, waiting for transfers between devices: 18.9 us -> 11.1 us  [send(): return [lax.ppermute(block, ('chip', 'core'), self.pairs)]]
    pallas_call x4 -> x8, Pallas kernels: 38.5 us -> 30.9 us  [backward_piece(): pl.pallas_call(functools.partial(backward_kernel, crops, len(before)), gr...]
    ppermute x14, waiting for transfers between devices: 16.2 us -> 11.8 us  [send(): lax.ppermute(block, 'chip', ring_pairs(direction))]
    dot_general x6, matrix products: 2.73 us -> 6.95 us  [product(): lax.dot_general(first, second, (((first_axis,), (second_axis,)), ((), ())...]
  transfers between devices with their start and end apart: 66 -> 65, of which waited for: 26 -> 24; matrix products, arithmetic and copies ran while one was open for 6% -> 10% of each run, Pallas kernels for 35% -> 30%
where the time goes in v6:
time: 376 us; the launch traced here: 373 us
  Pallas kernels  132 us (35%)
  starting transfers between devices  71.2 us (19%)
  waiting for transfers between devices  59.7 us (16%)
  local copies, waits for them, and re-layouts  56.6 us (15%)
  blocking collectives  29.3 us (8%)
  other arithmetic  16.2 us (4%)
  matrix products  6.95 us (2%)
    unnamed x201, local copies, waits for them, and re-layouts  45.7 us
    pallas_call x8, Pallas kernels, backward_piece(): pl.pallas_call(functools.partial(backward_kernel, crops, len(before)), gr...  30.9 us
    all_to_all x1, blocking collectives, to_heads(): return lax.all_to_all(blocks, 'chip', 0, 0, tiled=True)  29.3 us
    pallas_call x8, Pallas kernels, place(): pl.pallas_call(place_kernel, grid_spec=pltpu.PrefetchScalarGridSpec(num_s...  27.1 us
    ppermute x14, starting transfers between devices, send(): return [lax.ppermute(block, ('chip', 'core'), self.pairs)]  24.2 us
    pallas_call x1, Pallas kernels, attention_forward(): pl.pallas_call(functools.partial(forward_kernel, crops, key_step(count)),...  24.1 us
    all_to_all x4, waiting for transfers between devices, to_heads(): return lax.all_to_all(blocks, 'chip', 0, 0, tiled=True)  20.6 us
    all_to_all x4, starting transfers between devices, to_heads(): return lax.all_to_all(blocks, 'chip', 0, 0, tiled=True)  17 us
  transfers between devices with their start and end apart: 65, of which 24 were waited for; matrix products, arithmetic and copies ran while one was open for 10% of the time, Pallas kernels for 30%

profile of v6, /device:TPU:0, one launch (start us, length us, event | category | flops | bytes accessed | tf_op | source)
XLA Modules:
  0.0 373.3 jit_solution(5183521963489224559)
XLA Ops:
  8.8 3.6 project.1
  12.5 29.3 %all_to_all.25.query_ref.own.refs_1_ = bf16[8,208,256]{2,1,0:T(8,128)(2,1)S(1)} all-to-all(bf16[8,208,256]{2,1,0:T(8,128)(2,1)S(1)} %get-tuple-element.170), channel_id=1, replica_groups=mesh['chip'=8,'core'=2,'head'=2] {'chip'}, dimensions={0} | all-to-all | bytes 1703936 | tf_op jit(solution)/shard_map/all_to_all | solution.py:396
  44.1 24.1 %attention_forward.1 = (f32[8,64,256]{2,1,0:T(8,128)S(1)}, bf16[8,64,256]{2,1,0:T(8,128)(2,1)}, f32[8,1,256]{2,1,0:T(1,128)S(1)}) custom-call(bf16[8,208,256]{2,1,0:T(8,128)(2,1)S(1)} %all_to_all.25.query_ref.own.refs_1_, bf16[8,208,256]{2,1,0:T(8,128)(2,1)S(1)} %all_to_all.25.query_ref.own.refs_1_, ...), custom_call_target="tpu_custom_call" | custom-call | flops 34359738368 | bytes 4194304 | tf_op jit(solution)/shard_map/attention_forward/pallas_call | solution.py:328
  69.1 3.6 all-to-all-start.1
  72.7 9.4 %all-to-all-done.1 = bf16[8,64,256]{2,1,0:T(8,128)(2,1)S(1)} async-done(((bf16[8,64,256]{2,1,0:T(8,128)(2,1)}), bf16[8,64,256]{2,1,0:T(8,128)(2,1)S(1)}, u32[]{:S(2)}, u32[]{:S(2)}) %all-to-all-start.1) | async-done | bytes 262176 | tf_op jit(solution)/shard_map/all_to_all | solution.py:396
  82.6 1.6 collective-permute-start.5
  87.0 8.3 %collective-permute-done.5.refs_1_ = bf16[256,1024]{1,0:T(8,128)(2,1)S(1)} collective-permute-done((bf16[256,1024]{1,0:T(8,128)(2,1)S(1)}, bf16[256,1024]{1,0:T(8,128)(2,1)S(1)}, u32[]{:S(2)}, u32[]{:S(2)}) %collective-permute-start.5) | collective-permute-done | bytes 524320 | tf_op jit(solution)/shard_map/ppermute | solution.py:423
  97.8 1.7 collective-permute-start.6
  100.9 2.2 copy-done.35
  103.1 2.2 copy-done.36
  106.3 7.5 %mlp.1 = (bf16[2,256,2048]{2,1,0:T(8,128)(2,1)S(1)}, bf16[256,1024]{1,0:T(8,128)(2,1)}, f32[256,1024]{1,0:T(8,128)S(1)}, f32[1,2048]{1,0:T(1,128)S(1)}, bf16[256...) custom-call(bf16[256,1024]{1,0:T(8,128)(2,1)S(1)} %copy-done.1, bf16[256,1024]{1,0:T(8,128)(2,1)S(1)} %copy-done.14, ...), custom_call_target="tpu_custom_call" | custom-call | flops 4294967296 | bytes 16777216 | tf_op jit(solution)/shard_map/mlp/pallas_call | solution.py:146
  117.8 1.7 collective-permute-start.12
  121.2 5.8 %weight_partial.1.partial = bf16[1024,2048]{1,0:T(8,128)(2,1)} custom-call(s32[1]{0:T(128)} %bitcast.10.core, bf16[256,1024]{1,0:T(8,128)(2,1)} %grad_ref.3, bf16[256,1024]{1,0:T(8,128)(2,1)} %get-tuple-element.188.mlp_in, bf16[2,256,2048]{2,1,0:T(8,128)(2,1)} %copy-done.2, bf16[256,1024]{1,0:T(8,128)(2,1)} %collective-permute-done.8.grad_far, ...), custom_call_target="tpu_custom_call" | custom-call | flops 2147483648 | bytes 12582912 | tf_op jit(solution)/shard_map/weight_partial/pallas_call | solution.py:505
  128.2 1.8 collective-permute-start.11
  132.4 5.3 %collective-permute-done.11.arrived = bf16[128,2048]{1,0:T(8,128)(2,1)S(1)} collective-permute-done((bf16[128,2048]{1,0:T(8,128)(2,1)S(1)}, bf16[128,2048]{1,0:T(8,128)(2,1)S(1)}, u32[]{:S(2)}, u32[]{:S(2)}) %collective-permute-start.11) | collective-permute-done | bytes 524320 | tf_op jit(solution)/shard_map/ppermute | solution.py:563
  138.5 2.3 ring_add.7
  140.7 1.7 collective-permute-start.14
  143.5 3.1 middle.1
  147.6 3.4 all-to-all-start.2
  153.0 6.8 %all-to-all-done.2.grad_ref = bf16[8,64,256]{2,1,0:T(8,128)(2,1)S(1)} async-done(((bf16[8,64,256]{2,1,0:T(8,128)(2,1)}), bf16[8,64,256]{2,1,0:T(8,128)(2,1)S(1)}, u32[]{:S(2)}, u32[]{:S(2)}) %all-to-all-start.2) | async-done | bytes 262176 | tf_op jit(solution)/shard_map/all_to_all | solution.py:396
  159.8 2.2 ring_add.8
  164.8 3.8 %attention_backward.8 = (f32[8,64,256]{2,1,0:T(8,128)S(1)}, bf16[8,128,256]{2,1,0:T(8,128)(2,1)S(1)}) custom-call(bf16[8,208,256]{2,1,0:T(8,128)(2,1)S(1)} %copy-done.20, bf16[8,64,256]{2,1,0:T(8,128)(2,1)S(1)} %all-to-all-done.2.grad_ref, f32[8,64,256]{2,1,0:T(8,128)S(1)} %copy-done.46, f32[8,1,256]{2,1,0:T(1,128)S(1)} %get-tuple-element.201.logsum_ref, ...), custom_call_target="tpu_custom_call" | custom-call | flops 4294967296 | bytes 4194304 | tf_op jit(solution)/shard_map/attention_backward/pallas_call | solution.py:356
  169.4 2.1 collective-permute-done.15.arrived
  171.5 2.2 ring_add.9
  174.8 2.4 fusion.32
  178.2 3.8 %attention_backward.9 = (f32[8,64,256]{2,1,0:T(8,128)S(1)}, bf16[8,128,256]{2,1,0:T(8,128)(2,1)S(1)}) custom-call(bf16[8,208,256]{2,1,0:T(8,128)(2,1)S(1)} %copy-done.20, bf16[8,64,256]{2,1,0:T(8,128)(2,1)S(1)} %all-to-all-done.2.grad_ref, f32[8,64,256]{2,1,0:T(8,128)S(1)} %copy-done.47, ...), custom_call_target="tpu_custom_call", output_to_operand_aliasing={{1}: (6, {})} | custom-call | flops 4294967296 | bytes 4194304 | tf_op jit(solution)/shard_map/attention_backward/pallas_call | solution.py:356
  183.2 2.1 ring_add.10
  186.4 2.4 fusion.2
  188.8 3.9 %attention_backward.10 = (f32[8,64,256]{2,1,0:T(8,128)S(1)}, bf16[8,128,256]{2,1,0:T(8,128)(2,1)S(1)}) custom-call(bf16[8,208,256]{2,1,0:T(8,128)(2,1)S(1)} %copy-done.20, bf16[8,64,256]{2,1,0:T(8,128)(2,1)S(1)} %all-to-all-done.2.grad_ref, f32[8,64,256]{2,1,0:T(8,128)S(1)} %copy-done.47, ...), custom_call_target="tpu_custom_call", output_to_operand_aliasing={{1}: (6, {})} | custom-call | flops 4294967296 | bytes 4194304 | tf_op jit(solution)/shard_map/attention_backward/pallas_call | solution.py:356
  192.6 2.2 collective-permute-done.17.arrived
  194.8 2.1 ring_add.11
  198.0 2.0 fusion.16
  200.0 3.9 %attention_backward.11 = (f32[8,64,256]{2,1,0:T(8,128)S(1)}, bf16[8,128,256]{2,1,0:T(8,128)(2,1)S(1)}) custom-call(bf16[8,208,256]{2,1,0:T(8,128)(2,1)S(1)} %copy-done.20, bf16[8,64,256]{2,1,0:T(8,128)(2,1)S(1)} %all-to-all-done.2.grad_ref, f32[8,64,256]{2,1,0:T(8,128)S(1)} %copy-done.47, ...), custom_call_target="tpu_custom_call", output_to_operand_aliasing={{1}: (6, {})} | custom-call | flops 4294967296 | bytes 4194304 | tf_op jit(solution)/shard_map/attention_backward/pallas_call | solution.py:356
  207.1 2.2 ring_add.12
  211.7 4.2 %all-to-all-start.3 = ((bf16[8,40,1024]{2,1,0:T(8,128)(2,1)}), bf16[8,40,1024]{2,1,0:T(8,128)(2,1)}, u32[]{:S(2)}, u32[]{:S(2)}) async-start(bf16[8,40,1024]{2,1,0:T(8,128)(2,1)} %fusion.16), calls=%async_computation.3 | async-start | bytes 1310720 | tf_op jit(solution)/shard_map/all_to_all | solution.py:396
  216.9 3.9 %attention_backward.12 = (f32[8,64,256]{2,1,0:T(8,128)S(1)}, f32[8,128,256]{2,1,0:T(8,128)S(1)}) custom-call(bf16[8,208,256]{2,1,0:T(8,128)(2,1)S(1)} %copy-done.20, bf16[8,64,256]{2,1,0:T(8,128)(2,1)S(1)} %all-to-all-done.2.grad_ref, f32[8,64,256]{2,1,0:T(8,128)S(1)} %copy-done.48, f32[8,1,256]{2,1,0:T(1,128)S(1)} %get-tuple-element.201.logsum_ref, ...), custom_call_target="tpu_custom_call" | custom-call | flops 4294967296 | bytes 4194304 | tf_op jit(solution)/shard_map/attention_backward/pallas_call | solution.py:356
  221.8 2.2 ring_add.13.refs_0_
  224.1 4.9 %collective-permute-start.22 = (bf16[128,2048]{1,0:T(8,128)(2,1)}, bf16[128,2048]{1,0:T(8,128)(2,1)}, u32[]{:S(2)}, u32[]{:S(2)}) collective-permute-start(bf16[128,2048]{1,0:T(8,128)(2,1)} %ring_add.13.refs_0_), channel_id=1, source_target_pairs={{0,8},{2,6},{8,16},{10,2},{16,24},{18,10},{24,28},{26,18},{28,20},... | collective-permute-start | bytes 1572872 | tf_op jit(solution)/shard_map/ppermute | solution.py:563
  231.8 3.9 %attention_backward.13 = (f32[8,64,256]{2,1,0:T(8,128)S(1)}, f32[8,128,256]{2,1,0:T(8,128)S(1)}) custom-call(bf16[8,208,256]{2,1,0:T(8,128)(2,1)S(1)} %copy-done.20, bf16[8,64,256]{2,1,0:T(8,128)(2,1)S(1)} %all-to-all-done.2.grad_ref, f32[8,64,256]{2,1,0:T(8,128)S(1)} %copy-done.49, ...), custom_call_target="tpu_custom_call", output_to_operand_aliasing={{1}: (6, {})} | custom-call | flops 4294967296 | bytes 4194304 | tf_op jit(solution)/shard_map/attention_backward/pallas_call | solution.py:356
  236.5 2.5 collective-permute-start.24
  239.7 2.3 collective-permute-start.29
  244.1 3.9 %attention_backward.14 = (f32[8,64,256]{2,1,0:T(8,128)S(1)}, f32[8,128,256]{2,1,0:T(8,128)S(1)}) custom-call(bf16[8,208,256]{2,1,0:T(8,128)(2,1)S(1)} %copy-done.20, bf16[8,64,256]{2,1,0:T(8,128)(2,1)S(1)} %all-to-all-done.2.grad_ref, f32[8,64,256]{2,1,0:T(8,128)S(1)} %copy-done.50, ...), custom_call_target="tpu_custom_call", output_to_operand_aliasing={{1}: (6, {})} | custom-call | flops 4294967296 | bytes 4194304 | tf_op jit(solution)/shard_map/attention_backward/pallas_call | solution.py:356
  248.8 3.3 place.8
  252.3 3.5 place.9
  256.8 3.9 %attention_backward.15 = (bf16[8,64,256]{2,1,0:T(8,128)(2,1)S(1)}, f32[8,128,256]{2,1,0:T(8,128)S(1)}) custom-call(bf16[8,208,256]{2,1,0:T(8,128)(2,1)S(1)} %copy-done.20, bf16[8,64,256]{2,1,0:T(8,128)(2,1)S(1)} %all-to-all-done.2.grad_ref, f32[8,64,256]{2,1,0:T(8,128)S(1)} %copy-done.51, ...), custom_call_target="tpu_custom_call", output_to_operand_aliasing={{1}: (6, {})} | custom-call | flops 4294967296 | bytes 4194304 | tf_op jit(solution)/shard_map/attention_backward/pallas_call | solution.py:356
  263.1 5.8 %all-to-all-start.4 = ((bf16[8,192,256]{2,1,0:T(8,128)(2,1)}), bf16[8,192,256]{2,1,0:T(8,128)(2,1)}, u32[]{:S(2)}, u32[]{:S(2)}) async-start(bf16[8,192,256]{2,1,0:T(8,128)(2,1)} %pad_maximum_fusion.1), calls=%async_computation.4 | async-start | bytes 1572864 | tf_op jit(solution)/shard_map/all_to_all | solution.py:396
  269.8 7.9 %head_gradient.1 = bf16[192,1024]{1,0:T(8,128)(2,1)} custom-call(s32[8]{0:T(128)} %copy-done.87, bf16[8,64,256]{2,1,0:T(8,128)(2,1)} %copy-done.18, bf16[8,128,256]{2,1,0:T(8,128)(2,1)} %copy-done.65, bf16[256,1024]{1,0:T(8,128)(2,1)} %copy-done.27, bf16[256,1024]{1,0:T(8,128)(2,1)} %collective-permute-done.refs_1_, bf16[256,1024]{1,0:T(8,128)(2,1)} %copy-done.74, ...), custom_call_target="tpu_custom_call" | custom-call | flops 805306368 | bytes 6291456 | tf_op jit(solution)/shard_map/head_gradient/pallas_call | solution.py:672
  280.8 1.7 collective-permute-start.30
  282.5 3.5 place.10
  286.1 4.4 %all-to-all-done.4 = bf16[8,192,256]{2,1,0:T(8,128)(2,1)} async-done(((bf16[8,192,256]{2,1,0:T(8,128)(2,1)}), bf16[8,192,256]{2,1,0:T(8,128)(2,1)}, u32[]{:S(2)}, u32[]{:S(2)}) %all-to-all-start.4) | async-done | bytes 786464 | tf_op jit(solution)/shard_map/all_to_all | solution.py:396
  292.8 3.3 collective-permute-start.33
  298.0 2.0 collective-permute-start.38
  300.0 2.1 add_convert_fusion.1
  302.1 1.8 collective-permute-start.36
  304.6 3.5 place.11
  309.0 1.5 collective-permute-done.36.refs_2_
  319.3 3.5 place.12
  325.6 6.2 %collective-permute-done.42.refs_4_ = bf16[136,1024]{1,0:T(8,128)(2,1)S(1)} collective-permute-done((bf16[136,1024]{1,0:T(8,128)(2,1)S(1)}, bf16[136,1024]{1,0:T(8,128)(2,1)S(1)}, u32[]{:S(2)}, u32[]{:S(2)}) %collective-permute-start.42) | collective-permute-done | bytes 278560 | tf_op jit(solution)/shard_map/ppermute | solution.py:462
  335.1 3.4 place.13
  342.4 4.8 %collective-permute-done.48 = f32[3,1024]{1,0:T(4,128)S(1)} collective-permute-done((f32[3,1024]{1,0:T(4,128)S(1)}, f32[3,1024]{1,0:T(4,128)S(1)}, u32[]{:S(2)}, u32[]{:S(2)}) %collective-permute-start.48) | collective-permute-done | bytes 12320 | tf_op jit(solution)/shard_map/ppermute | solution.py:642
  351.2 3.3 place.14
  356.7 1.7 collective-permute-start.52
  358.4 3.3 place.15
  367.0 6.3 %projection_outputs.1 = (f32[1024,512]{1,0:T(8,128)}, f32[1024,512]{1,0:T(8,128)}, f32[1024,512]{1,0:T(8,128)}) custom-call(s32[9]{0:T(128)} %pad_add_fusion.order, bf16[136,1024]{1,0:T(8,128)(2,1)} %copy-done.68, bf16[136,1024]{1,0:T(8,128)(2,1)} %collective-permute-done.35.refs_1_, bf16[136,1024]{1,0:T(8,128)(2,1)} %copy-done.78, ...), custom_call_target="tpu_custom_call" | custom-call | tf_op jit(solution)/shard_map/projection_outputs/pallas_call | solution.py:723
  (365 shorter events, 100.5 us)
Async XLA Ops:
  41.8 2.4 collective-permute-start.2
  41.8 30.9 %collective-permute-start.1 = (bf16[256,1024]{1,0:T(8,128)(2,1)S(1)}, bf16[256,1024]{1,0:T(8,128)(2,1)S(1)}, u32[]{:S(2)}, u32[]{:S(2)}) collective-permute-start(bf16[256,1024]{1,0:T(8,128)(2,1)S(1)} %get-tuple-element.172.refs_0_), channel_id=1, source_target_pairs={{0,4},{8,0},{16,8},{24,16},{28,24},{20,28},{12,20},{4,12},{1,5},{9... | collective-permute-start | bytes 1572872 | tf_op jit(solution)/shard_map/ppermute | solution.py:462
  42.6 30.1 %collective-permute-start = (bf16[256,1024]{1,0:T(8,128)(2,1)S(1)}, bf16[256,1024]{1,0:T(8,128)(2,1)}, u32[]{:S(2)}, u32[]{:S(2)}) collective-permute-start(bf16[256,1024]{1,0:T(8,128)(2,1)S(1)} %get-tuple-element.172.refs_0_), channel_id=1, source_target_pairs={{0,8},{8,16},{16,24},{24,28},{28,20},{20,12},{12,4},{4,0},{1,9},{9... | collective-permute-start | bytes 1572872 | tf_op jit(solution)/shard_map/ppermute | solution.py:462
  69.1 13.0 %all-to-all-start.1 = ((bf16[8,64,256]{2,1,0:T(8,128)(2,1)}), bf16[8,64,256]{2,1,0:T(8,128)(2,1)S(1)}, u32[]{:S(2)}, u32[]{:S(2)}) async-start(bf16[8,64,256]{2,1,0:T(8,128)(2,1)} %get-tuple-element.174), calls=%async_computation.1 | async-start | bytes 524288 | tf_op jit(solution)/shard_map/all_to_all | solution.py:396
  82.6 12.6 %collective-permute-start.5 = (bf16[256,1024]{1,0:T(8,128)(2,1)S(1)}, bf16[256,1024]{1,0:T(8,128)(2,1)S(1)}, u32[]{:S(2)}, u32[]{:S(2)}) collective-permute-start(bf16[256,1024]{1,0:T(8,128)(2,1)S(1)} %convolution_convert_fusion.refs_0_), channel_id=1, source_target_pairs={{0,1},{1,0},{2,3},{3,2},{4,5},{5,4},{6,7},{7,6},{8,9},{9,8},{10,11... | collective-permute-start | bytes 1572872 | tf_op jit(solution)/shard_map/ppermute | solution.py:423
  84.9 12.5 %collective-permute-start.3 = (bf16[256,1024]{1,0:T(8,128)(2,1)}, bf16[256,1024]{1,0:T(8,128)(2,1)}, u32[]{:S(2)}, u32[]{:S(2)}) collective-permute-start(bf16[256,1024]{1,0:T(8,128)(2,1)} %collective-permute-done.refs_1_), channel_id=1, source_target_pairs={{0,8},{8,16},{16,24},{24,28},{28,20},{20,12},{12,4},{4,0},{1,9},{9... | collective-permute-start | bytes 1572872 | tf_op jit(solution)/shard_map/ppermute | solution.py:462
  86.0 11.8 %collective-permute-start.4 = (bf16[256,1024]{1,0:T(8,128)(2,1)S(1)}, bf16[256,1024]{1,0:T(8,128)(2,1)}, u32[]{:S(2)}, u32[]{:S(2)}) collective-permute-start(bf16[256,1024]{1,0:T(8,128)(2,1)S(1)} %collective-permute-done.1.refs_2_), channel_id=1, source_target_pairs={{0,4},{8,0},{16,8},{24,16},{28,24},{20,28},{12,20},{4,12},{1,5},{9... | collective-permute-start | bytes 1572872 | tf_op jit(solution)/shard_map/ppermute | solution.py:462
  97.8 17.8 %collective-permute-start.6 = (bf16[256,1024]{1,0:T(8,128)(2,1)}, bf16[256,1024]{1,0:T(8,128)(2,1)}, u32[]{:S(2)}, u32[]{:S(2)}) collective-permute-start(bf16[256,1024]{1,0:T(8,128)(2,1)} %collective-permute-done.3.refs_3_), channel_id=1, source_target_pairs={{0,8},{8,16},{16,24},{24,28},{28,20},{20,12},{12,4},{4,0},{1,9},{9... | collective-permute-start | bytes 1572872 | tf_op jit(solution)/shard_map/ppermute | solution.py:462
  99.5 16.1 %collective-permute-start.7 = (bf16[256,1024]{1,0:T(8,128)(2,1)}, bf16[256,1024]{1,0:T(8,128)(2,1)}, u32[]{:S(2)}, u32[]{:S(2)}) collective-permute-start(bf16[256,1024]{1,0:T(8,128)(2,1)} %collective-permute-done.4.refs_4_), channel_id=1, source_target_pairs={{0,4},{8,0},{16,8},{24,16},{28,24},{20,28},{12,20},{4,12},{1,5},{9... | collective-permute-start | bytes 1572872 | tf_op jit(solution)/shard_map/ppermute | solution.py:462
  116.7 4.5 %collective-permute-start.10 = (bf16[256,2048]{1,0:T(8,128)(2,1)}, bf16[256,2048]{1,0:T(8,128)(2,1)}, u32[]{:S(2)}, u32[]{:S(2)}) collective-permute-start(bf16[256,2048]{1,0:T(8,128)(2,1)} %dynamic-slice_bitcast_fusion), channel_id=1, source_target_pairs={{0,2},{2,0},{1,3},{3,1},{4,6},{6,4},{5,7},{7,5},{8,10},{10,8},{9,1... | collective-permute-start | bytes 3145736 | tf_op jit(solution)/shard_map/ppermute | solution.py:392
  116.7 3.9 %collective-permute-start.8 = (bf16[256,1024]{1,0:T(8,128)(2,1)S(1)}, bf16[256,1024]{1,0:T(8,128)(2,1)}, u32[]{:S(2)}, u32[]{:S(2)}) collective-permute-start(bf16[256,1024]{1,0:T(8,128)(2,1)S(1)} %copy-done.14), channel_id=1, source_target_pairs={{0,2},{2,0},{1,3},{3,1},{4,6},{6,4},{5,7},{7,5},{8,10},{10,8},{9,1... | collective-permute-start | bytes 1572872 | tf_op jit(solution)/shard_map/ppermute | solution.py:392
  117.2 4.0 %collective-permute-start.9 = (bf16[256,1024]{1,0:T(8,128)(2,1)}, bf16[256,1024]{1,0:T(8,128)(2,1)}, u32[]{:S(2)}, u32[]{:S(2)}) collective-permute-start(bf16[256,1024]{1,0:T(8,128)(2,1)} %get-tuple-element.188.mlp_in), channel_id=1, source_target_pairs={{0,2},{2,0},{1,3},{3,1},{4,6},{6,4},{5,7},{7,5},{8,10},{10,8},{9,1... | collective-permute-start | bytes 1572872 | tf_op jit(solution)/shard_map/ppermute | solution.py:392
  117.2 15.1 %collective-permute-start.13 = (bf16[256,1024]{1,0:T(8,128)(2,1)}, bf16[256,1024]{1,0:T(8,128)(2,1)}, u32[]{:S(2)}, u32[]{:S(2)}) collective-permute-start(bf16[256,1024]{1,0:T(8,128)(2,1)} %copy-done.25), channel_id=1, source_target_pairs={{0,1},{1,0},{2,3},{3,2},{4,5},{5,4},{6,7},{7,6},{8,9},{9,8},{10,11... | collective-permute-start | bytes 1572872 | tf_op jit(solution)/shard_map/ppermute | solution.py:423
  117.8 14.6 %collective-permute-start.12 = (bf16[256,1024]{1,0:T(8,128)(2,1)}, bf16[256,1024]{1,0:T(8,128)(2,1)}, u32[]{:S(2)}, u32[]{:S(2)}) collective-permute-start(bf16[256,1024]{1,0:T(8,128)(2,1)} %collective-permute-done.6.refs_5_), channel_id=1, source_target_pairs={{0,8},{8,16},{16,24},{24,28},{28,20},{20,12},{12,4},{4,0},{1,9},{9... | collective-permute-start | bytes 1572872 | tf_op jit(solution)/shard_map/ppermute | solution.py:462
  128.2 9.5 %collective-permute-start.11 = (bf16[128,2048]{1,0:T(8,128)(2,1)S(1)}, bf16[128,2048]{1,0:T(8,128)(2,1)S(1)}, u32[]{:S(2)}, u32[]{:S(2)}) collective-permute-start(bf16[128,2048]{1,0:T(8,128)(2,1)S(1)} %constant_dynamic-slice_fusion.2), channel_id=1, source_target_pairs={{0,8},{2,6},{8,16},{10,2},{16,24},{18,10},{24,28},{26,18},{28,20},... | collective-permute-start | bytes 1572872 | tf_op jit(solution)/shard_map/ppermute | solution.py:563
  140.7 19.0 %collective-permute-start.14 = (bf16[128,2048]{1,0:T(8,128)(2,1)}, bf16[128,2048]{1,0:T(8,128)(2,1)}, u32[]{:S(2)}, u32[]{:S(2)}) collective-permute-start(bf16[128,2048]{1,0:T(8,128)(2,1)} %ring_add.7), channel_id=1, source_target_pairs={{0,8},{2,6},{8,16},{10,2},{16,24},{18,10},{24,28},{26,18},{28,20},... | collective-permute-start | bytes 1572872 | tf_op jit(solution)/shard_map/ppermute | solution.py:563
  147.6 12.2 %all-to-all-start.2 = ((bf16[8,64,256]{2,1,0:T(8,128)(2,1)}), bf16[8,64,256]{2,1,0:T(8,128)(2,1)S(1)}, u32[]{:S(2)}, u32[]{:S(2)}) async-start(bf16[8,64,256]{2,1,0:T(8,128)(2,1)} %bitcast.18), calls=%async_computation.2 | async-start | bytes 524288 | tf_op jit(solution)/shard_map/all_to_all | solution.py:396
  152.4 22.4 %collective-permute-start.19 = (bf16[256,256]{1,0:T(8,128)(2,1)}, bf16[256,256]{1,0:T(8,128)(2,1)}, u32[]{:S(2)}, u32[]{:S(2)}) collective-permute-start(bf16[256,256]{1,0:T(8,128)(2,1)} %constant_dynamic-slice_fusion.1), channel_id=1, source_target_pairs={{0,2},{2,0},{1,3},{3,1},{4,6},{6,4},{5,7},{7,5},{8,10},{10,8},{9,1... | collective-permute-start | bytes 393224 | tf_op jit(solution)/shard_map/ppermute | solution.py:392
  152.4 22.4 %collective-permute-start.20 = (bf16[256,1024]{1,0:T(8,128)(2,1)S(1)}, bf16[256,1024]{1,0:T(8,128)(2,1)}, u32[]{:S(2)}, u32[]{:S(2)}) collective-permute-start(bf16[256,1024]{1,0:T(8,128)(2,1)S(1)} %get-tuple-element.218), channel_id=1, source_target_pairs={{0,2},{2,0},{1,3},{3,1},{4,6},{6,4},{5,7},{7,5},{8,10},{10,8},{9,1... | collective-permute-start | bytes 1572872 | tf_op jit(solution)/shard_map/ppermute | solution.py:392
  162.0 9.5 %collective-permute-start.15 = (bf16[128,2048]{1,0:T(8,128)(2,1)}, bf16[128,2048]{1,0:T(8,128)(2,1)}, u32[]{:S(2)}, u32[]{:S(2)}) collective-permute-start(bf16[128,2048]{1,0:T(8,128)(2,1)} %ring_add.8), channel_id=1, source_target_pairs={{0,8},{2,6},{8,16},{10,2},{16,24},{18,10},{24,28},{26,18},{28,20},... | collective-permute-start | bytes 1572872 | tf_op jit(solution)/shard_map/ppermute | solution.py:563
  173.7 9.5 %collective-permute-start.16 = (bf16[128,2048]{1,0:T(8,128)(2,1)}, bf16[128,2048]{1,0:T(8,128)(2,1)}, u32[]{:S(2)}, u32[]{:S(2)}) collective-permute-start(bf16[128,2048]{1,0:T(8,128)(2,1)} %ring_add.9), channel_id=1, source_target_pairs={{0,8},{2,6},{8,16},{10,2},{16,24},{18,10},{24,28},{26,18},{28,20},... | collective-permute-start | bytes 1572872 | tf_op jit(solution)/shard_map/ppermute | solution.py:563
  185.3 9.5 %collective-permute-start.17 = (bf16[128,2048]{1,0:T(8,128)(2,1)}, bf16[128,2048]{1,0:T(8,128)(2,1)}, u32[]{:S(2)}, u32[]{:S(2)}) collective-permute-start(bf16[128,2048]{1,0:T(8,128)(2,1)} %ring_add.10), channel_id=1, source_target_pairs={{0,8},{2,6},{8,16},{10,2},{16,24},{18,10},{24,28},{26,18},{28,20},... | collective-permute-start | bytes 1572872 | tf_op jit(solution)/shard_map/ppermute | solution.py:563
  196.9 9.4 %collective-permute-start.18 = (bf16[128,2048]{1,0:T(8,128)(2,1)}, bf16[128,2048]{1,0:T(8,128)(2,1)S(1)}, u32[]{:S(2)}, u32[]{:S(2)}) collective-permute-start(bf16[128,2048]{1,0:T(8,128)(2,1)} %ring_add.11), channel_id=1, source_target_pairs={{0,8},{2,6},{8,16},{10,2},{16,24},{18,10},{24,28},{26,18},{28,20},... | collective-permute-start | bytes 1572872 | tf_op jit(solution)/shard_map/ppermute | solution.py:563
  209.3 12.5 %collective-permute-start.21 = (bf16[128,2048]{1,0:T(8,128)(2,1)}, bf16[128,2048]{1,0:T(8,128)(2,1)}, u32[]{:S(2)}, u32[]{:S(2)}) collective-permute-start(bf16[128,2048]{1,0:T(8,128)(2,1)} %ring_add.12), channel_id=1, source_target_pairs={{0,8},{2,6},{8,16},{10,2},{16,24},{18,10},{24,28},{26,18},{28,20},... | collective-permute-start | bytes 1572872 | tf_op jit(solution)/shard_map/ppermute | solution.py:563
  211.7 40.5 %all-to-all-start.3 = ((bf16[8,40,1024]{2,1,0:T(8,128)(2,1)}), bf16[8,40,1024]{2,1,0:T(8,128)(2,1)}, u32[]{:S(2)}, u32[]{:S(2)}) async-start(bf16[8,40,1024]{2,1,0:T(8,128)(2,1)} %fusion.16), calls=%async_computation.3 | async-start | bytes 1310720 | tf_op jit(solution)/shard_map/all_to_all | solution.py:396
  224.1 12.4 %collective-permute-start.23 = (bf16[128,2048]{1,0:T(8,128)(2,1)}, bf16[128,2048]{1,0:T(8,128)(2,1)}, u32[]{:S(2)}, u32[]{:S(2)}) collective-permute-start(bf16[128,2048]{1,0:T(8,128)(2,1)} %ring_add.13.refs_0_), channel_id=1, source_target_pairs={{0,2},{2,0},{1,3},{3,1},{4,6},{6,4},{5,7},{7,5},{8,10},{10,8},{9,1... | collective-permute-start | bytes 1572872 | tf_op jit(solution)/shard_map/ppermute | solution.py:392
  224.1 12.4 %collective-permute-start.22 = (bf16[128,2048]{1,0:T(8,128)(2,1)}, bf16[128,2048]{1,0:T(8,128)(2,1)}, u32[]{:S(2)}, u32[]{:S(2)}) collective-permute-start(bf16[128,2048]{1,0:T(8,128)(2,1)} %ring_add.13.refs_0_), channel_id=1, source_target_pairs={{0,8},{2,6},{8,16},{10,2},{16,24},{18,10},{24,28},{26,18},{28,20},... | collective-permute-start | bytes 1572872 | tf_op jit(solution)/shard_map/ppermute | solution.py:563
  229.6 22.5 %collective-permute-start.26 = (bf16[256,1024]{1,0:T(8,128)(2,1)S(1)}, bf16[256,1024]{1,0:T(8,128)(2,1)}, u32[]{:S(2)}, u32[]{:S(2)}) collective-permute-start(bf16[256,1024]{1,0:T(8,128)(2,1)S(1)} %copy-done.22), channel_id=1, source_target_pairs={{0,1},{1,0},{2,3},{3,2},{4,5},{5,4},{6,7},{7,6},{8,9},{9,8},{10,11... | collective-permute-start | bytes 1572872 | tf_op jit(solution)/shard_map/ppermute | solution.py:423
  236.5 15.6 %collective-permute-start.25 = (bf16[128,2048]{1,0:T(8,128)(2,1)}, bf16[128,2048]{1,0:T(8,128)(2,1)}, u32[]{:S(2)}, u32[]{:S(2)}) collective-permute-start(bf16[128,2048]{1,0:T(8,128)(2,1)} %collective-permute-done.22.refs_2_), channel_id=1, source_target_pairs={{0,2},{2,0},{1,3},{3,1},{4,6},{6,4},{5,7},{7,5},{8,10},{10,8},{9,1... | collective-permute-start | bytes 1572872 | tf_op jit(solution)/shard_map/ppermute | solution.py:392
  236.5 15.6 %collective-permute-start.24 = (bf16[128,2048]{1,0:T(8,128)(2,1)}, bf16[128,2048]{1,0:T(8,128)(2,1)}, u32[]{:S(2)}, u32[]{:S(2)}) collective-permute-start(bf16[128,2048]{1,0:T(8,128)(2,1)} %collective-permute-done.22.refs_2_), channel_id=1, source_target_pairs={{0,8},{2,6},{8,16},{10,2},{16,24},{18,10},{24,28},{26,18},{28,20},... | collective-permute-start | bytes 1572872 | tf_op jit(solution)/shard_map/ppermute | solution.py:563
  239.7 21.0 %collective-permute-start.29 = (bf16[8,128,256]{2,1,0:T(8,128)(2,1)}, bf16[8,128,256]{2,1,0:T(8,128)(2,1)}, u32[]{:S(2)}, u32[]{:S(2)}) collective-permute-start(bf16[8,128,256]{2,1,0:T(8,128)(2,1)} %copy-done.41), channel_id=1, source_target_pairs={{0,2},{2,0},{1,3},{3,1},{4,6},{6,4},{5,7},{7,5},{8,10},{10,8},{9,1... | collective-permute-start | bytes 1572872 | tf_op jit(solution)/shard_map/ppermute | solution.py:392
  252.1 9.9 %collective-permute-start.28 = (bf16[128,2048]{1,0:T(8,128)(2,1)}, bf16[128,2048]{1,0:T(8,128)(2,1)}, u32[]{:S(2)}, u32[]{:S(2)}) collective-permute-start(bf16[128,2048]{1,0:T(8,128)(2,1)} %collective-permute-done.24.refs_2_), channel_id=1, source_target_pairs={{0,2},{2,0},{1,3},{3,1},{4,6},{6,4},{5,7},{7,5},{8,10},{10,8},{9,1... | collective-permute-start | bytes 1572872 | tf_op jit(solution)/shard_map/ppermute | solution.py:392
  252.2 9.8 %collective-permute-start.27 = (bf16[128,2048]{1,0:T(8,128)(2,1)}, bf16[128,2048]{1,0:T(8,128)(2,1)}, u32[]{:S(2)}, u32[]{:S(2)}) collective-permute-start(bf16[128,2048]{1,0:T(8,128)(2,1)} %collective-permute-done.24.refs_2_), channel_id=1, source_target_pairs={{0,8},{2,6},{8,16},{10,2},{16,24},{18,10},{24,28},{26,18},{28,20},... | collective-permute-start | bytes 1572872 | tf_op jit(solution)/shard_map/ppermute | solution.py:563
  263.1 27.5 %all-to-all-start.4 = ((bf16[8,192,256]{2,1,0:T(8,128)(2,1)}), bf16[8,192,256]{2,1,0:T(8,128)(2,1)}, u32[]{:S(2)}, u32[]{:S(2)}) async-start(bf16[8,192,256]{2,1,0:T(8,128)(2,1)} %pad_maximum_fusion.1), calls=%async_computation.4 | async-start | bytes 1572864 | tf_op jit(solution)/shard_map/all_to_all | solution.py:396
  278.6 7.3 %collective-permute-start.32 = (bf16[96,1024]{1,0:T(8,128)(2,1)S(1)}, bf16[96,1024]{1,0:T(8,128)(2,1)S(1)}, u32[]{:S(2)}, u32[]{:S(2)}) collective-permute-start(bf16[96,1024]{1,0:T(8,128)(2,1)S(1)} %constant_dynamic-slice_fusion), channel_id=1, source_target_pairs={{0,2},{2,0},{1,3},{3,1},{4,6},{6,4},{5,7},{7,5},{8,10},{10,8},{9,1... | collective-permute-start | bytes 589832 | tf_op jit(solution)/shard_map/ppermute | solution.py:392
  280.7 11.0 %collective-permute-start.31 = (bf16[128,2048]{1,0:T(8,128)(2,1)}, bf16[128,2048]{1,0:T(8,128)(2,1)}, u32[]{:S(2)}, u32[]{:S(2)}) collective-permute-start(bf16[128,2048]{1,0:T(8,128)(2,1)} %collective-permute-done.27.refs_2_), channel_id=1, source_target_pairs={{0,2},{2,0},{1,3},{3,1},{4,6},{6,4},{5,7},{7,5},{8,10},{10,8},{9,1... | collective-permute-start | bytes 1572872 | tf_op jit(solution)/shard_map/ppermute | solution.py:392
  280.8 10.9 %collective-permute-start.30 = (bf16[128,2048]{1,0:T(8,128)(2,1)}, bf16[128,2048]{1,0:T(8,128)(2,1)}, u32[]{:S(2)}, u32[]{:S(2)}) collective-permute-start(bf16[128,2048]{1,0:T(8,128)(2,1)} %collective-permute-done.27.refs_2_), channel_id=1, source_target_pairs={{0,8},{2,6},{8,16},{10,2},{16,24},{18,10},{24,28},{26,18},{28,20},... | collective-permute-start | bytes 1572872 | tf_op jit(solution)/shard_map/ppermute | solution.py:563
  291.7 20.0 %collective-permute-start.34 = (bf16[128,2048]{1,0:T(8,128)(2,1)}, bf16[128,2048]{1,0:T(8,128)(2,1)}, u32[]{:S(2)}, u32[]{:S(2)}) collective-permute-start(bf16[128,2048]{1,0:T(8,128)(2,1)} %collective-permute-done.30.refs_2_), channel_id=1, source_target_pairs={{0,2},{2,0},{1,3},{3,1},{4,6},{6,4},{5,7},{7,5},{8,10},{10,8},{9,1... | collective-permute-start | bytes 1572872 | tf_op jit(solution)/shard_map/ppermute | solution.py:392
  292.8 19.0 %collective-permute-start.33 = (bf16[128,2048]{1,0:T(8,128)(2,1)}, bf16[128,2048]{1,0:T(8,128)(2,1)}, u32[]{:S(2)}, u32[]{:S(2)}) collective-permute-start(bf16[128,2048]{1,0:T(8,128)(2,1)} %collective-permute-done.30.refs_2_), channel_id=1, source_target_pairs={{0,8},{2,6},{8,16},{10,2},{16,24},{18,10},{24,28},{26,18},{28,20},... | collective-permute-start | bytes 1572872 | tf_op jit(solution)/shard_map/ppermute | solution.py:563
  296.1 7.8 %collective-permute-start.53 = (bf16[136,1024]{1,0:T(8,128)(2,1)S(1)}, bf16[136,1024]{1,0:T(8,128)(2,1)S(1)}, u32[]{:S(2)}, u32[]{:S(2)}) collective-permute-start(bf16[136,1024]{1,0:T(8,128)(2,1)S(1)} %pad_maximum_fusion.2.refs_0_), channel_id=1, source_target_pairs={{0,2},{2,0},{1,3},{3,1},{4,6},{6,4},{5,7},{7,5},{8,10},{10,8},{9,1... | collective-permute-start | bytes 835592 | tf_op jit(solution)/shard_map/ppermute | solution.py:392
  297.9 4.2 %collective-permute-start.37 = (f32[3,1024]{1,0:T(4,128)S(1)}, f32[3,1024]{1,0:T(4,128)S(1)}, u32[]{:S(2)}, u32[]{:S(2)}) collective-permute-start(f32[3,1024]{1,0:T(4,128)S(1)} %pad_maximum_fusion.3), channel_id=1, source_target_pairs={{0,1},{1,0},{2,3},{3,2},{4,5},{5,4},{6,7},{7,6},{8,9},{9,8},{10,11... | collective-permute-start | bytes 36872 | tf_op jit(solution)/shard_map/ppermute | solution.py:423
  298.0 14.7 %collective-permute-start.38 = (bf16[256,1024]{1,0:T(8,128)(2,1)S(1)}, bf16[256,1024]{1,0:T(8,128)(2,1)S(1)}, u32[]{:S(2)}, u32[]{:S(2)}) collective-permute-start(bf16[256,1024]{1,0:T(8,128)(2,1)S(1)} %get-tuple-element.276), channel_id=1, source_target_pairs={{0,1},{1,0},{2,3},{3,2},{4,5},{5,4},{6,7},{7,6},{8,9},{9,8},{10,11... | collective-permute-start | bytes 1572872 | tf_op jit(solution)/shard_map/ppermute | solution.py:423
  302.1 8.5 %collective-permute-start.36 = (bf16[136,1024]{1,0:T(8,128)(2,1)S(1)}, bf16[136,1024]{1,0:T(8,128)(2,1)S(1)}, u32[]{:S(2)}, u32[]{:S(2)}) collective-permute-start(bf16[136,1024]{1,0:T(8,128)(2,1)S(1)} %pad_maximum_fusion.2.refs_0_), channel_id=1, source_target_pairs={{0,4},{8,0},{16,8},{24,16},{28,24},{20,28},{12,20},{4,12},{1,5},{9... | collective-permute-start | bytes 835592 | tf_op jit(solution)/shard_map/ppermute | solution.py:462
  303.9 7.8 %collective-permute-start.35 = (bf16[136,1024]{1,0:T(8,128)(2,1)S(1)}, bf16[136,1024]{1,0:T(8,128)(2,1)}, u32[]{:S(2)}, u32[]{:S(2)}) collective-permute-start(bf16[136,1024]{1,0:T(8,128)(2,1)S(1)} %pad_maximum_fusion.2.refs_0_), channel_id=1, source_target_pairs={{0,8},{8,16},{16,24},{24,28},{28,20},{20,12},{12,4},{4,0},{1,9},{9... | collective-permute-start | bytes 835592 | tf_op jit(solution)/shard_map/ppermute | solution.py:462
  312.6 10.1 %collective-permute-start.54 = (bf16[136,1024]{1,0:T(8,128)(2,1)}, bf16[136,1024]{1,0:T(8,128)(2,1)}, u32[]{:S(2)}, u32[]{:S(2)}) collective-permute-start(bf16[136,1024]{1,0:T(8,128)(2,1)} %collective-permute-done.35.refs_1_), channel_id=1, source_target_pairs={{0,2},{2,0},{1,3},{3,1},{4,6},{6,4},{5,7},{7,5},{8,10},{10,8},{9,1... | collective-permute-start | bytes 835592 | tf_op jit(solution)/shard_map/ppermute | solution.py:392
  312.6 12.9 %collective-permute-start.41 = (bf16[136,1024]{1,0:T(8,128)(2,1)}, bf16[136,1024]{1,0:T(8,128)(2,1)}, u32[]{:S(2)}, u32[]{:S(2)}) collective-permute-start(bf16[136,1024]{1,0:T(8,128)(2,1)} %collective-permute-done.35.refs_1_), channel_id=1, source_target_pairs={{0,8},{8,16},{16,24},{24,28},{28,20},{20,12},{12,4},{4,0},{1,9},{9... | collective-permute-start | bytes 835592 | tf_op jit(solution)/shard_map/ppermute | solution.py:462
  314.0 17.8 %collective-permute-start.40 = (bf16[128,2048]{1,0:T(8,128)(2,1)}, bf16[128,2048]{1,0:T(8,128)(2,1)S(1)}, u32[]{:S(2)}, u32[]{:S(2)}) collective-permute-start(bf16[128,2048]{1,0:T(8,128)(2,1)} %collective-permute-done.33.refs_2_), channel_id=1, source_target_pairs={{0,2},{2,0},{1,3},{3,1},{4,6},{6,4},{5,7},{7,5},{8,10},{10,8},{9,1... | collective-permute-start | bytes 1572872 | tf_op jit(solution)/shard_map/ppermute | solution.py:392
  314.3 17.5 %collective-permute-start.39 = (bf16[128,2048]{1,0:T(8,128)(2,1)}, bf16[128,2048]{1,0:T(8,128)(2,1)S(1)}, u32[]{:S(2)}, u32[]{:S(2)}) collective-permute-start(bf16[128,2048]{1,0:T(8,128)(2,1)} %collective-permute-done.33.refs_2_), channel_id=1, source_target_pairs={{0,8},{2,6},{8,16},{10,2},{16,24},{18,10},{24,28},{26,18},{28,20},... | collective-permute-start | bytes 1572872 | tf_op jit(solution)/shard_map/ppermute | solution.py:563
  316.1 8.2 %collective-permute-start.55 = (bf16[136,1024]{1,0:T(8,128)(2,1)}, bf16[136,1024]{1,0:T(8,128)(2,1)}, u32[]{:S(2)}, u32[]{:S(2)}) collective-permute-start(bf16[136,1024]{1,0:T(8,128)(2,1)} %copy-done.78), channel_id=1, source_target_pairs={{0,2},{2,0},{1,3},{3,1},{4,6},{6,4},{5,7},{7,5},{8,10},{10,8},{9,1... | collective-permute-start | bytes 835592 | tf_op jit(solution)/shard_map/ppermute | solution.py:392
  322.8 9.0 %collective-permute-start.42 = (bf16[136,1024]{1,0:T(8,128)(2,1)S(1)}, bf16[136,1024]{1,0:T(8,128)(2,1)S(1)}, u32[]{:S(2)}, u32[]{:S(2)}) collective-permute-start(bf16[136,1024]{1,0:T(8,128)(2,1)S(1)} %copy-done.79), channel_id=1, source_target_pairs={{0,4},{8,0},{16,8},{24,16},{28,24},{20,28},{12,20},{4,12},{1,5},{9... | collective-permute-start | bytes 835592 | tf_op jit(solution)/shard_map/ppermute | solution.py:462
  331.8 6.7 %collective-permute-start.56 = (bf16[136,1024]{1,0:T(8,128)(2,1)}, bf16[136,1024]{1,0:T(8,128)(2,1)}, u32[]{:S(2)}, u32[]{:S(2)}) collective-permute-start(bf16[136,1024]{1,0:T(8,128)(2,1)} %collective-permute-done.41.refs_3_), channel_id=1, source_target_pairs={{0,2},{2,0},{1,3},{3,1},{4,6},{6,4},{5,7},{7,5},{8,10},{10,8},{9,1... | collective-permute-start | bytes 835592 | tf_op jit(solution)/shard_map/ppermute | solution.py:392
  331.9 15.2 %collective-permute-start.46 = (bf16[136,1024]{1,0:T(8,128)(2,1)}, bf16[136,1024]{1,0:T(8,128)(2,1)}, u32[]{:S(2)}, u32[]{:S(2)}) collective-permute-start(bf16[136,1024]{1,0:T(8,128)(2,1)} %collective-permute-done.41.refs_3_), channel_id=1, source_target_pairs={{0,8},{8,16},{16,24},{24,28},{28,20},{20,12},{12,4},{4,0},{1,9},{9... | collective-permute-start | bytes 835592 | tf_op jit(solution)/shard_map/ppermute | solution.py:462
  332.3 14.9 %collective-permute-start.45 = (bf16[128,2048]{1,0:T(8,128)(2,1)S(1)}, bf16[128,2048]{1,0:T(8,128)(2,1)S(1)}, u32[]{:S(2)}, u32[]{:S(2)}) collective-permute-start(bf16[128,2048]{1,0:T(8,128)(2,1)S(1)} %collective-permute-done.39.refs_2_), channel_id=1, source_target_pairs={{0,2},{2,0},{1,3},{3,1},{4,6},{6,4},{5,7},{7,5},{8,10},{10,8},{9,1... | collective-permute-start | bytes 1572872 | tf_op jit(solution)/shard_map/ppermute | solution.py:392
  332.5 14.8 %collective-permute-start.44 = (bf16[128,2048]{1,0:T(8,128)(2,1)S(1)}, bf16[128,2048]{1,0:T(8,128)(2,1)S(1)}, u32[]{:S(2)}, u32[]{:S(2)}) collective-permute-start(bf16[128,2048]{1,0:T(8,128)(2,1)S(1)} %collective-permute-done.39.refs_2_), channel_id=1, source_target_pairs={{0,8},{2,6},{8,16},{10,2},{16,24},{18,10},{24,28},{26,18},{28,20},... | collective-permute-start | bytes 1572872 | tf_op jit(solution)/shard_map/ppermute | solution.py:563
  334.7 5.4 %collective-permute-start.57 = (bf16[136,1024]{1,0:T(8,128)(2,1)S(1)}, bf16[136,1024]{1,0:T(8,128)(2,1)}, u32[]{:S(2)}, u32[]{:S(2)}) collective-permute-start(bf16[136,1024]{1,0:T(8,128)(2,1)S(1)} %collective-permute-done.42.refs_4_), channel_id=1, source_target_pairs={{0,2},{2,0},{1,3},{3,1},{4,6},{6,4},{5,7},{7,5},{8,10},{10,8},{9,1... | collective-permute-start | bytes 835592 | tf_op jit(solution)/shard_map/ppermute | solution.py:392
  338.5 8.8 %collective-permute-start.47 = (bf16[136,1024]{1,0:T(8,128)(2,1)S(1)}, bf16[136,1024]{1,0:T(8,128)(2,1)S(1)}, u32[]{:S(2)}, u32[]{:S(2)}) collective-permute-start(bf16[136,1024]{1,0:T(8,128)(2,1)S(1)} %collective-permute-done.42.refs_4_), channel_id=1, source_target_pairs={{0,4},{8,0},{16,8},{24,16},{28,24},{20,28},{12,20},{4,12},{1,5},{9... | collective-permute-start | bytes 835592 | tf_op jit(solution)/shard_map/ppermute | solution.py:462
  340.1 7.0 %collective-permute-start.48 = (f32[3,1024]{1,0:T(4,128)S(1)}, f32[3,1024]{1,0:T(4,128)S(1)}, u32[]{:S(2)}, u32[]{:S(2)}) collective-permute-start(f32[3,1024]{1,0:T(4,128)S(1)} %add.265), channel_id=1, source_target_pairs={{0,4},{4,0},{8,12},{12,8},{16,20},{20,16},{24,28},{28,24},{1,5},{5... | collective-permute-start | bytes 36872 | tf_op jit(solution)/shard_map/ppermute | solution.py:642
  347.3 7.3 %collective-permute-start.58 = (bf16[136,1024]{1,0:T(8,128)(2,1)}, bf16[136,1024]{1,0:T(8,128)(2,1)S(1)}, u32[]{:S(2)}, u32[]{:S(2)}) collective-permute-start(bf16[136,1024]{1,0:T(8,128)(2,1)} %collective-permute-done.46.refs_5_), channel_id=1, source_target_pairs={{0,2},{2,0},{1,3},{3,1},{4,6},{6,4},{5,7},{7,5},{8,10},{10,8},{9,1... | collective-permute-start | bytes 835592 | tf_op jit(solution)/shard_map/ppermute | solution.py:392
  347.4 9.3 %collective-permute-start.50 = (bf16[136,1024]{1,0:T(8,128)(2,1)}, bf16[136,1024]{1,0:T(8,128)(2,1)S(1)}, u32[]{:S(2)}, u32[]{:S(2)}) collective-permute-start(bf16[136,1024]{1,0:T(8,128)(2,1)} %collective-permute-done.46.refs_5_), channel_id=1, source_target_pairs={{0,8},{8,16},{16,24},{24,28},{28,20},{20,12},{12,4},{4,0},{1,9},{9... | collective-permute-start | bytes 835592 | tf_op jit(solution)/shard_map/ppermute | solution.py:462
  349.5 5.1 %collective-permute-start.59 = (bf16[136,1024]{1,0:T(8,128)(2,1)S(1)}, bf16[136,1024]{1,0:T(8,128)(2,1)}, u32[]{:S(2)}, u32[]{:S(2)}) collective-permute-start(bf16[136,1024]{1,0:T(8,128)(2,1)S(1)} %collective-permute-done.47.refs_6_), channel_id=1, source_target_pairs={{0,2},{2,0},{1,3},{3,1},{4,6},{6,4},{5,7},{7,5},{8,10},{10,8},{9,1... | collective-permute-start | bytes 835592 | tf_op jit(solution)/shard_map/ppermute | solution.py:392
  349.7 7.0 %collective-permute-start.49 = (bf16[128,2048]{1,0:T(8,128)(2,1)S(1)}, bf16[128,2048]{1,0:T(8,128)(2,1)S(1)}, u32[]{:S(2)}, u32[]{:S(2)}) collective-permute-start(bf16[128,2048]{1,0:T(8,128)(2,1)S(1)} %collective-permute-done.44.refs_2_), channel_id=1, source_target_pairs={{0,2},{2,0},{1,3},{3,1},{4,6},{6,4},{5,7},{7,5},{8,10},{10,8},{9,1... | collective-permute-start | bytes 1572872 | tf_op jit(solution)/shard_map/ppermute | solution.py:392
  350.0 5.6 %collective-permute-start.51 = (f32[3,1024]{1,0:T(4,128)S(1)}, f32[3,1024]{1,0:T(4,128)S(1)}, u32[]{:S(2)}, u32[]{:S(2)}) collective-permute-start(f32[3,1024]{1,0:T(4,128)S(1)} %add.266), channel_id=1, source_target_pairs={{0,8},{4,12},{8,0},{12,4},{16,24},{20,28},{24,16},{28,20},{1,9},{5... | collective-permute-start | bytes 36872 | tf_op jit(solution)/shard_map/ppermute | solution.py:642
  356.7 5.1 %collective-permute-start.52 = (f32[3,1024]{1,0:T(4,128)S(1)}, f32[3,1024]{1,0:T(4,128)S(1)}, u32[]{:S(2)}, u32[]{:S(2)}) collective-permute-start(f32[3,1024]{1,0:T(4,128)S(1)} %add.267), channel_id=1, source_target_pairs={{0,16},{4,20},{8,24},{12,28},{16,0},{20,4},{24,8},{28,12},{1,17},{... | collective-permute-start | bytes 36872 | tf_op jit(solution)/shard_map/ppermute | solution.py:642
  358.4 4.0 %collective-permute-start.60 = (bf16[136,1024]{1,0:T(8,128)(2,1)S(1)}, bf16[136,1024]{1,0:T(8,128)(2,1)S(1)}, u32[]{:S(2)}, u32[]{:S(2)}) collective-permute-start(bf16[136,1024]{1,0:T(8,128)(2,1)S(1)} %collective-permute-done.50.refs_7_), channel_id=1, source_target_pairs={{0,2},{2,0},{1,3},{3,1},{4,6},{6,4},{5,7},{7,5},{8,10},{10,8},{9,1... | collective-permute-start | bytes 835592 | tf_op jit(solution)/shard_map/ppermute | solution.py:392
  (94 other events, 822.2 us)

commit v7 on v6

--- a/solution.py
+++ b/solution.py
@@ -16,7 +16,7 @@
 seg_row = 3 * HD
 payload_rows = 3 * HD + 16
 small_rows = 8
-params = pltpu.CompilerParams(vmem_limit_bytes=32 * 2**20)
+params = pltpu.CompilerParams(vmem_limit_bytes=48 * 2**20)
 streaming = pltpu.CompilerParams(vmem_limit_bytes=60 * 2**20)
 
 
@@ -97,7 +97,7 @@
             whole_spec((rows, model)),
         ],
         out_shape=[struct((heads, payload_rows, rows), BF16), struct((rows, model), BF16)],
-        compiler_params=params,
+        compiler_params=streaming,
         cost_estimate=cost(2 * rows * model * 3 * heads * HD, 8 * 2**20),
         name="project",
     )(block_input, segments[None], steps, gain[None], shift[None], lead_weight[None], *weights)
@@ -141,7 +141,7 @@
 def mlp(block_input, out_grad, branches, output_bias, gain, shift, up_weight, up_bias, down_weight):
     rows, model = block_input.shape
     units = up_weight.shape[1]
-    step = math.gcd(units, 512)
+    step = math.gcd(units, 256)
     tile, line = whole_spec((rows, model)), whole_spec((1, model))
     return pl.pallas_call(
         functools.partial(mlp_kernel, len(branches)),
@@ -170,7 +170,7 @@
             struct((rows, model), BF16),
         ],
         scratch_shapes=[pltpu.VMEM((rows, model), F32)] * 2,
-        compiler_params=params,
+        compiler_params=streaming,
         cost_estimate=cost(8 * rows * model * units, 16 * 2**20, 2 * rows * units),
         name="mlp",
     )(
@@ -214,7 +214,7 @@
             struct((width, rows), BF16),
             struct((4, model), F32),
         ],
-        compiler_params=params,
+        compiler_params=streaming,
         cost_estimate=cost(2 * rows * model * width, 6 * 2**20),
         name="middle",
     )(hidden, out_grad, *parts, gain[None], output_weight)
@@ -424,19 +424,20 @@
     return [lax.psum(part, "head")]
 
 
-def ring_position():
+def ring_pairs(direction):
+    chips = lax.axis_size("chip")
+    order = list(range(0, chips, 2)) + list(range(chips - 1, 0, -2))
+    return [(order[at], order[(at + direction) % chips]) for at in range(chips)]
+
+
+def ring_table():
     chips, chip = lax.axis_size("chip"), lax.axis_index("chip")
-    return jnp.where(chip % 2 == 0, chip // 2, chips - 1 - chip // 2)
-
-
-def ring_order():
-    chips = lax.axis_size("chip")
-    return list(range(0, chips, 2)) + list(range(chips - 1, 0, -2))
-
-
-def ring_pairs(direction):
-    order = ring_order()
-    return [(order[at], order[(at + direction) % len(order)]) for at in range(len(order))]
+    place = jnp.where(chip % 2 == 0, chip // 2, chips - 1 - chip // 2)
+    steps = jnp.arange(2 * chips + 1, dtype=jnp.int32)
+    places = (place + steps) % chips
+    there = jnp.where(places < chips // 2, 2 * places, 2 * (chips - 1 - places) + 1)
+    table = jnp.where(steps < chips, places, there)
+    return jnp.where(steps == 2 * chips, lax.axis_index("core"), table).astype(jnp.int32)
 
 
 def visit(streams, values):
@@ -448,32 +449,35 @@
 
 
 class Gather:
-    def __init__(self, block):
-        self.chips = lax.axis_size("chip")
-        self.blocks = [(0, block)]
-        self.step = 0
-        self.state = []
-        self.send([block, block])
-
-    def send(self, arrived):
-        self.step += 1
-        reach = [self.chips // 2, (self.chips - 1) // 2]
-        self.state = [
+    def __init__(self, block, swap=False, take=None):
+        self.chips, self.swap, self.take = lax.axis_size("chip"), swap, take
+        self.blocks, self.pairs, self.count = [], [], 0
+        self.state = ([], [], [])
+        self.send([(0, block)], [block, block], [])
+
+    def send(self, new, sides, outputs):
+        self.blocks += new
+        self.new = new
+        self.count += 1
+        reach = (self.chips // 2, (self.chips - 1) // 2)
+        flying = [
             lax.ppermute(block, "chip", ring_pairs(direction))
-            for block, direction, steps in zip(arrived, (1, -1), reach)
-            if self.step <= steps
+            for block, direction, steps in zip(sides, (1, -1), reach)
+            if self.count <= steps
         ]
+        self.state = (flying, [swap_cores(block) for _, block in new] if self.swap else [], outputs)
 
     def advance(self):
-        arrived = self.state
-        for block, direction in zip(arrived, (-1, 1)):
-            self.blocks.append((direction * self.step, block))
-        self.send(arrived)
-
-    def order(self):
-        table = jnp.array(ring_order(), jnp.int32)
-        steps = jnp.array([step for step, _ in self.blocks], jnp.int32)
-        return table[(ring_position() + steps + self.chips) % self.chips]
+        arrived, swapped, outputs = self.state
+        pairs = [(step, near, far) for (step, near), far in zip(self.new, swapped)]
+        self.pairs += pairs
+        if self.take and pairs:
+            outputs = self.take(outputs, pairs)
+        new = [(side * self.count, block) for block, side in zip(arrived, (-1, 1))]
+        self.send(new, arrived, outputs)
+
+    def busy(self):
+        return bool(self.state[0] or self.state[1])
 
 
 def partial_kernel(core, grad, mlp_in, wide, grad_far, mlp_in_far, wide_far, out_ref):
@@ -524,187 +528,157 @@
     )(core[None], grad, mlp_in, wide, grad_far, mlp_in_far, wide_far)
 
 
-def add_kernel(_, partial, arrived, output):
-    output[...] = (arrived[...].astype(F32) + partial[...].astype(F32)).astype(BF16)
-
-
-def place_kernel(order, *refs):
-    near, far, down, up = refs[-4:]
+class Reduce:
+    def __init__(self, partial, table):
+        self.chips, self.partial, self.table = lax.axis_size("chip"), partial, table
+        self.shape = (partial.shape[0] // self.chips, partial.shape[1])
+        self.reach = (self.chips // 2, (self.chips - 1) // 2)
+        self.count, self.gather = 0, None
+        self.send([self.block(self.reach[0]), self.block(-self.reach[1])], [])
+
+    def block(self, step):
+        start = self.table[step % self.chips] * self.shape[0]
+        return lax.dynamic_slice_in_dim(self.partial, start, self.shape[0], 0)
+
+    def send(self, sides, held):
+        self.count += 1
+        flying = [
+            lax.ppermute(block, "chip", ring_pairs(direction))
+            for block, direction in zip(sides, (1, -1))
+        ]
+        self.state = (flying, held)
+
+    def advance(self):
+        if self.gather:
+            self.gather.state = self.state
+            self.gather.advance()
+            self.state = self.gather.state
+            return
+        arrived, held = self.state
+        sums, done = [], self.count == self.reach[0]
+        for block, reach, side in zip(arrived, self.reach, (1, -1)):
+            left = reach - self.count
+            if left > 0 or done:
+                parts = held if done else []
+                sums.append(self.add([block] + parts, side * left))
+            else:
+                held = [block]
+        if done:
+            self.gather = Gather(sums[0], True, self.place)
+            self.state = self.gather.state
+        else:
+            self.send(sums, held)
+
+    def add(self, parts, step):
+        total = self.block(step).astype(F32)
+        for part in parts:
+            total += part.astype(F32)
+        return total.astype(BF16)
+
+    def place(self, outputs, pairs):
+        rows, columns = self.shape
+        half, chips = columns // 2, self.chips
+        first = pairs[0][0] % chips
+        stride = pairs[-1][0] % chips - first
+        block = pl.BlockSpec(self.shape, lambda at, table: (0, 0))
+        return pl.pallas_call(
+            functools.partial(place_kernel, len(pairs)),
+            grid_spec=pltpu.PrefetchScalarGridSpec(
+                num_scalar_prefetch=1,
+                grid=(len(pairs),),
+                in_specs=[pl.BlockSpec(memory_space=pl.ANY)] * len(outputs)
+                + [block] * (2 * len(pairs)),
+                out_specs=[
+                    pl.BlockSpec((2, rows, half), lambda at, table: (0, table[first + at * stride], 0)),
+                    pl.BlockSpec((rows, columns), lambda at, table: (table[first + at * stride], 0)),
+                ],
+            ),
+            out_shape=[
+                struct((2, chips * rows, half), F32),
+                struct((chips * rows, columns), F32),
+            ],
+            input_output_aliases={1 + at: at for at in range(len(outputs))},
+            compiler_params=streaming,
+            cost_estimate=cost(0, 2 * 2**20),
+            name="place",
+        )(self.table, *outputs, *[pair[1] for pair in pairs], *[pair[2] for pair in pairs])
+
+    def busy(self):
+        return self.gather is None or self.gather.busy()
+
+
+def place_kernel(count, table, *refs):
+    nears, fars, (down, up) = refs[-2 - 2 * count : -2 - count], refs[-2 - count : -2], refs[-2:]
     half = down.shape[2]
+    core = table[table.shape[0] - 1]
 
     def put(first, second):
         for side in range(2):
             down[side] = first[:, pl.ds(side * half, half)].astype(F32)
         up[...] = second[...].astype(F32)
 
-    pl.when(order[2] == 0)(lambda: put(near, far))
-    pl.when(order[2] != 0)(lambda: put(far, near))
-
-
-class Ring:
-    def __init__(self, partial, core):
-        self.chips, self.partial, self.core = lax.axis_size("chip"), partial, core
-        self.shape = (partial.shape[0] // self.chips, partial.shape[1])
-        self.step, self.near = 1, None
-        order, count = ring_order(), self.chips
-        self.pairs = []
-        for at in range(count):
-            self.pairs.append((2 * order[at], 2 * order[(at + 1) % count]))
-            self.pairs.append((2 * order[at] + 1, 2 * order[(at - 1) % count] + 1))
-        block = lax.dynamic_slice_in_dim(partial, self.index() * self.shape[0], self.shape[0], 0)
-        self.state = (self.send(block), [], [])
-
-    def index(self, direction=None):
-        if direction is None:
-            direction = 1 - 2 * self.core
-        return lax.rem(ring_position() + self.chips * 2 - direction * self.step, self.chips)
-
-    def send(self, block):
-        return [lax.ppermute(block, ("chip", "core"), self.pairs)]
-
-    def add(self, block):
-        whole = pl.BlockSpec(self.shape, lambda at, order: (0, 0))
-        return pl.pallas_call(
-            add_kernel,
-            grid_spec=pltpu.PrefetchScalarGridSpec(
-                num_scalar_prefetch=1,
-                grid=(1,),
-                in_specs=[pl.BlockSpec(self.shape, lambda at, order: (order[0], 0)), whole],
-                out_specs=whole,
-            ),
-            out_shape=struct(self.shape, BF16),
-            compiler_params=streaming,
-            name="ring_add",
-        )(self.index()[None].astype(jnp.int32), self.partial, block)
-
-    def place(self, far, outputs):
-        rows, columns = self.shape
-        half = columns // 2
-        order = jnp.stack([self.index(1), self.index(-1), self.core]).astype(jnp.int32)
-        block = pl.BlockSpec(self.shape, lambda at, order: (0, 0))
-        return pl.pallas_call(
-            place_kernel,
-            grid_spec=pltpu.PrefetchScalarGridSpec(
-                num_scalar_prefetch=1,
-                grid=(1,),
-                in_specs=[pl.BlockSpec(memory_space=pl.ANY)] * len(outputs) + [block] * 2,
-                out_specs=[
-                    pl.BlockSpec((2, rows, half), lambda at, order: (0, order[0], 0)),
-                    pl.BlockSpec((rows, columns), lambda at, order: (order[1], 0)),
-                ],
-            ),
-            out_shape=[
-                struct((2, self.chips * rows, half), F32),
-                struct((self.chips * rows, columns), F32),
-            ],
-            input_output_aliases={1 + at: at for at in range(len(outputs))},
-            compiler_params=streaming,
-            name="place",
-        )(order, *outputs, self.near, far)
-
-    def advance(self):
-        flying, swapped, outputs = self.state
-        if swapped:
-            outputs = self.place(swapped[0], outputs)
-            swapped = []
-        if flying:
-            self.step += 1
-            block, flying = flying[0], []
-            if self.step <= self.chips:
-                block = self.add(block)
-            if self.step < 2 * self.chips - 1:
-                flying = self.send(block)
-            if self.step >= self.chips:
-                self.near = block
-                swapped = [swap_cores(block)]
-        self.state = (flying, swapped, outputs)
-
-    def busy(self):
-        return bool(self.state[0] or self.state[1])
-
-
-class Doubling:
-    def __init__(self, values):
-        chips = lax.axis_size("chip")
-        self.moves = [lambda v: swap_cores(v)]
-        reach = 1
-        while reach < chips:
-            pairs = [(chip, chip ^ reach) for chip in range(chips)]
-            self.moves.append(functools.partial(lax.ppermute, axis_name="chip", perm=pairs))
-            reach *= 2
-        parts = across_heads(values)
-        self.state = (parts[0], parts[1:])
-
-    def advance(self):
-        values, arrived = self.state
-        for part in arrived:
-            values = values + part
-        self.state = (values, [self.moves.pop(0)(values)] if self.moves else [])
-
-    def busy(self):
-        return bool(self.state[1])
-
-
-def head_gradient_kernel(count, order, query_ref, key_value_ref, *refs):
-    blocks, (out_ref, accum) = refs[:count], refs[count:]
-    at = pl.program_id(0)
-
-    @pl.when(at == 0)
-    def _():
-        accum[...] = jnp.zeros_like(accum)
-
-    grads = jnp.concatenate([query_ref[0], key_value_ref[0]], axis=0)
-    for index, block in enumerate(blocks):
-
-        @pl.when(at == index)
-        def _(block=block):
-            accum[...] += product(grads, block[...])
-
-    @pl.when(at == count - 1)
-    def _():
-        out_ref[...] = accum[...].astype(BF16)
-
-
-def head_gradient(dquery, key_value, inputs):
+    for at, (near, far) in enumerate(zip(nears, fars)):
+        here = pl.program_id(0) == at
+        pl.when(here & (core == 0))(functools.partial(put, near, far))
+        pl.when(here & (core != 0))(functools.partial(put, far, near))
+
+
+def head_gradient_kernel(steps, table, query_ref, key_value_ref, *refs):
+    blocks, out_ref = refs[:-1], refs[-1]
+    chips = len(blocks)
+    total = jnp.zeros(out_ref.shape, F32)
+    for step, block in zip(steps, blocks):
+        chip = table[chips + step % chips]
+        grads = jnp.concatenate([query_ref[chip], key_value_ref[chip]], axis=0)
+        total += product(grads, block[...])
+    out_ref[...] = total.astype(BF16)
+
+
+def head_gradient(dquery, key_value, inputs, table):
     count, rows, patches = dquery.shape
-    blocks = [block for _, block in inputs.blocks]
+    steps, blocks = zip(*inputs.blocks)
     model = blocks[0].shape[1]
+    step = math.gcd(model, 256)
     return pl.pallas_call(
-        functools.partial(head_gradient_kernel, count),
+        functools.partial(head_gradient_kernel, steps),
         grid_spec=pltpu.PrefetchScalarGridSpec(
             num_scalar_prefetch=1,
-            grid=(count,),
+            grid=(model // step,),
             in_specs=[
-                pl.BlockSpec((1, rows, patches), lambda at, order: (order[at], 0, 0)),
-                pl.BlockSpec((1, 2 * rows, patches), lambda at, order: (order[at], 0, 0)),
+                pl.BlockSpec(dquery.shape, lambda at, table: (0, 0, 0)),
+                pl.BlockSpec(key_value.shape, lambda at, table: (0, 0, 0)),
             ]
-            + [pl.BlockSpec((patches, model), lambda at, order: (0, 0))] * count,
-            out_specs=pl.BlockSpec((3 * rows, model), lambda at, order: (0, 0)),
-            scratch_shapes=[pltpu.VMEM((3 * rows, model), F32)],
+            + [pl.BlockSpec((patches, step), lambda at, table: (0, at))] * count,
+            out_specs=pl.BlockSpec((3 * rows, step), lambda at, table: (0, at)),
         ),
         out_shape=struct((3 * rows, model), BF16),
         compiler_params=streaming,
         cost_estimate=cost(6 * rows * count * patches * model, 6 * 2**20),
         name="head_gradient",
-    )(inputs.order(), dquery, key_value, *blocks)
-
-
-def layout_kernel(count, size, order, *refs):
-    near, far, outputs, (held,) = (
+    )(table, dquery, key_value, *blocks)
+
+
+def layout_kernel(steps, size, extra, table, *refs):
+    count = len(steps)
+    nears, fars, outputs, output_ref, small_ref, held = (
         refs[:count],
         refs[count : 2 * count],
         refs[2 * count : 2 * count + 3],
-        refs[2 * count + 3 :],
+        refs[2 * count + 3],
+        refs[2 * count + 4],
+        refs[2 * count + 5],
     )
     at = pl.program_id(0)
 
     @pl.when(at == 0)
     def _():
-        core = order[count]
-        for index in range(count):
-            head = order[index]
-            for side, blocks in ((core, near), (1 - core, far)):
-                held[head, side] = blocks[index][pl.ds(0, size), :]
+        core = table[2 * count]
+        for step, near, far in zip(steps, nears, fars):
+            chip = table[count + step % count]
+            for side, block in ((core, near), (1 - core, far)):
+                held[chip, side] = block[pl.ds(0, size), :]
+                output_ref[side, chip] = block[pl.ds(size, extra), :].astype(F32)
+                small_ref[side, chip] = block[pl.ds(size + extra, small_rows), :].astype(F32)
 
     pair = [
         jnp.concatenate([held[2 * at + head, 0], held[2 * at + head, 1]], axis=0)
@@ -715,24 +689,32 @@
         output[...] = jnp.concatenate(rows, axis=0).astype(F32).T
 
 
-def projection_outputs(gathered, far, core, size):
-    count = gathered.chips
-    blocks = [block for _, block in gathered.blocks]
-    rows, model = blocks[0].shape
-    order = jnp.concatenate([gathered.order(), core[None].astype(jnp.int32)])
+def final_layout(pairs, size, table):
+    count = len(pairs)
+    steps, nears, fars = zip(*pairs)
+    rows, model = nears[0].shape
+    extra = rows - size - small_rows
     return pl.pallas_call(
-        functools.partial(layout_kernel, count, size),
+        functools.partial(layout_kernel, steps, size, extra),
         grid_spec=pltpu.PrefetchScalarGridSpec(
             num_scalar_prefetch=1,
             grid=(count // 2,),
-            in_specs=[pl.BlockSpec((rows, model), lambda at, order: (0, 0))] * (2 * count),
-            out_specs=[pl.BlockSpec((model, 2 * HD), lambda at, order: (0, at))] * 3,
+            in_specs=[pl.BlockSpec((rows, model), lambda at, table: (0, 0))] * (2 * count),
+            out_specs=[pl.BlockSpec((model, 2 * HD), lambda at, table: (0, at))] * 3
+            + [
+                pl.BlockSpec((2, count, extra, model), lambda at, table: (0, 0, 0, 0)),
+                pl.BlockSpec((2, count, small_rows, model), lambda at, table: (0, 0, 0, 0)),
+            ],
             scratch_shapes=[pltpu.VMEM((count, 2, size, model), BF16)],
         ),
-        out_shape=[struct((model, count * HD), F32)] * 3,
+        out_shape=[struct((model, count * HD), F32)] * 3
+        + [
+            struct((2, count, extra, model), F32),
+            struct((2, count, small_rows, model), F32),
+        ],
         compiler_params=streaming,
-        name="projection_outputs",
-    )(order, *blocks, *far)
+        name="final_layout",
+    )(table, *nears, *fars)
 
 
 def core_half(values, axis, side):
@@ -771,6 +753,7 @@
     chips, core = lax.axis_size("chip"), lax.axis_index("core")
     split = chips // heads
     crops = lead_steps.shape[0]
+    table = ring_table()
     weights = (query_weight, key_weight, value_weight)
     payload, attn_in = project(
         block_input, segments, lead_steps, gain_attn, shift_attn, lead_weight, weights
@@ -806,8 +789,8 @@
     wide, mlp_in = visit([inputs], (wide, mlp_in))
     mlp_in_far = swap_cores(mlp_in)
     wide_far = swap_cores(lax.dynamic_index_in_dim(wide, 1 - core, 0, keepdims=False))
-    ring = Ring(
-        weight_partial(core, out_grad, mlp_in, wide, grad_far, mlp_in_far, wide_far), core
+    ring = Reduce(
+        weight_partial(core, out_grad, mlp_in, wide, grad_far, mlp_in_far, wide_far), table
     )
     d_mlp = visit([ring, inputs], d_mlp)
     mlp_part, d_mlp = lax.optimization_barrier((mlp_part, d_mlp))
@@ -823,7 +806,7 @@
     out_near, out_far = share_halves(attn_out, 0)
     doutput = product(out_near, d_branch) + product(out_far, d_branch_far)
     doutput = jnp.concatenate([doutput.reshape(chips, -1, model), small], axis=1).astype(BF16)
-    pieces = math.gcd(chips, 4)
+    pieces = 2
     dquery, sums = [], {}
     for keys, dtype in ((other, BF16), (own, F32)):
         piece_sums = []
@@ -852,7 +835,7 @@
     if split == 1:
         dquery, key_value = visit([ring], (dquery, key_value))
         moved = to_heads(jnp.concatenate([dquery, key_value], axis=1))
-        projections = head_gradient(dquery, key_value, inputs)
+        projections = head_gradient(dquery, key_value, inputs, table)
         near, far = share_halves(projections, 0)
         projections = (near.astype(F32) + far.astype(F32)).astype(BF16)
         size = projections.shape[0]
@@ -871,45 +854,52 @@
             for grad in (dquery, dkey, dvalue)
         ]
     dquery, dkey, dvalue, blocks = visit([ring], (dquery, dkey, dvalue, blocks))
-    gathered = Gather(blocks)
+    gathered = Gather(blocks, True)
     d_part = (
         product(dquery, query_weight, 0, 1)
         + product(dkey, key_weight, 0, 1)
         + product(dvalue, value_weight, 0, 1)
     )
+    d_in = across_heads(d_part.astype(BF16))
     unit_attn, inverse_attn = normalize(block_input.astype(F32))
     onehot = (segments[:, None] == jnp.arange(crops, dtype=jnp.int32)[None, :]).astype(F32)
     lead = jnp.sum(onehot * lead_steps.astype(F32)[None, :], axis=1) / 12.0
-    ends = Doubling(
-        jnp.stack(
-            [
-                jnp.sum(d_part * unit_attn, axis=0),
-                jnp.sum(d_part, axis=0),
-                jnp.sum(lead[:, None] * d_part, axis=0),
-            ]
-        )
-    )
-    d_in = across_heads(d_part.astype(BF16))
-    d_in = visit([ring, gathered, ends], d_in)
+    ends = jnp.stack(
+        [
+            jnp.sum(d_part * unit_attn, axis=0),
+            jnp.sum(d_part, axis=0),
+            jnp.sum(lead[:, None] * d_part, axis=0),
+        ]
+    )
+    ends = jnp.pad(ends.reshape(-1, 128), ((0, -ends.size // 128 % 16), (0, 0))).astype(BF16)
+    everyone = ("chip", "core", "head")
+    ends = jnp.broadcast_to(ends, (lax.axis_size(everyone),) + ends.shape)
+    ends = lax.all_to_all(ends, everyone, 0, 0, tiled=True)
+    d_in = visit([ring, gathered], d_in)
     d_in = functools.reduce(jnp.add, (part.astype(F32) for part in d_in))
     input_grad = (d_hidden + normalize_back(d_in * gain_attn, unit_attn, inverse_attn)).astype(
         BF16
     )
-    while ring.busy() or gathered.state or ends.busy():
-        visit([ring, gathered, ends], ())
+    input_grad, ends = visit([ring, gathered], (input_grad, ends))
+    while ring.busy() or gathered.busy():
+        visit([ring, gathered], ())
+    ends = jnp.sum(ends.astype(F32), axis=0).reshape(-1)[: 3 * model].reshape(3, model)
     ddown_weight, dup_weight = ring.state[2]
     ddown_weight = ddown_weight.reshape(-1, model)
-    ends = ends.state[0]
-    far = [swap_cores(block) for _, block in gathered.blocks]
     if split == 1:
-        projections = projection_outputs(gathered, far, core, size)
-    position = jnp.argsort(gathered.order())
-    blocks = jnp.stack(
-        [jnp.stack([block[size:] for _, block in gathered.blocks]), jnp.stack([block[size:] for block in far])]
-    )
-    blocks = jnp.take(jnp.where(core == 0, blocks, blocks[::-1]), position, axis=1)
-    doutput_weight = blocks[:, :, :-small_rows].reshape(width, model).astype(F32)
-    small = jnp.sum(blocks[:, :, -small_rows, :lines].astype(F32), axis=0).reshape(-1)
+        *projections, doutput_weight, small = final_layout(gathered.pairs, size, table)
+        doutput_weight = doutput_weight.reshape(width, model)
+        small = small[:, :, 0, :lines]
+    else:
+        blocks = jnp.zeros((2, chips) + blocks.shape, F32)
+        for step, near, far in gathered.pairs:
+            for side, block in ((core, near), (1 - core, far)):
+                start = (side, table[chips + step % chips], 0, 0)
+                block = block[None, None].astype(F32)
+                blocks = lax.dynamic_update_slice(blocks, block, start)
+        doutput_weight = blocks[:, :, :-small_rows].reshape(width, model)
+        small = blocks[:, :, -small_rows, :lines]
+    small = jnp.sum(small, axis=0).reshape(-1)
     dup_bias = small[4 * model :]
     small = [small[at * model : at * model + model] for at in range(4)]
     return (

time: 376 us -> 344 us (0.915)
  local copies, waits for them, and re-layouts: 56.6 us -> 17.6 us
  waiting for transfers between devices: 59.7 us -> 88.4 us
  Pallas kernels: 132 us -> 114 us
  starting transfers between devices: 71.2 us -> 62.1 us
  between operations: 1.64 us -> 6.5 us
    unnamed x201 -> x83, local copies, waits for them, and re-layouts: 45.7 us -> 6.11 us
    ppermute x14 -> x28, waiting for transfers between devices: 11.8 us -> 50.9 us  [send(): lax.ppermute(block, 'chip', ring_pairs(direction))]
    ppermute x17 -> x0, starting transfers between devices: 28.4 us -> none  [the longest x14 24.2 us: send(): return [lax.ppermute(block, ('chip', 'core'), self.pairs)]]
    pallas_call x17 -> x7, Pallas kernels: 56.6 us -> 33 us  [the longest x5 20.1 us: place(): pl.pallas_call(functools.partial(place_kernel, len(pairs)), grid_spec=plt...]
    ppermute x14 -> x28, starting transfers between devices: 14.3 us -> 35.1 us  [send(): lax.ppermute(block, 'chip', ring_pairs(direction))]
    ppermute x17 -> x0, waiting for transfers between devices: 16 us -> none  [the longest x14 11.1 us: send(): return [lax.ppermute(block, ('chip', 'core'), self.pairs)]]
    convert_element_type x1 -> x4, other arithmetic: 0.24 us -> 7.55 us  [add(): return total.astype(BF16)]
    pallas_call x1, Pallas kernels: 7.51 us -> 12.9 us  [mlp(): pl.pallas_call(functools.partial(mlp_kernel, len(branches)), grid=(units...]
  transfers between devices with their start and end apart: 65 -> 61, of which waited for: 24 -> 23; matrix products, arithmetic and copies ran while one was open for 10% -> 7% of each run, Pallas kernels for 30% -> 30%
where the time goes in v7:
time: 344 us; the launch traced here: 343 us
  Pallas kernels  114 us (33%)
  waiting for transfers between devices  88.4 us (26%)
  starting transfers between devices  62.1 us (18%)
  blocking collectives  29.5 us (9%)
  other arithmetic  18.4 us (5%)
  local copies, waits for them, and re-layouts  17.6 us (5%)
  between operations  6.5 us (2%)
  matrix products  5.65 us (2%)
    ppermute x28, waiting for transfers between devices, send(): lax.ppermute(block, 'chip', ring_pairs(direction))  50.9 us
    ppermute x28, starting transfers between devices, send(): lax.ppermute(block, 'chip', ring_pairs(direction))  35.1 us
    all_to_all x1, blocking collectives, to_heads(): return lax.all_to_all(blocks, 'chip', 0, 0, tiled=True)  29.5 us
    pallas_call x4, Pallas kernels, backward_piece(): pl.pallas_call(functools.partial(backward_kernel, crops, len(before)), gr...  28.5 us
    pallas_call x1, Pallas kernels, attention_forward(): pl.pallas_call(functools.partial(forward_kernel, crops, key_step(count)),...  24.1 us
    all_to_all x4, waiting for transfers between devices, to_heads(): return lax.all_to_all(blocks, 'chip', 0, 0, tiled=True)  22.4 us
    pallas_call x5, Pallas kernels, place(): pl.pallas_call(functools.partial(place_kernel, len(pairs)), grid_spec=plt...  20.1 us
    all_to_all x4, starting transfers between devices, to_heads(): return lax.all_to_all(blocks, 'chip', 0, 0, tiled=True)  16.6 us
  transfers between devices with their start and end apart: 61, of which 23 were waited for; matrix products, arithmetic and copies ran while one was open for 7% of the time, Pallas kernels for 30%

profile of v7, /device:TPU:0, one launch (start us, length us, event | category | flops | bytes accessed | tf_op | source)
XLA Modules:
  0.0 342.5 jit_solution(2546700086483098278)
XLA Ops:
  0.6 1.3 broadcast_in_dim.52.steps_ref
  2.0 5.8 %project.1 = (bf16[8,208,256]{2,1,0:T(8,128)(2,1)}, bf16[256,1024]{1,0:T(8,128)(2,1)}) custom-call(bf16[256,1024]{1,0:T(8,128)(2,1)} %input_ref.3, s32[1,256]{1,0:T(1,128)} %bitcast.62, s32[32,128]{1,0:T(8,128)} %broadcast_in_dim.52.steps_ref, f32[1,1024]{1,0:T(1,128)} %bitcast.58, f32[1,1024]{1,0:T(1,128)} %bitcast.60, f32[1,1024]{1,0:T(1,128)} %bitcast.61, ...), custom_call_target="tpu_custom_call" | custom-call | flops 805306368 | bytes 8388608 | tf_op jit(solution)/shard_map/project/pallas_call | solution.py:89
  7.8 29.5 %all_to_all.30.query_ref.own.refs_1_ = bf16[8,208,256]{2,1,0:T(8,128)(2,1)S(1)} all-to-all(bf16[8,208,256]{2,1,0:T(8,128)(2,1)} %get-tuple-element.148), channel_id=1, replica_groups=mesh['chip'=8,'core'=2,'head'=2] {'chip'}, dimensions={0} | all-to-all | bytes 1703936 | tf_op jit(solution)/shard_map/all_to_all | solution.py:396
  39.7 24.1 %attention_forward.1 = (f32[8,64,256]{2,1,0:T(8,128)S(1)}, bf16[8,64,256]{2,1,0:T(8,128)(2,1)}, f32[8,1,256]{2,1,0:T(1,128)S(1)}) custom-call(bf16[8,208,256]{2,1,0:T(8,128)(2,1)S(1)} %all_to_all.30.query_ref.own.refs_1_, bf16[8,208,256]{2,1,0:T(8,128)(2,1)S(1)} %all_to_all.30.query_ref.own.refs_1_, ...), custom_call_target="tpu_custom_call" | custom-call | flops 34359738368 | bytes 4194304 | tf_op jit(solution)/shard_map/attention_forward/pallas_call | solution.py:328
  63.8 3.4 all-to-all-start.1
  67.2 9.4 %all-to-all-done.1 = bf16[8,64,256]{2,1,0:T(8,128)(2,1)S(1)} async-done(((bf16[8,64,256]{2,1,0:T(8,128)(2,1)}), bf16[8,64,256]{2,1,0:T(8,128)(2,1)S(1)}, u32[]{:S(2)}, u32[]{:S(2)}) %all-to-all-start.1) | async-done | bytes 262176 | tf_op jit(solution)/shard_map/all_to_all | solution.py:396
  76.7 1.7 convolution_convert_fusion.refs_0_
  78.4 1.5 collective-permute-start.5
  82.0 9.1 %collective-permute-done.5.refs_1_ = bf16[256,1024]{1,0:T(8,128)(2,1)S(1)} collective-permute-done((bf16[256,1024]{1,0:T(8,128)(2,1)S(1)}, bf16[256,1024]{1,0:T(8,128)(2,1)S(1)}, u32[]{:S(2)}, u32[]{:S(2)}) %collective-permute-start.5) | collective-permute-done | bytes 524320 | tf_op jit(solution)/shard_map/ppermute | solution.py:423
  93.0 1.7 collective-permute-start.6
  95.0 12.9 %mlp.1 = (bf16[2,256,2048]{2,1,0:T(8,128)(2,1)}, bf16[256,1024]{1,0:T(8,128)(2,1)}, f32[256,1024]{1,0:T(8,128)}, f32[1,2048]{1,0:T(1,128)}, bf16[256,1024]{1,0:T(8,128)(2,1)}, /*index=5*/bf16[256,1024]{1,0:T(8,128)(2,1)}) custom-call(bf16[256,1024]{1,0:T(8,128)(2,1)} %input_ref.3, bf16[256,1024]{1,0:T(8,128)(2,1)} %grad_ref.3, bf16[256,1024]{1,0:T(8,128)(2,1)} %copy-done.22, ...), custom_call_target="tpu_custom_call" | custom-call | flops 4294967296 | bytes 16777216 | tf_op jit(solution)/shard_map/mlp/pallas_call | solution.py:146
  107.9 2.3 dynamic-slice_bitcast_fusion
  113.4 1.7 collective-permute-start.13
  115.2 5.8 %weight_partial.1 = bf16[1024,2048]{1,0:T(8,128)(2,1)} custom-call(s32[1]{0:T(128)} %bitcast.9.core, bf16[256,1024]{1,0:T(8,128)(2,1)} %grad_ref.3, bf16[256,1024]{1,0:T(8,128)(2,1)} %get-tuple-element.166.mlp_in, bf16[2,256,2048]{2,1,0:T(8,128)(2,1)} %get-tuple-element.167.wide, bf16[256,1024]{1,0:T(8,128)(2,1)} %collective-permute-done.8.grad_far, ...), custom_call_target="tpu_custom_call" | custom-call | flops 2147483648 | bytes 12582912 | tf_op jit(solution)/shard_map/weight_partial/pallas_call | solution.py:509
  121.0 2.3 constant_dynamic-slice_fusion.2
  129.1 8.2 %collective-permute-done.12 = bf16[128,2048]{1,0:T(8,128)(2,1)S(1)} collective-permute-done((bf16[128,2048]{1,0:T(8,128)(2,1)}, bf16[128,2048]{1,0:T(8,128)(2,1)S(1)}, u32[]{:S(2)}, u32[]{:S(2)}) %collective-permute-start.12) | collective-permute-done | bytes 524320 | tf_op jit(solution)/shard_map/ppermute | solution.py:546
  137.3 1.7 collective-permute-done.11
  139.0 2.7 add_convert_fusion.6
  141.7 1.3 collective-permute-start.16
  143.8 4.3 %middle.1 = (f32[256,1024]{1,0:T(8,128)}, bf16[256,1024]{1,0:T(8,128)(2,1)}, bf16[512,256]{1,0:T(8,128)(2,1)}, f32[4,1024]{1,0:T(4,128)}) custom-call(f32[256,1024]{1,0:T(8,128)} %get-tuple-element.158.hidden_ref, bf16[256,1024]{1,0:T(8,128)(2,1)} %grad_ref.3, bf16[256,1024]{1,0:T(8,128)(2,1)} %get-tuple-element.174.refs_0_, ...), custom_call_target="tpu_custom_call" | custom-call | flops 268435456 | bytes 6291456 | tf_op jit(solution)/shard_map/middle/pallas_call | solution.py:209
  148.0 4.8 %all-to-all-start.2 = ((bf16[8,64,256]{2,1,0:T(8,128)(2,1)}), bf16[8,64,256]{2,1,0:T(8,128)(2,1)S(1)}, u32[]{:S(2)}, u32[]{:S(2)}) async-start(bf16[8,64,256]{2,1,0:T(8,128)(2,1)} %bitcast.57), calls=%async_computation.2 | async-start | bytes 524288 | tf_op jit(solution)/shard_map/all_to_all | solution.py:396
  153.0 1.5 collective-permute-start.25
  155.4 6.7 %all-to-all-done.2.grad_ref = bf16[8,64,256]{2,1,0:T(8,128)(2,1)S(1)} async-done(((bf16[8,64,256]{2,1,0:T(8,128)(2,1)}), bf16[8,64,256]{2,1,0:T(8,128)(2,1)S(1)}, u32[]{:S(2)}, u32[]{:S(2)}) %all-to-all-start.2) | async-done | bytes 262176 | tf_op jit(solution)/shard_map/all_to_all | solution.py:396
  162.1 2.0 add_convert_fusion.4
  168.6 7.1 %attention_backward.4 = (f32[8,64,256]{2,1,0:T(8,128)S(1)}, bf16[8,128,256]{2,1,0:T(8,128)(2,1)S(1)}) custom-call(bf16[8,208,256]{2,1,0:T(8,128)(2,1)S(1)} %all_to_all.30.query_ref.own.refs_1_, bf16[8,64,256]{2,1,0:T(8,128)(2,1)S(1)} %all-to-all-done.2.grad_ref, f32[8,64,256]{2,1,0:T(8,128)S(1)} %get-tuple-element.180.raw_ref, ...), custom_call_target="tpu_custom_call" | custom-call | flops 8589934592 | bytes 4194304 | tf_op jit(solution)/shard_map/attention_backward/pallas_call | solution.py:356
  176.3 1.3 add_convert_fusion.3
  177.5 1.6 collective-permute-start.19
  179.1 7.1 %attention_backward.5 = (f32[8,64,256]{2,1,0:T(8,128)S(1)}, bf16[8,128,256]{2,1,0:T(8,128)(2,1)S(1)}) custom-call(bf16[8,208,256]{2,1,0:T(8,128)(2,1)S(1)} %all_to_all.30.query_ref.own.refs_1_, bf16[8,64,256]{2,1,0:T(8,128)(2,1)S(1)} %all-to-all-done.2.grad_ref, f32[8,64,256]{2,1,0:T(8,128)S(1)} %get-tuple-element.180.raw_ref, ...), custom_call_target="tpu_custom_call", output_to_operand_aliasing={{1}: (6, {})} | custom-call | flops 8589934592 | bytes 4194304 | tf_op jit(solution)/shard_map/attention_backward/pallas_call | solution.py:356
  187.0 2.0 collective-permute-done.19
  189.1 4.2 %all-to-all-start.3 = ((bf16[8,40,1024]{2,1,0:T(8,128)(2,1)}), bf16[8,40,1024]{2,1,0:T(8,128)(2,1)}, u32[]{:S(2)}, u32[]{:S(2)}) async-start(bf16[8,40,1024]{2,1,0:T(8,128)(2,1)} %fusion.16), calls=%async_computation.3 | async-start | bytes 1310720 | tf_op jit(solution)/shard_map/all_to_all | solution.py:396
  193.3 1.6 add_convert_fusion.2.refs_0_
  195.0 1.9 collective-permute-start.23
  198.1 7.1 %attention_backward.6 = (f32[8,64,256]{2,1,0:T(8,128)S(1)}, f32[8,128,256]{2,1,0:T(8,128)S(1)}) custom-call(bf16[8,208,256]{2,1,0:T(8,128)(2,1)S(1)} %all_to_all.30.query_ref.own.refs_1_, bf16[8,64,256]{2,1,0:T(8,128)(2,1)S(1)} %all-to-all-done.2.grad_ref, f32[8,64,256]{2,1,0:T(8,128)S(1)} %get-tuple-element.180.raw_ref, ...), custom_call_target="tpu_custom_call" | custom-call | flops 8589934592 | bytes 4194304 | tf_op jit(solution)/shard_map/attention_backward/pallas_call | solution.py:356
  206.1 10.9 %collective-permute-done.23.refs_3_ = bf16[128,2048]{1,0:T(8,128)(2,1)S(1)} collective-permute-done((bf16[128,2048]{1,0:T(8,128)(2,1)S(1)}, bf16[128,2048]{1,0:T(8,128)(2,1)S(1)}, u32[]{:S(2)}, u32[]{:S(2)}) %collective-permute-start.23) | collective-permute-done | bytes 524320 | tf_op jit(solution)/shard_map/ppermute | solution.py:464
  217.7 4.4 %collective-permute-start.26 = (bf16[128,2048]{1,0:T(8,128)(2,1)}, bf16[128,2048]{1,0:T(8,128)(2,1)}, u32[]{:S(2)}, u32[]{:S(2)}) collective-permute-start(bf16[128,2048]{1,0:T(8,128)(2,1)} %collective-permute-done.22.refs_2_), channel_id=1, source_target_pairs={{0,8},{8,16},{16,24},{24,28},{28,20},{20,12},{12,4},{4,0},{1,9},{9... | collective-permute-start | bytes 1572872 | tf_op jit(solution)/shard_map/ppermute | solution.py:464
  223.3 7.2 %attention_backward.7 = (bf16[8,64,256]{2,1,0:T(8,128)(2,1)S(1)}, f32[8,128,256]{2,1,0:T(8,128)S(1)}) custom-call(bf16[8,208,256]{2,1,0:T(8,128)(2,1)S(1)} %all_to_all.30.query_ref.own.refs_1_, bf16[8,64,256]{2,1,0:T(8,128)(2,1)S(1)} %all-to-all-done.2.grad_ref, f32[8,64,256]{2,1,0:T(8,128)S(1)} %get-tuple-element.180.raw_ref, ...), custom_call_target="tpu_custom_call", output_to_operand_aliasing={{1}: (6, {})} | custom-call | flops 8589934592 | bytes 4194304 | tf_op jit(solution)/shard_map/attention_backward/pallas_call | solution.py:356
  230.5 3.5 %place.5 = (f32[2,1024,1024]{2,1,0:T(8,128)}, f32[1024,2048]{1,0:T(8,128)}) custom-call(s32[17]{0:T(128)} %copy-done.34, bf16[128,2048]{1,0:T(8,128)(2,1)} %copy-done.12, bf16[128,2048]{1,0:T(8,128)(2,1)} %copy-done.23), custom_call_target="tpu_custom_call" | custom-call | bytes 2097152 | tf_op jit(solution)/shard_map/place/pallas_call | solution.py:584
  235.2 1.6 collective-permute-done.27.refs_3_
  237.7 4.2 %all-to-all-start.4 = ((bf16[8,192,256]{2,1,0:T(8,128)(2,1)}), bf16[8,192,256]{2,1,0:T(8,128)(2,1)}, u32[]{:S(2)}, u32[]{:S(2)}) async-start(bf16[8,192,256]{2,1,0:T(8,128)(2,1)} %pad_maximum_fusion), calls=%async_computation.4 | async-start | bytes 1572864 | tf_op jit(solution)/shard_map/all_to_all | solution.py:396
  242.2 5.8 %head_gradient.1 = bf16[192,1024]{1,0:T(8,128)(2,1)} custom-call(s32[17]{0:T(128)} %copy-done.34, bf16[8,64,256]{2,1,0:T(8,128)(2,1)} %copy-done, bf16[8,128,256]{2,1,0:T(8,128)(2,1)} %copy-done.6, bf16[256,1024]{1,0:T(8,128)(2,1)} %get-tuple-element.150.refs_0_, bf16[256,1024]{1,0:T(8,128)(2,1)} %collective-permute-done.refs_1_, ...), custom_call_target="tpu_custom_call" | custom-call | flops 805306368 | bytes 6291456 | tf_op jit(solution)/shard_map/head_gradient/pallas_call | solution.py:642
  250.8 1.9 collective-permute-start.31
  252.8 4.4 %place.6 = (f32[2,1024,1024]{2,1,0:T(8,128)}, f32[1024,2048]{1,0:T(8,128)}) custom-call(s32[17]{0:T(128)} %copy-done.34, f32[2,1024,1024]{2,1,0:T(8,128)} %get-tuple-element.214.refs_0_, f32[1024,2048]{1,0:T(8,128)} %get-tuple-element.215.refs_1_, bf16[128,2048]{1,0:T(8,128)(2,1)} %collective-permute-done.22.refs_2_, ...), custom_call_target="tpu_custom_call", output_to_operand_aliasing={{0}: (1, {}), {1}: (2, {})} | custom-call | bytes 2097152 | tf_op jit(solution)/shard_map/place/pallas_call | solution.py:584
  257.3 6.2 %all-to-all-done.4 = bf16[8,192,256]{2,1,0:T(8,128)(2,1)} async-done(((bf16[8,192,256]{2,1,0:T(8,128)(2,1)}), bf16[8,192,256]{2,1,0:T(8,128)(2,1)}, u32[]{:S(2)}, u32[]{:S(2)}) %all-to-all-start.4) | async-done | bytes 786464 | tf_op jit(solution)/shard_map/all_to_all | solution.py:396
  263.5 1.3 fusion.20
  264.8 2.4 collective-permute-done.31.refs_2_
  267.2 3.1 collective-permute-done.32.refs_3_
  270.9 3.6 %collective-permute-start.36 = (bf16[128,2048]{1,0:T(8,128)(2,1)}, bf16[128,2048]{1,0:T(8,128)(2,1)S(1)}, u32[]{:S(2)}, u32[]{:S(2)}) collective-permute-start(bf16[128,2048]{1,0:T(8,128)(2,1)} %collective-permute-done.31.refs_2_), channel_id=1, source_target_pairs={{0,8},{8,16},{16,24},{24,28},{28,20},{20,12},{12,4},{4,0},{1,9},{9... | collective-permute-start | bytes 1572872 | tf_op jit(solution)/shard_map/ppermute | solution.py:464
  275.5 1.5 fusion.23
  278.0 3.4 collective-permute-done.40.refs_2_
  281.4 1.7 collective-permute-start.39
  283.5 4.5 %place.7 = (f32[2,1024,1024]{2,1,0:T(8,128)}, f32[1024,2048]{1,0:T(8,128)}) custom-call(s32[17]{0:T(128)} %copy-done.34, f32[2,1024,1024]{2,1,0:T(8,128)} %get-tuple-element.227.refs_0_, f32[1024,2048]{1,0:T(8,128)} %get-tuple-element.228.refs_1_, bf16[128,2048]{1,0:T(8,128)(2,1)} %collective-permute-done.26.refs_2_, ...), custom_call_target="tpu_custom_call", output_to_operand_aliasing={{0}: (1, {}), {1}: (2, {})} | custom-call | bytes 2097152 | tf_op jit(solution)/shard_map/place/pallas_call | solution.py:584
  288.0 6.2 %collective-permute-done.39.refs_1_ = bf16[136,1024]{1,0:T(8,128)(2,1)} collective-permute-done((bf16[136,1024]{1,0:T(8,128)(2,1)S(1)}, bf16[136,1024]{1,0:T(8,128)(2,1)}, u32[]{:S(2)}, u32[]{:S(2)}) %collective-permute-start.39) | collective-permute-done | bytes 278560 | tf_op jit(solution)/shard_map/ppermute | solution.py:464
  294.9 1.7 collective-permute-start.45
  298.0 2.7 all-to-all-start.5
  301.1 4.4 %place.8 = (f32[2,1024,1024]{2,1,0:T(8,128)}, f32[1024,2048]{1,0:T(8,128)}) custom-call(s32[17]{0:T(128)} %copy-done.34, f32[2,1024,1024]{2,1,0:T(8,128)} %get-tuple-element.238.refs_0_, f32[1024,2048]{1,0:T(8,128)} %get-tuple-element.239.refs_1_, bf16[128,2048]{1,0:T(8,128)(2,1)} %collective-permute-done.31.refs_2_, ...), custom_call_target="tpu_custom_call", output_to_operand_aliasing={{0}: (1, {}), {1}: (2, {})} | custom-call | bytes 2097152 | tf_op jit(solution)/shard_map/place/pallas_call | solution.py:584
  305.5 1.3 fusion.12
  306.8 4.7 %all-to-all-done.5 = bf16[32,32,128]{2,1,0:T(8,128)(2,1)S(1)} async-done(((bf16[32,32,128]{2,1,0:T(8,128)(2,1)}), bf16[32,32,128]{2,1,0:T(8,128)(2,1)S(1)}, u32[]{:S(2)}, u32[]{:S(2)}) %all-to-all-start.5) | async-done | bytes 262176 | tf_op jit(solution)/shard_map/all_to_all | solution.py:877
  312.3 1.5 collective-permute-start.49
  313.8 3.3 place.9
  317.1 3.7 %collective-permute-done.48.refs_5_ = bf16[136,1024]{1,0:T(8,128)(2,1)S(1)} collective-permute-done((bf16[136,1024]{1,0:T(8,128)(2,1)}, bf16[136,1024]{1,0:T(8,128)(2,1)S(1)}, u32[]{:S(2)}, u32[]{:S(2)}) %collective-permute-start.48) | collective-permute-done | bytes 278560 | tf_op jit(solution)/shard_map/ppermute | solution.py:464
  321.6 1.2 collective-permute-start.52
  323.1 2.2 add_convert_fusion.1
  325.4 5.3 %collective-permute-done.52.refs_7_ = bf16[136,1024]{1,0:T(8,128)(2,1)S(1)} collective-permute-done((bf16[136,1024]{1,0:T(8,128)(2,1)S(1)}, bf16[136,1024]{1,0:T(8,128)(2,1)S(1)}, u32[]{:S(2)}, u32[]{:S(2)}) %collective-permute-start.52) | collective-permute-done | bytes 278560 | tf_op jit(solution)/shard_map/ppermute | solution.py:464
  333.0 7.2 %final_layout.1 = (f32[1024,512]{1,0:T(8,128)}, f32[1024,512]{1,0:T(8,128)}, f32[1024,512]{1,0:T(8,128)}, f32[2,8,32,1024]{3,2,1,0:T(8,128)}, f32[2,8,8,1024]{3,2,1,0:T(8,128)}) custom-call(s32[17]{0:T(128)} %copy-done.34, bf16[136,1024]{1,0:T(8,128)(2,1)} %copy-done.15, bf16[136,1024]{1,0:T(8,128)(2,1)} %collective-permute-done.39.refs_1_, ...), custom_call_target="tpu_custom_call" | custom-call | tf_op jit(solution)/shard_map/final_layout/pallas_call | solution.py:697
  (210 shorter events, 39.3 us)
Async XLA Ops:
  37.3 2.4 collective-permute-start.2
  37.3 29.9 %collective-permute-start.1 = (bf16[256,1024]{1,0:T(8,128)(2,1)}, bf16[256,1024]{1,0:T(8,128)(2,1)S(1)}, u32[]{:S(2)}, u32[]{:S(2)}) collective-permute-start(bf16[256,1024]{1,0:T(8,128)(2,1)} %get-tuple-element.150.refs_0_), channel_id=1, source_target_pairs={{0,4},{8,0},{16,8},{24,16},{28,24},{20,28},{12,20},{4,12},{1,5},{9... | collective-permute-start | bytes 1572872 | tf_op jit(solution)/shard_map/ppermute | solution.py:464
  38.1 29.1 %collective-permute-start = (bf16[256,1024]{1,0:T(8,128)(2,1)}, bf16[256,1024]{1,0:T(8,128)(2,1)}, u32[]{:S(2)}, u32[]{:S(2)}) collective-permute-start(bf16[256,1024]{1,0:T(8,128)(2,1)} %get-tuple-element.150.refs_0_), channel_id=1, source_target_pairs={{0,8},{8,16},{16,24},{24,28},{28,20},{20,12},{12,4},{4,0},{1,9},{9... | collective-permute-start | bytes 1572872 | tf_op jit(solution)/shard_map/ppermute | solution.py:464
  63.8 12.9 %all-to-all-start.1 = ((bf16[8,64,256]{2,1,0:T(8,128)(2,1)}), bf16[8,64,256]{2,1,0:T(8,128)(2,1)S(1)}, u32[]{:S(2)}, u32[]{:S(2)}) async-start(bf16[8,64,256]{2,1,0:T(8,128)(2,1)} %get-tuple-element.152), calls=%async_computation.1 | async-start | bytes 524288 | tf_op jit(solution)/shard_map/all_to_all | solution.py:396
  78.4 12.7 %collective-permute-start.5 = (bf16[256,1024]{1,0:T(8,128)(2,1)S(1)}, bf16[256,1024]{1,0:T(8,128)(2,1)S(1)}, u32[]{:S(2)}, u32[]{:S(2)}) collective-permute-start(bf16[256,1024]{1,0:T(8,128)(2,1)S(1)} %convolution_convert_fusion.refs_0_), channel_id=1, source_target_pairs={{0,1},{1,0},{2,3},{3,2},{4,5},{5,4},{6,7},{7,6},{8,9},{9,8},{10,11... | collective-permute-start | bytes 1572872 | tf_op jit(solution)/shard_map/ppermute | solution.py:423
  79.9 12.5 %collective-permute-start.3 = (bf16[256,1024]{1,0:T(8,128)(2,1)}, bf16[256,1024]{1,0:T(8,128)(2,1)}, u32[]{:S(2)}, u32[]{:S(2)}) collective-permute-start(bf16[256,1024]{1,0:T(8,128)(2,1)} %collective-permute-done.refs_1_), channel_id=1, source_target_pairs={{0,8},{8,16},{16,24},{24,28},{28,20},{20,12},{12,4},{4,0},{1,9},{9... | collective-permute-start | bytes 1572872 | tf_op jit(solution)/shard_map/ppermute | solution.py:464
  81.0 12.0 %collective-permute-start.4 = (bf16[256,1024]{1,0:T(8,128)(2,1)}, bf16[256,1024]{1,0:T(8,128)(2,1)}, u32[]{:S(2)}, u32[]{:S(2)}) collective-permute-start(bf16[256,1024]{1,0:T(8,128)(2,1)} %copy-done.24), channel_id=1, source_target_pairs={{0,4},{8,0},{16,8},{24,16},{28,24},{20,28},{12,20},{4,12},{1,5},{9... | collective-permute-start | bytes 1572872 | tf_op jit(solution)/shard_map/ppermute | solution.py:464
  93.0 14.9 %collective-permute-start.6 = (bf16[256,1024]{1,0:T(8,128)(2,1)}, bf16[256,1024]{1,0:T(8,128)(2,1)}, u32[]{:S(2)}, u32[]{:S(2)}) collective-permute-start(bf16[256,1024]{1,0:T(8,128)(2,1)} %collective-permute-done.3.refs_3_), channel_id=1, source_target_pairs={{0,8},{8,16},{16,24},{24,28},{28,20},{20,12},{12,4},{4,0},{1,9},{9... | collective-permute-start | bytes 1572872 | tf_op jit(solution)/shard_map/ppermute | solution.py:464
  94.7 13.2 %collective-permute-start.7 = (bf16[256,1024]{1,0:T(8,128)(2,1)}, bf16[256,1024]{1,0:T(8,128)(2,1)}, u32[]{:S(2)}, u32[]{:S(2)}) collective-permute-start(bf16[256,1024]{1,0:T(8,128)(2,1)} %collective-permute-done.4.refs_4_), channel_id=1, source_target_pairs={{0,4},{8,0},{16,8},{24,16},{28,24},{20,28},{12,20},{4,12},{1,5},{9... | collective-permute-start | bytes 1572872 | tf_op jit(solution)/shard_map/ppermute | solution.py:464
  110.2 5.0 %collective-permute-start.10 = (bf16[256,2048]{1,0:T(8,128)(2,1)}, bf16[256,2048]{1,0:T(8,128)(2,1)}, u32[]{:S(2)}, u32[]{:S(2)}) collective-permute-start(bf16[256,2048]{1,0:T(8,128)(2,1)} %dynamic-slice_bitcast_fusion), channel_id=1, source_target_pairs={{0,2},{2,0},{1,3},{3,1},{4,6},{6,4},{5,7},{7,5},{8,10},{10,8},{9,1... | collective-permute-start | bytes 3145736 | tf_op jit(solution)/shard_map/ppermute | solution.py:392
  110.2 4.9 %collective-permute-start.8 = (bf16[256,1024]{1,0:T(8,128)(2,1)S(1)}, bf16[256,1024]{1,0:T(8,128)(2,1)}, u32[]{:S(2)}, u32[]{:S(2)}) collective-permute-start(bf16[256,1024]{1,0:T(8,128)(2,1)S(1)} %copy-done.13), channel_id=1, source_target_pairs={{0,2},{2,0},{1,3},{3,1},{4,6},{6,4},{5,7},{7,5},{8,10},{10,8},{9,1... | collective-permute-start | bytes 1572872 | tf_op jit(solution)/shard_map/ppermute | solution.py:392
  110.7 4.4 %collective-permute-start.9 = (bf16[256,1024]{1,0:T(8,128)(2,1)}, bf16[256,1024]{1,0:T(8,128)(2,1)}, u32[]{:S(2)}, u32[]{:S(2)}) collective-permute-start(bf16[256,1024]{1,0:T(8,128)(2,1)} %get-tuple-element.166.mlp_in), channel_id=1, source_target_pairs={{0,2},{2,0},{1,3},{3,1},{4,6},{6,4},{5,7},{7,5},{8,10},{10,8},{9,1... | collective-permute-start | bytes 1572872 | tf_op jit(solution)/shard_map/ppermute | solution.py:392
  112.7 16.4 %collective-permute-start.14 = (bf16[256,1024]{1,0:T(8,128)(2,1)}, bf16[256,1024]{1,0:T(8,128)(2,1)}, u32[]{:S(2)}, u32[]{:S(2)}) collective-permute-start(bf16[256,1024]{1,0:T(8,128)(2,1)} %get-tuple-element.174.refs_0_), channel_id=1, source_target_pairs={{0,1},{1,0},{2,3},{3,2},{4,5},{5,4},{6,7},{7,6},{8,9},{9,8},{10,11... | collective-permute-start | bytes 1572872 | tf_op jit(solution)/shard_map/ppermute | solution.py:423
  113.4 15.7 %collective-permute-start.13 = (bf16[256,1024]{1,0:T(8,128)(2,1)}, bf16[256,1024]{1,0:T(8,128)(2,1)}, u32[]{:S(2)}, u32[]{:S(2)}) collective-permute-start(bf16[256,1024]{1,0:T(8,128)(2,1)} %collective-permute-done.6.refs_5_), channel_id=1, source_target_pairs={{0,8},{8,16},{16,24},{24,28},{28,20},{20,12},{12,4},{4,0},{1,9},{9... | collective-permute-start | bytes 1572872 | tf_op jit(solution)/shard_map/ppermute | solution.py:464
  123.3 29.6 %copy-start.36 = (f32[1,2048]{1,0:T(1,128)S(1)}, f32[1,2048]{1,0:T(1,128)}, u32[]{:S(2)}) copy-start(f32[1,2048]{1,0:T(1,128)} %get-tuple-element.191) | copy-start | bytes 24580
  123.3 14.0 %collective-permute-start.12 = (bf16[128,2048]{1,0:T(8,128)(2,1)}, bf16[128,2048]{1,0:T(8,128)(2,1)S(1)}, u32[]{:S(2)}, u32[]{:S(2)}) collective-permute-start(bf16[128,2048]{1,0:T(8,128)(2,1)} %get-tuple-element.292), channel_id=1, source_target_pairs={{0,4},{8,0},{16,8},{24,16},{28,24},{20,28},{12,20},{4,12},{1,5},{9... | collective-permute-start | bytes 1572872 | tf_op jit(solution)/shard_map/ppermute | solution.py:546
  124.1 14.9 %collective-permute-start.11 = (bf16[128,2048]{1,0:T(8,128)(2,1)}, bf16[128,2048]{1,0:T(8,128)(2,1)}, u32[]{:S(2)}, u32[]{:S(2)}) collective-permute-start(bf16[128,2048]{1,0:T(8,128)(2,1)} %get-tuple-element.293), channel_id=1, source_target_pairs={{0,8},{8,16},{16,24},{24,28},{28,20},{20,12},{12,4},{4,0},{1,9},{9... | collective-permute-start | bytes 1572872 | tf_op jit(solution)/shard_map/ppermute | solution.py:546
  141.7 20.4 %collective-permute-start.16 = (bf16[128,2048]{1,0:T(8,128)(2,1)}, bf16[128,2048]{1,0:T(8,128)(2,1)}, u32[]{:S(2)}, u32[]{:S(2)}) collective-permute-start(bf16[128,2048]{1,0:T(8,128)(2,1)} %get-tuple-element.290), channel_id=1, source_target_pairs={{0,4},{8,0},{16,8},{24,16},{28,24},{20,28},{12,20},{4,12},{1,5},{9... | collective-permute-start | bytes 1572872 | tf_op jit(solution)/shard_map/ppermute | solution.py:546
  143.1 19.1 %collective-permute-start.15 = (bf16[128,2048]{1,0:T(8,128)(2,1)}, bf16[128,2048]{1,0:T(8,128)(2,1)}, u32[]{:S(2)}, u32[]{:S(2)}) collective-permute-start(bf16[128,2048]{1,0:T(8,128)(2,1)} %get-tuple-element.291), channel_id=1, source_target_pairs={{0,8},{8,16},{16,24},{24,28},{28,20},{20,12},{12,4},{4,0},{1,9},{9... | collective-permute-start | bytes 1572872 | tf_op jit(solution)/shard_map/ppermute | solution.py:546
  148.0 14.1 %all-to-all-start.2 = ((bf16[8,64,256]{2,1,0:T(8,128)(2,1)}), bf16[8,64,256]{2,1,0:T(8,128)(2,1)S(1)}, u32[]{:S(2)}, u32[]{:S(2)}) async-start(bf16[8,64,256]{2,1,0:T(8,128)(2,1)} %bitcast.57), calls=%async_computation.2 | async-start | bytes 524288 | tf_op jit(solution)/shard_map/all_to_all | solution.py:396
  152.8 13.3 %collective-permute-start.20 = (bf16[256,256]{1,0:T(8,128)(2,1)S(1)}, bf16[256,256]{1,0:T(8,128)(2,1)}, u32[]{:S(2)}, u32[]{:S(2)}) collective-permute-start(bf16[256,256]{1,0:T(8,128)(2,1)S(1)} %constant_dynamic-slice_fusion.1), channel_id=1, source_target_pairs={{0,2},{2,0},{1,3},{3,1},{4,6},{6,4},{5,7},{7,5},{8,10},{10,8},{9,1... | collective-permute-start | bytes 393224 | tf_op jit(solution)/shard_map/ppermute | solution.py:392
  153.0 53.1 %collective-permute-start.25 = (bf16[256,1024]{1,0:T(8,128)(2,1)}, bf16[256,1024]{1,0:T(8,128)(2,1)}, u32[]{:S(2)}, u32[]{:S(2)}) collective-permute-start(bf16[256,1024]{1,0:T(8,128)(2,1)} %get-tuple-element.199), channel_id=1, source_target_pairs={{0,1},{1,0},{2,3},{3,2},{4,5},{5,4},{6,7},{7,6},{8,9},{9,8},{10,11... | collective-permute-start | bytes 1572872 | tf_op jit(solution)/shard_map/ppermute | solution.py:423
  155.2 11.0 %collective-permute-start.21 = (bf16[256,1024]{1,0:T(8,128)(2,1)}, bf16[256,1024]{1,0:T(8,128)(2,1)S(1)}, u32[]{:S(2)}, u32[]{:S(2)}) collective-permute-start(bf16[256,1024]{1,0:T(8,128)(2,1)} %get-tuple-element.189), channel_id=1, source_target_pairs={{0,2},{2,0},{1,3},{3,1},{4,6},{6,4},{5,7},{7,5},{8,10},{10,8},{9,1... | collective-permute-start | bytes 1572872 | tf_op jit(solution)/shard_map/ppermute | solution.py:392
  164.1 12.1 %collective-permute-start.18 = (bf16[128,2048]{1,0:T(8,128)(2,1)S(1)}, bf16[128,2048]{1,0:T(8,128)(2,1)S(1)}, u32[]{:S(2)}, u32[]{:S(2)}) collective-permute-start(bf16[128,2048]{1,0:T(8,128)(2,1)S(1)} %get-tuple-element.288), channel_id=1, source_target_pairs={{0,4},{8,0},{16,8},{24,16},{28,24},{20,28},{12,20},{4,12},{1,5},{9... | collective-permute-start | bytes 1572872 | tf_op jit(solution)/shard_map/ppermute | solution.py:546
  165.3 10.9 %collective-permute-start.17 = (bf16[128,2048]{1,0:T(8,128)(2,1)S(1)}, bf16[128,2048]{1,0:T(8,128)(2,1)S(1)}, u32[]{:S(2)}, u32[]{:S(2)}) collective-permute-start(bf16[128,2048]{1,0:T(8,128)(2,1)S(1)} %get-tuple-element.289), channel_id=1, source_target_pairs={{0,8},{8,16},{16,24},{24,28},{28,20},{20,12},{12,4},{4,0},{1,9},{9... | collective-permute-start | bytes 1572872 | tf_op jit(solution)/shard_map/ppermute | solution.py:546
  177.5 11.5 %collective-permute-start.19 = (bf16[128,2048]{1,0:T(8,128)(2,1)S(1)}, bf16[128,2048]{1,0:T(8,128)(2,1)}, u32[]{:S(2)}, u32[]{:S(2)}) collective-permute-start(bf16[128,2048]{1,0:T(8,128)(2,1)S(1)} %add_convert_fusion.3), channel_id=1, source_target_pairs={{0,8},{8,16},{16,24},{24,28},{28,20},{20,12},{12,4},{4,0},{1,9},{9... | collective-permute-start | bytes 1572872 | tf_op jit(solution)/shard_map/ppermute | solution.py:546
  187.0 46.9 %collective-permute-start.30 = (bf16[8,128,256]{2,1,0:T(8,128)(2,1)S(1)}, bf16[8,128,256]{2,1,0:T(8,128)(2,1)}, u32[]{:S(2)}, u32[]{:S(2)}) collective-permute-start(bf16[8,128,256]{2,1,0:T(8,128)(2,1)S(1)} %get-tuple-element.211), channel_id=1, source_target_pairs={{0,2},{2,0},{1,3},{3,1},{4,6},{6,4},{5,7},{7,5},{8,10},{10,8},{9,1... | collective-permute-start | bytes 1572872 | tf_op jit(solution)/shard_map/ppermute | solution.py:392
  189.1 28.7 %all-to-all-start.3 = ((bf16[8,40,1024]{2,1,0:T(8,128)(2,1)}), bf16[8,40,1024]{2,1,0:T(8,128)(2,1)}, u32[]{:S(2)}, u32[]{:S(2)}) async-start(bf16[8,40,1024]{2,1,0:T(8,128)(2,1)} %fusion.16), calls=%async_computation.3 | async-start | bytes 1310720 | tf_op jit(solution)/shard_map/all_to_all | solution.py:396
  194.9 11.2 %collective-permute-start.24 = (bf16[128,2048]{1,0:T(8,128)(2,1)S(1)}, bf16[128,2048]{1,0:T(8,128)(2,1)S(1)}, u32[]{:S(2)}, u32[]{:S(2)}) collective-permute-start(bf16[128,2048]{1,0:T(8,128)(2,1)S(1)} %add_convert_fusion.2.refs_0_), channel_id=1, source_target_pairs={{0,2},{2,0},{1,3},{3,1},{4,6},{6,4},{5,7},{7,5},{8,10},{10,8},{9,1... | collective-permute-start | bytes 1572872 | tf_op jit(solution)/shard_map/ppermute | solution.py:392
  195.0 22.0 %collective-permute-start.23 = (bf16[128,2048]{1,0:T(8,128)(2,1)S(1)}, bf16[128,2048]{1,0:T(8,128)(2,1)S(1)}, u32[]{:S(2)}, u32[]{:S(2)}) collective-permute-start(bf16[128,2048]{1,0:T(8,128)(2,1)S(1)} %add_convert_fusion.2.refs_0_), channel_id=1, source_target_pairs={{0,4},{8,0},{16,8},{24,16},{28,24},{20,28},{12,20},{4,12},{1,5},{9... | collective-permute-start | bytes 1572872 | tf_op jit(solution)/shard_map/ppermute | solution.py:464
  196.9 20.8 %collective-permute-start.22 = (bf16[128,2048]{1,0:T(8,128)(2,1)S(1)}, bf16[128,2048]{1,0:T(8,128)(2,1)}, u32[]{:S(2)}, u32[]{:S(2)}) collective-permute-start(bf16[128,2048]{1,0:T(8,128)(2,1)S(1)} %add_convert_fusion.2.refs_0_), channel_id=1, source_target_pairs={{0,8},{8,16},{16,24},{24,28},{28,20},{20,12},{12,4},{4,0},{1,9},{9... | collective-permute-start | bytes 1572872 | tf_op jit(solution)/shard_map/ppermute | solution.py:464
  217.7 17.4 %collective-permute-start.28 = (bf16[128,2048]{1,0:T(8,128)(2,1)}, bf16[128,2048]{1,0:T(8,128)(2,1)}, u32[]{:S(2)}, u32[]{:S(2)}) collective-permute-start(bf16[128,2048]{1,0:T(8,128)(2,1)} %collective-permute-done.22.refs_2_), channel_id=1, source_target_pairs={{0,2},{2,0},{1,3},{3,1},{4,6},{6,4},{5,7},{7,5},{8,10},{10,8},{9,1... | collective-permute-start | bytes 1572872 | tf_op jit(solution)/shard_map/ppermute | solution.py:392
  217.7 17.4 %collective-permute-start.26 = (bf16[128,2048]{1,0:T(8,128)(2,1)}, bf16[128,2048]{1,0:T(8,128)(2,1)}, u32[]{:S(2)}, u32[]{:S(2)}) collective-permute-start(bf16[128,2048]{1,0:T(8,128)(2,1)} %collective-permute-done.22.refs_2_), channel_id=1, source_target_pairs={{0,8},{8,16},{16,24},{24,28},{28,20},{20,12},{12,4},{4,0},{1,9},{9... | collective-permute-start | bytes 1572872 | tf_op jit(solution)/shard_map/ppermute | solution.py:464
  222.1 13.1 %collective-permute-start.29 = (bf16[128,2048]{1,0:T(8,128)(2,1)}, bf16[128,2048]{1,0:T(8,128)(2,1)}, u32[]{:S(2)}, u32[]{:S(2)}) collective-permute-start(bf16[128,2048]{1,0:T(8,128)(2,1)} %copy-done.18), channel_id=1, source_target_pairs={{0,2},{2,0},{1,3},{3,1},{4,6},{6,4},{5,7},{7,5},{8,10},{10,8},{9,1... | collective-permute-start | bytes 1572872 | tf_op jit(solution)/shard_map/ppermute | solution.py:392
  222.3 14.5 %collective-permute-start.27 = (bf16[128,2048]{1,0:T(8,128)(2,1)}, bf16[128,2048]{1,0:T(8,128)(2,1)}, u32[]{:S(2)}, u32[]{:S(2)}) collective-permute-start(bf16[128,2048]{1,0:T(8,128)(2,1)} %copy-done.18), channel_id=1, source_target_pairs={{0,4},{8,0},{16,8},{24,16},{28,24},{20,28},{12,20},{4,12},{1,5},{9... | collective-permute-start | bytes 1572872 | tf_op jit(solution)/shard_map/ppermute | solution.py:464
  237.7 25.8 %all-to-all-start.4 = ((bf16[8,192,256]{2,1,0:T(8,128)(2,1)}), bf16[8,192,256]{2,1,0:T(8,128)(2,1)}, u32[]{:S(2)}, u32[]{:S(2)}) async-start(bf16[8,192,256]{2,1,0:T(8,128)(2,1)} %pad_maximum_fusion), calls=%async_computation.4 | async-start | bytes 1572864 | tf_op jit(solution)/shard_map/all_to_all | solution.py:396
  248.9 8.3 %collective-permute-start.35 = (bf16[96,1024]{1,0:T(8,128)(2,1)S(1)}, bf16[96,1024]{1,0:T(8,128)(2,1)S(1)}, u32[]{:S(2)}, u32[]{:S(2)}) collective-permute-start(bf16[96,1024]{1,0:T(8,128)(2,1)S(1)} %constant_dynamic-slice_fusion), channel_id=1, source_target_pairs={{0,2},{2,0},{1,3},{3,1},{4,6},{6,4},{5,7},{7,5},{8,10},{10,8},{9,1... | collective-permute-start | bytes 589832 | tf_op jit(solution)/shard_map/ppermute | solution.py:392
  250.2 24.3 %copy-start.8 = (bf16[1024,512]{1,0:T(8,128)(2,1)S(1)}, bf16[1024,512]{1,0:T(8,128)(2,1)}, u32[]{:S(2)}) copy-start(bf16[1024,512]{1,0:T(8,128)(2,1)} %refs_1_.1) | copy-start | bytes 3145732
  250.2 14.6 %collective-permute-start.33 = (bf16[128,2048]{1,0:T(8,128)(2,1)}, bf16[128,2048]{1,0:T(8,128)(2,1)}, u32[]{:S(2)}, u32[]{:S(2)}) collective-permute-start(bf16[128,2048]{1,0:T(8,128)(2,1)} %collective-permute-done.26.refs_2_), channel_id=1, source_target_pairs={{0,2},{2,0},{1,3},{3,1},{4,6},{6,4},{5,7},{7,5},{8,10},{10,8},{9,1... | collective-permute-start | bytes 1572872 | tf_op jit(solution)/shard_map/ppermute | solution.py:392
  250.8 16.5 %collective-permute-start.31 = (bf16[128,2048]{1,0:T(8,128)(2,1)}, bf16[128,2048]{1,0:T(8,128)(2,1)}, u32[]{:S(2)}, u32[]{:S(2)}) collective-permute-start(bf16[128,2048]{1,0:T(8,128)(2,1)} %collective-permute-done.26.refs_2_), channel_id=1, source_target_pairs={{0,8},{8,16},{16,24},{24,28},{28,20},{20,12},{12,4},{4,0},{1,9},{9... | collective-permute-start | bytes 1572872 | tf_op jit(solution)/shard_map/ppermute | solution.py:464
  252.6 14.6 %collective-permute-start.34 = (bf16[128,2048]{1,0:T(8,128)(2,1)}, bf16[128,2048]{1,0:T(8,128)(2,1)}, u32[]{:S(2)}, u32[]{:S(2)}) collective-permute-start(bf16[128,2048]{1,0:T(8,128)(2,1)} %collective-permute-done.27.refs_3_), channel_id=1, source_target_pairs={{0,2},{2,0},{1,3},{3,1},{4,6},{6,4},{5,7},{7,5},{8,10},{10,8},{9,1... | collective-permute-start | bytes 1572872 | tf_op jit(solution)/shard_map/ppermute | solution.py:392
  252.6 17.7 %collective-permute-start.32 = (bf16[128,2048]{1,0:T(8,128)(2,1)}, bf16[128,2048]{1,0:T(8,128)(2,1)}, u32[]{:S(2)}, u32[]{:S(2)}) collective-permute-start(bf16[128,2048]{1,0:T(8,128)(2,1)} %collective-permute-done.27.refs_3_), channel_id=1, source_target_pairs={{0,4},{8,0},{16,8},{24,16},{28,24},{20,28},{12,20},{4,12},{1,5},{9... | collective-permute-start | bytes 1572872 | tf_op jit(solution)/shard_map/ppermute | solution.py:464
  257.3 24.1 %copy-start.15 = (bf16[136,1024]{1,0:T(8,128)(2,1)}, bf16[136,1024]{1,0:T(8,128)(2,1)S(1)}, u32[]{:S(2)}) copy-start(bf16[136,1024]{1,0:T(8,128)(2,1)S(1)} %pad_maximum_fusion.1.refs_0_) | copy-start | bytes 835588
  270.4 6.6 %collective-permute-start.41 = (bf16[136,1024]{1,0:T(8,128)(2,1)S(1)}, bf16[136,1024]{1,0:T(8,128)(2,1)S(1)}, u32[]{:S(2)}, u32[]{:S(2)}) collective-permute-start(bf16[136,1024]{1,0:T(8,128)(2,1)S(1)} %pad_maximum_fusion.1.refs_0_), channel_id=1, source_target_pairs={{0,2},{2,0},{1,3},{3,1},{4,6},{6,4},{5,7},{7,5},{8,10},{10,8},{9,1... | collective-permute-start | bytes 835592 | tf_op jit(solution)/shard_map/ppermute | solution.py:392
  270.4 11.0 %collective-permute-start.40 = (bf16[136,1024]{1,0:T(8,128)(2,1)S(1)}, bf16[136,1024]{1,0:T(8,128)(2,1)}, u32[]{:S(2)}, u32[]{:S(2)}) collective-permute-start(bf16[136,1024]{1,0:T(8,128)(2,1)S(1)} %pad_maximum_fusion.1.refs_0_), channel_id=1, source_target_pairs={{0,4},{8,0},{16,8},{24,16},{28,24},{20,28},{12,20},{4,12},{1,5},{9... | collective-permute-start | bytes 835592 | tf_op jit(solution)/shard_map/ppermute | solution.py:464
  270.6 23.6 %collective-permute-start.37 = (bf16[128,2048]{1,0:T(8,128)(2,1)}, bf16[128,2048]{1,0:T(8,128)(2,1)}, u32[]{:S(2)}, u32[]{:S(2)}) collective-permute-start(bf16[128,2048]{1,0:T(8,128)(2,1)} %collective-permute-done.31.refs_2_), channel_id=1, source_target_pairs={{0,2},{2,0},{1,3},{3,1},{4,6},{6,4},{5,7},{7,5},{8,10},{10,8},{9,1... | collective-permute-start | bytes 1572872 | tf_op jit(solution)/shard_map/ppermute | solution.py:392
  270.9 23.3 %collective-permute-start.36 = (bf16[128,2048]{1,0:T(8,128)(2,1)}, bf16[128,2048]{1,0:T(8,128)(2,1)S(1)}, u32[]{:S(2)}, u32[]{:S(2)}) collective-permute-start(bf16[128,2048]{1,0:T(8,128)(2,1)} %collective-permute-done.31.refs_2_), channel_id=1, source_target_pairs={{0,8},{8,16},{16,24},{24,28},{28,20},{20,12},{12,4},{4,0},{1,9},{9... | collective-permute-start | bytes 1572872 | tf_op jit(solution)/shard_map/ppermute | solution.py:464
  274.5 19.8 %collective-permute-start.38 = (bf16[128,2048]{1,0:T(8,128)(2,1)}, bf16[128,2048]{1,0:T(8,128)(2,1)}, u32[]{:S(2)}, u32[]{:S(2)}) collective-permute-start(bf16[128,2048]{1,0:T(8,128)(2,1)} %collective-permute-done.32.refs_3_), channel_id=1, source_target_pairs={{0,2},{2,0},{1,3},{3,1},{4,6},{6,4},{5,7},{7,5},{8,10},{10,8},{9,1... | collective-permute-start | bytes 1572872 | tf_op jit(solution)/shard_map/ppermute | solution.py:392
  276.9 17.3 %collective-permute-start.42 = (bf16[256,1024]{1,0:T(8,128)(2,1)S(1)}, bf16[256,1024]{1,0:T(8,128)(2,1)S(1)}, u32[]{:S(2)}, u32[]{:S(2)}) collective-permute-start(bf16[256,1024]{1,0:T(8,128)(2,1)S(1)} %get-tuple-element.247), channel_id=1, source_target_pairs={{0,1},{1,0},{2,3},{3,2},{4,5},{5,4},{6,7},{7,6},{8,9},{9,8},{10,11... | collective-permute-start | bytes 1572872 | tf_op jit(solution)/shard_map/ppermute | solution.py:423
  281.4 12.8 %collective-permute-start.39 = (bf16[136,1024]{1,0:T(8,128)(2,1)S(1)}, bf16[136,1024]{1,0:T(8,128)(2,1)}, u32[]{:S(2)}, u32[]{:S(2)}) collective-permute-start(bf16[136,1024]{1,0:T(8,128)(2,1)S(1)} %pad_maximum_fusion.1.refs_0_), channel_id=1, source_target_pairs={{0,8},{8,16},{16,24},{24,28},{28,20},{20,12},{12,4},{4,0},{1,9},{9... | collective-permute-start | bytes 835592 | tf_op jit(solution)/shard_map/ppermute | solution.py:464
  294.3 12.5 %collective-permute-start.46 = (bf16[136,1024]{1,0:T(8,128)(2,1)}, bf16[136,1024]{1,0:T(8,128)(2,1)}, u32[]{:S(2)}, u32[]{:S(2)}) collective-permute-start(bf16[136,1024]{1,0:T(8,128)(2,1)} %collective-permute-done.39.refs_1_), channel_id=1, source_target_pairs={{0,2},{2,0},{1,3},{3,1},{4,6},{6,4},{5,7},{7,5},{8,10},{10,8},{9,1... | collective-permute-start | bytes 835592 | tf_op jit(solution)/shard_map/ppermute | solution.py:392
  294.3 12.4 %collective-permute-start.44 = (bf16[136,1024]{1,0:T(8,128)(2,1)}, bf16[136,1024]{1,0:T(8,128)(2,1)}, u32[]{:S(2)}, u32[]{:S(2)}) collective-permute-start(bf16[136,1024]{1,0:T(8,128)(2,1)} %collective-permute-done.39.refs_1_), channel_id=1, source_target_pairs={{0,8},{8,16},{16,24},{24,28},{28,20},{20,12},{12,4},{4,0},{1,9},{9... | collective-permute-start | bytes 835592 | tf_op jit(solution)/shard_map/ppermute | solution.py:464
  294.7 12.0 %collective-permute-start.47 = (bf16[136,1024]{1,0:T(8,128)(2,1)}, bf16[136,1024]{1,0:T(8,128)(2,1)}, u32[]{:S(2)}, u32[]{:S(2)}) collective-permute-start(bf16[136,1024]{1,0:T(8,128)(2,1)} %collective-permute-done.40.refs_2_), channel_id=1, source_target_pairs={{0,2},{2,0},{1,3},{3,1},{4,6},{6,4},{5,7},{7,5},{8,10},{10,8},{9,1... | collective-permute-start | bytes 835592 | tf_op jit(solution)/shard_map/ppermute | solution.py:392
  294.9 11.8 %collective-permute-start.45 = (bf16[136,1024]{1,0:T(8,128)(2,1)}, bf16[136,1024]{1,0:T(8,128)(2,1)}, u32[]{:S(2)}, u32[]{:S(2)}) collective-permute-start(bf16[136,1024]{1,0:T(8,128)(2,1)} %collective-permute-done.40.refs_2_), channel_id=1, source_target_pairs={{0,4},{8,0},{16,8},{24,16},{28,24},{20,28},{12,20},{4,12},{1,5},{9... | collective-permute-start | bytes 835592 | tf_op jit(solution)/shard_map/ppermute | solution.py:464
  298.0 13.4 %all-to-all-start.5 = ((bf16[32,32,128]{2,1,0:T(8,128)(2,1)}), bf16[32,32,128]{2,1,0:T(8,128)(2,1)S(1)}, u32[]{:S(2)}, u32[]{:S(2)}) async-start(bf16[32,32,128]{2,1,0:T(8,128)(2,1)} %broadcast_in_dim.62), calls=%async_computation.5 | async-start | bytes 524288 | tf_op jit(solution)/shard_map/all_to_all | solution.py:877
  300.8 10.7 %collective-permute-start.43 = (bf16[128,2048]{1,0:T(8,128)(2,1)}, bf16[128,2048]{1,0:T(8,128)(2,1)S(1)}, u32[]{:S(2)}, u32[]{:S(2)}) collective-permute-start(bf16[128,2048]{1,0:T(8,128)(2,1)} %copy-done.17), channel_id=1, source_target_pairs={{0,2},{2,0},{1,3},{3,1},{4,6},{6,4},{5,7},{7,5},{8,10},{10,8},{9,1... | collective-permute-start | bytes 1572872 | tf_op jit(solution)/shard_map/ppermute | solution.py:392
  311.4 5.7 %collective-permute-start.50 = (bf16[136,1024]{1,0:T(8,128)(2,1)}, bf16[136,1024]{1,0:T(8,128)(2,1)S(1)}, u32[]{:S(2)}, u32[]{:S(2)}) collective-permute-start(bf16[136,1024]{1,0:T(8,128)(2,1)} %collective-permute-done.44.refs_3_), channel_id=1, source_target_pairs={{0,2},{2,0},{1,3},{3,1},{4,6},{6,4},{5,7},{7,5},{8,10},{10,8},{9,1... | collective-permute-start | bytes 835592 | tf_op jit(solution)/shard_map/ppermute | solution.py:392
  311.6 9.2 %collective-permute-start.48 = (bf16[136,1024]{1,0:T(8,128)(2,1)}, bf16[136,1024]{1,0:T(8,128)(2,1)S(1)}, u32[]{:S(2)}, u32[]{:S(2)}) collective-permute-start(bf16[136,1024]{1,0:T(8,128)(2,1)} %collective-permute-done.44.refs_3_), channel_id=1, source_target_pairs={{0,8},{8,16},{16,24},{24,28},{28,20},{20,12},{12,4},{4,0},{1,9},{9... | collective-permute-start | bytes 835592 | tf_op jit(solution)/shard_map/ppermute | solution.py:464
  312.3 8.5 %collective-permute-start.51 = (bf16[136,1024]{1,0:T(8,128)(2,1)}, bf16[136,1024]{1,0:T(8,128)(2,1)S(1)}, u32[]{:S(2)}, u32[]{:S(2)}) collective-permute-start(bf16[136,1024]{1,0:T(8,128)(2,1)} %collective-permute-done.45.refs_4_), channel_id=1, source_target_pairs={{0,2},{2,0},{1,3},{3,1},{4,6},{6,4},{5,7},{7,5},{8,10},{10,8},{9,1... | collective-permute-start | bytes 835592 | tf_op jit(solution)/shard_map/ppermute | solution.py:392
  312.3 9.3 %collective-permute-start.49 = (bf16[136,1024]{1,0:T(8,128)(2,1)}, bf16[136,1024]{1,0:T(8,128)(2,1)S(1)}, u32[]{:S(2)}, u32[]{:S(2)}) collective-permute-start(bf16[136,1024]{1,0:T(8,128)(2,1)} %collective-permute-done.45.refs_4_), channel_id=1, source_target_pairs={{0,4},{8,0},{16,8},{24,16},{28,24},{20,28},{12,20},{4,12},{1,5},{9... | collective-permute-start | bytes 835592 | tf_op jit(solution)/shard_map/ppermute | solution.py:464
  321.6 3.7 %collective-permute-start.53 = (bf16[136,1024]{1,0:T(8,128)(2,1)S(1)}, bf16[136,1024]{1,0:T(8,128)(2,1)S(1)}, u32[]{:S(2)}, u32[]{:S(2)}) collective-permute-start(bf16[136,1024]{1,0:T(8,128)(2,1)S(1)} %collective-permute-done.48.refs_5_), channel_id=1, source_target_pairs={{0,2},{2,0},{1,3},{3,1},{4,6},{6,4},{5,7},{7,5},{8,10},{10,8},{9,1... | collective-permute-start | bytes 835592 | tf_op jit(solution)/shard_map/ppermute | solution.py:392
  321.6 9.1 %collective-permute-start.52 = (bf16[136,1024]{1,0:T(8,128)(2,1)S(1)}, bf16[136,1024]{1,0:T(8,128)(2,1)S(1)}, u32[]{:S(2)}, u32[]{:S(2)}) collective-permute-start(bf16[136,1024]{1,0:T(8,128)(2,1)S(1)} %collective-permute-done.48.refs_5_), channel_id=1, source_target_pairs={{0,8},{8,16},{16,24},{24,28},{28,20},{20,12},{12,4},{4,0},{1,9},{9... | collective-permute-start | bytes 835592 | tf_op jit(solution)/shard_map/ppermute | solution.py:464
  322.9 2.5 collective-permute-start.54
  330.7 1.6 collective-permute-start.55
  (38 other events, 307.1 us)

commit v8 on v7

--- a/solution.py
+++ b/solution.py
@@ -66,8 +66,11 @@
         unit, _ = normalize(input_ref[...].astype(F32))
         crops = steps_ref.shape[0]
         crop = lax.broadcasted_iota(jnp.int32, (crops, rows), 0)
-        onehot = jnp.where(crop == segment_ref[...], 1.0, 0.0)
-        lead = product(onehot, steps_ref[...].astype(F32), 0, 0)[:, :1] / 12.0
+        steps = jnp.zeros((crops, rows), jnp.int32)
+        for at in range(crops):
+            steps = jnp.where(crop == at, steps_ref[at], steps)
+        steps = jnp.where(crop == segment_ref[...], steps, 0).astype(F32)
+        lead = product(steps, jnp.ones((crops, 128), F32), 0, 0)[:, :1] / 12.0
         attn_in = unit * gain[...] + shift[...] + lead * lead_weight[...]
         attn_in_ref[...] = attn_in.astype(BF16)
 
@@ -83,13 +86,12 @@
 def project(block_input, segments, lead_steps, gain, shift, lead_weight, weights):
     rows, model = block_input.shape
     heads = weights[0].shape[1] // HD
-    steps = jnp.broadcast_to(lead_steps[:, None], (lead_steps.shape[0], 128))
     line = whole_spec((1, model))
     column = pl.BlockSpec((model, 2 * HD), lambda at: (0, at))
     return pl.pallas_call(
         project_kernel,
         grid=(heads // 2,),
-        in_specs=[whole_spec(block_input.shape), whole_spec((1, rows)), whole_spec(steps.shape)]
+        in_specs=[whole_spec(block_input.shape), whole_spec((1, rows)), pl.BlockSpec(memory_space=pltpu.SMEM)]
         + [line] * 3
         + [column] * 3,
         out_specs=[
@@ -100,14 +102,18 @@
         compiler_params=streaming,
         cost_estimate=cost(2 * rows * model * 3 * heads * HD, 8 * 2**20),
         name="project",
-    )(block_input, segments[None], steps, gain[None], shift[None], lead_weight[None], *weights)
-
-
-def mlp_kernel(count, input_ref, grad_ref, *refs):
+    )(block_input, segments[None], lead_steps, gain[None], shift[None], lead_weight[None], *weights)
+
+
+def mlp_kernel(count, core_ref, input_ref, grad_ref, *refs):
     branches, refs = refs[:count], refs[count:]
     output_bias, gain, shift, up_weight, up_bias, down_weight = refs[:6]
-    wide_ref, mlp_in_ref, hidden_ref, bias_ref, forward_ref, back_ref, forward, back = refs[6:]
+    keep_ref, give_ref, keep_in_ref, give_in_ref, hidden_ref, bias_ref, forward_ref, back_ref = refs[
+        6:14
+    ]
+    mlp_in_ref, forward, back = refs[14:]
     at = pl.program_id(0)
+    is_down = core_ref[core_ref.shape[0] - 1] == 0
 
     @pl.when(at == 0)
     def _():
@@ -116,7 +122,10 @@
             hidden += branch[...].astype(F32)
         hidden_ref[...] = hidden
         unit, _ = normalize(hidden)
-        mlp_in_ref[...] = (unit * gain[...] + shift[...]).astype(BF16)
+        mlp_in = (unit * gain[...] + shift[...]).astype(BF16)
+        mlp_in_ref[...] = mlp_in
+        keep_in_ref[...] = jnp.where(is_down, grad_ref[...], mlp_in)
+        give_in_ref[...] = jnp.where(is_down, mlp_in, grad_ref[...])
         forward[...] = jnp.zeros_like(forward)
         back[...] = jnp.zeros_like(back)
 
@@ -126,8 +135,8 @@
     active = (upper * share).astype(BF16)
     d_active = product(grad_ref[...], down_weight[...], 1, 1)
     d_upper = (d_active * slope).astype(BF16)
-    wide_ref[0] = active
-    wide_ref[1] = d_upper
+    keep_ref[...] = jnp.where(is_down, active, d_upper)
+    give_ref[...] = jnp.where(is_down, d_upper, active)
     bias_ref[...] = jnp.sum(d_upper.astype(F32), axis=0, keepdims=True)
     forward[...] += product(active, down_weight[...])
     back[...] += product(d_upper, up_weight[...], 1, 1)
@@ -138,42 +147,44 @@
         back_ref[...] = back[...].astype(BF16)
 
 
-def mlp(block_input, out_grad, branches, output_bias, gain, shift, up_weight, up_bias, down_weight):
+def mlp(
+    table, block_input, out_grad, branches, output_bias, gain, shift, up_weight, up_bias, down_weight
+):
     rows, model = block_input.shape
     units = up_weight.shape[1]
-    step = math.gcd(units, 256)
+    step = math.gcd(units, 512)
     tile, line = whole_spec((rows, model)), whole_spec((1, model))
+    wide = pl.BlockSpec((rows, step), lambda at, table: (0, at))
+    bias = pl.BlockSpec((1, step), lambda at, table: (0, at))
     return pl.pallas_call(
         functools.partial(mlp_kernel, len(branches)),
-        grid=(units // step,),
-        in_specs=[tile] * (2 + len(branches))
-        + [line] * 3
+        grid_spec=pltpu.PrefetchScalarGridSpec(
+            num_scalar_prefetch=1,
+            grid=(units // step,),
+            in_specs=[tile] * (2 + len(branches))
+            + [line] * 3
+            + [
+                pl.BlockSpec((model, step), lambda at, table: (0, at)),
+                bias,
+                pl.BlockSpec((step, model), lambda at, table: (at, 0)),
+            ],
+            out_specs=[wide, wide, tile, tile, tile, bias, tile, tile],
+            scratch_shapes=[pltpu.VMEM((rows, model), BF16)]
+            + [pltpu.VMEM((rows, model), F32)] * 2,
+        ),
+        out_shape=[struct((rows, units), BF16)] * 2
+        + [struct((rows, model), BF16)] * 2
         + [
-            pl.BlockSpec((model, step), lambda at: (0, at)),
-            pl.BlockSpec((1, step), lambda at: (0, at)),
-            pl.BlockSpec((step, model), lambda at: (at, 0)),
-        ],
-        out_specs=[
-            pl.BlockSpec((2, rows, step), lambda at: (0, 0, at)),
-            tile,
-            tile,
-            pl.BlockSpec((1, step), lambda at: (0, at)),
-            tile,
-            tile,
-        ],
-        out_shape=[
-            struct((2, rows, units), BF16),
-            struct((rows, model), BF16),
             struct((rows, model), F32),
             struct((1, units), F32),
             struct((rows, model), BF16),
             struct((rows, model), BF16),
         ],
-        scratch_shapes=[pltpu.VMEM((rows, model), F32)] * 2,
         compiler_params=streaming,
         cost_estimate=cost(8 * rows * model * units, 16 * 2**20, 2 * rows * units),
         name="mlp",
     )(
+        table,
         block_input,
         out_grad,
         *branches,
@@ -220,55 +231,68 @@
     )(hidden, out_grad, *parts, gain[None], output_weight)
 
 
-def load_keys(pieces, crops, keys, key_t, value_t, value_n):
-    start = 0
-    for piece in pieces:
-        chips, _, patches = piece.shape
-        for chip in range(chips):
-            crop = lax.broadcasted_iota(jnp.int32, (HD, patches), 0)
-            segment = piece[chip, pl.ds(seg_row, 16), :].astype(F32)[:1].astype(jnp.int32)
-            mask = jnp.where((crop != segment) & (crop < crops), masked_value, 0.0)
-            key = piece[chip, pl.ds(HD, HD), :]
-            value = piece[chip, pl.ds(2 * HD, HD), :]
-            place = pl.ds(start, patches)
-            keys[place, :] = jnp.concatenate([key.astype(F32), mask], axis=0).T.astype(BF16)
-            if key_t is not None:
-                key_t[:, place] = key
-            if value_t is not None:
-                value_t[pl.ds(0, HD), place] = value
-                value_t[pl.ds(HD, 16), place] = jnp.ones((16, patches), BF16)
-            if value_n is not None:
-                value_n[place, :] = value.astype(F32).T.astype(BF16)
-            start += patches
-
-
-def masked_query(query_ref):
+def mask_rows(piece, chip, crops):
+    crop = lax.broadcasted_iota(jnp.int32, (HD, piece.shape[2]), 0)
+    segment = piece[chip, pl.ds(seg_row, 16), :].astype(F32)[:1].astype(jnp.int32)
+    return jnp.where((crop != segment) & (crop < crops), masked_value, 0.0)
+
+
+def load_keys(piece, crops, keys, key_t, value_n):
+    chips, _, patches = piece.shape
+    for chip in range(chips):
+        key = piece[chip, pl.ds(HD, HD), :]
+        value = piece[chip, pl.ds(2 * HD, HD), :]
+        place = pl.ds(chip * patches, patches)
+        both = jnp.concatenate([key.astype(F32), mask_rows(piece, chip, crops)], axis=0)
+        keys[place, :] = both.T.astype(BF16)
+        key_t[:, place] = key
+        value_n[place, :] = value.astype(F32).T.astype(BF16)
+
+
+def masked_query(query_ref, dtype=BF16):
     query = query_ref[0, pl.ds(0, HD), :].astype(F32) * 0.125
     segment = query_ref[0, pl.ds(seg_row, 16), :].astype(F32)[:1].astype(jnp.int32)
     crop = lax.broadcasted_iota(jnp.int32, query.shape, 0)
     onehot = jnp.where(crop == segment, 1.0, 0.0)
-    return jnp.concatenate([query, onehot], axis=0).astype(BF16)
-
-
-def forward_kernel(crops, step, query_ref, own, other, raw_ref, out_ref, logsum_ref, keys, value_t):
+    return jnp.concatenate([query, onehot], axis=0).astype(dtype)
+
+
+def forward_kernel(
+    crops, step, query_ref, own, other, raw_ref, out_ref, logsum_ref, key_t, value_n, scores
+):
     @pl.when(pl.program_id(0) == 0)
     def _():
-        load_keys((own, other), crops, keys, None, value_t, None)
-
-    query = masked_query(query_ref)
-    count = query.shape[1]
-    top = jnp.full((1, count), masked_value, F32)
-    accum = jnp.zeros((HD + 16, count), F32)
-    for start in range(0, keys.shape[0], step):
-        scores = product(keys[pl.ds(start, step), :], query)
-        new_top = jnp.maximum(top, jnp.max(scores, axis=0, keepdims=True))
-        weights = jnp.exp(scores - new_top).astype(BF16)
-        accum = accum * jnp.exp(top - new_top) + product(value_t[:, pl.ds(start, step)], weights)
-        top = new_top
+        start = 0
+        for piece in (own, other):
+            chips, _, patches = piece.shape
+            for chip in range(chips):
+                place = pl.ds(start, patches)
+                key = piece[chip, pl.ds(HD, HD), :].astype(F32)
+                key_t[:, place] = jnp.concatenate([key, mask_rows(piece, chip, crops)], axis=0).astype(BF16)
+                value = piece[chip, pl.ds(2 * HD, HD), :].astype(F32)
+                value = jnp.concatenate([value, jnp.ones_like(value)], axis=0)
+                value_n[place, :] = value.T.astype(BF16)
+                start += patches
+
+    query = masked_query(query_ref, F32).T.astype(BF16)
+    count = query.shape[0]
+    top = jnp.full((count, 128), masked_value, F32)
+    for start in range(0, key_t.shape[1], step):
+        block = product(query, key_t[:, pl.ds(start, step)])
+        scores[:, pl.ds(start, step)] = block
+        for at in range(0, step, 128):
+            top = jnp.maximum(top, block[:, at : at + 128])
+    top = jnp.max(top, axis=1, keepdims=True)
+    accum = jnp.zeros((count, 2 * HD), F32)
+    for start in range(0, key_t.shape[1], step):
+        weights = jnp.exp(scores[:, pl.ds(start, step)] - top).astype(BF16)
+        accum += product(weights, value_n[pl.ds(start, step), :])
+    accum = accum.T
     total = accum[HD : HD + 1]
     raw = accum[:HD] / total
     raw_ref[0] = raw
     out_ref[0] = raw.astype(BF16)
+    top = jnp.broadcast_to(top, (count, 128)).T[:1]
     logsum_ref[0] = top + jnp.log(total)
 
 
@@ -287,7 +311,7 @@
 
     @pl.when(group == 0)
     def _():
-        load_keys((piece,), crops, keys, key_t, None, value_n)
+        load_keys(piece, crops, keys, key_t, value_n)
         sums[...] = jnp.zeros_like(sums)
 
     query = masked_query(query_ref)
@@ -339,8 +363,12 @@
             struct((groups, HD, patches), BF16),
             struct((groups, 1, patches), F32),
         ],
-        scratch_shapes=[pltpu.VMEM((count, 2 * HD), BF16), pltpu.VMEM((HD + 16, count), BF16)],
-        compiler_params=params,
+        scratch_shapes=[
+            pltpu.VMEM((2 * HD, count), BF16),
+            pltpu.VMEM((count, 2 * HD), BF16),
+            pltpu.VMEM((patches, count), F32),
+        ],
+        compiler_params=streaming,
         cost_estimate=cost(
             groups * patches * count * 4096, 4 * 2**20, groups * patches * count
         ),
@@ -480,65 +508,26 @@
         return bool(self.state[0] or self.state[1])
 
 
-def partial_kernel(core, grad, mlp_in, wide, grad_far, mlp_in_far, wide_far, out_ref):
-    is_down = core[0] == 0
-
-    @pl.when(is_down)
-    def _():
-        out_ref[...] = (
-            product(wide[0], grad[...], 0, 0) + product(wide_far[...], grad_far[...], 0, 0)
-        ).astype(BF16)
-
-    @pl.when(jnp.logical_not(is_down))
-    def _():
-        out_ref[...] = (
-            product(mlp_in[...], wide[0], 0, 0) + product(mlp_in_far[...], wide_far[...], 0, 0)
-        ).astype(BF16)
-
-
-def weight_partial(core, grad, mlp_in, wide, grad_far, mlp_in_far, wide_far):
-    rows, model = grad.shape
-    units = wide.shape[2]
-    half = units // 2
-    tile = whole_spec((rows, model))
-    if model != half:
-        down = product(wide[0], grad, 0, 0) + product(wide_far, grad_far, 0, 0)
-        down = down.reshape(2, half, model).transpose(1, 0, 2).reshape(model, units)
-        up = product(mlp_in, wide[1], 0, 0) + product(mlp_in_far, wide_far, 0, 0)
-        return jnp.where(core == 0, down, up).astype(BF16)
-    return pl.pallas_call(
-        partial_kernel,
-        grid_spec=pltpu.PrefetchScalarGridSpec(
-            num_scalar_prefetch=1,
-            grid=(2,),
-            in_specs=[
-                tile,
-                tile,
-                pl.BlockSpec((1, rows, half), lambda at, core: (core[0], 0, at)),
-                tile,
-                tile,
-                pl.BlockSpec((rows, half), lambda at, core: (0, at)),
-            ],
-            out_specs=pl.BlockSpec((model, half), lambda at, core: (0, at)),
-        ),
-        out_shape=struct((model, units), BF16),
-        compiler_params=streaming,
-        cost_estimate=cost(4 * rows * model * units, 12 * 2**20),
-        name="weight_partial",
-    )(core[None], grad, mlp_in, wide, grad_far, mlp_in_far, wide_far)
+def add_kernel(counts, _, *refs):
+    outputs, refs = refs[-len(counts) :], list(refs[: -len(counts)])
+    keep_in, far_in = refs.pop(0), refs.pop(0)
+    for count, output in zip(counts, outputs):
+        near, far = refs.pop(0), refs.pop(0)
+        total = product(near[...], keep_in[...], 0, 0) + product(far[...], far_in[...], 0, 0)
+        for _ in range(count):
+            total += refs.pop(0)[...].astype(F32)
+        output[...] = total.astype(BF16)
 
 
 class Reduce:
-    def __init__(self, partial, table):
-        self.chips, self.partial, self.table = lax.axis_size("chip"), partial, table
-        self.shape = (partial.shape[0] // self.chips, partial.shape[1])
+    def __init__(self, keep, far, keep_in, far_in, table):
+        self.chips, self.table = lax.axis_size("chip"), table
+        self.operands, self.sides = (keep, far), (keep_in, far_in)
+        self.units = keep.shape[1] // self.chips
+        self.tiled = self.units % 128 == 0
         self.reach = (self.chips // 2, (self.chips - 1) // 2)
         self.count, self.gather = 0, None
-        self.send([self.block(self.reach[0]), self.block(-self.reach[1])], [])
-
-    def block(self, step):
-        start = self.table[step % self.chips] * self.shape[0]
-        return lax.dynamic_slice_in_dim(self.partial, start, self.shape[0], 0)
+        self.send(self.add([(self.reach[0], []), (-self.reach[1], [])]), [])
 
     def send(self, sides, held):
         self.count += 1
@@ -555,32 +544,71 @@
             self.state = self.gather.state
             return
         arrived, held = self.state
-        sums, done = [], self.count == self.reach[0]
+        wanted, done = [], self.count == self.reach[0]
         for block, reach, side in zip(arrived, self.reach, (1, -1)):
             left = reach - self.count
             if left > 0 or done:
-                parts = held if done else []
-                sums.append(self.add([block] + parts, side * left))
+                wanted.append((side * left, [block] + held))
             else:
                 held = [block]
         if done:
-            self.gather = Gather(sums[0], True, self.place)
+            self.gather = Gather(self.add(wanted)[0], True, self.place)
             self.state = self.gather.state
         else:
-            self.send(sums, held)
-
-    def add(self, parts, step):
-        total = self.block(step).astype(F32)
-        for part in parts:
-            total += part.astype(F32)
-        return total.astype(BF16)
+            self.send(self.add([(step, parts[:1]) for step, parts in wanted]), held)
+
+    def add(self, wanted):
+        (rows, model), units, chips = self.sides[0].shape, self.units, self.chips
+        if not self.tiled:
+            sums = []
+            for step, parts in wanted:
+                start = self.table[step % chips] * units
+                total = functools.reduce(jnp.add, (part.astype(F32) for part in parts), 0.0)
+                for operand, side in zip(self.operands, self.sides):
+                    block = lax.dynamic_slice_in_dim(operand, start, units, 1)
+                    total += product(block, side, 0, 0)
+                sums.append(total.astype(BF16))
+            return sums
+        side = pl.BlockSpec((rows, model), lambda at, table: (0, 0))
+        whole = pl.BlockSpec((units, model), lambda at, table: (0, 0))
+        specs, arrays = [side] * 2, list(self.sides)
+        for step, parts in wanted:
+            block = pl.BlockSpec(
+                (rows, units), lambda at, table, step=step % chips: (0, table[step])
+            )
+            specs += [block] * 2 + [whole] * len(parts)
+            arrays += list(self.operands) + parts
+        return pl.pallas_call(
+            functools.partial(add_kernel, [len(parts) for _, parts in wanted]),
+            grid_spec=pltpu.PrefetchScalarGridSpec(
+                num_scalar_prefetch=1,
+                grid=(1,),
+                in_specs=specs,
+                out_specs=[whole] * len(wanted),
+            ),
+            out_shape=[struct((units, model), BF16)] * len(wanted),
+            compiler_params=streaming,
+            cost_estimate=cost(4 * rows * units * model * len(wanted), 4 * 2**20),
+            name="ring_add",
+        )(self.table, *arrays)
 
     def place(self, outputs, pairs):
-        rows, columns = self.shape
-        half, chips = columns // 2, self.chips
+        units, chips, model = self.units, self.chips, self.sides[0].shape[1]
+        shapes = [struct((chips * units, model), F32), struct((model, chips * units), F32)]
+        if not self.tiled:
+            outputs = outputs or [jnp.zeros(shape.shape, F32) for shape in shapes]
+            down, up = outputs
+            is_down = self.table[2 * chips] == 0
+            for step, near, far in pairs:
+                start = self.table[step % chips] * units
+                first = jnp.where(is_down, near, far).astype(F32)
+                second = jnp.where(is_down, far, near).astype(F32).T
+                down = lax.dynamic_update_slice_in_dim(down, first, start, 0)
+                up = lax.dynamic_update_slice_in_dim(up, second, start, 1)
+            return [down, up]
         first = pairs[0][0] % chips
         stride = pairs[-1][0] % chips - first
-        block = pl.BlockSpec(self.shape, lambda at, table: (0, 0))
+        block = pl.BlockSpec((units, model), lambda at, table: (0, 0))
         return pl.pallas_call(
             functools.partial(place_kernel, len(pairs)),
             grid_spec=pltpu.PrefetchScalarGridSpec(
@@ -589,14 +617,11 @@
                 in_specs=[pl.BlockSpec(memory_space=pl.ANY)] * len(outputs)
                 + [block] * (2 * len(pairs)),
                 out_specs=[
-                    pl.BlockSpec((2, rows, half), lambda at, table: (0, table[first + at * stride], 0)),
-                    pl.BlockSpec((rows, columns), lambda at, table: (table[first + at * stride], 0)),
+                    pl.BlockSpec((units, model), lambda at, table: (table[first + at * stride], 0)),
+                    pl.BlockSpec((model, units), lambda at, table: (0, table[first + at * stride])),
                 ],
             ),
-            out_shape=[
-                struct((2, chips * rows, half), F32),
-                struct((chips * rows, columns), F32),
-            ],
+            out_shape=shapes,
             input_output_aliases={1 + at: at for at in range(len(outputs))},
             compiler_params=streaming,
             cost_estimate=cost(0, 2 * 2**20),
@@ -609,13 +634,11 @@
 
 def place_kernel(count, table, *refs):
     nears, fars, (down, up) = refs[-2 - 2 * count : -2 - count], refs[-2 - count : -2], refs[-2:]
-    half = down.shape[2]
     core = table[table.shape[0] - 1]
 
     def put(first, second):
-        for side in range(2):
-            down[side] = first[:, pl.ds(side * half, half)].astype(F32)
-        up[...] = second[...].astype(F32)
+        down[...] = first[...].astype(F32)
+        up[...] = second[...].astype(F32).T
 
     for at, (near, far) in enumerate(zip(nears, fars)):
         here = pl.program_id(0) == at
@@ -766,14 +789,14 @@
         own = to_heads(jnp.repeat(payload, split, axis=0))
     own, attn_in = lax.optimization_barrier((own, attn_in))
     inputs = Gather(attn_in)
-    grad_far = swap_cores(out_grad)
     raw, out, logsum = attention_forward(queries, own, swap_cores(own), crops)
     other = swap_cores(own)
     attn_out = gather_queries(out, heads, split, rows)
     attn_out = visit([inputs], attn_out)
     branches = across_heads(product(attn_out, output_weight, 0, 0).astype(BF16))
     branches = visit([inputs], branches)
-    wide, mlp_in, hidden, dup_bias, mlp_part, d_mlp_part = mlp(
+    keep, give, keep_in, give_in, hidden, dup_bias, mlp_part, d_mlp_part = mlp(
+        table,
         block_input,
         out_grad,
         branches,
@@ -785,55 +808,51 @@
         down_weight,
     )
     d_mlp = across_heads(d_mlp_part)
-    (wide, mlp_in), d_mlp_part = lax.optimization_barrier(((wide, mlp_in), d_mlp_part))
-    wide, mlp_in = visit([inputs], (wide, mlp_in))
-    mlp_in_far = swap_cores(mlp_in)
-    wide_far = swap_cores(lax.dynamic_index_in_dim(wide, 1 - core, 0, keepdims=False))
-    ring = Reduce(
-        weight_partial(core, out_grad, mlp_in, wide, grad_far, mlp_in_far, wide_far), table
-    )
-    d_mlp = visit([ring, inputs], d_mlp)
+    ring = Reduce(keep, swap_cores(give), keep_in, swap_cores(give_in), table)
     mlp_part, d_mlp = lax.optimization_barrier((mlp_part, d_mlp))
     mlp_out = across_heads(mlp_part)
     d_hidden, d_branch, d_attn, sums = middle(hidden, out_grad, d_mlp, gain_mlp, output_weight)
-    d_branch_far = swap_cores(d_branch)
     grads = scatter_queries(d_attn, heads, split)
-    small = jnp.concatenate([sums.reshape(-1), dup_bias[0]])
-    lines = small.shape[0] // chips
-    small = jnp.pad(
-        small.reshape(chips, 1, lines), ((0, 0), (0, small_rows - 1), (0, model - lines))
-    )
+    d_branch = visit([ring, inputs], d_branch)
     out_near, out_far = share_halves(attn_out, 0)
-    doutput = product(out_near, d_branch) + product(out_far, d_branch_far)
-    doutput = jnp.concatenate([doutput.reshape(chips, -1, model), small], axis=1).astype(BF16)
+    doutput = product(out_near, d_branch) + product(out_far, swap_cores(d_branch))
+    doutput = doutput.astype(BF16).reshape(chips, -1, model)
     pieces = 2
-    dquery, sums = [], {}
+    dquery, turn = [], 0
     for keys, dtype in ((other, BF16), (own, F32)):
         piece_sums = []
         for index in range(pieces):
             last = keys is own and index == pieces - 1
-            if keys is own and index == 0:
-                grads, dquery, doutput = visit([ring], (grads, dquery, doutput))
-                far_sums = swap_cores(sums)
+            if turn == 1:
+                grads, dquery, piece_sums = visit([ring, inputs], (grads, dquery, piece_sums))
+            if turn == 2:
+                far_sums = swap_cores(far_sums)
+                doutput, dquery = lax.optimization_barrier((doutput, dquery))
                 doutput = to_heads(doutput)
-            elif not last:
-                grads, dquery = visit([ring], (grads, dquery))
-            else:
-                grads, dquery, doutput, mlp_out = visit([ring], (grads, dquery, doutput, mlp_out))
-                doutput = jnp.sum(doutput.astype(F32), axis=0).astype(BF16)
+            if turn == 3:
+                grads, dquery, piece_sums, mlp_out = visit(
+                    [ring], (grads, dquery, piece_sums, mlp_out)
+                )
                 block_output = hidden + down_bias
                 for part in mlp_out:
                     block_output += part.astype(F32)
                 block_output = block_output.astype(BF16)
             dtypes = (BF16 if last else F32, dtype)
-            *dquery, sums = backward_piece(
+            *dquery, piece = backward_piece(
                 queries, grads, raw, logsum, dquery, keys, piece_sums, index, pieces, crops, dtypes
             )
-            piece_sums = [sums]
+            piece_sums = [piece]
+            turn += 1
+        if keys is other:
+            far_sums = piece
     (dquery,) = dquery
-    key_value = (sums + far_sums.astype(F32)).astype(BF16)
+    key_value = (piece + far_sums.astype(F32)).astype(BF16)
+    doutput, key_value = lax.optimization_barrier((doutput, key_value))
+    doutput = jnp.sum(doutput.astype(F32), axis=0)
+    small = jnp.concatenate([sums.reshape(-1), dup_bias[0]])
+    small = jnp.pad(small, (0, small_rows * model - small.shape[0])).reshape(small_rows, model)
+    doutput = jnp.concatenate([doutput, small], axis=0).astype(BF16)
     if split == 1:
-        dquery, key_value = visit([ring], (dquery, key_value))
         moved = to_heads(jnp.concatenate([dquery, key_value], axis=1))
         projections = head_gradient(dquery, key_value, inputs, table)
         near, far = share_halves(projections, 0)
@@ -853,8 +872,10 @@
             lax.psum(product(attn_in, grad, 0, 1).astype(BF16), ("chip", "core")).astype(F32)
             for grad in (dquery, dkey, dvalue)
         ]
-    dquery, dkey, dvalue, blocks = visit([ring], (dquery, dkey, dvalue, blocks))
+    while inputs.busy():
+        visit([inputs], ())
     gathered = Gather(blocks, True)
+    visit([ring], blocks)
     d_part = (
         product(dquery, query_weight, 0, 1)
         + product(dkey, key_weight, 0, 1)
@@ -885,11 +906,9 @@
         visit([ring, gathered], ())
     ends = jnp.sum(ends.astype(F32), axis=0).reshape(-1)[: 3 * model].reshape(3, model)
     ddown_weight, dup_weight = ring.state[2]
-    ddown_weight = ddown_weight.reshape(-1, model)
     if split == 1:
         *projections, doutput_weight, small = final_layout(gathered.pairs, size, table)
         doutput_weight = doutput_weight.reshape(width, model)
-        small = small[:, :, 0, :lines]
     else:
         blocks = jnp.zeros((2, chips) + blocks.shape, F32)
         for step, near, far in gathered.pairs:
@@ -898,10 +917,9 @@
                 block = block[None, None].astype(F32)
                 blocks = lax.dynamic_update_slice(blocks, block, start)
         doutput_weight = blocks[:, :, :-small_rows].reshape(width, model)
-        small = blocks[:, :, -small_rows, :lines]
-    small = jnp.sum(small, axis=0).reshape(-1)
-    dup_bias = small[4 * model :]
-    small = [small[at * model : at * model + model] for at in range(4)]
+        small = blocks[:, :, -small_rows:]
+    small = jnp.sum(small, axis=(0, 1))
+    dup_bias = small[4:].reshape(-1)[: dup_bias.shape[1]]
     return (
         block_output,
         input_grad,

time: 344 us -> 356 us (1.035)
  starting transfers between devices: 62.1 us -> 77 us
  waiting for transfers between devices: 88.4 us -> 97 us
  local copies, waits for them, and re-layouts: 17.6 us -> 11.3 us
  between operations: 6.5 us -> 1.32 us
    ppermute x4, waiting for transfers between devices: 9.14 us -> 22.3 us  [across_heads(): return [part, lax.ppermute(part, 'head', [(0, 1), (1, 0)])]]
    all_to_all x4, waiting for transfers between devices: 22.4 us -> 9.89 us  [to_heads(): return lax.all_to_all(blocks, 'chip', 0, 0, tiled=True)]
    pallas_call x2 -> x6, Pallas kernels: 18.7 us -> 30 us  [the longest x5 18.3 us: add(): pl.pallas_call(functools.partial(add_kernel, [len(parts) for _, parts in...]
    ppermute x28, waiting for transfers between devices: 50.9 us -> 61.6 us  [send(): lax.ppermute(block, 'chip', ring_pairs(direction))]
    pallas_call x1, Pallas kernels: 24.1 us -> 15.3 us  [attention_forward(): pl.pallas_call(functools.partial(forward_kernel, crops, key_step(count)),...]
    convert_element_type x5 -> x1, other arithmetic: 8.71 us -> 1.26 us  [local(): key_value = (piece + far_sums.astype(F32)).astype(BF16)]
    all_to_all x4, starting transfers between devices: 16.6 us -> 22.8 us  [to_heads(): return lax.all_to_all(blocks, 'chip', 0, 0, tiled=True)]
    ppermute x28, starting transfers between devices: 35.1 us -> 41.3 us  [send(): lax.ppermute(block, 'chip', ring_pairs(direction))]
  transfers between devices with their start and end apart: 61 -> 60, of which waited for: 23 -> 27; matrix products, arithmetic and copies ran while one was open for 7% -> 6% of each run, Pallas kernels for 30% -> 25%
where the time goes in v8:
time: 356 us; the launch traced here: 354 us
  Pallas kernels  117 us (33%)
  waiting for transfers between devices  97 us (27%)
  starting transfers between devices  77 us (22%)
  blocking collectives  29.5 us (8%)
  other arithmetic  15 us (4%)
  local copies, waits for them, and re-layouts  11.3 us (3%)
  matrix products  5.66 us (2%)
    ppermute x28, waiting for transfers between devices, send(): lax.ppermute(block, 'chip', ring_pairs(direction))  61.6 us
    ppermute x28, starting transfers between devices, send(): lax.ppermute(block, 'chip', ring_pairs(direction))  41.3 us
    all_to_all x1, blocking collectives, to_heads(): return lax.all_to_all(blocks, 'chip', 0, 0, tiled=True)  29.5 us
    pallas_call x4, Pallas kernels, backward_piece(): pl.pallas_call(functools.partial(backward_kernel, crops, len(before)), gr...  28.6 us
    all_to_all x4, starting transfers between devices, to_heads(): return lax.all_to_all(blocks, 'chip', 0, 0, tiled=True)  22.8 us
    ppermute x4, waiting for transfers between devices, across_heads(): return [part, lax.ppermute(part, 'head', [(0, 1), (1, 0)])]  22.3 us
    pallas_call x5, Pallas kernels, place(): pl.pallas_call(functools.partial(place_kernel, len(pairs)), grid_spec=plt...  20.3 us
    pallas_call x5, Pallas kernels, add(): pl.pallas_call(functools.partial(add_kernel, [len(parts) for _, parts in...  18.3 us
  transfers between devices with their start and end apart: 60, of which 27 were waited for; matrix products, arithmetic and copies ran while one was open for 6% of the time, Pallas kernels for 25%

profile of v8, /device:TPU:0, one launch (start us, length us, event | category | flops | bytes accessed | tf_op | source)
XLA Modules:
  0.0 354.0 jit_solution(7904429338880735318)
XLA Ops:
  0.6 6.0 %project.1 = (bf16[8,208,256]{2,1,0:T(8,128)(2,1)}, bf16[256,1024]{1,0:T(8,128)(2,1)}) custom-call(bf16[256,1024]{1,0:T(8,128)(2,1)} %input_ref.3, s32[1,256]{1,0:T(1,128)} %bitcast.59, s32[32]{0:T(128)} %steps_ref.1, f32[1,1024]{1,0:T(1,128)} %bitcast.54, f32[1,1024]{1,0:T(1,128)} %bitcast.57, f32[1,1024]{1,0:T(1,128)} %bitcast.58, ...), custom_call_target="tpu_custom_call" | custom-call | flops 805306368 | bytes 8388608 | tf_op jit(solution)/shard_map/project/pallas_call | solution.py:91
  6.6 29.5 %all_to_all.30.query_ref.own.refs_1_ = bf16[8,208,256]{2,1,0:T(8,128)(2,1)S(1)} all-to-all(bf16[8,208,256]{2,1,0:T(8,128)(2,1)} %get-tuple-element.140), channel_id=1, replica_groups=mesh['chip'=8,'core'=2,'head'=2] {'chip'}, dimensions={0} | all-to-all | bytes 1703936 | tf_op jit(solution)/shard_map/all_to_all | solution.py:424
  39.4 15.3 %attention_forward.1 = (f32[8,64,256]{2,1,0:T(8,128)}, bf16[8,64,256]{2,1,0:T(8,128)(2,1)}, f32[8,1,256]{2,1,0:T(1,128)}) custom-call(bf16[8,208,256]{2,1,0:T(8,128)(2,1)} %copy-done.1, bf16[8,208,256]{2,1,0:T(8,128)(2,1)} %copy-done.1, bf16[8,208,256]{2,1,0:T(8,128)(2,1)} %copy-done.3), custom_call_target="tpu_custom_call" | custom-call | flops 34359738368 | bytes 4194304 | tf_op jit(solution)/shard_map/attention_forward/pallas_call | solution.py:352
  54.6 3.4 all-to-all-start.1
  58.1 9.4 %all-to-all-done.1 = bf16[8,64,256]{2,1,0:T(8,128)(2,1)S(1)} async-done(((bf16[8,64,256]{2,1,0:T(8,128)(2,1)}), bf16[8,64,256]{2,1,0:T(8,128)(2,1)S(1)}, u32[]{:S(2)}, u32[]{:S(2)}) %all-to-all-start.1) | async-done | bytes 262176 | tf_op jit(solution)/shard_map/all_to_all | solution.py:424
  68.0 1.5 collective-permute-start.5
  72.1 8.5 %collective-permute-done.5.refs_1_ = bf16[256,1024]{1,0:T(8,128)(2,1)S(1)} collective-permute-done((bf16[256,1024]{1,0:T(8,128)(2,1)S(1)}, bf16[256,1024]{1,0:T(8,128)(2,1)S(1)}, u32[]{:S(2)}, u32[]{:S(2)}) %collective-permute-start.5) | collective-permute-done | bytes 524320 | tf_op jit(solution)/shard_map/ppermute | solution.py:451
  83.3 11.7 %mlp.1 = (bf16[256,2048]{1,0:T(8,128)(2,1)}, bf16[256,2048]{1,0:T(8,128)(2,1)}, bf16[256,1024]{1,0:T(8,128)(2,1)}, bf16[256,1024]{1,0:T(8,128)(2,1)}, f32[256,10...) custom-call(s32[17]{0:T(128)} %compare_select_fusion.4.core_ref._.table, ...), custom_call_target="tpu_custom_call" | custom-call | flops 4294967296 | bytes 16777216 | tf_op jit(solution)/shard_map/mlp/pallas_call | solution.py:159
  96.2 1.8 collective-permute-start.10
  99.5 3.5 ring_add.5
  103.1 1.7 collective-permute-start.8
  105.1 4.8 %collective-permute-done.12.refs_1_ = bf16[256,1024]{1,0:T(8,128)(2,1)} collective-permute-done((bf16[256,1024]{1,0:T(8,128)(2,1)}, bf16[256,1024]{1,0:T(8,128)(2,1)}, u32[]{:S(2)}, u32[]{:S(2)}) %collective-permute-start.12) | collective-permute-done | bytes 524320 | tf_op jit(solution)/shard_map/ppermute | solution.py:451
  109.8 4.3 %middle.1 = (f32[256,1024]{1,0:T(8,128)}, bf16[256,1024]{1,0:T(8,128)(2,1)}, bf16[512,256]{1,0:T(8,128)(2,1)}, f32[4,1024]{1,0:T(4,128)}) custom-call(f32[256,1024]{1,0:T(8,128)} %get-tuple-element.150.hidden_ref, bf16[256,1024]{1,0:T(8,128)(2,1)} %grad_ref.3, bf16[256,1024]{1,0:T(8,128)(2,1)} %get-tuple-element.161.refs_0_, ...), custom_call_target="tpu_custom_call" | custom-call | flops 268435456 | bytes 6291456 | tf_op jit(solution)/shard_map/middle/pallas_call | solution.py:220
  114.1 4.6 %all-to-all-start.2 = ((bf16[8,64,256]{2,1,0:T(8,128)(2,1)}), bf16[8,64,256]{2,1,0:T(8,128)(2,1)S(1)}, u32[]{:S(2)}, u32[]{:S(2)}) async-start(bf16[8,64,256]{2,1,0:T(8,128)(2,1)} %bitcast.53), calls=%async_computation.2 | async-start | bytes 524288 | tf_op jit(solution)/shard_map/all_to_all | solution.py:424
  121.9 2.4 collective-permute-done.9.refs_7_
  124.2 3.9 %ring_add.6 = (bf16[256,1024]{1,0:T(8,128)(2,1)}, bf16[256,1024]{1,0:T(8,128)(2,1)}) custom-call(s32[17]{0:T(128)} %compare_select_fusion.4.core_ref._.table, bf16[256,1024]{1,0:T(8,128)(2,1)} %get-tuple-element.151.refs_0_, bf16[256,1024]{1,0:T(8,128)(2,1)} %copy-done.9, bf16[256,2048]{1,0:T(8,128)(2,1)} %get-tuple-element.153.refs_2_.refs_4_.refs_5_, ...), custom_call_target="tpu_custom_call" | custom-call | flops 536870912 | bytes 4194304 | tf_op jit(solution)/shard_map/ring_add/pallas_call | solution.py:581
  131.6 7.1 %attention_backward.4 = (f32[8,64,256]{2,1,0:T(8,128)S(1)}, bf16[8,128,256]{2,1,0:T(8,128)(2,1)S(1)}) custom-call(bf16[8,208,256]{2,1,0:T(8,128)(2,1)S(1)} %copy-done.2, bf16[8,64,256]{2,1,0:T(8,128)(2,1)S(1)} %all-to-all-done.2.grad_ref, f32[8,64,256]{2,1,0:T(8,128)S(1)} %copy-done.5, f32[8,1,256]{2,1,0:T(1,128)S(1)} %copy-done.8, ...), custom_call_target="tpu_custom_call" | custom-call | flops 8589934592 | bytes 4194304 | tf_op jit(solution)/shard_map/attention_backward/pallas_call | solution.py:384
  138.7 4.6 %collective-permute-done.13.refs_4_ = bf16[256,1024]{1,0:T(8,128)(2,1)} collective-permute-done((bf16[256,1024]{1,0:T(8,128)(2,1)}, bf16[256,1024]{1,0:T(8,128)(2,1)}, u32[]{:S(2)}, u32[]{:S(2)}) %collective-permute-start.13) | collective-permute-done | bytes 524320 | tf_op jit(solution)/shard_map/ppermute | solution.py:535
  143.3 1.4 collective-permute-start.20
  144.7 6.0 %collective-permute-done.15.refs_7_ = bf16[256,1024]{1,0:T(8,128)(2,1)} collective-permute-done((bf16[256,1024]{1,0:T(8,128)(2,1)}, bf16[256,1024]{1,0:T(8,128)(2,1)}, u32[]{:S(2)}, u32[]{:S(2)}) %collective-permute-start.15) | collective-permute-done | bytes 524320 | tf_op jit(solution)/shard_map/ppermute | solution.py:492
  150.7 1.4 fusion.23
  153.3 7.1 %attention_backward.5 = (f32[8,64,256]{2,1,0:T(8,128)S(1)}, bf16[8,128,256]{2,1,0:T(8,128)(2,1)S(1)}) custom-call(bf16[8,208,256]{2,1,0:T(8,128)(2,1)S(1)} %copy-done.2, bf16[8,64,256]{2,1,0:T(8,128)(2,1)S(1)} %all-to-all-done.2.grad_ref, f32[8,64,256]{2,1,0:T(8,128)S(1)} %copy-done.5, f32[8,1,256]{2,1,0:T(1,128)S(1)} %copy-done.8, ...), custom_call_target="tpu_custom_call", output_to_operand_aliasing={{1}: (6, {})} | custom-call | flops 8589934592 | bytes 4194304 | tf_op jit(solution)/shard_map/attention_backward/pallas_call | solution.py:384
  161.2 3.9 %ring_add.7 = (bf16[256,1024]{1,0:T(8,128)(2,1)}, bf16[256,1024]{1,0:T(8,128)(2,1)}) custom-call(s32[17]{0:T(128)} %compare_select_fusion.4.core_ref._.table, bf16[256,1024]{1,0:T(8,128)(2,1)} %get-tuple-element.151.refs_0_, bf16[256,1024]{1,0:T(8,128)(2,1)} %copy-done.9, bf16[256,2048]{1,0:T(8,128)(2,1)} %get-tuple-element.153.refs_2_.refs_4_.refs_5_, ...), custom_call_target="tpu_custom_call" | custom-call | flops 536870912 | bytes 4194304 | tf_op jit(solution)/shard_map/ring_add/pallas_call | solution.py:581
  165.1 1.7 collective-permute-start.16
  167.1 5.7 %all-to-all-start.3 = ((bf16[8,32,1024]{2,1,0:T(8,128)(2,1)}), bf16[8,32,1024]{2,1,0:T(8,128)(2,1)}, u32[]{:S(2)}, u32[]{:S(2)}) async-start(bf16[8,32,1024]{2,1,0:T(8,128)(2,1)} %bitcast.49), calls=%async_computation.3 | async-start | bytes 1048576 | tf_op jit(solution)/shard_map/all_to_all | solution.py:424
  173.9 7.2 %attention_backward.6 = (f32[8,64,256]{2,1,0:T(8,128)S(1)}, f32[8,128,256]{2,1,0:T(8,128)S(1)}) custom-call(bf16[8,208,256]{2,1,0:T(8,128)(2,1)S(1)} %copy-done.2, bf16[8,64,256]{2,1,0:T(8,128)(2,1)S(1)} %all-to-all-done.2.grad_ref, f32[8,64,256]{2,1,0:T(8,128)S(1)} %copy-done.5, f32[8,1,256]{2,1,0:T(1,128)S(1)} %copy-done.8, f32[8,64,256]{2,1,0:T(8,128)S(1)} %copy-done.7, ...), custom_call_target="tpu_custom_call" | custom-call | flops 8589934592 | bytes 4194304 | tf_op jit(solution)/shard_map/attention_backward/pallas_call | solution.py:384
  181.1 7.2 %attention_backward.7 = (bf16[8,64,256]{2,1,0:T(8,128)(2,1)S(1)}, f32[8,128,256]{2,1,0:T(8,128)S(1)}) custom-call(bf16[8,208,256]{2,1,0:T(8,128)(2,1)S(1)} %copy-done.2, bf16[8,64,256]{2,1,0:T(8,128)(2,1)S(1)} %all-to-all-done.2.grad_ref, f32[8,64,256]{2,1,0:T(8,128)S(1)} %copy-done.5, f32[8,1,256]{2,1,0:T(1,128)S(1)} %copy-done.8, ...), custom_call_target="tpu_custom_call", output_to_operand_aliasing={{1}: (6, {})} | custom-call | flops 8589934592 | bytes 4194304 | tf_op jit(solution)/shard_map/attention_backward/pallas_call | solution.py:384
  191.0 9.1 %all-to-all-start.4 = ((bf16[8,192,256]{2,1,0:T(8,128)(2,1)}), bf16[8,192,256]{2,1,0:T(8,128)(2,1)S(1)}, u32[]{:S(2)}, u32[]{:S(2)}) async-start(bf16[8,192,256]{2,1,0:T(8,128)(2,1)} %pad_maximum_fusion), calls=%async_computation.4 | async-start | bytes 1572864 | tf_op jit(solution)/shard_map/all_to_all | solution.py:424
  201.1 3.5 ring_add.8
  204.6 2.0 collective-permute-start.21
  206.6 5.7 %head_gradient.1 = bf16[192,1024]{1,0:T(8,128)(2,1)} custom-call(s32[17]{0:T(128)} %compare_select_fusion.4.core_ref._.table, bf16[8,64,256]{2,1,0:T(8,128)(2,1)} %copy-done, bf16[8,128,256]{2,1,0:T(8,128)(2,1)} %copy-done.11, bf16[256,1024]{1,0:T(8,128)(2,1)} %get-tuple-element.142.refs_0_, bf16[256,1024]{1,0:T(8,128)(2,1)} %copy-done.31, ...), custom_call_target="tpu_custom_call" | custom-call | flops 805306368 | bytes 6291456 | tf_op jit(solution)/shard_map/head_gradient/pallas_call | solution.py:665
  212.3 1.7 constant_dynamic-slice_fusion
  217.7 3.3 collective-permute-done.21.refs_4_
  221.0 3.5 ring_add.9.refs_0_
  224.5 5.6 %collective-permute-start.24 = (bf16[256,1024]{1,0:T(8,128)(2,1)}, bf16[256,1024]{1,0:T(8,128)(2,1)}, u32[]{:S(2)}, u32[]{:S(2)}) collective-permute-start(bf16[256,1024]{1,0:T(8,128)(2,1)} %ring_add.9.refs_0_), channel_id=1, source_target_pairs={{0,8},{8,16},{16,24},{24,28},{28,20},{20,12},{12,4},{4,0},{1,9},{9... | collective-permute-start | bytes 1572872 | tf_op jit(solution)/shard_map/ppermute | solution.py:492
  230.1 2.5 collective-permute-start.27
  234.3 1.7 convolution_add_fusion.2
  236.6 9.0 %collective-permute-done.27.refs_1_ = bf16[136,1024]{1,0:T(8,128)(2,1)} collective-permute-done((bf16[136,1024]{1,0:T(8,128)(2,1)}, bf16[136,1024]{1,0:T(8,128)(2,1)}, u32[]{:S(2)}, u32[]{:S(2)}) %collective-permute-start.27) | collective-permute-done | bytes 278560 | tf_op jit(solution)/shard_map/ppermute | solution.py:492
  245.5 2.7 collective-permute-start.30
  248.6 1.7 collective-permute-done.29.refs_8_
  250.3 9.0 %collective-permute-done.30 = bf16[256,1024]{1,0:T(8,128)(2,1)S(1)} collective-permute-done((bf16[256,1024]{1,0:T(8,128)(2,1)S(1)}, bf16[256,1024]{1,0:T(8,128)(2,1)S(1)}, u32[]{:S(2)}, u32[]{:S(2)}) %collective-permute-start.30) | collective-permute-done | bytes 524320 | tf_op jit(solution)/shard_map/ppermute | solution.py:451
  259.3 2.5 collective-permute-start.31
  261.8 2.5 collective-permute-start.35
  266.0 3.9 %all-to-all-start.5 = ((bf16[32,32,128]{2,1,0:T(8,128)(2,1)}), bf16[32,32,128]{2,1,0:T(8,128)(2,1)S(1)}, u32[]{:S(2)}, u32[]{:S(2)}) async-start(bf16[32,32,128]{2,1,0:T(8,128)(2,1)} %broadcast_in_dim.51), calls=%async_computation.5 | async-start | bytes 524288 | tf_op jit(solution)/shard_map/all_to_all | solution.py:898
  270.0 3.4 place.5
  273.4 6.5 %collective-permute-done.35.refs_3_ = bf16[136,1024]{1,0:T(8,128)(2,1)} collective-permute-done((bf16[136,1024]{1,0:T(8,128)(2,1)}, bf16[136,1024]{1,0:T(8,128)(2,1)}, u32[]{:S(2)}, u32[]{:S(2)}) %collective-permute-start.35) | collective-permute-done | bytes 278560 | tf_op jit(solution)/shard_map/ppermute | solution.py:492
  279.9 2.7 collective-permute-start.32
  283.1 2.5 fusion.10
  285.6 7.0 %collective-permute-done.32.refs_3_ = bf16[256,1024]{1,0:T(8,128)(2,1)S(1)} collective-permute-done((bf16[256,1024]{1,0:T(8,128)(2,1)}, bf16[256,1024]{1,0:T(8,128)(2,1)S(1)}, u32[]{:S(2)}, u32[]{:S(2)}) %collective-permute-start.32) | collective-permute-done | bytes 524320 | tf_op jit(solution)/shard_map/ppermute | solution.py:492
  292.7 3.0 collective-permute-start.43
  295.7 2.3 collective-permute-start.39
  298.2 3.1 collective-permute-done.43.refs_5_
  302.6 1.5 collective-permute-done.44.refs_6_
  304.6 4.5 %place.6 = (f32[2048,1024]{1,0:T(8,128)}, f32[1024,2048]{1,0:T(8,128)}) custom-call(s32[17]{0:T(128)} %compare_select_fusion.4.core_ref._.table, f32[2048,1024]{1,0:T(8,128)} %get-tuple-element.222.refs_0_, f32[1024,2048]{1,0:T(8,128)} %get-tuple-element.223.refs_1_, ...), custom_call_target="tpu_custom_call", output_to_operand_aliasing={{0}: (1, {}), {1}: (2, {})} | custom-call | bytes 2097152 | tf_op jit(solution)/shard_map/place/pallas_call | solution.py:612
  309.1 2.1 collective-permute-done.39.refs_2_
  311.2 2.8 collective-permute-done.40.refs_3_
  315.1 2.0 collective-permute-start.50
  317.8 7.2 %collective-permute-done.50.refs_7_ = bf16[136,1024]{1,0:T(8,128)(2,1)} collective-permute-done((bf16[136,1024]{1,0:T(8,128)(2,1)}, bf16[136,1024]{1,0:T(8,128)(2,1)}, u32[]{:S(2)}, u32[]{:S(2)}) %collective-permute-start.50) | collective-permute-done | bytes 278560 | tf_op jit(solution)/shard_map/ppermute | solution.py:492
  325.0 4.5 %place.7 = (f32[2048,1024]{1,0:T(8,128)}, f32[1024,2048]{1,0:T(8,128)}) custom-call(s32[17]{0:T(128)} %compare_select_fusion.4.core_ref._.table, f32[2048,1024]{1,0:T(8,128)} %get-tuple-element.232.refs_0_, f32[1024,2048]{1,0:T(8,128)} %get-tuple-element.233.refs_1_, bf16[256,1024]{1,0:T(8,128)(2,1)} %copy-done.18, ...), custom_call_target="tpu_custom_call", output_to_operand_aliasing={{0}: (1, {}), {1}: (2, {})} | custom-call | bytes 2097152 | tf_op jit(solution)/shard_map/place/pallas_call | solution.py:612
  329.5 2.9 collective-permute-done.47.refs_2_
  332.5 2.7 add_convert_fusion.1
  335.9 4.5 %place.8 = (f32[2048,1024]{1,0:T(8,128)}, f32[1024,2048]{1,0:T(8,128)}) custom-call(s32[17]{0:T(128)} %compare_select_fusion.4.core_ref._.table, f32[2048,1024]{1,0:T(8,128)} %get-tuple-element.247.refs_0_, f32[1024,2048]{1,0:T(8,128)} %get-tuple-element.248.refs_1_, bf16[256,1024]{1,0:T(8,128)(2,1)} %copy-done.22, ...), custom_call_target="tpu_custom_call", output_to_operand_aliasing={{0}: (1, {}), {1}: (2, {})} | custom-call | bytes 2097152 | tf_op jit(solution)/shard_map/place/pallas_call | solution.py:612
  341.1 7.2 %final_layout.1 = (f32[1024,512]{1,0:T(8,128)}, f32[1024,512]{1,0:T(8,128)}, f32[1024,512]{1,0:T(8,128)}, f32[2,8,32,1024]{3,2,1,0:T(8,128)}, f32[2,8,8,1024]{3,2,1,0:T(8,128)}) custom-call(s32[17]{0:T(128)} %compare_select_fusion.4.core_ref._.table, bf16[136,1024]{1,0:T(8,128)(2,1)} %pad_maximum_fusion.1.refs_0_, ...), custom_call_target="tpu_custom_call" | custom-call | tf_op jit(solution)/shard_map/final_layout/pallas_call | solution.py:720
  350.6 3.4 place.9
  (211 shorter events, 41.5 us)
Async XLA Ops:
  36.1 2.4 collective-permute-start.2
  36.1 22.0 %collective-permute-start = (bf16[256,1024]{1,0:T(8,128)(2,1)}, bf16[256,1024]{1,0:T(8,128)(2,1)S(1)}, u32[]{:S(2)}, u32[]{:S(2)}) collective-permute-start(bf16[256,1024]{1,0:T(8,128)(2,1)} %get-tuple-element.142.refs_0_), channel_id=1, source_target_pairs={{0,8},{8,16},{16,24},{24,28},{28,20},{20,12},{12,4},{4,0},{1,9},{9... | collective-permute-start | bytes 1572872 | tf_op jit(solution)/shard_map/ppermute | solution.py:492
  36.9 21.2 %collective-permute-start.1 = (bf16[256,1024]{1,0:T(8,128)(2,1)}, bf16[256,1024]{1,0:T(8,128)(2,1)}, u32[]{:S(2)}, u32[]{:S(2)}) collective-permute-start(bf16[256,1024]{1,0:T(8,128)(2,1)} %get-tuple-element.142.refs_0_), channel_id=1, source_target_pairs={{0,4},{8,0},{16,8},{24,16},{28,24},{20,28},{12,20},{4,12},{1,5},{9... | collective-permute-start | bytes 1572872 | tf_op jit(solution)/shard_map/ppermute | solution.py:492
  54.6 12.9 %all-to-all-start.1 = ((bf16[8,64,256]{2,1,0:T(8,128)(2,1)}), bf16[8,64,256]{2,1,0:T(8,128)(2,1)S(1)}, u32[]{:S(2)}, u32[]{:S(2)}) async-start(bf16[8,64,256]{2,1,0:T(8,128)(2,1)} %get-tuple-element.144), calls=%async_computation.1 | async-start | bytes 524288 | tf_op jit(solution)/shard_map/all_to_all | solution.py:424
  67.5 52.5 %copy-start.16 = (bf16[8,64,256]{2,1,0:T(8,128)(2,1)}, bf16[8,64,256]{2,1,0:T(8,128)(2,1)S(1)}, u32[]{:S(2)}) copy-start(bf16[8,64,256]{2,1,0:T(8,128)(2,1)S(1)} %all-to-all-done.1) | copy-start | bytes 786436
  68.0 12.7 %collective-permute-start.5 = (bf16[256,1024]{1,0:T(8,128)(2,1)S(1)}, bf16[256,1024]{1,0:T(8,128)(2,1)S(1)}, u32[]{:S(2)}, u32[]{:S(2)}) collective-permute-start(bf16[256,1024]{1,0:T(8,128)(2,1)S(1)} %convolution_convert_fusion.refs_0_), channel_id=1, source_target_pairs={{0,1},{1,0},{2,3},{3,2},{4,5},{5,4},{6,7},{7,6},{8,9},{9,8},{10,11... | collective-permute-start | bytes 1572872 | tf_op jit(solution)/shard_map/ppermute | solution.py:451
  69.5 12.5 %collective-permute-start.3 = (bf16[256,1024]{1,0:T(8,128)(2,1)}, bf16[256,1024]{1,0:T(8,128)(2,1)S(1)}, u32[]{:S(2)}, u32[]{:S(2)}) collective-permute-start(bf16[256,1024]{1,0:T(8,128)(2,1)} %copy-done.31), channel_id=1, source_target_pairs={{0,8},{8,16},{16,24},{24,28},{28,20},{20,12},{12,4},{4,0},{1,9},{9... | collective-permute-start | bytes 1572872 | tf_op jit(solution)/shard_map/ppermute | solution.py:492
  70.6 11.9 %collective-permute-start.4 = (bf16[256,1024]{1,0:T(8,128)(2,1)}, bf16[256,1024]{1,0:T(8,128)(2,1)S(1)}, u32[]{:S(2)}, u32[]{:S(2)}) collective-permute-start(bf16[256,1024]{1,0:T(8,128)(2,1)} %collective-permute-done.1.refs_2_), channel_id=1, source_target_pairs={{0,4},{8,0},{16,8},{24,16},{28,24},{20,28},{12,20},{4,12},{1,5},{9... | collective-permute-start | bytes 1572872 | tf_op jit(solution)/shard_map/ppermute | solution.py:492
  95.0 36.5 %copy-start.2 = (bf16[8,208,256]{2,1,0:T(8,128)(2,1)S(1)}, bf16[8,208,256]{2,1,0:T(8,128)(2,1)}, u32[]{:S(2)}) copy-start(bf16[8,208,256]{2,1,0:T(8,128)(2,1)} %copy-done.1) | copy-start | bytes 2555908
  95.0 36.5 %copy-start.4 = (bf16[8,208,256]{2,1,0:T(8,128)(2,1)S(1)}, bf16[8,208,256]{2,1,0:T(8,128)(2,1)}, u32[]{:S(2)}) copy-start(bf16[8,208,256]{2,1,0:T(8,128)(2,1)} %copy-done.3) | copy-start | bytes 2555908
  95.0 3.8 %collective-permute-start.7 = (bf16[256,2048]{1,0:T(8,128)(2,1)}, bf16[256,2048]{1,0:T(8,128)(2,1)}, u32[]{:S(2)}, u32[]{:S(2)}) collective-permute-start(bf16[256,2048]{1,0:T(8,128)(2,1)} %get-tuple-element.154), channel_id=1, source_target_pairs={{0,2},{2,0},{1,3},{3,1},{4,6},{6,4},{5,7},{7,5},{8,10},{10,8},{9,1... | collective-permute-start | bytes 3145736 | tf_op jit(solution)/shard_map/ppermute | solution.py:420
  95.1 3.6 %collective-permute-start.6 = (bf16[256,1024]{1,0:T(8,128)(2,1)}, bf16[256,1024]{1,0:T(8,128)(2,1)S(1)}, u32[]{:S(2)}, u32[]{:S(2)}) collective-permute-start(bf16[256,1024]{1,0:T(8,128)(2,1)} %get-tuple-element.152), channel_id=1, source_target_pairs={{0,2},{2,0},{1,3},{3,1},{4,6},{6,4},{5,7},{7,5},{8,10},{10,8},{9,1... | collective-permute-start | bytes 1572872 | tf_op jit(solution)/shard_map/ppermute | solution.py:420
  95.6 14.2 %collective-permute-start.12 = (bf16[256,1024]{1,0:T(8,128)(2,1)}, bf16[256,1024]{1,0:T(8,128)(2,1)}, u32[]{:S(2)}, u32[]{:S(2)}) collective-permute-start(bf16[256,1024]{1,0:T(8,128)(2,1)} %get-tuple-element.161.refs_0_), channel_id=1, source_target_pairs={{0,1},{1,0},{2,3},{3,2},{4,5},{5,4},{6,7},{7,6},{8,9},{9,8},{10,11... | collective-permute-start | bytes 1572872 | tf_op jit(solution)/shard_map/ppermute | solution.py:451
  96.2 24.5 %collective-permute-start.10 = (bf16[256,1024]{1,0:T(8,128)(2,1)}, bf16[256,1024]{1,0:T(8,128)(2,1)}, u32[]{:S(2)}, u32[]{:S(2)}) collective-permute-start(bf16[256,1024]{1,0:T(8,128)(2,1)} %copy-done.32), channel_id=1, source_target_pairs={{0,8},{8,16},{16,24},{24,28},{28,20},{20,12},{12,4},{4,0},{1,9},{9... | collective-permute-start | bytes 1572872 | tf_op jit(solution)/shard_map/ppermute | solution.py:492
  98.0 22.7 %collective-permute-start.11 = (bf16[256,1024]{1,0:T(8,128)(2,1)}, bf16[256,1024]{1,0:T(8,128)(2,1)}, u32[]{:S(2)}, u32[]{:S(2)}) collective-permute-start(bf16[256,1024]{1,0:T(8,128)(2,1)} %copy-done.33), channel_id=1, source_target_pairs={{0,4},{8,0},{16,8},{24,16},{28,24},{20,28},{12,20},{4,12},{1,5},{9... | collective-permute-start | bytes 1572872 | tf_op jit(solution)/shard_map/ppermute | solution.py:492
  103.1 18.8 %collective-permute-start.8 = (bf16[256,1024]{1,0:T(8,128)(2,1)}, bf16[256,1024]{1,0:T(8,128)(2,1)}, u32[]{:S(2)}, u32[]{:S(2)}) collective-permute-start(bf16[256,1024]{1,0:T(8,128)(2,1)} %get-tuple-element.155), channel_id=1, source_target_pairs={{0,8},{8,16},{16,24},{24,28},{28,20},{20,12},{12,4},{4,0},{1,9},{9... | collective-permute-start | bytes 1572872 | tf_op jit(solution)/shard_map/ppermute | solution.py:535
  104.8 19.4 %collective-permute-start.9 = (bf16[256,1024]{1,0:T(8,128)(2,1)}, bf16[256,1024]{1,0:T(8,128)(2,1)}, u32[]{:S(2)}, u32[]{:S(2)}) collective-permute-start(bf16[256,1024]{1,0:T(8,128)(2,1)} %get-tuple-element.156), channel_id=1, source_target_pairs={{0,4},{8,0},{16,8},{24,16},{28,24},{20,28},{12,20},{4,12},{1,5},{9... | collective-permute-start | bytes 1572872 | tf_op jit(solution)/shard_map/ppermute | solution.py:535
  114.1 17.4 %all-to-all-start.2 = ((bf16[8,64,256]{2,1,0:T(8,128)(2,1)}), bf16[8,64,256]{2,1,0:T(8,128)(2,1)S(1)}, u32[]{:S(2)}, u32[]{:S(2)}) async-start(bf16[8,64,256]{2,1,0:T(8,128)(2,1)} %bitcast.53), calls=%async_computation.2 | async-start | bytes 524288 | tf_op jit(solution)/shard_map/all_to_all | solution.py:424
  120.7 30.1 %collective-permute-start.18 = (bf16[256,256]{1,0:T(8,128)(2,1)}, bf16[256,256]{1,0:T(8,128)(2,1)}, u32[]{:S(2)}, u32[]{:S(2)}) collective-permute-start(bf16[256,256]{1,0:T(8,128)(2,1)} %constant_dynamic-slice_fusion.1), channel_id=1, source_target_pairs={{0,2},{2,0},{1,3},{3,1},{4,6},{6,4},{5,7},{7,5},{8,10},{10,8},{9,1... | collective-permute-start | bytes 393224 | tf_op jit(solution)/shard_map/ppermute | solution.py:420
  128.1 15.2 %collective-permute-start.13 = (bf16[256,1024]{1,0:T(8,128)(2,1)}, bf16[256,1024]{1,0:T(8,128)(2,1)}, u32[]{:S(2)}, u32[]{:S(2)}) collective-permute-start(bf16[256,1024]{1,0:T(8,128)(2,1)} %get-tuple-element.166), channel_id=1, source_target_pairs={{0,8},{8,16},{16,24},{24,28},{28,20},{20,12},{12,4},{4,0},{1,9},{9... | collective-permute-start | bytes 1572872 | tf_op jit(solution)/shard_map/ppermute | solution.py:535
  129.5 15.2 %collective-permute-start.14 = (bf16[256,1024]{1,0:T(8,128)(2,1)}, bf16[256,1024]{1,0:T(8,128)(2,1)}, u32[]{:S(2)}, u32[]{:S(2)}) collective-permute-start(bf16[256,1024]{1,0:T(8,128)(2,1)} %get-tuple-element.167), channel_id=1, source_target_pairs={{0,4},{8,0},{16,8},{24,16},{28,24},{20,28},{12,20},{4,12},{1,5},{9... | collective-permute-start | bytes 1572872 | tf_op jit(solution)/shard_map/ppermute | solution.py:535
  130.1 20.6 %collective-permute-start.15 = (bf16[256,1024]{1,0:T(8,128)(2,1)}, bf16[256,1024]{1,0:T(8,128)(2,1)}, u32[]{:S(2)}, u32[]{:S(2)}) collective-permute-start(bf16[256,1024]{1,0:T(8,128)(2,1)} %collective-permute-done.10.refs_5_), channel_id=1, source_target_pairs={{0,8},{8,16},{16,24},{24,28},{28,20},{20,12},{12,4},{4,0},{1,9},{9... | collective-permute-start | bytes 1572872 | tf_op jit(solution)/shard_map/ppermute | solution.py:492
  131.5 19.2 %collective-permute-start.19 = (bf16[256,1024]{1,0:T(8,128)(2,1)}, bf16[256,1024]{1,0:T(8,128)(2,1)}, u32[]{:S(2)}, u32[]{:S(2)}) collective-permute-start(bf16[256,1024]{1,0:T(8,128)(2,1)} %get-tuple-element.179), channel_id=1, source_target_pairs={{0,2},{2,0},{1,3},{3,1},{4,6},{6,4},{5,7},{7,5},{8,10},{10,8},{9,1... | collective-permute-start | bytes 1572872 | tf_op jit(solution)/shard_map/ppermute | solution.py:420
  143.3 37.7 %collective-permute-start.20 = (bf16[256,1024]{1,0:T(8,128)(2,1)}, bf16[256,1024]{1,0:T(8,128)(2,1)}, u32[]{:S(2)}, u32[]{:S(2)}) collective-permute-start(bf16[256,1024]{1,0:T(8,128)(2,1)} %get-tuple-element.187), channel_id=1, source_target_pairs={{0,1},{1,0},{2,3},{3,2},{4,5},{5,4},{6,7},{7,6},{8,9},{9,8},{10,11... | collective-permute-start | bytes 1572872 | tf_op jit(solution)/shard_map/ppermute | solution.py:451
  165.1 16.0 %collective-permute-start.16 = (bf16[256,1024]{1,0:T(8,128)(2,1)}, bf16[256,1024]{1,0:T(8,128)(2,1)}, u32[]{:S(2)}, u32[]{:S(2)}) collective-permute-start(bf16[256,1024]{1,0:T(8,128)(2,1)} %get-tuple-element.176), channel_id=1, source_target_pairs={{0,8},{8,16},{16,24},{24,28},{28,20},{20,12},{12,4},{4,0},{1,9},{9... | collective-permute-start | bytes 1572872 | tf_op jit(solution)/shard_map/ppermute | solution.py:535
  166.8 14.2 %collective-permute-start.17 = (bf16[256,1024]{1,0:T(8,128)(2,1)}, bf16[256,1024]{1,0:T(8,128)(2,1)}, u32[]{:S(2)}, u32[]{:S(2)}) collective-permute-start(bf16[256,1024]{1,0:T(8,128)(2,1)} %get-tuple-element.177), channel_id=1, source_target_pairs={{0,4},{8,0},{16,8},{24,16},{28,24},{20,28},{12,20},{4,12},{1,5},{9... | collective-permute-start | bytes 1572872 | tf_op jit(solution)/shard_map/ppermute | solution.py:535
  167.1 21.2 %collective-permute-start.22 = (bf16[8,128,256]{2,1,0:T(8,128)(2,1)S(1)}, bf16[8,128,256]{2,1,0:T(8,128)(2,1)}, u32[]{:S(2)}, u32[]{:S(2)}) collective-permute-start(bf16[8,128,256]{2,1,0:T(8,128)(2,1)S(1)} %get-tuple-element.197), channel_id=1, source_target_pairs={{0,2},{2,0},{1,3},{3,1},{4,6},{6,4},{5,7},{7,5},{8,10},{10,8},{9,1... | collective-permute-start | bytes 1572872 | tf_op jit(solution)/shard_map/ppermute | solution.py:420
  167.1 22.9 %all-to-all-start.3 = ((bf16[8,32,1024]{2,1,0:T(8,128)(2,1)}), bf16[8,32,1024]{2,1,0:T(8,128)(2,1)}, u32[]{:S(2)}, u32[]{:S(2)}) async-start(bf16[8,32,1024]{2,1,0:T(8,128)(2,1)} %bitcast.49), calls=%async_computation.3 | async-start | bytes 1048576 | tf_op jit(solution)/shard_map/all_to_all | solution.py:424
  191.0 42.8 %all-to-all-start.4 = ((bf16[8,192,256]{2,1,0:T(8,128)(2,1)}), bf16[8,192,256]{2,1,0:T(8,128)(2,1)S(1)}, u32[]{:S(2)}, u32[]{:S(2)}) async-start(bf16[8,192,256]{2,1,0:T(8,128)(2,1)} %pad_maximum_fusion), calls=%async_computation.4 | async-start | bytes 1572864 | tf_op jit(solution)/shard_map/all_to_all | solution.py:424
  204.6 16.4 %collective-permute-start.21 = (bf16[256,1024]{1,0:T(8,128)(2,1)}, bf16[256,1024]{1,0:T(8,128)(2,1)}, u32[]{:S(2)}, u32[]{:S(2)}) collective-permute-start(bf16[256,1024]{1,0:T(8,128)(2,1)} %ring_add.8), channel_id=1, source_target_pairs={{0,8},{8,16},{16,24},{24,28},{28,20},{20,12},{12,4},{4,0},{1,9},{9... | collective-permute-start | bytes 1572872 | tf_op jit(solution)/shard_map/ppermute | solution.py:535
  214.1 1.8 collective-permute-start.23
  216.9 47.6 %copy-start.37 = (f32[1024]{0:T(1024)S(1)}, f32[1024]{0:T(1024)}, u32[]{:S(2)}) copy-start(f32[1024]{0:T(1024)} %param.22) | copy-start | bytes 12292
  224.5 25.8 %collective-permute-start.24 = (bf16[256,1024]{1,0:T(8,128)(2,1)}, bf16[256,1024]{1,0:T(8,128)(2,1)}, u32[]{:S(2)}, u32[]{:S(2)}) collective-permute-start(bf16[256,1024]{1,0:T(8,128)(2,1)} %ring_add.9.refs_0_), channel_id=1, source_target_pairs={{0,8},{8,16},{16,24},{24,28},{28,20},{20,12},{12,4},{4,0},{1,9},{9... | collective-permute-start | bytes 1572872 | tf_op jit(solution)/shard_map/ppermute | solution.py:492
  230.1 20.2 %collective-permute-start.25 = (bf16[256,1024]{1,0:T(8,128)(2,1)}, bf16[256,1024]{1,0:T(8,128)(2,1)}, u32[]{:S(2)}, u32[]{:S(2)}) collective-permute-start(bf16[256,1024]{1,0:T(8,128)(2,1)} %ring_add.9.refs_0_), channel_id=1, source_target_pairs={{0,4},{8,0},{16,8},{24,16},{28,24},{20,28},{12,20},{4,12},{1,5},{9... | collective-permute-start | bytes 1572872 | tf_op jit(solution)/shard_map/ppermute | solution.py:492
  230.1 20.2 %collective-permute-start.26 = (bf16[256,1024]{1,0:T(8,128)(2,1)}, bf16[256,1024]{1,0:T(8,128)(2,1)}, u32[]{:S(2)}, u32[]{:S(2)}) collective-permute-start(bf16[256,1024]{1,0:T(8,128)(2,1)} %ring_add.9.refs_0_), channel_id=1, source_target_pairs={{0,2},{2,0},{1,3},{3,1},{4,6},{6,4},{5,7},{7,5},{8,10},{10,8},{9,1... | collective-permute-start | bytes 1572872 | tf_op jit(solution)/shard_map/ppermute | solution.py:420
  230.1 15.4 %collective-permute-start.27 = (bf16[136,1024]{1,0:T(8,128)(2,1)}, bf16[136,1024]{1,0:T(8,128)(2,1)}, u32[]{:S(2)}, u32[]{:S(2)}) collective-permute-start(bf16[136,1024]{1,0:T(8,128)(2,1)} %pad_maximum_fusion.1.refs_0_), channel_id=1, source_target_pairs={{0,8},{8,16},{16,24},{24,28},{28,20},{20,12},{12,4},{4,0},{1,9},{9... | collective-permute-start | bytes 835592 | tf_op jit(solution)/shard_map/ppermute | solution.py:492
  232.6 15.9 %collective-permute-start.28 = (bf16[136,1024]{1,0:T(8,128)(2,1)}, bf16[136,1024]{1,0:T(8,128)(2,1)}, u32[]{:S(2)}, u32[]{:S(2)}) collective-permute-start(bf16[136,1024]{1,0:T(8,128)(2,1)} %pad_maximum_fusion.1.refs_0_), channel_id=1, source_target_pairs={{0,4},{8,0},{16,8},{24,16},{28,24},{20,28},{12,20},{4,12},{1,5},{9... | collective-permute-start | bytes 835592 | tf_op jit(solution)/shard_map/ppermute | solution.py:492
  245.5 13.8 %collective-permute-start.30 = (bf16[256,1024]{1,0:T(8,128)(2,1)S(1)}, bf16[256,1024]{1,0:T(8,128)(2,1)S(1)}, u32[]{:S(2)}, u32[]{:S(2)}) collective-permute-start(bf16[256,1024]{1,0:T(8,128)(2,1)S(1)} %get-tuple-element.214), channel_id=1, source_target_pairs={{0,1},{1,0},{2,3},{3,2},{4,5},{5,4},{6,7},{7,6},{8,9},{9,8},{10,11... | collective-permute-start | bytes 1572872 | tf_op jit(solution)/shard_map/ppermute | solution.py:451
  248.5 1.8 collective-permute-start.29
  259.3 26.3 %collective-permute-start.31 = (bf16[256,1024]{1,0:T(8,128)(2,1)}, bf16[256,1024]{1,0:T(8,128)(2,1)S(1)}, u32[]{:S(2)}, u32[]{:S(2)}) collective-permute-start(bf16[256,1024]{1,0:T(8,128)(2,1)} %collective-permute-done.24.refs_2_), channel_id=1, source_target_pairs={{0,8},{8,16},{16,24},{24,28},{28,20},{20,12},{12,4},{4,0},{1,9},{9... | collective-permute-start | bytes 1572872 | tf_op jit(solution)/shard_map/ppermute | solution.py:492
  261.8 30.9 %collective-permute-start.33 = (bf16[256,1024]{1,0:T(8,128)(2,1)}, bf16[256,1024]{1,0:T(8,128)(2,1)S(1)}, u32[]{:S(2)}, u32[]{:S(2)}) collective-permute-start(bf16[256,1024]{1,0:T(8,128)(2,1)} %collective-permute-done.24.refs_2_), channel_id=1, source_target_pairs={{0,2},{2,0},{1,3},{3,1},{4,6},{6,4},{5,7},{7,5},{8,10},{10,8},{9,1... | collective-permute-start | bytes 1572872 | tf_op jit(solution)/shard_map/ppermute | solution.py:420
  261.8 18.1 %collective-permute-start.35 = (bf16[136,1024]{1,0:T(8,128)(2,1)}, bf16[136,1024]{1,0:T(8,128)(2,1)}, u32[]{:S(2)}, u32[]{:S(2)}) collective-permute-start(bf16[136,1024]{1,0:T(8,128)(2,1)} %collective-permute-done.27.refs_1_), channel_id=1, source_target_pairs={{0,8},{8,16},{16,24},{24,28},{28,20},{20,12},{12,4},{4,0},{1,9},{9... | collective-permute-start | bytes 835592 | tf_op jit(solution)/shard_map/ppermute | solution.py:492
  264.3 18.3 %collective-permute-start.37 = (bf16[136,1024]{1,0:T(8,128)(2,1)}, bf16[136,1024]{1,0:T(8,128)(2,1)}, u32[]{:S(2)}, u32[]{:S(2)}) collective-permute-start(bf16[136,1024]{1,0:T(8,128)(2,1)} %collective-permute-done.27.refs_1_), channel_id=1, source_target_pairs={{0,2},{2,0},{1,3},{3,1},{4,6},{6,4},{5,7},{7,5},{8,10},{10,8},{9,1... | collective-permute-start | bytes 835592 | tf_op jit(solution)/shard_map/ppermute | solution.py:420
  264.5 18.1 %collective-permute-start.36 = (bf16[136,1024]{1,0:T(8,128)(2,1)}, bf16[136,1024]{1,0:T(8,128)(2,1)}, u32[]{:S(2)}, u32[]{:S(2)}) collective-permute-start(bf16[136,1024]{1,0:T(8,128)(2,1)} %collective-permute-done.28.refs_2_), channel_id=1, source_target_pairs={{0,4},{8,0},{16,8},{24,16},{28,24},{20,28},{12,20},{4,12},{1,5},{9... | collective-permute-start | bytes 835592 | tf_op jit(solution)/shard_map/ppermute | solution.py:492
  266.0 19.6 %all-to-all-start.5 = ((bf16[32,32,128]{2,1,0:T(8,128)(2,1)}), bf16[32,32,128]{2,1,0:T(8,128)(2,1)S(1)}, u32[]{:S(2)}, u32[]{:S(2)}) async-start(bf16[32,32,128]{2,1,0:T(8,128)(2,1)} %broadcast_in_dim.51), calls=%async_computation.5 | async-start | bytes 524288 | tf_op jit(solution)/shard_map/all_to_all | solution.py:898
  279.9 12.7 %collective-permute-start.32 = (bf16[256,1024]{1,0:T(8,128)(2,1)}, bf16[256,1024]{1,0:T(8,128)(2,1)S(1)}, u32[]{:S(2)}, u32[]{:S(2)}) collective-permute-start(bf16[256,1024]{1,0:T(8,128)(2,1)} %collective-permute-done.25.refs_3_), channel_id=1, source_target_pairs={{0,4},{8,0},{16,8},{24,16},{28,24},{20,28},{12,20},{4,12},{1,5},{9... | collective-permute-start | bytes 1572872 | tf_op jit(solution)/shard_map/ppermute | solution.py:492
  282.6 10.1 %collective-permute-start.34 = (bf16[256,1024]{1,0:T(8,128)(2,1)}, bf16[256,1024]{1,0:T(8,128)(2,1)}, u32[]{:S(2)}, u32[]{:S(2)}) collective-permute-start(bf16[256,1024]{1,0:T(8,128)(2,1)} %collective-permute-done.25.refs_3_), channel_id=1, source_target_pairs={{0,2},{2,0},{1,3},{3,1},{4,6},{6,4},{5,7},{7,5},{8,10},{10,8},{9,1... | collective-permute-start | bytes 1572872 | tf_op jit(solution)/shard_map/ppermute | solution.py:420
  282.6 3.0 collective-permute-start.38
  292.7 8.7 %collective-permute-start.43 = (bf16[136,1024]{1,0:T(8,128)(2,1)}, bf16[136,1024]{1,0:T(8,128)(2,1)S(1)}, u32[]{:S(2)}, u32[]{:S(2)}) collective-permute-start(bf16[136,1024]{1,0:T(8,128)(2,1)} %collective-permute-done.35.refs_3_), channel_id=1, source_target_pairs={{0,8},{8,16},{16,24},{24,28},{28,20},{20,12},{12,4},{4,0},{1,9},{9... | collective-permute-start | bytes 835592 | tf_op jit(solution)/shard_map/ppermute | solution.py:492
  295.7 8.4 %collective-permute-start.44 = (bf16[136,1024]{1,0:T(8,128)(2,1)}, bf16[136,1024]{1,0:T(8,128)(2,1)}, u32[]{:S(2)}, u32[]{:S(2)}) collective-permute-start(bf16[136,1024]{1,0:T(8,128)(2,1)} %collective-permute-done.36.refs_4_), channel_id=1, source_target_pairs={{0,4},{8,0},{16,8},{24,16},{28,24},{20,28},{12,20},{4,12},{1,5},{9... | collective-permute-start | bytes 835592 | tf_op jit(solution)/shard_map/ppermute | solution.py:492
  295.7 8.4 %collective-permute-start.45 = (bf16[136,1024]{1,0:T(8,128)(2,1)}, bf16[136,1024]{1,0:T(8,128)(2,1)}, u32[]{:S(2)}, u32[]{:S(2)}) collective-permute-start(bf16[136,1024]{1,0:T(8,128)(2,1)} %collective-permute-done.35.refs_3_), channel_id=1, source_target_pairs={{0,2},{2,0},{1,3},{3,1},{4,6},{6,4},{5,7},{7,5},{8,10},{10,8},{9,1... | collective-permute-start | bytes 835592 | tf_op jit(solution)/shard_map/ppermute | solution.py:420
  295.7 15.5 %collective-permute-start.39 = (bf16[256,1024]{1,0:T(8,128)(2,1)S(1)}, bf16[256,1024]{1,0:T(8,128)(2,1)S(1)}, u32[]{:S(2)}, u32[]{:S(2)}) collective-permute-start(bf16[256,1024]{1,0:T(8,128)(2,1)S(1)} %collective-permute-done.31.refs_2_), channel_id=1, source_target_pairs={{0,8},{8,16},{16,24},{24,28},{28,20},{20,12},{12,4},{4,0},{1,9},{9... | collective-permute-start | bytes 1572872 | tf_op jit(solution)/shard_map/ppermute | solution.py:492
  298.0 16.0 %collective-permute-start.41 = (bf16[256,1024]{1,0:T(8,128)(2,1)S(1)}, bf16[256,1024]{1,0:T(8,128)(2,1)S(1)}, u32[]{:S(2)}, u32[]{:S(2)}) collective-permute-start(bf16[256,1024]{1,0:T(8,128)(2,1)S(1)} %collective-permute-done.31.refs_2_), channel_id=1, source_target_pairs={{0,2},{2,0},{1,3},{3,1},{4,6},{6,4},{5,7},{7,5},{8,10},{10,8},{9,1... | collective-permute-start | bytes 1572872 | tf_op jit(solution)/shard_map/ppermute | solution.py:420
  301.3 12.6 %collective-permute-start.40 = (bf16[256,1024]{1,0:T(8,128)(2,1)S(1)}, bf16[256,1024]{1,0:T(8,128)(2,1)S(1)}, u32[]{:S(2)}, u32[]{:S(2)}) collective-permute-start(bf16[256,1024]{1,0:T(8,128)(2,1)S(1)} %collective-permute-done.32.refs_3_), channel_id=1, source_target_pairs={{0,4},{8,0},{16,8},{24,16},{28,24},{20,28},{12,20},{4,12},{1,5},{9... | collective-permute-start | bytes 1572872 | tf_op jit(solution)/shard_map/ppermute | solution.py:492
  304.1 9.9 %collective-permute-start.42 = (bf16[256,1024]{1,0:T(8,128)(2,1)S(1)}, bf16[256,1024]{1,0:T(8,128)(2,1)S(1)}, u32[]{:S(2)}, u32[]{:S(2)}) collective-permute-start(bf16[256,1024]{1,0:T(8,128)(2,1)S(1)} %collective-permute-done.32.refs_3_), channel_id=1, source_target_pairs={{0,2},{2,0},{1,3},{3,1},{4,6},{6,4},{5,7},{7,5},{8,10},{10,8},{9,1... | collective-permute-start | bytes 1572872 | tf_op jit(solution)/shard_map/ppermute | solution.py:420
  304.1 5.0 %collective-permute-start.46 = (bf16[136,1024]{1,0:T(8,128)(2,1)}, bf16[136,1024]{1,0:T(8,128)(2,1)}, u32[]{:S(2)}, u32[]{:S(2)}) collective-permute-start(bf16[136,1024]{1,0:T(8,128)(2,1)} %collective-permute-done.36.refs_4_), channel_id=1, source_target_pairs={{0,2},{2,0},{1,3},{3,1},{4,6},{6,4},{5,7},{7,5},{8,10},{10,8},{9,1... | collective-permute-start | bytes 835592 | tf_op jit(solution)/shard_map/ppermute | solution.py:420
  315.1 9.9 %collective-permute-start.50 = (bf16[136,1024]{1,0:T(8,128)(2,1)}, bf16[136,1024]{1,0:T(8,128)(2,1)}, u32[]{:S(2)}, u32[]{:S(2)}) collective-permute-start(bf16[136,1024]{1,0:T(8,128)(2,1)} %copy-done.35), channel_id=1, source_target_pairs={{0,8},{8,16},{16,24},{24,28},{28,20},{20,12},{12,4},{4,0},{1,9},{9... | collective-permute-start | bytes 835592 | tf_op jit(solution)/shard_map/ppermute | solution.py:492
  317.1 15.3 %collective-permute-start.47 = (bf16[256,1024]{1,0:T(8,128)(2,1)S(1)}, bf16[256,1024]{1,0:T(8,128)(2,1)S(1)}, u32[]{:S(2)}, u32[]{:S(2)}) collective-permute-start(bf16[256,1024]{1,0:T(8,128)(2,1)S(1)} %collective-permute-done.39.refs_2_), channel_id=1, source_target_pairs={{0,8},{8,16},{16,24},{24,28},{28,20},{20,12},{12,4},{4,0},{1,9},{9... | collective-permute-start | bytes 1572872 | tf_op jit(solution)/shard_map/ppermute | solution.py:492
  317.3 15.1 %collective-permute-start.48 = (bf16[256,1024]{1,0:T(8,128)(2,1)S(1)}, bf16[256,1024]{1,0:T(8,128)(2,1)S(1)}, u32[]{:S(2)}, u32[]{:S(2)}) collective-permute-start(bf16[256,1024]{1,0:T(8,128)(2,1)S(1)} %collective-permute-done.39.refs_2_), channel_id=1, source_target_pairs={{0,2},{2,0},{1,3},{3,1},{4,6},{6,4},{5,7},{7,5},{8,10},{10,8},{9,1... | collective-permute-start | bytes 1572872 | tf_op jit(solution)/shard_map/ppermute | solution.py:420
  317.3 15.1 %collective-permute-start.49 = (bf16[256,1024]{1,0:T(8,128)(2,1)}, bf16[256,1024]{1,0:T(8,128)(2,1)S(1)}, u32[]{:S(2)}, u32[]{:S(2)}) collective-permute-start(bf16[256,1024]{1,0:T(8,128)(2,1)} %copy-done.24), channel_id=1, source_target_pairs={{0,2},{2,0},{1,3},{3,1},{4,6},{6,4},{5,7},{7,5},{8,10},{10,8},{9,1... | collective-permute-start | bytes 1572872 | tf_op jit(solution)/shard_map/ppermute | solution.py:420
  317.8 11.7 %collective-permute-start.51 = (bf16[136,1024]{1,0:T(8,128)(2,1)}, bf16[136,1024]{1,0:T(8,128)(2,1)}, u32[]{:S(2)}, u32[]{:S(2)}) collective-permute-start(bf16[136,1024]{1,0:T(8,128)(2,1)} %copy-done.35), channel_id=1, source_target_pairs={{0,2},{2,0},{1,3},{3,1},{4,6},{6,4},{5,7},{7,5},{8,10},{10,8},{9,1... | collective-permute-start | bytes 835592 | tf_op jit(solution)/shard_map/ppermute | solution.py:420
  325.0 4.5 %collective-permute-start.52 = (bf16[136,1024]{1,0:T(8,128)(2,1)}, bf16[136,1024]{1,0:T(8,128)(2,1)}, u32[]{:S(2)}, u32[]{:S(2)}) collective-permute-start(bf16[136,1024]{1,0:T(8,128)(2,1)} %collective-permute-done.44.refs_6_), channel_id=1, source_target_pairs={{0,2},{2,0},{1,3},{3,1},{4,6},{6,4},{5,7},{7,5},{8,10},{10,8},{9,1... | collective-permute-start | bytes 835592 | tf_op jit(solution)/shard_map/ppermute | solution.py:420
  332.4 8.0 %collective-permute-start.53 = (bf16[256,1024]{1,0:T(8,128)(2,1)S(1)}, bf16[256,1024]{1,0:T(8,128)(2,1)S(1)}, u32[]{:S(2)}, u32[]{:S(2)}) collective-permute-start(bf16[256,1024]{1,0:T(8,128)(2,1)S(1)} %collective-permute-done.47.refs_2_), channel_id=1, source_target_pairs={{0,2},{2,0},{1,3},{3,1},{4,6},{6,4},{5,7},{7,5},{8,10},{10,8},{9,1... | collective-permute-start | bytes 1572872 | tf_op jit(solution)/shard_map/ppermute | solution.py:420
  335.2 5.2 %collective-permute-start.54 = (bf16[136,1024]{1,0:T(8,128)(2,1)}, bf16[136,1024]{1,0:T(8,128)(2,1)S(1)}, u32[]{:S(2)}, u32[]{:S(2)}) collective-permute-start(bf16[136,1024]{1,0:T(8,128)(2,1)} %collective-permute-done.50.refs_7_), channel_id=1, source_target_pairs={{0,2},{2,0},{1,3},{3,1},{4,6},{6,4},{5,7},{7,5},{8,10},{10,8},{9,1... | collective-permute-start | bytes 835592 | tf_op jit(solution)/shard_map/ppermute | solution.py:420
  (41 other events, 587.9 us)

commit v9 on v8

--- a/solution.py
+++ b/solution.py
@@ -51,8 +51,7 @@
     return pl.BlockSpec(shape, lambda *at: (0,) * len(shape))
 
 
-def cost(flops, size, exps=0):
-    return pl.CostEstimate(flops=flops, bytes_accessed=size, transcendentals=exps)
+light = pl.CostEstimate(flops=1, bytes_accessed=1, transcendentals=0)
 
 
 def project_kernel(
@@ -100,7 +99,7 @@
         ],
         out_shape=[struct((heads, payload_rows, rows), BF16), struct((rows, model), BF16)],
         compiler_params=streaming,
-        cost_estimate=cost(2 * rows * model * 3 * heads * HD, 8 * 2**20),
+        cost_estimate=light,
         name="project",
     )(block_input, segments[None], lead_steps, gain[None], shift[None], lead_weight[None], *weights)
 
@@ -181,7 +180,7 @@
             struct((rows, model), BF16),
         ],
         compiler_params=streaming,
-        cost_estimate=cost(8 * rows * model * units, 16 * 2**20, 2 * rows * units),
+        cost_estimate=light,
         name="mlp",
     )(
         table,
@@ -226,7 +225,7 @@
             struct((4, model), F32),
         ],
         compiler_params=streaming,
-        cost_estimate=cost(2 * rows * model * width, 6 * 2**20),
+        cost_estimate=light,
         name="middle",
     )(hidden, out_grad, *parts, gain[None], output_weight)
 
@@ -369,9 +368,7 @@
             pltpu.VMEM((patches, count), F32),
         ],
         compiler_params=streaming,
-        cost_estimate=cost(
-            groups * patches * count * 4096, 4 * 2**20, groups * patches * count
-        ),
+        cost_estimate=light,
         name="attention_forward",
     )(queries, own, other)
 
@@ -409,9 +406,7 @@
             pltpu.VMEM((count, 2 * HD), F32),
         ],
         compiler_params=params,
-        cost_estimate=cost(
-            groups * patches * count * 4096, 4 * 2**20, groups * patches * count
-        ),
+        cost_estimate=light,
         name="attention_backward",
     )(queries, grads, raw, logsum, *before, keys, *earlier)
 
@@ -471,8 +466,10 @@
 def visit(streams, values):
     states, values = lax.optimization_barrier(([stream.state for stream in streams], values))
     for stream, state in zip(streams, states):
-        stream.state = state
-        stream.advance()
+        stream.advance(state)
+    ready, values = lax.optimization_barrier(([stream.ready for stream in streams], values))
+    for stream, blocks in zip(streams, ready):
+        stream.send(blocks)
     return values
 
 
@@ -480,29 +477,30 @@
     def __init__(self, block, swap=False, take=None):
         self.chips, self.swap, self.take = lax.axis_size("chip"), swap, take
         self.blocks, self.pairs, self.count = [], [], 0
-        self.state = ([], [], [])
-        self.send([(0, block)], [block, block], [])
-
-    def send(self, new, sides, outputs):
+        self.new, self.outputs = [0], []
+        self.ready = [block]
+
+    def send(self, ready):
+        new = list(zip(self.new, ready))
         self.blocks += new
         self.new = new
         self.count += 1
+        sides = ready if len(ready) > 1 else ready * 2
         reach = (self.chips // 2, (self.chips - 1) // 2)
         flying = [
             lax.ppermute(block, "chip", ring_pairs(direction))
             for block, direction, steps in zip(sides, (1, -1), reach)
             if self.count <= steps
         ]
-        self.state = (flying, [swap_cores(block) for _, block in new] if self.swap else [], outputs)
-
-    def advance(self):
-        arrived, swapped, outputs = self.state
+        self.state = (flying, [swap_cores(block) for block in ready] if self.swap else [], self.outputs)
+
+    def advance(self, state):
+        self.ready, swapped, self.outputs = state
         pairs = [(step, near, far) for (step, near), far in zip(self.new, swapped)]
         self.pairs += pairs
         if self.take and pairs:
-            outputs = self.take(outputs, pairs)
-        new = [(side * self.count, block) for block, side in zip(arrived, (-1, 1))]
-        self.send(new, arrived, outputs)
+            self.outputs = self.take(self.outputs, pairs)
+        self.new = [side * self.count for side in (-1, 1)][: len(self.ready)]
 
     def busy(self):
         return bool(self.state[0] or self.state[1])
@@ -526,36 +524,39 @@
         self.units = keep.shape[1] // self.chips
         self.tiled = self.units % 128 == 0
         self.reach = (self.chips // 2, (self.chips - 1) // 2)
-        self.count, self.gather = 0, None
-        self.send(self.add([(self.reach[0], []), (-self.reach[1], [])]), [])
-
-    def send(self, sides, held):
+        self.count, self.gather, self.held = 0, None, []
+        self.send(self.add([(self.reach[0], []), (-self.reach[1], [])]))
+
+    def send(self, ready):
+        if self.gather:
+            self.gather.send(ready)
+            self.state = self.gather.state
+            return
         self.count += 1
         flying = [
             lax.ppermute(block, "chip", ring_pairs(direction))
-            for block, direction in zip(sides, (1, -1))
+            for block, direction in zip(ready, (1, -1))
         ]
-        self.state = (flying, held)
-
-    def advance(self):
+        self.state = (flying, self.held)
+
+    def advance(self, state):
         if self.gather:
-            self.gather.state = self.state
-            self.gather.advance()
-            self.state = self.gather.state
+            self.gather.advance(state)
+            self.ready = self.gather.ready
             return
-        arrived, held = self.state
+        arrived, self.held = state
         wanted, done = [], self.count == self.reach[0]
         for block, reach, side in zip(arrived, self.reach, (1, -1)):
             left = reach - self.count
-            if left > 0 or done:
-                wanted.append((side * left, [block] + held))
+            if left > 0:
+                wanted.append((side * left, [block]))
+            elif done:
+                wanted.append((0, [block] + self.held))
             else:
-                held = [block]
+                self.held = [block]
+        self.ready = self.add(wanted)
         if done:
-            self.gather = Gather(self.add(wanted)[0], True, self.place)
-            self.state = self.gather.state
-        else:
-            self.send(self.add([(step, parts[:1]) for step, parts in wanted]), held)
+            self.gather = Gather(self.ready[0], True, self.place)
 
     def add(self, wanted):
         (rows, model), units, chips = self.sides[0].shape, self.units, self.chips
@@ -588,7 +589,7 @@
             ),
             out_shape=[struct((units, model), BF16)] * len(wanted),
             compiler_params=streaming,
-            cost_estimate=cost(4 * rows * units * model * len(wanted), 4 * 2**20),
+            cost_estimate=light,
             name="ring_add",
         )(self.table, *arrays)
 
@@ -624,7 +625,7 @@
             out_shape=shapes,
             input_output_aliases={1 + at: at for at in range(len(outputs))},
             compiler_params=streaming,
-            cost_estimate=cost(0, 2 * 2**20),
+            cost_estimate=light,
             name="place",
         )(self.table, *outputs, *[pair[1] for pair in pairs], *[pair[2] for pair in pairs])
 
@@ -676,7 +677,7 @@
         ),
         out_shape=struct((3 * rows, model), BF16),
         compiler_params=streaming,
-        cost_estimate=cost(6 * rows * count * patches * model, 6 * 2**20),
+        cost_estimate=light,
         name="head_gradient",
     )(table, dquery, key_value, *blocks)
 
@@ -736,6 +737,7 @@
             struct((2, count, small_rows, model), F32),
         ],
         compiler_params=streaming,
+        cost_estimate=light,
         name="final_layout",
     )(table, *nears, *fars)
 
@@ -789,6 +791,7 @@
         own = to_heads(jnp.repeat(payload, split, axis=0))
     own, attn_in = lax.optimization_barrier((own, attn_in))
     inputs = Gather(attn_in)
+    inputs.send(inputs.ready)
     raw, out, logsum = attention_forward(queries, own, swap_cores(own), crops)
     other = swap_cores(own)
     attn_out = gather_queries(out, heads, split, rows)
@@ -874,8 +877,9 @@
         ]
     while inputs.busy():
         visit([inputs], ())
+    blocks = visit([ring], blocks)
     gathered = Gather(blocks, True)
-    visit([ring], blocks)
+    gathered.send(gathered.ready)
     d_part = (
         product(dquery, query_weight, 0, 1)
         + product(dkey, key_weight, 0, 1)
@@ -896,12 +900,12 @@
     everyone = ("chip", "core", "head")
     ends = jnp.broadcast_to(ends, (lax.axis_size(everyone),) + ends.shape)
     ends = lax.all_to_all(ends, everyone, 0, 0, tiled=True)
+    visit([ring, gathered], ())
     d_in = visit([ring, gathered], d_in)
     d_in = functools.reduce(jnp.add, (part.astype(F32) for part in d_in))
     input_grad = (d_hidden + normalize_back(d_in * gain_attn, unit_attn, inverse_attn)).astype(
         BF16
     )
-    input_grad, ends = visit([ring, gathered], (input_grad, ends))
     while ring.busy() or gathered.busy():
         visit([ring, gathered], ())
     ends = jnp.sum(ends.astype(F32), axis=0).reshape(-1)[: 3 * model].reshape(3, model)

time: 356 us -> 357 us (level)
  waiting for transfers between devices: 97 us -> 110 us
  starting transfers between devices: 77 us -> 65.3 us
  other arithmetic: 15 us -> 9.72 us
    ppermute x28, waiting for transfers between devices: 61.6 us -> 87 us  [send(): lax.ppermute(block, 'chip', ring_pairs(direction))]
    ppermute x4, waiting for transfers between devices: 22.3 us -> 8.79 us  [across_heads(): return [part, lax.ppermute(part, 'head', [(0, 1), (1, 0)])]]
    ppermute x28, starting transfers between devices: 41.3 us -> 35.1 us  [send(): lax.ppermute(block, 'chip', ring_pairs(direction))]
  transfers between devices with their start and end apart: 60 -> 60, of which waited for: 27 -> 26; matrix products, arithmetic and copies ran while one was open for 6% -> 5% of each run, Pallas kernels for 25% -> 23%
where the time goes in v9:
time: 357 us; the launch traced here: 355 us
  Pallas kernels  119 us (33%)
  waiting for transfers between devices  110 us (31%)
  starting transfers between devices  65.3 us (18%)
  blocking collectives  29.5 us (8%)
  local copies, waits for them, and re-layouts  13.1 us (4%)
  other arithmetic  9.72 us (3%)
  matrix products  6.77 us (2%)
    ppermute x28, waiting for transfers between devices, send(): lax.ppermute(block, 'chip', ring_pairs(direction))  87 us
    ppermute x28, starting transfers between devices, send(): lax.ppermute(block, 'chip', ring_pairs(direction))  35.1 us
    pallas_call x4, Pallas kernels, backward_piece(): pl.pallas_call(functools.partial(backward_kernel, crops, len(before)), gr...  30 us
    all_to_all x1, blocking collectives, to_heads(): return lax.all_to_all(blocks, 'chip', 0, 0, tiled=True)  29.5 us
    pallas_call x5, Pallas kernels, place(): pl.pallas_call(functools.partial(place_kernel, len(pairs)), grid_spec=plt...  20.6 us
    all_to_all x4, starting transfers between devices, to_heads(): return lax.all_to_all(blocks, 'chip', 0, 0, tiled=True)  20 us
    pallas_call x5, Pallas kernels, add(): pl.pallas_call(functools.partial(add_kernel, [len(parts) for _, parts in...  18.4 us
    pallas_call x1, Pallas kernels, attention_forward(): pl.pallas_call(functools.partial(forward_kernel, crops, key_step(count)),...  15.3 us
  transfers between devices with their start and end apart: 60, of which 26 were waited for; matrix products, arithmetic and copies ran while one was open for 5% of the time, Pallas kernels for 23%

profile of v9, /device:TPU:0, one launch (start us, length us, event | category | flops | bytes accessed | tf_op | source)
XLA Modules:
  0.0 355.1 jit_solution(10009544058349361721)
XLA Ops:
  0.7 6.0 %project.1 = (bf16[8,208,256]{2,1,0:T(8,128)(2,1)}, bf16[256,1024]{1,0:T(8,128)(2,1)}) custom-call(bf16[256,1024]{1,0:T(8,128)(2,1)} %input_ref.3, s32[1,256]{1,0:T(1,128)} %bitcast.64, s32[32]{0:T(128)} %steps_ref.1, f32[1,1024]{1,0:T(1,128)} %bitcast.54, f32[1,1024]{1,0:T(1,128)} %bitcast.62, f32[1,1024]{1,0:T(1,128)} %bitcast.63, ...), custom_call_target="tpu_custom_call" | custom-call | flops 1 | bytes 1 | tf_op jit(solution)/shard_map/project/pallas_call | solution.py:90
  6.7 29.5 %all_to_all.30.query_ref.own.refs_1_ = bf16[8,208,256]{2,1,0:T(8,128)(2,1)S(1)} all-to-all(bf16[8,208,256]{2,1,0:T(8,128)(2,1)} %get-tuple-element.174), channel_id=1, replica_groups=mesh['chip'=8,'core'=2,'head'=2] {'chip'}, dimensions={0} | all-to-all | bytes 1703936 | tf_op jit(solution)/shard_map/all_to_all | solution.py:419
  39.4 15.3 %attention_forward.1 = (f32[8,64,256]{2,1,0:T(8,128)}, bf16[8,64,256]{2,1,0:T(8,128)(2,1)}, f32[8,1,256]{2,1,0:T(1,128)}) custom-call(bf16[8,208,256]{2,1,0:T(8,128)(2,1)} %copy-done, bf16[8,208,256]{2,1,0:T(8,128)(2,1)} %copy-done, bf16[8,208,256]{2,1,0:T(8,128)(2,1)} %copy-done.3), custom_call_target="tpu_custom_call" | custom-call | flops 1 | bytes 1 | tf_op jit(solution)/shard_map/attention_forward/pallas_call | solution.py:351
  54.7 3.4 all-to-all-start.1
  58.2 9.4 %all-to-all-done.1 = bf16[8,64,256]{2,1,0:T(8,128)(2,1)S(1)} async-done(((bf16[8,64,256]{2,1,0:T(8,128)(2,1)}), bf16[8,64,256]{2,1,0:T(8,128)(2,1)S(1)}, u32[]{:S(2)}, u32[]{:S(2)}) %all-to-all-start.1) | async-done | bytes 262176 | tf_op jit(solution)/shard_map/all_to_all | solution.py:419
  70.1 1.5 collective-permute-start.5
  72.2 8.1 %collective-permute-done.3.refs_3_ = bf16[256,1024]{1,0:T(8,128)(2,1)} collective-permute-done((bf16[256,1024]{1,0:T(8,128)(2,1)S(1)}, bf16[256,1024]{1,0:T(8,128)(2,1)}, u32[]{:S(2)}, u32[]{:S(2)}) %collective-permute-start.3) | collective-permute-done | bytes 524320 | tf_op jit(solution)/shard_map/ppermute | solution.py:491
  80.8 1.5 collective-permute-done.5.refs_1_
  83.1 11.7 %mlp.1 = (bf16[256,2048]{1,0:T(8,128)(2,1)}, bf16[256,2048]{1,0:T(8,128)(2,1)}, bf16[256,1024]{1,0:T(8,128)(2,1)}, bf16[256,1024]{1,0:T(8,128)(2,1)}, f32[256,10...) custom-call(s32[17]{0:T(128)} %compare_select_fusion.4.core_ref._.table, ...), custom_call_target="tpu_custom_call" | custom-call | flops 1 | bytes 1 | tf_op jit(solution)/shard_map/mlp/pallas_call | solution.py:158
  95.4 1.5 collective-permute-start.12
  97.6 1.3 collective-permute-start.11
  100.0 3.6 %ring_add.5 = (bf16[256,1024]{1,0:T(8,128)(2,1)}, bf16[256,1024]{1,0:T(8,128)(2,1)}) custom-call(s32[17]{0:T(128)} %compare_select_fusion.4.core_ref._.table, bf16[256,1024]{1,0:T(8,128)(2,1)} %get-tuple-element.185.refs_0_, bf16[256,1024]{1,0:T(8,128)(2,1)} %copy-done.11, bf16[256,2048]{1,0:T(8,128)(2,1)} %get-tuple-element.187.refs_2_.refs_4_.refs_5_, ...), custom_call_target="tpu_custom_call" | custom-call | flops 1 | bytes 1 | tf_op jit(solution)/shard_map/ring_add/pallas_call | solution.py:582
  105.6 4.0 %collective-permute-done.12.refs_1_ = bf16[256,1024]{1,0:T(8,128)(2,1)} collective-permute-done((bf16[256,1024]{1,0:T(8,128)(2,1)}, bf16[256,1024]{1,0:T(8,128)(2,1)}, u32[]{:S(2)}, u32[]{:S(2)}) %collective-permute-start.12) | collective-permute-done | bytes 524320 | tf_op jit(solution)/shard_map/ppermute | solution.py:446
  109.6 4.3 %middle.1 = (f32[256,1024]{1,0:T(8,128)}, bf16[256,1024]{1,0:T(8,128)(2,1)}, bf16[512,256]{1,0:T(8,128)(2,1)}, f32[4,1024]{1,0:T(4,128)}) custom-call(f32[256,1024]{1,0:T(8,128)} %get-tuple-element.184.hidden_ref, bf16[256,1024]{1,0:T(8,128)(2,1)} %grad_ref.3, bf16[256,1024]{1,0:T(8,128)(2,1)} %get-tuple-element.195.refs_0_, ...), custom_call_target="tpu_custom_call" | custom-call | flops 1 | bytes 1 | tf_op jit(solution)/shard_map/middle/pallas_call | solution.py:219
  113.9 4.8 %all-to-all-start.2 = ((bf16[8,64,256]{2,1,0:T(8,128)(2,1)}), bf16[8,64,256]{2,1,0:T(8,128)(2,1)S(1)}, u32[]{:S(2)}, u32[]{:S(2)}) async-start(bf16[8,64,256]{2,1,0:T(8,128)(2,1)} %bitcast.53), calls=%async_computation.2 | async-start | bytes 524288 | tf_op jit(solution)/shard_map/all_to_all | solution.py:419
  118.7 4.3 %collective-permute-done.8.refs_4_ = bf16[256,1024]{1,0:T(8,128)(2,1)S(1)} collective-permute-done((bf16[256,1024]{1,0:T(8,128)(2,1)}, bf16[256,1024]{1,0:T(8,128)(2,1)S(1)}, u32[]{:S(2)}, u32[]{:S(2)}) %collective-permute-start.8) | collective-permute-done | bytes 524320 | tf_op jit(solution)/shard_map/ppermute | solution.py:537
  123.8 3.9 %ring_add.6 = (bf16[256,1024]{1,0:T(8,128)(2,1)}, bf16[256,1024]{1,0:T(8,128)(2,1)}) custom-call(s32[17]{0:T(128)} %compare_select_fusion.4.core_ref._.table, bf16[256,1024]{1,0:T(8,128)(2,1)} %get-tuple-element.185.refs_0_, bf16[256,1024]{1,0:T(8,128)(2,1)} %copy-done.11, bf16[256,2048]{1,0:T(8,128)(2,1)} %get-tuple-element.187.refs_2_.refs_4_.refs_5_, ...), custom_call_target="tpu_custom_call" | custom-call | flops 1 | bytes 1 | tf_op jit(solution)/shard_map/ring_add/pallas_call | solution.py:582
  127.7 2.9 collective-permute-start.13
  130.6 2.5 collective-permute-start.15
  134.3 7.8 %attention_backward.4 = (f32[8,64,256]{2,1,0:T(8,128)S(1)}, bf16[8,128,256]{2,1,0:T(8,128)(2,1)}) custom-call(bf16[8,208,256]{2,1,0:T(8,128)(2,1)S(1)} %copy-done.1, bf16[8,64,256]{2,1,0:T(8,128)(2,1)S(1)} %all-to-all-done.2.grad_ref, f32[8,64,256]{2,1,0:T(8,128)S(1)} %copy-done.2, f32[8,1,256]{2,1,0:T(1,128)S(1)} %copy-done.8, ...), custom_call_target="tpu_custom_call" | custom-call | flops 1 | bytes 1 | tf_op jit(solution)/shard_map/attention_backward/pallas_call | solution.py:381
  142.1 1.4 fusion.14
  143.6 7.5 %collective-permute-done.15.refs_7_ = bf16[256,1024]{1,0:T(8,128)(2,1)} collective-permute-done((bf16[256,1024]{1,0:T(8,128)(2,1)}, bf16[256,1024]{1,0:T(8,128)(2,1)}, u32[]{:S(2)}, u32[]{:S(2)}) %collective-permute-start.15) | collective-permute-done | bytes 524320 | tf_op jit(solution)/shard_map/ppermute | solution.py:491
  151.1 3.9 %ring_add.7 = (bf16[256,1024]{1,0:T(8,128)(2,1)}, bf16[256,1024]{1,0:T(8,128)(2,1)}) custom-call(s32[17]{0:T(128)} %compare_select_fusion.4.core_ref._.table, bf16[256,1024]{1,0:T(8,128)(2,1)} %get-tuple-element.185.refs_0_, bf16[256,1024]{1,0:T(8,128)(2,1)} %copy-done.11, bf16[256,2048]{1,0:T(8,128)(2,1)} %get-tuple-element.187.refs_2_.refs_4_.refs_5_, ...), custom_call_target="tpu_custom_call" | custom-call | flops 1 | bytes 1 | tf_op jit(solution)/shard_map/ring_add/pallas_call | solution.py:582
  155.0 2.2 fusion
  157.2 7.8 %attention_backward.5 = (f32[8,64,256]{2,1,0:T(8,128)S(1)}, bf16[8,128,256]{2,1,0:T(8,128)(2,1)}) custom-call(bf16[8,208,256]{2,1,0:T(8,128)(2,1)S(1)} %copy-done.1, bf16[8,64,256]{2,1,0:T(8,128)(2,1)S(1)} %all-to-all-done.2.grad_ref, f32[8,64,256]{2,1,0:T(8,128)S(1)} %copy-done.2, f32[8,1,256]{2,1,0:T(1,128)S(1)} %copy-done.8, ...), custom_call_target="tpu_custom_call", output_to_operand_aliasing={{1}: (6, {})} | custom-call | flops 1 | bytes 1 | tf_op jit(solution)/shard_map/attention_backward/pallas_call | solution.py:381
  165.8 5.4 %all-to-all-start.3 = ((bf16[8,32,1024]{2,1,0:T(8,128)(2,1)}), bf16[8,32,1024]{2,1,0:T(8,128)(2,1)S(1)}, u32[]{:S(2)}, u32[]{:S(2)}) async-start(bf16[8,32,1024]{2,1,0:T(8,128)(2,1)} %bitcast.49), calls=%async_computation.3 | async-start | bytes 1048576 | tf_op jit(solution)/shard_map/all_to_all | solution.py:419
  171.3 2.0 collective-permute-start.16
  174.4 7.2 %attention_backward.6 = (f32[8,64,256]{2,1,0:T(8,128)S(1)}, f32[8,128,256]{2,1,0:T(8,128)S(1)}) custom-call(bf16[8,208,256]{2,1,0:T(8,128)(2,1)S(1)} %copy-done.1, bf16[8,64,256]{2,1,0:T(8,128)(2,1)S(1)} %all-to-all-done.2.grad_ref, f32[8,64,256]{2,1,0:T(8,128)S(1)} %copy-done.2, f32[8,1,256]{2,1,0:T(1,128)S(1)} %copy-done.8, f32[8,64,256]{2,1,0:T(8,128)S(1)} %copy-done.7, ...), custom_call_target="tpu_custom_call" | custom-call | flops 1 | bytes 1 | tf_op jit(solution)/shard_map/attention_backward/pallas_call | solution.py:381
  182.8 6.2 %collective-permute-done.16.refs_4_ = bf16[256,1024]{1,0:T(8,128)(2,1)} collective-permute-done((bf16[256,1024]{1,0:T(8,128)(2,1)}, bf16[256,1024]{1,0:T(8,128)(2,1)}, u32[]{:S(2)}, u32[]{:S(2)}) %collective-permute-start.16) | collective-permute-done | bytes 524320 | tf_op jit(solution)/shard_map/ppermute | solution.py:537
  189.0 2.3 collective-permute-done.17.refs_5_
  191.2 3.4 ring_add.8
  194.6 7.2 %attention_backward.7 = (bf16[8,64,256]{2,1,0:T(8,128)(2,1)S(1)}, f32[8,128,256]{2,1,0:T(8,128)S(1)}) custom-call(bf16[8,208,256]{2,1,0:T(8,128)(2,1)S(1)} %copy-done.1, bf16[8,64,256]{2,1,0:T(8,128)(2,1)S(1)} %all-to-all-done.2.grad_ref, f32[8,64,256]{2,1,0:T(8,128)S(1)} %copy-done.2, f32[8,1,256]{2,1,0:T(1,128)S(1)} %copy-done.8, ...), custom_call_target="tpu_custom_call", output_to_operand_aliasing={{1}: (6, {})} | custom-call | flops 1 | bytes 1 | tf_op jit(solution)/shard_map/attention_backward/pallas_call | solution.py:381
  201.8 1.3 add_convert_fusion.key_value_ref
  204.1 6.4 %all-to-all-start.4 = ((bf16[8,192,256]{2,1,0:T(8,128)(2,1)}), bf16[8,192,256]{2,1,0:T(8,128)(2,1)}, u32[]{:S(2)}, u32[]{:S(2)}) async-start(bf16[8,192,256]{2,1,0:T(8,128)(2,1)} %pad_maximum_fusion), calls=%async_computation.4 | async-start | bytes 1572864 | tf_op jit(solution)/shard_map/all_to_all | solution.py:419
  210.5 2.1 collective-permute-start.21
  212.6 5.7 %head_gradient.1 = bf16[192,1024]{1,0:T(8,128)(2,1)} custom-call(s32[17]{0:T(128)} %compare_select_fusion.4.core_ref._.table, bf16[8,64,256]{2,1,0:T(8,128)(2,1)} %copy-done.5, bf16[8,128,256]{2,1,0:T(8,128)(2,1)} %copy-done.12, bf16[256,1024]{1,0:T(8,128)(2,1)} %get-tuple-element.176.refs_0_, bf16[256,1024]{1,0:T(8,128)(2,1)} %copy-done.29, ...), custom_call_target="tpu_custom_call" | custom-call | flops 1 | bytes 1 | tf_op jit(solution)/shard_map/head_gradient/pallas_call | solution.py:666
  221.9 11.7 %collective-permute-done.21.refs_4_ = bf16[256,1024]{1,0:T(8,128)(2,1)} collective-permute-done((bf16[256,1024]{1,0:T(8,128)(2,1)}, bf16[256,1024]{1,0:T(8,128)(2,1)}, u32[]{:S(2)}, u32[]{:S(2)}) %collective-permute-start.21) | collective-permute-done | bytes 524320 | tf_op jit(solution)/shard_map/ppermute | solution.py:537
  233.5 3.5 ring_add.9.refs_0_
  237.0 5.6 %collective-permute-start.27 = (bf16[136,1024]{1,0:T(8,128)(2,1)S(1)}, bf16[136,1024]{1,0:T(8,128)(2,1)}, u32[]{:S(2)}, u32[]{:S(2)}) collective-permute-start(bf16[136,1024]{1,0:T(8,128)(2,1)S(1)} %pad_maximum_fusion.1.refs_0_), channel_id=1, source_target_pairs={{0,8},{8,16},{16,24},{24,28},{28,20},{20,12},{12,4},{4,0},{1,9},{9... | collective-permute-start | bytes 835592 | tf_op jit(solution)/shard_map/ppermute | solution.py:491
  242.6 2.5 collective-permute-start.24
  246.4 3.4 collective-permute-done.27.refs_1_
  249.8 13.8 %collective-permute-done.28.refs_2_ = bf16[136,1024]{1,0:T(8,128)(2,1)} collective-permute-done((bf16[136,1024]{1,0:T(8,128)(2,1)S(1)}, bf16[136,1024]{1,0:T(8,128)(2,1)}, u32[]{:S(2)}, u32[]{:S(2)}) %collective-permute-start.28) | collective-permute-done | bytes 278560 | tf_op jit(solution)/shard_map/ppermute | solution.py:491
  264.0 1.7 collective-permute-start.35
  268.4 1.7 fusion.23
  270.2 1.7 collective-permute-done.34.refs_3_
  271.9 1.5 collective-permute-done.35.refs_4_
  273.4 1.7 collective-permute-start.31
  275.3 3.4 place.5
  278.8 3.0 collective-permute-done.30.refs_2_
  281.8 5.5 %collective-permute-done.31.refs_3_ = bf16[256,1024]{1,0:T(8,128)(2,1)} collective-permute-done((bf16[256,1024]{1,0:T(8,128)(2,1)}, bf16[256,1024]{1,0:T(8,128)(2,1)}, u32[]{:S(2)}, u32[]{:S(2)}) %collective-permute-start.31) | collective-permute-done | bytes 524320 | tf_op jit(solution)/shard_map/ppermute | solution.py:491
  287.3 2.2 collective-permute-done.38
  289.8 1.7 collective-permute-start.44
  292.4 6.8 %collective-permute-done.43.refs_5_ = bf16[136,1024]{1,0:T(8,128)(2,1)S(1)} collective-permute-done((bf16[136,1024]{1,0:T(8,128)(2,1)}, bf16[136,1024]{1,0:T(8,128)(2,1)S(1)}, u32[]{:S(2)}, u32[]{:S(2)}) %collective-permute-start.43) | collective-permute-done | bytes 278560 | tf_op jit(solution)/shard_map/ppermute | solution.py:491
  300.4 4.6 %place.6 = (f32[2048,1024]{1,0:T(8,128)}, f32[1024,2048]{1,0:T(8,128)}) custom-call(s32[17]{0:T(128)} %compare_select_fusion.4.core_ref._.table, f32[2048,1024]{1,0:T(8,128)} %get-tuple-element.284.refs_0_, f32[1024,2048]{1,0:T(8,128)} %get-tuple-element.285.refs_1_, ...), custom_call_target="tpu_custom_call", output_to_operand_aliasing={{0}: (1, {}), {1}: (2, {})} | custom-call | flops 1 | bytes 1 | tf_op jit(solution)/shard_map/place/pallas_call | solution.py:613
  305.0 4.2 %collective-permute-done.39.refs_2_ = bf16[256,1024]{1,0:T(8,128)(2,1)} collective-permute-done((bf16[256,1024]{1,0:T(8,128)(2,1)}, bf16[256,1024]{1,0:T(8,128)(2,1)}, u32[]{:S(2)}, u32[]{:S(2)}) %collective-permute-start.39) | collective-permute-done | bytes 524320 | tf_op jit(solution)/shard_map/ppermute | solution.py:491
  309.2 1.6 collective-permute-done.40.refs_3_
  311.1 2.2 add_convert_fusion.1
  315.6 4.8 %collective-permute-done.50.refs_7_ = bf16[136,1024]{1,0:T(8,128)(2,1)S(1)} collective-permute-done((bf16[136,1024]{1,0:T(8,128)(2,1)S(1)}, bf16[136,1024]{1,0:T(8,128)(2,1)S(1)}, u32[]{:S(2)}, u32[]{:S(2)}) %collective-permute-start.50) | collective-permute-done | bytes 278560 | tf_op jit(solution)/shard_map/ppermute | solution.py:491
  321.9 3.7 %all-to-all-start.5 = ((bf16[32,32,128]{2,1,0:T(8,128)(2,1)}), bf16[32,32,128]{2,1,0:T(8,128)(2,1)S(1)}, u32[]{:S(2)}, u32[]{:S(2)}) async-start(bf16[32,32,128]{2,1,0:T(8,128)(2,1)} %broadcast_in_dim.51), calls=%async_computation.5 | async-start | bytes 524288 | tf_op jit(solution)/shard_map/all_to_all | solution.py:902
  325.7 4.6 %place.7 = (f32[2048,1024]{1,0:T(8,128)}, f32[1024,2048]{1,0:T(8,128)}) custom-call(s32[17]{0:T(128)} %compare_select_fusion.4.core_ref._.table, f32[2048,1024]{1,0:T(8,128)} %get-tuple-element.298.refs_0_, f32[1024,2048]{1,0:T(8,128)} %get-tuple-element.299.refs_1_, ...), custom_call_target="tpu_custom_call", output_to_operand_aliasing={{0}: (1, {}), {1}: (2, {})} | custom-call | flops 1 | bytes 1 | tf_op jit(solution)/shard_map/place/pallas_call | solution.py:613
  332.9 3.4 all-to-all-done.5
  337.0 4.5 %place.8 = (f32[2048,1024]{1,0:T(8,128)}, f32[1024,2048]{1,0:T(8,128)}) custom-call(s32[17]{0:T(128)} %compare_select_fusion.4.core_ref._.table, f32[2048,1024]{1,0:T(8,128)} %get-tuple-element.315.refs_0_, f32[1024,2048]{1,0:T(8,128)} %get-tuple-element.316.refs_1_, ...), custom_call_target="tpu_custom_call", output_to_operand_aliasing={{0}: (1, {}), {1}: (2, {})} | custom-call | flops 1 | bytes 1 | tf_op jit(solution)/shard_map/place/pallas_call | solution.py:613
  342.2 7.2 %final_layout.1 = (f32[1024,512]{1,0:T(8,128)}, f32[1024,512]{1,0:T(8,128)}, f32[1024,512]{1,0:T(8,128)}, f32[2,8,32,1024]{3,2,1,0:T(8,128)}, f32[2,8,8,1024]{3,2,1,0:T(8,128)}) custom-call(s32[17]{0:T(128)} %compare_select_fusion.4.core_ref._.table, bf16[136,1024]{1,0:T(8,128)(2,1)} %copy-done.22, bf16[136,1024]{1,0:T(8,128)(2,1)} %collective-permute-done.27.refs_1_, ...), custom_call_target="tpu_custom_call" | custom-call | flops 1 | bytes 1 | tf_op jit(solution)/shard_map/final_layout/pallas_call | solution.py:721
  351.7 3.4 place.9
  (211 shorter events, 38.8 us)
Async XLA Ops:
  0.6 69.0 %copy-start.16 = (bf16[512,1024]{1,0:T(8,128)(2,1)S(1)}, bf16[512,1024]{1,0:T(8,128)(2,1)}, u32[]{:S(2)}) copy-start(bf16[512,1024]{1,0:T(8,128)(2,1)} %refs_3_.1) | copy-start | bytes 3145732
  36.1 2.4 collective-permute-start.2
  36.2 22.0 %collective-permute-start = (bf16[256,1024]{1,0:T(8,128)(2,1)}, bf16[256,1024]{1,0:T(8,128)(2,1)S(1)}, u32[]{:S(2)}, u32[]{:S(2)}) collective-permute-start(bf16[256,1024]{1,0:T(8,128)(2,1)} %get-tuple-element.176.refs_0_), channel_id=1, source_target_pairs={{0,8},{8,16},{16,24},{24,28},{28,20},{20,12},{12,4},{4,0},{1,9},{9... | collective-permute-start | bytes 1572872 | tf_op jit(solution)/shard_map/ppermute | solution.py:491
  36.9 21.3 %collective-permute-start.1 = (bf16[256,1024]{1,0:T(8,128)(2,1)}, bf16[256,1024]{1,0:T(8,128)(2,1)S(1)}, u32[]{:S(2)}, u32[]{:S(2)}) collective-permute-start(bf16[256,1024]{1,0:T(8,128)(2,1)} %get-tuple-element.176.refs_0_), channel_id=1, source_target_pairs={{0,4},{8,0},{16,8},{24,16},{28,24},{20,28},{12,20},{4,12},{1,5},{9... | collective-permute-start | bytes 1572872 | tf_op jit(solution)/shard_map/ppermute | solution.py:491
  54.7 12.9 %all-to-all-start.1 = ((bf16[8,64,256]{2,1,0:T(8,128)(2,1)}), bf16[8,64,256]{2,1,0:T(8,128)(2,1)S(1)}, u32[]{:S(2)}, u32[]{:S(2)}) async-start(bf16[8,64,256]{2,1,0:T(8,128)(2,1)} %get-tuple-element.178), calls=%async_computation.1 | async-start | bytes 524288 | tf_op jit(solution)/shard_map/all_to_all | solution.py:419
  67.6 12.7 %collective-permute-start.3 = (bf16[256,1024]{1,0:T(8,128)(2,1)S(1)}, bf16[256,1024]{1,0:T(8,128)(2,1)}, u32[]{:S(2)}, u32[]{:S(2)}) collective-permute-start(bf16[256,1024]{1,0:T(8,128)(2,1)S(1)} %collective-permute-done.refs_1_), channel_id=1, source_target_pairs={{0,8},{8,16},{16,24},{24,28},{28,20},{20,12},{12,4},{4,0},{1,9},{9... | collective-permute-start | bytes 1572872 | tf_op jit(solution)/shard_map/ppermute | solution.py:491
  68.7 12.1 %collective-permute-start.4 = (bf16[256,1024]{1,0:T(8,128)(2,1)S(1)}, bf16[256,1024]{1,0:T(8,128)(2,1)}, u32[]{:S(2)}, u32[]{:S(2)}) collective-permute-start(bf16[256,1024]{1,0:T(8,128)(2,1)S(1)} %collective-permute-done.1.refs_2_), channel_id=1, source_target_pairs={{0,4},{8,0},{16,8},{24,16},{28,24},{20,28},{12,20},{4,12},{1,5},{9... | collective-permute-start | bytes 1572872 | tf_op jit(solution)/shard_map/ppermute | solution.py:491
  70.1 12.1 %collective-permute-start.5 = (bf16[256,1024]{1,0:T(8,128)(2,1)S(1)}, bf16[256,1024]{1,0:T(8,128)(2,1)S(1)}, u32[]{:S(2)}, u32[]{:S(2)}) collective-permute-start(bf16[256,1024]{1,0:T(8,128)(2,1)S(1)} %convolution_convert_fusion.refs_0_), channel_id=1, source_target_pairs={{0,1},{1,0},{2,3},{3,2},{4,5},{5,4},{6,7},{7,6},{8,9},{9,8},{10,11... | collective-permute-start | bytes 1572872 | tf_op jit(solution)/shard_map/ppermute | solution.py:446
  94.8 4.1 %collective-permute-start.7 = (bf16[256,2048]{1,0:T(8,128)(2,1)}, bf16[256,2048]{1,0:T(8,128)(2,1)S(1)}, u32[]{:S(2)}, u32[]{:S(2)}) collective-permute-start(bf16[256,2048]{1,0:T(8,128)(2,1)} %get-tuple-element.188), channel_id=1, source_target_pairs={{0,2},{2,0},{1,3},{3,1},{4,6},{6,4},{5,7},{7,5},{8,10},{10,8},{9,1... | collective-permute-start | bytes 3145736 | tf_op jit(solution)/shard_map/ppermute | solution.py:415
  94.9 4.0 %collective-permute-start.6 = (bf16[256,1024]{1,0:T(8,128)(2,1)}, bf16[256,1024]{1,0:T(8,128)(2,1)S(1)}, u32[]{:S(2)}, u32[]{:S(2)}) collective-permute-start(bf16[256,1024]{1,0:T(8,128)(2,1)} %get-tuple-element.186), channel_id=1, source_target_pairs={{0,2},{2,0},{1,3},{3,1},{4,6},{6,4},{5,7},{7,5},{8,10},{10,8},{9,1... | collective-permute-start | bytes 1572872 | tf_op jit(solution)/shard_map/ppermute | solution.py:415
  95.4 14.2 %collective-permute-start.12 = (bf16[256,1024]{1,0:T(8,128)(2,1)}, bf16[256,1024]{1,0:T(8,128)(2,1)}, u32[]{:S(2)}, u32[]{:S(2)}) collective-permute-start(bf16[256,1024]{1,0:T(8,128)(2,1)} %get-tuple-element.195.refs_0_), channel_id=1, source_target_pairs={{0,1},{1,0},{2,3},{3,2},{4,5},{5,4},{6,7},{7,6},{8,9},{9,8},{10,11... | collective-permute-start | bytes 1572872 | tf_op jit(solution)/shard_map/ppermute | solution.py:446
  96.8 21.8 %collective-permute-start.10 = (bf16[256,1024]{1,0:T(8,128)(2,1)}, bf16[256,1024]{1,0:T(8,128)(2,1)}, u32[]{:S(2)}, u32[]{:S(2)}) collective-permute-start(bf16[256,1024]{1,0:T(8,128)(2,1)} %collective-permute-done.3.refs_3_), channel_id=1, source_target_pairs={{0,8},{8,16},{16,24},{24,28},{28,20},{20,12},{12,4},{4,0},{1,9},{9... | collective-permute-start | bytes 1572872 | tf_op jit(solution)/shard_map/ppermute | solution.py:491
  97.6 21.1 %collective-permute-start.11 = (bf16[256,1024]{1,0:T(8,128)(2,1)}, bf16[256,1024]{1,0:T(8,128)(2,1)}, u32[]{:S(2)}, u32[]{:S(2)}) collective-permute-start(bf16[256,1024]{1,0:T(8,128)(2,1)} %collective-permute-done.4.refs_4_), channel_id=1, source_target_pairs={{0,4},{8,0},{16,8},{24,16},{28,24},{20,28},{12,20},{4,12},{1,5},{9... | collective-permute-start | bytes 1572872 | tf_op jit(solution)/shard_map/ppermute | solution.py:491
  103.6 19.4 %collective-permute-start.8 = (bf16[256,1024]{1,0:T(8,128)(2,1)}, bf16[256,1024]{1,0:T(8,128)(2,1)S(1)}, u32[]{:S(2)}, u32[]{:S(2)}) collective-permute-start(bf16[256,1024]{1,0:T(8,128)(2,1)} %get-tuple-element.189), channel_id=1, source_target_pairs={{0,8},{8,16},{16,24},{24,28},{28,20},{20,12},{12,4},{4,0},{1,9},{9... | collective-permute-start | bytes 1572872 | tf_op jit(solution)/shard_map/ppermute | solution.py:537
  104.3 18.8 %collective-permute-start.9 = (bf16[256,1024]{1,0:T(8,128)(2,1)}, bf16[256,1024]{1,0:T(8,128)(2,1)}, u32[]{:S(2)}, u32[]{:S(2)}) collective-permute-start(bf16[256,1024]{1,0:T(8,128)(2,1)} %get-tuple-element.190), channel_id=1, source_target_pairs={{0,4},{8,0},{16,8},{24,16},{28,24},{20,28},{12,20},{4,12},{1,5},{9... | collective-permute-start | bytes 1572872 | tf_op jit(solution)/shard_map/ppermute | solution.py:537
  113.9 20.4 %all-to-all-start.2 = ((bf16[8,64,256]{2,1,0:T(8,128)(2,1)}), bf16[8,64,256]{2,1,0:T(8,128)(2,1)S(1)}, u32[]{:S(2)}, u32[]{:S(2)}) async-start(bf16[8,64,256]{2,1,0:T(8,128)(2,1)} %bitcast.53), calls=%async_computation.2 | async-start | bytes 524288 | tf_op jit(solution)/shard_map/all_to_all | solution.py:419
  127.7 15.9 %collective-permute-start.13 = (bf16[256,1024]{1,0:T(8,128)(2,1)}, bf16[256,1024]{1,0:T(8,128)(2,1)}, u32[]{:S(2)}, u32[]{:S(2)}) collective-permute-start(bf16[256,1024]{1,0:T(8,128)(2,1)} %get-tuple-element.205), channel_id=1, source_target_pairs={{0,8},{8,16},{16,24},{24,28},{28,20},{20,12},{12,4},{4,0},{1,9},{9... | collective-permute-start | bytes 1572872 | tf_op jit(solution)/shard_map/ppermute | solution.py:537
  130.6 13.0 %collective-permute-start.14 = (bf16[256,1024]{1,0:T(8,128)(2,1)}, bf16[256,1024]{1,0:T(8,128)(2,1)}, u32[]{:S(2)}, u32[]{:S(2)}) collective-permute-start(bf16[256,1024]{1,0:T(8,128)(2,1)} %get-tuple-element.206), channel_id=1, source_target_pairs={{0,4},{8,0},{16,8},{24,16},{28,24},{20,28},{12,20},{4,12},{1,5},{9... | collective-permute-start | bytes 1572872 | tf_op jit(solution)/shard_map/ppermute | solution.py:537
  130.6 20.4 %collective-permute-start.15 = (bf16[256,1024]{1,0:T(8,128)(2,1)}, bf16[256,1024]{1,0:T(8,128)(2,1)}, u32[]{:S(2)}, u32[]{:S(2)}) collective-permute-start(bf16[256,1024]{1,0:T(8,128)(2,1)} %collective-permute-done.10.refs_5_), channel_id=1, source_target_pairs={{0,8},{8,16},{16,24},{24,28},{28,20},{20,12},{12,4},{4,0},{1,9},{9... | collective-permute-start | bytes 1572872 | tf_op jit(solution)/shard_map/ppermute | solution.py:491
  133.1 21.9 %collective-permute-start.19 = (bf16[256,1024]{1,0:T(8,128)(2,1)}, bf16[256,1024]{1,0:T(8,128)(2,1)}, u32[]{:S(2)}, u32[]{:S(2)}) collective-permute-start(bf16[256,1024]{1,0:T(8,128)(2,1)} %get-tuple-element.224), channel_id=1, source_target_pairs={{0,2},{2,0},{1,3},{3,1},{4,6},{6,4},{5,7},{7,5},{8,10},{10,8},{9,1... | collective-permute-start | bytes 1572872 | tf_op jit(solution)/shard_map/ppermute | solution.py:415
  133.8 21.2 %collective-permute-start.18 = (bf16[256,256]{1,0:T(8,128)(2,1)}, bf16[256,256]{1,0:T(8,128)(2,1)}, u32[]{:S(2)}, u32[]{:S(2)}) collective-permute-start(bf16[256,256]{1,0:T(8,128)(2,1)} %constant_dynamic-slice_fusion.1), channel_id=1, source_target_pairs={{0,2},{2,0},{1,3},{3,1},{4,6},{6,4},{5,7},{7,5},{8,10},{10,8},{9,1... | collective-permute-start | bytes 393224 | tf_op jit(solution)/shard_map/ppermute | solution.py:415
  165.8 37.4 %all-to-all-start.3 = ((bf16[8,32,1024]{2,1,0:T(8,128)(2,1)}), bf16[8,32,1024]{2,1,0:T(8,128)(2,1)S(1)}, u32[]{:S(2)}, u32[]{:S(2)}) async-start(bf16[8,32,1024]{2,1,0:T(8,128)(2,1)} %bitcast.49), calls=%async_computation.3 | async-start | bytes 1048576 | tf_op jit(solution)/shard_map/all_to_all | solution.py:419
  171.2 11.6 %collective-permute-start.20 = (bf16[256,1024]{1,0:T(8,128)(2,1)}, bf16[256,1024]{1,0:T(8,128)(2,1)}, u32[]{:S(2)}, u32[]{:S(2)}) collective-permute-start(bf16[256,1024]{1,0:T(8,128)(2,1)} %get-tuple-element.238), channel_id=1, source_target_pairs={{0,1},{1,0},{2,3},{3,2},{4,5},{5,4},{6,7},{7,6},{8,9},{9,8},{10,11... | collective-permute-start | bytes 1572872 | tf_op jit(solution)/shard_map/ppermute | solution.py:446
  171.3 17.7 %collective-permute-start.16 = (bf16[256,1024]{1,0:T(8,128)(2,1)}, bf16[256,1024]{1,0:T(8,128)(2,1)}, u32[]{:S(2)}, u32[]{:S(2)}) collective-permute-start(bf16[256,1024]{1,0:T(8,128)(2,1)} %get-tuple-element.221), channel_id=1, source_target_pairs={{0,8},{8,16},{16,24},{24,28},{28,20},{20,12},{12,4},{4,0},{1,9},{9... | collective-permute-start | bytes 1572872 | tf_op jit(solution)/shard_map/ppermute | solution.py:537
  173.3 18.0 %collective-permute-start.17 = (bf16[256,1024]{1,0:T(8,128)(2,1)}, bf16[256,1024]{1,0:T(8,128)(2,1)}, u32[]{:S(2)}, u32[]{:S(2)}) collective-permute-start(bf16[256,1024]{1,0:T(8,128)(2,1)} %get-tuple-element.222), channel_id=1, source_target_pairs={{0,4},{8,0},{16,8},{24,16},{28,24},{20,28},{12,20},{4,12},{1,5},{9... | collective-permute-start | bytes 1572872 | tf_op jit(solution)/shard_map/ppermute | solution.py:537
  173.4 28.5 %collective-permute-start.22 = (bf16[8,128,256]{2,1,0:T(8,128)(2,1)}, bf16[8,128,256]{2,1,0:T(8,128)(2,1)}, u32[]{:S(2)}, u32[]{:S(2)}) collective-permute-start(bf16[8,128,256]{2,1,0:T(8,128)(2,1)} %get-tuple-element.249), channel_id=1, source_target_pairs={{0,2},{2,0},{1,3},{3,1},{4,6},{6,4},{5,7},{7,5},{8,10},{10,8},{9,1... | collective-permute-start | bytes 1572872 | tf_op jit(solution)/shard_map/ppermute | solution.py:415
  203.2 64.3 %copy-start.13 = (bf16[1024,512]{1,0:T(8,128)(2,1)S(1)}, bf16[1024,512]{1,0:T(8,128)(2,1)}, u32[]{:S(2)}) copy-start(bf16[1024,512]{1,0:T(8,128)(2,1)} %refs_0_.1) | copy-start | bytes 3145732
  204.1 62.1 %all-to-all-start.4 = ((bf16[8,192,256]{2,1,0:T(8,128)(2,1)}), bf16[8,192,256]{2,1,0:T(8,128)(2,1)}, u32[]{:S(2)}, u32[]{:S(2)}) async-start(bf16[8,192,256]{2,1,0:T(8,128)(2,1)} %pad_maximum_fusion), calls=%async_computation.4 | async-start | bytes 1572864 | tf_op jit(solution)/shard_map/all_to_all | solution.py:419
  210.5 23.0 %collective-permute-start.21 = (bf16[256,1024]{1,0:T(8,128)(2,1)}, bf16[256,1024]{1,0:T(8,128)(2,1)}, u32[]{:S(2)}, u32[]{:S(2)}) collective-permute-start(bf16[256,1024]{1,0:T(8,128)(2,1)} %ring_add.8), channel_id=1, source_target_pairs={{0,8},{8,16},{16,24},{24,28},{28,20},{20,12},{12,4},{4,0},{1,9},{9... | collective-permute-start | bytes 1572872 | tf_op jit(solution)/shard_map/ppermute | solution.py:537
  219.3 1.5 collective-permute-start.23
  221.8 69.9 %copy-start.44 = (s32[32]{0:T(128)S(1)}, s32[32]{0:T(128)}, u32[]{:S(2)}) copy-start(s32[32]{0:T(128)} %steps_ref.1) | copy-start | bytes 388
  221.8 78.3 %copy-start.43 = (s32[256]{0:T(256)S(1)}, s32[256]{0:T(256)}, u32[]{:S(2)}) copy-start(s32[256]{0:T(256)} %param.20) | copy-start | bytes 3076
  237.0 12.7 %collective-permute-start.27 = (bf16[136,1024]{1,0:T(8,128)(2,1)S(1)}, bf16[136,1024]{1,0:T(8,128)(2,1)}, u32[]{:S(2)}, u32[]{:S(2)}) collective-permute-start(bf16[136,1024]{1,0:T(8,128)(2,1)S(1)} %pad_maximum_fusion.1.refs_0_), channel_id=1, source_target_pairs={{0,8},{8,16},{16,24},{24,28},{28,20},{20,12},{12,4},{4,0},{1,9},{9... | collective-permute-start | bytes 835592 | tf_op jit(solution)/shard_map/ppermute | solution.py:491
  242.6 21.0 %collective-permute-start.24 = (bf16[256,1024]{1,0:T(8,128)(2,1)}, bf16[256,1024]{1,0:T(8,128)(2,1)}, u32[]{:S(2)}, u32[]{:S(2)}) collective-permute-start(bf16[256,1024]{1,0:T(8,128)(2,1)} %ring_add.9.refs_0_), channel_id=1, source_target_pairs={{0,8},{8,16},{16,24},{24,28},{28,20},{20,12},{12,4},{4,0},{1,9},{9... | collective-permute-start | bytes 1572872 | tf_op jit(solution)/shard_map/ppermute | solution.py:491
  245.1 18.5 %collective-permute-start.25 = (bf16[256,1024]{1,0:T(8,128)(2,1)}, bf16[256,1024]{1,0:T(8,128)(2,1)}, u32[]{:S(2)}, u32[]{:S(2)}) collective-permute-start(bf16[256,1024]{1,0:T(8,128)(2,1)} %ring_add.9.refs_0_), channel_id=1, source_target_pairs={{0,4},{8,0},{16,8},{24,16},{28,24},{20,28},{12,20},{4,12},{1,5},{9... | collective-permute-start | bytes 1572872 | tf_op jit(solution)/shard_map/ppermute | solution.py:491
  245.1 18.5 %collective-permute-start.26 = (bf16[256,1024]{1,0:T(8,128)(2,1)}, bf16[256,1024]{1,0:T(8,128)(2,1)}, u32[]{:S(2)}, u32[]{:S(2)}) collective-permute-start(bf16[256,1024]{1,0:T(8,128)(2,1)} %ring_add.9.refs_0_), channel_id=1, source_target_pairs={{0,2},{2,0},{1,3},{3,1},{4,6},{6,4},{5,7},{7,5},{8,10},{10,8},{9,1... | collective-permute-start | bytes 1572872 | tf_op jit(solution)/shard_map/ppermute | solution.py:415
  245.2 18.4 %collective-permute-start.28 = (bf16[136,1024]{1,0:T(8,128)(2,1)S(1)}, bf16[136,1024]{1,0:T(8,128)(2,1)}, u32[]{:S(2)}, u32[]{:S(2)}) collective-permute-start(bf16[136,1024]{1,0:T(8,128)(2,1)S(1)} %pad_maximum_fusion.1.refs_0_), channel_id=1, source_target_pairs={{0,4},{8,0},{16,8},{24,16},{28,24},{20,28},{12,20},{4,12},{1,5},{9... | collective-permute-start | bytes 835592 | tf_op jit(solution)/shard_map/ppermute | solution.py:491
  249.7 13.9 %collective-permute-start.29 = (bf16[136,1024]{1,0:T(8,128)(2,1)S(1)}, bf16[136,1024]{1,0:T(8,128)(2,1)S(1)}, u32[]{:S(2)}, u32[]{:S(2)}) collective-permute-start(bf16[136,1024]{1,0:T(8,128)(2,1)S(1)} %pad_maximum_fusion.1.refs_0_), channel_id=1, source_target_pairs={{0,2},{2,0},{1,3},{3,1},{4,6},{6,4},{5,7},{7,5},{8,10},{10,8},{9,1... | collective-permute-start | bytes 835592 | tf_op jit(solution)/shard_map/ppermute | solution.py:415
  263.6 8.3 %collective-permute-start.34 = (bf16[136,1024]{1,0:T(8,128)(2,1)}, bf16[136,1024]{1,0:T(8,128)(2,1)}, u32[]{:S(2)}, u32[]{:S(2)}) collective-permute-start(bf16[136,1024]{1,0:T(8,128)(2,1)} %collective-permute-done.27.refs_1_), channel_id=1, source_target_pairs={{0,8},{8,16},{16,24},{24,28},{28,20},{20,12},{12,4},{4,0},{1,9},{9... | collective-permute-start | bytes 835592 | tf_op jit(solution)/shard_map/ppermute | solution.py:491
  264.0 11.1 %collective-permute-start.36 = (bf16[136,1024]{1,0:T(8,128)(2,1)}, bf16[136,1024]{1,0:T(8,128)(2,1)}, u32[]{:S(2)}, u32[]{:S(2)}) collective-permute-start(bf16[136,1024]{1,0:T(8,128)(2,1)} %collective-permute-done.27.refs_1_), channel_id=1, source_target_pairs={{0,2},{2,0},{1,3},{3,1},{4,6},{6,4},{5,7},{7,5},{8,10},{10,8},{9,1... | collective-permute-start | bytes 835592 | tf_op jit(solution)/shard_map/ppermute | solution.py:415
  264.0 9.4 %collective-permute-start.35 = (bf16[136,1024]{1,0:T(8,128)(2,1)}, bf16[136,1024]{1,0:T(8,128)(2,1)}, u32[]{:S(2)}, u32[]{:S(2)}) collective-permute-start(bf16[136,1024]{1,0:T(8,128)(2,1)} %collective-permute-done.28.refs_2_), channel_id=1, source_target_pairs={{0,4},{8,0},{16,8},{24,16},{28,24},{20,28},{12,20},{4,12},{1,5},{9... | collective-permute-start | bytes 835592 | tf_op jit(solution)/shard_map/ppermute | solution.py:491
  265.7 9.4 %collective-permute-start.37 = (bf16[136,1024]{1,0:T(8,128)(2,1)}, bf16[136,1024]{1,0:T(8,128)(2,1)}, u32[]{:S(2)}, u32[]{:S(2)}) collective-permute-start(bf16[136,1024]{1,0:T(8,128)(2,1)} %collective-permute-done.28.refs_2_), channel_id=1, source_target_pairs={{0,2},{2,0},{1,3},{3,1},{4,6},{6,4},{5,7},{7,5},{8,10},{10,8},{9,1... | collective-permute-start | bytes 835592 | tf_op jit(solution)/shard_map/ppermute | solution.py:415
  265.9 15.8 %collective-permute-start.30 = (bf16[256,1024]{1,0:T(8,128)(2,1)}, bf16[256,1024]{1,0:T(8,128)(2,1)}, u32[]{:S(2)}, u32[]{:S(2)}) collective-permute-start(bf16[256,1024]{1,0:T(8,128)(2,1)} %collective-permute-done.24.refs_2_), channel_id=1, source_target_pairs={{0,8},{8,16},{16,24},{24,28},{28,20},{20,12},{12,4},{4,0},{1,9},{9... | collective-permute-start | bytes 1572872 | tf_op jit(solution)/shard_map/ppermute | solution.py:491
  271.9 15.4 %collective-permute-start.32 = (bf16[256,1024]{1,0:T(8,128)(2,1)}, bf16[256,1024]{1,0:T(8,128)(2,1)S(1)}, u32[]{:S(2)}, u32[]{:S(2)}) collective-permute-start(bf16[256,1024]{1,0:T(8,128)(2,1)} %collective-permute-done.24.refs_2_), channel_id=1, source_target_pairs={{0,2},{2,0},{1,3},{3,1},{4,6},{6,4},{5,7},{7,5},{8,10},{10,8},{9,1... | collective-permute-start | bytes 1572872 | tf_op jit(solution)/shard_map/ppermute | solution.py:415
  273.4 13.9 %collective-permute-start.31 = (bf16[256,1024]{1,0:T(8,128)(2,1)}, bf16[256,1024]{1,0:T(8,128)(2,1)}, u32[]{:S(2)}, u32[]{:S(2)}) collective-permute-start(bf16[256,1024]{1,0:T(8,128)(2,1)} %collective-permute-done.25.refs_3_), channel_id=1, source_target_pairs={{0,4},{8,0},{16,8},{24,16},{28,24},{20,28},{12,20},{4,12},{1,5},{9... | collective-permute-start | bytes 1572872 | tf_op jit(solution)/shard_map/ppermute | solution.py:491
  275.1 12.2 %collective-permute-start.33 = (bf16[256,1024]{1,0:T(8,128)(2,1)}, bf16[256,1024]{1,0:T(8,128)(2,1)S(1)}, u32[]{:S(2)}, u32[]{:S(2)}) collective-permute-start(bf16[256,1024]{1,0:T(8,128)(2,1)} %collective-permute-done.25.refs_3_), channel_id=1, source_target_pairs={{0,2},{2,0},{1,3},{3,1},{4,6},{6,4},{5,7},{7,5},{8,10},{10,8},{9,1... | collective-permute-start | bytes 1572872 | tf_op jit(solution)/shard_map/ppermute | solution.py:415
  275.1 14.3 %collective-permute-start.38 = (bf16[256,1024]{1,0:T(8,128)(2,1)S(1)}, bf16[256,1024]{1,0:T(8,128)(2,1)S(1)}, u32[]{:S(2)}, u32[]{:S(2)}) collective-permute-start(bf16[256,1024]{1,0:T(8,128)(2,1)S(1)} %get-tuple-element.278), channel_id=1, source_target_pairs={{0,1},{1,0},{2,3},{3,2},{4,5},{5,4},{6,7},{7,6},{8,9},{9,8},{10,11... | collective-permute-start | bytes 1572872 | tf_op jit(solution)/shard_map/ppermute | solution.py:446
  289.4 9.8 %collective-permute-start.43 = (bf16[136,1024]{1,0:T(8,128)(2,1)}, bf16[136,1024]{1,0:T(8,128)(2,1)S(1)}, u32[]{:S(2)}, u32[]{:S(2)}) collective-permute-start(bf16[136,1024]{1,0:T(8,128)(2,1)} %collective-permute-done.34.refs_3_), channel_id=1, source_target_pairs={{0,8},{8,16},{16,24},{24,28},{28,20},{20,12},{12,4},{4,0},{1,9},{9... | collective-permute-start | bytes 835592 | tf_op jit(solution)/shard_map/ppermute | solution.py:491
  289.8 9.8 %collective-permute-start.44 = (bf16[136,1024]{1,0:T(8,128)(2,1)}, bf16[136,1024]{1,0:T(8,128)(2,1)S(1)}, u32[]{:S(2)}, u32[]{:S(2)}) collective-permute-start(bf16[136,1024]{1,0:T(8,128)(2,1)} %collective-permute-done.35.refs_4_), channel_id=1, source_target_pairs={{0,4},{8,0},{16,8},{24,16},{28,24},{20,28},{12,20},{4,12},{1,5},{9... | collective-permute-start | bytes 835592 | tf_op jit(solution)/shard_map/ppermute | solution.py:491
  291.5 8.1 %collective-permute-start.45 = (bf16[136,1024]{1,0:T(8,128)(2,1)}, bf16[136,1024]{1,0:T(8,128)(2,1)S(1)}, u32[]{:S(2)}, u32[]{:S(2)}) collective-permute-start(bf16[136,1024]{1,0:T(8,128)(2,1)} %collective-permute-done.34.refs_3_), channel_id=1, source_target_pairs={{0,2},{2,0},{1,3},{3,1},{4,6},{6,4},{5,7},{7,5},{8,10},{10,8},{9,1... | collective-permute-start | bytes 835592 | tf_op jit(solution)/shard_map/ppermute | solution.py:415
  291.8 17.4 %collective-permute-start.39 = (bf16[256,1024]{1,0:T(8,128)(2,1)}, bf16[256,1024]{1,0:T(8,128)(2,1)}, u32[]{:S(2)}, u32[]{:S(2)}) collective-permute-start(bf16[256,1024]{1,0:T(8,128)(2,1)} %collective-permute-done.30.refs_2_), channel_id=1, source_target_pairs={{0,8},{8,16},{16,24},{24,28},{28,20},{20,12},{12,4},{4,0},{1,9},{9... | collective-permute-start | bytes 1572872 | tf_op jit(solution)/shard_map/ppermute | solution.py:491
  292.1 18.6 %collective-permute-start.41 = (bf16[256,1024]{1,0:T(8,128)(2,1)}, bf16[256,1024]{1,0:T(8,128)(2,1)}, u32[]{:S(2)}, u32[]{:S(2)}) collective-permute-start(bf16[256,1024]{1,0:T(8,128)(2,1)} %collective-permute-done.30.refs_2_), channel_id=1, source_target_pairs={{0,2},{2,0},{1,3},{3,1},{4,6},{6,4},{5,7},{7,5},{8,10},{10,8},{9,1... | collective-permute-start | bytes 1572872 | tf_op jit(solution)/shard_map/ppermute | solution.py:415
  299.2 11.5 %collective-permute-start.40 = (bf16[256,1024]{1,0:T(8,128)(2,1)}, bf16[256,1024]{1,0:T(8,128)(2,1)}, u32[]{:S(2)}, u32[]{:S(2)}) collective-permute-start(bf16[256,1024]{1,0:T(8,128)(2,1)} %collective-permute-done.31.refs_3_), channel_id=1, source_target_pairs={{0,4},{8,0},{16,8},{24,16},{28,24},{20,28},{12,20},{4,12},{1,5},{9... | collective-permute-start | bytes 1572872 | tf_op jit(solution)/shard_map/ppermute | solution.py:491
  299.6 11.2 %collective-permute-start.42 = (bf16[256,1024]{1,0:T(8,128)(2,1)}, bf16[256,1024]{1,0:T(8,128)(2,1)}, u32[]{:S(2)}, u32[]{:S(2)}) collective-permute-start(bf16[256,1024]{1,0:T(8,128)(2,1)} %collective-permute-done.31.refs_3_), channel_id=1, source_target_pairs={{0,2},{2,0},{1,3},{3,1},{4,6},{6,4},{5,7},{7,5},{8,10},{10,8},{9,1... | collective-permute-start | bytes 1572872 | tf_op jit(solution)/shard_map/ppermute | solution.py:415
  299.6 5.4 %collective-permute-start.46 = (bf16[136,1024]{1,0:T(8,128)(2,1)}, bf16[136,1024]{1,0:T(8,128)(2,1)}, u32[]{:S(2)}, u32[]{:S(2)}) collective-permute-start(bf16[136,1024]{1,0:T(8,128)(2,1)} %collective-permute-done.35.refs_4_), channel_id=1, source_target_pairs={{0,2},{2,0},{1,3},{3,1},{4,6},{6,4},{5,7},{7,5},{8,10},{10,8},{9,1... | collective-permute-start | bytes 835592 | tf_op jit(solution)/shard_map/ppermute | solution.py:415
  310.8 9.6 %collective-permute-start.50 = (bf16[136,1024]{1,0:T(8,128)(2,1)S(1)}, bf16[136,1024]{1,0:T(8,128)(2,1)S(1)}, u32[]{:S(2)}, u32[]{:S(2)}) collective-permute-start(bf16[136,1024]{1,0:T(8,128)(2,1)S(1)} %collective-permute-done.43.refs_5_), channel_id=1, source_target_pairs={{0,8},{8,16},{16,24},{24,28},{28,20},{20,12},{12,4},{4,0},{1,9},{9... | collective-permute-start | bytes 835592 | tf_op jit(solution)/shard_map/ppermute | solution.py:491
  313.3 17.0 %collective-permute-start.47 = (bf16[256,1024]{1,0:T(8,128)(2,1)}, bf16[256,1024]{1,0:T(8,128)(2,1)}, u32[]{:S(2)}, u32[]{:S(2)}) collective-permute-start(bf16[256,1024]{1,0:T(8,128)(2,1)} %collective-permute-done.39.refs_2_), channel_id=1, source_target_pairs={{0,8},{8,16},{16,24},{24,28},{28,20},{20,12},{12,4},{4,0},{1,9},{9... | collective-permute-start | bytes 1572872 | tf_op jit(solution)/shard_map/ppermute | solution.py:491
  314.3 16.0 %collective-permute-start.48 = (bf16[256,1024]{1,0:T(8,128)(2,1)}, bf16[256,1024]{1,0:T(8,128)(2,1)}, u32[]{:S(2)}, u32[]{:S(2)}) collective-permute-start(bf16[256,1024]{1,0:T(8,128)(2,1)} %collective-permute-done.39.refs_2_), channel_id=1, source_target_pairs={{0,2},{2,0},{1,3},{3,1},{4,6},{6,4},{5,7},{7,5},{8,10},{10,8},{9,1... | collective-permute-start | bytes 1572872 | tf_op jit(solution)/shard_map/ppermute | solution.py:415
  314.3 16.0 %collective-permute-start.49 = (bf16[256,1024]{1,0:T(8,128)(2,1)}, bf16[256,1024]{1,0:T(8,128)(2,1)}, u32[]{:S(2)}, u32[]{:S(2)}) collective-permute-start(bf16[256,1024]{1,0:T(8,128)(2,1)} %collective-permute-done.40.refs_3_), channel_id=1, source_target_pairs={{0,2},{2,0},{1,3},{3,1},{4,6},{6,4},{5,7},{7,5},{8,10},{10,8},{9,1... | collective-permute-start | bytes 1572872 | tf_op jit(solution)/shard_map/ppermute | solution.py:415
  315.5 14.8 %collective-permute-start.51 = (bf16[136,1024]{1,0:T(8,128)(2,1)S(1)}, bf16[136,1024]{1,0:T(8,128)(2,1)S(1)}, u32[]{:S(2)}, u32[]{:S(2)}) collective-permute-start(bf16[136,1024]{1,0:T(8,128)(2,1)S(1)} %collective-permute-done.43.refs_5_), channel_id=1, source_target_pairs={{0,2},{2,0},{1,3},{3,1},{4,6},{6,4},{5,7},{7,5},{8,10},{10,8},{9,1... | collective-permute-start | bytes 835592 | tf_op jit(solution)/shard_map/ppermute | solution.py:415
  321.1 9.2 %collective-permute-start.52 = (bf16[136,1024]{1,0:T(8,128)(2,1)}, bf16[136,1024]{1,0:T(8,128)(2,1)S(1)}, u32[]{:S(2)}, u32[]{:S(2)}) collective-permute-start(bf16[136,1024]{1,0:T(8,128)(2,1)} %copy-done.33), channel_id=1, source_target_pairs={{0,2},{2,0},{1,3},{3,1},{4,6},{6,4},{5,7},{7,5},{8,10},{10,8},{9,1... | collective-permute-start | bytes 835592 | tf_op jit(solution)/shard_map/ppermute | solution.py:415
  321.9 14.4 %all-to-all-start.5 = ((bf16[32,32,128]{2,1,0:T(8,128)(2,1)}), bf16[32,32,128]{2,1,0:T(8,128)(2,1)S(1)}, u32[]{:S(2)}, u32[]{:S(2)}) async-start(bf16[32,32,128]{2,1,0:T(8,128)(2,1)} %broadcast_in_dim.51), calls=%async_computation.5 | async-start | bytes 524288 | tf_op jit(solution)/shard_map/all_to_all | solution.py:902
  331.1 10.3 %collective-permute-start.53 = (bf16[256,1024]{1,0:T(8,128)(2,1)}, bf16[256,1024]{1,0:T(8,128)(2,1)S(1)}, u32[]{:S(2)}, u32[]{:S(2)}) collective-permute-start(bf16[256,1024]{1,0:T(8,128)(2,1)} %collective-permute-done.47.refs_2_), channel_id=1, source_target_pairs={{0,2},{2,0},{1,3},{3,1},{4,6},{6,4},{5,7},{7,5},{8,10},{10,8},{9,1... | collective-permute-start | bytes 1572872 | tf_op jit(solution)/shard_map/ppermute | solution.py:415
  332.6 8.8 %collective-permute-start.54 = (bf16[136,1024]{1,0:T(8,128)(2,1)}, bf16[136,1024]{1,0:T(8,128)(2,1)S(1)}, u32[]{:S(2)}, u32[]{:S(2)}) collective-permute-start(bf16[136,1024]{1,0:T(8,128)(2,1)} %copy-done.35), channel_id=1, source_target_pairs={{0,2},{2,0},{1,3},{3,1},{4,6},{6,4},{5,7},{7,5},{8,10},{10,8},{9,1... | collective-permute-start | bytes 835592 | tf_op jit(solution)/shard_map/ppermute | solution.py:415
  (41 other events, 668.0 us)

commit v10 on v9

--- a/solution.py
+++ b/solution.py
@@ -112,7 +112,7 @@
     ]
     mlp_in_ref, forward, back = refs[14:]
     at = pl.program_id(0)
-    is_down = core_ref[core_ref.shape[0] - 1] == 0
+    is_down = core_ref[core_ref.shape[0] - 2] == 0
 
     @pl.when(at == 0)
     def _():
@@ -456,11 +456,12 @@
 def ring_table():
     chips, chip = lax.axis_size("chip"), lax.axis_index("chip")
     place = jnp.where(chip % 2 == 0, chip // 2, chips - 1 - chip // 2)
-    steps = jnp.arange(2 * chips + 1, dtype=jnp.int32)
+    steps = jnp.arange(2 * chips + 2, dtype=jnp.int32)
     places = (place + steps) % chips
     there = jnp.where(places < chips // 2, 2 * places, 2 * (chips - 1 - places) + 1)
     table = jnp.where(steps < chips, places, there)
-    return jnp.where(steps == 2 * chips, lax.axis_index("core"), table).astype(jnp.int32)
+    table = jnp.where(steps == 2 * chips, lax.axis_index("core"), table)
+    return jnp.where(steps == 2 * chips + 1, lax.axis_index("head"), table).astype(jnp.int32)
 
 
 def visit(streams, values):
@@ -475,7 +476,7 @@
 
 class Gather:
     def __init__(self, block, swap=False, take=None):
-        self.chips, self.swap, self.take = lax.axis_size("chip"), swap, take
+        self.reach, self.swap, self.take = lax.axis_size("chip") // 2, swap, take
         self.blocks, self.pairs, self.count = [], [], 0
         self.new, self.outputs = [0], []
         self.ready = [block]
@@ -486,35 +487,48 @@
         self.new = new
         self.count += 1
         sides = ready if len(ready) > 1 else ready * 2
-        reach = (self.chips // 2, (self.chips - 1) // 2)
-        flying = [
-            lax.ppermute(block, "chip", ring_pairs(direction))
-            for block, direction, steps in zip(sides, (1, -1), reach)
-            if self.count <= steps
-        ]
-        self.state = (flying, [swap_cores(block) for block in ready] if self.swap else [], self.outputs)
+        if self.count == self.reach:
+            half = ready[0].shape[1] // 2
+            sides = [sides[0][:, :half], sides[1][:, half:]]
+        flying = []
+        if self.count <= self.reach:
+            flying = [
+                lax.ppermute(block, "chip", ring_pairs(direction))
+                for block, direction in zip(sides, (1, -1))
+            ]
+        swapped = [swap_cores(block) for block in ready] if self.swap else []
+        self.state = (flying, swapped, self.outputs)
 
     def advance(self, state):
-        self.ready, swapped, self.outputs = state
+        arrived, swapped, self.outputs = state
         pairs = [(step, near, far) for (step, near), far in zip(self.new, swapped)]
         self.pairs += pairs
         if self.take and pairs:
             self.outputs = self.take(self.outputs, pairs)
-        self.new = [side * self.count for side in (-1, 1)][: len(self.ready)]
+        self.new = [-self.count, self.count]
+        if arrived and self.count == self.reach:
+            arrived, self.new = [jnp.concatenate(arrived, axis=1)], [self.count]
+        self.ready = arrived
 
     def busy(self):
         return bool(self.state[0] or self.state[1])
 
 
-def add_kernel(counts, _, *refs):
-    outputs, refs = refs[-len(counts) :], list(refs[: -len(counts)])
+def add_kernel(wanted, _, *refs):
+    outputs, refs = refs[-len(wanted) :], list(refs[: -len(wanted)])
     keep_in, far_in = refs.pop(0), refs.pop(0)
-    for count, output in zip(counts, outputs):
+    for starts, output in zip(wanted, outputs):
         near, far = refs.pop(0), refs.pop(0)
         total = product(near[...], keep_in[...], 0, 0) + product(far[...], far_in[...], 0, 0)
-        for _ in range(count):
-            total += refs.pop(0)[...].astype(F32)
         output[...] = total.astype(BF16)
+        arrived = [refs.pop(0) for _ in starts]
+        for start in sorted(set(starts)):
+            parts = [part for part, at in zip(arrived, starts) if at == start]
+            columns = slice(start, start + parts[0].shape[1])
+            summed = total[:, columns]
+            for part in parts:
+                summed += part[...].astype(F32)
+            output[:, columns] = summed.astype(BF16)
 
 
 class Reduce:
@@ -523,39 +537,36 @@
         self.operands, self.sides = (keep, far), (keep_in, far_in)
         self.units = keep.shape[1] // self.chips
         self.tiled = self.units % 128 == 0
-        self.reach = (self.chips // 2, (self.chips - 1) // 2)
-        self.count, self.gather, self.held = 0, None, []
-        self.send(self.add([(self.reach[0], []), (-self.reach[1], [])]))
+        self.left, self.gather = self.chips // 2, None
+        (block,) = self.add([(self.left, [])])
+        half = block.shape[1] // 2
+        self.send([block[:, :half], block[:, half:]])
 
     def send(self, ready):
         if self.gather:
             self.gather.send(ready)
             self.state = self.gather.state
             return
-        self.count += 1
-        flying = [
+        self.left -= 1
+        self.state = [
             lax.ppermute(block, "chip", ring_pairs(direction))
             for block, direction in zip(ready, (1, -1))
         ]
-        self.state = (flying, self.held)
 
     def advance(self, state):
         if self.gather:
             self.gather.advance(state)
             self.ready = self.gather.ready
             return
-        arrived, self.held = state
-        wanted, done = [], self.count == self.reach[0]
-        for block, reach, side in zip(arrived, self.reach, (1, -1)):
-            left = reach - self.count
-            if left > 0:
-                wanted.append((side * left, [block]))
-            elif done:
-                wanted.append((0, [block] + self.held))
-            else:
-                self.held = [block]
+        half = self.sides[0].shape[1] // 2
+        ahead, behind = state
+        first = 0 if ahead.shape[1] != half else half
+        if self.left:
+            wanted = [(self.left, [(ahead, 0)]), (-self.left, [(behind, first)])]
+        else:
+            wanted = [(0, [(ahead, 0), (behind, first)])]
         self.ready = self.add(wanted)
-        if done:
+        if not self.left:
             self.gather = Gather(self.ready[0], True, self.place)
 
     def add(self, wanted):
@@ -564,10 +575,12 @@
             sums = []
             for step, parts in wanted:
                 start = self.table[step % chips] * units
-                total = functools.reduce(jnp.add, (part.astype(F32) for part in parts), 0.0)
+                total = jnp.zeros((units, model), F32)
                 for operand, side in zip(self.operands, self.sides):
                     block = lax.dynamic_slice_in_dim(operand, start, units, 1)
                     total += product(block, side, 0, 0)
+                for part, start in parts:
+                    total = total.at[:, start : start + part.shape[1]].add(part.astype(F32))
                 sums.append(total.astype(BF16))
             return sums
         side = pl.BlockSpec((rows, model), lambda at, table: (0, 0))
@@ -577,10 +590,11 @@
             block = pl.BlockSpec(
                 (rows, units), lambda at, table, step=step % chips: (0, table[step])
             )
-            specs += [block] * 2 + [whole] * len(parts)
-            arrays += list(self.operands) + parts
+            specs += [block] * 2
+            specs += [pl.BlockSpec(part.shape, lambda at, table: (0, 0)) for part, _ in parts]
+            arrays += list(self.operands) + [part for part, _ in parts]
         return pl.pallas_call(
-            functools.partial(add_kernel, [len(parts) for _, parts in wanted]),
+            functools.partial(add_kernel, [[start for _, start in parts] for _, parts in wanted]),
             grid_spec=pltpu.PrefetchScalarGridSpec(
                 num_scalar_prefetch=1,
                 grid=(1,),
@@ -635,7 +649,7 @@
 
 def place_kernel(count, table, *refs):
     nears, fars, (down, up) = refs[-2 - 2 * count : -2 - count], refs[-2 - count : -2], refs[-2:]
-    core = table[table.shape[0] - 1]
+    core = table[table.shape[0] - 2]
 
     def put(first, second):
         down[...] = first[...].astype(F32)
@@ -647,39 +661,45 @@
         pl.when(here & (core != 0))(functools.partial(put, far, near))
 
 
-def head_gradient_kernel(steps, table, query_ref, key_value_ref, *refs):
-    blocks, out_ref = refs[:-1], refs[-1]
-    chips = len(blocks)
-    total = jnp.zeros(out_ref.shape, F32)
-    for step, block in zip(steps, blocks):
-        chip = table[chips + step % chips]
-        grads = jnp.concatenate([query_ref[chip], key_value_ref[chip]], axis=0)
-        total += product(grads, block[...])
-    out_ref[...] = total.astype(BF16)
-
-
-def head_gradient(dquery, key_value, inputs, table):
-    count, rows, patches = dquery.shape
-    steps, blocks = zip(*inputs.blocks)
-    model = blocks[0].shape[1]
-    step = math.gcd(model, 256)
+def head_gradient_kernel(steps, chips, table, query_ref, key_value_ref, *refs):
+    parts, out_ref = refs[:-1], refs[-1]
+    patches = query_ref.shape[2]
+    for at, part in enumerate(parts):
+
+        @pl.when(pl.program_id(0) == at)
+        def _(part=part):
+            total = jnp.zeros(out_ref.shape, F32)
+            for index, step in enumerate(steps):
+                chip = table[chips + step % chips]
+                grads = jnp.concatenate([query_ref[chip], key_value_ref[chip]], axis=0)
+                total += product(grads, part[pl.ds(index * patches, patches), :])
+            out_ref[...] = total.astype(BF16)
+
+
+def head_gradient(dquery, key_value, parts, steps, table):
+    chips, rows, _ = dquery.shape
+    columns = parts[0].shape[1]
+
+    def column(at, table):
+        mine = table[2 * chips + 1] if len(parts) > 1 else 0
+        return (0, jnp.where(at == 0, mine, 1 - mine))
+
     return pl.pallas_call(
-        functools.partial(head_gradient_kernel, steps),
+        functools.partial(head_gradient_kernel, steps, chips),
         grid_spec=pltpu.PrefetchScalarGridSpec(
             num_scalar_prefetch=1,
-            grid=(model // step,),
+            grid=(len(parts),),
             in_specs=[
-                pl.BlockSpec(dquery.shape, lambda at, table: (0, 0, 0)),
-                pl.BlockSpec(key_value.shape, lambda at, table: (0, 0, 0)),
-            ]
-            + [pl.BlockSpec((patches, step), lambda at, table: (0, at))] * count,
-            out_specs=pl.BlockSpec((3 * rows, step), lambda at, table: (0, at)),
+                pl.BlockSpec(array.shape, lambda at, table, rank=array.ndim: (0,) * rank)
+                for array in (dquery, key_value, *parts)
+            ],
+            out_specs=pl.BlockSpec((3 * rows, columns), column),
         ),
-        out_shape=struct((3 * rows, model), BF16),
+        out_shape=struct((3 * rows, columns * len(parts)), BF16),
         compiler_params=streaming,
         cost_estimate=light,
         name="head_gradient",
-    )(table, dquery, key_value, *blocks)
+    )(table, dquery, key_value, *parts)
 
 
 def layout_kernel(steps, size, extra, table, *refs):
@@ -790,10 +810,14 @@
         queries = scatter_queries(payload.reshape(-1, rows), heads, split)
         own = to_heads(jnp.repeat(payload, split, axis=0))
     own, attn_in = lax.optimization_barrier((own, attn_in))
-    inputs = Gather(attn_in)
+    cut = model // 2 if lax.axis_size("head") == 2 else model
+    inputs = Gather(
+        lax.dynamic_slice_in_dim(attn_in, lax.axis_index("head") * cut % model, cut, 1)
+    )
     inputs.send(inputs.ready)
-    raw, out, logsum = attention_forward(queries, own, swap_cores(own), crops)
     other = swap_cores(own)
+    raw, out, logsum = attention_forward(queries, own, other, crops)
+    out = visit([inputs], out)
     attn_out = gather_queries(out, heads, split, rows)
     attn_out = visit([inputs], attn_out)
     branches = across_heads(product(attn_out, output_weight, 0, 0).astype(BF16))
@@ -810,46 +834,41 @@
         up_bias,
         down_weight,
     )
+    keep, give, keep_in, give_in, d_mlp_part = visit(
+        [inputs], (keep, give, keep_in, give_in, d_mlp_part)
+    )
     d_mlp = across_heads(d_mlp_part)
     ring = Reduce(keep, swap_cores(give), keep_in, swap_cores(give_in), table)
-    mlp_part, d_mlp = lax.optimization_barrier((mlp_part, d_mlp))
-    mlp_out = across_heads(mlp_part)
+    while inputs.busy():
+        visit([inputs], ())
+    steps, inputs = zip(*inputs.blocks)
+    inputs = jnp.concatenate(inputs, axis=0)
+    mlp_part, inputs, d_mlp = lax.optimization_barrier((mlp_part, inputs, d_mlp))
+    parts = [inputs]
+    if cut != model:
+        parts = across_heads(inputs)
     d_hidden, d_branch, d_attn, sums = middle(hidden, out_grad, d_mlp, gain_mlp, output_weight)
     grads = scatter_queries(d_attn, heads, split)
-    d_branch = visit([ring, inputs], d_branch)
+    d_branch, mlp_part = visit([ring], (d_branch, mlp_part))
+    mlp_out = across_heads(mlp_part)
     out_near, out_far = share_halves(attn_out, 0)
     doutput = product(out_near, d_branch) + product(out_far, swap_cores(d_branch))
-    doutput = doutput.astype(BF16).reshape(chips, -1, model)
-    pieces = 2
-    dquery, turn = [], 0
-    for keys, dtype in ((other, BF16), (own, F32)):
-        piece_sums = []
-        for index in range(pieces):
-            last = keys is own and index == pieces - 1
-            if turn == 1:
-                grads, dquery, piece_sums = visit([ring, inputs], (grads, dquery, piece_sums))
-            if turn == 2:
-                far_sums = swap_cores(far_sums)
-                doutput, dquery = lax.optimization_barrier((doutput, dquery))
-                doutput = to_heads(doutput)
-            if turn == 3:
-                grads, dquery, piece_sums, mlp_out = visit(
-                    [ring], (grads, dquery, piece_sums, mlp_out)
-                )
-                block_output = hidden + down_bias
-                for part in mlp_out:
-                    block_output += part.astype(F32)
-                block_output = block_output.astype(BF16)
-            dtypes = (BF16 if last else F32, dtype)
-            *dquery, piece = backward_piece(
-                queries, grads, raw, logsum, dquery, keys, piece_sums, index, pieces, crops, dtypes
-            )
-            piece_sums = [piece]
-            turn += 1
-        if keys is other:
-            far_sums = piece
+    doutput = to_heads(doutput.astype(BF16).reshape(chips, -1, model))
+    *dquery, far_sums = backward_piece(
+        queries, grads, raw, logsum, [], other, [], 0, 1, crops, (F32, BF16)
+    )
+    grads, dquery, far_sums = visit([ring], (grads, dquery, far_sums))
+    far_sums = swap_cores(far_sums)
+    *dquery, near_sums = backward_piece(
+        queries, grads, raw, logsum, dquery, own, [], 0, 1, crops, (BF16, F32)
+    )
+    near_sums, dquery, mlp_out = visit([ring], (near_sums, dquery, mlp_out))
+    block_output = hidden + down_bias
+    for part in mlp_out:
+        block_output += part.astype(F32)
+    block_output = block_output.astype(BF16)
     (dquery,) = dquery
-    key_value = (piece + far_sums.astype(F32)).astype(BF16)
+    key_value = (near_sums + far_sums.astype(F32)).astype(BF16)
     doutput, key_value = lax.optimization_barrier((doutput, key_value))
     doutput = jnp.sum(doutput.astype(F32), axis=0)
     small = jnp.concatenate([sums.reshape(-1), dup_bias[0]])
@@ -857,7 +876,7 @@
     doutput = jnp.concatenate([doutput, small], axis=0).astype(BF16)
     if split == 1:
         moved = to_heads(jnp.concatenate([dquery, key_value], axis=1))
-        projections = head_gradient(dquery, key_value, inputs, table)
+        projections = head_gradient(dquery, key_value, parts, steps, table)
         near, far = share_halves(projections, 0)
         projections = (near.astype(F32) + far.astype(F32)).astype(BF16)
         size = projections.shape[0]
@@ -875,16 +894,15 @@
             lax.psum(product(attn_in, grad, 0, 1).astype(BF16), ("chip", "core")).astype(F32)
             for grad in (dquery, dkey, dvalue)
         ]
-    while inputs.busy():
-        visit([inputs], ())
-    blocks = visit([ring], blocks)
     gathered = Gather(blocks, True)
     gathered.send(gathered.ready)
+    visit([ring], blocks)
     d_part = (
         product(dquery, query_weight, 0, 1)
         + product(dkey, key_weight, 0, 1)
         + product(dvalue, value_weight, 0, 1)
     )
+    d_part = visit([ring, gathered], d_part)
     d_in = across_heads(d_part.astype(BF16))
     unit_attn, inverse_attn = normalize(block_input.astype(F32))
     onehot = (segments[:, None] == jnp.arange(crops, dtype=jnp.int32)[None, :]).astype(F32)
@@ -906,14 +924,17 @@
     input_grad = (d_hidden + normalize_back(d_in * gain_attn, unit_attn, inverse_attn)).astype(
         BF16
     )
-    while ring.busy() or gathered.busy():
-        visit([ring, gathered], ())
+    while gathered.busy():
+        visit([gathered], ())
     ends = jnp.sum(ends.astype(F32), axis=0).reshape(-1)[: 3 * model].reshape(3, model)
+    if split == 1:
+        layout = final_layout(gathered.pairs, size, table)
+        *projections, doutput_weight, small = visit([ring], layout)
+        doutput_weight = doutput_weight.reshape(width, model)
+    while ring.busy():
+        visit([ring], ())
     ddown_weight, dup_weight = ring.state[2]
-    if split == 1:
-        *projections, doutput_weight, small = final_layout(gathered.pairs, size, table)
-        doutput_weight = doutput_weight.reshape(width, model)
-    else:
+    if split != 1:
         blocks = jnp.zeros((2, chips) + blocks.shape, F32)
         for step, near, far in gathered.pairs:
             for side, block in ((core, near), (1 - core, far)):

time: 357 us -> 351 us (0.983)
  waiting for transfers between devices: 110 us -> 91.8 us
  local copies, waits for them, and re-layouts: 13.1 us -> 23.8 us
  starting transfers between devices: 65.3 us -> 73.8 us
  Pallas kernels: 119 us -> 113 us
    ppermute x28 -> x32, waiting for transfers between devices: 87 us -> 62.1 us  [send(): lax.ppermute(block, 'chip', ring_pairs(direction))]
    ppermute x4 -> x5, waiting for transfers between devices: 8.79 us -> 20.4 us  [across_heads(): return [part, lax.ppermute(part, 'head', [(0, 1), (1, 0)])]]
    slice x0 -> x7, local copies, waits for them, and re-layouts: none -> 6.69 us  [the longest x6 5.59 us: send(): sides = [sides[0][:, :half], sides[1][:, half:]]]
    unnamed x93 -> x108, local copies, waits for them, and re-layouts: 8.34 us -> 14.1 us
    all_to_all x4, waiting for transfers between devices: 9.43 us -> 4.08 us  [to_heads(): return lax.all_to_all(blocks, 'chip', 0, 0, tiled=True)]
    pallas_call x4 -> x2, Pallas kernels: 30 us -> 24.8 us  [backward_piece(): pl.pallas_call(functools.partial(backward_kernel, crops, len(before)), gr...]
    ppermute x28 -> x32, starting transfers between devices: 35.1 us -> 40.1 us  [send(): lax.ppermute(block, 'chip', ring_pairs(direction))]
    ppermute x4 -> x5, starting transfers between devices: 3.15 us -> 7.76 us  [across_heads(): return [part, lax.ppermute(part, 'head', [(0, 1), (1, 0)])]]
  transfers between devices with their start and end apart: 60 -> 65, of which waited for: 26 -> 22; matrix products, arithmetic and copies ran while one was open for 5% -> 9% of each run, Pallas kernels for 23% -> 29%
where the time goes in v10:
time: 351 us; the launch traced here: 349 us
  Pallas kernels  113 us (32%)
  waiting for transfers between devices  91.8 us (26%)
  starting transfers between devices  73.8 us (21%)
  blocking collectives  29.5 us (8%)
  local copies, waits for them, and re-layouts  23.8 us (7%)
  other arithmetic  11.3 us (3%)
  matrix products  4.36 us (1%)
    ppermute x32, waiting for transfers between devices, send(): lax.ppermute(block, 'chip', ring_pairs(direction))  62.1 us
    ppermute x32, starting transfers between devices, send(): lax.ppermute(block, 'chip', ring_pairs(direction))  40.1 us
    all_to_all x1, blocking collectives, to_heads(): return lax.all_to_all(blocks, 'chip', 0, 0, tiled=True)  29.5 us
    pallas_call x2, Pallas kernels, backward_piece(): pl.pallas_call(functools.partial(backward_kernel, crops, len(before)), gr...  24.8 us
    pallas_call x5, Pallas kernels, place(): pl.pallas_call(functools.partial(place_kernel, len(pairs)), grid_spec=plt...  20.5 us
    ppermute x5, waiting for transfers between devices, across_heads(): return [part, lax.ppermute(part, 'head', [(0, 1), (1, 0)])]  20.4 us
    pallas_call x5, Pallas kernels, add(): pl.pallas_call(functools.partial(add_kernel, [[start for _, start in part...  18.2 us
    all_to_all x4, starting transfers between devices, to_heads(): return lax.all_to_all(blocks, 'chip', 0, 0, tiled=True)  17.6 us
  transfers between devices with their start and end apart: 65, of which 22 were waited for; matrix products, arithmetic and copies ran while one was open for 9% of the time, Pallas kernels for 29%

profile of v10, /device:TPU:0, one launch (start us, length us, event | category | flops | bytes accessed | tf_op | source)
XLA Modules:
  0.0 349.3 jit_solution(7329686075954859091)
XLA Ops:
  0.6 6.0 %project.1 = (bf16[8,208,256]{2,1,0:T(8,128)(2,1)}, bf16[256,1024]{1,0:T(8,128)(2,1)}) custom-call(bf16[256,1024]{1,0:T(8,128)(2,1)} %input_ref.3, s32[1,256]{1,0:T(1,128)} %bitcast.62, s32[32]{0:T(128)} %steps_ref.1, f32[1,1024]{1,0:T(1,128)} %bitcast.52, f32[1,1024]{1,0:T(1,128)} %bitcast.60, f32[1,1024]{1,0:T(1,128)} %bitcast.61, ...), custom_call_target="tpu_custom_call" | custom-call | flops 1 | bytes 1 | tf_op jit(solution)/shard_map/project/pallas_call | solution.py:90
  6.6 29.5 %all_to_all.30.query_ref.own.refs_1_ = bf16[8,208,256]{2,1,0:T(8,128)(2,1)S(1)} all-to-all(bf16[8,208,256]{2,1,0:T(8,128)(2,1)} %get-tuple-element.189), channel_id=1, replica_groups=mesh['chip'=8,'core'=2,'head'=2] {'chip'}, dimensions={0} | all-to-all | bytes 1703936 | tf_op jit(solution)/shard_map/all_to_all | solution.py:419
  36.1 2.0 constant_dynamic-update-slice_fusion.7
  41.0 15.3 %attention_forward.1 = (f32[8,64,256]{2,1,0:T(8,128)}, bf16[8,64,256]{2,1,0:T(8,128)(2,1)}, f32[8,1,256]{2,1,0:T(1,128)}) custom-call(bf16[8,208,256]{2,1,0:T(8,128)(2,1)} %copy-done, bf16[8,208,256]{2,1,0:T(8,128)(2,1)} %copy-done, bf16[8,208,256]{2,1,0:T(8,128)(2,1)} %copy-done.2), custom_call_target="tpu_custom_call" | custom-call | flops 1 | bytes 1 | tf_op jit(solution)/shard_map/attention_forward/pallas_call | solution.py:351
  56.3 3.4 all-to-all-start.1
  59.7 1.9 collective-permute-start.3
  61.8 8.7 %collective-permute-done.3 = bf16[256,512]{1,0:T(8,128)(2,1)S(1)} collective-permute-done((bf16[256,512]{1,0:T(8,128)(2,1)S(1)}, bf16[256,512]{1,0:T(8,128)(2,1)S(1)}, u32[]{:S(2)}, u32[]{:S(2)}) %collective-permute-start.3) | collective-permute-done | bytes 262176 | tf_op jit(solution)/shard_map/ppermute | solution.py:496
  70.5 2.0 collective-permute-done.4
  73.0 1.5 collective-permute-start.7
  74.6 2.3 collective-permute-start.5
  76.9 5.0 %collective-permute-done.5 = bf16[256,512]{1,0:T(8,128)(2,1)S(1)} collective-permute-done((bf16[256,512]{1,0:T(8,128)(2,1)S(1)}, bf16[256,512]{1,0:T(8,128)(2,1)S(1)}, u32[]{:S(2)}, u32[]{:S(2)}) %collective-permute-start.5) | collective-permute-done | bytes 262176 | tf_op jit(solution)/shard_map/ppermute | solution.py:496
  83.4 2.9 collective-permute-done.7.refs_1_
  86.3 1.8 collective-permute-start.8
  89.1 11.8 %mlp.1 = (bf16[256,2048]{1,0:T(8,128)(2,1)}, bf16[256,2048]{1,0:T(8,128)(2,1)}, bf16[256,1024]{1,0:T(8,128)(2,1)}, bf16[256,1024]{1,0:T(8,128)(2,1)}, f32[256,10...) custom-call(s32[18]{0:T(128)} %compare_select_fusion.5.core_ref._.table, ...), custom_call_target="tpu_custom_call" | custom-call | flops 1 | bytes 1 | tf_op jit(solution)/shard_map/mlp/pallas_call | solution.py:158
  105.1 1.6 collective-permute-start.14
  108.4 3.2 ring_add.5
  112.7 1.8 collective-permute-start.12
  116.8 2.5 collective-permute-done.14.refs_1_
  119.3 4.3 %middle.1 = (f32[256,1024]{1,0:T(8,128)}, bf16[256,1024]{1,0:T(8,128)(2,1)}, bf16[512,256]{1,0:T(8,128)(2,1)}, f32[4,1024]{1,0:T(4,128)}) custom-call(f32[256,1024]{1,0:T(8,128)} %get-tuple-element.202.hidden_ref, bf16[256,1024]{1,0:T(8,128)(2,1)} %grad_ref.3, bf16[256,1024]{1,0:T(8,128)(2,1)} %get-tuple-element.224.refs_0_, ...), custom_call_target="tpu_custom_call" | custom-call | flops 1 | bytes 1 | tf_op jit(solution)/shard_map/middle/pallas_call | solution.py:219
  124.4 3.7 %ring_add.6 = (bf16[256,1024]{1,0:T(8,128)(2,1)}, bf16[256,1024]{1,0:T(8,128)(2,1)}) custom-call(s32[18]{0:T(128)} %compare_select_fusion.5.core_ref._.table, bf16[256,1024]{1,0:T(8,128)(2,1)} %get-tuple-element.217.refs_0_, bf16[256,1024]{1,0:T(8,128)(2,1)} %copy-done.9, bf16[256,2048]{1,0:T(8,128)(2,1)} %get-tuple-element.219.refs_2_.refs_5_, ...), custom_call_target="tpu_custom_call" | custom-call | flops 1 | bytes 1 | tf_op jit(solution)/shard_map/ring_add/pallas_call | solution.py:596
  128.7 4.8 %all-to-all-start.2 = ((bf16[8,64,256]{2,1,0:T(8,128)(2,1)}), bf16[8,64,256]{2,1,0:T(8,128)(2,1)S(1)}, u32[]{:S(2)}, u32[]{:S(2)}) async-start(bf16[8,64,256]{2,1,0:T(8,128)(2,1)} %bitcast.9), calls=%async_computation.2 | async-start | bytes 524288 | tf_op jit(solution)/shard_map/all_to_all | solution.py:419
  135.1 2.0 collective-permute-start.15
  139.6 4.1 %all-to-all-done.2.grad_ref = bf16[8,64,256]{2,1,0:T(8,128)(2,1)S(1)} async-done(((bf16[8,64,256]{2,1,0:T(8,128)(2,1)}), bf16[8,64,256]{2,1,0:T(8,128)(2,1)S(1)}, u32[]{:S(2)}, u32[]{:S(2)}) %all-to-all-start.2) | async-done | bytes 262176 | tf_op jit(solution)/shard_map/all_to_all | solution.py:419
  143.7 3.7 %all-to-all-start.3 = ((bf16[8,32,1024]{2,1,0:T(8,128)(2,1)}), bf16[8,32,1024]{2,1,0:T(8,128)(2,1)S(1)}, u32[]{:S(2)}, u32[]{:S(2)}) async-start(bf16[8,32,1024]{2,1,0:T(8,128)(2,1)} %bitcast.10), calls=%async_computation.3 | async-start | bytes 1048576 | tf_op jit(solution)/shard_map/all_to_all | solution.py:419
  147.4 12.7 %attention_backward.2 = (f32[8,64,256]{2,1,0:T(8,128)S(1)}, bf16[8,128,256]{2,1,0:T(8,128)(2,1)}) custom-call(bf16[8,208,256]{2,1,0:T(8,128)(2,1)S(1)} %copy-done.1, bf16[8,64,256]{2,1,0:T(8,128)(2,1)S(1)} %all-to-all-done.2.grad_ref, f32[8,64,256]{2,1,0:T(8,128)S(1)} %copy-done.4, f32[8,1,256]{2,1,0:T(1,128)S(1)} %copy-done.6, ...), custom_call_target="tpu_custom_call" | custom-call | flops 1 | bytes 1 | tf_op jit(solution)/shard_map/attention_backward/pallas_call | solution.py:381
  160.2 1.6 collective-permute-start.19
  161.8 3.9 %ring_add.7 = (bf16[256,1024]{1,0:T(8,128)(2,1)}, bf16[256,1024]{1,0:T(8,128)(2,1)}) custom-call(s32[18]{0:T(128)} %compare_select_fusion.5.core_ref._.table, bf16[256,1024]{1,0:T(8,128)(2,1)} %get-tuple-element.217.refs_0_, bf16[256,1024]{1,0:T(8,128)(2,1)} %copy-done.9, bf16[256,2048]{1,0:T(8,128)(2,1)} %get-tuple-element.219.refs_2_.refs_5_, ...), custom_call_target="tpu_custom_call" | custom-call | flops 1 | bytes 1 | tf_op jit(solution)/shard_map/ring_add/pallas_call | solution.py:596
  165.7 1.7 collective-permute-start.17
  167.7 12.0 %attention_backward.3 = (bf16[8,64,256]{2,1,0:T(8,128)(2,1)S(1)}, f32[8,128,256]{2,1,0:T(8,128)S(1)}) custom-call(bf16[8,208,256]{2,1,0:T(8,128)(2,1)S(1)} %copy-done.1, bf16[8,64,256]{2,1,0:T(8,128)(2,1)S(1)} %all-to-all-done.2.grad_ref, f32[8,64,256]{2,1,0:T(8,128)S(1)} %copy-done.4, f32[8,1,256]{2,1,0:T(1,128)S(1)} %copy-done.6, ...), custom_call_target="tpu_custom_call" | custom-call | flops 1 | bytes 1 | tf_op jit(solution)/shard_map/attention_backward/pallas_call | solution.py:381
  179.8 12.7 %collective-permute-done.19 = bf16[256,1024]{1,0:T(8,128)(2,1)} collective-permute-done((bf16[256,1024]{1,0:T(8,128)(2,1)}, bf16[256,1024]{1,0:T(8,128)(2,1)}, u32[]{:S(2)}, u32[]{:S(2)}) %collective-permute-start.19) | collective-permute-done | bytes 524320 | tf_op jit(solution)/shard_map/ppermute | solution.py:446
  192.5 3.9 %ring_add.8 = (bf16[256,1024]{1,0:T(8,128)(2,1)}, bf16[256,1024]{1,0:T(8,128)(2,1)}) custom-call(s32[18]{0:T(128)} %compare_select_fusion.5.core_ref._.table, bf16[256,1024]{1,0:T(8,128)(2,1)} %get-tuple-element.217.refs_0_, bf16[256,1024]{1,0:T(8,128)(2,1)} %copy-done.9, bf16[256,2048]{1,0:T(8,128)(2,1)} %get-tuple-element.219.refs_2_.refs_5_, ...), custom_call_target="tpu_custom_call" | custom-call | flops 1 | bytes 1 | tf_op jit(solution)/shard_map/ring_add/pallas_call | solution.py:596
  198.6 5.7 %all-to-all-start.4 = ((bf16[8,192,256]{2,1,0:T(8,128)(2,1)}), bf16[8,192,256]{2,1,0:T(8,128)(2,1)S(1)}, u32[]{:S(2)}, u32[]{:S(2)}) async-start(bf16[8,192,256]{2,1,0:T(8,128)(2,1)} %pad_maximum_fusion), calls=%async_computation.4 | async-start | bytes 1572864 | tf_op jit(solution)/shard_map/all_to_all | solution.py:419
  204.4 2.1 collective-permute-start.20
  206.5 5.0 %head_gradient.1 = bf16[192,1024]{1,0:T(8,128)(2,1)} custom-call(s32[18]{0:T(128)} %compare_select_fusion.5.core_ref._.table, bf16[8,64,256]{2,1,0:T(8,128)(2,1)} %copy-done.5, bf16[8,128,256]{2,1,0:T(8,128)(2,1)} %copy-done.10, bf16[2048,512]{1,0:T(8,128)(2,1)} %copy-done.17, bf16[2048,512]{1,0:T(8,128)(2,1)} %collective-permute-done.25.refs_1_), custom_call_target="tpu_custom_call" | custom-call | flops 1 | bytes 1 | tf_op jit(solution)/shard_map/head_gradient/pallas_call | solution.py:687
  215.7 11.6 %collective-permute-done.20.refs_4_ = bf16[256,1024]{1,0:T(8,128)(2,1)S(1)} collective-permute-done((bf16[256,1024]{1,0:T(8,128)(2,1)}, bf16[256,1024]{1,0:T(8,128)(2,1)S(1)}, u32[]{:S(2)}, u32[]{:S(2)}) %collective-permute-start.20) | collective-permute-done | bytes 524320 | tf_op jit(solution)/shard_map/ppermute | solution.py:552
  227.3 2.0 collective-permute-done.21.refs_5_
  230.1 3.5 %ring_add.9.refs_0_ = bf16[256,1024]{1,0:T(8,128)(2,1)} custom-call(s32[18]{0:T(128)} %compare_select_fusion.5.core_ref._.table, bf16[256,1024]{1,0:T(8,128)(2,1)} %get-tuple-element.217.refs_0_, bf16[256,1024]{1,0:T(8,128)(2,1)} %copy-done.9, bf16[256,2048]{1,0:T(8,128)(2,1)} %get-tuple-element.219.refs_2_.refs_5_, bf16[256,2048]{1,0:T(8,128)(2,1)} %copy-done.7, ...), custom_call_target="tpu_custom_call" | custom-call | flops 1 | bytes 1 | tf_op jit(solution)/shard_map/ring_add/pallas_call | solution.py:596
  233.6 5.8 %collective-permute-start.27 = (bf16[256,1024]{1,0:T(8,128)(2,1)}, bf16[256,1024]{1,0:T(8,128)(2,1)}, u32[]{:S(2)}, u32[]{:S(2)}) collective-permute-start(bf16[256,1024]{1,0:T(8,128)(2,1)} %ring_add.9.refs_0_), channel_id=1, source_target_pairs={{0,8},{8,16},{16,24},{24,28},{28,20},{20,12},{12,4},{4,0},{1,9},{9... | collective-permute-start | bytes 1572872 | tf_op jit(solution)/shard_map/ppermute | solution.py:496
  239.4 2.0 collective-permute-start.30
  242.7 12.4 %collective-permute-done.30.refs_1_ = bf16[136,1024]{1,0:T(8,128)(2,1)} collective-permute-done((bf16[136,1024]{1,0:T(8,128)(2,1)}, bf16[136,1024]{1,0:T(8,128)(2,1)}, u32[]{:S(2)}, u32[]{:S(2)}) %collective-permute-start.30) | collective-permute-done | bytes 278560 | tf_op jit(solution)/shard_map/ppermute | solution.py:496
  255.6 1.8 collective-permute-done.31.refs_2_
  257.5 1.9 collective-permute-start.37
  261.6 6.3 %collective-permute-done.37.refs_3_ = bf16[136,1024]{1,0:T(8,128)(2,1)} collective-permute-done((bf16[136,1024]{1,0:T(8,128)(2,1)}, bf16[136,1024]{1,0:T(8,128)(2,1)}, u32[]{:S(2)}, u32[]{:S(2)}) %collective-permute-start.37) | collective-permute-done | bytes 278560 | tf_op jit(solution)/shard_map/ppermute | solution.py:496
  267.9 2.1 collective-permute-start.34
  270.7 1.9 collective-permute-done.40.refs_10_
  274.1 3.4 place.5
  278.7 2.5 collective-permute-done.34.refs_3_
  284.4 2.2 collective-permute-done.49
  286.6 1.8 collective-permute-start.42
  288.3 2.6 collective-permute-done.45.refs_5_
  291.6 2.0 collective-permute-done.47.refs_11_
  293.8 2.2 add_convert_fusion.1
  296.0 4.6 %place.6 = (f32[2048,1024]{1,0:T(8,128)}, f32[1024,2048]{1,0:T(8,128)}) custom-call(s32[18]{0:T(128)} %compare_select_fusion.5.core_ref._.table, f32[2048,1024]{1,0:T(8,128)} %get-tuple-element.297.refs_0_, f32[1024,2048]{1,0:T(8,128)} %get-tuple-element.298.refs_1_, ...), custom_call_target="tpu_custom_call", output_to_operand_aliasing={{0}: (1, {}), {1}: (2, {})} | custom-call | flops 1 | bytes 1 | tf_op jit(solution)/shard_map/place/pallas_call | solution.py:627
  302.7 1.6 slice.78
  305.0 4.3 %all-to-all-start.5 = ((bf16[32,32,128]{2,1,0:T(8,128)(2,1)}), bf16[32,32,128]{2,1,0:T(8,128)(2,1)S(1)}, u32[]{:S(2)}, u32[]{:S(2)}) async-start(bf16[32,32,128]{2,1,0:T(8,128)(2,1)} %broadcast_in_dim.55), calls=%async_computation.5 | async-start | bytes 524288 | tf_op jit(solution)/shard_map/all_to_all | solution.py:920
  309.6 1.7 collective-permute-start.54
  311.7 1.7 slice.75
  313.3 1.7 slice.76
  315.0 3.0 collective-permute-done.54
  319.5 2.7 collective-permute-start.50
  324.4 4.5 %place.7 = (f32[2048,1024]{1,0:T(8,128)}, f32[1024,2048]{1,0:T(8,128)}) custom-call(s32[18]{0:T(128)} %compare_select_fusion.5.core_ref._.table, f32[2048,1024]{1,0:T(8,128)} %get-tuple-element.316.refs_0_, f32[1024,2048]{1,0:T(8,128)} %get-tuple-element.317.refs_1_, ...), custom_call_target="tpu_custom_call", output_to_operand_aliasing={{0}: (1, {}), {1}: (2, {})} | custom-call | flops 1 | bytes 1 | tf_op jit(solution)/shard_map/place/pallas_call | solution.py:627
  329.7 7.2 %final_layout.1 = (f32[1024,512]{1,0:T(8,128)}, f32[1024,512]{1,0:T(8,128)}, f32[1024,512]{1,0:T(8,128)}, f32[2,8,32,1024]{3,2,1,0:T(8,128)}, f32[2,8,8,1024]{3,2,1,0:T(8,128)}) custom-call(s32[18]{0:T(128)} %compare_select_fusion.5.core_ref._.table, bf16[136,1024]{1,0:T(8,128)(2,1)} %pad_maximum_fusion.2.refs_0_, ...), custom_call_target="tpu_custom_call" | custom-call | flops 1 | bytes 1 | tf_op jit(solution)/shard_map/final_layout/pallas_call | solution.py:741
  339.2 4.6 %place.8 = (f32[2048,1024]{1,0:T(8,128)}, f32[1024,2048]{1,0:T(8,128)}) custom-call(s32[18]{0:T(128)} %compare_select_fusion.5.core_ref._.table, f32[2048,1024]{1,0:T(8,128)} %get-tuple-element.351.refs_0_, f32[1024,2048]{1,0:T(8,128)} %get-tuple-element.352.refs_1_, ...), custom_call_target="tpu_custom_call", output_to_operand_aliasing={{0}: (1, {}), {1}: (2, {})} | custom-call | flops 1 | bytes 1 | tf_op jit(solution)/shard_map/place/pallas_call | solution.py:627
  345.9 3.4 place.9
  (246 shorter events, 51.5 us)
Async XLA Ops:
  36.1 4.0 %collective-permute-start.2 = (bf16[8,208,256]{2,1,0:T(8,128)(2,1)S(1)}, bf16[8,208,256]{2,1,0:T(8,128)(2,1)S(1)}, u32[]{:S(2)}, u32[]{:S(2)}) collective-permute-start(bf16[8,208,256]{2,1,0:T(8,128)(2,1)S(1)} %all_to_all.30.query_ref.own.refs_1_), channel_id=1, source_target_pairs={{0,2},{2,0},{1,3},{3,1},{4,6},{6,4},{5,7},{7,5},{8,10},{10,8},{9,1... | collective-permute-start | bytes 2555912 | tf_op jit(solution)/shard_map/ppermute | solution.py:415
  38.0 18.2 %collective-permute-start = (bf16[256,512]{1,0:T(8,128)(2,1)S(1)}, bf16[256,512]{1,0:T(8,128)(2,1)S(1)}, u32[]{:S(2)}, u32[]{:S(2)}) collective-permute-start(bf16[256,512]{1,0:T(8,128)(2,1)S(1)} %get-tuple-element.371), channel_id=1, source_target_pairs={{0,8},{8,16},{16,24},{24,28},{28,20},{20,12},{12,4},{4,0},{1,9},{9... | collective-permute-start | bytes 786440 | tf_op jit(solution)/shard_map/ppermute | solution.py:496
  38.8 17.5 %collective-permute-start.1 = (bf16[256,512]{1,0:T(8,128)(2,1)S(1)}, bf16[256,512]{1,0:T(8,128)(2,1)S(1)}, u32[]{:S(2)}, u32[]{:S(2)}) collective-permute-start(bf16[256,512]{1,0:T(8,128)(2,1)S(1)} %get-tuple-element.371), channel_id=1, source_target_pairs={{0,4},{8,0},{16,8},{24,16},{28,24},{20,28},{12,20},{4,12},{1,5},{9... | collective-permute-start | bytes 786440 | tf_op jit(solution)/shard_map/ppermute | solution.py:496
  56.3 16.2 %all-to-all-start.1 = ((bf16[8,64,256]{2,1,0:T(8,128)(2,1)}), bf16[8,64,256]{2,1,0:T(8,128)(2,1)S(1)}, u32[]{:S(2)}, u32[]{:S(2)}) async-start(bf16[8,64,256]{2,1,0:T(8,128)(2,1)} %get-tuple-element.196), calls=%async_computation.1 | async-start | bytes 524288 | tf_op jit(solution)/shard_map/all_to_all | solution.py:419
  59.7 10.8 %collective-permute-start.3 = (bf16[256,512]{1,0:T(8,128)(2,1)S(1)}, bf16[256,512]{1,0:T(8,128)(2,1)S(1)}, u32[]{:S(2)}, u32[]{:S(2)}) collective-permute-start(bf16[256,512]{1,0:T(8,128)(2,1)S(1)} %collective-permute-done), channel_id=1, source_target_pairs={{0,8},{8,16},{16,24},{24,28},{28,20},{20,12},{12,4},{4,0},{1,9},{9... | collective-permute-start | bytes 786440 | tf_op jit(solution)/shard_map/ppermute | solution.py:496
  61.7 10.8 %collective-permute-start.4 = (bf16[256,512]{1,0:T(8,128)(2,1)S(1)}, bf16[256,512]{1,0:T(8,128)(2,1)S(1)}, u32[]{:S(2)}, u32[]{:S(2)}) collective-permute-start(bf16[256,512]{1,0:T(8,128)(2,1)S(1)} %collective-permute-done.1), channel_id=1, source_target_pairs={{0,4},{8,0},{16,8},{24,16},{28,24},{20,28},{12,20},{4,12},{1,5},{9... | collective-permute-start | bytes 786440 | tf_op jit(solution)/shard_map/ppermute | solution.py:496
  73.0 13.3 %collective-permute-start.7 = (bf16[256,1024]{1,0:T(8,128)(2,1)S(1)}, bf16[256,1024]{1,0:T(8,128)(2,1)S(1)}, u32[]{:S(2)}, u32[]{:S(2)}) collective-permute-start(bf16[256,1024]{1,0:T(8,128)(2,1)S(1)} %convolution_convert_fusion.refs_0_), channel_id=1, source_target_pairs={{0,1},{1,0},{2,3},{3,2},{4,5},{5,4},{6,7},{7,6},{8,9},{9,8},{10,11... | collective-permute-start | bytes 1572872 | tf_op jit(solution)/shard_map/ppermute | solution.py:446
  74.6 7.3 %collective-permute-start.5 = (bf16[256,512]{1,0:T(8,128)(2,1)S(1)}, bf16[256,512]{1,0:T(8,128)(2,1)S(1)}, u32[]{:S(2)}, u32[]{:S(2)}) collective-permute-start(bf16[256,512]{1,0:T(8,128)(2,1)S(1)} %collective-permute-done.3), channel_id=1, source_target_pairs={{0,8},{8,16},{16,24},{24,28},{28,20},{20,12},{12,4},{4,0},{1,9},{9... | collective-permute-start | bytes 786440 | tf_op jit(solution)/shard_map/ppermute | solution.py:496
  76.9 6.4 %collective-permute-start.6 = (bf16[256,512]{1,0:T(8,128)(2,1)S(1)}, bf16[256,512]{1,0:T(8,128)(2,1)S(1)}, u32[]{:S(2)}, u32[]{:S(2)}) collective-permute-start(bf16[256,512]{1,0:T(8,128)(2,1)S(1)} %collective-permute-done.4), channel_id=1, source_target_pairs={{0,4},{8,0},{16,8},{24,16},{28,24},{20,28},{12,20},{4,12},{1,5},{9... | collective-permute-start | bytes 786440 | tf_op jit(solution)/shard_map/ppermute | solution.py:496
  86.3 14.6 %collective-permute-start.8 = (bf16[256,256]{1,0:T(8,128)(2,1)S(1)}, bf16[256,256]{1,0:T(8,128)(2,1)S(1)}, u32[]{:S(2)}, u32[]{:S(2)}) collective-permute-start(bf16[256,256]{1,0:T(8,128)(2,1)S(1)} %slice.65), channel_id=1, source_target_pairs={{0,8},{8,16},{16,24},{24,28},{28,20},{20,12},{12,4},{4,0},{1,9},{9... | collective-permute-start | bytes 393224 | tf_op jit(solution)/shard_map/ppermute | solution.py:496
  88.1 12.8 %collective-permute-start.9 = (bf16[256,256]{1,0:T(8,128)(2,1)S(1)}, bf16[256,256]{1,0:T(8,128)(2,1)S(1)}, u32[]{:S(2)}, u32[]{:S(2)}) collective-permute-start(bf16[256,256]{1,0:T(8,128)(2,1)S(1)} %slice.66), channel_id=1, source_target_pairs={{0,4},{8,0},{16,8},{24,16},{28,24},{20,28},{12,20},{4,12},{1,5},{9... | collective-permute-start | bytes 393224 | tf_op jit(solution)/shard_map/ppermute | solution.py:496
  101.7 5.0 %collective-permute-start.11 = (bf16[256,2048]{1,0:T(8,128)(2,1)}, bf16[256,2048]{1,0:T(8,128)(2,1)S(1)}, u32[]{:S(2)}, u32[]{:S(2)}) collective-permute-start(bf16[256,2048]{1,0:T(8,128)(2,1)} %get-tuple-element.220), channel_id=1, source_target_pairs={{0,2},{2,0},{1,3},{3,1},{4,6},{6,4},{5,7},{7,5},{8,10},{10,8},{9,1... | collective-permute-start | bytes 3145736 | tf_op jit(solution)/shard_map/ppermute | solution.py:415
  101.7 5.0 %collective-permute-start.10 = (bf16[256,1024]{1,0:T(8,128)(2,1)}, bf16[256,1024]{1,0:T(8,128)(2,1)S(1)}, u32[]{:S(2)}, u32[]{:S(2)}) collective-permute-start(bf16[256,1024]{1,0:T(8,128)(2,1)} %get-tuple-element.218), channel_id=1, source_target_pairs={{0,2},{2,0},{1,3},{3,1},{4,6},{6,4},{5,7},{7,5},{8,10},{10,8},{9,1... | collective-permute-start | bytes 1572872 | tf_op jit(solution)/shard_map/ppermute | solution.py:415
  105.1 14.2 %collective-permute-start.14 = (bf16[256,1024]{1,0:T(8,128)(2,1)}, bf16[256,1024]{1,0:T(8,128)(2,1)}, u32[]{:S(2)}, u32[]{:S(2)}) collective-permute-start(bf16[256,1024]{1,0:T(8,128)(2,1)} %get-tuple-element.224.refs_0_), channel_id=1, source_target_pairs={{0,1},{1,0},{2,3},{3,2},{4,5},{5,4},{6,7},{7,6},{8,9},{9,8},{10,11... | collective-permute-start | bytes 1572872 | tf_op jit(solution)/shard_map/ppermute | solution.py:446
  112.7 10.9 %collective-permute-start.12 = (bf16[256,512]{1,0:T(8,128)(2,1)S(1)}, bf16[256,512]{1,0:T(8,128)(2,1)S(1)}, u32[]{:S(2)}, u32[]{:S(2)}) collective-permute-start(bf16[256,512]{1,0:T(8,128)(2,1)S(1)} %get-tuple-element.376), channel_id=1, source_target_pairs={{0,8},{8,16},{16,24},{24,28},{28,20},{20,12},{12,4},{4,0},{1,9},{9... | collective-permute-start | bytes 786440 | tf_op jit(solution)/shard_map/ppermute | solution.py:552
  114.5 9.1 %collective-permute-start.13 = (bf16[256,512]{1,0:T(8,128)(2,1)S(1)}, bf16[256,512]{1,0:T(8,128)(2,1)S(1)}, u32[]{:S(2)}, u32[]{:S(2)}) collective-permute-start(bf16[256,512]{1,0:T(8,128)(2,1)S(1)} %get-tuple-element.375), channel_id=1, source_target_pairs={{0,4},{8,0},{16,8},{24,16},{28,24},{20,28},{12,20},{4,12},{1,5},{9... | collective-permute-start | bytes 786440 | tf_op jit(solution)/shard_map/ppermute | solution.py:552
  128.1 10.4 %collective-permute-start.23 = (bf16[256,1024]{1,0:T(8,128)(2,1)}, bf16[256,1024]{1,0:T(8,128)(2,1)S(1)}, u32[]{:S(2)}, u32[]{:S(2)}) collective-permute-start(bf16[256,1024]{1,0:T(8,128)(2,1)} %get-tuple-element.269), channel_id=1, source_target_pairs={{0,2},{2,0},{1,3},{3,1},{4,6},{6,4},{5,7},{7,5},{8,10},{10,8},{9,1... | collective-permute-start | bytes 1572872 | tf_op jit(solution)/shard_map/ppermute | solution.py:415
  128.2 10.3 %collective-permute-start.22 = (bf16[256,256]{1,0:T(8,128)(2,1)S(1)}, bf16[256,256]{1,0:T(8,128)(2,1)S(1)}, u32[]{:S(2)}, u32[]{:S(2)}) collective-permute-start(bf16[256,256]{1,0:T(8,128)(2,1)S(1)} %constant_dynamic-slice_fusion.1), channel_id=1, source_target_pairs={{0,2},{2,0},{1,3},{3,1},{4,6},{6,4},{5,7},{7,5},{8,10},{10,8},{9,1... | collective-permute-start | bytes 393224 | tf_op jit(solution)/shard_map/ppermute | solution.py:415
  128.7 15.0 %all-to-all-start.2 = ((bf16[8,64,256]{2,1,0:T(8,128)(2,1)}), bf16[8,64,256]{2,1,0:T(8,128)(2,1)S(1)}, u32[]{:S(2)}, u32[]{:S(2)}) async-start(bf16[8,64,256]{2,1,0:T(8,128)(2,1)} %bitcast.9), calls=%async_computation.2 | async-start | bytes 524288 | tf_op jit(solution)/shard_map/all_to_all | solution.py:419
  133.6 72.9 %collective-permute-start.25 = (bf16[2048,512]{1,0:T(8,128)(2,1)}, bf16[2048,512]{1,0:T(8,128)(2,1)}, u32[]{:S(2)}, u32[]{:S(2)}) collective-permute-start(bf16[2048,512]{1,0:T(8,128)(2,1)} %copy-done.17), channel_id=1, source_target_pairs={{0,1},{1,0},{2,3},{3,2},{4,5},{5,4},{6,7},{7,6},{8,9},{9,8},{10,11... | collective-permute-start | bytes 6291464 | tf_op jit(solution)/shard_map/ppermute | solution.py:446
  135.1 26.7 %collective-permute-start.15 = (bf16[256,1024]{1,0:T(8,128)(2,1)}, bf16[256,1024]{1,0:T(8,128)(2,1)}, u32[]{:S(2)}, u32[]{:S(2)}) collective-permute-start(bf16[256,1024]{1,0:T(8,128)(2,1)} %get-tuple-element.234), channel_id=1, source_target_pairs={{0,8},{8,16},{16,24},{24,28},{28,20},{20,12},{12,4},{4,0},{1,9},{9... | collective-permute-start | bytes 1572872 | tf_op jit(solution)/shard_map/ppermute | solution.py:552
  137.1 24.7 %collective-permute-start.16 = (bf16[256,1024]{1,0:T(8,128)(2,1)}, bf16[256,1024]{1,0:T(8,128)(2,1)}, u32[]{:S(2)}, u32[]{:S(2)}) collective-permute-start(bf16[256,1024]{1,0:T(8,128)(2,1)} %get-tuple-element.235), channel_id=1, source_target_pairs={{0,4},{8,0},{16,8},{24,16},{28,24},{20,28},{12,20},{4,12},{1,5},{9... | collective-permute-start | bytes 1572872 | tf_op jit(solution)/shard_map/ppermute | solution.py:552
  143.7 53.9 %all-to-all-start.3 = ((bf16[8,32,1024]{2,1,0:T(8,128)(2,1)}), bf16[8,32,1024]{2,1,0:T(8,128)(2,1)S(1)}, u32[]{:S(2)}, u32[]{:S(2)}) async-start(bf16[8,32,1024]{2,1,0:T(8,128)(2,1)} %bitcast.10), calls=%async_computation.3 | async-start | bytes 1048576 | tf_op jit(solution)/shard_map/all_to_all | solution.py:419
  160.2 32.3 %collective-permute-start.19 = (bf16[256,1024]{1,0:T(8,128)(2,1)}, bf16[256,1024]{1,0:T(8,128)(2,1)}, u32[]{:S(2)}, u32[]{:S(2)}) collective-permute-start(bf16[256,1024]{1,0:T(8,128)(2,1)} %get-tuple-element.263), channel_id=1, source_target_pairs={{0,1},{1,0},{2,3},{3,2},{4,5},{5,4},{6,7},{7,6},{8,9},{9,8},{10,11... | collective-permute-start | bytes 1572872 | tf_op jit(solution)/shard_map/ppermute | solution.py:446
  165.7 26.8 %collective-permute-start.17 = (bf16[256,1024]{1,0:T(8,128)(2,1)}, bf16[256,1024]{1,0:T(8,128)(2,1)}, u32[]{:S(2)}, u32[]{:S(2)}) collective-permute-start(bf16[256,1024]{1,0:T(8,128)(2,1)} %get-tuple-element.248), channel_id=1, source_target_pairs={{0,8},{8,16},{16,24},{24,28},{28,20},{20,12},{12,4},{4,0},{1,9},{9... | collective-permute-start | bytes 1572872 | tf_op jit(solution)/shard_map/ppermute | solution.py:552
  167.4 25.1 %collective-permute-start.18 = (bf16[256,1024]{1,0:T(8,128)(2,1)}, bf16[256,1024]{1,0:T(8,128)(2,1)}, u32[]{:S(2)}, u32[]{:S(2)}) collective-permute-start(bf16[256,1024]{1,0:T(8,128)(2,1)} %get-tuple-element.249), channel_id=1, source_target_pairs={{0,4},{8,0},{16,8},{24,16},{28,24},{20,28},{12,20},{4,12},{1,5},{9... | collective-permute-start | bytes 1572872 | tf_op jit(solution)/shard_map/ppermute | solution.py:552
  167.7 28.7 %collective-permute-start.24 = (bf16[8,128,256]{2,1,0:T(8,128)(2,1)}, bf16[8,128,256]{2,1,0:T(8,128)(2,1)}, u32[]{:S(2)}, u32[]{:S(2)}) collective-permute-start(bf16[8,128,256]{2,1,0:T(8,128)(2,1)} %get-tuple-element.271), channel_id=1, source_target_pairs={{0,2},{2,0},{1,3},{3,1},{4,6},{6,4},{5,7},{7,5},{8,10},{10,8},{9,1... | collective-permute-start | bytes 1572872 | tf_op jit(solution)/shard_map/ppermute | solution.py:415
  198.6 42.9 %all-to-all-start.4 = ((bf16[8,192,256]{2,1,0:T(8,128)(2,1)}), bf16[8,192,256]{2,1,0:T(8,128)(2,1)S(1)}, u32[]{:S(2)}, u32[]{:S(2)}) async-start(bf16[8,192,256]{2,1,0:T(8,128)(2,1)} %pad_maximum_fusion), calls=%async_computation.4 | async-start | bytes 1572864 | tf_op jit(solution)/shard_map/all_to_all | solution.py:419
  204.4 22.9 %collective-permute-start.20 = (bf16[256,1024]{1,0:T(8,128)(2,1)}, bf16[256,1024]{1,0:T(8,128)(2,1)S(1)}, u32[]{:S(2)}, u32[]{:S(2)}) collective-permute-start(bf16[256,1024]{1,0:T(8,128)(2,1)} %get-tuple-element.266), channel_id=1, source_target_pairs={{0,8},{8,16},{16,24},{24,28},{28,20},{20,12},{12,4},{4,0},{1,9},{9... | collective-permute-start | bytes 1572872 | tf_op jit(solution)/shard_map/ppermute | solution.py:552
  206.5 22.8 %collective-permute-start.21 = (bf16[256,1024]{1,0:T(8,128)(2,1)}, bf16[256,1024]{1,0:T(8,128)(2,1)S(1)}, u32[]{:S(2)}, u32[]{:S(2)}) collective-permute-start(bf16[256,1024]{1,0:T(8,128)(2,1)} %get-tuple-element.267), channel_id=1, source_target_pairs={{0,4},{8,0},{16,8},{24,16},{28,24},{20,28},{12,20},{4,12},{1,5},{9... | collective-permute-start | bytes 1572872 | tf_op jit(solution)/shard_map/ppermute | solution.py:552
  233.6 23.8 %collective-permute-start.27 = (bf16[256,1024]{1,0:T(8,128)(2,1)}, bf16[256,1024]{1,0:T(8,128)(2,1)}, u32[]{:S(2)}, u32[]{:S(2)}) collective-permute-start(bf16[256,1024]{1,0:T(8,128)(2,1)} %ring_add.9.refs_0_), channel_id=1, source_target_pairs={{0,8},{8,16},{16,24},{24,28},{28,20},{20,12},{12,4},{4,0},{1,9},{9... | collective-permute-start | bytes 1572872 | tf_op jit(solution)/shard_map/ppermute | solution.py:496
  239.4 18.0 %collective-permute-start.28 = (bf16[256,1024]{1,0:T(8,128)(2,1)}, bf16[256,1024]{1,0:T(8,128)(2,1)}, u32[]{:S(2)}, u32[]{:S(2)}) collective-permute-start(bf16[256,1024]{1,0:T(8,128)(2,1)} %ring_add.9.refs_0_), channel_id=1, source_target_pairs={{0,4},{8,0},{16,8},{24,16},{28,24},{20,28},{12,20},{4,12},{1,5},{9... | collective-permute-start | bytes 1572872 | tf_op jit(solution)/shard_map/ppermute | solution.py:496
  239.4 18.0 %collective-permute-start.29 = (bf16[256,1024]{1,0:T(8,128)(2,1)}, bf16[256,1024]{1,0:T(8,128)(2,1)}, u32[]{:S(2)}, u32[]{:S(2)}) collective-permute-start(bf16[256,1024]{1,0:T(8,128)(2,1)} %ring_add.9.refs_0_), channel_id=1, source_target_pairs={{0,2},{2,0},{1,3},{3,1},{4,6},{6,4},{5,7},{7,5},{8,10},{10,8},{9,1... | collective-permute-start | bytes 1572872 | tf_op jit(solution)/shard_map/ppermute | solution.py:415
  239.4 15.6 %collective-permute-start.30 = (bf16[136,1024]{1,0:T(8,128)(2,1)}, bf16[136,1024]{1,0:T(8,128)(2,1)}, u32[]{:S(2)}, u32[]{:S(2)}) collective-permute-start(bf16[136,1024]{1,0:T(8,128)(2,1)} %pad_maximum_fusion.2.refs_0_), channel_id=1, source_target_pairs={{0,8},{8,16},{16,24},{24,28},{28,20},{20,12},{12,4},{4,0},{1,9},{9... | collective-permute-start | bytes 835592 | tf_op jit(solution)/shard_map/ppermute | solution.py:496
  241.5 16.0 %collective-permute-start.31 = (bf16[136,1024]{1,0:T(8,128)(2,1)}, bf16[136,1024]{1,0:T(8,128)(2,1)}, u32[]{:S(2)}, u32[]{:S(2)}) collective-permute-start(bf16[136,1024]{1,0:T(8,128)(2,1)} %pad_maximum_fusion.2.refs_0_), channel_id=1, source_target_pairs={{0,4},{8,0},{16,8},{24,16},{28,24},{20,28},{12,20},{4,12},{1,5},{9... | collective-permute-start | bytes 835592 | tf_op jit(solution)/shard_map/ppermute | solution.py:496
  255.0 2.4 collective-permute-start.32
  257.5 10.5 %collective-permute-start.37 = (bf16[136,1024]{1,0:T(8,128)(2,1)}, bf16[136,1024]{1,0:T(8,128)(2,1)}, u32[]{:S(2)}, u32[]{:S(2)}) collective-permute-start(bf16[136,1024]{1,0:T(8,128)(2,1)} %collective-permute-done.30.refs_1_), channel_id=1, source_target_pairs={{0,8},{8,16},{16,24},{24,28},{28,20},{20,12},{12,4},{4,0},{1,9},{9... | collective-permute-start | bytes 835592 | tf_op jit(solution)/shard_map/ppermute | solution.py:496
  259.4 10.6 %collective-permute-start.38 = (bf16[136,1024]{1,0:T(8,128)(2,1)}, bf16[136,1024]{1,0:T(8,128)(2,1)}, u32[]{:S(2)}, u32[]{:S(2)}) collective-permute-start(bf16[136,1024]{1,0:T(8,128)(2,1)} %collective-permute-done.31.refs_2_), channel_id=1, source_target_pairs={{0,4},{8,0},{16,8},{24,16},{28,24},{20,28},{12,20},{4,12},{1,5},{9... | collective-permute-start | bytes 835592 | tf_op jit(solution)/shard_map/ppermute | solution.py:496
  260.2 9.8 %collective-permute-start.39 = (bf16[136,1024]{1,0:T(8,128)(2,1)}, bf16[136,1024]{1,0:T(8,128)(2,1)}, u32[]{:S(2)}, u32[]{:S(2)}) collective-permute-start(bf16[136,1024]{1,0:T(8,128)(2,1)} %collective-permute-done.30.refs_1_), channel_id=1, source_target_pairs={{0,2},{2,0},{1,3},{3,1},{4,6},{6,4},{5,7},{7,5},{8,10},{10,8},{9,1... | collective-permute-start | bytes 835592 | tf_op jit(solution)/shard_map/ppermute | solution.py:415
  260.2 18.4 %collective-permute-start.33 = (bf16[256,1024]{1,0:T(8,128)(2,1)}, bf16[256,1024]{1,0:T(8,128)(2,1)}, u32[]{:S(2)}, u32[]{:S(2)}) collective-permute-start(bf16[256,1024]{1,0:T(8,128)(2,1)} %collective-permute-done.27.refs_2_), channel_id=1, source_target_pairs={{0,8},{8,16},{16,24},{24,28},{28,20},{20,12},{12,4},{4,0},{1,9},{9... | collective-permute-start | bytes 1572872 | tf_op jit(solution)/shard_map/ppermute | solution.py:496
  261.4 19.8 %collective-permute-start.35 = (bf16[256,1024]{1,0:T(8,128)(2,1)}, bf16[256,1024]{1,0:T(8,128)(2,1)}, u32[]{:S(2)}, u32[]{:S(2)}) collective-permute-start(bf16[256,1024]{1,0:T(8,128)(2,1)} %collective-permute-done.27.refs_2_), channel_id=1, source_target_pairs={{0,2},{2,0},{1,3},{3,1},{4,6},{6,4},{5,7},{7,5},{8,10},{10,8},{9,1... | collective-permute-start | bytes 1572872 | tf_op jit(solution)/shard_map/ppermute | solution.py:415
  267.9 13.3 %collective-permute-start.34 = (bf16[256,1024]{1,0:T(8,128)(2,1)}, bf16[256,1024]{1,0:T(8,128)(2,1)}, u32[]{:S(2)}, u32[]{:S(2)}) collective-permute-start(bf16[256,1024]{1,0:T(8,128)(2,1)} %collective-permute-done.28.refs_3_), channel_id=1, source_target_pairs={{0,4},{8,0},{16,8},{24,16},{28,24},{20,28},{12,20},{4,12},{1,5},{9... | collective-permute-start | bytes 1572872 | tf_op jit(solution)/shard_map/ppermute | solution.py:496
  270.0 11.2 %collective-permute-start.36 = (bf16[256,1024]{1,0:T(8,128)(2,1)}, bf16[256,1024]{1,0:T(8,128)(2,1)}, u32[]{:S(2)}, u32[]{:S(2)}) collective-permute-start(bf16[256,1024]{1,0:T(8,128)(2,1)} %collective-permute-done.28.refs_3_), channel_id=1, source_target_pairs={{0,2},{2,0},{1,3},{3,1},{4,6},{6,4},{5,7},{7,5},{8,10},{10,8},{9,1... | collective-permute-start | bytes 1572872 | tf_op jit(solution)/shard_map/ppermute | solution.py:415
  270.0 2.6 collective-permute-start.40
  272.6 14.0 %collective-permute-start.49 = (bf16[256,1024]{1,0:T(8,128)(2,1)S(1)}, bf16[256,1024]{1,0:T(8,128)(2,1)S(1)}, u32[]{:S(2)}, u32[]{:S(2)}) collective-permute-start(bf16[256,1024]{1,0:T(8,128)(2,1)S(1)} %convert_element_type.73), channel_id=1, source_target_pairs={{0,1},{1,0},{2,3},{3,2},{4,5},{5,4},{6,7},{7,6},{8,9},{9,8},{10,11... | collective-permute-start | bytes 1572872 | tf_op jit(solution)/shard_map/ppermute | solution.py:446
  281.2 9.8 %collective-permute-start.45 = (bf16[136,1024]{1,0:T(8,128)(2,1)}, bf16[136,1024]{1,0:T(8,128)(2,1)S(1)}, u32[]{:S(2)}, u32[]{:S(2)}) collective-permute-start(bf16[136,1024]{1,0:T(8,128)(2,1)} %collective-permute-done.37.refs_3_), channel_id=1, source_target_pairs={{0,8},{8,16},{16,24},{24,28},{28,20},{20,12},{12,4},{4,0},{1,9},{9... | collective-permute-start | bytes 835592 | tf_op jit(solution)/shard_map/ppermute | solution.py:496
  282.0 9.0 %collective-permute-start.46 = (bf16[136,1024]{1,0:T(8,128)(2,1)}, bf16[136,1024]{1,0:T(8,128)(2,1)}, u32[]{:S(2)}, u32[]{:S(2)}) collective-permute-start(bf16[136,1024]{1,0:T(8,128)(2,1)} %collective-permute-done.38.refs_4_), channel_id=1, source_target_pairs={{0,4},{8,0},{16,8},{24,16},{28,24},{20,28},{12,20},{4,12},{1,5},{9... | collective-permute-start | bytes 835592 | tf_op jit(solution)/shard_map/ppermute | solution.py:496
  283.5 17.1 %collective-permute-start.41 = (bf16[256,1024]{1,0:T(8,128)(2,1)}, bf16[256,1024]{1,0:T(8,128)(2,1)}, u32[]{:S(2)}, u32[]{:S(2)}) collective-permute-start(bf16[256,1024]{1,0:T(8,128)(2,1)} %collective-permute-done.33.refs_2_), channel_id=1, source_target_pairs={{0,8},{8,16},{16,24},{24,28},{28,20},{20,12},{12,4},{4,0},{1,9},{9... | collective-permute-start | bytes 1572872 | tf_op jit(solution)/shard_map/ppermute | solution.py:496
  284.4 16.3 %collective-permute-start.43 = (bf16[256,1024]{1,0:T(8,128)(2,1)}, bf16[256,1024]{1,0:T(8,128)(2,1)}, u32[]{:S(2)}, u32[]{:S(2)}) collective-permute-start(bf16[256,1024]{1,0:T(8,128)(2,1)} %collective-permute-done.33.refs_2_), channel_id=1, source_target_pairs={{0,2},{2,0},{1,3},{3,1},{4,6},{6,4},{5,7},{7,5},{8,10},{10,8},{9,1... | collective-permute-start | bytes 1572872 | tf_op jit(solution)/shard_map/ppermute | solution.py:415
  286.6 14.1 %collective-permute-start.42 = (bf16[256,1024]{1,0:T(8,128)(2,1)}, bf16[256,1024]{1,0:T(8,128)(2,1)}, u32[]{:S(2)}, u32[]{:S(2)}) collective-permute-start(bf16[256,1024]{1,0:T(8,128)(2,1)} %collective-permute-done.34.refs_3_), channel_id=1, source_target_pairs={{0,4},{8,0},{16,8},{24,16},{28,24},{20,28},{12,20},{4,12},{1,5},{9... | collective-permute-start | bytes 1572872 | tf_op jit(solution)/shard_map/ppermute | solution.py:496
  291.0 9.7 %collective-permute-start.44 = (bf16[256,1024]{1,0:T(8,128)(2,1)}, bf16[256,1024]{1,0:T(8,128)(2,1)}, u32[]{:S(2)}, u32[]{:S(2)}) collective-permute-start(bf16[256,1024]{1,0:T(8,128)(2,1)} %collective-permute-done.34.refs_3_), channel_id=1, source_target_pairs={{0,2},{2,0},{1,3},{3,1},{4,6},{6,4},{5,7},{7,5},{8,10},{10,8},{9,1... | collective-permute-start | bytes 1572872 | tf_op jit(solution)/shard_map/ppermute | solution.py:415
  291.0 2.6 collective-permute-start.47
  293.6 7.0 %collective-permute-start.48 = (bf16[136,1024]{1,0:T(8,128)(2,1)}, bf16[136,1024]{1,0:T(8,128)(2,1)}, u32[]{:S(2)}, u32[]{:S(2)}) collective-permute-start(bf16[136,1024]{1,0:T(8,128)(2,1)} %collective-permute-done.38.refs_4_), channel_id=1, source_target_pairs={{0,2},{2,0},{1,3},{3,1},{4,6},{6,4},{5,7},{7,5},{8,10},{10,8},{9,1... | collective-permute-start | bytes 835592 | tf_op jit(solution)/shard_map/ppermute | solution.py:415
  301.4 20.9 %collective-permute-start.56 = (bf16[136,1024]{1,0:T(8,128)(2,1)S(1)}, bf16[136,1024]{1,0:T(8,128)(2,1)S(1)}, u32[]{:S(2)}, u32[]{:S(2)}) collective-permute-start(bf16[136,1024]{1,0:T(8,128)(2,1)S(1)} %collective-permute-done.45.refs_5_), channel_id=1, source_target_pairs={{0,2},{2,0},{1,3},{3,1},{4,6},{6,4},{5,7},{7,5},{8,10},{10,8},{9,1... | collective-permute-start | bytes 835592 | tf_op jit(solution)/shard_map/ppermute | solution.py:415
  301.8 21.1 %collective-permute-start.57 = (bf16[136,1024]{1,0:T(8,128)(2,1)}, bf16[136,1024]{1,0:T(8,128)(2,1)}, u32[]{:S(2)}, u32[]{:S(2)}) collective-permute-start(bf16[136,1024]{1,0:T(8,128)(2,1)} %collective-permute-done.46.refs_6_), channel_id=1, source_target_pairs={{0,2},{2,0},{1,3},{3,1},{4,6},{6,4},{5,7},{7,5},{8,10},{10,8},{9,1... | collective-permute-start | bytes 835592 | tf_op jit(solution)/shard_map/ppermute | solution.py:415
  305.0 23.9 %all-to-all-start.5 = ((bf16[32,32,128]{2,1,0:T(8,128)(2,1)}), bf16[32,32,128]{2,1,0:T(8,128)(2,1)S(1)}, u32[]{:S(2)}, u32[]{:S(2)}) async-start(bf16[32,32,128]{2,1,0:T(8,128)(2,1)} %broadcast_in_dim.55), calls=%async_computation.5 | async-start | bytes 524288 | tf_op jit(solution)/shard_map/all_to_all | solution.py:920
  309.3 27.6 %collective-permute-start.52 = (bf16[256,1024]{1,0:T(8,128)(2,1)}, bf16[256,1024]{1,0:T(8,128)(2,1)}, u32[]{:S(2)}, u32[]{:S(2)}) collective-permute-start(bf16[256,1024]{1,0:T(8,128)(2,1)} %collective-permute-done.41.refs_2_), channel_id=1, source_target_pairs={{0,2},{2,0},{1,3},{3,1},{4,6},{6,4},{5,7},{7,5},{8,10},{10,8},{9,1... | collective-permute-start | bytes 1572872 | tf_op jit(solution)/shard_map/ppermute | solution.py:415
  309.6 8.4 %collective-permute-start.54 = (bf16[136,512]{1,0:T(8,128)(2,1)}, bf16[136,512]{1,0:T(8,128)(2,1)S(1)}, u32[]{:S(2)}, u32[]{:S(2)}) collective-permute-start(bf16[136,512]{1,0:T(8,128)(2,1)} %slice.77), channel_id=1, source_target_pairs={{0,8},{8,16},{16,24},{24,28},{28,20},{20,12},{12,4},{4,0},{1,9},{9... | collective-permute-start | bytes 417800 | tf_op jit(solution)/shard_map/ppermute | solution.py:496
  311.3 8.2 %collective-permute-start.55 = (bf16[136,512]{1,0:T(8,128)(2,1)}, bf16[136,512]{1,0:T(8,128)(2,1)S(1)}, u32[]{:S(2)}, u32[]{:S(2)}) collective-permute-start(bf16[136,512]{1,0:T(8,128)(2,1)} %slice.78), channel_id=1, source_target_pairs={{0,4},{8,0},{16,8},{24,16},{28,24},{20,28},{12,20},{4,12},{1,5},{9... | collective-permute-start | bytes 417800 | tf_op jit(solution)/shard_map/ppermute | solution.py:496
  318.0 19.0 %collective-permute-start.53 = (bf16[256,1024]{1,0:T(8,128)(2,1)}, bf16[256,1024]{1,0:T(8,128)(2,1)}, u32[]{:S(2)}, u32[]{:S(2)}) collective-permute-start(bf16[256,1024]{1,0:T(8,128)(2,1)} %collective-permute-done.42.refs_3_), channel_id=1, source_target_pairs={{0,2},{2,0},{1,3},{3,1},{4,6},{6,4},{5,7},{7,5},{8,10},{10,8},{9,1... | collective-permute-start | bytes 1572872 | tf_op jit(solution)/shard_map/ppermute | solution.py:415
  319.5 17.4 %collective-permute-start.50 = (bf16[256,512]{1,0:T(8,128)(2,1)}, bf16[256,512]{1,0:T(8,128)(2,1)}, u32[]{:S(2)}, u32[]{:S(2)}) collective-permute-start(bf16[256,512]{1,0:T(8,128)(2,1)} %slice.75), channel_id=1, source_target_pairs={{0,8},{8,16},{16,24},{24,28},{28,20},{20,12},{12,4},{4,0},{1,9},{9... | collective-permute-start | bytes 786440 | tf_op jit(solution)/shard_map/ppermute | solution.py:496
  322.3 14.7 %collective-permute-start.51 = (bf16[256,512]{1,0:T(8,128)(2,1)}, bf16[256,512]{1,0:T(8,128)(2,1)}, u32[]{:S(2)}, u32[]{:S(2)}) collective-permute-start(bf16[256,512]{1,0:T(8,128)(2,1)} %slice.76), channel_id=1, source_target_pairs={{0,4},{8,0},{16,8},{24,16},{28,24},{20,28},{12,20},{4,12},{1,5},{9... | collective-permute-start | bytes 786440 | tf_op jit(solution)/shard_map/ppermute | solution.py:496
  323.0 5.9 %collective-permute-start.58 = (bf16[136,1024]{1,0:T(8,128)(2,1)S(1)}, bf16[136,1024]{1,0:T(8,128)(2,1)S(1)}, u32[]{:S(2)}, u32[]{:S(2)}) collective-permute-start(bf16[136,1024]{1,0:T(8,128)(2,1)S(1)} %pad_maximum_fusion.3.refs_7_), channel_id=1, source_target_pairs={{0,2},{2,0},{1,3},{3,1},{4,6},{6,4},{5,7},{7,5},{8,10},{10,8},{9,1... | collective-permute-start | bytes 835592 | tf_op jit(solution)/shard_map/ppermute | solution.py:415
  338.1 7.0 %collective-permute-start.59 = (bf16[256,1024]{1,0:T(8,128)(2,1)S(1)}, bf16[256,1024]{1,0:T(8,128)(2,1)S(1)}, u32[]{:S(2)}, u32[]{:S(2)}) collective-permute-start(bf16[256,1024]{1,0:T(8,128)(2,1)S(1)} %pad_maximum_fusion.1.refs_2_), channel_id=1, source_target_pairs={{0,2},{2,0},{1,3},{3,1},{4,6},{6,4},{5,7},{7,5},{8,10},{10,8},{9,1... | collective-permute-start | bytes 1572872 | tf_op jit(solution)/shard_map/ppermute | solution.py:415
  (50 other events, 595.6 us)

commit v11 on v10

--- a/solution.py
+++ b/solution.py
@@ -15,7 +15,7 @@
 masked_value = -1e30
 seg_row = 3 * HD
 payload_rows = 3 * HD + 16
-small_rows = 8
+small_rows = 16
 params = pltpu.CompilerParams(vmem_limit_bytes=48 * 2**20)
 streaming = pltpu.CompilerParams(vmem_limit_bytes=60 * 2**20)
 
@@ -55,9 +55,9 @@
 
 
 def project_kernel(
-    input_ref, segment_ref, steps_ref, gain, shift, lead_weight, *refs
+    table, input_ref, segment_ref, steps_ref, gain, shift, lead_weight, *refs
 ):
-    weights, (payload_ref, attn_in_ref) = refs[:3], refs[3:]
+    weights, (payload_ref, attn_in_ref, cut_ref) = refs[:3], refs[3:]
     rows = input_ref.shape[0]
 
     @pl.when(pl.program_id(0) == 0)
@@ -71,7 +71,11 @@
         steps = jnp.where(crop == segment_ref[...], steps, 0).astype(F32)
         lead = product(steps, jnp.ones((crops, 128), F32), 0, 0)[:, :1] / 12.0
         attn_in = unit * gain[...] + shift[...] + lead * lead_weight[...]
-        attn_in_ref[...] = attn_in.astype(BF16)
+        attn_in = attn_in.astype(BF16)
+        attn_in_ref[...] = attn_in
+        columns = cut_ref.shape[1]
+        first = table[table.shape[0] - 1] % (attn_in.shape[1] // columns) == 0
+        cut_ref[...] = jnp.where(first, attn_in[:, :columns], attn_in[:, -columns:])
 
     for at, weight in enumerate(weights):
         part = product(attn_in_ref[...], weight[...]).T.astype(BF16)
@@ -82,26 +86,38 @@
         payload_ref[head, pl.ds(seg_row, 16), :] = segment
 
 
-def project(block_input, segments, lead_steps, gain, shift, lead_weight, weights):
+def project(table, cut, block_input, segments, lead_steps, gain, shift, lead_weight, weights):
     rows, model = block_input.shape
     heads = weights[0].shape[1] // HD
     line = whole_spec((1, model))
-    column = pl.BlockSpec((model, 2 * HD), lambda at: (0, at))
+    column = pl.BlockSpec((model, 2 * HD), lambda at, table: (0, at))
     return pl.pallas_call(
         project_kernel,
-        grid=(heads // 2,),
-        in_specs=[whole_spec(block_input.shape), whole_spec((1, rows)), pl.BlockSpec(memory_space=pltpu.SMEM)]
-        + [line] * 3
-        + [column] * 3,
-        out_specs=[
-            pl.BlockSpec((2, payload_rows, rows), lambda at: (at, 0, 0)),
-            whole_spec((rows, model)),
+        grid_spec=pltpu.PrefetchScalarGridSpec(
+            num_scalar_prefetch=1,
+            grid=(heads // 2,),
+            in_specs=[
+                whole_spec(block_input.shape),
+                whole_spec((1, rows)),
+                pl.BlockSpec(memory_space=pltpu.SMEM),
+            ]
+            + [line] * 3
+            + [column] * 3,
+            out_specs=[
+                pl.BlockSpec((2, payload_rows, rows), lambda at, table: (at, 0, 0)),
+                whole_spec((rows, model)),
+                whole_spec((rows, cut)),
+            ],
+        ),
+        out_shape=[
+            struct((heads, payload_rows, rows), BF16),
+            struct((rows, model), BF16),
+            struct((rows, cut), BF16),
         ],
-        out_shape=[struct((heads, payload_rows, rows), BF16), struct((rows, model), BF16)],
         compiler_params=streaming,
         cost_estimate=light,
         name="project",
-    )(block_input, segments[None], lead_steps, gain[None], shift[None], lead_weight[None], *weights)
+    )(table, block_input, segments[None], lead_steps, gain[None], shift[None], lead_weight[None], *weights)
 
 
 def mlp_kernel(count, core_ref, input_ref, grad_ref, *refs):
@@ -474,6 +490,44 @@
     return values
 
 
+def join_kernel(*refs):
+    start = 0
+    for block in refs[:-1]:
+        refs[-1][pl.ds(start, block.shape[0]), :] = block[...]
+        start += block.shape[0]
+
+
+def join(blocks):
+    rows = sum(block.shape[0] for block in blocks)
+    return pl.pallas_call(
+        join_kernel,
+        out_shape=struct((rows, blocks[0].shape[1]), blocks[0].dtype),
+        compiler_params=streaming,
+        name="join",
+    )(*blocks)
+
+
+def halves_kernel(left, right, left_ref, right_ref):
+    left_ref[...] = left[...]
+    right_ref[...] = right[...]
+
+
+def halves(left, right):
+    rows, columns = left.shape
+    if rows % 16 or columns % 256:
+        return [left[:, : columns // 2], right[:, columns // 2 :]]
+    out = pl.BlockSpec((rows, columns // 2), lambda at: (0, 0))
+    return pl.pallas_call(
+        halves_kernel,
+        grid=(1,),
+        in_specs=[out, pl.BlockSpec((rows, columns // 2), lambda at: (0, 1))],
+        out_specs=[out, out],
+        out_shape=[struct((rows, columns // 2), left.dtype)] * 2,
+        compiler_params=streaming,
+        name="halves",
+    )(left, right)
+
+
 class Gather:
     def __init__(self, block, swap=False, take=None):
         self.reach, self.swap, self.take = lax.axis_size("chip") // 2, swap, take
@@ -488,8 +542,7 @@
         self.count += 1
         sides = ready if len(ready) > 1 else ready * 2
         if self.count == self.reach:
-            half = ready[0].shape[1] // 2
-            sides = [sides[0][:, :half], sides[1][:, half:]]
+            sides = halves(*sides)
         flying = []
         if self.count <= self.reach:
             flying = [
@@ -537,16 +590,11 @@
         self.operands, self.sides = (keep, far), (keep_in, far_in)
         self.units = keep.shape[1] // self.chips
         self.tiled = self.units % 128 == 0
-        self.left, self.gather = self.chips // 2, None
+        self.left, self.rest = self.chips // 2, None
         (block,) = self.add([(self.left, [])])
-        half = block.shape[1] // 2
-        self.send([block[:, :half], block[:, half:]])
+        self.send(halves(block, block))
 
     def send(self, ready):
-        if self.gather:
-            self.gather.send(ready)
-            self.state = self.gather.state
-            return
         self.left -= 1
         self.state = [
             lax.ppermute(block, "chip", ring_pairs(direction))
@@ -554,20 +602,15 @@
         ]
 
     def advance(self, state):
-        if self.gather:
-            self.gather.advance(state)
-            self.ready = self.gather.ready
-            return
         half = self.sides[0].shape[1] // 2
         ahead, behind = state
         first = 0 if ahead.shape[1] != half else half
-        if self.left:
-            wanted = [(self.left, [(ahead, 0)]), (-self.left, [(behind, first)])]
-        else:
-            wanted = [(0, [(ahead, 0), (behind, first)])]
-        self.ready = self.add(wanted)
-        if not self.left:
-            self.gather = Gather(self.ready[0], True, self.place)
+        self.ready = self.add([(self.left, [(ahead, 0)]), (-self.left, [(behind, first)])])
+
+    def finish(self, values):
+        (ahead, behind), values = lax.optimization_barrier((self.state, values))
+        (total,) = self.add([(0, [(ahead, 0), (behind, 0)])])
+        return total, values
 
     def add(self, wanted):
         (rows, model), units, chips = self.sides[0].shape, self.units, self.chips
@@ -616,6 +659,7 @@
             is_down = self.table[2 * chips] == 0
             for step, near, far in pairs:
                 start = self.table[step % chips] * units
+                near, far = near[:units], far[:units]
                 first = jnp.where(is_down, near, far).astype(F32)
                 second = jnp.where(is_down, far, near).astype(F32).T
                 down = lax.dynamic_update_slice_in_dim(down, first, start, 0)
@@ -643,9 +687,6 @@
             name="place",
         )(self.table, *outputs, *[pair[1] for pair in pairs], *[pair[2] for pair in pairs])
 
-    def busy(self):
-        return self.gather is None or self.gather.busy()
-
 
 def place_kernel(count, table, *refs):
     nears, fars, (down, up) = refs[-2 - 2 * count : -2 - count], refs[-2 - count : -2], refs[-2:]
@@ -704,14 +745,10 @@
 
 def layout_kernel(steps, size, extra, table, *refs):
     count = len(steps)
-    nears, fars, outputs, output_ref, small_ref, held = (
-        refs[:count],
-        refs[count : 2 * count],
-        refs[2 * count : 2 * count + 3],
-        refs[2 * count + 3],
-        refs[2 * count + 4],
-        refs[2 * count + 5],
-    )
+    blocks, refs = refs[: 4 * count], refs[4 * count :]
+    nears = list(zip(blocks[:count], blocks[2 * count : 3 * count]))
+    fars = list(zip(blocks[count : 2 * count], blocks[3 * count :]))
+    outputs, (output_ref, small_ref, held) = refs[:3], refs[3:]
     at = pl.program_id(0)
 
     @pl.when(at == 0)
@@ -719,10 +756,10 @@
         core = table[2 * count]
         for step, near, far in zip(steps, nears, fars):
             chip = table[count + step % count]
-            for side, block in ((core, near), (1 - core, far)):
+            for side, (block, small) in ((core, near), (1 - core, far)):
                 held[chip, side] = block[pl.ds(0, size), :]
                 output_ref[side, chip] = block[pl.ds(size, extra), :].astype(F32)
-                small_ref[side, chip] = block[pl.ds(size + extra, small_rows), :].astype(F32)
+                small_ref[side, chip] = small[...].astype(F32)
 
     pair = [
         jnp.concatenate([held[2 * at + head, 0], held[2 * at + head, 1]], axis=0)
@@ -733,17 +770,19 @@
         output[...] = jnp.concatenate(rows, axis=0).astype(F32).T
 
 
-def final_layout(pairs, size, table):
+def final_layout(pairs, start, size, table):
     count = len(pairs)
     steps, nears, fars = zip(*pairs)
     rows, model = nears[0].shape
-    extra = rows - size - small_rows
+    extra = rows - start - size - small_rows
+    part = pl.BlockSpec((size + extra, model), lambda at, table: (start // (size + extra), 0))
+    last = pl.BlockSpec((small_rows, model), lambda at, table: (rows // small_rows - 1, 0))
     return pl.pallas_call(
         functools.partial(layout_kernel, steps, size, extra),
         grid_spec=pltpu.PrefetchScalarGridSpec(
             num_scalar_prefetch=1,
             grid=(count // 2,),
-            in_specs=[pl.BlockSpec((rows, model), lambda at, table: (0, 0))] * (2 * count),
+            in_specs=[part] * (2 * count) + [last] * (2 * count),
             out_specs=[pl.BlockSpec((model, 2 * HD), lambda at, table: (0, at))] * 3
             + [
                 pl.BlockSpec((2, count, extra, model), lambda at, table: (0, 0, 0, 0)),
@@ -759,7 +798,7 @@
         compiler_params=streaming,
         cost_estimate=light,
         name="final_layout",
-    )(table, *nears, *fars)
+    )(table, *nears, *fars, *nears, *fars)
 
 
 def core_half(values, axis, side):
@@ -800,8 +839,9 @@
     crops = lead_steps.shape[0]
     table = ring_table()
     weights = (query_weight, key_weight, value_weight)
-    payload, attn_in = project(
-        block_input, segments, lead_steps, gain_attn, shift_attn, lead_weight, weights
+    cut = model // 2 if lax.axis_size("head") == 2 else model
+    payload, attn_in, attn_in_cut = project(
+        table, cut, block_input, segments, lead_steps, gain_attn, shift_attn, lead_weight, weights
     )
     if split == 1:
         own = to_heads(payload)
@@ -809,11 +849,8 @@
     else:
         queries = scatter_queries(payload.reshape(-1, rows), heads, split)
         own = to_heads(jnp.repeat(payload, split, axis=0))
-    own, attn_in = lax.optimization_barrier((own, attn_in))
-    cut = model // 2 if lax.axis_size("head") == 2 else model
-    inputs = Gather(
-        lax.dynamic_slice_in_dim(attn_in, lax.axis_index("head") * cut % model, cut, 1)
-    )
+    own, attn_in_cut = lax.optimization_barrier((own, attn_in_cut))
+    inputs = Gather(attn_in_cut)
     inputs.send(inputs.ready)
     other = swap_cores(own)
     raw, out, logsum = attention_forward(queries, own, other, crops)
@@ -842,7 +879,7 @@
     while inputs.busy():
         visit([inputs], ())
     steps, inputs = zip(*inputs.blocks)
-    inputs = jnp.concatenate(inputs, axis=0)
+    inputs = join(inputs)
     mlp_part, inputs, d_mlp = lax.optimization_barrier((mlp_part, inputs, d_mlp))
     parts = [inputs]
     if cut != model:
@@ -854,6 +891,7 @@
     out_near, out_far = share_halves(attn_out, 0)
     doutput = product(out_near, d_branch) + product(out_far, swap_cores(d_branch))
     doutput = to_heads(doutput.astype(BF16).reshape(chips, -1, model))
+    grads = visit([ring], grads)
     *dquery, far_sums = backward_piece(
         queries, grads, raw, logsum, [], other, [], 0, 1, crops, (F32, BF16)
     )
@@ -862,11 +900,6 @@
     *dquery, near_sums = backward_piece(
         queries, grads, raw, logsum, dquery, own, [], 0, 1, crops, (BF16, F32)
     )
-    near_sums, dquery, mlp_out = visit([ring], (near_sums, dquery, mlp_out))
-    block_output = hidden + down_bias
-    for part in mlp_out:
-        block_output += part.astype(F32)
-    block_output = block_output.astype(BF16)
     (dquery,) = dquery
     key_value = (near_sums + far_sums.astype(F32)).astype(BF16)
     doutput, key_value = lax.optimization_barrier((doutput, key_value))
@@ -894,15 +927,16 @@
             lax.psum(product(attn_in, grad, 0, 1).astype(BF16), ("chip", "core")).astype(F32)
             for grad in (dquery, dkey, dvalue)
         ]
-    gathered = Gather(blocks, True)
+    total, blocks = ring.finish(blocks)
+    start = total.shape[0]
+    gathered = Gather(jnp.concatenate([total, blocks], axis=0), True, ring.place)
     gathered.send(gathered.ready)
-    visit([ring], blocks)
     d_part = (
         product(dquery, query_weight, 0, 1)
         + product(dkey, key_weight, 0, 1)
         + product(dvalue, value_weight, 0, 1)
     )
-    d_part = visit([ring, gathered], d_part)
+    d_part = visit([gathered], d_part)
     d_in = across_heads(d_part.astype(BF16))
     unit_attn, inverse_attn = normalize(block_input.astype(F32))
     onehot = (segments[:, None] == jnp.arange(crops, dtype=jnp.int32)[None, :]).astype(F32)
@@ -918,29 +952,30 @@
     everyone = ("chip", "core", "head")
     ends = jnp.broadcast_to(ends, (lax.axis_size(everyone),) + ends.shape)
     ends = lax.all_to_all(ends, everyone, 0, 0, tiled=True)
-    visit([ring, gathered], ())
-    d_in = visit([ring, gathered], d_in)
+    visit([gathered], ())
+    d_in, mlp_out = visit([gathered], (d_in, mlp_out))
+    block_output = hidden + down_bias
+    for part in mlp_out:
+        block_output += part.astype(F32)
+    block_output = block_output.astype(BF16)
     d_in = functools.reduce(jnp.add, (part.astype(F32) for part in d_in))
     input_grad = (d_hidden + normalize_back(d_in * gain_attn, unit_attn, inverse_attn)).astype(
         BF16
     )
     while gathered.busy():
         visit([gathered], ())
+    ddown_weight, dup_weight = gathered.outputs
     ends = jnp.sum(ends.astype(F32), axis=0).reshape(-1)[: 3 * model].reshape(3, model)
     if split == 1:
-        layout = final_layout(gathered.pairs, size, table)
-        *projections, doutput_weight, small = visit([ring], layout)
+        *projections, doutput_weight, small = final_layout(gathered.pairs, start, size, table)
         doutput_weight = doutput_weight.reshape(width, model)
-    while ring.busy():
-        visit([ring], ())
-    ddown_weight, dup_weight = ring.state[2]
     if split != 1:
         blocks = jnp.zeros((2, chips) + blocks.shape, F32)
         for step, near, far in gathered.pairs:
-            for side, block in ((core, near), (1 - core, far)):
-                start = (side, table[chips + step % chips], 0, 0)
+            for side, block in ((core, near[start:]), (1 - core, far[start:])):
+                at = (side, table[chips + step % chips], 0, 0)
                 block = block[None, None].astype(F32)
-                blocks = lax.dynamic_update_slice(blocks, block, start)
+                blocks = lax.dynamic_update_slice(blocks, block, at)
         doutput_weight = blocks[:, :, :-small_rows].reshape(width, model)
         small = blocks[:, :, -small_rows:]
     small = jnp.sum(small, axis=(0, 1))

time: 351 us -> 342 us (0.974)
  starting transfers between devices: 73.8 us -> 60.5 us
  local copies, waits for them, and re-layouts: 23.8 us -> 13.7 us
  Pallas kernels: 113 us -> 122 us
    ppermute x32 -> x24, starting transfers between devices: 40.1 us -> 29.2 us  [send(): lax.ppermute(block, 'chip', ring_pairs(direction))]
    ppermute x5, waiting for transfers between devices: 20.4 us -> 10.1 us  [across_heads(): return [part, lax.ppermute(part, 'head', [(0, 1), (1, 0)])]]
    pallas_call x1 -> x5, Pallas kernels: 5.95 us -> 15.4 us  [the longest x1 6.64 us: project(): pl.pallas_call(project_kernel, grid_spec=pltpu.PrefetchScalarGridSpec(num...]
    all_to_all x4, waiting for transfers between devices: 4.08 us -> 12.3 us  [to_heads(): return lax.all_to_all(blocks, 'chip', 0, 0, tiled=True)]
    ppermute x32 -> x24, waiting for transfers between devices: 62.1 us -> 69.7 us  [send(): lax.ppermute(block, 'chip', ring_pairs(direction))]
    slice x7 -> x0, local copies, waits for them, and re-layouts: 6.69 us -> none  [the longest x6 5.59 us: send(): sides = [sides[0][:, :half], sides[1][:, half:]]]
    unnamed x108 -> x101, local copies, waits for them, and re-layouts: 14.1 us -> 9.5 us
  transfers between devices with their start and end apart: 65 -> 49, of which waited for: 22 -> 21; matrix products, arithmetic and copies ran while one was open for 9% -> 5% of each run, Pallas kernels for 29% -> 29%
where the time goes in v11:
time: 342 us; the launch traced here: 340 us
  Pallas kernels  122 us (36%)
  waiting for transfers between devices  94.9 us (28%)
  starting transfers between devices  60.5 us (18%)
  blocking collectives  29.6 us (9%)
  local copies, waits for them, and re-layouts  13.7 us (4%)
  other arithmetic  13.6 us (4%)
  matrix products  4.35 us (1%)
    ppermute x24, waiting for transfers between devices, send(): lax.ppermute(block, 'chip', ring_pairs(direction))  69.7 us
    all_to_all x1, blocking collectives, to_heads(): return lax.all_to_all(blocks, 'chip', 0, 0, tiled=True)  29.6 us
    ppermute x24, starting transfers between devices, send(): lax.ppermute(block, 'chip', ring_pairs(direction))  29.2 us
    pallas_call x2, Pallas kernels, backward_piece(): pl.pallas_call(functools.partial(backward_kernel, crops, len(before)), gr...  24 us
    pallas_call x5, Pallas kernels, place(): pl.pallas_call(functools.partial(place_kernel, len(pairs)), grid_spec=plt...  20.6 us
    all_to_all x4, starting transfers between devices, to_heads(): return lax.all_to_all(blocks, 'chip', 0, 0, tiled=True)  18.5 us
    pallas_call x5, Pallas kernels, add(): pl.pallas_call(functools.partial(add_kernel, [[start for _, start in part...  18.2 us
    pallas_call x1, Pallas kernels, attention_forward(): pl.pallas_call(functools.partial(forward_kernel, crops, key_step(count)),...  15.3 us
  transfers between devices with their start and end apart: 49, of which 21 were waited for; matrix products, arithmetic and copies ran while one was open for 5% of the time, Pallas kernels for 29%

profile of v11, /device:TPU:0, one launch (start us, length us, event | category | flops | bytes accessed | tf_op | source)
XLA Modules:
  0.0 339.9 jit_solution(6066943365862195491)
XLA Ops:
  1.2 6.6 %project.1 = (bf16[8,208,256]{2,1,0:T(8,128)(2,1)}, bf16[256,1024]{1,0:T(8,128)(2,1)}, bf16[256,512]{1,0:T(8,128)(2,1)}) custom-call(s32[18]{0:T(128)} %compare_select_fusion.5.table.core_ref._, bf16[256,1024]{1,0:T(8,128)(2,1)} %input_ref.3, s32[1,256]{1,0:T(1,128)} %bitcast.66, s32[32]{0:T(128)} %steps_ref.1, f32[1,1024]{1,0:T(1,128)} %bitcast.52, ...), custom_call_target="tpu_custom_call" | custom-call | flops 1 | bytes 1 | tf_op jit(solution)/shard_map/project/pallas_call | solution.py:94
  7.8 29.6 %all_to_all.30.query_ref.own.refs_1_ = bf16[8,208,256]{2,1,0:T(8,128)(2,1)S(1)} all-to-all(bf16[8,208,256]{2,1,0:T(8,128)(2,1)} %get-tuple-element.162), channel_id=1, replica_groups=mesh['chip'=8,'core'=2,'head'=2] {'chip'}, dimensions={0} | all-to-all | bytes 1703936 | tf_op jit(solution)/shard_map/all_to_all | solution.py:435
  38.2 1.3 collective-permute-start.1
  40.7 15.3 %attention_forward.1 = (f32[8,64,256]{2,1,0:T(8,128)}, bf16[8,64,256]{2,1,0:T(8,128)(2,1)}, f32[8,1,256]{2,1,0:T(1,128)}) custom-call(bf16[8,208,256]{2,1,0:T(8,128)(2,1)} %copy-done, bf16[8,208,256]{2,1,0:T(8,128)(2,1)} %copy-done, bf16[8,208,256]{2,1,0:T(8,128)(2,1)} %copy-done.2), custom_call_target="tpu_custom_call" | custom-call | flops 1 | bytes 1 | tf_op jit(solution)/shard_map/attention_forward/pallas_call | solution.py:367
  56.0 3.4 %all-to-all-start.1 = ((bf16[8,64,256]{2,1,0:T(8,128)(2,1)}), bf16[8,64,256]{2,1,0:T(8,128)(2,1)S(1)}, u32[]{:S(2)}, u32[]{:S(2)}) async-start(bf16[8,64,256]{2,1,0:T(8,128)(2,1)} %get-tuple-element.169), calls=%async_computation.1 | async-start | bytes 524288 | tf_op jit(solution)/shard_map/all_to_all | solution.py:435
  59.5 1.9 collective-permute-start.3
  61.5 9.2 %collective-permute-done.3.refs_3_ = bf16[256,512]{1,0:T(8,128)(2,1)S(1)} collective-permute-done((bf16[256,512]{1,0:T(8,128)(2,1)S(1)}, bf16[256,512]{1,0:T(8,128)(2,1)S(1)}, u32[]{:S(2)}, u32[]{:S(2)}) %collective-permute-start.3) | collective-permute-done | bytes 262176 | tf_op jit(solution)/shard_map/ppermute | solution.py:549
  70.7 1.5 collective-permute-done.4.refs_4_
  72.7 1.6 collective-permute-start.7
  74.3 2.7 collective-permute-start.5
  77.1 4.9 %collective-permute-done.5.left.refs_5_ = bf16[256,512]{1,0:T(8,128)(2,1)S(1)} collective-permute-done((bf16[256,512]{1,0:T(8,128)(2,1)S(1)}, bf16[256,512]{1,0:T(8,128)(2,1)S(1)}, u32[]{:S(2)}, u32[]{:S(2)}) %collective-permute-start.5) | collective-permute-done | bytes 262176 | tf_op jit(solution)/shard_map/ppermute | solution.py:549
  82.0 2.0 collective-permute-done.6.right.refs_6_
  84.0 2.3 collective-permute-done.7.refs_1_
  86.3 1.9 halves.3
  88.2 2.4 collective-permute-start.8
  90.6 11.7 %mlp.1 = (bf16[256,2048]{1,0:T(8,128)(2,1)}, bf16[256,2048]{1,0:T(8,128)(2,1)}, bf16[256,1024]{1,0:T(8,128)(2,1)}, bf16[256,1024]{1,0:T(8,128)(2,1)}, f32[256,10...) custom-call(s32[18]{0:T(128)} %compare_select_fusion.5.table.core_ref._, ...), custom_call_target="tpu_custom_call" | custom-call | flops 1 | bytes 1 | tf_op jit(solution)/shard_map/mlp/pallas_call | solution.py:174
  103.6 1.5 collective-permute-start.14
  105.1 1.7 collective-permute-done.10.refs_1_
  108.5 3.2 ring_add.5.left.right
  111.7 1.9 halves.4
  113.5 2.0 collective-permute-start.12
  115.5 3.0 join.1.refs_0_
  119.3 4.3 %middle.1 = (f32[256,1024]{1,0:T(8,128)}, bf16[256,1024]{1,0:T(8,128)(2,1)}, bf16[512,256]{1,0:T(8,128)(2,1)}, f32[4,1024]{1,0:T(4,128)}) custom-call(f32[256,1024]{1,0:T(8,128)} %get-tuple-element.175.hidden_ref, bf16[256,1024]{1,0:T(8,128)(2,1)} %grad_ref.3, bf16[256,1024]{1,0:T(8,128)(2,1)} %get-tuple-element.201.refs_0_, bf16[256,1024]{1,0:T(8,128)(2,1)} %copy-done.34, ...), custom_call_target="tpu_custom_call" | custom-call | flops 1 | bytes 1 | tf_op jit(solution)/shard_map/middle/pallas_call | solution.py:235
  124.5 3.7 %ring_add.6 = (bf16[256,1024]{1,0:T(8,128)(2,1)}, bf16[256,1024]{1,0:T(8,128)(2,1)}) custom-call(s32[18]{0:T(128)} %compare_select_fusion.5.table.core_ref._, bf16[256,1024]{1,0:T(8,128)(2,1)} %get-tuple-element.192.refs_0_, bf16[256,1024]{1,0:T(8,128)(2,1)} %copy-done.9, bf16[256,2048]{1,0:T(8,128)(2,1)} %get-tuple-element.194.refs_2_.refs_5_, ...), custom_call_target="tpu_custom_call" | custom-call | flops 1 | bytes 1 | tf_op jit(solution)/shard_map/ring_add/pallas_call | solution.py:639
  128.2 1.9 collective-permute-start.15
  130.2 4.7 %all-to-all-start.2 = ((bf16[8,64,256]{2,1,0:T(8,128)(2,1)}), bf16[8,64,256]{2,1,0:T(8,128)(2,1)S(1)}, u32[]{:S(2)}, u32[]{:S(2)}) async-start(bf16[8,64,256]{2,1,0:T(8,128)(2,1)} %bitcast.9), calls=%async_computation.2 | async-start | bytes 524288 | tf_op jit(solution)/shard_map/all_to_all | solution.py:435
  135.5 1.4 collective-permute-start.24
  137.0 12.3 %all-to-all-done.2.grad_ref = bf16[8,64,256]{2,1,0:T(8,128)(2,1)S(1)} async-done(((bf16[8,64,256]{2,1,0:T(8,128)(2,1)}), bf16[8,64,256]{2,1,0:T(8,128)(2,1)S(1)}, u32[]{:S(2)}, u32[]{:S(2)}) %all-to-all-start.2) | async-done | bytes 262176 | tf_op jit(solution)/shard_map/all_to_all | solution.py:435
  150.9 3.9 %ring_add.7 = (bf16[256,1024]{1,0:T(8,128)(2,1)}, bf16[256,1024]{1,0:T(8,128)(2,1)}) custom-call(s32[18]{0:T(128)} %compare_select_fusion.5.table.core_ref._, bf16[256,1024]{1,0:T(8,128)(2,1)} %get-tuple-element.192.refs_0_, bf16[256,1024]{1,0:T(8,128)(2,1)} %copy-done.9, bf16[256,2048]{1,0:T(8,128)(2,1)} %get-tuple-element.194.refs_2_.refs_5_, ...), custom_call_target="tpu_custom_call" | custom-call | flops 1 | bytes 1 | tf_op jit(solution)/shard_map/ring_add/pallas_call | solution.py:639
  155.5 1.4 collective-permute-start.18
  156.9 1.3 fusion.14
  159.4 4.3 %all-to-all-start.3 = ((bf16[8,32,1024]{2,1,0:T(8,128)(2,1)}), bf16[8,32,1024]{2,1,0:T(8,128)(2,1)}, u32[]{:S(2)}, u32[]{:S(2)}) async-start(bf16[8,32,1024]{2,1,0:T(8,128)(2,1)} %bitcast.10), calls=%async_computation.3 | async-start | bytes 1048576 | tf_op jit(solution)/shard_map/all_to_all | solution.py:435
  163.7 11.9 %attention_backward.2 = (f32[8,64,256]{2,1,0:T(8,128)S(1)}, bf16[8,128,256]{2,1,0:T(8,128)(2,1)S(1)}) custom-call(bf16[8,208,256]{2,1,0:T(8,128)(2,1)S(1)} %copy-done.1, bf16[8,64,256]{2,1,0:T(8,128)(2,1)S(1)} %all-to-all-done.2.grad_ref, f32[8,64,256]{2,1,0:T(8,128)S(1)} %copy-done.4, f32[8,1,256]{2,1,0:T(1,128)S(1)} %copy-done.6, ...), custom_call_target="tpu_custom_call" | custom-call | flops 1 | bytes 1 | tf_op jit(solution)/shard_map/attention_backward/pallas_call | solution.py:397
  175.7 3.9 %ring_add.8 = (bf16[256,1024]{1,0:T(8,128)(2,1)}, bf16[256,1024]{1,0:T(8,128)(2,1)}) custom-call(s32[18]{0:T(128)} %compare_select_fusion.5.table.core_ref._, bf16[256,1024]{1,0:T(8,128)(2,1)} %get-tuple-element.192.refs_0_, bf16[256,1024]{1,0:T(8,128)(2,1)} %copy-done.9, bf16[256,2048]{1,0:T(8,128)(2,1)} %get-tuple-element.194.refs_2_.refs_5_, ...), custom_call_target="tpu_custom_call" | custom-call | flops 1 | bytes 1 | tf_op jit(solution)/shard_map/ring_add/pallas_call | solution.py:639
  179.6 12.0 %attention_backward.3 = (bf16[8,64,256]{2,1,0:T(8,128)(2,1)S(1)}, f32[8,128,256]{2,1,0:T(8,128)S(1)}) custom-call(bf16[8,208,256]{2,1,0:T(8,128)(2,1)S(1)} %copy-done.1, bf16[8,64,256]{2,1,0:T(8,128)(2,1)S(1)} %all-to-all-done.2.grad_ref, f32[8,64,256]{2,1,0:T(8,128)S(1)} %copy-done.4, f32[8,1,256]{2,1,0:T(1,128)S(1)} %copy-done.6, ...), custom_call_target="tpu_custom_call" | custom-call | flops 1 | bytes 1 | tf_op jit(solution)/shard_map/attention_backward/pallas_call | solution.py:397
  192.8 6.0 %all-to-all-start.4 = ((bf16[8,192,256]{2,1,0:T(8,128)(2,1)}), bf16[8,192,256]{2,1,0:T(8,128)(2,1)}, u32[]{:S(2)}, u32[]{:S(2)}) async-start(bf16[8,192,256]{2,1,0:T(8,128)(2,1)} %pad_maximum_fusion.2), calls=%async_computation.4 | async-start | bytes 1572864 | tf_op jit(solution)/shard_map/all_to_all | solution.py:435
  198.9 2.1 collective-permute-start.19
  201.1 5.0 %head_gradient.1 = bf16[192,1024]{1,0:T(8,128)(2,1)} custom-call(s32[18]{0:T(128)} %compare_select_fusion.5.table.core_ref._, bf16[8,64,256]{2,1,0:T(8,128)(2,1)} %copy-done.5, bf16[8,128,256]{2,1,0:T(8,128)(2,1)} %copy-done.19, bf16[2048,512]{1,0:T(8,128)(2,1)} %join.1.refs_0_, bf16[2048,512]{1,0:T(8,128)(2,1)} %collective-permute-done.24.refs_1_), custom_call_target="tpu_custom_call" | custom-call | flops 1 | bytes 1 | tf_op jit(solution)/shard_map/head_gradient/pallas_call | solution.py:728
  209.5 14.7 %collective-permute-done.19.refs_4_ = bf16[256,1024]{1,0:T(8,128)(2,1)S(1)} collective-permute-done((bf16[256,1024]{1,0:T(8,128)(2,1)S(1)}, bf16[256,1024]{1,0:T(8,128)(2,1)S(1)}, u32[]{:S(2)}, u32[]{:S(2)}) %collective-permute-start.19) | collective-permute-done | bytes 524320 | tf_op jit(solution)/shard_map/ppermute | solution.py:600
  224.2 1.5 collective-permute-done.20.refs_5_
  226.5 3.5 %ring_add.9 = bf16[256,1024]{1,0:T(8,128)(2,1)} custom-call(s32[18]{0:T(128)} %compare_select_fusion.5.table.core_ref._, bf16[256,1024]{1,0:T(8,128)(2,1)} %get-tuple-element.192.refs_0_, bf16[256,1024]{1,0:T(8,128)(2,1)} %copy-done.9, bf16[256,2048]{1,0:T(8,128)(2,1)} %get-tuple-element.194.refs_2_.refs_5_, bf16[256,2048]{1,0:T(8,128)(2,1)} %copy-done.7, ...), custom_call_target="tpu_custom_call" | custom-call | flops 1 | bytes 1 | tf_op jit(solution)/shard_map/ring_add/pallas_call | solution.py:639
  231.3 5.8 %collective-permute-start.26 = (bf16[400,1024]{1,0:T(8,128)(2,1)S(1)}, bf16[400,1024]{1,0:T(8,128)(2,1)}, u32[]{:S(2)}, u32[]{:S(2)}) collective-permute-start(bf16[400,1024]{1,0:T(8,128)(2,1)S(1)} %pad_maximum_fusion.refs_0_.refs_16_), channel_id=1, source_target_pairs={{0,8},{8,16},{16,24},{24,28},{28,20},{20,12},{12,4},{4,0},{1,9},{9... | collective-permute-start | bytes 2457608 | tf_op jit(solution)/shard_map/ppermute | solution.py:549
  240.6 13.5 %collective-permute-done.26.refs_2_.refs_1_.refs_17_ = bf16[400,1024]{1,0:T(8,128)(2,1)} collective-permute-done((bf16[400,1024]{1,0:T(8,128)(2,1)S(1)}, bf16[400,1024]{1,0:T(8,128)(2,1)}, u32[]{:S(2)}, u32[]{:S(2)}) %collective-permute-start.26) | collective-permute-done | bytes 819232 | tf_op jit(solution)/shard_map/ppermute | solution.py:549
  254.1 2.8 collective-permute-done.27.refs_3_.refs_2_.refs_18_
  256.9 1.7 collective-permute-start.29
  259.5 1.5 collective-permute-start.38
  260.9 3.4 %place.5 = (f32[2048,1024]{1,0:T(8,128)}, f32[1024,2048]{1,0:T(8,128)}) custom-call(s32[18]{0:T(128)} %compare_select_fusion.5.table.core_ref._, bf16[400,1024]{1,0:T(8,128)(2,1)} %copy-done.10, bf16[400,1024]{1,0:T(8,128)(2,1)} %copy-done.14), custom_call_target="tpu_custom_call" | custom-call | flops 1 | bytes 1 | tf_op jit(solution)/shard_map/place/pallas_call | solution.py:671
  264.4 11.8 %collective-permute-done.29.refs_2_.refs_3_.refs_19_ = bf16[400,1024]{1,0:T(8,128)(2,1)} collective-permute-done((bf16[400,1024]{1,0:T(8,128)(2,1)}, bf16[400,1024]{1,0:T(8,128)(2,1)}, u32[]{:S(2)}, u32[]{:S(2)}) %collective-permute-start.29) | collective-permute-done | bytes 819232 | tf_op jit(solution)/shard_map/ppermute | solution.py:549
  276.1 1.5 collective-permute-done.30.refs_3_.refs_4_.refs_20_
  280.2 1.5 collective-permute-start.37
  282.2 4.6 %place.6 = (f32[2048,1024]{1,0:T(8,128)}, f32[1024,2048]{1,0:T(8,128)}) custom-call(s32[18]{0:T(128)} %compare_select_fusion.5.table.core_ref._, f32[2048,1024]{1,0:T(8,128)} %get-tuple-element.261.refs_0_, f32[1024,2048]{1,0:T(8,128)} %get-tuple-element.262.refs_1_, ...), custom_call_target="tpu_custom_call", output_to_operand_aliasing={{0}: (1, {}), {1}: (2, {})} | custom-call | flops 1 | bytes 1 | tf_op jit(solution)/shard_map/place/pallas_call | solution.py:671
  286.8 7.7 %collective-permute-done.37 = bf16[256,1024]{1,0:T(8,128)(2,1)} collective-permute-done((bf16[256,1024]{1,0:T(8,128)(2,1)S(1)}, bf16[256,1024]{1,0:T(8,128)(2,1)}, u32[]{:S(2)}, u32[]{:S(2)}) %collective-permute-start.37) | collective-permute-done | bytes 524320 | tf_op jit(solution)/shard_map/ppermute | solution.py:462
  294.5 1.3 collective-permute-done.33.left.refs_2_.refs_5_.refs_21_
  295.9 3.6 %collective-permute-done.34.right.refs_3_.refs_6_.refs_22_ = bf16[400,1024]{1,0:T(8,128)(2,1)S(1)} collective-permute-done((bf16[400,1024]{1,0:T(8,128)(2,1)}, bf16[400,1024]{1,0:T(8,128)(2,1)S(1)}, u32[]{:S(2)}, u32[]{:S(2)}) %collective-permute-start.34) | collective-permute-done | bytes 819232 | tf_op jit(solution)/shard_map/ppermute | solution.py:549
  300.4 2.0 halves.5
  303.1 1.4 collective-permute-start.40
  304.5 1.7 fusion.13
  307.0 2.9 all-to-all-start.5
  309.9 4.6 %place.7 = (f32[2048,1024]{1,0:T(8,128)}, f32[1024,2048]{1,0:T(8,128)}) custom-call(s32[18]{0:T(128)} %compare_select_fusion.5.table.core_ref._, f32[2048,1024]{1,0:T(8,128)} %get-tuple-element.284.refs_0_, f32[1024,2048]{1,0:T(8,128)} %get-tuple-element.285.refs_1_, ...), custom_call_target="tpu_custom_call", output_to_operand_aliasing={{0}: (1, {}), {1}: (2, {})} | custom-call | flops 1 | bytes 1 | tf_op jit(solution)/shard_map/place/pallas_call | solution.py:671
  316.8 3.0 fusion.10
  321.2 4.5 %place.8 = (f32[2048,1024]{1,0:T(8,128)}, f32[1024,2048]{1,0:T(8,128)}) custom-call(s32[18]{0:T(128)} %compare_select_fusion.5.table.core_ref._, f32[2048,1024]{1,0:T(8,128)} %get-tuple-element.294.refs_0_, f32[1024,2048]{1,0:T(8,128)} %get-tuple-element.295.refs_1_, bf16[400,1024]{1,0:T(8,128)(2,1)} %copy-done.11, ...), custom_call_target="tpu_custom_call", output_to_operand_aliasing={{0}: (1, {}), {1}: (2, {})} | custom-call | flops 1 | bytes 1 | tf_op jit(solution)/shard_map/place/pallas_call | solution.py:671
  326.5 7.5 %final_layout.1 = (f32[1024,512]{1,0:T(8,128)}, f32[1024,512]{1,0:T(8,128)}, f32[1024,512]{1,0:T(8,128)}, f32[2,8,32,1024]{3,2,1,0:T(8,128)}, f32[2,8,16,1024]{3,2,1,0:T(8,128)}) custom-call(s32[18]{0:T(128)} %compare_select_fusion.5.table.core_ref._, bf16[400,1024]{1,0:T(8,128)(2,1)} %copy-done.10, ...), custom_call_target="tpu_custom_call" | custom-call | flops 1 | bytes 1 | tf_op jit(solution)/shard_map/final_layout/pallas_call | solution.py:780
  334.0 1.3 reduce_sum.109
  336.5 3.4 %place.9 = (f32[2048,1024]{1,0:T(8,128)}, f32[1024,2048]{1,0:T(8,128)}) custom-call(s32[18]{0:T(128)} %compare_select_fusion.5.table.core_ref._, f32[2048,1024]{1,0:T(8,128)} %get-tuple-element.304.refs_0_, f32[1024,2048]{1,0:T(8,128)} %get-tuple-element.305.refs_1_, bf16[400,1024]{1,0:T(8,128)(2,1)} %copy-done.13, ...), custom_call_target="tpu_custom_call", output_to_operand_aliasing={{0}: (1, {}), {1}: (2, {})} | custom-call | flops 1 | bytes 1 | tf_op jit(solution)/shard_map/place/pallas_call | solution.py:671
  (203 shorter events, 33.9 us)
Async XLA Ops:
  7.8 64.5 %copy-start.21 = (bf16[512,1024]{1,0:T(8,128)(2,1)S(1)}, bf16[512,1024]{1,0:T(8,128)(2,1)}, u32[]{:S(2)}) copy-start(bf16[512,1024]{1,0:T(8,128)(2,1)} %refs_3_.1) | copy-start | bytes 3145732
  37.4 2.4 collective-permute-start.2
  37.4 18.6 %collective-permute-start = (bf16[256,512]{1,0:T(8,128)(2,1)}, bf16[256,512]{1,0:T(8,128)(2,1)S(1)}, u32[]{:S(2)}, u32[]{:S(2)}) collective-permute-start(bf16[256,512]{1,0:T(8,128)(2,1)} %get-tuple-element.164.refs_0_), channel_id=1, source_target_pairs={{0,8},{8,16},{16,24},{24,28},{28,20},{20,12},{12,4},{4,0},{1,9},{9... | collective-permute-start | bytes 786440 | tf_op jit(solution)/shard_map/ppermute | solution.py:549
  38.2 17.9 %collective-permute-start.1 = (bf16[256,512]{1,0:T(8,128)(2,1)}, bf16[256,512]{1,0:T(8,128)(2,1)S(1)}, u32[]{:S(2)}, u32[]{:S(2)}) collective-permute-start(bf16[256,512]{1,0:T(8,128)(2,1)} %get-tuple-element.164.refs_0_), channel_id=1, source_target_pairs={{0,4},{8,0},{16,8},{24,16},{28,24},{20,28},{12,20},{4,12},{1,5},{9... | collective-permute-start | bytes 786440 | tf_op jit(solution)/shard_map/ppermute | solution.py:549
  56.0 46.3 %copy-start.35 = (bf16[256,512]{1,0:T(8,128)(2,1)}, bf16[256,512]{1,0:T(8,128)(2,1)S(1)}, u32[]{:S(2)}) copy-start(bf16[256,512]{1,0:T(8,128)(2,1)S(1)} %collective-permute-done.refs_1_) | copy-start | bytes 786436
  56.0 46.3 %copy-start.36 = (bf16[256,512]{1,0:T(8,128)(2,1)}, bf16[256,512]{1,0:T(8,128)(2,1)S(1)}, u32[]{:S(2)}) copy-start(bf16[256,512]{1,0:T(8,128)(2,1)S(1)} %collective-permute-done.1.refs_2_) | copy-start | bytes 786436
  56.0 16.2 %all-to-all-start.1 = ((bf16[8,64,256]{2,1,0:T(8,128)(2,1)}), bf16[8,64,256]{2,1,0:T(8,128)(2,1)S(1)}, u32[]{:S(2)}, u32[]{:S(2)}) async-start(bf16[8,64,256]{2,1,0:T(8,128)(2,1)} %get-tuple-element.169), calls=%async_computation.1 | async-start | bytes 524288 | tf_op jit(solution)/shard_map/all_to_all | solution.py:435
  59.5 11.3 %collective-permute-start.3 = (bf16[256,512]{1,0:T(8,128)(2,1)S(1)}, bf16[256,512]{1,0:T(8,128)(2,1)S(1)}, u32[]{:S(2)}, u32[]{:S(2)}) collective-permute-start(bf16[256,512]{1,0:T(8,128)(2,1)S(1)} %collective-permute-done.refs_1_), channel_id=1, source_target_pairs={{0,8},{8,16},{16,24},{24,28},{28,20},{20,12},{12,4},{4,0},{1,9},{9... | collective-permute-start | bytes 786440 | tf_op jit(solution)/shard_map/ppermute | solution.py:549
  61.4 10.9 %collective-permute-start.4 = (bf16[256,512]{1,0:T(8,128)(2,1)S(1)}, bf16[256,512]{1,0:T(8,128)(2,1)S(1)}, u32[]{:S(2)}, u32[]{:S(2)}) collective-permute-start(bf16[256,512]{1,0:T(8,128)(2,1)S(1)} %collective-permute-done.1.refs_2_), channel_id=1, source_target_pairs={{0,4},{8,0},{16,8},{24,16},{28,24},{20,28},{12,20},{4,12},{1,5},{9... | collective-permute-start | bytes 786440 | tf_op jit(solution)/shard_map/ppermute | solution.py:549
  70.7 31.6 %copy-start.37 = (bf16[256,512]{1,0:T(8,128)(2,1)}, bf16[256,512]{1,0:T(8,128)(2,1)S(1)}, u32[]{:S(2)}) copy-start(bf16[256,512]{1,0:T(8,128)(2,1)S(1)} %collective-permute-done.3.refs_3_) | copy-start | bytes 786436
  72.3 30.1 %copy-start.38 = (bf16[256,512]{1,0:T(8,128)(2,1)}, bf16[256,512]{1,0:T(8,128)(2,1)S(1)}, u32[]{:S(2)}) copy-start(bf16[256,512]{1,0:T(8,128)(2,1)S(1)} %collective-permute-done.4.refs_4_) | copy-start | bytes 786436
  72.7 17.9 %copy-start.25 = (bf16[256,1024]{1,0:T(8,128)(2,1)}, bf16[256,1024]{1,0:T(8,128)(2,1)S(1)}, u32[]{:S(2)}) copy-start(bf16[256,1024]{1,0:T(8,128)(2,1)S(1)} %convolution_convert_fusion.refs_0_) | copy-start | bytes 1572868
  72.7 13.6 %collective-permute-start.7 = (bf16[256,1024]{1,0:T(8,128)(2,1)S(1)}, bf16[256,1024]{1,0:T(8,128)(2,1)S(1)}, u32[]{:S(2)}, u32[]{:S(2)}) collective-permute-start(bf16[256,1024]{1,0:T(8,128)(2,1)S(1)} %convolution_convert_fusion.refs_0_), channel_id=1, source_target_pairs={{0,1},{1,0},{2,3},{3,2},{4,5},{5,4},{6,7},{7,6},{8,9},{9,8},{10,11... | collective-permute-start | bytes 1572872 | tf_op jit(solution)/shard_map/ppermute | solution.py:462
  74.3 7.7 %collective-permute-start.5 = (bf16[256,512]{1,0:T(8,128)(2,1)S(1)}, bf16[256,512]{1,0:T(8,128)(2,1)S(1)}, u32[]{:S(2)}, u32[]{:S(2)}) collective-permute-start(bf16[256,512]{1,0:T(8,128)(2,1)S(1)} %collective-permute-done.3.refs_3_), channel_id=1, source_target_pairs={{0,8},{8,16},{16,24},{24,28},{28,20},{20,12},{12,4},{4,0},{1,9},{9... | collective-permute-start | bytes 786440 | tf_op jit(solution)/shard_map/ppermute | solution.py:549
  77.1 6.9 %collective-permute-start.6 = (bf16[256,512]{1,0:T(8,128)(2,1)S(1)}, bf16[256,512]{1,0:T(8,128)(2,1)S(1)}, u32[]{:S(2)}, u32[]{:S(2)}) collective-permute-start(bf16[256,512]{1,0:T(8,128)(2,1)S(1)} %collective-permute-done.4.refs_4_), channel_id=1, source_target_pairs={{0,4},{8,0},{16,8},{24,16},{28,24},{20,28},{12,20},{4,12},{1,5},{9... | collective-permute-start | bytes 786440 | tf_op jit(solution)/shard_map/ppermute | solution.py:549
  88.2 14.2 %collective-permute-start.8 = (bf16[256,256]{1,0:T(8,128)(2,1)}, bf16[256,256]{1,0:T(8,128)(2,1)S(1)}, u32[]{:S(2)}, u32[]{:S(2)}) collective-permute-start(bf16[256,256]{1,0:T(8,128)(2,1)} %get-tuple-element.178), channel_id=1, source_target_pairs={{0,8},{8,16},{16,24},{24,28},{28,20},{20,12},{12,4},{4,0},{1,9},{9... | collective-permute-start | bytes 393224 | tf_op jit(solution)/shard_map/ppermute | solution.py:549
  90.6 11.8 %collective-permute-start.9 = (bf16[256,256]{1,0:T(8,128)(2,1)}, bf16[256,256]{1,0:T(8,128)(2,1)S(1)}, u32[]{:S(2)}, u32[]{:S(2)}) collective-permute-start(bf16[256,256]{1,0:T(8,128)(2,1)} %get-tuple-element.179), channel_id=1, source_target_pairs={{0,4},{8,0},{16,8},{24,16},{28,24},{20,28},{12,20},{4,12},{1,5},{9... | collective-permute-start | bytes 393224 | tf_op jit(solution)/shard_map/ppermute | solution.py:549
  103.1 3.6 %collective-permute-start.11 = (bf16[256,2048]{1,0:T(8,128)(2,1)}, bf16[256,2048]{1,0:T(8,128)(2,1)S(1)}, u32[]{:S(2)}, u32[]{:S(2)}) collective-permute-start(bf16[256,2048]{1,0:T(8,128)(2,1)} %get-tuple-element.195), channel_id=1, source_target_pairs={{0,2},{2,0},{1,3},{3,1},{4,6},{6,4},{5,7},{7,5},{8,10},{10,8},{9,1... | collective-permute-start | bytes 3145736 | tf_op jit(solution)/shard_map/ppermute | solution.py:431
  103.1 3.6 %collective-permute-start.10 = (bf16[256,1024]{1,0:T(8,128)(2,1)}, bf16[256,1024]{1,0:T(8,128)(2,1)S(1)}, u32[]{:S(2)}, u32[]{:S(2)}) collective-permute-start(bf16[256,1024]{1,0:T(8,128)(2,1)} %get-tuple-element.193), channel_id=1, source_target_pairs={{0,2},{2,0},{1,3},{3,1},{4,6},{6,4},{5,7},{7,5},{8,10},{10,8},{9,1... | collective-permute-start | bytes 1572872 | tf_op jit(solution)/shard_map/ppermute | solution.py:431
  103.6 14.9 %collective-permute-start.14 = (bf16[256,1024]{1,0:T(8,128)(2,1)}, bf16[256,1024]{1,0:T(8,128)(2,1)S(1)}, u32[]{:S(2)}, u32[]{:S(2)}) collective-permute-start(bf16[256,1024]{1,0:T(8,128)(2,1)} %get-tuple-element.201.refs_0_), channel_id=1, source_target_pairs={{0,1},{1,0},{2,3},{3,2},{4,5},{5,4},{6,7},{7,6},{8,9},{9,8},{10,11... | collective-permute-start | bytes 1572872 | tf_op jit(solution)/shard_map/ppermute | solution.py:462
  113.5 10.1 %collective-permute-start.12 = (bf16[256,512]{1,0:T(8,128)(2,1)}, bf16[256,512]{1,0:T(8,128)(2,1)S(1)}, u32[]{:S(2)}, u32[]{:S(2)}) collective-permute-start(bf16[256,512]{1,0:T(8,128)(2,1)} %get-tuple-element.196), channel_id=1, source_target_pairs={{0,8},{8,16},{16,24},{24,28},{28,20},{20,12},{12,4},{4,0},{1,9},{9... | collective-permute-start | bytes 786440 | tf_op jit(solution)/shard_map/ppermute | solution.py:600
  115.5 8.3 %collective-permute-start.13 = (bf16[256,512]{1,0:T(8,128)(2,1)}, bf16[256,512]{1,0:T(8,128)(2,1)S(1)}, u32[]{:S(2)}, u32[]{:S(2)}) collective-permute-start(bf16[256,512]{1,0:T(8,128)(2,1)} %get-tuple-element.197), channel_id=1, source_target_pairs={{0,4},{8,0},{16,8},{24,16},{28,24},{20,28},{12,20},{4,12},{1,5},{9... | collective-permute-start | bytes 786440 | tf_op jit(solution)/shard_map/ppermute | solution.py:600
  128.2 21.1 %collective-permute-start.15 = (bf16[256,1024]{1,0:T(8,128)(2,1)}, bf16[256,1024]{1,0:T(8,128)(2,1)S(1)}, u32[]{:S(2)}, u32[]{:S(2)}) collective-permute-start(bf16[256,1024]{1,0:T(8,128)(2,1)} %get-tuple-element.211), channel_id=1, source_target_pairs={{0,8},{8,16},{16,24},{24,28},{28,20},{20,12},{12,4},{4,0},{1,9},{9... | collective-permute-start | bytes 1572872 | tf_op jit(solution)/shard_map/ppermute | solution.py:600
  130.1 19.2 %collective-permute-start.16 = (bf16[256,1024]{1,0:T(8,128)(2,1)}, bf16[256,1024]{1,0:T(8,128)(2,1)S(1)}, u32[]{:S(2)}, u32[]{:S(2)}) collective-permute-start(bf16[256,1024]{1,0:T(8,128)(2,1)} %get-tuple-element.212), channel_id=1, source_target_pairs={{0,4},{8,0},{16,8},{24,16},{28,24},{20,28},{12,20},{4,12},{1,5},{9... | collective-permute-start | bytes 1572872 | tf_op jit(solution)/shard_map/ppermute | solution.py:600
  130.2 19.0 %all-to-all-start.2 = ((bf16[8,64,256]{2,1,0:T(8,128)(2,1)}), bf16[8,64,256]{2,1,0:T(8,128)(2,1)S(1)}, u32[]{:S(2)}, u32[]{:S(2)}) async-start(bf16[8,64,256]{2,1,0:T(8,128)(2,1)} %bitcast.9), calls=%async_computation.2 | async-start | bytes 524288 | tf_op jit(solution)/shard_map/all_to_all | solution.py:435
  135.0 23.3 %collective-permute-start.22 = (bf16[256,1024]{1,0:T(8,128)(2,1)}, bf16[256,1024]{1,0:T(8,128)(2,1)S(1)}, u32[]{:S(2)}, u32[]{:S(2)}) collective-permute-start(bf16[256,1024]{1,0:T(8,128)(2,1)} %get-tuple-element.238), channel_id=1, source_target_pairs={{0,2},{2,0},{1,3},{3,1},{4,6},{6,4},{5,7},{7,5},{8,10},{10,8},{9,1... | collective-permute-start | bytes 1572872 | tf_op jit(solution)/shard_map/ppermute | solution.py:431
  135.0 23.3 %collective-permute-start.21 = (bf16[256,256]{1,0:T(8,128)(2,1)S(1)}, bf16[256,256]{1,0:T(8,128)(2,1)S(1)}, u32[]{:S(2)}, u32[]{:S(2)}) collective-permute-start(bf16[256,256]{1,0:T(8,128)(2,1)S(1)} %constant_dynamic-slice_fusion.1), channel_id=1, source_target_pairs={{0,2},{2,0},{1,3},{3,1},{4,6},{6,4},{5,7},{7,5},{8,10},{10,8},{9,1... | collective-permute-start | bytes 393224 | tf_op jit(solution)/shard_map/ppermute | solution.py:431
  135.5 65.5 %collective-permute-start.24 = (bf16[2048,512]{1,0:T(8,128)(2,1)}, bf16[2048,512]{1,0:T(8,128)(2,1)}, u32[]{:S(2)}, u32[]{:S(2)}) collective-permute-start(bf16[2048,512]{1,0:T(8,128)(2,1)} %join.1.refs_0_), channel_id=1, source_target_pairs={{0,1},{1,0},{2,3},{3,2},{4,5},{5,4},{6,7},{7,6},{8,9},{9,8},{10,11... | collective-permute-start | bytes 6291464 | tf_op jit(solution)/shard_map/ppermute | solution.py:462
  154.8 8.9 %copy-start.4 = (f32[8,64,256]{2,1,0:T(8,128)S(1)}, f32[8,64,256]{2,1,0:T(8,128)}, u32[]{:S(2)}) copy-start(f32[8,64,256]{2,1,0:T(8,128)} %get-tuple-element.222.raw_ref) | copy-start | bytes 1572868
  154.8 8.9 %copy-start.6 = (f32[8,1,256]{2,1,0:T(1,128)S(1)}, f32[8,1,256]{2,1,0:T(1,128)}, u32[]{:S(2)}) copy-start(f32[8,1,256]{2,1,0:T(1,128)} %get-tuple-element.223.logsum_ref) | copy-start | bytes 24580
  154.8 20.9 %collective-permute-start.17 = (bf16[256,1024]{1,0:T(8,128)(2,1)}, bf16[256,1024]{1,0:T(8,128)(2,1)}, u32[]{:S(2)}, u32[]{:S(2)}) collective-permute-start(bf16[256,1024]{1,0:T(8,128)(2,1)} %get-tuple-element.219), channel_id=1, source_target_pairs={{0,8},{8,16},{16,24},{24,28},{28,20},{20,12},{12,4},{4,0},{1,9},{9... | collective-permute-start | bytes 1572872 | tf_op jit(solution)/shard_map/ppermute | solution.py:600
  155.5 20.2 %collective-permute-start.18 = (bf16[256,1024]{1,0:T(8,128)(2,1)}, bf16[256,1024]{1,0:T(8,128)(2,1)}, u32[]{:S(2)}, u32[]{:S(2)}) collective-permute-start(bf16[256,1024]{1,0:T(8,128)(2,1)} %get-tuple-element.220), channel_id=1, source_target_pairs={{0,4},{8,0},{16,8},{24,16},{28,24},{20,28},{12,20},{4,12},{1,5},{9... | collective-permute-start | bytes 1572872 | tf_op jit(solution)/shard_map/ppermute | solution.py:600
  159.4 32.5 %all-to-all-start.3 = ((bf16[8,32,1024]{2,1,0:T(8,128)(2,1)}), bf16[8,32,1024]{2,1,0:T(8,128)(2,1)}, u32[]{:S(2)}, u32[]{:S(2)}) async-start(bf16[8,32,1024]{2,1,0:T(8,128)(2,1)} %bitcast.10), calls=%async_computation.3 | async-start | bytes 1048576 | tf_op jit(solution)/shard_map/all_to_all | solution.py:435
  179.6 12.1 %collective-permute-start.23 = (bf16[8,128,256]{2,1,0:T(8,128)(2,1)S(1)}, bf16[8,128,256]{2,1,0:T(8,128)(2,1)S(1)}, u32[]{:S(2)}, u32[]{:S(2)}) collective-permute-start(bf16[8,128,256]{2,1,0:T(8,128)(2,1)S(1)} %get-tuple-element.240), channel_id=1, source_target_pairs={{0,2},{2,0},{1,3},{3,1},{4,6},{6,4},{5,7},{7,5},{8,10},{10,8},{9,1... | collective-permute-start | bytes 1572872 | tf_op jit(solution)/shard_map/ppermute | solution.py:431
  191.8 9.2 %copy-start.19 = (bf16[8,128,256]{2,1,0:T(8,128)(2,1)}, bf16[8,128,256]{2,1,0:T(8,128)(2,1)S(1)}, u32[]{:S(2)}) copy-start(bf16[8,128,256]{2,1,0:T(8,128)(2,1)S(1)} %add_convert_fusion.1.key_value_ref) | copy-start | bytes 1572868
  191.9 9.1 %copy-start.47 = (bf16[256,1024]{1,0:T(8,128)(2,1)S(1)}, bf16[256,1024]{1,0:T(8,128)(2,1)}, u32[]{:S(2)}) copy-start(bf16[256,1024]{1,0:T(8,128)(2,1)} %get-tuple-element.234) | copy-start | bytes 1572868
  192.8 44.2 %all-to-all-start.4 = ((bf16[8,192,256]{2,1,0:T(8,128)(2,1)}), bf16[8,192,256]{2,1,0:T(8,128)(2,1)}, u32[]{:S(2)}, u32[]{:S(2)}) async-start(bf16[8,192,256]{2,1,0:T(8,128)(2,1)} %pad_maximum_fusion.2), calls=%async_computation.4 | async-start | bytes 1572864 | tf_op jit(solution)/shard_map/all_to_all | solution.py:435
  198.9 25.3 %collective-permute-start.19 = (bf16[256,1024]{1,0:T(8,128)(2,1)S(1)}, bf16[256,1024]{1,0:T(8,128)(2,1)S(1)}, u32[]{:S(2)}, u32[]{:S(2)}) collective-permute-start(bf16[256,1024]{1,0:T(8,128)(2,1)S(1)} %copy-done.48), channel_id=1, source_target_pairs={{0,8},{8,16},{16,24},{24,28},{28,20},{20,12},{12,4},{4,0},{1,9},{9... | collective-permute-start | bytes 1572872 | tf_op jit(solution)/shard_map/ppermute | solution.py:600
  201.0 24.8 %collective-permute-start.20 = (bf16[256,1024]{1,0:T(8,128)(2,1)S(1)}, bf16[256,1024]{1,0:T(8,128)(2,1)S(1)}, u32[]{:S(2)}, u32[]{:S(2)}) collective-permute-start(bf16[256,1024]{1,0:T(8,128)(2,1)S(1)} %copy-done.47), channel_id=1, source_target_pairs={{0,4},{8,0},{16,8},{24,16},{28,24},{20,28},{12,20},{4,12},{1,5},{9... | collective-permute-start | bytes 1572872 | tf_op jit(solution)/shard_map/ppermute | solution.py:600
  207.0 1.5 collective-permute-start.25
  231.3 22.8 %collective-permute-start.26 = (bf16[400,1024]{1,0:T(8,128)(2,1)S(1)}, bf16[400,1024]{1,0:T(8,128)(2,1)}, u32[]{:S(2)}, u32[]{:S(2)}) collective-permute-start(bf16[400,1024]{1,0:T(8,128)(2,1)S(1)} %pad_maximum_fusion.refs_0_.refs_16_), channel_id=1, source_target_pairs={{0,8},{8,16},{16,24},{24,28},{28,20},{20,12},{12,4},{4,0},{1,9},{9... | collective-permute-start | bytes 2457608 | tf_op jit(solution)/shard_map/ppermute | solution.py:549
  237.1 19.9 %collective-permute-start.27 = (bf16[400,1024]{1,0:T(8,128)(2,1)S(1)}, bf16[400,1024]{1,0:T(8,128)(2,1)}, u32[]{:S(2)}, u32[]{:S(2)}) collective-permute-start(bf16[400,1024]{1,0:T(8,128)(2,1)S(1)} %pad_maximum_fusion.refs_0_.refs_16_), channel_id=1, source_target_pairs={{0,4},{8,0},{16,8},{24,16},{28,24},{20,28},{12,20},{4,12},{1,5},{9... | collective-permute-start | bytes 2457608 | tf_op jit(solution)/shard_map/ppermute | solution.py:549
  237.1 19.9 %collective-permute-start.28 = (bf16[400,1024]{1,0:T(8,128)(2,1)S(1)}, bf16[400,1024]{1,0:T(8,128)(2,1)S(1)}, u32[]{:S(2)}, u32[]{:S(2)}) collective-permute-start(bf16[400,1024]{1,0:T(8,128)(2,1)S(1)} %pad_maximum_fusion.refs_0_.refs_16_), channel_id=1, source_target_pairs={{0,2},{2,0},{1,3},{3,1},{4,6},{6,4},{5,7},{7,5},{8,10},{10,8},{9,1... | collective-permute-start | bytes 2457608 | tf_op jit(solution)/shard_map/ppermute | solution.py:431
  240.1 39.9 %copy-start.8 = (bf16[256,1024]{1,0:T(8,128)(2,1)S(1)}, bf16[256,1024]{1,0:T(8,128)(2,1)}, u32[]{:S(2)}) copy-start(bf16[256,1024]{1,0:T(8,128)(2,1)} %input_ref.3) | copy-start | bytes 1572868
  240.6 41.2 %copy-start.46 = (s32[32]{0:T(128)S(1)}, s32[32]{0:T(128)}, u32[]{:S(2)}) copy-start(s32[32]{0:T(128)} %steps_ref.1) | copy-start | bytes 388
  240.6 41.2 %copy-start.45 = (s32[256]{0:T(256)S(1)}, s32[256]{0:T(256)}, u32[]{:S(2)}) copy-start(s32[256]{0:T(256)} %param.20) | copy-start | bytes 3076
  256.9 19.2 %collective-permute-start.29 = (bf16[400,1024]{1,0:T(8,128)(2,1)}, bf16[400,1024]{1,0:T(8,128)(2,1)}, u32[]{:S(2)}, u32[]{:S(2)}) collective-permute-start(bf16[400,1024]{1,0:T(8,128)(2,1)} %collective-permute-done.26.refs_2_.refs_1_.refs_17_), channel_id=1, source_target_pairs={{0,8},{8,16},{16,24},{24,28},{28,20},{20,12},{12,4},{4,0},{1,9},{9... | collective-permute-start | bytes 2457608 | tf_op jit(solution)/shard_map/ppermute | solution.py:549
  258.7 19.0 %collective-permute-start.30 = (bf16[400,1024]{1,0:T(8,128)(2,1)}, bf16[400,1024]{1,0:T(8,128)(2,1)S(1)}, u32[]{:S(2)}, u32[]{:S(2)}) collective-permute-start(bf16[400,1024]{1,0:T(8,128)(2,1)} %collective-permute-done.27.refs_3_.refs_2_.refs_18_), channel_id=1, source_target_pairs={{0,4},{8,0},{16,8},{24,16},{28,24},{20,28},{12,20},{4,12},{1,5},{9... | collective-permute-start | bytes 2457608 | tf_op jit(solution)/shard_map/ppermute | solution.py:549
  259.0 18.7 %collective-permute-start.31 = (bf16[400,1024]{1,0:T(8,128)(2,1)}, bf16[400,1024]{1,0:T(8,128)(2,1)}, u32[]{:S(2)}, u32[]{:S(2)}) collective-permute-start(bf16[400,1024]{1,0:T(8,128)(2,1)} %collective-permute-done.26.refs_2_.refs_1_.refs_17_), channel_id=1, source_target_pairs={{0,2},{2,0},{1,3},{3,1},{4,6},{6,4},{5,7},{7,5},{8,10},{10,8},{9,1... | collective-permute-start | bytes 2457608 | tf_op jit(solution)/shard_map/ppermute | solution.py:431
  259.0 18.7 %collective-permute-start.32 = (bf16[400,1024]{1,0:T(8,128)(2,1)}, bf16[400,1024]{1,0:T(8,128)(2,1)}, u32[]{:S(2)}, u32[]{:S(2)}) collective-permute-start(bf16[400,1024]{1,0:T(8,128)(2,1)} %collective-permute-done.27.refs_3_.refs_2_.refs_18_), channel_id=1, source_target_pairs={{0,2},{2,0},{1,3},{3,1},{4,6},{6,4},{5,7},{7,5},{8,10},{10,8},{9,1... | collective-permute-start | bytes 2457608 | tf_op jit(solution)/shard_map/ppermute | solution.py:431
  259.5 20.7 %collective-permute-start.38 = (bf16[256,1024]{1,0:T(8,128)(2,1)}, bf16[256,1024]{1,0:T(8,128)(2,1)}, u32[]{:S(2)}, u32[]{:S(2)}) collective-permute-start(bf16[256,1024]{1,0:T(8,128)(2,1)} %get-tuple-element.275), channel_id=1, source_target_pairs={{0,1},{1,0},{2,3},{3,2},{4,5},{5,4},{6,7},{7,6},{8,9},{9,8},{10,11... | collective-permute-start | bytes 1572872 | tf_op jit(solution)/shard_map/ppermute | solution.py:462
  277.7 18.2 %collective-permute-start.33 = (bf16[400,1024]{1,0:T(8,128)(2,1)}, bf16[400,1024]{1,0:T(8,128)(2,1)S(1)}, u32[]{:S(2)}, u32[]{:S(2)}) collective-permute-start(bf16[400,1024]{1,0:T(8,128)(2,1)} %collective-permute-done.29.refs_2_.refs_3_.refs_19_), channel_id=1, source_target_pairs={{0,8},{8,16},{16,24},{24,28},{28,20},{20,12},{12,4},{4,0},{1,9},{9... | collective-permute-start | bytes 2457608 | tf_op jit(solution)/shard_map/ppermute | solution.py:549
  278.6 20.9 %collective-permute-start.35 = (bf16[400,1024]{1,0:T(8,128)(2,1)}, bf16[400,1024]{1,0:T(8,128)(2,1)}, u32[]{:S(2)}, u32[]{:S(2)}) collective-permute-start(bf16[400,1024]{1,0:T(8,128)(2,1)} %collective-permute-done.29.refs_2_.refs_3_.refs_19_), channel_id=1, source_target_pairs={{0,2},{2,0},{1,3},{3,1},{4,6},{6,4},{5,7},{7,5},{8,10},{10,8},{9,1... | collective-permute-start | bytes 2457608 | tf_op jit(solution)/shard_map/ppermute | solution.py:431
  278.6 20.9 %collective-permute-start.34 = (bf16[400,1024]{1,0:T(8,128)(2,1)}, bf16[400,1024]{1,0:T(8,128)(2,1)S(1)}, u32[]{:S(2)}, u32[]{:S(2)}) collective-permute-start(bf16[400,1024]{1,0:T(8,128)(2,1)} %copy-done.15), channel_id=1, source_target_pairs={{0,4},{8,0},{16,8},{24,16},{28,24},{20,28},{12,20},{4,12},{1,5},{9... | collective-permute-start | bytes 2457608 | tf_op jit(solution)/shard_map/ppermute | solution.py:549
  279.7 19.7 %collective-permute-start.36 = (bf16[400,1024]{1,0:T(8,128)(2,1)}, bf16[400,1024]{1,0:T(8,128)(2,1)}, u32[]{:S(2)}, u32[]{:S(2)}) collective-permute-start(bf16[400,1024]{1,0:T(8,128)(2,1)} %copy-done.15), channel_id=1, source_target_pairs={{0,2},{2,0},{1,3},{3,1},{4,6},{6,4},{5,7},{7,5},{8,10},{10,8},{9,1... | collective-permute-start | bytes 2457608 | tf_op jit(solution)/shard_map/ppermute | solution.py:431
  280.2 24.2 %copy-start.17 = (bf16[256,1024]{1,0:T(8,128)(2,1)}, bf16[256,1024]{1,0:T(8,128)(2,1)S(1)}, u32[]{:S(2)}) copy-start(bf16[256,1024]{1,0:T(8,128)(2,1)S(1)} %convert_element_type.69) | copy-start | bytes 1572868
  280.2 14.3 %collective-permute-start.37 = (bf16[256,1024]{1,0:T(8,128)(2,1)S(1)}, bf16[256,1024]{1,0:T(8,128)(2,1)}, u32[]{:S(2)}, u32[]{:S(2)}) collective-permute-start(bf16[256,1024]{1,0:T(8,128)(2,1)S(1)} %convert_element_type.69), channel_id=1, source_target_pairs={{0,1},{1,0},{2,3},{3,2},{4,5},{5,4},{6,7},{7,6},{8,9},{9,8},{10,11... | collective-permute-start | bytes 1572872 | tf_op jit(solution)/shard_map/ppermute | solution.py:462
  282.1 22.3 %copy-start.41 = (f32[1024]{0:T(1024)S(1)}, f32[1024]{0:T(1024)}, u32[]{:S(2)}) copy-start(f32[1024]{0:T(1024)} %param.22) | copy-start | bytes 12292
  299.5 16.0 %collective-permute-start.41 = (bf16[400,1024]{1,0:T(8,128)(2,1)S(1)}, bf16[400,1024]{1,0:T(8,128)(2,1)}, u32[]{:S(2)}, u32[]{:S(2)}) collective-permute-start(bf16[400,1024]{1,0:T(8,128)(2,1)S(1)} %collective-permute-done.33.left.refs_2_.refs_5_.refs_21_), channel_id=1, source_target_pairs={{0,2},{2,0},{1,3},{3,1},{4,6},{6,4},{5,7},{7,5},{8,10},{10,8},{9,1... | collective-permute-start | bytes 2457608 | tf_op jit(solution)/shard_map/ppermute | solution.py:431
  299.6 15.9 %collective-permute-start.42 = (bf16[400,1024]{1,0:T(8,128)(2,1)S(1)}, bf16[400,1024]{1,0:T(8,128)(2,1)}, u32[]{:S(2)}, u32[]{:S(2)}) collective-permute-start(bf16[400,1024]{1,0:T(8,128)(2,1)S(1)} %collective-permute-done.34.right.refs_3_.refs_6_.refs_22_), channel_id=1, source_target_pairs={{0,2},{2,0},{1,3},{3,1},{4,6},{6,4},{5,7},{7,5},{8,10},{10,8},{9,1... | collective-permute-start | bytes 2457608 | tf_op jit(solution)/shard_map/ppermute | solution.py:431
  302.4 12.1 %collective-permute-start.39 = (bf16[400,512]{1,0:T(8,128)(2,1)}, bf16[400,512]{1,0:T(8,128)(2,1)}, u32[]{:S(2)}, u32[]{:S(2)}) collective-permute-start(bf16[400,512]{1,0:T(8,128)(2,1)} %get-tuple-element.282), channel_id=1, source_target_pairs={{0,8},{8,16},{16,24},{24,28},{28,20},{20,12},{12,4},{4,0},{1,9},{9... | collective-permute-start | bytes 1228808 | tf_op jit(solution)/shard_map/ppermute | solution.py:549
  303.1 12.4 %collective-permute-start.40 = (bf16[400,512]{1,0:T(8,128)(2,1)}, bf16[400,512]{1,0:T(8,128)(2,1)}, u32[]{:S(2)}, u32[]{:S(2)}) collective-permute-start(bf16[400,512]{1,0:T(8,128)(2,1)} %get-tuple-element.283), channel_id=1, source_target_pairs={{0,4},{8,0},{16,8},{24,16},{28,24},{20,28},{12,20},{4,12},{1,5},{9... | collective-permute-start | bytes 1228808 | tf_op jit(solution)/shard_map/ppermute | solution.py:549
  307.0 13.6 %all-to-all-start.5 = ((bf16[32,32,128]{2,1,0:T(8,128)(2,1)}), bf16[32,32,128]{2,1,0:T(8,128)(2,1)S(1)}, u32[]{:S(2)}, u32[]{:S(2)}) async-start(bf16[32,32,128]{2,1,0:T(8,128)(2,1)} %broadcast_in_dim.55), calls=%async_computation.5 | async-start | bytes 524288 | tf_op jit(solution)/shard_map/all_to_all | solution.py:954
  316.7 8.9 %collective-permute-start.43 = (bf16[400,1024]{1,0:T(8,128)(2,1)S(1)}, bf16[400,1024]{1,0:T(8,128)(2,1)S(1)}, u32[]{:S(2)}, u32[]{:S(2)}) collective-permute-start(bf16[400,1024]{1,0:T(8,128)(2,1)S(1)} %pad_maximum_fusion.1.refs_7_.refs_23_.refs_2_), channel_id=1, source_target_pairs={{0,2},{2,0},{1,3},{3,1},{4,6},{6,4},{5,7},{7,5},{8,10},{10,8},{9,1... | collective-permute-start | bytes 2457608 | tf_op jit(solution)/shard_map/ppermute | solution.py:431
  (34 other events, 119.0 us)

commit v12 on v11

--- a/solution.py
+++ b/solution.py
@@ -549,30 +549,34 @@
                 lax.ppermute(block, "chip", ring_pairs(direction))
                 for block, direction in zip(sides, (1, -1))
             ]
-        swapped = [swap_cores(block) for block in ready] if self.swap else []
-        self.state = (flying, swapped, self.outputs)
+        if self.swap and ready:
+            pairs = [(step, block, swap_cores(block)) for step, block in new]
+            self.pairs += pairs
+            self.outputs = self.take(self.outputs, pairs)
+        self.state = (flying, self.outputs)
 
     def advance(self, state):
-        arrived, swapped, self.outputs = state
-        pairs = [(step, near, far) for (step, near), far in zip(self.new, swapped)]
-        self.pairs += pairs
-        if self.take and pairs:
-            self.outputs = self.take(self.outputs, pairs)
+        arrived, self.outputs = state
         self.new = [-self.count, self.count]
         if arrived and self.count == self.reach:
             arrived, self.new = [jnp.concatenate(arrived, axis=1)], [self.count]
         self.ready = arrived
 
     def busy(self):
-        return bool(self.state[0] or self.state[1])
-
-
-def add_kernel(wanted, _, *refs):
-    outputs, refs = refs[-len(wanted) :], list(refs[: -len(wanted)])
+        return bool(self.state[0])
+
+
+def add_kernel(wanted, count, _, *refs):
+    outputs, refs = refs[-count:], list(refs[:-count])
     keep_in, far_in = refs.pop(0), refs.pop(0)
     for starts, output in zip(wanted, outputs):
         near, far = refs.pop(0), refs.pop(0)
         total = product(near[...], keep_in[...], 0, 0) + product(far[...], far_in[...], 0, 0)
+        if len(outputs) > len(wanted):
+            for at, output in enumerate(outputs):
+                columns = output.shape[1]
+                output[...] = total[:, at * columns : at * columns + columns].astype(BF16)
+            return
         output[...] = total.astype(BF16)
         arrived = [refs.pop(0) for _ in starts]
         for start in sorted(set(starts)):
@@ -591,8 +595,8 @@
         self.units = keep.shape[1] // self.chips
         self.tiled = self.units % 128 == 0
         self.left, self.rest = self.chips // 2, None
-        (block,) = self.add([(self.left, [])])
-        self.send(halves(block, block))
+        blocks = self.add([(self.left, [])], True)
+        self.send(blocks if len(blocks) > 1 else halves(blocks[0], blocks[0]))
 
     def send(self, ready):
         self.left -= 1
@@ -607,12 +611,15 @@
         first = 0 if ahead.shape[1] != half else half
         self.ready = self.add([(self.left, [(ahead, 0)]), (-self.left, [(behind, first)])])
 
-    def finish(self, values):
-        (ahead, behind), values = lax.optimization_barrier((self.state, values))
-        (total,) = self.add([(0, [(ahead, 0), (behind, 0)])])
-        return total, values
-
-    def add(self, wanted):
+    def arrive(self, values):
+        self.state, values = lax.optimization_barrier((self.state, values))
+        return values
+
+    def finish(self):
+        ahead, behind = self.state
+        return self.add([(0, [(ahead, 0), (behind, 0)])])[0]
+
+    def add(self, wanted, split=False):
         (rows, model), units, chips = self.sides[0].shape, self.units, self.chips
         if not self.tiled:
             sums = []
@@ -636,15 +643,19 @@
             specs += [block] * 2
             specs += [pl.BlockSpec(part.shape, lambda at, table: (0, 0)) for part, _ in parts]
             arrays += list(self.operands) + [part for part, _ in parts]
+        starts = [[start for _, start in parts] for _, parts in wanted]
+        shapes = [struct((units, model), BF16)] * len(wanted)
+        if split:
+            shapes = [struct((units, model // 2), BF16)] * 2
         return pl.pallas_call(
-            functools.partial(add_kernel, [[start for _, start in parts] for _, parts in wanted]),
+            functools.partial(add_kernel, starts, len(shapes)),
             grid_spec=pltpu.PrefetchScalarGridSpec(
                 num_scalar_prefetch=1,
                 grid=(1,),
                 in_specs=specs,
-                out_specs=[whole] * len(wanted),
+                out_specs=[pl.BlockSpec(shape.shape, lambda at, table: (0, 0)) for shape in shapes],
             ),
-            out_shape=[struct((units, model), BF16)] * len(wanted),
+            out_shape=shapes,
             compiler_params=streaming,
             cost_estimate=light,
             name="ring_add",
@@ -652,6 +663,7 @@
 
     def place(self, outputs, pairs):
         units, chips, model = self.units, self.chips, self.sides[0].shape[1]
+        size, extra = self.size, self.extra
         shapes = [struct((chips * units, model), F32), struct((model, chips * units), F32)]
         if not self.tiled:
             outputs = outputs or [jnp.zeros(shape.shape, F32) for shape in shapes]
@@ -667,20 +679,37 @@
             return [down, up]
         first = pairs[0][0] % chips
         stride = pairs[-1][0] % chips - first
-        block = pl.BlockSpec((units, model), lambda at, table: (0, 0))
+        block = pl.BlockSpec(pairs[0][1].shape, lambda at, table: (0, 0))
+
+        def place(at, table):
+            return table[first + at * stride]
+
+        def chip(at, table):
+            return table[chips + first + at * stride]
+
         return pl.pallas_call(
-            functools.partial(place_kernel, len(pairs)),
+            functools.partial(place_kernel, len(pairs), (units, size, extra)),
             grid_spec=pltpu.PrefetchScalarGridSpec(
                 num_scalar_prefetch=1,
                 grid=(len(pairs),),
                 in_specs=[pl.BlockSpec(memory_space=pl.ANY)] * len(outputs)
                 + [block] * (2 * len(pairs)),
                 out_specs=[
-                    pl.BlockSpec((units, model), lambda at, table: (table[first + at * stride], 0)),
-                    pl.BlockSpec((model, units), lambda at, table: (0, table[first + at * stride])),
+                    pl.BlockSpec((units, model), lambda at, table: (place(at, table), 0)),
+                    pl.BlockSpec((model, units), lambda at, table: (0, place(at, table))),
+                    pl.BlockSpec((1, 2, size, model), lambda at, table: (chip(at, table), 0, 0, 0)),
+                    pl.BlockSpec((2, 1, extra, model), lambda at, table: (0, chip(at, table), 0, 0)),
+                    pl.BlockSpec(
+                        (1, 2, small_rows, model), lambda at, table: (chip(at, table), 0, 0, 0)
+                    ),
                 ],
             ),
-            out_shape=shapes,
+            out_shape=shapes
+            + [
+                struct((chips, 2, size, model), BF16),
+                struct((2, chips, extra, model), F32),
+                struct((chips, 2, small_rows, model), F32),
+            ],
             input_output_aliases={1 + at: at for at in range(len(outputs))},
             compiler_params=streaming,
             cost_estimate=light,
@@ -688,15 +717,23 @@
         )(self.table, *outputs, *[pair[1] for pair in pairs], *[pair[2] for pair in pairs])
 
 
-def place_kernel(count, table, *refs):
-    nears, fars, (down, up) = refs[-2 - 2 * count : -2 - count], refs[-2 - count : -2], refs[-2:]
+def place_kernel(count, sizes, table, *refs):
+    blocks, (down, up, projections, weight, small) = refs[-5 - 2 * count : -5], refs[-5:]
     core = table[table.shape[0] - 2]
+    units, size, extra = sizes
+    rows = [pl.ds(0, units), pl.ds(units, size), pl.ds(units + size, extra)]
+    rows.append(pl.ds(units + size + extra, small_rows))
 
     def put(first, second):
-        down[...] = first[...].astype(F32)
-        up[...] = second[...].astype(F32).T
-
-    for at, (near, far) in enumerate(zip(nears, fars)):
+        down[...] = first[rows[0], :].astype(F32)
+        up[...] = second[rows[0], :].astype(F32).T
+        for side, block in ((0, first), (1, second)):
+            projections[0, side] = block[rows[1], :]
+            weight[side, 0] = block[rows[2], :].astype(F32)
+            small[0, side] = block[rows[3], :].astype(F32)
+
+    for at in range(count):
+        near, far = blocks[at], blocks[count + at]
         here = pl.program_id(0) == at
         pl.when(here & (core == 0))(functools.partial(put, near, far))
         pl.when(here & (core != 0))(functools.partial(put, far, near))
@@ -743,62 +780,25 @@
     )(table, dquery, key_value, *parts)
 
 
-def layout_kernel(steps, size, extra, table, *refs):
-    count = len(steps)
-    blocks, refs = refs[: 4 * count], refs[4 * count :]
-    nears = list(zip(blocks[:count], blocks[2 * count : 3 * count]))
-    fars = list(zip(blocks[count : 2 * count], blocks[3 * count :]))
-    outputs, (output_ref, small_ref, held) = refs[:3], refs[3:]
-    at = pl.program_id(0)
-
-    @pl.when(at == 0)
-    def _():
-        core = table[2 * count]
-        for step, near, far in zip(steps, nears, fars):
-            chip = table[count + step % count]
-            for side, (block, small) in ((core, near), (1 - core, far)):
-                held[chip, side] = block[pl.ds(0, size), :]
-                output_ref[side, chip] = block[pl.ds(size, extra), :].astype(F32)
-                small_ref[side, chip] = small[...].astype(F32)
-
-    pair = [
-        jnp.concatenate([held[2 * at + head, 0], held[2 * at + head, 1]], axis=0)
-        for head in range(2)
-    ]
+def layout_kernel(held, *outputs):
+    pair = [jnp.concatenate([held[head, 0], held[head, 1]], axis=0) for head in range(2)]
     for index, output in enumerate(outputs):
         rows = [part[index * HD : index * HD + HD] for part in pair]
         output[...] = jnp.concatenate(rows, axis=0).astype(F32).T
 
 
-def final_layout(pairs, start, size, table):
-    count = len(pairs)
-    steps, nears, fars = zip(*pairs)
-    rows, model = nears[0].shape
-    extra = rows - start - size - small_rows
-    part = pl.BlockSpec((size + extra, model), lambda at, table: (start // (size + extra), 0))
-    last = pl.BlockSpec((small_rows, model), lambda at, table: (rows // small_rows - 1, 0))
+def final_layout(held):
+    count, _, size, model = held.shape
     return pl.pallas_call(
-        functools.partial(layout_kernel, steps, size, extra),
-        grid_spec=pltpu.PrefetchScalarGridSpec(
-            num_scalar_prefetch=1,
-            grid=(count // 2,),
-            in_specs=[part] * (2 * count) + [last] * (2 * count),
-            out_specs=[pl.BlockSpec((model, 2 * HD), lambda at, table: (0, at))] * 3
-            + [
-                pl.BlockSpec((2, count, extra, model), lambda at, table: (0, 0, 0, 0)),
-                pl.BlockSpec((2, count, small_rows, model), lambda at, table: (0, 0, 0, 0)),
-            ],
-            scratch_shapes=[pltpu.VMEM((count, 2, size, model), BF16)],
-        ),
-        out_shape=[struct((model, count * HD), F32)] * 3
-        + [
-            struct((2, count, extra, model), F32),
-            struct((2, count, small_rows, model), F32),
-        ],
+        layout_kernel,
+        grid=(count // 2,),
+        in_specs=[pl.BlockSpec((2, 2, size, model), lambda at: (at, 0, 0, 0))],
+        out_specs=[pl.BlockSpec((model, 2 * HD), lambda at: (0, at))] * 3,
+        out_shape=[struct((model, count * HD), F32)] * 3,
         compiler_params=streaming,
         cost_estimate=light,
         name="final_layout",
-    )(table, *nears, *fars, *nears, *fars)
+    )(held)
 
 
 def core_half(values, axis, side):
@@ -858,7 +858,6 @@
     attn_out = gather_queries(out, heads, split, rows)
     attn_out = visit([inputs], attn_out)
     branches = across_heads(product(attn_out, output_weight, 0, 0).astype(BF16))
-    branches = visit([inputs], branches)
     keep, give, keep_in, give_in, hidden, dup_bias, mlp_part, d_mlp_part = mlp(
         table,
         block_input,
@@ -876,18 +875,17 @@
     )
     d_mlp = across_heads(d_mlp_part)
     ring = Reduce(keep, swap_cores(give), keep_in, swap_cores(give_in), table)
+    mlp_part, d_mlp = lax.optimization_barrier((mlp_part, d_mlp))
+    d_hidden, d_branch, d_attn, sums = middle(hidden, out_grad, d_mlp, gain_mlp, output_weight)
+    grads = scatter_queries(d_attn, heads, split)
+    d_branch, mlp_part = visit([ring, inputs], (d_branch, mlp_part))
     while inputs.busy():
         visit([inputs], ())
+    mlp_out = across_heads(mlp_part)
     steps, inputs = zip(*inputs.blocks)
-    inputs = join(inputs)
-    mlp_part, inputs, d_mlp = lax.optimization_barrier((mlp_part, inputs, d_mlp))
-    parts = [inputs]
+    parts = [join(inputs)]
     if cut != model:
-        parts = across_heads(inputs)
-    d_hidden, d_branch, d_attn, sums = middle(hidden, out_grad, d_mlp, gain_mlp, output_weight)
-    grads = scatter_queries(d_attn, heads, split)
-    d_branch, mlp_part = visit([ring], (d_branch, mlp_part))
-    mlp_out = across_heads(mlp_part)
+        parts = across_heads(parts[0])
     out_near, out_far = share_halves(attn_out, 0)
     doutput = product(out_near, d_branch) + product(out_far, swap_cores(d_branch))
     doutput = to_heads(doutput.astype(BF16).reshape(chips, -1, model))
@@ -900,6 +898,7 @@
     *dquery, near_sums = backward_piece(
         queries, grads, raw, logsum, dquery, own, [], 0, 1, crops, (BF16, F32)
     )
+    near_sums, dquery = ring.arrive((near_sums, dquery))
     (dquery,) = dquery
     key_value = (near_sums + far_sums.astype(F32)).astype(BF16)
     doutput, key_value = lax.optimization_barrier((doutput, key_value))
@@ -927,8 +926,9 @@
             lax.psum(product(attn_in, grad, 0, 1).astype(BF16), ("chip", "core")).astype(F32)
             for grad in (dquery, dkey, dvalue)
         ]
-    total, blocks = ring.finish(blocks)
+    total = ring.finish()
     start = total.shape[0]
+    ring.size, ring.extra = size, blocks.shape[0] - size - small_rows
     gathered = Gather(jnp.concatenate([total, blocks], axis=0), True, ring.place)
     gathered.send(gathered.ready)
     d_part = (
@@ -964,10 +964,11 @@
     )
     while gathered.busy():
         visit([gathered], ())
-    ddown_weight, dup_weight = gathered.outputs
+    ddown_weight, dup_weight, *rest = gathered.outputs
     ends = jnp.sum(ends.astype(F32), axis=0).reshape(-1)[: 3 * model].reshape(3, model)
     if split == 1:
-        *projections, doutput_weight, small = final_layout(gathered.pairs, start, size, table)
+        held, doutput_weight, small = rest
+        projections = final_layout(held)
         doutput_weight = doutput_weight.reshape(width, model)
     if split != 1:
         blocks = jnp.zeros((2, chips) + blocks.shape, F32)

time: 342 us -> 322 us (0.942)
  waiting for transfers between devices: 94.9 us -> 81.3 us
  starting transfers between devices: 60.5 us -> 56.9 us
    ppermute x24, waiting for transfers between devices: 69.7 us -> 35 us  [send(): lax.ppermute(block, 'chip', ring_pairs(direction))]
    ppermute x5, waiting for transfers between devices: 10.1 us -> 26.5 us  [across_heads(): return [part, lax.ppermute(part, 'head', [(0, 1), (1, 0)])]]
    ppermute x24, starting transfers between devices: 29.2 us -> 25.4 us  [send(): lax.ppermute(block, 'chip', ring_pairs(direction))]
    all_to_all x4, waiting for transfers between devices: 12.3 us -> 15.8 us  [to_heads(): return lax.all_to_all(blocks, 'chip', 0, 0, tiled=True)]
    unnamed x101 -> x91, local copies, waits for them, and re-layouts: 9.5 us -> 9.41 us
  transfers between devices with their start and end apart: 49 -> 49, of which waited for: 21 -> 20; matrix products, arithmetic and copies ran while one was open for 5% -> 5% of each run, Pallas kernels for 29% -> 32%
where the time goes in v12:
time: 322 us; the launch traced here: 320 us
  Pallas kernels  121 us (38%)
  waiting for transfers between devices  81.3 us (25%)
  starting transfers between devices  56.9 us (18%)
  blocking collectives  29.6 us (9%)
  local copies, waits for them, and re-layouts  13.6 us (4%)
  other arithmetic  11.5 us (4%)
  matrix products  4.35 us (1%)
    ppermute x24, waiting for transfers between devices, send(): lax.ppermute(block, 'chip', ring_pairs(direction))  35 us
    all_to_all x1, blocking collectives, to_heads(): return lax.all_to_all(blocks, 'chip', 0, 0, tiled=True)  29.6 us
    ppermute x5, waiting for transfers between devices, across_heads(): return [part, lax.ppermute(part, 'head', [(0, 1), (1, 0)])]  26.5 us
    ppermute x24, starting transfers between devices, send(): lax.ppermute(block, 'chip', ring_pairs(direction))  25.4 us
    pallas_call x5, Pallas kernels, place(): pl.pallas_call(functools.partial(place_kernel, len(pairs), (units, size,...  24.3 us
    pallas_call x2, Pallas kernels, backward_piece(): pl.pallas_call(functools.partial(backward_kernel, crops, len(before)), gr...  24 us
    pallas_call x5, Pallas kernels, add(): pl.pallas_call(functools.partial(add_kernel, starts, len(shapes)), grid_s...  18.2 us
    all_to_all x4, starting transfers between devices, to_heads(): return lax.all_to_all(blocks, 'chip', 0, 0, tiled=True)  17.9 us
  transfers between devices with their start and end apart: 49, of which 20 were waited for; matrix products, arithmetic and copies ran while one was open for 5% of the time, Pallas kernels for 32%

profile of v12, /device:TPU:0, one launch (start us, length us, event | category | flops | bytes accessed | tf_op | source)
XLA Modules:
  0.0 320.1 jit_solution(16171150716667750737)
XLA Ops:
  1.2 6.6 %project.1 = (bf16[8,208,256]{2,1,0:T(8,128)(2,1)}, bf16[256,1024]{1,0:T(8,128)(2,1)}, bf16[256,512]{1,0:T(8,128)(2,1)}) custom-call(s32[18]{0:T(128)} %compare_select_fusion.5.table.core_ref._, bf16[256,1024]{1,0:T(8,128)(2,1)} %input_ref.3, s32[1,256]{1,0:T(1,128)} %bitcast.67, s32[32]{0:T(128)} %steps_ref.1, f32[1,1024]{1,0:T(1,128)} %bitcast.53, ...), custom_call_target="tpu_custom_call" | custom-call | flops 1 | bytes 1 | tf_op jit(solution)/shard_map/project/pallas_call | solution.py:94
  7.8 29.6 %all_to_all.30.query_ref.own.refs_1_ = bf16[8,208,256]{2,1,0:T(8,128)(2,1)S(1)} all-to-all(bf16[8,208,256]{2,1,0:T(8,128)(2,1)} %get-tuple-element.172), channel_id=1, replica_groups=mesh['chip'=8,'core'=2,'head'=2] {'chip'}, dimensions={0} | all-to-all | bytes 1703936 | tf_op jit(solution)/shard_map/all_to_all | solution.py:435
  38.2 1.3 collective-permute-start.1
  40.7 15.3 %attention_forward.1 = (f32[8,64,256]{2,1,0:T(8,128)}, bf16[8,64,256]{2,1,0:T(8,128)(2,1)}, f32[8,1,256]{2,1,0:T(1,128)}) custom-call(bf16[8,208,256]{2,1,0:T(8,128)(2,1)} %copy-done, bf16[8,208,256]{2,1,0:T(8,128)(2,1)} %copy-done, bf16[8,208,256]{2,1,0:T(8,128)(2,1)} %copy-done.2), custom_call_target="tpu_custom_call" | custom-call | flops 1 | bytes 1 | tf_op jit(solution)/shard_map/attention_forward/pallas_call | solution.py:367
  56.1 3.4 %all-to-all-start.1 = ((bf16[8,64,256]{2,1,0:T(8,128)(2,1)}), bf16[8,64,256]{2,1,0:T(8,128)(2,1)S(1)}, u32[]{:S(2)}, u32[]{:S(2)}) async-start(bf16[8,64,256]{2,1,0:T(8,128)(2,1)} %get-tuple-element.179), calls=%async_computation.1 | async-start | bytes 524288 | tf_op jit(solution)/shard_map/all_to_all | solution.py:435
  59.5 1.9 collective-permute-start.3
  61.6 9.1 %collective-permute-done.3.refs_3_ = bf16[256,512]{1,0:T(8,128)(2,1)S(1)} collective-permute-done((bf16[256,512]{1,0:T(8,128)(2,1)S(1)}, bf16[256,512]{1,0:T(8,128)(2,1)S(1)}, u32[]{:S(2)}, u32[]{:S(2)}) %collective-permute-start.3) | collective-permute-done | bytes 262176 | tf_op jit(solution)/shard_map/ppermute | solution.py:549
  70.7 1.6 collective-permute-done.4.refs_4_
  72.8 1.5 collective-permute-start.5
  74.4 2.7 collective-permute-start.6
  77.1 9.3 %collective-permute-done.5.refs_1_ = bf16[256,1024]{1,0:T(8,128)(2,1)S(1)} collective-permute-done((bf16[256,1024]{1,0:T(8,128)(2,1)S(1)}, bf16[256,1024]{1,0:T(8,128)(2,1)S(1)}, u32[]{:S(2)}, u32[]{:S(2)}) %collective-permute-start.5) | collective-permute-done | bytes 524320 | tf_op jit(solution)/shard_map/ppermute | solution.py:462
  87.2 11.7 %mlp.1 = (bf16[256,2048]{1,0:T(8,128)(2,1)}, bf16[256,2048]{1,0:T(8,128)(2,1)}, bf16[256,1024]{1,0:T(8,128)(2,1)}, bf16[256,1024]{1,0:T(8,128)(2,1)}, f32[256,10...) custom-call(s32[18]{0:T(128)} %compare_select_fusion.5.table.core_ref._, ...), custom_call_target="tpu_custom_call" | custom-call | flops 1 | bytes 1 | tf_op jit(solution)/shard_map/mlp/pallas_call | solution.py:174
  99.6 1.5 collective-permute-start.14
  101.1 1.6 collective-permute-done.8.refs_1_
  104.5 3.1 ring_add.5
  107.6 2.3 collective-permute-start.10
  109.8 1.7 halves.2
  111.5 2.0 collective-permute-start.12
  114.5 4.3 %middle.1 = (f32[256,1024]{1,0:T(8,128)}, bf16[256,1024]{1,0:T(8,128)(2,1)}, bf16[512,256]{1,0:T(8,128)(2,1)}, f32[4,1024]{1,0:T(4,128)}) custom-call(f32[256,1024]{1,0:T(8,128)} %get-tuple-element.181.hidden_ref, bf16[256,1024]{1,0:T(8,128)(2,1)} %grad_ref.3, bf16[256,1024]{1,0:T(8,128)(2,1)} %get-tuple-element.201.refs_0_, bf16[256,1024]{1,0:T(8,128)(2,1)} %copy-done.31, ...), custom_call_target="tpu_custom_call" | custom-call | flops 1 | bytes 1 | tf_op jit(solution)/shard_map/middle/pallas_call | solution.py:235
  118.9 2.0 collective-permute-done.13
  121.8 3.7 %ring_add.6 = (bf16[256,1024]{1,0:T(8,128)(2,1)}, bf16[256,1024]{1,0:T(8,128)(2,1)}) custom-call(s32[18]{0:T(128)} %compare_select_fusion.5.table.core_ref._, bf16[256,1024]{1,0:T(8,128)(2,1)} %get-tuple-element.189.refs_0_, bf16[256,1024]{1,0:T(8,128)(2,1)} %copy-done.9, bf16[256,2048]{1,0:T(8,128)(2,1)} %get-tuple-element.191.refs_2_.refs_5_, ...), custom_call_target="tpu_custom_call" | custom-call | flops 1 | bytes 1 | tf_op jit(solution)/shard_map/ring_add/pallas_call | solution.py:650
  126.3 1.2 collective-permute-start.16
  127.5 4.3 %all-to-all-start.2 = ((bf16[8,64,256]{2,1,0:T(8,128)(2,1)}), bf16[8,64,256]{2,1,0:T(8,128)(2,1)S(1)}, u32[]{:S(2)}, u32[]{:S(2)}) async-start(bf16[8,64,256]{2,1,0:T(8,128)(2,1)} %bitcast.9), calls=%async_computation.2 | async-start | bytes 524288 | tf_op jit(solution)/shard_map/all_to_all | solution.py:435
  132.4 3.0 join.1.refs_0_
  135.4 1.5 collective-permute-start.24
  136.9 8.0 %all-to-all-done.2.grad_ref = bf16[8,64,256]{2,1,0:T(8,128)(2,1)S(1)} async-done(((bf16[8,64,256]{2,1,0:T(8,128)(2,1)}), bf16[8,64,256]{2,1,0:T(8,128)(2,1)S(1)}, u32[]{:S(2)}, u32[]{:S(2)}) %all-to-all-start.2) | async-done | bytes 262176 | tf_op jit(solution)/shard_map/all_to_all | solution.py:435
  146.4 3.9 %ring_add.7 = (bf16[256,1024]{1,0:T(8,128)(2,1)}, bf16[256,1024]{1,0:T(8,128)(2,1)}) custom-call(s32[18]{0:T(128)} %compare_select_fusion.5.table.core_ref._, bf16[256,1024]{1,0:T(8,128)(2,1)} %get-tuple-element.189.refs_0_, bf16[256,1024]{1,0:T(8,128)(2,1)} %copy-done.9, bf16[256,2048]{1,0:T(8,128)(2,1)} %get-tuple-element.191.refs_2_.refs_5_, ...), custom_call_target="tpu_custom_call" | custom-call | flops 1 | bytes 1 | tf_op jit(solution)/shard_map/ring_add/pallas_call | solution.py:650
  150.9 1.6 collective-permute-start.18
  152.4 1.3 fusion.14
  153.8 1.1 fusion
  154.9 4.2 %all-to-all-start.3 = ((bf16[8,32,1024]{2,1,0:T(8,128)(2,1)}), bf16[8,32,1024]{2,1,0:T(8,128)(2,1)S(1)}, u32[]{:S(2)}, u32[]{:S(2)}) async-start(bf16[8,32,1024]{2,1,0:T(8,128)(2,1)} %bitcast.10), calls=%async_computation.3 | async-start | bytes 1048576 | tf_op jit(solution)/shard_map/all_to_all | solution.py:435
  159.1 11.9 %attention_backward.2 = (f32[8,64,256]{2,1,0:T(8,128)S(1)}, bf16[8,128,256]{2,1,0:T(8,128)(2,1)S(1)}) custom-call(bf16[8,208,256]{2,1,0:T(8,128)(2,1)S(1)} %copy-done.1, bf16[8,64,256]{2,1,0:T(8,128)(2,1)S(1)} %all-to-all-done.2.grad_ref, f32[8,64,256]{2,1,0:T(8,128)S(1)} %copy-done.4, f32[8,1,256]{2,1,0:T(1,128)S(1)} %copy-done.6, ...), custom_call_target="tpu_custom_call" | custom-call | flops 1 | bytes 1 | tf_op jit(solution)/shard_map/attention_backward/pallas_call | solution.py:397
  171.1 3.9 %ring_add.8 = (bf16[256,1024]{1,0:T(8,128)(2,1)}, bf16[256,1024]{1,0:T(8,128)(2,1)}) custom-call(s32[18]{0:T(128)} %compare_select_fusion.5.table.core_ref._, bf16[256,1024]{1,0:T(8,128)(2,1)} %get-tuple-element.189.refs_0_, bf16[256,1024]{1,0:T(8,128)(2,1)} %copy-done.9, bf16[256,2048]{1,0:T(8,128)(2,1)} %get-tuple-element.191.refs_2_.refs_5_, ...), custom_call_target="tpu_custom_call" | custom-call | flops 1 | bytes 1 | tf_op jit(solution)/shard_map/ring_add/pallas_call | solution.py:650
  174.9 2.0 collective-permute-start.19
  177.0 12.0 %attention_backward.3 = (bf16[8,64,256]{2,1,0:T(8,128)(2,1)S(1)}, f32[8,128,256]{2,1,0:T(8,128)S(1)}) custom-call(bf16[8,208,256]{2,1,0:T(8,128)(2,1)S(1)} %copy-done.1, bf16[8,64,256]{2,1,0:T(8,128)(2,1)S(1)} %all-to-all-done.2.grad_ref, f32[8,64,256]{2,1,0:T(8,128)S(1)} %copy-done.4, f32[8,1,256]{2,1,0:T(1,128)S(1)} %copy-done.6, ...), custom_call_target="tpu_custom_call" | custom-call | flops 1 | bytes 1 | tf_op jit(solution)/shard_map/attention_backward/pallas_call | solution.py:397
  191.0 6.0 %all-to-all-start.4 = ((bf16[8,192,256]{2,1,0:T(8,128)(2,1)}), bf16[8,192,256]{2,1,0:T(8,128)(2,1)}, u32[]{:S(2)}, u32[]{:S(2)}) async-start(bf16[8,192,256]{2,1,0:T(8,128)(2,1)} %pad_maximum_fusion.2), calls=%async_computation.4 | async-start | bytes 1572864 | tf_op jit(solution)/shard_map/all_to_all | solution.py:435
  197.1 5.0 %head_gradient.1 = bf16[192,1024]{1,0:T(8,128)(2,1)} custom-call(s32[18]{0:T(128)} %compare_select_fusion.5.table.core_ref._, bf16[8,64,256]{2,1,0:T(8,128)(2,1)} %copy-done.5, bf16[8,128,256]{2,1,0:T(8,128)(2,1)} %copy-done.10, bf16[2048,512]{1,0:T(8,128)(2,1)} %join.1.refs_0_, bf16[2048,512]{1,0:T(8,128)(2,1)} %collective-permute-done.24.refs_1_), custom_call_target="tpu_custom_call" | custom-call | flops 1 | bytes 1 | tf_op jit(solution)/shard_map/head_gradient/pallas_call | solution.py:765
  203.4 3.7 %ring_add.9 = bf16[256,1024]{1,0:T(8,128)(2,1)} custom-call(s32[18]{0:T(128)} %compare_select_fusion.5.table.core_ref._, bf16[256,1024]{1,0:T(8,128)(2,1)} %get-tuple-element.189.refs_0_, bf16[256,1024]{1,0:T(8,128)(2,1)} %copy-done.9, bf16[256,2048]{1,0:T(8,128)(2,1)} %get-tuple-element.191.refs_2_.refs_5_, bf16[256,2048]{1,0:T(8,128)(2,1)} %copy-done.7, ...), custom_call_target="tpu_custom_call" | custom-call | flops 1 | bytes 1 | tf_op jit(solution)/shard_map/ring_add/pallas_call | solution.py:650
  207.3 1.2 pad_maximum_fusion.refs_0_
  208.8 2.0 collective-permute-start.26
  210.9 7.8 %all-to-all-done.4 = bf16[8,192,256]{2,1,0:T(8,128)(2,1)} async-done(((bf16[8,192,256]{2,1,0:T(8,128)(2,1)}), bf16[8,192,256]{2,1,0:T(8,128)(2,1)}, u32[]{:S(2)}, u32[]{:S(2)}) %all-to-all-start.4) | async-done | bytes 786464 | tf_op jit(solution)/shard_map/all_to_all | solution.py:435
  218.7 1.2 fusion.21
  222.1 3.9 %place.5 = (f32[2048,1024]{1,0:T(8,128)}, f32[1024,2048]{1,0:T(8,128)}, bf16[8,2,96,1024]{3,2,1,0:T(8,128)(2,1)}, f32[2,8,32,1024]{3,2,1,0:T(8,128)}, f32[8,2,16,1024]{3,2,1,0:T(8,128)}) custom-call(s32[18]{0:T(128)} %compare_select_fusion.5.table.core_ref._, bf16[400,1024]{1,0:T(8,128)(2,1)} %copy-done.16, bf16[400,1024]{1,0:T(8,128)(2,1)} %collective-permute-done.28.refs_1_), custom_call_target="tpu_custom_call" | custom-call | flops 1 | bytes 1 | tf_op jit(solution)/shard_map/place/pallas_call | solution.py:690
  226.0 4.9 %collective-permute-done.26.refs_5_ = bf16[400,1024]{1,0:T(8,128)(2,1)} collective-permute-done((bf16[400,1024]{1,0:T(8,128)(2,1)S(1)}, bf16[400,1024]{1,0:T(8,128)(2,1)}, u32[]{:S(2)}, u32[]{:S(2)}) %collective-permute-start.26) | collective-permute-done | bytes 819232 | tf_op jit(solution)/shard_map/ppermute | solution.py:549
  230.9 3.2 collective-permute-done.27.refs_6_
  234.6 2.0 collective-permute-start.29
  236.8 1.2 collective-permute-done.32.refs_8_
  237.9 5.4 %place.6 = (f32[2048,1024]{1,0:T(8,128)}, f32[1024,2048]{1,0:T(8,128)}, bf16[8,2,96,1024]{3,2,1,0:T(8,128)(2,1)}, f32[2,8,32,1024]{3,2,1,0:T(8,128)}, f32[8,2,16,1024]{3,2,1,0:T(8,128)}) custom-call(s32[18]{0:T(128)} %compare_select_fusion.5.table.core_ref._, ...), custom_call_target="tpu_custom_call", output_to_operand_aliasing={{0}: (1, {}), {1}: (2, {}), {2}: (3, {}), {3}: (4, {}), {4}... | custom-call | flops 1 | bytes 1 | tf_op jit(solution)/shard_map/place/pallas_call | solution.py:690
  243.4 11.7 %collective-permute-done.29.refs_5_ = bf16[400,1024]{1,0:T(8,128)(2,1)} collective-permute-done((bf16[400,1024]{1,0:T(8,128)(2,1)}, bf16[400,1024]{1,0:T(8,128)(2,1)}, u32[]{:S(2)}, u32[]{:S(2)}) %collective-permute-start.29) | collective-permute-done | bytes 819232 | tf_op jit(solution)/shard_map/ppermute | solution.py:549
  255.1 1.6 collective-permute-done.30.refs_6_
  258.8 1.1 collective-permute-start.34
  260.1 1.6 collective-permute-start.38
  262.7 5.5 %place.7 = (f32[2048,1024]{1,0:T(8,128)}, f32[1024,2048]{1,0:T(8,128)}, bf16[8,2,96,1024]{3,2,1,0:T(8,128)(2,1)}, f32[2,8,32,1024]{3,2,1,0:T(8,128)}, f32[8,2,16,1024]{3,2,1,0:T(8,128)}) custom-call(s32[18]{0:T(128)} %compare_select_fusion.5.table.core_ref._, ...), custom_call_target="tpu_custom_call", output_to_operand_aliasing={{0}: (1, {}), {1}: (2, {}), {2}: (3, {}), {3}: (4, {}), {4}... | custom-call | flops 1 | bytes 1 | tf_op jit(solution)/shard_map/place/pallas_call | solution.py:690
  268.2 6.8 %collective-permute-done.38 = bf16[256,1024]{1,0:T(8,128)(2,1)} collective-permute-done((bf16[256,1024]{1,0:T(8,128)(2,1)S(1)}, bf16[256,1024]{1,0:T(8,128)(2,1)}, u32[]{:S(2)}, u32[]{:S(2)}) %collective-permute-start.38) | collective-permute-done | bytes 524320 | tf_op jit(solution)/shard_map/ppermute | solution.py:462
  275.0 10.2 %collective-permute-done.37 = bf16[256,1024]{1,0:T(8,128)(2,1)S(1)} collective-permute-done((bf16[256,1024]{1,0:T(8,128)(2,1)S(1)}, bf16[256,1024]{1,0:T(8,128)(2,1)S(1)}, u32[]{:S(2)}, u32[]{:S(2)}) %collective-permute-start.37) | collective-permute-done | bytes 524320 | tf_op jit(solution)/shard_map/ppermute | solution.py:462
  286.1 2.0 halves.3
  289.1 1.1 collective-permute-start.40
  291.7 3.8 %all-to-all-start.5 = ((bf16[32,32,128]{2,1,0:T(8,128)(2,1)}), bf16[32,32,128]{2,1,0:T(8,128)(2,1)}, u32[]{:S(2)}, u32[]{:S(2)}) async-start(bf16[32,32,128]{2,1,0:T(8,128)(2,1)} %broadcast_in_dim.55), calls=%async_computation.5 | async-start | bytes 524288 | tf_op jit(solution)/shard_map/all_to_all | solution.py:954
  295.5 5.6 %place.8 = (f32[2048,1024]{1,0:T(8,128)}, f32[1024,2048]{1,0:T(8,128)}, bf16[8,2,96,1024]{3,2,1,0:T(8,128)(2,1)}, f32[2,8,32,1024]{3,2,1,0:T(8,128)}, f32[8,2,16,1024]{3,2,1,0:T(8,128)}) custom-call(s32[18]{0:T(128)} %compare_select_fusion.5.table.core_ref._, ...), custom_call_target="tpu_custom_call", output_to_operand_aliasing={{0}: (1, {}), {1}: (2, {}), {2}: (3, {}), {3}: (4, {}), {4}... | custom-call | flops 1 | bytes 1 | tf_op jit(solution)/shard_map/place/pallas_call | solution.py:690
  301.7 1.2 pad_maximum_fusion.1.refs_5_
  303.1 3.0 fusion.10
  308.5 3.9 %place.9 = (f32[2048,1024]{1,0:T(8,128)}, f32[1024,2048]{1,0:T(8,128)}, bf16[8,2,96,1024]{3,2,1,0:T(8,128)(2,1)}, f32[2,8,32,1024]{3,2,1,0:T(8,128)}, f32[8,2,16,1024]{3,2,1,0:T(8,128)}) custom-call(s32[18]{0:T(128)} %compare_select_fusion.5.table.core_ref._, ...), custom_call_target="tpu_custom_call", output_to_operand_aliasing={{0}: (1, {}), {1}: (2, {}), {2}: (3, {}), {3}: (4, {}), {4}... | custom-call | flops 1 | bytes 1 | tf_op jit(solution)/shard_map/place/pallas_call | solution.py:690
  312.4 1.3 reduce_sum.109
  314.3 5.2 %final_layout.1 = (f32[1024,512]{1,0:T(8,128)}, f32[1024,512]{1,0:T(8,128)}, f32[1024,512]{1,0:T(8,128)}) custom-call(bf16[8,2,96,1024]{3,2,1,0:T(8,128)(2,1)} %get-tuple-element.320.held), custom_call_target="tpu_custom_call" | custom-call | flops 1 | bytes 1 | tf_op jit(solution)/shard_map/final_layout/pallas_call | solution.py:792
  (191 shorter events, 29.2 us)
Async XLA Ops:
  7.8 64.5 %copy-start.12 = (bf16[512,1024]{1,0:T(8,128)(2,1)S(1)}, bf16[512,1024]{1,0:T(8,128)(2,1)}, u32[]{:S(2)}) copy-start(bf16[512,1024]{1,0:T(8,128)(2,1)} %refs_3_.1) | copy-start | bytes 3145732
  37.4 2.4 collective-permute-start.2
  37.5 18.6 %collective-permute-start = (bf16[256,512]{1,0:T(8,128)(2,1)}, bf16[256,512]{1,0:T(8,128)(2,1)S(1)}, u32[]{:S(2)}, u32[]{:S(2)}) collective-permute-start(bf16[256,512]{1,0:T(8,128)(2,1)} %get-tuple-element.174.refs_0_), channel_id=1, source_target_pairs={{0,8},{8,16},{16,24},{24,28},{28,20},{20,12},{12,4},{4,0},{1,9},{9... | collective-permute-start | bytes 786440 | tf_op jit(solution)/shard_map/ppermute | solution.py:549
  38.2 17.9 %collective-permute-start.1 = (bf16[256,512]{1,0:T(8,128)(2,1)}, bf16[256,512]{1,0:T(8,128)(2,1)S(1)}, u32[]{:S(2)}, u32[]{:S(2)}) collective-permute-start(bf16[256,512]{1,0:T(8,128)(2,1)} %get-tuple-element.174.refs_0_), channel_id=1, source_target_pairs={{0,4},{8,0},{16,8},{24,16},{28,24},{20,28},{12,20},{4,12},{1,5},{9... | collective-permute-start | bytes 786440 | tf_op jit(solution)/shard_map/ppermute | solution.py:549
  56.1 42.9 %copy-start.32 = (bf16[256,512]{1,0:T(8,128)(2,1)}, bf16[256,512]{1,0:T(8,128)(2,1)S(1)}, u32[]{:S(2)}) copy-start(bf16[256,512]{1,0:T(8,128)(2,1)S(1)} %collective-permute-done.refs_1_) | copy-start | bytes 786436
  56.1 42.9 %copy-start.33 = (bf16[256,512]{1,0:T(8,128)(2,1)}, bf16[256,512]{1,0:T(8,128)(2,1)S(1)}, u32[]{:S(2)}) copy-start(bf16[256,512]{1,0:T(8,128)(2,1)S(1)} %collective-permute-done.1.refs_2_) | copy-start | bytes 786436
  56.1 16.2 %all-to-all-start.1 = ((bf16[8,64,256]{2,1,0:T(8,128)(2,1)}), bf16[8,64,256]{2,1,0:T(8,128)(2,1)S(1)}, u32[]{:S(2)}, u32[]{:S(2)}) async-start(bf16[8,64,256]{2,1,0:T(8,128)(2,1)} %get-tuple-element.179), calls=%async_computation.1 | async-start | bytes 524288 | tf_op jit(solution)/shard_map/all_to_all | solution.py:435
  59.5 11.2 %collective-permute-start.3 = (bf16[256,512]{1,0:T(8,128)(2,1)S(1)}, bf16[256,512]{1,0:T(8,128)(2,1)S(1)}, u32[]{:S(2)}, u32[]{:S(2)}) collective-permute-start(bf16[256,512]{1,0:T(8,128)(2,1)S(1)} %collective-permute-done.refs_1_), channel_id=1, source_target_pairs={{0,8},{8,16},{16,24},{24,28},{28,20},{20,12},{12,4},{4,0},{1,9},{9... | collective-permute-start | bytes 786440 | tf_op jit(solution)/shard_map/ppermute | solution.py:549
  61.4 10.9 %collective-permute-start.4 = (bf16[256,512]{1,0:T(8,128)(2,1)S(1)}, bf16[256,512]{1,0:T(8,128)(2,1)S(1)}, u32[]{:S(2)}, u32[]{:S(2)}) collective-permute-start(bf16[256,512]{1,0:T(8,128)(2,1)S(1)} %collective-permute-done.1.refs_2_), channel_id=1, source_target_pairs={{0,4},{8,0},{16,8},{24,16},{28,24},{20,28},{12,20},{4,12},{1,5},{9... | collective-permute-start | bytes 786440 | tf_op jit(solution)/shard_map/ppermute | solution.py:549
  70.7 28.2 %copy-start.34 = (bf16[256,512]{1,0:T(8,128)(2,1)}, bf16[256,512]{1,0:T(8,128)(2,1)S(1)}, u32[]{:S(2)}) copy-start(bf16[256,512]{1,0:T(8,128)(2,1)S(1)} %collective-permute-done.3.refs_3_) | copy-start | bytes 786436
  72.3 26.6 %copy-start.35 = (bf16[256,512]{1,0:T(8,128)(2,1)}, bf16[256,512]{1,0:T(8,128)(2,1)S(1)}, u32[]{:S(2)}) copy-start(bf16[256,512]{1,0:T(8,128)(2,1)S(1)} %collective-permute-done.4.refs_4_) | copy-start | bytes 786436
  72.8 13.6 %copy-start.19 = (bf16[256,1024]{1,0:T(8,128)(2,1)}, bf16[256,1024]{1,0:T(8,128)(2,1)S(1)}, u32[]{:S(2)}) copy-start(bf16[256,1024]{1,0:T(8,128)(2,1)S(1)} %convolution_convert_fusion.refs_0_) | copy-start | bytes 1572868
  72.8 13.6 %collective-permute-start.5 = (bf16[256,1024]{1,0:T(8,128)(2,1)S(1)}, bf16[256,1024]{1,0:T(8,128)(2,1)S(1)}, u32[]{:S(2)}, u32[]{:S(2)}) collective-permute-start(bf16[256,1024]{1,0:T(8,128)(2,1)S(1)} %convolution_convert_fusion.refs_0_), channel_id=1, source_target_pairs={{0,1},{1,0},{2,3},{3,2},{4,5},{5,4},{6,7},{7,6},{8,9},{9,8},{10,11... | collective-permute-start | bytes 1572872 | tf_op jit(solution)/shard_map/ppermute | solution.py:462
  74.4 24.6 %collective-permute-start.6 = (bf16[256,512]{1,0:T(8,128)(2,1)S(1)}, bf16[256,512]{1,0:T(8,128)(2,1)S(1)}, u32[]{:S(2)}, u32[]{:S(2)}) collective-permute-start(bf16[256,512]{1,0:T(8,128)(2,1)S(1)} %collective-permute-done.3.refs_3_), channel_id=1, source_target_pairs={{0,8},{8,16},{16,24},{24,28},{28,20},{20,12},{12,4},{4,0},{1,9},{9... | collective-permute-start | bytes 786440 | tf_op jit(solution)/shard_map/ppermute | solution.py:549
  77.1 21.9 %collective-permute-start.7 = (bf16[256,512]{1,0:T(8,128)(2,1)S(1)}, bf16[256,512]{1,0:T(8,128)(2,1)S(1)}, u32[]{:S(2)}, u32[]{:S(2)}) collective-permute-start(bf16[256,512]{1,0:T(8,128)(2,1)S(1)} %collective-permute-done.4.refs_4_), channel_id=1, source_target_pairs={{0,4},{8,0},{16,8},{24,16},{28,24},{20,28},{12,20},{4,12},{1,5},{9... | collective-permute-start | bytes 786440 | tf_op jit(solution)/shard_map/ppermute | solution.py:549
  99.0 10.9 %copy-start.21 = (bf16[256,512]{1,0:T(8,128)(2,1)}, bf16[256,512]{1,0:T(8,128)(2,1)S(1)}, u32[]{:S(2)}) copy-start(bf16[256,512]{1,0:T(8,128)(2,1)S(1)} %collective-permute-done.6.left.refs_5_) | copy-start | bytes 786436
  99.0 3.7 %collective-permute-start.9 = (bf16[256,2048]{1,0:T(8,128)(2,1)}, bf16[256,2048]{1,0:T(8,128)(2,1)S(1)}, u32[]{:S(2)}, u32[]{:S(2)}) collective-permute-start(bf16[256,2048]{1,0:T(8,128)(2,1)} %get-tuple-element.192), channel_id=1, source_target_pairs={{0,2},{2,0},{1,3},{3,1},{4,6},{6,4},{5,7},{7,5},{8,10},{10,8},{9,1... | collective-permute-start | bytes 3145736 | tf_op jit(solution)/shard_map/ppermute | solution.py:431
  99.1 3.6 %collective-permute-start.8 = (bf16[256,1024]{1,0:T(8,128)(2,1)}, bf16[256,1024]{1,0:T(8,128)(2,1)S(1)}, u32[]{:S(2)}, u32[]{:S(2)}) collective-permute-start(bf16[256,1024]{1,0:T(8,128)(2,1)} %get-tuple-element.190), channel_id=1, source_target_pairs={{0,2},{2,0},{1,3},{3,1},{4,6},{6,4},{5,7},{7,5},{8,10},{10,8},{9,1... | collective-permute-start | bytes 1572872 | tf_op jit(solution)/shard_map/ppermute | solution.py:431
  99.6 14.1 %collective-permute-start.14 = (bf16[256,1024]{1,0:T(8,128)(2,1)}, bf16[256,1024]{1,0:T(8,128)(2,1)S(1)}, u32[]{:S(2)}, u32[]{:S(2)}) collective-permute-start(bf16[256,1024]{1,0:T(8,128)(2,1)} %get-tuple-element.201.refs_0_), channel_id=1, source_target_pairs={{0,1},{1,0},{2,3},{3,2},{4,5},{5,4},{6,7},{7,6},{8,9},{9,8},{10,11... | collective-permute-start | bytes 1572872 | tf_op jit(solution)/shard_map/ppermute | solution.py:462
  107.6 13.4 %collective-permute-start.10 = (bf16[256,512]{1,0:T(8,128)(2,1)}, bf16[256,512]{1,0:T(8,128)(2,1)S(1)}, u32[]{:S(2)}, u32[]{:S(2)}) collective-permute-start(bf16[256,512]{1,0:T(8,128)(2,1)} %get-tuple-element.193), channel_id=1, source_target_pairs={{0,8},{8,16},{16,24},{24,28},{28,20},{20,12},{12,4},{4,0},{1,9},{9... | collective-permute-start | bytes 786440 | tf_op jit(solution)/shard_map/ppermute | solution.py:604
  109.8 11.1 %collective-permute-start.11 = (bf16[256,512]{1,0:T(8,128)(2,1)}, bf16[256,512]{1,0:T(8,128)(2,1)S(1)}, u32[]{:S(2)}, u32[]{:S(2)}) collective-permute-start(bf16[256,512]{1,0:T(8,128)(2,1)} %get-tuple-element.194), channel_id=1, source_target_pairs={{0,4},{8,0},{16,8},{24,16},{28,24},{20,28},{12,20},{4,12},{1,5},{9... | collective-permute-start | bytes 786440 | tf_op jit(solution)/shard_map/ppermute | solution.py:604
  111.5 7.4 %collective-permute-start.12 = (bf16[256,256]{1,0:T(8,128)(2,1)}, bf16[256,256]{1,0:T(8,128)(2,1)S(1)}, u32[]{:S(2)}, u32[]{:S(2)}) collective-permute-start(bf16[256,256]{1,0:T(8,128)(2,1)} %get-tuple-element.197), channel_id=1, source_target_pairs={{0,8},{8,16},{16,24},{24,28},{28,20},{20,12},{12,4},{4,0},{1,9},{9... | collective-permute-start | bytes 393224 | tf_op jit(solution)/shard_map/ppermute | solution.py:549
  113.6 7.4 %collective-permute-start.13 = (bf16[256,256]{1,0:T(8,128)(2,1)}, bf16[256,256]{1,0:T(8,128)(2,1)S(1)}, u32[]{:S(2)}, u32[]{:S(2)}) collective-permute-start(bf16[256,256]{1,0:T(8,128)(2,1)} %get-tuple-element.198), channel_id=1, source_target_pairs={{0,4},{8,0},{16,8},{24,16},{28,24},{20,28},{12,20},{4,12},{1,5},{9... | collective-permute-start | bytes 393224 | tf_op jit(solution)/shard_map/ppermute | solution.py:549
  125.5 19.4 %collective-permute-start.15 = (bf16[256,1024]{1,0:T(8,128)(2,1)}, bf16[256,1024]{1,0:T(8,128)(2,1)S(1)}, u32[]{:S(2)}, u32[]{:S(2)}) collective-permute-start(bf16[256,1024]{1,0:T(8,128)(2,1)} %get-tuple-element.213), channel_id=1, source_target_pairs={{0,8},{8,16},{16,24},{24,28},{28,20},{20,12},{12,4},{4,0},{1,9},{9... | collective-permute-start | bytes 1572872 | tf_op jit(solution)/shard_map/ppermute | solution.py:604
  126.3 18.5 %collective-permute-start.16 = (bf16[256,1024]{1,0:T(8,128)(2,1)}, bf16[256,1024]{1,0:T(8,128)(2,1)S(1)}, u32[]{:S(2)}, u32[]{:S(2)}) collective-permute-start(bf16[256,1024]{1,0:T(8,128)(2,1)} %get-tuple-element.214), channel_id=1, source_target_pairs={{0,4},{8,0},{16,8},{24,16},{28,24},{20,28},{12,20},{4,12},{1,5},{9... | collective-permute-start | bytes 1572872 | tf_op jit(solution)/shard_map/ppermute | solution.py:604
  127.5 17.3 %all-to-all-start.2 = ((bf16[8,64,256]{2,1,0:T(8,128)(2,1)}), bf16[8,64,256]{2,1,0:T(8,128)(2,1)S(1)}, u32[]{:S(2)}, u32[]{:S(2)}) async-start(bf16[8,64,256]{2,1,0:T(8,128)(2,1)} %bitcast.9), calls=%async_computation.2 | async-start | bytes 524288 | tf_op jit(solution)/shard_map/all_to_all | solution.py:435
  131.8 21.9 %collective-permute-start.22 = (bf16[256,1024]{1,0:T(8,128)(2,1)}, bf16[256,1024]{1,0:T(8,128)(2,1)S(1)}, u32[]{:S(2)}, u32[]{:S(2)}) collective-permute-start(bf16[256,1024]{1,0:T(8,128)(2,1)} %get-tuple-element.244), channel_id=1, source_target_pairs={{0,2},{2,0},{1,3},{3,1},{4,6},{6,4},{5,7},{7,5},{8,10},{10,8},{9,1... | collective-permute-start | bytes 1572872 | tf_op jit(solution)/shard_map/ppermute | solution.py:431
  131.9 21.9 %collective-permute-start.21 = (bf16[256,256]{1,0:T(8,128)(2,1)S(1)}, bf16[256,256]{1,0:T(8,128)(2,1)S(1)}, u32[]{:S(2)}, u32[]{:S(2)}) collective-permute-start(bf16[256,256]{1,0:T(8,128)(2,1)S(1)} %constant_dynamic-slice_fusion.1), channel_id=1, source_target_pairs={{0,2},{2,0},{1,3},{3,1},{4,6},{6,4},{5,7},{7,5},{8,10},{10,8},{9,1... | collective-permute-start | bytes 393224 | tf_op jit(solution)/shard_map/ppermute | solution.py:431
  135.4 61.7 %collective-permute-start.24 = (bf16[2048,512]{1,0:T(8,128)(2,1)}, bf16[2048,512]{1,0:T(8,128)(2,1)}, u32[]{:S(2)}, u32[]{:S(2)}) collective-permute-start(bf16[2048,512]{1,0:T(8,128)(2,1)} %join.1.refs_0_), channel_id=1, source_target_pairs={{0,1},{1,0},{2,3},{3,2},{4,5},{5,4},{6,7},{7,6},{8,9},{9,8},{10,11... | collective-permute-start | bytes 6291464 | tf_op jit(solution)/shard_map/ppermute | solution.py:462
  150.3 20.7 %collective-permute-start.17 = (bf16[256,1024]{1,0:T(8,128)(2,1)}, bf16[256,1024]{1,0:T(8,128)(2,1)}, u32[]{:S(2)}, u32[]{:S(2)}) collective-permute-start(bf16[256,1024]{1,0:T(8,128)(2,1)} %get-tuple-element.221), channel_id=1, source_target_pairs={{0,8},{8,16},{16,24},{24,28},{28,20},{20,12},{12,4},{4,0},{1,9},{9... | collective-permute-start | bytes 1572872 | tf_op jit(solution)/shard_map/ppermute | solution.py:604
  150.9 20.2 %collective-permute-start.18 = (bf16[256,1024]{1,0:T(8,128)(2,1)}, bf16[256,1024]{1,0:T(8,128)(2,1)}, u32[]{:S(2)}, u32[]{:S(2)}) collective-permute-start(bf16[256,1024]{1,0:T(8,128)(2,1)} %get-tuple-element.222), channel_id=1, source_target_pairs={{0,4},{8,0},{16,8},{24,16},{28,24},{20,28},{12,20},{4,12},{1,5},{9... | collective-permute-start | bytes 1572872 | tf_op jit(solution)/shard_map/ppermute | solution.py:604
  154.9 35.2 %all-to-all-start.3 = ((bf16[8,32,1024]{2,1,0:T(8,128)(2,1)}), bf16[8,32,1024]{2,1,0:T(8,128)(2,1)S(1)}, u32[]{:S(2)}, u32[]{:S(2)}) async-start(bf16[8,32,1024]{2,1,0:T(8,128)(2,1)} %bitcast.10), calls=%async_computation.3 | async-start | bytes 1048576 | tf_op jit(solution)/shard_map/all_to_all | solution.py:435
  174.9 14.1 %collective-permute-start.19 = (bf16[256,1024]{1,0:T(8,128)(2,1)}, bf16[256,1024]{1,0:T(8,128)(2,1)S(1)}, u32[]{:S(2)}, u32[]{:S(2)}) collective-permute-start(bf16[256,1024]{1,0:T(8,128)(2,1)} %get-tuple-element.235), channel_id=1, source_target_pairs={{0,8},{8,16},{16,24},{24,28},{28,20},{20,12},{12,4},{4,0},{1,9},{9... | collective-permute-start | bytes 1572872 | tf_op jit(solution)/shard_map/ppermute | solution.py:604
  177.0 12.1 %collective-permute-start.20 = (bf16[256,1024]{1,0:T(8,128)(2,1)}, bf16[256,1024]{1,0:T(8,128)(2,1)S(1)}, u32[]{:S(2)}, u32[]{:S(2)}) collective-permute-start(bf16[256,1024]{1,0:T(8,128)(2,1)} %get-tuple-element.236), channel_id=1, source_target_pairs={{0,4},{8,0},{16,8},{24,16},{28,24},{20,28},{12,20},{4,12},{1,5},{9... | collective-permute-start | bytes 1572872 | tf_op jit(solution)/shard_map/ppermute | solution.py:604
  177.0 12.1 %collective-permute-start.23 = (bf16[8,128,256]{2,1,0:T(8,128)(2,1)S(1)}, bf16[8,128,256]{2,1,0:T(8,128)(2,1)S(1)}, u32[]{:S(2)}, u32[]{:S(2)}) collective-permute-start(bf16[8,128,256]{2,1,0:T(8,128)(2,1)S(1)} %get-tuple-element.246), channel_id=1, source_target_pairs={{0,2},{2,0},{1,3},{3,1},{4,6},{6,4},{5,7},{7,5},{8,10},{10,8},{9,1... | collective-permute-start | bytes 1572872 | tf_op jit(solution)/shard_map/ppermute | solution.py:431
  191.0 27.7 %all-to-all-start.4 = ((bf16[8,192,256]{2,1,0:T(8,128)(2,1)}), bf16[8,192,256]{2,1,0:T(8,128)(2,1)}, u32[]{:S(2)}, u32[]{:S(2)}) async-start(bf16[8,192,256]{2,1,0:T(8,128)(2,1)} %pad_maximum_fusion.2), calls=%async_computation.4 | async-start | bytes 1572864 | tf_op jit(solution)/shard_map/all_to_all | solution.py:435
  203.1 4.1 %collective-permute-start.25 = (bf16[96,1024]{1,0:T(8,128)(2,1)S(1)}, bf16[96,1024]{1,0:T(8,128)(2,1)S(1)}, u32[]{:S(2)}, u32[]{:S(2)}) collective-permute-start(bf16[96,1024]{1,0:T(8,128)(2,1)S(1)} %constant_dynamic-slice_fusion), channel_id=1, source_target_pairs={{0,2},{2,0},{1,3},{3,1},{4,6},{6,4},{5,7},{7,5},{8,10},{10,8},{9,1... | collective-permute-start | bytes 589832 | tf_op jit(solution)/shard_map/ppermute | solution.py:431
  207.1 12.8 %copy-start.13 = (bf16[1024,512]{1,0:T(8,128)(2,1)S(1)}, bf16[1024,512]{1,0:T(8,128)(2,1)}, u32[]{:S(2)}) copy-start(bf16[1024,512]{1,0:T(8,128)(2,1)} %refs_0_.1) | copy-start | bytes 3145732
  208.5 12.4 %copy-start.16 = (bf16[400,1024]{1,0:T(8,128)(2,1)}, bf16[400,1024]{1,0:T(8,128)(2,1)S(1)}, u32[]{:S(2)}) copy-start(bf16[400,1024]{1,0:T(8,128)(2,1)S(1)} %pad_maximum_fusion.refs_0_) | copy-start | bytes 2457604
  208.5 11.9 %copy-start.14 = (bf16[1024,512]{1,0:T(8,128)(2,1)S(1)}, bf16[1024,512]{1,0:T(8,128)(2,1)}, u32[]{:S(2)}) copy-start(bf16[1024,512]{1,0:T(8,128)(2,1)} %refs_1_.1) | copy-start | bytes 3145732
  208.5 13.6 %collective-permute-start.28 = (bf16[400,1024]{1,0:T(8,128)(2,1)S(1)}, bf16[400,1024]{1,0:T(8,128)(2,1)}, u32[]{:S(2)}, u32[]{:S(2)}) collective-permute-start(bf16[400,1024]{1,0:T(8,128)(2,1)S(1)} %pad_maximum_fusion.refs_0_), channel_id=1, source_target_pairs={{0,2},{2,0},{1,3},{3,1},{4,6},{6,4},{5,7},{7,5},{8,10},{10,8},{9,1... | collective-permute-start | bytes 2457608 | tf_op jit(solution)/shard_map/ppermute | solution.py:431
  208.8 22.1 %collective-permute-start.26 = (bf16[400,1024]{1,0:T(8,128)(2,1)S(1)}, bf16[400,1024]{1,0:T(8,128)(2,1)}, u32[]{:S(2)}, u32[]{:S(2)}) collective-permute-start(bf16[400,1024]{1,0:T(8,128)(2,1)S(1)} %pad_maximum_fusion.refs_0_), channel_id=1, source_target_pairs={{0,8},{8,16},{16,24},{24,28},{28,20},{20,12},{12,4},{4,0},{1,9},{9... | collective-permute-start | bytes 2457608 | tf_op jit(solution)/shard_map/ppermute | solution.py:549
  210.8 23.2 %collective-permute-start.27 = (bf16[400,1024]{1,0:T(8,128)(2,1)S(1)}, bf16[400,1024]{1,0:T(8,128)(2,1)}, u32[]{:S(2)}, u32[]{:S(2)}) collective-permute-start(bf16[400,1024]{1,0:T(8,128)(2,1)S(1)} %pad_maximum_fusion.refs_0_), channel_id=1, source_target_pairs={{0,4},{8,0},{16,8},{24,16},{28,24},{20,28},{12,20},{4,12},{1,5},{9... | collective-permute-start | bytes 2457608 | tf_op jit(solution)/shard_map/ppermute | solution.py:549
  234.1 25.8 %copy-start.8 = (bf16[256,1024]{1,0:T(8,128)(2,1)S(1)}, bf16[256,1024]{1,0:T(8,128)(2,1)}, u32[]{:S(2)}) copy-start(bf16[256,1024]{1,0:T(8,128)(2,1)} %input_ref.3) | copy-start | bytes 1572868
  234.1 26.0 %copy-start.24 = (bf16[256,1024]{1,0:T(8,128)(2,1)S(1)}, bf16[256,1024]{1,0:T(8,128)(2,1)}, u32[]{:S(2)}) copy-start(bf16[256,1024]{1,0:T(8,128)(2,1)} %get-tuple-element.294) | copy-start | bytes 1572868
  234.1 2.7 collective-permute-start.31
  234.1 3.8 %collective-permute-start.32 = (bf16[400,1024]{1,0:T(8,128)(2,1)}, bf16[400,1024]{1,0:T(8,128)(2,1)}, u32[]{:S(2)}, u32[]{:S(2)}) collective-permute-start(bf16[400,1024]{1,0:T(8,128)(2,1)} %collective-permute-done.27.refs_6_), channel_id=1, source_target_pairs={{0,2},{2,0},{1,3},{3,1},{4,6},{6,4},{5,7},{7,5},{8,10},{10,8},{9,1... | collective-permute-start | bytes 2457608 | tf_op jit(solution)/shard_map/ppermute | solution.py:431
  234.6 20.5 %collective-permute-start.29 = (bf16[400,1024]{1,0:T(8,128)(2,1)}, bf16[400,1024]{1,0:T(8,128)(2,1)}, u32[]{:S(2)}, u32[]{:S(2)}) collective-permute-start(bf16[400,1024]{1,0:T(8,128)(2,1)} %collective-permute-done.26.refs_5_), channel_id=1, source_target_pairs={{0,8},{8,16},{16,24},{24,28},{28,20},{20,12},{12,4},{4,0},{1,9},{9... | collective-permute-start | bytes 2457608 | tf_op jit(solution)/shard_map/ppermute | solution.py:549
  236.6 20.1 %collective-permute-start.30 = (bf16[400,1024]{1,0:T(8,128)(2,1)}, bf16[400,1024]{1,0:T(8,128)(2,1)S(1)}, u32[]{:S(2)}, u32[]{:S(2)}) collective-permute-start(bf16[400,1024]{1,0:T(8,128)(2,1)} %collective-permute-done.27.refs_6_), channel_id=1, source_target_pairs={{0,4},{8,0},{16,8},{24,16},{28,24},{20,28},{12,20},{4,12},{1,5},{9... | collective-permute-start | bytes 2457608 | tf_op jit(solution)/shard_map/ppermute | solution.py:549
  243.4 18.9 %copy-start.43 = (s32[32]{0:T(128)S(1)}, s32[32]{0:T(128)}, u32[]{:S(2)}) copy-start(s32[32]{0:T(128)} %steps_ref.1) | copy-start | bytes 388
  243.4 18.9 %copy-start.42 = (s32[256]{0:T(256)S(1)}, s32[256]{0:T(256)}, u32[]{:S(2)}) copy-start(s32[256]{0:T(256)} %param.20) | copy-start | bytes 3076
  257.7 4.1 %collective-permute-start.35 = (bf16[400,1024]{1,0:T(8,128)(2,1)}, bf16[400,1024]{1,0:T(8,128)(2,1)}, u32[]{:S(2)}, u32[]{:S(2)}) collective-permute-start(bf16[400,1024]{1,0:T(8,128)(2,1)} %collective-permute-done.29.refs_5_), channel_id=1, source_target_pairs={{0,2},{2,0},{1,3},{3,1},{4,6},{6,4},{5,7},{7,5},{8,10},{10,8},{9,1... | collective-permute-start | bytes 2457608 | tf_op jit(solution)/shard_map/ppermute | solution.py:431
  257.7 27.5 %collective-permute-start.33 = (bf16[400,1024]{1,0:T(8,128)(2,1)}, bf16[400,1024]{1,0:T(8,128)(2,1)S(1)}, u32[]{:S(2)}, u32[]{:S(2)}) collective-permute-start(bf16[400,1024]{1,0:T(8,128)(2,1)} %collective-permute-done.29.refs_5_), channel_id=1, source_target_pairs={{0,8},{8,16},{16,24},{24,28},{28,20},{20,12},{12,4},{4,0},{1,9},{9... | collective-permute-start | bytes 2457608 | tf_op jit(solution)/shard_map/ppermute | solution.py:549
  258.6 4.2 %collective-permute-start.36 = (bf16[400,1024]{1,0:T(8,128)(2,1)}, bf16[400,1024]{1,0:T(8,128)(2,1)}, u32[]{:S(2)}, u32[]{:S(2)}) collective-permute-start(bf16[400,1024]{1,0:T(8,128)(2,1)} %copy-done.23), channel_id=1, source_target_pairs={{0,2},{2,0},{1,3},{3,1},{4,6},{6,4},{5,7},{7,5},{8,10},{10,8},{9,1... | collective-permute-start | bytes 2457608 | tf_op jit(solution)/shard_map/ppermute | solution.py:431
  258.8 26.4 %collective-permute-start.34 = (bf16[400,1024]{1,0:T(8,128)(2,1)}, bf16[400,1024]{1,0:T(8,128)(2,1)}, u32[]{:S(2)}, u32[]{:S(2)}) collective-permute-start(bf16[400,1024]{1,0:T(8,128)(2,1)} %copy-done.23), channel_id=1, source_target_pairs={{0,4},{8,0},{16,8},{24,16},{28,24},{20,28},{12,20},{4,12},{1,5},{9... | collective-permute-start | bytes 2457608 | tf_op jit(solution)/shard_map/ppermute | solution.py:549
  260.1 15.0 %collective-permute-start.38 = (bf16[256,1024]{1,0:T(8,128)(2,1)S(1)}, bf16[256,1024]{1,0:T(8,128)(2,1)}, u32[]{:S(2)}, u32[]{:S(2)}) collective-permute-start(bf16[256,1024]{1,0:T(8,128)(2,1)S(1)} %copy-done.24), channel_id=1, source_target_pairs={{0,1},{1,0},{2,3},{3,2},{4,5},{5,4},{6,7},{7,6},{8,9},{9,8},{10,11... | collective-permute-start | bytes 1572872 | tf_op jit(solution)/shard_map/ppermute | solution.py:462
  261.7 23.5 %collective-permute-start.37 = (bf16[256,1024]{1,0:T(8,128)(2,1)S(1)}, bf16[256,1024]{1,0:T(8,128)(2,1)S(1)}, u32[]{:S(2)}, u32[]{:S(2)}) collective-permute-start(bf16[256,1024]{1,0:T(8,128)(2,1)S(1)} %convert_element_type.69), channel_id=1, source_target_pairs={{0,1},{1,0},{2,3},{3,2},{4,5},{5,4},{6,7},{7,6},{8,9},{9,8},{10,11... | collective-permute-start | bytes 1572872 | tf_op jit(solution)/shard_map/ppermute | solution.py:462
  262.7 27.5 %copy-start.38 = (f32[1024]{0:T(1024)S(1)}, f32[1024]{0:T(1024)}, u32[]{:S(2)}) copy-start(f32[1024]{0:T(1024)} %param.22) | copy-start | bytes 12292
  285.2 10.3 %collective-permute-start.41 = (bf16[400,1024]{1,0:T(8,128)(2,1)S(1)}, bf16[400,1024]{1,0:T(8,128)(2,1)}, u32[]{:S(2)}, u32[]{:S(2)}) collective-permute-start(bf16[400,1024]{1,0:T(8,128)(2,1)S(1)} %collective-permute-done.33.left.refs_5_), channel_id=1, source_target_pairs={{0,2},{2,0},{1,3},{3,1},{4,6},{6,4},{5,7},{7,5},{8,10},{10,8},{9,1... | collective-permute-start | bytes 2457608 | tf_op jit(solution)/shard_map/ppermute | solution.py:431
  285.3 10.2 %collective-permute-start.42 = (bf16[400,1024]{1,0:T(8,128)(2,1)}, bf16[400,1024]{1,0:T(8,128)(2,1)}, u32[]{:S(2)}, u32[]{:S(2)}) collective-permute-start(bf16[400,1024]{1,0:T(8,128)(2,1)} %collective-permute-done.34.right.refs_6_), channel_id=1, source_target_pairs={{0,2},{2,0},{1,3},{3,1},{4,6},{6,4},{5,7},{7,5},{8,10},{10,8},{9,1... | collective-permute-start | bytes 2457608 | tf_op jit(solution)/shard_map/ppermute | solution.py:431
  288.2 12.9 %collective-permute-start.39 = (bf16[400,512]{1,0:T(8,128)(2,1)}, bf16[400,512]{1,0:T(8,128)(2,1)}, u32[]{:S(2)}, u32[]{:S(2)}) collective-permute-start(bf16[400,512]{1,0:T(8,128)(2,1)} %get-tuple-element.301), channel_id=1, source_target_pairs={{0,8},{8,16},{16,24},{24,28},{28,20},{20,12},{12,4},{4,0},{1,9},{9... | collective-permute-start | bytes 1228808 | tf_op jit(solution)/shard_map/ppermute | solution.py:549
  289.1 12.7 %collective-permute-start.40 = (bf16[400,512]{1,0:T(8,128)(2,1)}, bf16[400,512]{1,0:T(8,128)(2,1)}, u32[]{:S(2)}, u32[]{:S(2)}) collective-permute-start(bf16[400,512]{1,0:T(8,128)(2,1)} %get-tuple-element.302), channel_id=1, source_target_pairs={{0,4},{8,0},{16,8},{24,16},{28,24},{20,28},{12,20},{4,12},{1,5},{9... | collective-permute-start | bytes 1228808 | tf_op jit(solution)/shard_map/ppermute | solution.py:549
  291.7 15.2 %all-to-all-start.5 = ((bf16[32,32,128]{2,1,0:T(8,128)(2,1)}), bf16[32,32,128]{2,1,0:T(8,128)(2,1)}, u32[]{:S(2)}, u32[]{:S(2)}) async-start(bf16[32,32,128]{2,1,0:T(8,128)(2,1)} %broadcast_in_dim.55), calls=%async_computation.5 | async-start | bytes 524288 | tf_op jit(solution)/shard_map/all_to_all | solution.py:954
  302.9 5.5 %collective-permute-start.43 = (bf16[400,1024]{1,0:T(8,128)(2,1)S(1)}, bf16[400,1024]{1,0:T(8,128)(2,1)}, u32[]{:S(2)}, u32[]{:S(2)}) collective-permute-start(bf16[400,1024]{1,0:T(8,128)(2,1)S(1)} %pad_maximum_fusion.1.refs_5_), channel_id=1, source_target_pairs={{0,2},{2,0},{1,3},{3,1},{4,6},{6,4},{5,7},{7,5},{8,10},{10,8},{9,1... | collective-permute-start | bytes 2457608 | tf_op jit(solution)/shard_map/ppermute | solution.py:431
  (29 other events, 108.8 us)

commit v13 on v12

--- a/solution.py
+++ b/solution.py
@@ -854,9 +854,9 @@
     inputs.send(inputs.ready)
     other = swap_cores(own)
     raw, out, logsum = attention_forward(queries, own, other, crops)
-    out = visit([inputs], out)
     attn_out = gather_queries(out, heads, split, rows)
     attn_out = visit([inputs], attn_out)
+    visit([inputs], ())
     branches = across_heads(product(attn_out, output_weight, 0, 0).astype(BF16))
     keep, give, keep_in, give_in, hidden, dup_bias, mlp_part, d_mlp_part = mlp(
         table,
@@ -888,8 +888,9 @@
         parts = across_heads(parts[0])
     out_near, out_far = share_halves(attn_out, 0)
     doutput = product(out_near, d_branch) + product(out_far, swap_cores(d_branch))
-    doutput = to_heads(doutput.astype(BF16).reshape(chips, -1, model))
-    grads = visit([ring], grads)
+    doutput = doutput.astype(BF16).reshape(chips, -1, model)
+    grads, doutput = visit([ring], (grads, doutput))
+    doutput = to_heads(doutput)
     *dquery, far_sums = backward_piece(
         queries, grads, raw, logsum, [], other, [], 0, 1, crops, (F32, BF16)
     )
@@ -926,6 +927,11 @@
             lax.psum(product(attn_in, grad, 0, 1).astype(BF16), ("chip", "core")).astype(F32)
             for grad in (dquery, dkey, dvalue)
         ]
+    blocks, mlp_out = lax.optimization_barrier((blocks, mlp_out))
+    block_output = hidden + down_bias
+    for part in mlp_out:
+        block_output += part.astype(F32)
+    block_output = block_output.astype(BF16)
     total = ring.finish()
     start = total.shape[0]
     ring.size, ring.extra = size, blocks.shape[0] - size - small_rows
@@ -936,7 +942,6 @@
         + product(dkey, key_weight, 0, 1)
         + product(dvalue, value_weight, 0, 1)
     )
-    d_part = visit([gathered], d_part)
     d_in = across_heads(d_part.astype(BF16))
     unit_attn, inverse_attn = normalize(block_input.astype(F32))
     onehot = (segments[:, None] == jnp.arange(crops, dtype=jnp.int32)[None, :]).astype(F32)
@@ -952,20 +957,17 @@
     everyone = ("chip", "core", "head")
     ends = jnp.broadcast_to(ends, (lax.axis_size(everyone),) + ends.shape)
     ends = lax.all_to_all(ends, everyone, 0, 0, tiled=True)
-    visit([gathered], ())
-    d_in, mlp_out = visit([gathered], (d_in, mlp_out))
-    block_output = hidden + down_bias
-    for part in mlp_out:
-        block_output += part.astype(F32)
-    block_output = block_output.astype(BF16)
+    visit([gathered], d_part)
+    d_in, block_output = visit([gathered], (d_in, block_output))
+    ends = visit([gathered], ends)
+    ends = jnp.sum(ends.astype(F32), axis=0).reshape(-1)[: 3 * model].reshape(3, model)
     d_in = functools.reduce(jnp.add, (part.astype(F32) for part in d_in))
     input_grad = (d_hidden + normalize_back(d_in * gain_attn, unit_attn, inverse_attn)).astype(
         BF16
     )
     while gathered.busy():
-        visit([gathered], ())
+        ends, input_grad = visit([gathered], (ends, input_grad))
     ddown_weight, dup_weight, *rest = gathered.outputs
-    ends = jnp.sum(ends.astype(F32), axis=0).reshape(-1)[: 3 * model].reshape(3, model)
     if split == 1:
         held, doutput_weight, small = rest
         projections = final_layout(held)

time: 322 us -> 323 us (level)
    ppermute x5, waiting for transfers between devices: 26.5 us -> 5.21 us  [across_heads(): return [part, lax.ppermute(part, 'head', [(0, 1), (1, 0)])]]
    all_to_all x1, waiting for transfers between devices: 0.76 us -> 15.7 us  [local(): ends = lax.all_to_all(ends, everyone, 0, 0, tiled=True)]
    ppermute x24, waiting for transfers between devices: 35 us -> 45.7 us  [send(): lax.ppermute(block, 'chip', ring_pairs(direction))]
    all_to_all x4, waiting for transfers between devices: 15.8 us -> 7.54 us  [to_heads(): return lax.all_to_all(blocks, 'chip', 0, 0, tiled=True)]
    unnamed x91 -> x99, local copies, waits for them, and re-layouts: 9.41 us -> 8.69 us
  transfers between devices with their start and end apart: 49 -> 49, of which waited for: 20 -> 21; matrix products, arithmetic and copies ran while one was open for 5% -> 5% of each run, Pallas kernels for 32% -> 27%
where the time goes in v13:
time: 323 us; the launch traced here: 321 us
  Pallas kernels  122 us (38%)
  waiting for transfers between devices  80 us (25%)
  starting transfers between devices  58.3 us (18%)
  blocking collectives  29.6 us (9%)
  local copies, waits for them, and re-layouts  13 us (4%)
  other arithmetic  12.8 us (4%)
  matrix products  4.29 us (1%)
    ppermute x24, waiting for transfers between devices, send(): lax.ppermute(block, 'chip', ring_pairs(direction))  45.7 us
    all_to_all x1, blocking collectives, to_heads(): return lax.all_to_all(blocks, 'chip', 0, 0, tiled=True)  29.6 us
    ppermute x24, starting transfers between devices, send(): lax.ppermute(block, 'chip', ring_pairs(direction))  26.3 us
    pallas_call x5, Pallas kernels, place(): pl.pallas_call(functools.partial(place_kernel, len(pairs), (units, size,...  24.2 us
    pallas_call x2, Pallas kernels, backward_piece(): pl.pallas_call(functools.partial(backward_kernel, crops, len(before)), gr...  24 us
    pallas_call x5, Pallas kernels, add(): pl.pallas_call(functools.partial(add_kernel, starts, len(shapes)), grid_s...  18.6 us
    all_to_all x4, starting transfers between devices, to_heads(): return lax.all_to_all(blocks, 'chip', 0, 0, tiled=True)  18.6 us
    all_to_all x1, waiting for transfers between devices, local(): ends = lax.all_to_all(ends, everyone, 0, 0, tiled=True)  15.7 us
  transfers between devices with their start and end apart: 49, of which 21 were waited for; matrix products, arithmetic and copies ran while one was open for 5% of the time, Pallas kernels for 27%

profile of v13, /device:TPU:0, one launch (start us, length us, event | category | flops | bytes accessed | tf_op | source)
XLA Modules:
  0.0 321.0 jit_solution(10283875034744091460)
XLA Ops:
  1.2 6.6 %project.1 = (bf16[8,208,256]{2,1,0:T(8,128)(2,1)}, bf16[256,1024]{1,0:T(8,128)(2,1)}, bf16[256,512]{1,0:T(8,128)(2,1)}) custom-call(s32[18]{0:T(128)} %compare_select_fusion.5.table.core_ref._, bf16[256,1024]{1,0:T(8,128)(2,1)} %input_ref.3, s32[1,256]{1,0:T(1,128)} %bitcast.67, s32[32]{0:T(128)} %steps_ref.1, f32[1,1024]{1,0:T(1,128)} %bitcast.50, ...), custom_call_target="tpu_custom_call" | custom-call | flops 1 | bytes 1 | tf_op jit(solution)/shard_map/project/pallas_call | solution.py:94
  7.8 29.6 %all_to_all.30.query_ref.own.refs_1_ = bf16[8,208,256]{2,1,0:T(8,128)(2,1)S(1)} all-to-all(bf16[8,208,256]{2,1,0:T(8,128)(2,1)} %get-tuple-element.179), channel_id=1, replica_groups=mesh['chip'=8,'core'=2,'head'=2] {'chip'}, dimensions={0} | all-to-all | bytes 1703936 | tf_op jit(solution)/shard_map/all_to_all | solution.py:435
  37.5 2.4 collective-permute-done.2.other.refs_0_
  40.7 15.3 %attention_forward.1 = (f32[8,64,256]{2,1,0:T(8,128)}, bf16[8,64,256]{2,1,0:T(8,128)(2,1)}, f32[8,1,256]{2,1,0:T(1,128)}) custom-call(bf16[8,208,256]{2,1,0:T(8,128)(2,1)} %copy-done, bf16[8,208,256]{2,1,0:T(8,128)(2,1)} %copy-done, bf16[8,208,256]{2,1,0:T(8,128)(2,1)} %copy-done.2), custom_call_target="tpu_custom_call" | custom-call | flops 1 | bytes 1 | tf_op jit(solution)/shard_map/attention_forward/pallas_call | solution.py:367
  56.0 3.4 %all-to-all-start.1 = ((bf16[8,64,256]{2,1,0:T(8,128)(2,1)}), bf16[8,64,256]{2,1,0:T(8,128)(2,1)S(1)}, u32[]{:S(2)}, u32[]{:S(2)}) async-start(bf16[8,64,256]{2,1,0:T(8,128)(2,1)} %get-tuple-element.183), calls=%async_computation.1 | async-start | bytes 524288 | tf_op jit(solution)/shard_map/all_to_all | solution.py:435
  59.5 1.9 collective-permute-start.1
  61.5 10.6 %collective-permute-done.1.refs_2_ = bf16[256,512]{1,0:T(8,128)(2,1)S(1)} collective-permute-done((bf16[256,512]{1,0:T(8,128)(2,1)S(1)}, bf16[256,512]{1,0:T(8,128)(2,1)S(1)}, u32[]{:S(2)}, u32[]{:S(2)}) %collective-permute-start.1) | collective-permute-done | bytes 262176 | tf_op jit(solution)/shard_map/ppermute | solution.py:549
  72.6 1.5 collective-permute-start.7
  74.2 2.9 collective-permute-start.3
  77.1 4.8 %collective-permute-done.3.refs_3_ = bf16[256,512]{1,0:T(8,128)(2,1)S(1)} collective-permute-done((bf16[256,512]{1,0:T(8,128)(2,1)S(1)}, bf16[256,512]{1,0:T(8,128)(2,1)S(1)}, u32[]{:S(2)}, u32[]{:S(2)}) %collective-permute-start.3) | collective-permute-done | bytes 262176 | tf_op jit(solution)/shard_map/ppermute | solution.py:549
  81.8 2.2 collective-permute-done.4.refs_4_
  84.8 1.3 collective-permute-start.6
  86.9 11.7 %mlp.1 = (bf16[256,2048]{1,0:T(8,128)(2,1)}, bf16[256,2048]{1,0:T(8,128)(2,1)}, bf16[256,1024]{1,0:T(8,128)(2,1)}, bf16[256,1024]{1,0:T(8,128)(2,1)}, f32[256,10...) custom-call(s32[18]{0:T(128)} %compare_select_fusion.5.table.core_ref._, ...), custom_call_target="tpu_custom_call" | custom-call | flops 1 | bytes 1 | tf_op jit(solution)/shard_map/mlp/pallas_call | solution.py:174
  99.2 1.3 collective-permute-start.14
  100.4 1.8 collective-permute-done.8.refs_1_
  104.1 3.1 ring_add.5
  107.2 2.7 collective-permute-start.10
  109.9 1.7 halves.2
  111.6 2.0 collective-permute-start.12
  114.4 4.3 %middle.1 = (f32[256,1024]{1,0:T(8,128)}, bf16[256,1024]{1,0:T(8,128)(2,1)}, bf16[512,256]{1,0:T(8,128)(2,1)}, f32[4,1024]{1,0:T(4,128)}) custom-call(f32[256,1024]{1,0:T(8,128)} %get-tuple-element.204.hidden_ref, bf16[256,1024]{1,0:T(8,128)(2,1)} %grad_ref.3, bf16[256,1024]{1,0:T(8,128)(2,1)} %get-tuple-element.207.refs_0_, bf16[256,1024]{1,0:T(8,128)(2,1)} %copy-done.34, ...), custom_call_target="tpu_custom_call" | custom-call | flops 1 | bytes 1 | tf_op jit(solution)/shard_map/middle/pallas_call | solution.py:235
  118.9 2.1 collective-permute-done.13
  121.9 3.8 %ring_add.6 = (bf16[256,1024]{1,0:T(8,128)(2,1)}, bf16[256,1024]{1,0:T(8,128)(2,1)}) custom-call(s32[18]{0:T(128)} %compare_select_fusion.5.table.core_ref._, bf16[256,1024]{1,0:T(8,128)(2,1)} %get-tuple-element.194.refs_0_, bf16[256,1024]{1,0:T(8,128)(2,1)} %copy-done.9, bf16[256,2048]{1,0:T(8,128)(2,1)} %get-tuple-element.196.refs_2_.refs_5_, ...), custom_call_target="tpu_custom_call" | custom-call | flops 1 | bytes 1 | tf_op jit(solution)/shard_map/ring_add/pallas_call | solution.py:650
  126.3 4.3 %all-to-all-start.2 = ((bf16[8,64,256]{2,1,0:T(8,128)(2,1)}), bf16[8,64,256]{2,1,0:T(8,128)(2,1)S(1)}, u32[]{:S(2)}, u32[]{:S(2)}) async-start(bf16[8,64,256]{2,1,0:T(8,128)(2,1)} %bitcast.9), calls=%async_computation.2 | async-start | bytes 524288 | tf_op jit(solution)/shard_map/all_to_all | solution.py:435
  130.6 2.0 collective-permute-start.15
  133.0 3.0 join.1.refs_0_
  135.9 1.5 collective-permute-start.24
  138.5 2.4 all-to-all-done.2.grad_ref
  140.9 6.3 %collective-permute-done.15.refs_4_ = bf16[256,1024]{1,0:T(8,128)(2,1)S(1)} collective-permute-done((bf16[256,1024]{1,0:T(8,128)(2,1)}, bf16[256,1024]{1,0:T(8,128)(2,1)S(1)}, u32[]{:S(2)}, u32[]{:S(2)}) %collective-permute-start.15) | collective-permute-done | bytes 524320 | tf_op jit(solution)/shard_map/ppermute | solution.py:604
  147.2 1.9 collective-permute-done.16.refs_7_
  149.9 4.0 %ring_add.7 = (bf16[256,1024]{1,0:T(8,128)(2,1)}, bf16[256,1024]{1,0:T(8,128)(2,1)}) custom-call(s32[18]{0:T(128)} %compare_select_fusion.5.table.core_ref._, bf16[256,1024]{1,0:T(8,128)(2,1)} %get-tuple-element.194.refs_0_, bf16[256,1024]{1,0:T(8,128)(2,1)} %copy-done.9, bf16[256,2048]{1,0:T(8,128)(2,1)} %get-tuple-element.196.refs_2_.refs_5_, ...), custom_call_target="tpu_custom_call" | custom-call | flops 1 | bytes 1 | tf_op jit(solution)/shard_map/ring_add/pallas_call | solution.py:650
  153.9 2.3 collective-permute-start.19
  156.3 4.4 %all-to-all-start.3 = ((bf16[8,32,1024]{2,1,0:T(8,128)(2,1)}), bf16[8,32,1024]{2,1,0:T(8,128)(2,1)}, u32[]{:S(2)}, u32[]{:S(2)}) async-start(bf16[8,32,1024]{2,1,0:T(8,128)(2,1)} %bitcast.10), calls=%async_computation.3 | async-start | bytes 1048576 | tf_op jit(solution)/shard_map/all_to_all | solution.py:435
  160.7 11.9 %attention_backward.2 = (f32[8,64,256]{2,1,0:T(8,128)S(1)}, bf16[8,128,256]{2,1,0:T(8,128)(2,1)S(1)}) custom-call(bf16[8,208,256]{2,1,0:T(8,128)(2,1)S(1)} %copy-done.1, bf16[8,64,256]{2,1,0:T(8,128)(2,1)S(1)} %all-to-all-done.2.grad_ref, f32[8,64,256]{2,1,0:T(8,128)S(1)} %copy-done.4, f32[8,1,256]{2,1,0:T(1,128)S(1)} %copy-done.6, ...), custom_call_target="tpu_custom_call" | custom-call | flops 1 | bytes 1 | tf_op jit(solution)/shard_map/attention_backward/pallas_call | solution.py:397
  172.7 4.0 %ring_add.8 = (bf16[256,1024]{1,0:T(8,128)(2,1)}, bf16[256,1024]{1,0:T(8,128)(2,1)}) custom-call(s32[18]{0:T(128)} %compare_select_fusion.5.table.core_ref._, bf16[256,1024]{1,0:T(8,128)(2,1)} %get-tuple-element.194.refs_0_, bf16[256,1024]{1,0:T(8,128)(2,1)} %copy-done.9, bf16[256,2048]{1,0:T(8,128)(2,1)} %get-tuple-element.196.refs_2_.refs_5_, ...), custom_call_target="tpu_custom_call" | custom-call | flops 1 | bytes 1 | tf_op jit(solution)/shard_map/ring_add/pallas_call | solution.py:650
  176.7 2.0 collective-permute-start.21
  178.9 12.1 %attention_backward.3 = (bf16[8,64,256]{2,1,0:T(8,128)(2,1)S(1)}, f32[8,128,256]{2,1,0:T(8,128)S(1)}) custom-call(bf16[8,208,256]{2,1,0:T(8,128)(2,1)S(1)} %copy-done.1, bf16[8,64,256]{2,1,0:T(8,128)(2,1)S(1)} %all-to-all-done.2.grad_ref, f32[8,64,256]{2,1,0:T(8,128)S(1)} %copy-done.4, f32[8,1,256]{2,1,0:T(1,128)S(1)} %copy-done.6, ...), custom_call_target="tpu_custom_call" | custom-call | flops 1 | bytes 1 | tf_op jit(solution)/shard_map/attention_backward/pallas_call | solution.py:397
  194.3 6.5 %all-to-all-start.4 = ((bf16[8,192,256]{2,1,0:T(8,128)(2,1)}), bf16[8,192,256]{2,1,0:T(8,128)(2,1)}, u32[]{:S(2)}, u32[]{:S(2)}) async-start(bf16[8,192,256]{2,1,0:T(8,128)(2,1)} %pad_maximum_fusion.2), calls=%async_computation.4 | async-start | bytes 1572864 | tf_op jit(solution)/shard_map/all_to_all | solution.py:435
  200.9 1.5 collective-permute-start.26
  202.4 5.0 %head_gradient.1 = bf16[192,1024]{1,0:T(8,128)(2,1)} custom-call(s32[18]{0:T(128)} %compare_select_fusion.5.table.core_ref._, bf16[8,64,256]{2,1,0:T(8,128)(2,1)} %copy-done.5, bf16[8,128,256]{2,1,0:T(8,128)(2,1)} %copy-done.10, bf16[2048,512]{1,0:T(8,128)(2,1)} %join.1.refs_0_, bf16[2048,512]{1,0:T(8,128)(2,1)} %collective-permute-done.24.refs_1_), custom_call_target="tpu_custom_call" | custom-call | flops 1 | bytes 1 | tf_op jit(solution)/shard_map/head_gradient/pallas_call | solution.py:765
  208.5 3.7 %ring_add.9 = bf16[256,1024]{1,0:T(8,128)(2,1)} custom-call(s32[18]{0:T(128)} %compare_select_fusion.5.table.core_ref._, bf16[256,1024]{1,0:T(8,128)(2,1)} %get-tuple-element.194.refs_0_, bf16[256,1024]{1,0:T(8,128)(2,1)} %copy-done.9, bf16[256,2048]{1,0:T(8,128)(2,1)} %get-tuple-element.196.refs_2_.refs_5_, bf16[256,2048]{1,0:T(8,128)(2,1)} %copy-done.7, ...), custom_call_target="tpu_custom_call" | custom-call | flops 1 | bytes 1 | tf_op jit(solution)/shard_map/ring_add/pallas_call | solution.py:650
  213.5 1.6 collective-permute-done.26
  215.3 1.8 collective-permute-start.28
  217.3 5.1 %all-to-all-done.4 = bf16[8,192,256]{2,1,0:T(8,128)(2,1)} async-done(((bf16[8,192,256]{2,1,0:T(8,128)(2,1)}), bf16[8,192,256]{2,1,0:T(8,128)(2,1)}, u32[]{:S(2)}, u32[]{:S(2)}) %all-to-all-start.4) | async-done | bytes 786464 | tf_op jit(solution)/shard_map/all_to_all | solution.py:435
  225.4 1.5 fusion.24
  226.8 3.9 %place.5 = (f32[2048,1024]{1,0:T(8,128)}, f32[1024,2048]{1,0:T(8,128)}, bf16[8,2,96,1024]{3,2,1,0:T(8,128)(2,1)}, f32[2,8,32,1024]{3,2,1,0:T(8,128)}, f32[8,2,16,1024]{3,2,1,0:T(8,128)}) custom-call(s32[18]{0:T(128)} %compare_select_fusion.5.table.core_ref._, bf16[400,1024]{1,0:T(8,128)(2,1)} %copy-done.17, bf16[400,1024]{1,0:T(8,128)(2,1)} %collective-permute-done.29.refs_1_), custom_call_target="tpu_custom_call" | custom-call | flops 1 | bytes 1 | tf_op jit(solution)/shard_map/place/pallas_call | solution.py:690
  230.7 8.5 %collective-permute-done.28.refs_6_ = bf16[400,1024]{1,0:T(8,128)(2,1)} collective-permute-done((bf16[400,1024]{1,0:T(8,128)(2,1)S(1)}, bf16[400,1024]{1,0:T(8,128)(2,1)}, u32[]{:S(2)}, u32[]{:S(2)}) %collective-permute-start.28) | collective-permute-done | bytes 819232 | tf_op jit(solution)/shard_map/ppermute | solution.py:549
  240.1 1.4 collective-permute-start.31
  241.5 1.5 collective-permute-start.34
  243.3 2.1 add_convert_fusion
  246.2 5.4 %place.6 = (f32[2048,1024]{1,0:T(8,128)}, f32[1024,2048]{1,0:T(8,128)}, bf16[8,2,96,1024]{3,2,1,0:T(8,128)(2,1)}, f32[2,8,32,1024]{3,2,1,0:T(8,128)}, f32[8,2,16,1024]{3,2,1,0:T(8,128)}) custom-call(s32[18]{0:T(128)} %compare_select_fusion.5.table.core_ref._, ...), custom_call_target="tpu_custom_call", output_to_operand_aliasing={{0}: (1, {}), {1}: (2, {}), {2}: (3, {}), {3}: (4, {}), {4}... | custom-call | flops 1 | bytes 1 | tf_op jit(solution)/shard_map/place/pallas_call | solution.py:690
  251.7 3.6 %collective-permute-done.34 = bf16[256,1024]{1,0:T(8,128)(2,1)S(1)} collective-permute-done((bf16[256,1024]{1,0:T(8,128)(2,1)S(1)}, bf16[256,1024]{1,0:T(8,128)(2,1)S(1)}, u32[]{:S(2)}, u32[]{:S(2)}) %collective-permute-start.34) | collective-permute-done | bytes 524320 | tf_op jit(solution)/shard_map/ppermute | solution.py:462
  255.3 4.9 %collective-permute-done.30.refs_5_ = bf16[400,1024]{1,0:T(8,128)(2,1)} collective-permute-done((bf16[400,1024]{1,0:T(8,128)(2,1)}, bf16[400,1024]{1,0:T(8,128)(2,1)}, u32[]{:S(2)}, u32[]{:S(2)}) %collective-permute-start.30) | collective-permute-done | bytes 819232 | tf_op jit(solution)/shard_map/ppermute | solution.py:549
  264.6 3.8 %all-to-all-start.5 = ((bf16[32,32,128]{2,1,0:T(8,128)(2,1)}), bf16[32,32,128]{2,1,0:T(8,128)(2,1)}, u32[]{:S(2)}, u32[]{:S(2)}) async-start(bf16[32,32,128]{2,1,0:T(8,128)(2,1)} %broadcast_in_dim.55), calls=%async_computation.5 | async-start | bytes 524288 | tf_op jit(solution)/shard_map/all_to_all | solution.py:959
  268.4 5.5 %place.7 = (f32[2048,1024]{1,0:T(8,128)}, f32[1024,2048]{1,0:T(8,128)}, bf16[8,2,96,1024]{3,2,1,0:T(8,128)(2,1)}, f32[2,8,32,1024]{3,2,1,0:T(8,128)}, f32[8,2,16,1024]{3,2,1,0:T(8,128)}) custom-call(s32[18]{0:T(128)} %compare_select_fusion.5.table.core_ref._, ...), custom_call_target="tpu_custom_call", output_to_operand_aliasing={{0}: (1, {}), {1}: (2, {}), {2}: (3, {}), {3}: (4, {}), {4}... | custom-call | flops 1 | bytes 1 | tf_op jit(solution)/shard_map/place/pallas_call | solution.py:690
  273.8 15.7 %all-to-all-done.5 = bf16[32,32,128]{2,1,0:T(8,128)(2,1)} async-done(((bf16[32,32,128]{2,1,0:T(8,128)(2,1)}), bf16[32,32,128]{2,1,0:T(8,128)(2,1)}, u32[]{:S(2)}, u32[]{:S(2)}) %all-to-all-start.5) | async-done | bytes 262176 | tf_op jit(solution)/shard_map/all_to_all | solution.py:959
  290.4 2.1 halves.3
  293.3 1.3 collective-permute-start.40
  294.5 1.3 fusion.11
  296.9 5.5 %place.8 = (f32[2048,1024]{1,0:T(8,128)}, f32[1024,2048]{1,0:T(8,128)}, bf16[8,2,96,1024]{3,2,1,0:T(8,128)(2,1)}, f32[2,8,32,1024]{3,2,1,0:T(8,128)}, f32[8,2,16,1024]{3,2,1,0:T(8,128)}) custom-call(s32[18]{0:T(128)} %compare_select_fusion.5.table.core_ref._, ...), custom_call_target="tpu_custom_call", output_to_operand_aliasing={{0}: (1, {}), {1}: (2, {}), {2}: (3, {}), {3}: (4, {}), {4}... | custom-call | flops 1 | bytes 1 | tf_op jit(solution)/shard_map/place/pallas_call | solution.py:690
  302.3 1.9 collective-permute-done.39
  306.8 1.6 collective-permute-done.43.refs_6_
  309.3 3.9 %place.9 = (f32[2048,1024]{1,0:T(8,128)}, f32[1024,2048]{1,0:T(8,128)}, bf16[8,2,96,1024]{3,2,1,0:T(8,128)(2,1)}, f32[2,8,32,1024]{3,2,1,0:T(8,128)}, f32[8,2,16,1024]{3,2,1,0:T(8,128)}) custom-call(s32[18]{0:T(128)} %compare_select_fusion.5.table.core_ref._, ...), custom_call_target="tpu_custom_call", output_to_operand_aliasing={{0}: (1, {}), {1}: (2, {}), {2}: (3, {}), {3}: (4, {}), {4}... | custom-call | flops 1 | bytes 1 | tf_op jit(solution)/shard_map/place/pallas_call | solution.py:690
  313.2 1.3 reduce_sum.109
  315.8 5.2 %final_layout.1 = (f32[1024,512]{1,0:T(8,128)}, f32[1024,512]{1,0:T(8,128)}, f32[1024,512]{1,0:T(8,128)}) custom-call(bf16[8,2,96,1024]{3,2,1,0:T(8,128)(2,1)} %get-tuple-element.334.held), custom_call_target="tpu_custom_call" | custom-call | flops 1 | bytes 1 | tf_op jit(solution)/shard_map/final_layout/pallas_call | solution.py:792
  (201 shorter events, 33.7 us)
Async XLA Ops:
  7.8 51.6 %copy-start.35 = (bf16[256,512]{1,0:T(8,128)(2,1)S(1)}, bf16[256,512]{1,0:T(8,128)(2,1)}, u32[]{:S(2)}) copy-start(bf16[256,512]{1,0:T(8,128)(2,1)} %get-tuple-element.181.refs_0_) | copy-start | bytes 786436
  7.8 64.3 %copy-start.12 = (bf16[512,1024]{1,0:T(8,128)(2,1)S(1)}, bf16[512,1024]{1,0:T(8,128)(2,1)}, u32[]{:S(2)}) copy-start(bf16[512,1024]{1,0:T(8,128)(2,1)} %refs_3_.1) | copy-start | bytes 3145732
  37.5 2.4 collective-permute-start.2
  56.0 16.1 %all-to-all-start.1 = ((bf16[8,64,256]{2,1,0:T(8,128)(2,1)}), bf16[8,64,256]{2,1,0:T(8,128)(2,1)S(1)}, u32[]{:S(2)}, u32[]{:S(2)}) async-start(bf16[8,64,256]{2,1,0:T(8,128)(2,1)} %get-tuple-element.183), calls=%async_computation.1 | async-start | bytes 524288 | tf_op jit(solution)/shard_map/all_to_all | solution.py:435
  59.5 12.7 %collective-permute-start.1 = (bf16[256,512]{1,0:T(8,128)(2,1)S(1)}, bf16[256,512]{1,0:T(8,128)(2,1)S(1)}, u32[]{:S(2)}, u32[]{:S(2)}) collective-permute-start(bf16[256,512]{1,0:T(8,128)(2,1)S(1)} %copy-done.35), channel_id=1, source_target_pairs={{0,4},{8,0},{16,8},{24,16},{28,24},{20,28},{12,20},{4,12},{1,5},{9... | collective-permute-start | bytes 786440 | tf_op jit(solution)/shard_map/ppermute | solution.py:549
  61.4 10.8 %collective-permute-start = (bf16[256,512]{1,0:T(8,128)(2,1)S(1)}, bf16[256,512]{1,0:T(8,128)(2,1)S(1)}, u32[]{:S(2)}, u32[]{:S(2)}) collective-permute-start(bf16[256,512]{1,0:T(8,128)(2,1)S(1)} %copy-done.35), channel_id=1, source_target_pairs={{0,8},{8,16},{16,24},{24,28},{28,20},{20,12},{12,4},{4,0},{1,9},{9... | collective-permute-start | bytes 786440 | tf_op jit(solution)/shard_map/ppermute | solution.py:549
  72.1 26.4 %copy-start.37 = (bf16[256,512]{1,0:T(8,128)(2,1)}, bf16[256,512]{1,0:T(8,128)(2,1)S(1)}, u32[]{:S(2)}) copy-start(bf16[256,512]{1,0:T(8,128)(2,1)S(1)} %collective-permute-done.refs_1_) | copy-start | bytes 786436
  72.6 13.4 %copy-start.20 = (bf16[256,1024]{1,0:T(8,128)(2,1)}, bf16[256,1024]{1,0:T(8,128)(2,1)S(1)}, u32[]{:S(2)}) copy-start(bf16[256,1024]{1,0:T(8,128)(2,1)S(1)} %convolution_convert_fusion.refs_0_) | copy-start | bytes 1572868
  72.6 13.4 %collective-permute-start.7 = (bf16[256,1024]{1,0:T(8,128)(2,1)S(1)}, bf16[256,1024]{1,0:T(8,128)(2,1)S(1)}, u32[]{:S(2)}, u32[]{:S(2)}) collective-permute-start(bf16[256,1024]{1,0:T(8,128)(2,1)S(1)} %convolution_convert_fusion.refs_0_), channel_id=1, source_target_pairs={{0,1},{1,0},{2,3},{3,2},{4,5},{5,4},{6,7},{7,6},{8,9},{9,8},{10,11... | collective-permute-start | bytes 1572872 | tf_op jit(solution)/shard_map/ppermute | solution.py:462
  74.2 7.6 %collective-permute-start.3 = (bf16[256,512]{1,0:T(8,128)(2,1)S(1)}, bf16[256,512]{1,0:T(8,128)(2,1)S(1)}, u32[]{:S(2)}, u32[]{:S(2)}) collective-permute-start(bf16[256,512]{1,0:T(8,128)(2,1)S(1)} %collective-permute-done.refs_1_), channel_id=1, source_target_pairs={{0,8},{8,16},{16,24},{24,28},{28,20},{20,12},{12,4},{4,0},{1,9},{9... | collective-permute-start | bytes 786440 | tf_op jit(solution)/shard_map/ppermute | solution.py:549
  77.1 7.0 %collective-permute-start.4 = (bf16[256,512]{1,0:T(8,128)(2,1)S(1)}, bf16[256,512]{1,0:T(8,128)(2,1)S(1)}, u32[]{:S(2)}, u32[]{:S(2)}) collective-permute-start(bf16[256,512]{1,0:T(8,128)(2,1)S(1)} %collective-permute-done.1.refs_2_), channel_id=1, source_target_pairs={{0,4},{8,0},{16,8},{24,16},{28,24},{20,28},{12,20},{4,12},{1,5},{9... | collective-permute-start | bytes 786440 | tf_op jit(solution)/shard_map/ppermute | solution.py:549
  81.8 25.3 %copy-start.38 = (bf16[256,512]{1,0:T(8,128)(2,1)}, bf16[256,512]{1,0:T(8,128)(2,1)S(1)}, u32[]{:S(2)}) copy-start(bf16[256,512]{1,0:T(8,128)(2,1)S(1)} %collective-permute-done.3.refs_3_) | copy-start | bytes 786436
  84.0 23.1 %copy-start.39 = (bf16[256,512]{1,0:T(8,128)(2,1)}, bf16[256,512]{1,0:T(8,128)(2,1)S(1)}, u32[]{:S(2)}) copy-start(bf16[256,512]{1,0:T(8,128)(2,1)S(1)} %collective-permute-done.4.refs_4_) | copy-start | bytes 786436
  84.0 14.5 %collective-permute-start.5 = (bf16[256,512]{1,0:T(8,128)(2,1)S(1)}, bf16[256,512]{1,0:T(8,128)(2,1)S(1)}, u32[]{:S(2)}, u32[]{:S(2)}) collective-permute-start(bf16[256,512]{1,0:T(8,128)(2,1)S(1)} %collective-permute-done.3.refs_3_), channel_id=1, source_target_pairs={{0,8},{8,16},{16,24},{24,28},{28,20},{20,12},{12,4},{4,0},{1,9},{9... | collective-permute-start | bytes 786440 | tf_op jit(solution)/shard_map/ppermute | solution.py:549
  84.8 13.8 %collective-permute-start.6 = (bf16[256,512]{1,0:T(8,128)(2,1)S(1)}, bf16[256,512]{1,0:T(8,128)(2,1)S(1)}, u32[]{:S(2)}, u32[]{:S(2)}) collective-permute-start(bf16[256,512]{1,0:T(8,128)(2,1)S(1)} %collective-permute-done.4.refs_4_), channel_id=1, source_target_pairs={{0,4},{8,0},{16,8},{24,16},{28,24},{20,28},{12,20},{4,12},{1,5},{9... | collective-permute-start | bytes 786440 | tf_op jit(solution)/shard_map/ppermute | solution.py:549
  98.6 11.3 %copy-start.24 = (bf16[256,512]{1,0:T(8,128)(2,1)}, bf16[256,512]{1,0:T(8,128)(2,1)S(1)}, u32[]{:S(2)}) copy-start(bf16[256,512]{1,0:T(8,128)(2,1)S(1)} %collective-permute-done.5.left.refs_5_) | copy-start | bytes 786436
  98.6 11.3 %copy-start.25 = (bf16[256,512]{1,0:T(8,128)(2,1)}, bf16[256,512]{1,0:T(8,128)(2,1)S(1)}, u32[]{:S(2)}) copy-start(bf16[256,512]{1,0:T(8,128)(2,1)S(1)} %collective-permute-done.6.right.refs_6_) | copy-start | bytes 786436
  98.6 3.7 %collective-permute-start.9 = (bf16[256,2048]{1,0:T(8,128)(2,1)}, bf16[256,2048]{1,0:T(8,128)(2,1)S(1)}, u32[]{:S(2)}, u32[]{:S(2)}) collective-permute-start(bf16[256,2048]{1,0:T(8,128)(2,1)} %get-tuple-element.197), channel_id=1, source_target_pairs={{0,2},{2,0},{1,3},{3,1},{4,6},{6,4},{5,7},{7,5},{8,10},{10,8},{9,1... | collective-permute-start | bytes 3145736 | tf_op jit(solution)/shard_map/ppermute | solution.py:431
  98.7 3.6 %collective-permute-start.8 = (bf16[256,1024]{1,0:T(8,128)(2,1)}, bf16[256,1024]{1,0:T(8,128)(2,1)S(1)}, u32[]{:S(2)}, u32[]{:S(2)}) collective-permute-start(bf16[256,1024]{1,0:T(8,128)(2,1)} %get-tuple-element.195), channel_id=1, source_target_pairs={{0,2},{2,0},{1,3},{3,1},{4,6},{6,4},{5,7},{7,5},{8,10},{10,8},{9,1... | collective-permute-start | bytes 1572872 | tf_op jit(solution)/shard_map/ppermute | solution.py:431
  99.2 14.4 %collective-permute-start.14 = (bf16[256,1024]{1,0:T(8,128)(2,1)}, bf16[256,1024]{1,0:T(8,128)(2,1)S(1)}, u32[]{:S(2)}, u32[]{:S(2)}) collective-permute-start(bf16[256,1024]{1,0:T(8,128)(2,1)} %get-tuple-element.207.refs_0_), channel_id=1, source_target_pairs={{0,1},{1,0},{2,3},{3,2},{4,5},{5,4},{6,7},{7,6},{8,9},{9,8},{10,11... | collective-permute-start | bytes 1572872 | tf_op jit(solution)/shard_map/ppermute | solution.py:462
  107.2 13.8 %collective-permute-start.10 = (bf16[256,512]{1,0:T(8,128)(2,1)}, bf16[256,512]{1,0:T(8,128)(2,1)S(1)}, u32[]{:S(2)}, u32[]{:S(2)}) collective-permute-start(bf16[256,512]{1,0:T(8,128)(2,1)} %get-tuple-element.198), channel_id=1, source_target_pairs={{0,8},{8,16},{16,24},{24,28},{28,20},{20,12},{12,4},{4,0},{1,9},{9... | collective-permute-start | bytes 786440 | tf_op jit(solution)/shard_map/ppermute | solution.py:604
  109.9 11.1 %collective-permute-start.11 = (bf16[256,512]{1,0:T(8,128)(2,1)}, bf16[256,512]{1,0:T(8,128)(2,1)S(1)}, u32[]{:S(2)}, u32[]{:S(2)}) collective-permute-start(bf16[256,512]{1,0:T(8,128)(2,1)} %get-tuple-element.199), channel_id=1, source_target_pairs={{0,4},{8,0},{16,8},{24,16},{28,24},{20,28},{12,20},{4,12},{1,5},{9... | collective-permute-start | bytes 786440 | tf_op jit(solution)/shard_map/ppermute | solution.py:604
  111.6 7.3 %collective-permute-start.12 = (bf16[256,256]{1,0:T(8,128)(2,1)}, bf16[256,256]{1,0:T(8,128)(2,1)S(1)}, u32[]{:S(2)}, u32[]{:S(2)}) collective-permute-start(bf16[256,256]{1,0:T(8,128)(2,1)} %get-tuple-element.202), channel_id=1, source_target_pairs={{0,8},{8,16},{16,24},{24,28},{28,20},{20,12},{12,4},{4,0},{1,9},{9... | collective-permute-start | bytes 393224 | tf_op jit(solution)/shard_map/ppermute | solution.py:549
  113.6 7.4 %collective-permute-start.13 = (bf16[256,256]{1,0:T(8,128)(2,1)}, bf16[256,256]{1,0:T(8,128)(2,1)S(1)}, u32[]{:S(2)}, u32[]{:S(2)}) collective-permute-start(bf16[256,256]{1,0:T(8,128)(2,1)} %get-tuple-element.203), channel_id=1, source_target_pairs={{0,4},{8,0},{16,8},{24,16},{28,24},{20,28},{12,20},{4,12},{1,5},{9... | collective-permute-start | bytes 393224 | tf_op jit(solution)/shard_map/ppermute | solution.py:549
  125.7 11.7 %collective-permute-start.18 = (bf16[256,1024]{1,0:T(8,128)(2,1)S(1)}, bf16[256,1024]{1,0:T(8,128)(2,1)S(1)}, u32[]{:S(2)}, u32[]{:S(2)}) collective-permute-start(bf16[256,1024]{1,0:T(8,128)(2,1)S(1)} %copy-done.33), channel_id=1, source_target_pairs={{0,2},{2,0},{1,3},{3,1},{4,6},{6,4},{5,7},{7,5},{8,10},{10,8},{9,1... | collective-permute-start | bytes 1572872 | tf_op jit(solution)/shard_map/ppermute | solution.py:431
  125.7 11.6 %collective-permute-start.17 = (bf16[256,256]{1,0:T(8,128)(2,1)S(1)}, bf16[256,256]{1,0:T(8,128)(2,1)S(1)}, u32[]{:S(2)}, u32[]{:S(2)}) collective-permute-start(bf16[256,256]{1,0:T(8,128)(2,1)S(1)} %constant_dynamic-slice_fusion.1), channel_id=1, source_target_pairs={{0,2},{2,0},{1,3},{3,1},{4,6},{6,4},{5,7},{7,5},{8,10},{10,8},{9,1... | collective-permute-start | bytes 393224 | tf_op jit(solution)/shard_map/ppermute | solution.py:431
  126.3 14.6 %all-to-all-start.2 = ((bf16[8,64,256]{2,1,0:T(8,128)(2,1)}), bf16[8,64,256]{2,1,0:T(8,128)(2,1)S(1)}, u32[]{:S(2)}, u32[]{:S(2)}) async-start(bf16[8,64,256]{2,1,0:T(8,128)(2,1)} %bitcast.9), calls=%async_computation.2 | async-start | bytes 524288 | tf_op jit(solution)/shard_map/all_to_all | solution.py:435
  130.6 16.6 %collective-permute-start.15 = (bf16[256,1024]{1,0:T(8,128)(2,1)}, bf16[256,1024]{1,0:T(8,128)(2,1)S(1)}, u32[]{:S(2)}, u32[]{:S(2)}) collective-permute-start(bf16[256,1024]{1,0:T(8,128)(2,1)} %get-tuple-element.219), channel_id=1, source_target_pairs={{0,8},{8,16},{16,24},{24,28},{28,20},{20,12},{12,4},{4,0},{1,9},{9... | collective-permute-start | bytes 1572872 | tf_op jit(solution)/shard_map/ppermute | solution.py:604
  132.6 16.5 %collective-permute-start.16 = (bf16[256,1024]{1,0:T(8,128)(2,1)}, bf16[256,1024]{1,0:T(8,128)(2,1)S(1)}, u32[]{:S(2)}, u32[]{:S(2)}) collective-permute-start(bf16[256,1024]{1,0:T(8,128)(2,1)} %get-tuple-element.220), channel_id=1, source_target_pairs={{0,4},{8,0},{16,8},{24,16},{28,24},{20,28},{12,20},{4,12},{1,5},{9... | collective-permute-start | bytes 1572872 | tf_op jit(solution)/shard_map/ppermute | solution.py:604
  135.9 66.5 %collective-permute-start.24 = (bf16[2048,512]{1,0:T(8,128)(2,1)}, bf16[2048,512]{1,0:T(8,128)(2,1)}, u32[]{:S(2)}, u32[]{:S(2)}) collective-permute-start(bf16[2048,512]{1,0:T(8,128)(2,1)} %join.1.refs_0_), channel_id=1, source_target_pairs={{0,1},{1,0},{2,3},{3,2},{4,5},{5,4},{6,7},{7,6},{8,9},{9,8},{10,11... | collective-permute-start | bytes 6291464 | tf_op jit(solution)/shard_map/ppermute | solution.py:462
  149.9 10.7 %copy-start.6 = (f32[8,1,256]{2,1,0:T(1,128)S(1)}, f32[8,1,256]{2,1,0:T(1,128)}, u32[]{:S(2)}) copy-start(f32[8,1,256]{2,1,0:T(1,128)} %get-tuple-element.233.logsum_ref) | copy-start | bytes 24580
  153.9 18.7 %collective-permute-start.19 = (bf16[256,1024]{1,0:T(8,128)(2,1)}, bf16[256,1024]{1,0:T(8,128)(2,1)}, u32[]{:S(2)}, u32[]{:S(2)}) collective-permute-start(bf16[256,1024]{1,0:T(8,128)(2,1)} %get-tuple-element.229), channel_id=1, source_target_pairs={{0,8},{8,16},{16,24},{24,28},{28,20},{20,12},{12,4},{4,0},{1,9},{9... | collective-permute-start | bytes 1572872 | tf_op jit(solution)/shard_map/ppermute | solution.py:604
  156.3 16.4 %collective-permute-start.20 = (bf16[256,1024]{1,0:T(8,128)(2,1)}, bf16[256,1024]{1,0:T(8,128)(2,1)}, u32[]{:S(2)}, u32[]{:S(2)}) collective-permute-start(bf16[256,1024]{1,0:T(8,128)(2,1)} %get-tuple-element.230), channel_id=1, source_target_pairs={{0,4},{8,0},{16,8},{24,16},{28,24},{20,28},{12,20},{4,12},{1,5},{9... | collective-permute-start | bytes 1572872 | tf_op jit(solution)/shard_map/ppermute | solution.py:604
  156.3 37.1 %all-to-all-start.3 = ((bf16[8,32,1024]{2,1,0:T(8,128)(2,1)}), bf16[8,32,1024]{2,1,0:T(8,128)(2,1)}, u32[]{:S(2)}, u32[]{:S(2)}) async-start(bf16[8,32,1024]{2,1,0:T(8,128)(2,1)} %bitcast.10), calls=%async_computation.3 | async-start | bytes 1048576 | tf_op jit(solution)/shard_map/all_to_all | solution.py:435
  176.7 14.4 %collective-permute-start.21 = (bf16[256,1024]{1,0:T(8,128)(2,1)}, bf16[256,1024]{1,0:T(8,128)(2,1)}, u32[]{:S(2)}, u32[]{:S(2)}) collective-permute-start(bf16[256,1024]{1,0:T(8,128)(2,1)} %get-tuple-element.243), channel_id=1, source_target_pairs={{0,8},{8,16},{16,24},{24,28},{28,20},{20,12},{12,4},{4,0},{1,9},{9... | collective-permute-start | bytes 1572872 | tf_op jit(solution)/shard_map/ppermute | solution.py:604
  178.7 13.5 %collective-permute-start.22 = (bf16[256,1024]{1,0:T(8,128)(2,1)}, bf16[256,1024]{1,0:T(8,128)(2,1)}, u32[]{:S(2)}, u32[]{:S(2)}) collective-permute-start(bf16[256,1024]{1,0:T(8,128)(2,1)} %get-tuple-element.244), channel_id=1, source_target_pairs={{0,4},{8,0},{16,8},{24,16},{28,24},{20,28},{12,20},{4,12},{1,5},{9... | collective-permute-start | bytes 1572872 | tf_op jit(solution)/shard_map/ppermute | solution.py:604
  178.7 13.5 %collective-permute-start.23 = (bf16[8,128,256]{2,1,0:T(8,128)(2,1)S(1)}, bf16[8,128,256]{2,1,0:T(8,128)(2,1)}, u32[]{:S(2)}, u32[]{:S(2)}) collective-permute-start(bf16[8,128,256]{2,1,0:T(8,128)(2,1)S(1)} %get-tuple-element.254), channel_id=1, source_target_pairs={{0,2},{2,0},{1,3},{3,1},{4,6},{6,4},{5,7},{7,5},{8,10},{10,8},{9,1... | collective-permute-start | bytes 1572872 | tf_op jit(solution)/shard_map/ppermute | solution.py:431
  194.3 28.2 %all-to-all-start.4 = ((bf16[8,192,256]{2,1,0:T(8,128)(2,1)}), bf16[8,192,256]{2,1,0:T(8,128)(2,1)}, u32[]{:S(2)}, u32[]{:S(2)}) async-start(bf16[8,192,256]{2,1,0:T(8,128)(2,1)} %pad_maximum_fusion.2), calls=%async_computation.4 | async-start | bytes 1572864 | tf_op jit(solution)/shard_map/all_to_all | solution.py:435
  200.9 14.2 %collective-permute-start.26 = (bf16[256,1024]{1,0:T(8,128)(2,1)S(1)}, bf16[256,1024]{1,0:T(8,128)(2,1)}, u32[]{:S(2)}, u32[]{:S(2)}) collective-permute-start(bf16[256,1024]{1,0:T(8,128)(2,1)S(1)} %copy-done.28), channel_id=1, source_target_pairs={{0,1},{1,0},{2,3},{3,2},{4,5},{5,4},{6,7},{7,6},{8,9},{9,8},{10,11... | collective-permute-start | bytes 1572872 | tf_op jit(solution)/shard_map/ppermute | solution.py:462
  208.4 5.0 %collective-permute-start.25 = (bf16[96,1024]{1,0:T(8,128)(2,1)S(1)}, bf16[96,1024]{1,0:T(8,128)(2,1)S(1)}, u32[]{:S(2)}, u32[]{:S(2)}) collective-permute-start(bf16[96,1024]{1,0:T(8,128)(2,1)S(1)} %constant_dynamic-slice_fusion), channel_id=1, source_target_pairs={{0,2},{2,0},{1,3},{3,1},{4,6},{6,4},{5,7},{7,5},{8,10},{10,8},{9,1... | collective-permute-start | bytes 589832 | tf_op jit(solution)/shard_map/ppermute | solution.py:431
  215.2 11.7 %collective-permute-start.29 = (bf16[400,1024]{1,0:T(8,128)(2,1)S(1)}, bf16[400,1024]{1,0:T(8,128)(2,1)}, u32[]{:S(2)}, u32[]{:S(2)}) collective-permute-start(bf16[400,1024]{1,0:T(8,128)(2,1)S(1)} %pad_maximum_fusion.refs_0_), channel_id=1, source_target_pairs={{0,2},{2,0},{1,3},{3,1},{4,6},{6,4},{5,7},{7,5},{8,10},{10,8},{9,1... | collective-permute-start | bytes 2457608 | tf_op jit(solution)/shard_map/ppermute | solution.py:431
  215.3 23.9 %collective-permute-start.28 = (bf16[400,1024]{1,0:T(8,128)(2,1)S(1)}, bf16[400,1024]{1,0:T(8,128)(2,1)}, u32[]{:S(2)}, u32[]{:S(2)}) collective-permute-start(bf16[400,1024]{1,0:T(8,128)(2,1)S(1)} %pad_maximum_fusion.refs_0_), channel_id=1, source_target_pairs={{0,4},{8,0},{16,8},{24,16},{28,24},{20,28},{12,20},{4,12},{1,5},{9... | collective-permute-start | bytes 2457608 | tf_op jit(solution)/shard_map/ppermute | solution.py:549
  217.1 22.2 %collective-permute-start.27 = (bf16[400,1024]{1,0:T(8,128)(2,1)S(1)}, bf16[400,1024]{1,0:T(8,128)(2,1)}, u32[]{:S(2)}, u32[]{:S(2)}) collective-permute-start(bf16[400,1024]{1,0:T(8,128)(2,1)S(1)} %pad_maximum_fusion.refs_0_), channel_id=1, source_target_pairs={{0,8},{8,16},{16,24},{24,28},{28,20},{20,12},{12,4},{4,0},{1,9},{9... | collective-permute-start | bytes 2457608 | tf_op jit(solution)/shard_map/ppermute | solution.py:549
  225.4 17.9 %copy-start.11 = (f32[256,1024]{1,0:T(8,128)S(1)}, f32[256,1024]{1,0:T(8,128)}, u32[]{:S(2)}) copy-start(f32[256,1024]{1,0:T(8,128)} %get-tuple-element.204.hidden_ref) | copy-start | bytes 3145732
  225.4 17.9 %copy-start.29 = (bf16[256,1024]{1,0:T(8,128)(2,1)S(1)}, bf16[256,1024]{1,0:T(8,128)(2,1)}, u32[]{:S(2)}) copy-start(bf16[256,1024]{1,0:T(8,128)(2,1)} %get-tuple-element.281) | copy-start | bytes 1572868
  225.4 17.9 %copy-start.45 = (f32[1024]{0:T(1024)S(1)}, f32[1024]{0:T(1024)}, u32[]{:S(2)}) copy-start(f32[1024]{0:T(1024)} %param.35) | copy-start | bytes 12292
  239.2 6.1 %collective-permute-start.32 = (bf16[400,1024]{1,0:T(8,128)(2,1)}, bf16[400,1024]{1,0:T(8,128)(2,1)S(1)}, u32[]{:S(2)}, u32[]{:S(2)}) collective-permute-start(bf16[400,1024]{1,0:T(8,128)(2,1)} %collective-permute-done.27.refs_5_), channel_id=1, source_target_pairs={{0,2},{2,0},{1,3},{3,1},{4,6},{6,4},{5,7},{7,5},{8,10},{10,8},{9,1... | collective-permute-start | bytes 2457608 | tf_op jit(solution)/shard_map/ppermute | solution.py:431
  239.2 21.0 %collective-permute-start.30 = (bf16[400,1024]{1,0:T(8,128)(2,1)}, bf16[400,1024]{1,0:T(8,128)(2,1)}, u32[]{:S(2)}, u32[]{:S(2)}) collective-permute-start(bf16[400,1024]{1,0:T(8,128)(2,1)} %collective-permute-done.27.refs_5_), channel_id=1, source_target_pairs={{0,8},{8,16},{16,24},{24,28},{28,20},{20,12},{12,4},{4,0},{1,9},{9... | collective-permute-start | bytes 2457608 | tf_op jit(solution)/shard_map/ppermute | solution.py:549
  239.9 5.5 %collective-permute-start.33 = (bf16[400,1024]{1,0:T(8,128)(2,1)}, bf16[400,1024]{1,0:T(8,128)(2,1)}, u32[]{:S(2)}, u32[]{:S(2)}) collective-permute-start(bf16[400,1024]{1,0:T(8,128)(2,1)} %collective-permute-done.28.refs_6_), channel_id=1, source_target_pairs={{0,2},{2,0},{1,3},{3,1},{4,6},{6,4},{5,7},{7,5},{8,10},{10,8},{9,1... | collective-permute-start | bytes 2457608 | tf_op jit(solution)/shard_map/ppermute | solution.py:431
  240.1 20.7 %collective-permute-start.31 = (bf16[400,1024]{1,0:T(8,128)(2,1)}, bf16[400,1024]{1,0:T(8,128)(2,1)}, u32[]{:S(2)}, u32[]{:S(2)}) collective-permute-start(bf16[400,1024]{1,0:T(8,128)(2,1)} %collective-permute-done.28.refs_6_), channel_id=1, source_target_pairs={{0,4},{8,0},{16,8},{24,16},{28,24},{20,28},{12,20},{4,12},{1,5},{9... | collective-permute-start | bytes 2457608 | tf_op jit(solution)/shard_map/ppermute | solution.py:549
  241.5 13.8 %collective-permute-start.34 = (bf16[256,1024]{1,0:T(8,128)(2,1)S(1)}, bf16[256,1024]{1,0:T(8,128)(2,1)S(1)}, u32[]{:S(2)}, u32[]{:S(2)}) collective-permute-start(bf16[256,1024]{1,0:T(8,128)(2,1)S(1)} %get-tuple-element.320), channel_id=1, source_target_pairs={{0,1},{1,0},{2,3},{3,2},{4,5},{5,4},{6,7},{7,6},{8,9},{9,8},{10,11... | collective-permute-start | bytes 1572872 | tf_op jit(solution)/shard_map/ppermute | solution.py:462
  245.3 17.8 %copy-start.15 = (f32[256,1024]{1,0:T(8,128)S(1)}, f32[256,1024]{1,0:T(8,128)}, u32[]{:S(2)}) copy-start(f32[256,1024]{1,0:T(8,128)} %get-tuple-element.361) | copy-start | bytes 3145732
  245.3 17.8 %copy-start.42 = (f32[1024]{0:T(1024)S(1)}, f32[1024]{0:T(1024)}, u32[]{:S(2)}) copy-start(f32[1024]{0:T(1024)} %param.22) | copy-start | bytes 12292
  260.9 7.5 %collective-permute-start.37 = (bf16[400,1024]{1,0:T(8,128)(2,1)}, bf16[400,1024]{1,0:T(8,128)(2,1)}, u32[]{:S(2)}, u32[]{:S(2)}) collective-permute-start(bf16[400,1024]{1,0:T(8,128)(2,1)} %collective-permute-done.30.refs_5_), channel_id=1, source_target_pairs={{0,2},{2,0},{1,3},{3,1},{4,6},{6,4},{5,7},{7,5},{8,10},{10,8},{9,1... | collective-permute-start | bytes 2457608 | tf_op jit(solution)/shard_map/ppermute | solution.py:431
  260.9 28.7 %collective-permute-start.35 = (bf16[400,1024]{1,0:T(8,128)(2,1)}, bf16[400,1024]{1,0:T(8,128)(2,1)S(1)}, u32[]{:S(2)}, u32[]{:S(2)}) collective-permute-start(bf16[400,1024]{1,0:T(8,128)(2,1)} %collective-permute-done.30.refs_5_), channel_id=1, source_target_pairs={{0,8},{8,16},{16,24},{24,28},{28,20},{20,12},{12,4},{4,0},{1,9},{9... | collective-permute-start | bytes 2457608 | tf_op jit(solution)/shard_map/ppermute | solution.py:549
  261.7 6.7 %collective-permute-start.38 = (bf16[400,1024]{1,0:T(8,128)(2,1)}, bf16[400,1024]{1,0:T(8,128)(2,1)}, u32[]{:S(2)}, u32[]{:S(2)}) collective-permute-start(bf16[400,1024]{1,0:T(8,128)(2,1)} %collective-permute-done.31.refs_6_), channel_id=1, source_target_pairs={{0,2},{2,0},{1,3},{3,1},{4,6},{6,4},{5,7},{7,5},{8,10},{10,8},{9,1... | collective-permute-start | bytes 2457608 | tf_op jit(solution)/shard_map/ppermute | solution.py:431
  261.9 27.6 %collective-permute-start.36 = (bf16[400,1024]{1,0:T(8,128)(2,1)}, bf16[400,1024]{1,0:T(8,128)(2,1)}, u32[]{:S(2)}, u32[]{:S(2)}) collective-permute-start(bf16[400,1024]{1,0:T(8,128)(2,1)} %collective-permute-done.31.refs_6_), channel_id=1, source_target_pairs={{0,4},{8,0},{16,8},{24,16},{28,24},{20,28},{12,20},{4,12},{1,5},{9... | collective-permute-start | bytes 2457608 | tf_op jit(solution)/shard_map/ppermute | solution.py:549
  264.6 24.9 %all-to-all-start.5 = ((bf16[32,32,128]{2,1,0:T(8,128)(2,1)}), bf16[32,32,128]{2,1,0:T(8,128)(2,1)}, u32[]{:S(2)}, u32[]{:S(2)}) async-start(bf16[32,32,128]{2,1,0:T(8,128)(2,1)} %broadcast_in_dim.55), calls=%async_computation.5 | async-start | bytes 524288 | tf_op jit(solution)/shard_map/all_to_all | solution.py:959
  273.8 20.7 %copy-start.23 = (f32[256,1024]{1,0:T(8,128)S(1)}, f32[256,1024]{1,0:T(8,128)}, u32[]{:S(2)}) copy-start(f32[256,1024]{1,0:T(8,128)} %get-tuple-element.319) | copy-start | bytes 3145732
  289.5 7.3 %collective-permute-start.41 = (bf16[400,1024]{1,0:T(8,128)(2,1)S(1)}, bf16[400,1024]{1,0:T(8,128)(2,1)}, u32[]{:S(2)}, u32[]{:S(2)}) collective-permute-start(bf16[400,1024]{1,0:T(8,128)(2,1)S(1)} %collective-permute-done.35.left.refs_5_), channel_id=1, source_target_pairs={{0,2},{2,0},{1,3},{3,1},{4,6},{6,4},{5,7},{7,5},{8,10},{10,8},{9,1... | collective-permute-start | bytes 2457608 | tf_op jit(solution)/shard_map/ppermute | solution.py:431
  289.6 7.2 %collective-permute-start.42 = (bf16[400,1024]{1,0:T(8,128)(2,1)}, bf16[400,1024]{1,0:T(8,128)(2,1)}, u32[]{:S(2)}, u32[]{:S(2)}) collective-permute-start(bf16[400,1024]{1,0:T(8,128)(2,1)} %collective-permute-done.36.right.refs_6_), channel_id=1, source_target_pairs={{0,2},{2,0},{1,3},{3,1},{4,6},{6,4},{5,7},{7,5},{8,10},{10,8},{9,1... | collective-permute-start | bytes 2457608 | tf_op jit(solution)/shard_map/ppermute | solution.py:431
  292.5 11.7 %collective-permute-start.39 = (bf16[400,512]{1,0:T(8,128)(2,1)}, bf16[400,512]{1,0:T(8,128)(2,1)}, u32[]{:S(2)}, u32[]{:S(2)}) collective-permute-start(bf16[400,512]{1,0:T(8,128)(2,1)} %get-tuple-element.306), channel_id=1, source_target_pairs={{0,8},{8,16},{16,24},{24,28},{28,20},{20,12},{12,4},{4,0},{1,9},{9... | collective-permute-start | bytes 1228808 | tf_op jit(solution)/shard_map/ppermute | solution.py:549
  293.3 11.6 %collective-permute-start.40 = (bf16[400,512]{1,0:T(8,128)(2,1)}, bf16[400,512]{1,0:T(8,128)(2,1)}, u32[]{:S(2)}, u32[]{:S(2)}) collective-permute-start(bf16[400,512]{1,0:T(8,128)(2,1)} %get-tuple-element.307), channel_id=1, source_target_pairs={{0,4},{8,0},{16,8},{24,16},{28,24},{20,28},{12,20},{4,12},{1,5},{9... | collective-permute-start | bytes 1228808 | tf_op jit(solution)/shard_map/ppermute | solution.py:549
  306.0 2.4 collective-permute-start.43
  (33 other events, 152.8 us)

commit v14 on v12

--- a/solution.py
+++ b/solution.py
@@ -687,29 +687,35 @@
         def chip(at, table):
             return table[chips + first + at * stride]
 
+        column = pl.BlockSpec(
+            (model, 2 * HD), lambda at, table: (0, lax.div(chip(at, table), 2))
+        )
+        columns = [column] * (3 if outputs else 0)
+        heads = [[first, first + stride][at] + chips for at in range(len(pairs))]
         return pl.pallas_call(
-            functools.partial(place_kernel, len(pairs), (units, size, extra)),
+            functools.partial(place_kernel, heads, (units, size, extra)),
             grid_spec=pltpu.PrefetchScalarGridSpec(
                 num_scalar_prefetch=1,
                 grid=(len(pairs),),
-                in_specs=[pl.BlockSpec(memory_space=pl.ANY)] * len(outputs)
+                in_specs=[pl.BlockSpec(memory_space=pl.ANY)] * (len(outputs) - len(columns))
+                + columns
                 + [block] * (2 * len(pairs)),
                 out_specs=[
                     pl.BlockSpec((units, model), lambda at, table: (place(at, table), 0)),
                     pl.BlockSpec((model, units), lambda at, table: (0, place(at, table))),
-                    pl.BlockSpec((1, 2, size, model), lambda at, table: (chip(at, table), 0, 0, 0)),
                     pl.BlockSpec((2, 1, extra, model), lambda at, table: (0, chip(at, table), 0, 0)),
                     pl.BlockSpec(
                         (1, 2, small_rows, model), lambda at, table: (chip(at, table), 0, 0, 0)
                     ),
-                ],
+                ]
+                + [column] * 3,
             ),
             out_shape=shapes
             + [
-                struct((chips, 2, size, model), BF16),
                 struct((2, chips, extra, model), F32),
                 struct((chips, 2, small_rows, model), F32),
-            ],
+            ]
+            + [struct((model, chips * HD), F32)] * 3,
             input_output_aliases={1 + at: at for at in range(len(outputs))},
             compiler_params=streaming,
             cost_estimate=light,
@@ -717,26 +723,35 @@
         )(self.table, *outputs, *[pair[1] for pair in pairs], *[pair[2] for pair in pairs])
 
 
-def place_kernel(count, sizes, table, *refs):
-    blocks, (down, up, projections, weight, small) = refs[-5 - 2 * count : -5], refs[-5:]
+def place_kernel(heads, sizes, table, *refs):
+    count = len(heads)
+    refs, (down, up, weight, small), projections = refs[:-7], refs[-7:-3], refs[-3:]
+    blocks, refs = refs[-2 * count :], refs[: -2 * count]
     core = table[table.shape[0] - 2]
     units, size, extra = sizes
     rows = [pl.ds(0, units), pl.ds(units, size), pl.ds(units + size, extra)]
     rows.append(pl.ds(units + size + extra, small_rows))
 
-    def put(first, second):
+    def put(first, second, head):
         down[...] = first[rows[0], :].astype(F32)
         up[...] = second[rows[0], :].astype(F32).T
         for side, block in ((0, first), (1, second)):
-            projections[0, side] = block[rows[1], :]
             weight[side, 0] = block[rows[2], :].astype(F32)
             small[0, side] = block[rows[3], :].astype(F32)
+        both = jnp.concatenate([first[rows[1], :], second[rows[1], :]], axis=0)
+        for at, output in enumerate(projections):
+            part = both[at * HD : at * HD + HD].astype(F32)
+            part = jnp.concatenate([part, part], axis=0).T
+            if refs:
+                mine = lax.broadcasted_iota(jnp.int32, part.shape, 1) // HD == head % 2
+                part = jnp.where(mine, part, refs[at - 3][...])
+            output[...] = part
 
     for at in range(count):
-        near, far = blocks[at], blocks[count + at]
+        near, far, head = blocks[at], blocks[count + at], table[heads[at]]
         here = pl.program_id(0) == at
-        pl.when(here & (core == 0))(functools.partial(put, near, far))
-        pl.when(here & (core != 0))(functools.partial(put, far, near))
+        pl.when(here & (core == 0))(functools.partial(put, near, far, head))
+        pl.when(here & (core != 0))(functools.partial(put, far, near, head))
 
 
 def head_gradient_kernel(steps, chips, table, query_ref, key_value_ref, *refs):
@@ -778,27 +793,6 @@
         cost_estimate=light,
         name="head_gradient",
     )(table, dquery, key_value, *parts)
-
-
-def layout_kernel(held, *outputs):
-    pair = [jnp.concatenate([held[head, 0], held[head, 1]], axis=0) for head in range(2)]
-    for index, output in enumerate(outputs):
-        rows = [part[index * HD : index * HD + HD] for part in pair]
-        output[...] = jnp.concatenate(rows, axis=0).astype(F32).T
-
-
-def final_layout(held):
-    count, _, size, model = held.shape
-    return pl.pallas_call(
-        layout_kernel,
-        grid=(count // 2,),
-        in_specs=[pl.BlockSpec((2, 2, size, model), lambda at: (at, 0, 0, 0))],
-        out_specs=[pl.BlockSpec((model, 2 * HD), lambda at: (0, at))] * 3,
-        out_shape=[struct((model, count * HD), F32)] * 3,
-        compiler_params=streaming,
-        cost_estimate=light,
-        name="final_layout",
-    )(held)
 
 
 def core_half(values, axis, side):
@@ -854,10 +848,11 @@
     inputs.send(inputs.ready)
     other = swap_cores(own)
     raw, out, logsum = attention_forward(queries, own, other, crops)
-    out = visit([inputs], out)
+    inputs.state, out = lax.optimization_barrier((inputs.state, out))
     attn_out = gather_queries(out, heads, split, rows)
     attn_out = visit([inputs], attn_out)
     branches = across_heads(product(attn_out, output_weight, 0, 0).astype(BF16))
+    visit([inputs], ())
     keep, give, keep_in, give_in, hidden, dup_bias, mlp_part, d_mlp_part = mlp(
         table,
         block_input,
@@ -888,17 +883,17 @@
         parts = across_heads(parts[0])
     out_near, out_far = share_halves(attn_out, 0)
     doutput = product(out_near, d_branch) + product(out_far, swap_cores(d_branch))
-    doutput = to_heads(doutput.astype(BF16).reshape(chips, -1, model))
-    grads = visit([ring], grads)
+    doutput = doutput.astype(BF16).reshape(chips, -1, model)
+    doutput = to_heads(doutput)
     *dquery, far_sums = backward_piece(
         queries, grads, raw, logsum, [], other, [], 0, 1, crops, (F32, BF16)
     )
-    grads, dquery, far_sums = visit([ring], (grads, dquery, far_sums))
+    grads, dquery, far_sums, doutput = visit([ring], (grads, dquery, far_sums, doutput))
     far_sums = swap_cores(far_sums)
     *dquery, near_sums = backward_piece(
         queries, grads, raw, logsum, dquery, own, [], 0, 1, crops, (BF16, F32)
     )
-    near_sums, dquery = ring.arrive((near_sums, dquery))
+    near_sums, dquery = visit([ring], (near_sums, dquery))
     (dquery,) = dquery
     key_value = (near_sums + far_sums.astype(F32)).astype(BF16)
     doutput, key_value = lax.optimization_barrier((doutput, key_value))
@@ -926,6 +921,7 @@
             lax.psum(product(attn_in, grad, 0, 1).astype(BF16), ("chip", "core")).astype(F32)
             for grad in (dquery, dkey, dvalue)
         ]
+    blocks = ring.arrive(blocks)
     total = ring.finish()
     start = total.shape[0]
     ring.size, ring.extra = size, blocks.shape[0] - size - small_rows
@@ -936,7 +932,6 @@
         + product(dkey, key_weight, 0, 1)
         + product(dvalue, value_weight, 0, 1)
     )
-    d_part = visit([gathered], d_part)
     d_in = across_heads(d_part.astype(BF16))
     unit_attn, inverse_attn = normalize(block_input.astype(F32))
     onehot = (segments[:, None] == jnp.arange(crops, dtype=jnp.int32)[None, :]).astype(F32)
@@ -952,23 +947,23 @@
     everyone = ("chip", "core", "head")
     ends = jnp.broadcast_to(ends, (lax.axis_size(everyone),) + ends.shape)
     ends = lax.all_to_all(ends, everyone, 0, 0, tiled=True)
-    visit([gathered], ())
-    d_in, mlp_out = visit([gathered], (d_in, mlp_out))
+    _, mlp_out = visit([gathered], (d_part, mlp_out))
     block_output = hidden + down_bias
     for part in mlp_out:
         block_output += part.astype(F32)
     block_output = block_output.astype(BF16)
+    d_in, block_output = visit([gathered], (d_in, block_output))
+    visit([gathered], ())
     d_in = functools.reduce(jnp.add, (part.astype(F32) for part in d_in))
     input_grad = (d_hidden + normalize_back(d_in * gain_attn, unit_attn, inverse_attn)).astype(
         BF16
     )
     while gathered.busy():
-        visit([gathered], ())
+        input_grad = visit([gathered], input_grad)
     ddown_weight, dup_weight, *rest = gathered.outputs
     ends = jnp.sum(ends.astype(F32), axis=0).reshape(-1)[: 3 * model].reshape(3, model)
     if split == 1:
-        held, doutput_weight, small = rest
-        projections = final_layout(held)
+        doutput_weight, small, *projections = rest
         doutput_weight = doutput_weight.reshape(width, model)
     if split != 1:
         blocks = jnp.zeros((2, chips) + blocks.shape, F32)

time: 322 us -> 331 us (1.028)
  blocking collectives: 29.6 us -> 42.4 us
  waiting for transfers between devices: 81.3 us -> 71.6 us
    ppermute x24, waiting for transfers between devices: 35 us -> 60 us  [send(): lax.ppermute(block, 'chip', ring_pairs(direction))]
    ppermute x5, waiting for transfers between devices: 26.5 us -> 4.65 us  [across_heads(): return [part, lax.ppermute(part, 'head', [(0, 1), (1, 0)])]]
    all_to_all x4 -> x3, waiting for transfers between devices: 15.8 us -> 0.97 us  [to_heads(): return lax.all_to_all(blocks, 'chip', 0, 0, tiled=True)]
    all_to_all x1 -> x2, blocking collectives: 29.6 us -> 42.4 us  [to_heads(): return lax.all_to_all(blocks, 'chip', 0, 0, tiled=True)]
    ppermute x24, starting transfers between devices: 25.4 us -> 30.3 us  [send(): lax.ppermute(block, 'chip', ring_pairs(direction))]
    all_to_all x4 -> x3, starting transfers between devices: 17.9 us -> 14.3 us  [to_heads(): return lax.all_to_all(blocks, 'chip', 0, 0, tiled=True)]
    unnamed x91 -> x101, local copies, waits for them, and re-layouts: 9.41 us -> 9.99 us
    pallas_call x6 -> x5, Pallas kernels: 29.6 us -> 30.1 us  [place(): pl.pallas_call(functools.partial(place_kernel, heads, (units, size, extra...]
  transfers between devices with their start and end apart: 49 -> 48, of which waited for: 20 -> 27; matrix products, arithmetic and copies ran while one was open for 5% -> 6% of each run, Pallas kernels for 32% -> 33%
where the time goes in v14:
time: 331 us; the launch traced here: 330 us
  Pallas kernels  123 us (37%)
  waiting for transfers between devices  71.6 us (22%)
  starting transfers between devices  58.2 us (18%)
  blocking collectives  42.4 us (13%)
  local copies, waits for them, and re-layouts  15 us (5%)
  other arithmetic  13.1 us (4%)
  matrix products  5.47 us (2%)
    ppermute x24, waiting for transfers between devices, send(): lax.ppermute(block, 'chip', ring_pairs(direction))  60 us
    all_to_all x2, blocking collectives, to_heads(): return lax.all_to_all(blocks, 'chip', 0, 0, tiled=True)  42.4 us
    ppermute x24, starting transfers between devices, send(): lax.ppermute(block, 'chip', ring_pairs(direction))  30.3 us
    pallas_call x5, Pallas kernels, place(): pl.pallas_call(functools.partial(place_kernel, heads, (units, size, extra...  30.1 us
    pallas_call x2, Pallas kernels, backward_piece(): pl.pallas_call(functools.partial(backward_kernel, crops, len(before)), gr...  24.8 us
    pallas_call x5, Pallas kernels, add(): pl.pallas_call(functools.partial(add_kernel, starts, len(shapes)), grid_s...  18.3 us
    pallas_call x1, Pallas kernels, attention_forward(): pl.pallas_call(functools.partial(forward_kernel, crops, key_step(count)),...  15.3 us
    all_to_all x3, starting transfers between devices, to_heads(): return lax.all_to_all(blocks, 'chip', 0, 0, tiled=True)  14.3 us
  transfers between devices with their start and end apart: 48, of which 27 were waited for; matrix products, arithmetic and copies ran while one was open for 6% of the time, Pallas kernels for 33%

profile of v14, /device:TPU:0, one launch (start us, length us, event | category | flops | bytes accessed | tf_op | source)
XLA Modules:
  0.0 329.9 jit_solution(3116947149998947387)
XLA Ops:
  1.2 6.6 %project.1 = (bf16[8,208,256]{2,1,0:T(8,128)(2,1)}, bf16[256,1024]{1,0:T(8,128)(2,1)}, bf16[256,512]{1,0:T(8,128)(2,1)}) custom-call(s32[18]{0:T(128)} %compare_select_fusion.5.table.core_ref._, bf16[256,1024]{1,0:T(8,128)(2,1)} %input_ref.3, s32[1,256]{1,0:T(1,128)} %bitcast.68, s32[32]{0:T(128)} %steps_ref.1, f32[1,1024]{1,0:T(1,128)} %bitcast.54, ...), custom_call_target="tpu_custom_call" | custom-call | flops 1 | bytes 1 | tf_op jit(solution)/shard_map/project/pallas_call | solution.py:94
  7.8 29.6 %all_to_all.30.query_ref.own.refs_1_ = bf16[8,208,256]{2,1,0:T(8,128)(2,1)S(1)} all-to-all(bf16[8,208,256]{2,1,0:T(8,128)(2,1)} %get-tuple-element.195), channel_id=1, replica_groups=mesh['chip'=8,'core'=2,'head'=2] {'chip'}, dimensions={0} | all-to-all | bytes 1703936 | tf_op jit(solution)/shard_map/all_to_all | solution.py:435
  38.2 1.3 collective-permute-start.1
  40.7 15.3 %attention_forward.1 = (f32[8,64,256]{2,1,0:T(8,128)}, bf16[8,64,256]{2,1,0:T(8,128)(2,1)}, f32[8,1,256]{2,1,0:T(1,128)}) custom-call(bf16[8,208,256]{2,1,0:T(8,128)(2,1)} %copy-done, bf16[8,208,256]{2,1,0:T(8,128)(2,1)} %copy-done, bf16[8,208,256]{2,1,0:T(8,128)(2,1)} %copy-done.2), custom_call_target="tpu_custom_call" | custom-call | flops 1 | bytes 1 | tf_op jit(solution)/shard_map/attention_forward/pallas_call | solution.py:367
  56.1 12.8 %all_to_all.31 = bf16[8,64,256]{2,1,0:T(8,128)(2,1)S(1)} all-to-all(bf16[8,64,256]{2,1,0:T(8,128)(2,1)} %get-tuple-element.202), channel_id=1, replica_groups=mesh['chip'=8,'core'=2,'head'=2] {'chip'}, dimensions={0} | all-to-all | bytes 524288 | tf_op jit(solution)/shard_map/all_to_all | solution.py:435
  69.4 1.6 collective-permute-start.7
  72.9 4.6 %collective-permute-done.3.refs_3_ = bf16[256,512]{1,0:T(8,128)(2,1)S(1)} collective-permute-done((bf16[256,512]{1,0:T(8,128)(2,1)S(1)}, bf16[256,512]{1,0:T(8,128)(2,1)S(1)}, u32[]{:S(2)}, u32[]{:S(2)}) %collective-permute-start.3) | collective-permute-done | bytes 262176 | tf_op jit(solution)/shard_map/ppermute | solution.py:549
  78.4 1.4 collective-permute-start.5
  80.4 1.5 collective-permute-done.7.refs_1_
  82.7 11.7 %mlp.1 = (bf16[256,2048]{1,0:T(8,128)(2,1)}, bf16[256,2048]{1,0:T(8,128)(2,1)}, bf16[256,1024]{1,0:T(8,128)(2,1)}, bf16[256,1024]{1,0:T(8,128)(2,1)}, f32[256,10...) custom-call(s32[18]{0:T(128)} %compare_select_fusion.5.table.core_ref._, ...), custom_call_target="tpu_custom_call" | custom-call | flops 1 | bytes 1 | tf_op jit(solution)/shard_map/mlp/pallas_call | solution.py:174
  95.1 1.6 collective-permute-start.14
  96.6 1.5 collective-permute-done.8.refs_1_
  99.9 3.1 ring_add.5
  103.4 1.7 collective-permute-start.11
  105.1 1.7 halves.2
  107.3 1.5 collective-permute-start.13
  110.0 4.3 %middle.1 = (f32[256,1024]{1,0:T(8,128)}, bf16[256,1024]{1,0:T(8,128)(2,1)}, bf16[512,256]{1,0:T(8,128)(2,1)}, f32[4,1024]{1,0:T(4,128)}) custom-call(f32[256,1024]{1,0:T(8,128)} %get-tuple-element.223.hidden_ref, bf16[256,1024]{1,0:T(8,128)(2,1)} %grad_ref.3, bf16[256,1024]{1,0:T(8,128)(2,1)} %get-tuple-element.226.refs_0_, bf16[256,1024]{1,0:T(8,128)(2,1)} %copy-done.35, ...), custom_call_target="tpu_custom_call" | custom-call | flops 1 | bytes 1 | tf_op jit(solution)/shard_map/middle/pallas_call | solution.py:235
  115.8 3.8 %ring_add.6 = (bf16[256,1024]{1,0:T(8,128)(2,1)}, bf16[256,1024]{1,0:T(8,128)(2,1)}) custom-call(s32[18]{0:T(128)} %compare_select_fusion.5.table.core_ref._, bf16[256,1024]{1,0:T(8,128)(2,1)} %get-tuple-element.213.refs_0_, bf16[256,1024]{1,0:T(8,128)(2,1)} %copy-done.11, bf16[256,2048]{1,0:T(8,128)(2,1)} %get-tuple-element.215.refs_2_.refs_5_, ...), custom_call_target="tpu_custom_call" | custom-call | flops 1 | bytes 1 | tf_op jit(solution)/shard_map/ring_add/pallas_call | solution.py:650
  120.8 4.6 %all-to-all-start.2 = ((bf16[8,64,256]{2,1,0:T(8,128)(2,1)}), bf16[8,64,256]{2,1,0:T(8,128)(2,1)S(1)}, u32[]{:S(2)}, u32[]{:S(2)}) async-start(bf16[8,64,256]{2,1,0:T(8,128)(2,1)} %bitcast.9), calls=%async_computation.2 | async-start | bytes 524288 | tf_op jit(solution)/shard_map/all_to_all | solution.py:435
  125.4 1.3 fusion.14
  126.7 3.0 join.1.refs_0_
  129.7 1.6 collective-permute-start.24
  131.3 2.2 fusion
  134.5 5.0 %all-to-all-start.3 = ((bf16[8,32,1024]{2,1,0:T(8,128)(2,1)}), bf16[8,32,1024]{2,1,0:T(8,128)(2,1)S(1)}, u32[]{:S(2)}, u32[]{:S(2)}) async-start(bf16[8,32,1024]{2,1,0:T(8,128)(2,1)} %bitcast.50), calls=%async_computation.3 | async-start | bytes 1048576 | tf_op jit(solution)/shard_map/all_to_all | solution.py:435
  139.5 2.0 collective-permute-start.15
  141.6 12.7 %attention_backward.2 = (f32[8,64,256]{2,1,0:T(8,128)S(1)}, bf16[8,128,256]{2,1,0:T(8,128)(2,1)}) custom-call(bf16[8,208,256]{2,1,0:T(8,128)(2,1)S(1)} %copy-done.1, bf16[8,64,256]{2,1,0:T(8,128)(2,1)S(1)} %all-to-all-done.2.grad_ref, f32[8,64,256]{2,1,0:T(8,128)S(1)} %copy-done.4, f32[8,1,256]{2,1,0:T(1,128)S(1)} %copy-done.8, ...), custom_call_target="tpu_custom_call" | custom-call | flops 1 | bytes 1 | tf_op jit(solution)/shard_map/attention_backward/pallas_call | solution.py:397
  155.1 3.7 %collective-permute-done.15.refs_4_ = bf16[256,1024]{1,0:T(8,128)(2,1)S(1)} collective-permute-done((bf16[256,1024]{1,0:T(8,128)(2,1)}, bf16[256,1024]{1,0:T(8,128)(2,1)S(1)}, u32[]{:S(2)}, u32[]{:S(2)}) %collective-permute-start.15) | collective-permute-done | bytes 524320 | tf_op jit(solution)/shard_map/ppermute | solution.py:604
  158.8 2.2 collective-permute-done.16.refs_7_
  161.1 4.0 %ring_add.7 = (bf16[256,1024]{1,0:T(8,128)(2,1)}, bf16[256,1024]{1,0:T(8,128)(2,1)}) custom-call(s32[18]{0:T(128)} %compare_select_fusion.5.table.core_ref._, bf16[256,1024]{1,0:T(8,128)(2,1)} %get-tuple-element.213.refs_0_, bf16[256,1024]{1,0:T(8,128)(2,1)} %copy-done.11, bf16[256,2048]{1,0:T(8,128)(2,1)} %get-tuple-element.215.refs_2_.refs_5_, ...), custom_call_target="tpu_custom_call" | custom-call | flops 1 | bytes 1 | tf_op jit(solution)/shard_map/ring_add/pallas_call | solution.py:650
  165.1 4.3 %collective-permute-start.19 = (bf16[256,1024]{1,0:T(8,128)(2,1)}, bf16[256,1024]{1,0:T(8,128)(2,1)}, u32[]{:S(2)}, u32[]{:S(2)}) collective-permute-start(bf16[256,1024]{1,0:T(8,128)(2,1)} %get-tuple-element.254), channel_id=1, source_target_pairs={{0,8},{8,16},{16,24},{24,28},{28,20},{20,12},{12,4},{4,0},{1,9},{9... | collective-permute-start | bytes 1572872 | tf_op jit(solution)/shard_map/ppermute | solution.py:604
  169.4 12.1 %attention_backward.3 = (bf16[8,64,256]{2,1,0:T(8,128)(2,1)S(1)}, f32[8,128,256]{2,1,0:T(8,128)S(1)}) custom-call(bf16[8,208,256]{2,1,0:T(8,128)(2,1)S(1)} %copy-done.1, bf16[8,64,256]{2,1,0:T(8,128)(2,1)S(1)} %all-to-all-done.2.grad_ref, f32[8,64,256]{2,1,0:T(8,128)S(1)} %copy-done.4, f32[8,1,256]{2,1,0:T(1,128)S(1)} %copy-done.8, ...), custom_call_target="tpu_custom_call" | custom-call | flops 1 | bytes 1 | tf_op jit(solution)/shard_map/attention_backward/pallas_call | solution.py:397
  181.7 3.9 %ring_add.8 = (bf16[256,1024]{1,0:T(8,128)(2,1)}, bf16[256,1024]{1,0:T(8,128)(2,1)}) custom-call(s32[18]{0:T(128)} %compare_select_fusion.5.table.core_ref._, bf16[256,1024]{1,0:T(8,128)(2,1)} %get-tuple-element.213.refs_0_, bf16[256,1024]{1,0:T(8,128)(2,1)} %copy-done.11, bf16[256,2048]{1,0:T(8,128)(2,1)} %get-tuple-element.215.refs_2_.refs_5_, ...), custom_call_target="tpu_custom_call" | custom-call | flops 1 | bytes 1 | tf_op jit(solution)/shard_map/ring_add/pallas_call | solution.py:650
  185.6 1.2 add_convert_fusion.1.key_value_ref
  187.8 4.6 %all-to-all-start.4 = ((bf16[8,192,256]{2,1,0:T(8,128)(2,1)}), bf16[8,192,256]{2,1,0:T(8,128)(2,1)}, u32[]{:S(2)}, u32[]{:S(2)}) async-start(bf16[8,192,256]{2,1,0:T(8,128)(2,1)} %pad_maximum_fusion.2), calls=%async_computation.4 | async-start | bytes 1572864 | tf_op jit(solution)/shard_map/all_to_all | solution.py:435
  192.5 2.0 collective-permute-start.21
  194.6 5.0 %head_gradient.1 = bf16[192,1024]{1,0:T(8,128)(2,1)} custom-call(s32[18]{0:T(128)} %compare_select_fusion.5.table.core_ref._, bf16[8,64,256]{2,1,0:T(8,128)(2,1)} %copy-done.5, bf16[8,128,256]{2,1,0:T(8,128)(2,1)} %copy-done.12, bf16[2048,512]{1,0:T(8,128)(2,1)} %join.1.refs_0_, bf16[2048,512]{1,0:T(8,128)(2,1)} %collective-permute-done.24.refs_1_), custom_call_target="tpu_custom_call" | custom-call | flops 1 | bytes 1 | tf_op jit(solution)/shard_map/head_gradient/pallas_call | solution.py:780
  200.8 1.3 collective-permute-done.25
  203.1 14.9 %collective-permute-done.21.refs_4_ = bf16[256,1024]{1,0:T(8,128)(2,1)S(1)} collective-permute-done((bf16[256,1024]{1,0:T(8,128)(2,1)}, bf16[256,1024]{1,0:T(8,128)(2,1)S(1)}, u32[]{:S(2)}, u32[]{:S(2)}) %collective-permute-start.21) | collective-permute-done | bytes 524320 | tf_op jit(solution)/shard_map/ppermute | solution.py:604
  218.0 1.4 collective-permute-done.22.refs_5_
  220.2 3.5 %ring_add.9 = bf16[256,1024]{1,0:T(8,128)(2,1)} custom-call(s32[18]{0:T(128)} %compare_select_fusion.5.table.core_ref._, bf16[256,1024]{1,0:T(8,128)(2,1)} %get-tuple-element.213.refs_0_, bf16[256,1024]{1,0:T(8,128)(2,1)} %copy-done.11, bf16[256,2048]{1,0:T(8,128)(2,1)} %get-tuple-element.215.refs_2_.refs_5_, bf16[256,2048]{1,0:T(8,128)(2,1)} %copy-done.9, ...), custom_call_target="tpu_custom_call" | custom-call | flops 1 | bytes 1 | tf_op jit(solution)/shard_map/ring_add/pallas_call | solution.py:650
  225.8 5.7 %collective-permute-start.26 = (bf16[400,1024]{1,0:T(8,128)(2,1)S(1)}, bf16[400,1024]{1,0:T(8,128)(2,1)}, u32[]{:S(2)}, u32[]{:S(2)}) collective-permute-start(bf16[400,1024]{1,0:T(8,128)(2,1)S(1)} %pad_maximum_fusion.refs_0_), channel_id=1, source_target_pairs={{0,8},{8,16},{16,24},{24,28},{28,20},{20,12},{12,4},{4,0},{1,9},{9... | collective-permute-start | bytes 2457608 | tf_op jit(solution)/shard_map/ppermute | solution.py:549
  232.4 4.5 %place.5 = (f32[2048,1024]{1,0:T(8,128)}, f32[1024,2048]{1,0:T(8,128)}, f32[2,8,32,1024]{3,2,1,0:T(8,128)}, f32[8,2,16,1024]{3,2,1,0:T(8,128)}, f32[1024,512]{1,...) custom-call(s32[18]{0:T(128)} %compare_select_fusion.5.table.core_ref._, bf16[400,1024]{1,0:T(8,128)(2,1)} %copy-done.18, ...), custom_call_target="tpu_custom_call" | custom-call | flops 1 | bytes 1 | tf_op jit(solution)/shard_map/place/pallas_call | solution.py:695
  236.9 1.3 fusion.21
  240.4 8.9 %collective-permute-done.26.refs_7_ = bf16[400,1024]{1,0:T(8,128)(2,1)} collective-permute-done((bf16[400,1024]{1,0:T(8,128)(2,1)S(1)}, bf16[400,1024]{1,0:T(8,128)(2,1)}, u32[]{:S(2)}, u32[]{:S(2)}) %collective-permute-start.26) | collective-permute-done | bytes 819232 | tf_op jit(solution)/shard_map/ppermute | solution.py:549
  249.3 2.3 collective-permute-done.27.refs_8_
  252.1 1.6 collective-permute-start.30
  254.2 1.3 collective-permute-start.34
  255.8 2.1 add_convert_fusion
  257.9 6.9 %place.6 = (f32[2048,1024]{1,0:T(8,128)}, f32[1024,2048]{1,0:T(8,128)}, f32[2,8,32,1024]{3,2,1,0:T(8,128)}, f32[8,2,16,1024]{3,2,1,0:T(8,128)}, f32[1024,512]{1,...) custom-call(s32[18]{0:T(128)} %compare_select_fusion.5.table.core_re, ...), custom_call_target="tpu_custom_call", output_to_operand_aliasing={{0}: (1, {}), {1}: (2, {}), {2}: (3, {}), {3}: (4, {}), {4}... | custom-call | flops 1 | bytes 1 | tf_op jit(solution)/shard_map/place/pallas_call | solution.py:695
  264.8 2.7 collective-permute-done.34
  267.5 5.2 %collective-permute-done.30.refs_7_ = bf16[400,1024]{1,0:T(8,128)(2,1)} collective-permute-done((bf16[400,1024]{1,0:T(8,128)(2,1)}, bf16[400,1024]{1,0:T(8,128)(2,1)}, u32[]{:S(2)}, u32[]{:S(2)}) %collective-permute-start.30) | collective-permute-done | bytes 819232 | tf_op jit(solution)/shard_map/ppermute | solution.py:549
  275.3 1.6 collective-permute-start.36
  278.6 6.9 %place.7 = (f32[2048,1024]{1,0:T(8,128)}, f32[1024,2048]{1,0:T(8,128)}, f32[2,8,32,1024]{3,2,1,0:T(8,128)}, f32[8,2,16,1024]{3,2,1,0:T(8,128)}, f32[1024,512]{1,...) custom-call(s32[18]{0:T(128)} %compare_select_fusion.5.table.core_re, ...), custom_call_target="tpu_custom_call", output_to_operand_aliasing={{0}: (1, {}), {1}: (2, {}), {2}: (3, {}), {3}: (4, {}), {4}... | custom-call | flops 1 | bytes 1 | tf_op jit(solution)/shard_map/place/pallas_call | solution.py:695
  285.4 10.1 %collective-permute-done.35.left.refs_7_ = bf16[400,1024]{1,0:T(8,128)(2,1)S(1)} collective-permute-done((bf16[400,1024]{1,0:T(8,128)(2,1)}, bf16[400,1024]{1,0:T(8,128)(2,1)S(1)}, u32[]{:S(2)}, u32[]{:S(2)}) %collective-permute-start.35) | collective-permute-done | bytes 819232 | tf_op jit(solution)/shard_map/ppermute | solution.py:549
  298.1 4.3 %all-to-all-start.5 = ((bf16[32,32,128]{2,1,0:T(8,128)(2,1)}), bf16[32,32,128]{2,1,0:T(8,128)(2,1)S(1)}, u32[]{:S(2)}, u32[]{:S(2)}) async-start(bf16[32,32,128]{2,1,0:T(8,128)(2,1)} %broadcast_in_dim.55), calls=%async_computation.5 | async-start | bytes 524288 | tf_op jit(solution)/shard_map/all_to_all | solution.py:949
  302.3 2.0 halves.3
  304.4 1.8 collective-permute-start.39
  306.4 2.5 fusion.10
  308.9 6.9 %place.8 = (f32[2048,1024]{1,0:T(8,128)}, f32[1024,2048]{1,0:T(8,128)}, f32[2,8,32,1024]{3,2,1,0:T(8,128)}, f32[8,2,16,1024]{3,2,1,0:T(8,128)}, f32[1024,512]{1,...) custom-call(s32[18]{0:T(128)} %compare_select_fusion.5.table.core_re, ...), custom_call_target="tpu_custom_call", output_to_operand_aliasing={{0}: (1, {}), {1}: (2, {}), {2}: (3, {}), {3}: (4, {}), {4}... | custom-call | flops 1 | bytes 1 | tf_op jit(solution)/shard_map/place/pallas_call | solution.py:695
  315.8 2.0 collective-permute-done.39
  317.8 1.2 collective-permute-done.40
  320.0 1.5 collective-permute-done.43.refs_8_
  322.4 5.0 %place.9 = (f32[2048,1024]{1,0:T(8,128)}, f32[1024,2048]{1,0:T(8,128)}, f32[2,8,32,1024]{3,2,1,0:T(8,128)}, f32[8,2,16,1024]{3,2,1,0:T(8,128)}, f32[1024,512]{1,...) custom-call(s32[18]{0:T(128)} %compare_select_fusion.5.table.core_re, ...), custom_call_target="tpu_custom_call", output_to_operand_aliasing={{0}: (1, {}), {1}: (2, {}), {2}: (3, {}), {3}: (4, {}), {4}... | custom-call | flops 1 | bytes 1 | tf_op jit(solution)/shard_map/place/pallas_call | solution.py:695
  327.4 1.3 reduce_sum.109
  (199 shorter events, 36.7 us)
Async XLA Ops:
  7.8 61.0 %copy-start.14 = (bf16[512,1024]{1,0:T(8,128)(2,1)S(1)}, bf16[512,1024]{1,0:T(8,128)(2,1)}, u32[]{:S(2)}) copy-start(bf16[512,1024]{1,0:T(8,128)(2,1)} %refs_3_.1) | copy-start | bytes 3145732
  37.4 2.4 collective-permute-start.2
  37.5 18.6 %collective-permute-start = (bf16[256,512]{1,0:T(8,128)(2,1)}, bf16[256,512]{1,0:T(8,128)(2,1)S(1)}, u32[]{:S(2)}, u32[]{:S(2)}) collective-permute-start(bf16[256,512]{1,0:T(8,128)(2,1)} %get-tuple-element.197.refs_0_), channel_id=1, source_target_pairs={{0,8},{8,16},{16,24},{24,28},{28,20},{20,12},{12,4},{4,0},{1,9},{9... | collective-permute-start | bytes 786440 | tf_op jit(solution)/shard_map/ppermute | solution.py:549
  38.2 17.9 %collective-permute-start.1 = (bf16[256,512]{1,0:T(8,128)(2,1)}, bf16[256,512]{1,0:T(8,128)(2,1)S(1)}, u32[]{:S(2)}, u32[]{:S(2)}) collective-permute-start(bf16[256,512]{1,0:T(8,128)(2,1)} %get-tuple-element.197.refs_0_), channel_id=1, source_target_pairs={{0,4},{8,0},{16,8},{24,16},{28,24},{20,28},{12,20},{4,12},{1,5},{9... | collective-permute-start | bytes 786440 | tf_op jit(solution)/shard_map/ppermute | solution.py:549
  56.1 38.4 %copy-start.36 = (bf16[256,512]{1,0:T(8,128)(2,1)}, bf16[256,512]{1,0:T(8,128)(2,1)S(1)}, u32[]{:S(2)}) copy-start(bf16[256,512]{1,0:T(8,128)(2,1)S(1)} %collective-permute-done.refs_1_) | copy-start | bytes 786436
  56.1 38.4 %copy-start.37 = (bf16[256,512]{1,0:T(8,128)(2,1)}, bf16[256,512]{1,0:T(8,128)(2,1)S(1)}, u32[]{:S(2)}) copy-start(bf16[256,512]{1,0:T(8,128)(2,1)S(1)} %collective-permute-done.1.refs_2_) | copy-start | bytes 786436
  69.3 12.6 %copy-start.21 = (bf16[256,1024]{1,0:T(8,128)(2,1)}, bf16[256,1024]{1,0:T(8,128)(2,1)S(1)}, u32[]{:S(2)}) copy-start(bf16[256,1024]{1,0:T(8,128)(2,1)S(1)} %convolution_convert_fusion.refs_0_) | copy-start | bytes 1572868
  69.4 12.6 %collective-permute-start.7 = (bf16[256,1024]{1,0:T(8,128)(2,1)S(1)}, bf16[256,1024]{1,0:T(8,128)(2,1)S(1)}, u32[]{:S(2)}, u32[]{:S(2)}) collective-permute-start(bf16[256,1024]{1,0:T(8,128)(2,1)S(1)} %convolution_convert_fusion.refs_0_), channel_id=1, source_target_pairs={{0,1},{1,0},{2,3},{3,2},{4,5},{5,4},{6,7},{7,6},{8,9},{9,8},{10,11... | collective-permute-start | bytes 1572872 | tf_op jit(solution)/shard_map/ppermute | solution.py:462
  70.9 6.7 %collective-permute-start.3 = (bf16[256,512]{1,0:T(8,128)(2,1)S(1)}, bf16[256,512]{1,0:T(8,128)(2,1)S(1)}, u32[]{:S(2)}, u32[]{:S(2)}) collective-permute-start(bf16[256,512]{1,0:T(8,128)(2,1)S(1)} %collective-permute-done.refs_1_), channel_id=1, source_target_pairs={{0,8},{8,16},{16,24},{24,28},{28,20},{20,12},{12,4},{4,0},{1,9},{9... | collective-permute-start | bytes 786440 | tf_op jit(solution)/shard_map/ppermute | solution.py:549
  72.0 6.4 %collective-permute-start.4 = (bf16[256,512]{1,0:T(8,128)(2,1)S(1)}, bf16[256,512]{1,0:T(8,128)(2,1)S(1)}, u32[]{:S(2)}, u32[]{:S(2)}) collective-permute-start(bf16[256,512]{1,0:T(8,128)(2,1)S(1)} %collective-permute-done.1.refs_2_), channel_id=1, source_target_pairs={{0,4},{8,0},{16,8},{24,16},{28,24},{20,28},{12,20},{4,12},{1,5},{9... | collective-permute-start | bytes 786440 | tf_op jit(solution)/shard_map/ppermute | solution.py:549
  77.6 16.9 %copy-start.38 = (bf16[256,512]{1,0:T(8,128)(2,1)}, bf16[256,512]{1,0:T(8,128)(2,1)S(1)}, u32[]{:S(2)}) copy-start(bf16[256,512]{1,0:T(8,128)(2,1)S(1)} %collective-permute-done.3.refs_3_) | copy-start | bytes 786436
  78.4 16.1 %copy-start.39 = (bf16[256,512]{1,0:T(8,128)(2,1)}, bf16[256,512]{1,0:T(8,128)(2,1)S(1)}, u32[]{:S(2)}) copy-start(bf16[256,512]{1,0:T(8,128)(2,1)S(1)} %collective-permute-done.4.refs_4_) | copy-start | bytes 786436
  78.4 16.1 %collective-permute-start.5 = (bf16[256,512]{1,0:T(8,128)(2,1)S(1)}, bf16[256,512]{1,0:T(8,128)(2,1)S(1)}, u32[]{:S(2)}, u32[]{:S(2)}) collective-permute-start(bf16[256,512]{1,0:T(8,128)(2,1)S(1)} %collective-permute-done.3.refs_3_), channel_id=1, source_target_pairs={{0,8},{8,16},{16,24},{24,28},{28,20},{20,12},{12,4},{4,0},{1,9},{9... | collective-permute-start | bytes 786440 | tf_op jit(solution)/shard_map/ppermute | solution.py:549
  79.8 14.7 %collective-permute-start.6 = (bf16[256,512]{1,0:T(8,128)(2,1)S(1)}, bf16[256,512]{1,0:T(8,128)(2,1)S(1)}, u32[]{:S(2)}, u32[]{:S(2)}) collective-permute-start(bf16[256,512]{1,0:T(8,128)(2,1)S(1)} %collective-permute-done.4.refs_4_), channel_id=1, source_target_pairs={{0,4},{8,0},{16,8},{24,16},{28,24},{20,28},{12,20},{4,12},{1,5},{9... | collective-permute-start | bytes 786440 | tf_op jit(solution)/shard_map/ppermute | solution.py:549
  94.5 3.7 %collective-permute-start.9 = (bf16[256,2048]{1,0:T(8,128)(2,1)}, bf16[256,2048]{1,0:T(8,128)(2,1)S(1)}, u32[]{:S(2)}, u32[]{:S(2)}) collective-permute-start(bf16[256,2048]{1,0:T(8,128)(2,1)} %get-tuple-element.216), channel_id=1, source_target_pairs={{0,2},{2,0},{1,3},{3,1},{4,6},{6,4},{5,7},{7,5},{8,10},{10,8},{9,1... | collective-permute-start | bytes 3145736 | tf_op jit(solution)/shard_map/ppermute | solution.py:431
  94.6 3.6 %collective-permute-start.8 = (bf16[256,1024]{1,0:T(8,128)(2,1)}, bf16[256,1024]{1,0:T(8,128)(2,1)S(1)}, u32[]{:S(2)}, u32[]{:S(2)}) collective-permute-start(bf16[256,1024]{1,0:T(8,128)(2,1)} %get-tuple-element.214), channel_id=1, source_target_pairs={{0,2},{2,0},{1,3},{3,1},{4,6},{6,4},{5,7},{7,5},{8,10},{10,8},{9,1... | collective-permute-start | bytes 1572872 | tf_op jit(solution)/shard_map/ppermute | solution.py:431
  95.1 14.1 %collective-permute-start.14 = (bf16[256,1024]{1,0:T(8,128)(2,1)}, bf16[256,1024]{1,0:T(8,128)(2,1)S(1)}, u32[]{:S(2)}, u32[]{:S(2)}) collective-permute-start(bf16[256,1024]{1,0:T(8,128)(2,1)} %get-tuple-element.226.refs_0_), channel_id=1, source_target_pairs={{0,1},{1,0},{2,3},{3,2},{4,5},{5,4},{6,7},{7,6},{8,9},{9,8},{10,11... | collective-permute-start | bytes 1572872 | tf_op jit(solution)/shard_map/ppermute | solution.py:462
  103.1 11.9 %collective-permute-start.10 = (bf16[256,512]{1,0:T(8,128)(2,1)}, bf16[256,512]{1,0:T(8,128)(2,1)S(1)}, u32[]{:S(2)}, u32[]{:S(2)}) collective-permute-start(bf16[256,512]{1,0:T(8,128)(2,1)} %get-tuple-element.217), channel_id=1, source_target_pairs={{0,8},{8,16},{16,24},{24,28},{28,20},{20,12},{12,4},{4,0},{1,9},{9... | collective-permute-start | bytes 786440 | tf_op jit(solution)/shard_map/ppermute | solution.py:604
  103.4 11.6 %collective-permute-start.11 = (bf16[256,512]{1,0:T(8,128)(2,1)}, bf16[256,512]{1,0:T(8,128)(2,1)S(1)}, u32[]{:S(2)}, u32[]{:S(2)}) collective-permute-start(bf16[256,512]{1,0:T(8,128)(2,1)} %get-tuple-element.218), channel_id=1, source_target_pairs={{0,4},{8,0},{16,8},{24,16},{28,24},{20,28},{12,20},{4,12},{1,5},{9... | collective-permute-start | bytes 786440 | tf_op jit(solution)/shard_map/ppermute | solution.py:604
  106.8 7.7 %collective-permute-start.12 = (bf16[256,256]{1,0:T(8,128)(2,1)}, bf16[256,256]{1,0:T(8,128)(2,1)S(1)}, u32[]{:S(2)}, u32[]{:S(2)}) collective-permute-start(bf16[256,256]{1,0:T(8,128)(2,1)} %get-tuple-element.221), channel_id=1, source_target_pairs={{0,8},{8,16},{16,24},{24,28},{28,20},{20,12},{12,4},{4,0},{1,9},{9... | collective-permute-start | bytes 393224 | tf_op jit(solution)/shard_map/ppermute | solution.py:549
  107.3 7.7 %collective-permute-start.13 = (bf16[256,256]{1,0:T(8,128)(2,1)}, bf16[256,256]{1,0:T(8,128)(2,1)S(1)}, u32[]{:S(2)}, u32[]{:S(2)}) collective-permute-start(bf16[256,256]{1,0:T(8,128)(2,1)} %get-tuple-element.222), channel_id=1, source_target_pairs={{0,4},{8,0},{16,8},{24,16},{28,24},{20,28},{12,20},{4,12},{1,5},{9... | collective-permute-start | bytes 393224 | tf_op jit(solution)/shard_map/ppermute | solution.py:549
  119.6 11.7 %collective-permute-start.18 = (bf16[256,1024]{1,0:T(8,128)(2,1)}, bf16[256,1024]{1,0:T(8,128)(2,1)}, u32[]{:S(2)}, u32[]{:S(2)}) collective-permute-start(bf16[256,1024]{1,0:T(8,128)(2,1)} %get-tuple-element.245), channel_id=1, source_target_pairs={{0,2},{2,0},{1,3},{3,1},{4,6},{6,4},{5,7},{7,5},{8,10},{10,8},{9,1... | collective-permute-start | bytes 1572872 | tf_op jit(solution)/shard_map/ppermute | solution.py:431
  120.3 11.0 %collective-permute-start.17 = (bf16[256,256]{1,0:T(8,128)(2,1)}, bf16[256,256]{1,0:T(8,128)(2,1)}, u32[]{:S(2)}, u32[]{:S(2)}) collective-permute-start(bf16[256,256]{1,0:T(8,128)(2,1)} %constant_dynamic-slice_fusion.1), channel_id=1, source_target_pairs={{0,2},{2,0},{1,3},{3,1},{4,6},{6,4},{5,7},{7,5},{8,10},{10,8},{9,1... | collective-permute-start | bytes 393224 | tf_op jit(solution)/shard_map/ppermute | solution.py:431
  120.8 13.7 %all-to-all-start.2 = ((bf16[8,64,256]{2,1,0:T(8,128)(2,1)}), bf16[8,64,256]{2,1,0:T(8,128)(2,1)S(1)}, u32[]{:S(2)}, u32[]{:S(2)}) async-start(bf16[8,64,256]{2,1,0:T(8,128)(2,1)} %bitcast.9), calls=%async_computation.2 | async-start | bytes 524288 | tf_op jit(solution)/shard_map/all_to_all | solution.py:435
  129.7 11.9 %copy-start.4 = (f32[8,64,256]{2,1,0:T(8,128)S(1)}, f32[8,64,256]{2,1,0:T(8,128)}, u32[]{:S(2)}) copy-start(f32[8,64,256]{2,1,0:T(8,128)} %get-tuple-element.241.raw_ref) | copy-start | bytes 1572868
  129.7 64.8 %collective-permute-start.24 = (bf16[2048,512]{1,0:T(8,128)(2,1)}, bf16[2048,512]{1,0:T(8,128)(2,1)}, u32[]{:S(2)}, u32[]{:S(2)}) collective-permute-start(bf16[2048,512]{1,0:T(8,128)(2,1)} %join.1.refs_0_), channel_id=1, source_target_pairs={{0,1},{1,0},{2,3},{3,2},{4,5},{5,4},{6,7},{7,6},{8,9},{9,8},{10,11... | collective-permute-start | bytes 6291464 | tf_op jit(solution)/shard_map/ppermute | solution.py:462
  134.5 26.6 %all-to-all-start.3 = ((bf16[8,32,1024]{2,1,0:T(8,128)(2,1)}), bf16[8,32,1024]{2,1,0:T(8,128)(2,1)S(1)}, u32[]{:S(2)}, u32[]{:S(2)}) async-start(bf16[8,32,1024]{2,1,0:T(8,128)(2,1)} %bitcast.50), calls=%async_computation.3 | async-start | bytes 1048576 | tf_op jit(solution)/shard_map/all_to_all | solution.py:435
  139.5 19.3 %collective-permute-start.15 = (bf16[256,1024]{1,0:T(8,128)(2,1)}, bf16[256,1024]{1,0:T(8,128)(2,1)S(1)}, u32[]{:S(2)}, u32[]{:S(2)}) collective-permute-start(bf16[256,1024]{1,0:T(8,128)(2,1)} %get-tuple-element.238), channel_id=1, source_target_pairs={{0,8},{8,16},{16,24},{24,28},{28,20},{20,12},{12,4},{4,0},{1,9},{9... | collective-permute-start | bytes 1572872 | tf_op jit(solution)/shard_map/ppermute | solution.py:604
  141.5 19.5 %collective-permute-start.16 = (bf16[256,1024]{1,0:T(8,128)(2,1)}, bf16[256,1024]{1,0:T(8,128)(2,1)}, u32[]{:S(2)}, u32[]{:S(2)}) collective-permute-start(bf16[256,1024]{1,0:T(8,128)(2,1)} %get-tuple-element.239), channel_id=1, source_target_pairs={{0,4},{8,0},{16,8},{24,16},{28,24},{20,28},{12,20},{4,12},{1,5},{9... | collective-permute-start | bytes 1572872 | tf_op jit(solution)/shard_map/ppermute | solution.py:604
  165.1 16.4 %collective-permute-start.19 = (bf16[256,1024]{1,0:T(8,128)(2,1)}, bf16[256,1024]{1,0:T(8,128)(2,1)}, u32[]{:S(2)}, u32[]{:S(2)}) collective-permute-start(bf16[256,1024]{1,0:T(8,128)(2,1)} %get-tuple-element.254), channel_id=1, source_target_pairs={{0,8},{8,16},{16,24},{24,28},{28,20},{20,12},{12,4},{4,0},{1,9},{9... | collective-permute-start | bytes 1572872 | tf_op jit(solution)/shard_map/ppermute | solution.py:604
  169.3 12.4 %collective-permute-start.20 = (bf16[256,1024]{1,0:T(8,128)(2,1)}, bf16[256,1024]{1,0:T(8,128)(2,1)}, u32[]{:S(2)}, u32[]{:S(2)}) collective-permute-start(bf16[256,1024]{1,0:T(8,128)(2,1)} %get-tuple-element.255), channel_id=1, source_target_pairs={{0,4},{8,0},{16,8},{24,16},{28,24},{20,28},{12,20},{4,12},{1,5},{9... | collective-permute-start | bytes 1572872 | tf_op jit(solution)/shard_map/ppermute | solution.py:604
  169.3 16.2 %collective-permute-start.23 = (bf16[8,128,256]{2,1,0:T(8,128)(2,1)}, bf16[8,128,256]{2,1,0:T(8,128)(2,1)}, u32[]{:S(2)}, u32[]{:S(2)}) collective-permute-start(bf16[8,128,256]{2,1,0:T(8,128)(2,1)} %get-tuple-element.271), channel_id=1, source_target_pairs={{0,2},{2,0},{1,3},{3,1},{4,6},{6,4},{5,7},{7,5},{8,10},{10,8},{9,1... | collective-permute-start | bytes 1572872 | tf_op jit(solution)/shard_map/ppermute | solution.py:431
  187.8 49.0 %all-to-all-start.4 = ((bf16[8,192,256]{2,1,0:T(8,128)(2,1)}), bf16[8,192,256]{2,1,0:T(8,128)(2,1)}, u32[]{:S(2)}, u32[]{:S(2)}) async-start(bf16[8,192,256]{2,1,0:T(8,128)(2,1)} %pad_maximum_fusion.2), calls=%async_computation.4 | async-start | bytes 1572864 | tf_op jit(solution)/shard_map/all_to_all | solution.py:435
  192.5 25.5 %collective-permute-start.21 = (bf16[256,1024]{1,0:T(8,128)(2,1)}, bf16[256,1024]{1,0:T(8,128)(2,1)S(1)}, u32[]{:S(2)}, u32[]{:S(2)}) collective-permute-start(bf16[256,1024]{1,0:T(8,128)(2,1)} %get-tuple-element.266), channel_id=1, source_target_pairs={{0,8},{8,16},{16,24},{24,28},{28,20},{20,12},{12,4},{4,0},{1,9},{9... | collective-permute-start | bytes 1572872 | tf_op jit(solution)/shard_map/ppermute | solution.py:604
  194.5 24.9 %collective-permute-start.22 = (bf16[256,1024]{1,0:T(8,128)(2,1)S(1)}, bf16[256,1024]{1,0:T(8,128)(2,1)S(1)}, u32[]{:S(2)}, u32[]{:S(2)}) collective-permute-start(bf16[256,1024]{1,0:T(8,128)(2,1)S(1)} %copy-done.48), channel_id=1, source_target_pairs={{0,4},{8,0},{16,8},{24,16},{28,24},{20,28},{12,20},{4,12},{1,5},{9... | collective-permute-start | bytes 1572872 | tf_op jit(solution)/shard_map/ppermute | solution.py:604
  200.5 1.5 collective-permute-start.25
  203.1 22.0 %copy-start.29 = (bf16[256,1024]{1,0:T(8,128)(2,1)S(1)}, bf16[256,1024]{1,0:T(8,128)(2,1)}, u32[]{:S(2)}) copy-start(bf16[256,1024]{1,0:T(8,128)(2,1)} %get-tuple-element.308) | copy-start | bytes 1572868
  223.7 14.4 %copy-start.15 = (bf16[1024,512]{1,0:T(8,128)(2,1)S(1)}, bf16[1024,512]{1,0:T(8,128)(2,1)}, u32[]{:S(2)}) copy-start(bf16[1024,512]{1,0:T(8,128)(2,1)} %refs_0_.1) | copy-start | bytes 3145732
  224.9 6.6 %collective-permute-start.28 = (bf16[400,1024]{1,0:T(8,128)(2,1)S(1)}, bf16[400,1024]{1,0:T(8,128)(2,1)S(1)}, u32[]{:S(2)}, u32[]{:S(2)}) collective-permute-start(bf16[400,1024]{1,0:T(8,128)(2,1)S(1)} %pad_maximum_fusion.refs_0_), channel_id=1, source_target_pairs={{0,2},{2,0},{1,3},{3,1},{4,6},{6,4},{5,7},{7,5},{8,10},{10,8},{9,1... | collective-permute-start | bytes 2457608 | tf_op jit(solution)/shard_map/ppermute | solution.py:431
  225.0 15.3 %collective-permute-start.29 = (bf16[256,1024]{1,0:T(8,128)(2,1)S(1)}, bf16[256,1024]{1,0:T(8,128)(2,1)}, u32[]{:S(2)}, u32[]{:S(2)}) collective-permute-start(bf16[256,1024]{1,0:T(8,128)(2,1)S(1)} %copy-done.29), channel_id=1, source_target_pairs={{0,1},{1,0},{2,3},{3,2},{4,5},{5,4},{6,7},{7,6},{8,9},{9,8},{10,11... | collective-permute-start | bytes 1572872 | tf_op jit(solution)/shard_map/ppermute | solution.py:462
  225.8 23.5 %collective-permute-start.26 = (bf16[400,1024]{1,0:T(8,128)(2,1)S(1)}, bf16[400,1024]{1,0:T(8,128)(2,1)}, u32[]{:S(2)}, u32[]{:S(2)}) collective-permute-start(bf16[400,1024]{1,0:T(8,128)(2,1)S(1)} %pad_maximum_fusion.refs_0_), channel_id=1, source_target_pairs={{0,8},{8,16},{16,24},{24,28},{28,20},{20,12},{12,4},{4,0},{1,9},{9... | collective-permute-start | bytes 2457608 | tf_op jit(solution)/shard_map/ppermute | solution.py:549
  231.5 20.1 %collective-permute-start.27 = (bf16[400,1024]{1,0:T(8,128)(2,1)S(1)}, bf16[400,1024]{1,0:T(8,128)(2,1)}, u32[]{:S(2)}, u32[]{:S(2)}) collective-permute-start(bf16[400,1024]{1,0:T(8,128)(2,1)S(1)} %pad_maximum_fusion.refs_0_), channel_id=1, source_target_pairs={{0,4},{8,0},{16,8},{24,16},{28,24},{20,28},{12,20},{4,12},{1,5},{9... | collective-permute-start | bytes 2457608 | tf_op jit(solution)/shard_map/ppermute | solution.py:549
  239.2 15.0 %copy-start.47 = (s32[32]{0:T(128)S(1)}, s32[32]{0:T(128)}, u32[]{:S(2)}) copy-start(s32[32]{0:T(128)} %steps_ref.1) | copy-start | bytes 388
  239.2 16.3 %copy-start.46 = (s32[256]{0:T(256)S(1)}, s32[256]{0:T(256)}, u32[]{:S(2)}) copy-start(s32[256]{0:T(256)} %param.20) | copy-start | bytes 3076
  239.2 16.4 %copy-start.10 = (bf16[256,1024]{1,0:T(8,128)(2,1)S(1)}, bf16[256,1024]{1,0:T(8,128)(2,1)}, u32[]{:S(2)}) copy-start(bf16[256,1024]{1,0:T(8,128)(2,1)} %input_ref.3) | copy-start | bytes 1572868
  239.9 15.9 %copy-start.13 = (f32[256,1024]{1,0:T(8,128)S(1)}, f32[256,1024]{1,0:T(8,128)}, u32[]{:S(2)}) copy-start(f32[256,1024]{1,0:T(8,128)} %get-tuple-element.223.hidden_ref) | copy-start | bytes 3145732
  239.9 15.9 %copy-start.30 = (bf16[256,1024]{1,0:T(8,128)(2,1)S(1)}, bf16[256,1024]{1,0:T(8,128)(2,1)}, u32[]{:S(2)}) copy-start(bf16[256,1024]{1,0:T(8,128)(2,1)} %get-tuple-element.308) | copy-start | bytes 1572868
  239.9 15.9 %copy-start.45 = (f32[1024]{0:T(1024)S(1)}, f32[1024]{0:T(1024)}, u32[]{:S(2)}) copy-start(f32[1024]{0:T(1024)} %param.35) | copy-start | bytes 12292
  251.6 6.2 %collective-permute-start.32 = (bf16[400,1024]{1,0:T(8,128)(2,1)}, bf16[400,1024]{1,0:T(8,128)(2,1)}, u32[]{:S(2)}, u32[]{:S(2)}) collective-permute-start(bf16[400,1024]{1,0:T(8,128)(2,1)} %collective-permute-done.26.refs_7_), channel_id=1, source_target_pairs={{0,2},{2,0},{1,3},{3,1},{4,6},{6,4},{5,7},{7,5},{8,10},{10,8},{9,1... | collective-permute-start | bytes 2457608 | tf_op jit(solution)/shard_map/ppermute | solution.py:431
  251.6 6.2 %collective-permute-start.33 = (bf16[400,1024]{1,0:T(8,128)(2,1)}, bf16[400,1024]{1,0:T(8,128)(2,1)}, u32[]{:S(2)}, u32[]{:S(2)}) collective-permute-start(bf16[400,1024]{1,0:T(8,128)(2,1)} %collective-permute-done.27.refs_8_), channel_id=1, source_target_pairs={{0,2},{2,0},{1,3},{3,1},{4,6},{6,4},{5,7},{7,5},{8,10},{10,8},{9,1... | collective-permute-start | bytes 2457608 | tf_op jit(solution)/shard_map/ppermute | solution.py:431
  252.1 20.5 %collective-permute-start.30 = (bf16[400,1024]{1,0:T(8,128)(2,1)}, bf16[400,1024]{1,0:T(8,128)(2,1)}, u32[]{:S(2)}, u32[]{:S(2)}) collective-permute-start(bf16[400,1024]{1,0:T(8,128)(2,1)} %collective-permute-done.26.refs_7_), channel_id=1, source_target_pairs={{0,8},{8,16},{16,24},{24,28},{28,20},{20,12},{12,4},{4,0},{1,9},{9... | collective-permute-start | bytes 2457608 | tf_op jit(solution)/shard_map/ppermute | solution.py:549
  253.7 20.1 %collective-permute-start.31 = (bf16[400,1024]{1,0:T(8,128)(2,1)}, bf16[400,1024]{1,0:T(8,128)(2,1)S(1)}, u32[]{:S(2)}, u32[]{:S(2)}) collective-permute-start(bf16[400,1024]{1,0:T(8,128)(2,1)} %collective-permute-done.27.refs_8_), channel_id=1, source_target_pairs={{0,4},{8,0},{16,8},{24,16},{28,24},{20,28},{12,20},{4,12},{1,5},{9... | collective-permute-start | bytes 2457608 | tf_op jit(solution)/shard_map/ppermute | solution.py:549
  254.2 13.3 %collective-permute-start.34 = (bf16[256,1024]{1,0:T(8,128)(2,1)S(1)}, bf16[256,1024]{1,0:T(8,128)(2,1)S(1)}, u32[]{:S(2)}, u32[]{:S(2)}) collective-permute-start(bf16[256,1024]{1,0:T(8,128)(2,1)S(1)} %get-tuple-element.353), channel_id=1, source_target_pairs={{0,1},{1,0},{2,3},{3,2},{4,5},{5,4},{6,7},{7,6},{8,9},{9,8},{10,11... | collective-permute-start | bytes 1572872 | tf_op jit(solution)/shard_map/ppermute | solution.py:462
  274.7 2.7 collective-permute-start.37
  274.7 20.9 %collective-permute-start.35 = (bf16[400,1024]{1,0:T(8,128)(2,1)}, bf16[400,1024]{1,0:T(8,128)(2,1)S(1)}, u32[]{:S(2)}, u32[]{:S(2)}) collective-permute-start(bf16[400,1024]{1,0:T(8,128)(2,1)} %collective-permute-done.30.refs_7_), channel_id=1, source_target_pairs={{0,8},{8,16},{16,24},{24,28},{28,20},{20,12},{12,4},{4,0},{1,9},{9... | collective-permute-start | bytes 2457608 | tf_op jit(solution)/shard_map/ppermute | solution.py:549
  275.1 3.5 %collective-permute-start.38 = (bf16[400,1024]{1,0:T(8,128)(2,1)}, bf16[400,1024]{1,0:T(8,128)(2,1)}, u32[]{:S(2)}, u32[]{:S(2)}) collective-permute-start(bf16[400,1024]{1,0:T(8,128)(2,1)} %copy-done.27), channel_id=1, source_target_pairs={{0,2},{2,0},{1,3},{3,1},{4,6},{6,4},{5,7},{7,5},{8,10},{10,8},{9,1... | collective-permute-start | bytes 2457608 | tf_op jit(solution)/shard_map/ppermute | solution.py:431
  275.3 20.7 %collective-permute-start.36 = (bf16[400,1024]{1,0:T(8,128)(2,1)}, bf16[400,1024]{1,0:T(8,128)(2,1)}, u32[]{:S(2)}, u32[]{:S(2)}) collective-permute-start(bf16[400,1024]{1,0:T(8,128)(2,1)} %copy-done.27), channel_id=1, source_target_pairs={{0,4},{8,0},{16,8},{24,16},{28,24},{20,28},{12,20},{4,12},{1,5},{9... | collective-permute-start | bytes 2457608 | tf_op jit(solution)/shard_map/ppermute | solution.py:549
  277.3 19.3 %copy-start.42 = (f32[1024]{0:T(1024)S(1)}, f32[1024]{0:T(1024)}, u32[]{:S(2)}) copy-start(f32[1024]{0:T(1024)} %param.22) | copy-start | bytes 12292
  296.1 12.8 %collective-permute-start.41 = (bf16[400,1024]{1,0:T(8,128)(2,1)S(1)}, bf16[400,1024]{1,0:T(8,128)(2,1)}, u32[]{:S(2)}, u32[]{:S(2)}) collective-permute-start(bf16[400,1024]{1,0:T(8,128)(2,1)S(1)} %collective-permute-done.35.left.refs_7_), channel_id=1, source_target_pairs={{0,2},{2,0},{1,3},{3,1},{4,6},{6,4},{5,7},{7,5},{8,10},{10,8},{9,1... | collective-permute-start | bytes 2457608 | tf_op jit(solution)/shard_map/ppermute | solution.py:431
  296.1 12.8 %collective-permute-start.42 = (bf16[400,1024]{1,0:T(8,128)(2,1)}, bf16[400,1024]{1,0:T(8,128)(2,1)}, u32[]{:S(2)}, u32[]{:S(2)}) collective-permute-start(bf16[400,1024]{1,0:T(8,128)(2,1)} %collective-permute-done.36.right.refs_8_), channel_id=1, source_target_pairs={{0,2},{2,0},{1,3},{3,1},{4,6},{6,4},{5,7},{7,5},{8,10},{10,8},{9,1... | collective-permute-start | bytes 2457608 | tf_op jit(solution)/shard_map/ppermute | solution.py:431
  298.1 21.1 %all-to-all-start.5 = ((bf16[32,32,128]{2,1,0:T(8,128)(2,1)}), bf16[32,32,128]{2,1,0:T(8,128)(2,1)S(1)}, u32[]{:S(2)}, u32[]{:S(2)}) async-start(bf16[32,32,128]{2,1,0:T(8,128)(2,1)} %broadcast_in_dim.55), calls=%async_computation.5 | async-start | bytes 524288 | tf_op jit(solution)/shard_map/all_to_all | solution.py:949
  304.4 13.4 %collective-permute-start.39 = (bf16[400,512]{1,0:T(8,128)(2,1)}, bf16[400,512]{1,0:T(8,128)(2,1)S(1)}, u32[]{:S(2)}, u32[]{:S(2)}) collective-permute-start(bf16[400,512]{1,0:T(8,128)(2,1)} %get-tuple-element.336), channel_id=1, source_target_pairs={{0,8},{8,16},{16,24},{24,28},{28,20},{20,12},{12,4},{4,0},{1,9},{9... | collective-permute-start | bytes 1228808 | tf_op jit(solution)/shard_map/ppermute | solution.py:549
  306.1 12.9 %collective-permute-start.40 = (bf16[400,512]{1,0:T(8,128)(2,1)}, bf16[400,512]{1,0:T(8,128)(2,1)S(1)}, u32[]{:S(2)}, u32[]{:S(2)}) collective-permute-start(bf16[400,512]{1,0:T(8,128)(2,1)} %get-tuple-element.337), channel_id=1, source_target_pairs={{0,4},{8,0},{16,8},{24,16},{28,24},{20,28},{12,20},{4,12},{1,5},{9... | collective-permute-start | bytes 1228808 | tf_op jit(solution)/shard_map/ppermute | solution.py:549
  319.1 2.4 collective-permute-start.43
  (33 other events, 149.9 us)

commit v15 on v14

--- a/solution.py
+++ b/solution.py
@@ -884,16 +884,17 @@
     out_near, out_far = share_halves(attn_out, 0)
     doutput = product(out_near, d_branch) + product(out_far, swap_cores(d_branch))
     doutput = doutput.astype(BF16).reshape(chips, -1, model)
+    grads, doutput = visit([ring], (grads, doutput))
     doutput = to_heads(doutput)
     *dquery, far_sums = backward_piece(
         queries, grads, raw, logsum, [], other, [], 0, 1, crops, (F32, BF16)
     )
-    grads, dquery, far_sums, doutput = visit([ring], (grads, dquery, far_sums, doutput))
+    grads, dquery, far_sums = visit([ring], (grads, dquery, far_sums))
     far_sums = swap_cores(far_sums)
     *dquery, near_sums = backward_piece(
         queries, grads, raw, logsum, dquery, own, [], 0, 1, crops, (BF16, F32)
     )
-    near_sums, dquery = visit([ring], (near_sums, dquery))
+    near_sums, dquery = ring.arrive((near_sums, dquery))
     (dquery,) = dquery
     key_value = (near_sums + far_sums.astype(F32)).astype(BF16)
     doutput, key_value = lax.optimization_barrier((doutput, key_value))
@@ -921,7 +922,6 @@
             lax.psum(product(attn_in, grad, 0, 1).astype(BF16), ("chip", "core")).astype(F32)
             for grad in (dquery, dkey, dvalue)
         ]
-    blocks = ring.arrive(blocks)
     total = ring.finish()
     start = total.shape[0]
     ring.size, ring.extra = size, blocks.shape[0] - size - small_rows
@@ -947,13 +947,14 @@
     everyone = ("chip", "core", "head")
     ends = jnp.broadcast_to(ends, (lax.axis_size(everyone),) + ends.shape)
     ends = lax.all_to_all(ends, everyone, 0, 0, tiled=True)
-    _, mlp_out = visit([gathered], (d_part, mlp_out))
+    ends = visit([gathered], ends)
+    ends = jnp.sum(ends.astype(F32), axis=0).reshape(-1)[: 3 * model].reshape(3, model)
+    ends, mlp_out = visit([gathered], (ends, mlp_out))
     block_output = hidden + down_bias
     for part in mlp_out:
         block_output += part.astype(F32)
     block_output = block_output.astype(BF16)
     d_in, block_output = visit([gathered], (d_in, block_output))
-    visit([gathered], ())
     d_in = functools.reduce(jnp.add, (part.astype(F32) for part in d_in))
     input_grad = (d_hidden + normalize_back(d_in * gain_attn, unit_attn, inverse_attn)).astype(
         BF16
@@ -961,7 +962,6 @@
     while gathered.busy():
         input_grad = visit([gathered], input_grad)
     ddown_weight, dup_weight, *rest = gathered.outputs
-    ends = jnp.sum(ends.astype(F32), axis=0).reshape(-1)[: 3 * model].reshape(3, model)
     if split == 1:
         doutput_weight, small, *projections = rest
         doutput_weight = doutput_weight.reshape(width, model)

time: 331 us -> 315 us (0.952)
  waiting for transfers between devices: 71.6 us -> 60.4 us
  starting transfers between devices: 58.2 us -> 53.9 us
    ppermute x24, waiting for transfers between devices: 60 us -> 31.6 us  [send(): lax.ppermute(block, 'chip', ring_pairs(direction))]
    all_to_all x3, waiting for transfers between devices: 0.97 us -> 11.7 us  [to_heads(): return lax.all_to_all(blocks, 'chip', 0, 0, tiled=True)]
    ppermute x24, starting transfers between devices: 30.3 us -> 24.7 us  [send(): lax.ppermute(block, 'chip', ring_pairs(direction))]
    all_to_all x1, waiting for transfers between devices: 0.01 us -> 4.45 us  [local(): ends = lax.all_to_all(ends, everyone, 0, 0, tiled=True)]
    ppermute x5, waiting for transfers between devices: 4.65 us -> 9.06 us  [across_heads(): return [part, lax.ppermute(part, 'head', [(0, 1), (1, 0)])]]
    unnamed x101 -> x93, local copies, waits for them, and re-layouts: 9.99 us -> 9.92 us
  transfers between devices with their start and end apart: 48 -> 48, of which waited for: 27 -> 23; matrix products, arithmetic and copies ran while one was open for 6% -> 6% of each run, Pallas kernels for 33% -> 33%
where the time goes in v15:
time: 315 us; the launch traced here: 313 us
  Pallas kernels  122 us (39%)
  waiting for transfers between devices  60.4 us (19%)
  starting transfers between devices  53.9 us (17%)
  blocking collectives  42.4 us (13%)
  other arithmetic  15.1 us (5%)
  local copies, waits for them, and re-layouts  14.2 us (5%)
  matrix products  3.52 us (1%)
    all_to_all x2, blocking collectives, to_heads(): return lax.all_to_all(blocks, 'chip', 0, 0, tiled=True)  42.4 us
    ppermute x24, waiting for transfers between devices, send(): lax.ppermute(block, 'chip', ring_pairs(direction))  31.6 us
    pallas_call x5, Pallas kernels, place(): pl.pallas_call(functools.partial(place_kernel, heads, (units, size, extra...  30.1 us
    ppermute x24, starting transfers between devices, send(): lax.ppermute(block, 'chip', ring_pairs(direction))  24.7 us
    pallas_call x2, Pallas kernels, backward_piece(): pl.pallas_call(functools.partial(backward_kernel, crops, len(before)), gr...  24 us
    pallas_call x5, Pallas kernels, add(): pl.pallas_call(functools.partial(add_kernel, starts, len(shapes)), grid_s...  18.6 us
    pallas_call x1, Pallas kernels, attention_forward(): pl.pallas_call(functools.partial(forward_kernel, crops, key_step(count)),...  15.3 us
    all_to_all x3, starting transfers between devices, to_heads(): return lax.all_to_all(blocks, 'chip', 0, 0, tiled=True)  15 us
  transfers between devices with their start and end apart: 48, of which 23 were waited for; matrix products, arithmetic and copies ran while one was open for 6% of the time, Pallas kernels for 33%

profile of v15, /device:TPU:0, one launch (start us, length us, event | category | flops | bytes accessed | tf_op | source)
XLA Modules:
  0.0 313.3 jit_solution(10459298241326964530)
XLA Ops:
  1.2 6.6 %project.1 = (bf16[8,208,256]{2,1,0:T(8,128)(2,1)}, bf16[256,1024]{1,0:T(8,128)(2,1)}, bf16[256,512]{1,0:T(8,128)(2,1)}) custom-call(s32[18]{0:T(128)} %compare_select_fusion.5.table.core_ref._, bf16[256,1024]{1,0:T(8,128)(2,1)} %input_ref.3, s32[1,256]{1,0:T(1,128)} %bitcast.67, s32[32]{0:T(128)} %steps_ref.1, f32[1,1024]{1,0:T(1,128)} %bitcast.50, ...), custom_call_target="tpu_custom_call" | custom-call | flops 1 | bytes 1 | tf_op jit(solution)/shard_map/project/pallas_call | solution.py:94
  7.8 29.6 %all_to_all.30.query_ref.own.refs_1_ = bf16[8,208,256]{2,1,0:T(8,128)(2,1)S(1)} all-to-all(bf16[8,208,256]{2,1,0:T(8,128)(2,1)} %get-tuple-element.198), channel_id=1, replica_groups=mesh['chip'=8,'core'=2,'head'=2] {'chip'}, dimensions={0} | all-to-all | bytes 1703936 | tf_op jit(solution)/shard_map/all_to_all | solution.py:435
  38.2 1.3 collective-permute-start.1
  40.7 15.3 %attention_forward.1 = (f32[8,64,256]{2,1,0:T(8,128)}, bf16[8,64,256]{2,1,0:T(8,128)(2,1)}, f32[8,1,256]{2,1,0:T(1,128)}) custom-call(bf16[8,208,256]{2,1,0:T(8,128)(2,1)} %copy-done, bf16[8,208,256]{2,1,0:T(8,128)(2,1)} %copy-done, bf16[8,208,256]{2,1,0:T(8,128)(2,1)} %copy-done.2), custom_call_target="tpu_custom_call" | custom-call | flops 1 | bytes 1 | tf_op jit(solution)/shard_map/attention_forward/pallas_call | solution.py:367
  56.1 12.8 %all_to_all.31 = bf16[8,64,256]{2,1,0:T(8,128)(2,1)S(1)} all-to-all(bf16[8,64,256]{2,1,0:T(8,128)(2,1)} %get-tuple-element.205), channel_id=1, replica_groups=mesh['chip'=8,'core'=2,'head'=2] {'chip'}, dimensions={0} | all-to-all | bytes 524288 | tf_op jit(solution)/shard_map/all_to_all | solution.py:435
  69.4 1.6 collective-permute-start.7
  72.9 4.6 %collective-permute-done.3.refs_3_ = bf16[256,512]{1,0:T(8,128)(2,1)S(1)} collective-permute-done((bf16[256,512]{1,0:T(8,128)(2,1)S(1)}, bf16[256,512]{1,0:T(8,128)(2,1)S(1)}, u32[]{:S(2)}, u32[]{:S(2)}) %collective-permute-start.3) | collective-permute-done | bytes 262176 | tf_op jit(solution)/shard_map/ppermute | solution.py:549
  78.4 1.4 collective-permute-start.5
  80.4 1.5 collective-permute-done.7.refs_1_
  82.7 11.7 %mlp.1 = (bf16[256,2048]{1,0:T(8,128)(2,1)}, bf16[256,2048]{1,0:T(8,128)(2,1)}, bf16[256,1024]{1,0:T(8,128)(2,1)}, bf16[256,1024]{1,0:T(8,128)(2,1)}, f32[256,10...) custom-call(s32[18]{0:T(128)} %compare_select_fusion.5.table.core_ref._, ...), custom_call_target="tpu_custom_call" | custom-call | flops 1 | bytes 1 | tf_op jit(solution)/shard_map/mlp/pallas_call | solution.py:174
  95.1 1.6 collective-permute-start.14
  96.6 1.5 collective-permute-done.8.refs_1_
  100.0 3.1 %ring_add.5 = (bf16[256,512]{1,0:T(8,128)(2,1)}, bf16[256,512]{1,0:T(8,128)(2,1)}) custom-call(s32[18]{0:T(128)} %compare_select_fusion.5.table.core_ref._, bf16[256,1024]{1,0:T(8,128)(2,1)} %get-tuple-element.216.refs_0_, bf16[256,1024]{1,0:T(8,128)(2,1)} %copy-done.9, bf16[256,2048]{1,0:T(8,128)(2,1)} %get-tuple-element.218.refs_2_.refs_5_, ...), custom_call_target="tpu_custom_call" | custom-call | flops 1 | bytes 1 | tf_op jit(solution)/shard_map/ring_add/pallas_call | solution.py:650
  103.5 1.7 collective-permute-start.11
  105.2 1.7 halves.2
  107.4 1.5 collective-permute-start.13
  110.0 4.3 %middle.1 = (f32[256,1024]{1,0:T(8,128)}, bf16[256,1024]{1,0:T(8,128)(2,1)}, bf16[512,256]{1,0:T(8,128)(2,1)}, f32[4,1024]{1,0:T(4,128)}) custom-call(f32[256,1024]{1,0:T(8,128)} %get-tuple-element.226.hidden_ref, bf16[256,1024]{1,0:T(8,128)(2,1)} %grad_ref.3, bf16[256,1024]{1,0:T(8,128)(2,1)} %get-tuple-element.229.refs_0_, bf16[256,1024]{1,0:T(8,128)(2,1)} %copy-done.32, ...), custom_call_target="tpu_custom_call" | custom-call | flops 1 | bytes 1 | tf_op jit(solution)/shard_map/middle/pallas_call | solution.py:235
  115.9 3.9 %ring_add.6 = (bf16[256,1024]{1,0:T(8,128)(2,1)}, bf16[256,1024]{1,0:T(8,128)(2,1)}) custom-call(s32[18]{0:T(128)} %compare_select_fusion.5.table.core_ref._, bf16[256,1024]{1,0:T(8,128)(2,1)} %get-tuple-element.216.refs_0_, bf16[256,1024]{1,0:T(8,128)(2,1)} %copy-done.9, bf16[256,2048]{1,0:T(8,128)(2,1)} %get-tuple-element.218.refs_2_.refs_5_, ...), custom_call_target="tpu_custom_call" | custom-call | flops 1 | bytes 1 | tf_op jit(solution)/shard_map/ring_add/pallas_call | solution.py:650
  120.4 4.6 %all-to-all-start.2 = ((bf16[8,64,256]{2,1,0:T(8,128)(2,1)}), bf16[8,64,256]{2,1,0:T(8,128)(2,1)S(1)}, u32[]{:S(2)}, u32[]{:S(2)}) async-start(bf16[8,64,256]{2,1,0:T(8,128)(2,1)} %bitcast.9), calls=%async_computation.2 | async-start | bytes 524288 | tf_op jit(solution)/shard_map/all_to_all | solution.py:435
  125.0 2.0 collective-permute-start.15
  128.5 6.8 %all-to-all-done.2.grad_ref = bf16[8,64,256]{2,1,0:T(8,128)(2,1)S(1)} async-done(((bf16[8,64,256]{2,1,0:T(8,128)(2,1)}), bf16[8,64,256]{2,1,0:T(8,128)(2,1)S(1)}, u32[]{:S(2)}, u32[]{:S(2)}) %all-to-all-start.2) | async-done | bytes 262176 | tf_op jit(solution)/shard_map/all_to_all | solution.py:435
  135.3 6.3 %collective-permute-done.15.refs_4_ = bf16[256,1024]{1,0:T(8,128)(2,1)S(1)} collective-permute-done((bf16[256,1024]{1,0:T(8,128)(2,1)}, bf16[256,1024]{1,0:T(8,128)(2,1)S(1)}, u32[]{:S(2)}, u32[]{:S(2)}) %collective-permute-start.15) | collective-permute-done | bytes 524320 | tf_op jit(solution)/shard_map/ppermute | solution.py:604
  141.6 1.9 collective-permute-done.16.refs_7_
  144.3 3.9 %ring_add.7 = (bf16[256,1024]{1,0:T(8,128)(2,1)}, bf16[256,1024]{1,0:T(8,128)(2,1)}) custom-call(s32[18]{0:T(128)} %compare_select_fusion.5.table.core_ref._, bf16[256,1024]{1,0:T(8,128)(2,1)} %get-tuple-element.216.refs_0_, bf16[256,1024]{1,0:T(8,128)(2,1)} %copy-done.9, bf16[256,2048]{1,0:T(8,128)(2,1)} %get-tuple-element.218.refs_2_.refs_5_, ...), custom_call_target="tpu_custom_call" | custom-call | flops 1 | bytes 1 | tf_op jit(solution)/shard_map/ring_add/pallas_call | solution.py:650
  148.2 2.4 collective-permute-start.19
  150.6 3.0 join.1.refs_0_
  153.6 1.5 collective-permute-start.24
  155.1 4.4 %all-to-all-start.3 = ((bf16[8,32,1024]{2,1,0:T(8,128)(2,1)}), bf16[8,32,1024]{2,1,0:T(8,128)(2,1)}, u32[]{:S(2)}, u32[]{:S(2)}) async-start(bf16[8,32,1024]{2,1,0:T(8,128)(2,1)} %bitcast.10), calls=%async_computation.3 | async-start | bytes 1048576 | tf_op jit(solution)/shard_map/all_to_all | solution.py:435
  159.5 11.9 %attention_backward.2 = (f32[8,64,256]{2,1,0:T(8,128)S(1)}, bf16[8,128,256]{2,1,0:T(8,128)(2,1)S(1)}) custom-call(bf16[8,208,256]{2,1,0:T(8,128)(2,1)S(1)} %copy-done.1, bf16[8,64,256]{2,1,0:T(8,128)(2,1)S(1)} %all-to-all-done.2.grad_ref, f32[8,64,256]{2,1,0:T(8,128)S(1)} %copy-done.4, f32[8,1,256]{2,1,0:T(1,128)S(1)} %copy-done.6, ...), custom_call_target="tpu_custom_call" | custom-call | flops 1 | bytes 1 | tf_op jit(solution)/shard_map/attention_backward/pallas_call | solution.py:397
  171.4 4.0 %ring_add.8 = (bf16[256,1024]{1,0:T(8,128)(2,1)}, bf16[256,1024]{1,0:T(8,128)(2,1)}) custom-call(s32[18]{0:T(128)} %compare_select_fusion.5.table.core_ref._, bf16[256,1024]{1,0:T(8,128)(2,1)} %get-tuple-element.216.refs_0_, bf16[256,1024]{1,0:T(8,128)(2,1)} %copy-done.9, bf16[256,2048]{1,0:T(8,128)(2,1)} %get-tuple-element.218.refs_2_.refs_5_, ...), custom_call_target="tpu_custom_call" | custom-call | flops 1 | bytes 1 | tf_op jit(solution)/shard_map/ring_add/pallas_call | solution.py:650
  175.5 2.0 collective-permute-start.21
  178.0 12.1 %attention_backward.3 = (bf16[8,64,256]{2,1,0:T(8,128)(2,1)S(1)}, f32[8,128,256]{2,1,0:T(8,128)S(1)}) custom-call(bf16[8,208,256]{2,1,0:T(8,128)(2,1)S(1)} %copy-done.1, bf16[8,64,256]{2,1,0:T(8,128)(2,1)S(1)} %all-to-all-done.2.grad_ref, f32[8,64,256]{2,1,0:T(8,128)S(1)} %copy-done.4, f32[8,1,256]{2,1,0:T(1,128)S(1)} %copy-done.6, ...), custom_call_target="tpu_custom_call" | custom-call | flops 1 | bytes 1 | tf_op jit(solution)/shard_map/attention_backward/pallas_call | solution.py:397
  190.1 1.2 add_convert_fusion.1.key_value_ref
  192.3 6.0 %all-to-all-start.4 = ((bf16[8,192,256]{2,1,0:T(8,128)(2,1)}), bf16[8,192,256]{2,1,0:T(8,128)(2,1)}, u32[]{:S(2)}, u32[]{:S(2)}) async-start(bf16[8,192,256]{2,1,0:T(8,128)(2,1)} %pad_maximum_fusion.2), calls=%async_computation.4 | async-start | bytes 1572864 | tf_op jit(solution)/shard_map/all_to_all | solution.py:435
  198.5 1.8 collective-permute-done.24.refs_1_
  200.2 5.0 %head_gradient.1 = bf16[192,1024]{1,0:T(8,128)(2,1)} custom-call(s32[18]{0:T(128)} %compare_select_fusion.5.table.core_ref._, bf16[8,64,256]{2,1,0:T(8,128)(2,1)} %copy-done.5, bf16[8,128,256]{2,1,0:T(8,128)(2,1)} %copy-done.10, bf16[2048,512]{1,0:T(8,128)(2,1)} %join.1.refs_0_, bf16[2048,512]{1,0:T(8,128)(2,1)} %collective-permute-done.24.refs_1_), custom_call_target="tpu_custom_call" | custom-call | flops 1 | bytes 1 | tf_op jit(solution)/shard_map/head_gradient/pallas_call | solution.py:780
  206.3 3.7 %ring_add.9 = bf16[256,1024]{1,0:T(8,128)(2,1)} custom-call(s32[18]{0:T(128)} %compare_select_fusion.5.table.core_ref._, bf16[256,1024]{1,0:T(8,128)(2,1)} %get-tuple-element.216.refs_0_, bf16[256,1024]{1,0:T(8,128)(2,1)} %copy-done.9, bf16[256,2048]{1,0:T(8,128)(2,1)} %get-tuple-element.218.refs_2_.refs_5_, bf16[256,2048]{1,0:T(8,128)(2,1)} %copy-done.7, ...), custom_call_target="tpu_custom_call" | custom-call | flops 1 | bytes 1 | tf_op jit(solution)/shard_map/ring_add/pallas_call | solution.py:650
  210.0 1.2 reduce
  213.0 1.5 collective-permute-start.26
  215.0 4.9 %all-to-all-done.4 = bf16[8,192,256]{2,1,0:T(8,128)(2,1)} async-done(((bf16[8,192,256]{2,1,0:T(8,128)(2,1)}), bf16[8,192,256]{2,1,0:T(8,128)(2,1)}, u32[]{:S(2)}, u32[]{:S(2)}) %all-to-all-start.4) | async-done | bytes 786464 | tf_op jit(solution)/shard_map/all_to_all | solution.py:435
  224.3 2.6 all-to-all-start.5
  227.0 4.5 %place.5 = (f32[2048,1024]{1,0:T(8,128)}, f32[1024,2048]{1,0:T(8,128)}, f32[2,8,32,1024]{3,2,1,0:T(8,128)}, f32[8,2,16,1024]{3,2,1,0:T(8,128)}, f32[1024,512]{1,...) custom-call(s32[18]{0:T(128)} %compare_select_fusion.5.table.core_ref._, bf16[400,1024]{1,0:T(8,128)(2,1)} %copy-done.15, ...), custom_call_target="tpu_custom_call" | custom-call | flops 1 | bytes 1 | tf_op jit(solution)/shard_map/place/pallas_call | solution.py:695
  231.4 2.4 collective-permute-done.26.refs_7_
  233.8 4.0 %collective-permute-done.27.refs_8_ = bf16[400,1024]{1,0:T(8,128)(2,1)} collective-permute-done((bf16[400,1024]{1,0:T(8,128)(2,1)S(1)}, bf16[400,1024]{1,0:T(8,128)(2,1)}, u32[]{:S(2)}, u32[]{:S(2)}) %collective-permute-start.27) | collective-permute-done | bytes 819232 | tf_op jit(solution)/shard_map/ppermute | solution.py:549
  237.8 4.5 %all-to-all-done.5 = bf16[32,32,128]{2,1,0:T(8,128)(2,1)S(1)} async-done(((bf16[32,32,128]{2,1,0:T(8,128)(2,1)}), bf16[32,32,128]{2,1,0:T(8,128)(2,1)S(1)}, u32[]{:S(2)}, u32[]{:S(2)}) %all-to-all-start.5) | async-done | bytes 262176 | tf_op jit(solution)/shard_map/all_to_all | solution.py:949
  243.6 1.2 collective-permute-start.30
  244.8 2.0 collective-permute-start.33
  249.0 6.9 %place.6 = (f32[2048,1024]{1,0:T(8,128)}, f32[1024,2048]{1,0:T(8,128)}, f32[2,8,32,1024]{3,2,1,0:T(8,128)}, f32[8,2,16,1024]{3,2,1,0:T(8,128)}, f32[1024,512]{1,...) custom-call(s32[18]{0:T(128)} %compare_select_fusion.5.table.core_re, ...), custom_call_target="tpu_custom_call", output_to_operand_aliasing={{0}: (1, {}), {1}: (2, {}), {2}: (3, {}), {3}: (4, {}), {4}... | custom-call | flops 1 | bytes 1 | tf_op jit(solution)/shard_map/place/pallas_call | solution.py:695
  255.9 2.9 collective-permute-done.33
  258.8 4.9 %collective-permute-done.29.refs_7_ = bf16[400,1024]{1,0:T(8,128)(2,1)} collective-permute-done((bf16[400,1024]{1,0:T(8,128)(2,1)}, bf16[400,1024]{1,0:T(8,128)(2,1)}, u32[]{:S(2)}, u32[]{:S(2)}) %collective-permute-start.29) | collective-permute-done | bytes 819232 | tf_op jit(solution)/shard_map/ppermute | solution.py:549
  265.4 1.2 collective-permute-start.35
  266.6 1.7 collective-permute-start.38
  268.3 2.2 add_convert_fusion
  270.5 6.9 %place.7 = (f32[2048,1024]{1,0:T(8,128)}, f32[1024,2048]{1,0:T(8,128)}, f32[2,8,32,1024]{3,2,1,0:T(8,128)}, f32[8,2,16,1024]{3,2,1,0:T(8,128)}, f32[1024,512]{1,...) custom-call(s32[18]{0:T(128)} %compare_select_fusion.5.table.core_re, ...), custom_call_target="tpu_custom_call", output_to_operand_aliasing={{0}: (1, {}), {1}: (2, {}), {2}: (3, {}), {3}: (4, {}), {4}... | custom-call | flops 1 | bytes 1 | tf_op jit(solution)/shard_map/place/pallas_call | solution.py:695
  277.4 2.5 collective-permute-done.38
  280.0 5.0 %collective-permute-done.34.left.refs_7_ = bf16[400,1024]{1,0:T(8,128)(2,1)S(1)} collective-permute-done((bf16[400,1024]{1,0:T(8,128)(2,1)}, bf16[400,1024]{1,0:T(8,128)(2,1)S(1)}, u32[]{:S(2)}, u32[]{:S(2)}) %collective-permute-start.34) | collective-permute-done | bytes 819232 | tf_op jit(solution)/shard_map/ppermute | solution.py:549
  286.4 2.0 halves.3
  290.5 1.5 fusion.13
  292.0 2.3 fusion.11
  294.3 6.9 %place.8 = (f32[2048,1024]{1,0:T(8,128)}, f32[1024,2048]{1,0:T(8,128)}, f32[2,8,32,1024]{3,2,1,0:T(8,128)}, f32[8,2,16,1024]{3,2,1,0:T(8,128)}, f32[1024,512]{1,...) custom-call(s32[18]{0:T(128)} %compare_select_fusion.5.table.core_re, ...), custom_call_target="tpu_custom_call", output_to_operand_aliasing={{0}: (1, {}), {1}: (2, {}), {2}: (3, {}), {3}: (4, {}), {4}... | custom-call | flops 1 | bytes 1 | tf_op jit(solution)/shard_map/place/pallas_call | solution.py:695
  301.2 1.2 pad_maximum_fusion.1.refs_7_
  303.3 1.6 collective-permute-done.43.refs_8_
  305.8 5.0 %place.9 = (f32[2048,1024]{1,0:T(8,128)}, f32[1024,2048]{1,0:T(8,128)}, f32[2,8,32,1024]{3,2,1,0:T(8,128)}, f32[8,2,16,1024]{3,2,1,0:T(8,128)}, f32[1024,512]{1,...) custom-call(s32[18]{0:T(128)} %compare_select_fusion.5.table.core_re, ...), custom_call_target="tpu_custom_call", output_to_operand_aliasing={{0}: (1, {}), {1}: (2, {}), {2}: (3, {}), {3}: (4, {}), {4}... | custom-call | flops 1 | bytes 1 | tf_op jit(solution)/shard_map/place/pallas_call | solution.py:695
  310.7 1.3 reduce_sum.109
  (192 shorter events, 36.9 us)
Async XLA Ops:
  7.8 61.0 %copy-start.12 = (bf16[512,1024]{1,0:T(8,128)(2,1)S(1)}, bf16[512,1024]{1,0:T(8,128)(2,1)}, u32[]{:S(2)}) copy-start(bf16[512,1024]{1,0:T(8,128)(2,1)} %refs_3_.1) | copy-start | bytes 3145732
  37.4 2.4 collective-permute-start.2
  37.5 18.6 %collective-permute-start = (bf16[256,512]{1,0:T(8,128)(2,1)}, bf16[256,512]{1,0:T(8,128)(2,1)S(1)}, u32[]{:S(2)}, u32[]{:S(2)}) collective-permute-start(bf16[256,512]{1,0:T(8,128)(2,1)} %get-tuple-element.200.refs_0_), channel_id=1, source_target_pairs={{0,8},{8,16},{16,24},{24,28},{28,20},{20,12},{12,4},{4,0},{1,9},{9... | collective-permute-start | bytes 786440 | tf_op jit(solution)/shard_map/ppermute | solution.py:549
  38.2 17.9 %collective-permute-start.1 = (bf16[256,512]{1,0:T(8,128)(2,1)}, bf16[256,512]{1,0:T(8,128)(2,1)S(1)}, u32[]{:S(2)}, u32[]{:S(2)}) collective-permute-start(bf16[256,512]{1,0:T(8,128)(2,1)} %get-tuple-element.200.refs_0_), channel_id=1, source_target_pairs={{0,4},{8,0},{16,8},{24,16},{28,24},{20,28},{12,20},{4,12},{1,5},{9... | collective-permute-start | bytes 786440 | tf_op jit(solution)/shard_map/ppermute | solution.py:549
  56.1 38.4 %copy-start.33 = (bf16[256,512]{1,0:T(8,128)(2,1)}, bf16[256,512]{1,0:T(8,128)(2,1)S(1)}, u32[]{:S(2)}) copy-start(bf16[256,512]{1,0:T(8,128)(2,1)S(1)} %collective-permute-done.refs_1_) | copy-start | bytes 786436
  56.1 22.3 %copy-start.34 = (bf16[256,512]{1,0:T(8,128)(2,1)}, bf16[256,512]{1,0:T(8,128)(2,1)S(1)}, u32[]{:S(2)}) copy-start(bf16[256,512]{1,0:T(8,128)(2,1)S(1)} %collective-permute-done.1.refs_2_) | copy-start | bytes 786436
  69.3 12.6 %copy-start.19 = (bf16[256,1024]{1,0:T(8,128)(2,1)}, bf16[256,1024]{1,0:T(8,128)(2,1)S(1)}, u32[]{:S(2)}) copy-start(bf16[256,1024]{1,0:T(8,128)(2,1)S(1)} %convolution_convert_fusion.refs_0_) | copy-start | bytes 1572868
  69.4 12.6 %collective-permute-start.7 = (bf16[256,1024]{1,0:T(8,128)(2,1)S(1)}, bf16[256,1024]{1,0:T(8,128)(2,1)S(1)}, u32[]{:S(2)}, u32[]{:S(2)}) collective-permute-start(bf16[256,1024]{1,0:T(8,128)(2,1)S(1)} %convolution_convert_fusion.refs_0_), channel_id=1, source_target_pairs={{0,1},{1,0},{2,3},{3,2},{4,5},{5,4},{6,7},{7,6},{8,9},{9,8},{10,11... | collective-permute-start | bytes 1572872 | tf_op jit(solution)/shard_map/ppermute | solution.py:462
  70.9 6.7 %collective-permute-start.3 = (bf16[256,512]{1,0:T(8,128)(2,1)S(1)}, bf16[256,512]{1,0:T(8,128)(2,1)S(1)}, u32[]{:S(2)}, u32[]{:S(2)}) collective-permute-start(bf16[256,512]{1,0:T(8,128)(2,1)S(1)} %collective-permute-done.refs_1_), channel_id=1, source_target_pairs={{0,8},{8,16},{16,24},{24,28},{28,20},{20,12},{12,4},{4,0},{1,9},{9... | collective-permute-start | bytes 786440 | tf_op jit(solution)/shard_map/ppermute | solution.py:549
  72.0 6.4 %collective-permute-start.4 = (bf16[256,512]{1,0:T(8,128)(2,1)S(1)}, bf16[256,512]{1,0:T(8,128)(2,1)S(1)}, u32[]{:S(2)}, u32[]{:S(2)}) collective-permute-start(bf16[256,512]{1,0:T(8,128)(2,1)S(1)} %collective-permute-done.1.refs_2_), channel_id=1, source_target_pairs={{0,4},{8,0},{16,8},{24,16},{28,24},{20,28},{12,20},{4,12},{1,5},{9... | collective-permute-start | bytes 786440 | tf_op jit(solution)/shard_map/ppermute | solution.py:549
  77.6 16.9 %copy-start.35 = (bf16[256,512]{1,0:T(8,128)(2,1)}, bf16[256,512]{1,0:T(8,128)(2,1)S(1)}, u32[]{:S(2)}) copy-start(bf16[256,512]{1,0:T(8,128)(2,1)S(1)} %collective-permute-done.3.refs_3_) | copy-start | bytes 786436
  78.4 16.1 %copy-start.36 = (bf16[256,512]{1,0:T(8,128)(2,1)}, bf16[256,512]{1,0:T(8,128)(2,1)S(1)}, u32[]{:S(2)}) copy-start(bf16[256,512]{1,0:T(8,128)(2,1)S(1)} %collective-permute-done.4.refs_4_) | copy-start | bytes 786436
  78.4 16.1 %collective-permute-start.5 = (bf16[256,512]{1,0:T(8,128)(2,1)S(1)}, bf16[256,512]{1,0:T(8,128)(2,1)S(1)}, u32[]{:S(2)}, u32[]{:S(2)}) collective-permute-start(bf16[256,512]{1,0:T(8,128)(2,1)S(1)} %collective-permute-done.3.refs_3_), channel_id=1, source_target_pairs={{0,8},{8,16},{16,24},{24,28},{28,20},{20,12},{12,4},{4,0},{1,9},{9... | collective-permute-start | bytes 786440 | tf_op jit(solution)/shard_map/ppermute | solution.py:549
  79.8 14.6 %collective-permute-start.6 = (bf16[256,512]{1,0:T(8,128)(2,1)S(1)}, bf16[256,512]{1,0:T(8,128)(2,1)S(1)}, u32[]{:S(2)}, u32[]{:S(2)}) collective-permute-start(bf16[256,512]{1,0:T(8,128)(2,1)S(1)} %collective-permute-done.4.refs_4_), channel_id=1, source_target_pairs={{0,4},{8,0},{16,8},{24,16},{28,24},{20,28},{12,20},{4,12},{1,5},{9... | collective-permute-start | bytes 786440 | tf_op jit(solution)/shard_map/ppermute | solution.py:549
  94.4 10.7 %copy-start.22 = (bf16[256,512]{1,0:T(8,128)(2,1)}, bf16[256,512]{1,0:T(8,128)(2,1)S(1)}, u32[]{:S(2)}) copy-start(bf16[256,512]{1,0:T(8,128)(2,1)S(1)} %collective-permute-done.5.left.refs_5_) | copy-start | bytes 786436
  94.5 3.7 %collective-permute-start.9 = (bf16[256,2048]{1,0:T(8,128)(2,1)}, bf16[256,2048]{1,0:T(8,128)(2,1)S(1)}, u32[]{:S(2)}, u32[]{:S(2)}) collective-permute-start(bf16[256,2048]{1,0:T(8,128)(2,1)} %get-tuple-element.219), channel_id=1, source_target_pairs={{0,2},{2,0},{1,3},{3,1},{4,6},{6,4},{5,7},{7,5},{8,10},{10,8},{9,1... | collective-permute-start | bytes 3145736 | tf_op jit(solution)/shard_map/ppermute | solution.py:431
  94.6 3.6 %collective-permute-start.8 = (bf16[256,1024]{1,0:T(8,128)(2,1)}, bf16[256,1024]{1,0:T(8,128)(2,1)S(1)}, u32[]{:S(2)}, u32[]{:S(2)}) collective-permute-start(bf16[256,1024]{1,0:T(8,128)(2,1)} %get-tuple-element.217), channel_id=1, source_target_pairs={{0,2},{2,0},{1,3},{3,1},{4,6},{6,4},{5,7},{7,5},{8,10},{10,8},{9,1... | collective-permute-start | bytes 1572872 | tf_op jit(solution)/shard_map/ppermute | solution.py:431
  95.1 14.1 %collective-permute-start.14 = (bf16[256,1024]{1,0:T(8,128)(2,1)}, bf16[256,1024]{1,0:T(8,128)(2,1)S(1)}, u32[]{:S(2)}, u32[]{:S(2)}) collective-permute-start(bf16[256,1024]{1,0:T(8,128)(2,1)} %get-tuple-element.229.refs_0_), channel_id=1, source_target_pairs={{0,1},{1,0},{2,3},{3,2},{4,5},{5,4},{6,7},{7,6},{8,9},{9,8},{10,11... | collective-permute-start | bytes 1572872 | tf_op jit(solution)/shard_map/ppermute | solution.py:462
  103.1 11.9 %collective-permute-start.10 = (bf16[256,512]{1,0:T(8,128)(2,1)}, bf16[256,512]{1,0:T(8,128)(2,1)S(1)}, u32[]{:S(2)}, u32[]{:S(2)}) collective-permute-start(bf16[256,512]{1,0:T(8,128)(2,1)} %get-tuple-element.220), channel_id=1, source_target_pairs={{0,8},{8,16},{16,24},{24,28},{28,20},{20,12},{12,4},{4,0},{1,9},{9... | collective-permute-start | bytes 786440 | tf_op jit(solution)/shard_map/ppermute | solution.py:604
  103.5 11.6 %collective-permute-start.11 = (bf16[256,512]{1,0:T(8,128)(2,1)}, bf16[256,512]{1,0:T(8,128)(2,1)S(1)}, u32[]{:S(2)}, u32[]{:S(2)}) collective-permute-start(bf16[256,512]{1,0:T(8,128)(2,1)} %get-tuple-element.221), channel_id=1, source_target_pairs={{0,4},{8,0},{16,8},{24,16},{28,24},{20,28},{12,20},{4,12},{1,5},{9... | collective-permute-start | bytes 786440 | tf_op jit(solution)/shard_map/ppermute | solution.py:604
  106.8 7.7 %collective-permute-start.12 = (bf16[256,256]{1,0:T(8,128)(2,1)}, bf16[256,256]{1,0:T(8,128)(2,1)S(1)}, u32[]{:S(2)}, u32[]{:S(2)}) collective-permute-start(bf16[256,256]{1,0:T(8,128)(2,1)} %get-tuple-element.224), channel_id=1, source_target_pairs={{0,8},{8,16},{16,24},{24,28},{28,20},{20,12},{12,4},{4,0},{1,9},{9... | collective-permute-start | bytes 393224 | tf_op jit(solution)/shard_map/ppermute | solution.py:549
  107.4 7.6 %collective-permute-start.13 = (bf16[256,256]{1,0:T(8,128)(2,1)}, bf16[256,256]{1,0:T(8,128)(2,1)S(1)}, u32[]{:S(2)}, u32[]{:S(2)}) collective-permute-start(bf16[256,256]{1,0:T(8,128)(2,1)} %get-tuple-element.225), channel_id=1, source_target_pairs={{0,4},{8,0},{16,8},{24,16},{28,24},{20,28},{12,20},{4,12},{1,5},{9... | collective-permute-start | bytes 393224 | tf_op jit(solution)/shard_map/ppermute | solution.py:549
  119.8 7.6 %collective-permute-start.18 = (bf16[256,1024]{1,0:T(8,128)(2,1)S(1)}, bf16[256,1024]{1,0:T(8,128)(2,1)S(1)}, u32[]{:S(2)}, u32[]{:S(2)}) collective-permute-start(bf16[256,1024]{1,0:T(8,128)(2,1)S(1)} %copy-done.31), channel_id=1, source_target_pairs={{0,2},{2,0},{1,3},{3,1},{4,6},{6,4},{5,7},{7,5},{8,10},{10,8},{9,1... | collective-permute-start | bytes 1572872 | tf_op jit(solution)/shard_map/ppermute | solution.py:431
  119.8 7.5 %collective-permute-start.17 = (bf16[256,256]{1,0:T(8,128)(2,1)S(1)}, bf16[256,256]{1,0:T(8,128)(2,1)S(1)}, u32[]{:S(2)}, u32[]{:S(2)}) collective-permute-start(bf16[256,256]{1,0:T(8,128)(2,1)S(1)} %constant_dynamic-slice_fusion.1), channel_id=1, source_target_pairs={{0,2},{2,0},{1,3},{3,1},{4,6},{6,4},{5,7},{7,5},{8,10},{10,8},{9,1... | collective-permute-start | bytes 393224 | tf_op jit(solution)/shard_map/ppermute | solution.py:431
  120.4 14.9 %all-to-all-start.2 = ((bf16[8,64,256]{2,1,0:T(8,128)(2,1)}), bf16[8,64,256]{2,1,0:T(8,128)(2,1)S(1)}, u32[]{:S(2)}, u32[]{:S(2)}) async-start(bf16[8,64,256]{2,1,0:T(8,128)(2,1)} %bitcast.9), calls=%async_computation.2 | async-start | bytes 524288 | tf_op jit(solution)/shard_map/all_to_all | solution.py:435
  125.0 16.6 %collective-permute-start.15 = (bf16[256,1024]{1,0:T(8,128)(2,1)}, bf16[256,1024]{1,0:T(8,128)(2,1)S(1)}, u32[]{:S(2)}, u32[]{:S(2)}) collective-permute-start(bf16[256,1024]{1,0:T(8,128)(2,1)} %get-tuple-element.241), channel_id=1, source_target_pairs={{0,8},{8,16},{16,24},{24,28},{28,20},{20,12},{12,4},{4,0},{1,9},{9... | collective-permute-start | bytes 1572872 | tf_op jit(solution)/shard_map/ppermute | solution.py:604
  127.0 16.5 %collective-permute-start.16 = (bf16[256,1024]{1,0:T(8,128)(2,1)}, bf16[256,1024]{1,0:T(8,128)(2,1)S(1)}, u32[]{:S(2)}, u32[]{:S(2)}) collective-permute-start(bf16[256,1024]{1,0:T(8,128)(2,1)} %get-tuple-element.242), channel_id=1, source_target_pairs={{0,4},{8,0},{16,8},{24,16},{28,24},{20,28},{12,20},{4,12},{1,5},{9... | collective-permute-start | bytes 1572872 | tf_op jit(solution)/shard_map/ppermute | solution.py:604
  148.2 11.2 %copy-start.1 = (bf16[8,208,256]{2,1,0:T(8,128)(2,1)S(1)}, bf16[8,208,256]{2,1,0:T(8,128)(2,1)}, u32[]{:S(2)}) copy-start(bf16[8,208,256]{2,1,0:T(8,128)(2,1)} %copy-done) | copy-start | bytes 2555908
  148.2 11.2 %copy-start.3 = (bf16[8,208,256]{2,1,0:T(8,128)(2,1)S(1)}, bf16[8,208,256]{2,1,0:T(8,128)(2,1)}, u32[]{:S(2)}) copy-start(bf16[8,208,256]{2,1,0:T(8,128)(2,1)} %copy-done.2) | copy-start | bytes 2555908
  148.2 11.2 %copy-start.4 = (f32[8,64,256]{2,1,0:T(8,128)S(1)}, f32[8,64,256]{2,1,0:T(8,128)}, u32[]{:S(2)}) copy-start(f32[8,64,256]{2,1,0:T(8,128)} %get-tuple-element.254.raw_ref) | copy-start | bytes 1572868
  148.2 11.2 %copy-start.6 = (f32[8,1,256]{2,1,0:T(1,128)S(1)}, f32[8,1,256]{2,1,0:T(1,128)}, u32[]{:S(2)}) copy-start(f32[8,1,256]{2,1,0:T(1,128)} %get-tuple-element.255.logsum_ref) | copy-start | bytes 24580
  148.2 23.2 %collective-permute-start.19 = (bf16[256,1024]{1,0:T(8,128)(2,1)}, bf16[256,1024]{1,0:T(8,128)(2,1)}, u32[]{:S(2)}, u32[]{:S(2)}) collective-permute-start(bf16[256,1024]{1,0:T(8,128)(2,1)} %get-tuple-element.251), channel_id=1, source_target_pairs={{0,8},{8,16},{16,24},{24,28},{28,20},{20,12},{12,4},{4,0},{1,9},{9... | collective-permute-start | bytes 1572872 | tf_op jit(solution)/shard_map/ppermute | solution.py:604
  150.6 20.8 %collective-permute-start.20 = (bf16[256,1024]{1,0:T(8,128)(2,1)}, bf16[256,1024]{1,0:T(8,128)(2,1)}, u32[]{:S(2)}, u32[]{:S(2)}) collective-permute-start(bf16[256,1024]{1,0:T(8,128)(2,1)} %get-tuple-element.252), channel_id=1, source_target_pairs={{0,4},{8,0},{16,8},{24,16},{28,24},{20,28},{12,20},{4,12},{1,5},{9... | collective-permute-start | bytes 1572872 | tf_op jit(solution)/shard_map/ppermute | solution.py:604
  153.6 46.7 %collective-permute-start.24 = (bf16[2048,512]{1,0:T(8,128)(2,1)}, bf16[2048,512]{1,0:T(8,128)(2,1)}, u32[]{:S(2)}, u32[]{:S(2)}) collective-permute-start(bf16[2048,512]{1,0:T(8,128)(2,1)} %join.1.refs_0_), channel_id=1, source_target_pairs={{0,1},{1,0},{2,3},{3,2},{4,5},{5,4},{6,7},{7,6},{8,9},{9,8},{10,11... | collective-permute-start | bytes 6291464 | tf_op jit(solution)/shard_map/ppermute | solution.py:462
  155.1 36.3 %all-to-all-start.3 = ((bf16[8,32,1024]{2,1,0:T(8,128)(2,1)}), bf16[8,32,1024]{2,1,0:T(8,128)(2,1)}, u32[]{:S(2)}, u32[]{:S(2)}) async-start(bf16[8,32,1024]{2,1,0:T(8,128)(2,1)} %bitcast.10), calls=%async_computation.3 | async-start | bytes 1048576 | tf_op jit(solution)/shard_map/all_to_all | solution.py:435
  175.5 14.6 %collective-permute-start.21 = (bf16[256,1024]{1,0:T(8,128)(2,1)}, bf16[256,1024]{1,0:T(8,128)(2,1)}, u32[]{:S(2)}, u32[]{:S(2)}) collective-permute-start(bf16[256,1024]{1,0:T(8,128)(2,1)} %get-tuple-element.265), channel_id=1, source_target_pairs={{0,8},{8,16},{16,24},{24,28},{28,20},{20,12},{12,4},{4,0},{1,9},{9... | collective-permute-start | bytes 1572872 | tf_op jit(solution)/shard_map/ppermute | solution.py:604
  177.5 12.6 %collective-permute-start.22 = (bf16[256,1024]{1,0:T(8,128)(2,1)}, bf16[256,1024]{1,0:T(8,128)(2,1)}, u32[]{:S(2)}, u32[]{:S(2)}) collective-permute-start(bf16[256,1024]{1,0:T(8,128)(2,1)} %get-tuple-element.266), channel_id=1, source_target_pairs={{0,4},{8,0},{16,8},{24,16},{28,24},{20,28},{12,20},{4,12},{1,5},{9... | collective-permute-start | bytes 1572872 | tf_op jit(solution)/shard_map/ppermute | solution.py:604
  177.5 12.6 %collective-permute-start.23 = (bf16[8,128,256]{2,1,0:T(8,128)(2,1)S(1)}, bf16[8,128,256]{2,1,0:T(8,128)(2,1)}, u32[]{:S(2)}, u32[]{:S(2)}) collective-permute-start(bf16[8,128,256]{2,1,0:T(8,128)(2,1)S(1)} %get-tuple-element.276), channel_id=1, source_target_pairs={{0,2},{2,0},{1,3},{3,1},{4,6},{6,4},{5,7},{7,5},{8,10},{10,8},{9,1... | collective-permute-start | bytes 1572872 | tf_op jit(solution)/shard_map/ppermute | solution.py:431
  192.3 27.6 %all-to-all-start.4 = ((bf16[8,192,256]{2,1,0:T(8,128)(2,1)}), bf16[8,192,256]{2,1,0:T(8,128)(2,1)}, u32[]{:S(2)}, u32[]{:S(2)}) async-start(bf16[8,192,256]{2,1,0:T(8,128)(2,1)} %pad_maximum_fusion.2), calls=%async_computation.4 | async-start | bytes 1572864 | tf_op jit(solution)/shard_map/all_to_all | solution.py:435
  206.2 5.0 %collective-permute-start.25 = (bf16[96,1024]{1,0:T(8,128)(2,1)S(1)}, bf16[96,1024]{1,0:T(8,128)(2,1)S(1)}, u32[]{:S(2)}, u32[]{:S(2)}) collective-permute-start(bf16[96,1024]{1,0:T(8,128)(2,1)S(1)} %constant_dynamic-slice_fusion), channel_id=1, source_target_pairs={{0,2},{2,0},{1,3},{3,1},{4,6},{6,4},{5,7},{7,5},{8,10},{10,8},{9,1... | collective-permute-start | bytes 589832 | tf_op jit(solution)/shard_map/ppermute | solution.py:431
  210.0 11.1 %copy-start.13 = (bf16[1024,512]{1,0:T(8,128)(2,1)S(1)}, bf16[1024,512]{1,0:T(8,128)(2,1)}, u32[]{:S(2)}) copy-start(bf16[1024,512]{1,0:T(8,128)(2,1)} %refs_0_.1) | copy-start | bytes 3145732
  212.4 14.5 %collective-permute-start.28 = (bf16[400,1024]{1,0:T(8,128)(2,1)S(1)}, bf16[400,1024]{1,0:T(8,128)(2,1)}, u32[]{:S(2)}, u32[]{:S(2)}) collective-permute-start(bf16[400,1024]{1,0:T(8,128)(2,1)S(1)} %pad_maximum_fusion.refs_0_), channel_id=1, source_target_pairs={{0,2},{2,0},{1,3},{3,1},{4,6},{6,4},{5,7},{7,5},{8,10},{10,8},{9,1... | collective-permute-start | bytes 2457608 | tf_op jit(solution)/shard_map/ppermute | solution.py:431
  213.0 20.8 %collective-permute-start.26 = (bf16[400,1024]{1,0:T(8,128)(2,1)S(1)}, bf16[400,1024]{1,0:T(8,128)(2,1)}, u32[]{:S(2)}, u32[]{:S(2)}) collective-permute-start(bf16[400,1024]{1,0:T(8,128)(2,1)S(1)} %pad_maximum_fusion.refs_0_), channel_id=1, source_target_pairs={{0,8},{8,16},{16,24},{24,28},{28,20},{20,12},{12,4},{4,0},{1,9},{9... | collective-permute-start | bytes 2457608 | tf_op jit(solution)/shard_map/ppermute | solution.py:549
  214.5 23.3 %collective-permute-start.27 = (bf16[400,1024]{1,0:T(8,128)(2,1)S(1)}, bf16[400,1024]{1,0:T(8,128)(2,1)}, u32[]{:S(2)}, u32[]{:S(2)}) collective-permute-start(bf16[400,1024]{1,0:T(8,128)(2,1)S(1)} %pad_maximum_fusion.refs_0_), channel_id=1, source_target_pairs={{0,4},{8,0},{16,8},{24,16},{28,24},{20,28},{12,20},{4,12},{1,5},{9... | collective-permute-start | bytes 2457608 | tf_op jit(solution)/shard_map/ppermute | solution.py:549
  224.3 17.9 %all-to-all-start.5 = ((bf16[32,32,128]{2,1,0:T(8,128)(2,1)}), bf16[32,32,128]{2,1,0:T(8,128)(2,1)S(1)}, u32[]{:S(2)}, u32[]{:S(2)}) async-start(bf16[32,32,128]{2,1,0:T(8,128)(2,1)} %broadcast_in_dim.55), calls=%async_computation.5 | async-start | bytes 524288 | tf_op jit(solution)/shard_map/all_to_all | solution.py:949
  242.3 4.7 %collective-permute-start.31 = (bf16[400,1024]{1,0:T(8,128)(2,1)}, bf16[400,1024]{1,0:T(8,128)(2,1)S(1)}, u32[]{:S(2)}, u32[]{:S(2)}) collective-permute-start(bf16[400,1024]{1,0:T(8,128)(2,1)} %collective-permute-done.26.refs_7_), channel_id=1, source_target_pairs={{0,2},{2,0},{1,3},{3,1},{4,6},{6,4},{5,7},{7,5},{8,10},{10,8},{9,1... | collective-permute-start | bytes 2457608 | tf_op jit(solution)/shard_map/ppermute | solution.py:431
  242.6 4.3 %collective-permute-start.32 = (bf16[400,1024]{1,0:T(8,128)(2,1)}, bf16[400,1024]{1,0:T(8,128)(2,1)S(1)}, u32[]{:S(2)}, u32[]{:S(2)}) collective-permute-start(bf16[400,1024]{1,0:T(8,128)(2,1)} %collective-permute-done.27.refs_8_), channel_id=1, source_target_pairs={{0,2},{2,0},{1,3},{3,1},{4,6},{6,4},{5,7},{7,5},{8,10},{10,8},{9,1... | collective-permute-start | bytes 2457608 | tf_op jit(solution)/shard_map/ppermute | solution.py:431
  242.8 20.8 %collective-permute-start.29 = (bf16[400,1024]{1,0:T(8,128)(2,1)}, bf16[400,1024]{1,0:T(8,128)(2,1)}, u32[]{:S(2)}, u32[]{:S(2)}) collective-permute-start(bf16[400,1024]{1,0:T(8,128)(2,1)} %collective-permute-done.26.refs_7_), channel_id=1, source_target_pairs={{0,8},{8,16},{16,24},{24,28},{28,20},{20,12},{12,4},{4,0},{1,9},{9... | collective-permute-start | bytes 2457608 | tf_op jit(solution)/shard_map/ppermute | solution.py:549
  243.6 20.5 %collective-permute-start.30 = (bf16[400,1024]{1,0:T(8,128)(2,1)}, bf16[400,1024]{1,0:T(8,128)(2,1)}, u32[]{:S(2)}, u32[]{:S(2)}) collective-permute-start(bf16[400,1024]{1,0:T(8,128)(2,1)} %collective-permute-done.27.refs_8_), channel_id=1, source_target_pairs={{0,4},{8,0},{16,8},{24,16},{28,24},{20,28},{12,20},{4,12},{1,5},{9... | collective-permute-start | bytes 2457608 | tf_op jit(solution)/shard_map/ppermute | solution.py:549
  244.8 13.9 %collective-permute-start.33 = (bf16[256,1024]{1,0:T(8,128)(2,1)}, bf16[256,1024]{1,0:T(8,128)(2,1)}, u32[]{:S(2)}, u32[]{:S(2)}) collective-permute-start(bf16[256,1024]{1,0:T(8,128)(2,1)} %get-tuple-element.331), channel_id=1, source_target_pairs={{0,1},{1,0},{2,3},{3,2},{4,5},{5,4},{6,7},{7,6},{8,9},{9,8},{10,11... | collective-permute-start | bytes 1572872 | tf_op jit(solution)/shard_map/ppermute | solution.py:462
  246.9 21.4 %copy-start.11 = (f32[256,1024]{1,0:T(8,128)S(1)}, f32[256,1024]{1,0:T(8,128)}, u32[]{:S(2)}) copy-start(f32[256,1024]{1,0:T(8,128)} %get-tuple-element.226.hidden_ref) | copy-start | bytes 3145732
  246.9 21.4 %copy-start.42 = (f32[1024]{0:T(1024)S(1)}, f32[1024]{0:T(1024)}, u32[]{:S(2)}) copy-start(f32[1024]{0:T(1024)} %param.35) | copy-start | bytes 12292
  264.1 6.5 %collective-permute-start.36 = (bf16[400,1024]{1,0:T(8,128)(2,1)}, bf16[400,1024]{1,0:T(8,128)(2,1)}, u32[]{:S(2)}, u32[]{:S(2)}) collective-permute-start(bf16[400,1024]{1,0:T(8,128)(2,1)} %collective-permute-done.29.refs_7_), channel_id=1, source_target_pairs={{0,2},{2,0},{1,3},{3,1},{4,6},{6,4},{5,7},{7,5},{8,10},{10,8},{9,1... | collective-permute-start | bytes 2457608 | tf_op jit(solution)/shard_map/ppermute | solution.py:431
  264.1 6.5 %collective-permute-start.37 = (bf16[400,1024]{1,0:T(8,128)(2,1)}, bf16[400,1024]{1,0:T(8,128)(2,1)}, u32[]{:S(2)}, u32[]{:S(2)}) collective-permute-start(bf16[400,1024]{1,0:T(8,128)(2,1)} %collective-permute-done.30.refs_8_), channel_id=1, source_target_pairs={{0,2},{2,0},{1,3},{3,1},{4,6},{6,4},{5,7},{7,5},{8,10},{10,8},{9,1... | collective-permute-start | bytes 2457608 | tf_op jit(solution)/shard_map/ppermute | solution.py:431
  264.6 20.4 %collective-permute-start.34 = (bf16[400,1024]{1,0:T(8,128)(2,1)}, bf16[400,1024]{1,0:T(8,128)(2,1)S(1)}, u32[]{:S(2)}, u32[]{:S(2)}) collective-permute-start(bf16[400,1024]{1,0:T(8,128)(2,1)} %collective-permute-done.29.refs_7_), channel_id=1, source_target_pairs={{0,8},{8,16},{16,24},{24,28},{28,20},{20,12},{12,4},{4,0},{1,9},{9... | collective-permute-start | bytes 2457608 | tf_op jit(solution)/shard_map/ppermute | solution.py:549
  265.4 20.1 %collective-permute-start.35 = (bf16[400,1024]{1,0:T(8,128)(2,1)}, bf16[400,1024]{1,0:T(8,128)(2,1)S(1)}, u32[]{:S(2)}, u32[]{:S(2)}) collective-permute-start(bf16[400,1024]{1,0:T(8,128)(2,1)} %collective-permute-done.30.refs_8_), channel_id=1, source_target_pairs={{0,4},{8,0},{16,8},{24,16},{28,24},{20,28},{12,20},{4,12},{1,5},{9... | collective-permute-start | bytes 2457608 | tf_op jit(solution)/shard_map/ppermute | solution.py:549
  266.6 13.4 %collective-permute-start.38 = (bf16[256,1024]{1,0:T(8,128)(2,1)S(1)}, bf16[256,1024]{1,0:T(8,128)(2,1)}, u32[]{:S(2)}, u32[]{:S(2)}) collective-permute-start(bf16[256,1024]{1,0:T(8,128)(2,1)S(1)} %get-tuple-element.358), channel_id=1, source_target_pairs={{0,1},{1,0},{2,3},{3,2},{4,5},{5,4},{6,7},{7,6},{8,9},{9,8},{10,11... | collective-permute-start | bytes 1572872 | tf_op jit(solution)/shard_map/ppermute | solution.py:462
  270.5 20.0 %copy-start.39 = (f32[1024]{0:T(1024)S(1)}, f32[1024]{0:T(1024)}, u32[]{:S(2)}) copy-start(f32[1024]{0:T(1024)} %param.22) | copy-start | bytes 12292
  277.4 14.6 %copy-start.21 = (f32[256,1024]{1,0:T(8,128)S(1)}, f32[256,1024]{1,0:T(8,128)}, u32[]{:S(2)}) copy-start(f32[256,1024]{1,0:T(8,128)} %get-tuple-element.357) | copy-start | bytes 3145732
  285.5 8.8 %collective-permute-start.41 = (bf16[400,1024]{1,0:T(8,128)(2,1)S(1)}, bf16[400,1024]{1,0:T(8,128)(2,1)}, u32[]{:S(2)}, u32[]{:S(2)}) collective-permute-start(bf16[400,1024]{1,0:T(8,128)(2,1)S(1)} %collective-permute-done.34.left.refs_7_), channel_id=1, source_target_pairs={{0,2},{2,0},{1,3},{3,1},{4,6},{6,4},{5,7},{7,5},{8,10},{10,8},{9,1... | collective-permute-start | bytes 2457608 | tf_op jit(solution)/shard_map/ppermute | solution.py:431
  285.5 8.8 %collective-permute-start.42 = (bf16[400,1024]{1,0:T(8,128)(2,1)S(1)}, bf16[400,1024]{1,0:T(8,128)(2,1)}, u32[]{:S(2)}, u32[]{:S(2)}) collective-permute-start(bf16[400,1024]{1,0:T(8,128)(2,1)S(1)} %collective-permute-done.35.right.refs_8_), channel_id=1, source_target_pairs={{0,2},{2,0},{1,3},{3,1},{4,6},{6,4},{5,7},{7,5},{8,10},{10,8},{9,1... | collective-permute-start | bytes 2457608 | tf_op jit(solution)/shard_map/ppermute | solution.py:431
  288.5 12.8 %collective-permute-start.39 = (bf16[400,512]{1,0:T(8,128)(2,1)}, bf16[400,512]{1,0:T(8,128)(2,1)}, u32[]{:S(2)}, u32[]{:S(2)}) collective-permute-start(bf16[400,512]{1,0:T(8,128)(2,1)} %get-tuple-element.341), channel_id=1, source_target_pairs={{0,8},{8,16},{16,24},{24,28},{28,20},{20,12},{12,4},{4,0},{1,9},{9... | collective-permute-start | bytes 1228808 | tf_op jit(solution)/shard_map/ppermute | solution.py:549
  289.6 11.7 %collective-permute-start.40 = (bf16[400,512]{1,0:T(8,128)(2,1)}, bf16[400,512]{1,0:T(8,128)(2,1)}, u32[]{:S(2)}, u32[]{:S(2)}) collective-permute-start(bf16[400,512]{1,0:T(8,128)(2,1)} %get-tuple-element.342), channel_id=1, source_target_pairs={{0,4},{8,0},{16,8},{24,16},{28,24},{20,28},{12,20},{4,12},{1,5},{9... | collective-permute-start | bytes 1228808 | tf_op jit(solution)/shard_map/ppermute | solution.py:549
  302.5 2.4 collective-permute-start.43
  (29 other events, 102.5 us)

commit v16 on v15

--- a/solution.py
+++ b/solution.py
@@ -490,21 +490,36 @@
     return values
 
 
-def join_kernel(*refs):
-    start = 0
-    for block in refs[:-1]:
-        refs[-1][pl.ds(start, block.shape[0]), :] = block[...]
-        start += block.shape[0]
+def pieces_of(block):
+    return list(block) if isinstance(block, tuple) else [block]
+
+
+def whole_block(block):
+    return jnp.concatenate(pieces_of(block), axis=1)
+
+
+def join_kernel(counts, *refs):
+    output, refs, start = refs[-1], list(refs[:-1]), 0
+    for count in counts:
+        column = 0
+        for _ in range(count):
+            piece = refs.pop(0)
+            rows, columns = piece.shape
+            output[pl.ds(start, rows), pl.ds(column, columns)] = piece[...]
+            column += columns
+        start += rows
 
 
 def join(blocks):
-    rows = sum(block.shape[0] for block in blocks)
+    blocks = [pieces_of(block) for block in blocks]
+    rows = sum(block[0].shape[0] for block in blocks)
+    columns = sum(piece.shape[1] for piece in blocks[0])
     return pl.pallas_call(
-        join_kernel,
-        out_shape=struct((rows, blocks[0].shape[1]), blocks[0].dtype),
+        functools.partial(join_kernel, [len(block) for block in blocks]),
+        out_shape=struct((rows, columns), blocks[0][0].dtype),
         compiler_params=streaming,
         name="join",
-    )(*blocks)
+    )(*[piece for block in blocks for piece in block])
 
 
 def halves_kernel(left, right, left_ref, right_ref):
@@ -536,6 +551,8 @@
         self.ready = [block]
 
     def send(self, ready):
+        if len(self.new) < len(ready):
+            ready = [tuple(ready)]
         new = list(zip(self.new, ready))
         self.blocks += new
         self.new = new
@@ -550,7 +567,7 @@
                 for block, direction in zip(sides, (1, -1))
             ]
         if self.swap and ready:
-            pairs = [(step, block, swap_cores(block)) for step, block in new]
+            pairs = [(step, block, jax.tree.map(swap_cores, block)) for step, block in new]
             self.pairs += pairs
             self.outputs = self.take(self.outputs, pairs)
         self.state = (flying, self.outputs)
@@ -558,8 +575,8 @@
     def advance(self, state):
         arrived, self.outputs = state
         self.new = [-self.count, self.count]
-        if arrived and self.count == self.reach:
-            arrived, self.new = [jnp.concatenate(arrived, axis=1)], [self.count]
+        if self.count == self.reach:
+            self.new = [self.count]
         self.ready = arrived
 
     def busy(self):
@@ -671,7 +688,7 @@
             is_down = self.table[2 * chips] == 0
             for step, near, far in pairs:
                 start = self.table[step % chips] * units
-                near, far = near[:units], far[:units]
+                near, far = whole_block(near)[:units], whole_block(far)[:units]
                 first = jnp.where(is_down, near, far).astype(F32)
                 second = jnp.where(is_down, far, near).astype(F32).T
                 down = lax.dynamic_update_slice_in_dim(down, first, start, 0)
@@ -679,7 +696,8 @@
             return [down, up]
         first = pairs[0][0] % chips
         stride = pairs[-1][0] % chips - first
-        block = pl.BlockSpec(pairs[0][1].shape, lambda at, table: (0, 0))
+        blocks = [pieces_of(pair[1]) + pieces_of(pair[2]) for pair in pairs]
+        flat = [piece for block in blocks for piece in block]
 
         def place(at, table):
             return table[first + at * stride]
@@ -693,13 +711,13 @@
         columns = [column] * (3 if outputs else 0)
         heads = [[first, first + stride][at] + chips for at in range(len(pairs))]
         return pl.pallas_call(
-            functools.partial(place_kernel, heads, (units, size, extra)),
+            functools.partial(place_kernel, heads, len(blocks[0]) // 2, (units, size, extra)),
             grid_spec=pltpu.PrefetchScalarGridSpec(
                 num_scalar_prefetch=1,
                 grid=(len(pairs),),
                 in_specs=[pl.BlockSpec(memory_space=pl.ANY)] * (len(outputs) - len(columns))
                 + columns
-                + [block] * (2 * len(pairs)),
+                + [pl.BlockSpec(piece.shape, lambda at, table: (0, 0)) for piece in flat],
                 out_specs=[
                     pl.BlockSpec((units, model), lambda at, table: (place(at, table), 0)),
                     pl.BlockSpec((model, units), lambda at, table: (0, place(at, table))),
@@ -720,25 +738,28 @@
             compiler_params=streaming,
             cost_estimate=light,
             name="place",
-        )(self.table, *outputs, *[pair[1] for pair in pairs], *[pair[2] for pair in pairs])
-
-
-def place_kernel(heads, sizes, table, *refs):
+        )(self.table, *outputs, *flat)
+
+
+def place_kernel(heads, width, sizes, table, *refs):
     count = len(heads)
     refs, (down, up, weight, small), projections = refs[:-7], refs[-7:-3], refs[-3:]
-    blocks, refs = refs[-2 * count :], refs[: -2 * count]
+    blocks, refs = refs[-2 * width * count :], refs[: -2 * width * count]
     core = table[table.shape[0] - 2]
     units, size, extra = sizes
     rows = [pl.ds(0, units), pl.ds(units, size), pl.ds(units + size, extra)]
     rows.append(pl.ds(units + size + extra, small_rows))
 
+    def read(block, which):
+        return jnp.concatenate([piece[rows[which], :] for piece in block], axis=1)
+
     def put(first, second, head):
-        down[...] = first[rows[0], :].astype(F32)
-        up[...] = second[rows[0], :].astype(F32).T
+        down[...] = read(first, 0).astype(F32)
+        up[...] = read(second, 0).astype(F32).T
         for side, block in ((0, first), (1, second)):
-            weight[side, 0] = block[rows[2], :].astype(F32)
-            small[0, side] = block[rows[3], :].astype(F32)
-        both = jnp.concatenate([first[rows[1], :], second[rows[1], :]], axis=0)
+            weight[side, 0] = read(block, 2).astype(F32)
+            small[0, side] = read(block, 3).astype(F32)
+        both = jnp.concatenate([read(first, 1), read(second, 1)], axis=0)
         for at, output in enumerate(projections):
             part = both[at * HD : at * HD + HD].astype(F32)
             part = jnp.concatenate([part, part], axis=0).T
@@ -748,7 +769,10 @@
             output[...] = part
 
     for at in range(count):
-        near, far, head = blocks[at], blocks[count + at], table[heads[at]]
+        near, far = (
+            blocks[(2 * at + side) * width : (2 * at + side + 1) * width] for side in range(2)
+        )
+        head = table[heads[at]]
         here = pl.program_id(0) == at
         pl.when(here & (core == 0))(functools.partial(put, near, far, head))
         pl.when(here & (core != 0))(functools.partial(put, far, near, head))
@@ -877,15 +901,14 @@
     while inputs.busy():
         visit([inputs], ())
     mlp_out = across_heads(mlp_part)
-    steps, inputs = zip(*inputs.blocks)
-    parts = [join(inputs)]
-    if cut != model:
-        parts = across_heads(parts[0])
     out_near, out_far = share_halves(attn_out, 0)
     doutput = product(out_near, d_branch) + product(out_far, swap_cores(d_branch))
     doutput = doutput.astype(BF16).reshape(chips, -1, model)
-    grads, doutput = visit([ring], (grads, doutput))
     doutput = to_heads(doutput)
+    steps, inputs = zip(*inputs.blocks)
+    inputs = join(inputs)
+    parts = across_heads(inputs) if cut != model else [inputs]
+    grads, doutput, _ = visit([ring], (grads, doutput, inputs))
     *dquery, far_sums = backward_piece(
         queries, grads, raw, logsum, [], other, [], 0, 1, crops, (F32, BF16)
     )
@@ -943,24 +966,35 @@
             jnp.sum(lead[:, None] * d_part, axis=0),
         ]
     )
-    ends = jnp.pad(ends.reshape(-1, 128), ((0, -ends.size // 128 % 16), (0, 0))).astype(BF16)
-    everyone = ("chip", "core", "head")
-    ends = jnp.broadcast_to(ends, (lax.axis_size(everyone),) + ends.shape)
-    ends = lax.all_to_all(ends, everyone, 0, 0, tiled=True)
-    ends = visit([gathered], ends)
-    ends = jnp.sum(ends.astype(F32), axis=0).reshape(-1)[: 3 * model].reshape(3, model)
+    ends = ends.reshape(-1, 128)
+    ends = functools.reduce(jnp.add, across_heads(ends))
+    ends = ends + swap_cores(ends)
+    moves = [chips >> (at + 1) for at in range(chips.bit_length() - 1)][::-1]
+
+    def step_ends(ends):
+        if not moves:
+            return [ends]
+        reach = moves.pop(0)
+        pairs = [(chip, chip ^ reach) for chip in range(chips)]
+        return [ends, lax.ppermute(ends, "chip", pairs)]
+
+    ends = step_ends(visit([gathered], ends))
     ends, mlp_out = visit([gathered], (ends, mlp_out))
+    ends = step_ends(functools.reduce(jnp.add, ends))
     block_output = hidden + down_bias
     for part in mlp_out:
         block_output += part.astype(F32)
     block_output = block_output.astype(BF16)
-    d_in, block_output = visit([gathered], (d_in, block_output))
+    d_in, block_output, ends = visit([gathered], (d_in, block_output, ends))
+    ends = step_ends(functools.reduce(jnp.add, ends))
     d_in = functools.reduce(jnp.add, (part.astype(F32) for part in d_in))
     input_grad = (d_hidden + normalize_back(d_in * gain_attn, unit_attn, inverse_attn)).astype(
         BF16
     )
-    while gathered.busy():
-        input_grad = visit([gathered], input_grad)
+    while gathered.busy() or moves:
+        input_grad, ends = visit([gathered], (input_grad, ends))
+        ends = step_ends(functools.reduce(jnp.add, ends))
+    ends = functools.reduce(jnp.add, ends).reshape(3, model)
     ddown_weight, dup_weight, *rest = gathered.outputs
     if split == 1:
         doutput_weight, small, *projections = rest
@@ -968,9 +1002,9 @@
     if split != 1:
         blocks = jnp.zeros((2, chips) + blocks.shape, F32)
         for step, near, far in gathered.pairs:
-            for side, block in ((core, near[start:]), (1 - core, far[start:])):
+            for side, block in ((core, near), (1 - core, far)):
                 at = (side, table[chips + step % chips], 0, 0)
-                block = block[None, None].astype(F32)
+                block = whole_block(block)[None, None, start:].astype(F32)
                 blocks = lax.dynamic_update_slice(blocks, block, at)
         doutput_weight = blocks[:, :, :-small_rows].reshape(width, model)
         small = blocks[:, :, -small_rows:]

time: 315 us -> 322 us (1.022)
  waiting for transfers between devices: 60.4 us -> 67.8 us
  starting transfers between devices: 53.9 us -> 58.1 us
    ppermute x0 -> x3, waiting for transfers between devices: none -> 10.5 us  [step_ends(): return [ends, lax.ppermute(ends, 'chip', pairs)]]
    ppermute x5 -> x6, waiting for transfers between devices: 9.06 us -> 15 us  [across_heads(): return [part, lax.ppermute(part, 'head', [(0, 1), (1, 0)])]]
    ppermute x0 -> x3, starting transfers between devices: none -> 4.82 us  [step_ends(): return [ends, lax.ppermute(ends, 'chip', pairs)]]
    all_to_all x1 -> x0, waiting for transfers between devices: 4.45 us -> none  [local(): ends = lax.all_to_all(ends, everyone, 0, 0, tiled=True)]
    all_to_all x3, waiting for transfers between devices: 11.7 us -> 8.12 us  [to_heads(): return lax.all_to_all(blocks, 'chip', 0, 0, tiled=True)]
    ppermute x5 -> x6, starting transfers between devices: 8.34 us -> 8.75 us  [across_heads(): return [part, lax.ppermute(part, 'head', [(0, 1), (1, 0)])]]
    unnamed x93 -> x103, local copies, waits for them, and re-layouts: 9.92 us -> 9.95 us
  transfers between devices with their start and end apart: 48 -> 53, of which waited for: 23 -> 23; matrix products, arithmetic and copies ran while one was open for 6% -> 5% of each run, Pallas kernels for 33% -> 32%
where the time goes in v16:
time: 322 us; the launch traced here: 321 us
  Pallas kernels  123 us (38%)
  waiting for transfers between devices  67.8 us (21%)
  starting transfers between devices  58.1 us (18%)
  blocking collectives  42.4 us (13%)
  local copies, waits for them, and re-layouts  13.3 us (4%)
  other arithmetic  12 us (4%)
  matrix products  3.52 us (1%)
    all_to_all x2, blocking collectives, to_heads(): return lax.all_to_all(blocks, 'chip', 0, 0, tiled=True)  42.4 us
    ppermute x24, waiting for transfers between devices, send(): lax.ppermute(block, 'chip', ring_pairs(direction))  30.8 us
    pallas_call x5, Pallas kernels, place(): pl.pallas_call(functools.partial(place_kernel, heads, len(blocks[0]) // 2...  30.2 us
    ppermute x24, starting transfers between devices, send(): lax.ppermute(block, 'chip', ring_pairs(direction))  27.9 us
    pallas_call x2, Pallas kernels, backward_piece(): pl.pallas_call(functools.partial(backward_kernel, crops, len(before)), gr...  24 us
    pallas_call x5, Pallas kernels, add(): pl.pallas_call(functools.partial(add_kernel, starts, len(shapes)), grid_s...  18.6 us
    pallas_call x1, Pallas kernels, attention_forward(): pl.pallas_call(functools.partial(forward_kernel, crops, key_step(count)),...  15.3 us
    ppermute x6, waiting for transfers between devices, across_heads(): return [part, lax.ppermute(part, 'head', [(0, 1), (1, 0)])]  15 us
  transfers between devices with their start and end apart: 53, of which 23 were waited for; matrix products, arithmetic and copies ran while one was open for 5% of the time, Pallas kernels for 32%

profile of v16, /device:TPU:0, one launch (start us, length us, event | category | flops | bytes accessed | tf_op | source)
XLA Modules:
  0.0 321.0 jit_solution(7549019322818897285)
XLA Ops:
  1.2 6.6 %project.1 = (bf16[8,208,256]{2,1,0:T(8,128)(2,1)}, bf16[256,1024]{1,0:T(8,128)(2,1)}, bf16[256,512]{1,0:T(8,128)(2,1)}) custom-call(s32[18]{0:T(128)} %compare_select_fusion.5.table.core_ref._, bf16[256,1024]{1,0:T(8,128)(2,1)} %input_ref.3, s32[1,256]{1,0:T(1,128)} %bitcast.73, s32[32]{0:T(128)} %steps_ref.1, f32[1,1024]{1,0:T(1,128)} %bitcast.56, ...), custom_call_target="tpu_custom_call" | custom-call | flops 1 | bytes 1 | tf_op jit(solution)/shard_map/project/pallas_call | solution.py:94
  7.8 29.6 %all_to_all.25.query_ref.own.refs_1_ = bf16[8,208,256]{2,1,0:T(8,128)(2,1)S(1)} all-to-all(bf16[8,208,256]{2,1,0:T(8,128)(2,1)} %get-tuple-element.210), channel_id=1, replica_groups=mesh['chip'=8,'core'=2,'head'=2] {'chip'}, dimensions={0} | all-to-all | bytes 1703936 | tf_op jit(solution)/shard_map/all_to_all | solution.py:435
  38.2 1.3 collective-permute-start.1
  40.7 15.3 %attention_forward.1 = (f32[8,64,256]{2,1,0:T(8,128)}, bf16[8,64,256]{2,1,0:T(8,128)(2,1)}, f32[8,1,256]{2,1,0:T(1,128)}) custom-call(bf16[8,208,256]{2,1,0:T(8,128)(2,1)} %copy-done, bf16[8,208,256]{2,1,0:T(8,128)(2,1)} %copy-done, bf16[8,208,256]{2,1,0:T(8,128)(2,1)} %copy-done.2), custom_call_target="tpu_custom_call" | custom-call | flops 1 | bytes 1 | tf_op jit(solution)/shard_map/attention_forward/pallas_call | solution.py:367
  56.1 12.8 %all_to_all.26 = bf16[8,64,256]{2,1,0:T(8,128)(2,1)S(1)} all-to-all(bf16[8,64,256]{2,1,0:T(8,128)(2,1)} %get-tuple-element.217), channel_id=1, replica_groups=mesh['chip'=8,'core'=2,'head'=2] {'chip'}, dimensions={0} | all-to-all | bytes 524288 | tf_op jit(solution)/shard_map/all_to_all | solution.py:435
  69.4 1.6 collective-permute-start.7
  72.9 4.6 %collective-permute-done.3.refs_3_ = bf16[256,512]{1,0:T(8,128)(2,1)S(1)} collective-permute-done((bf16[256,512]{1,0:T(8,128)(2,1)S(1)}, bf16[256,512]{1,0:T(8,128)(2,1)S(1)}, u32[]{:S(2)}, u32[]{:S(2)}) %collective-permute-start.3) | collective-permute-done | bytes 262176 | tf_op jit(solution)/shard_map/ppermute | solution.py:566
  78.4 1.4 collective-permute-start.5
  80.4 1.5 collective-permute-done.7.refs_1_
  82.7 11.7 %mlp.1 = (bf16[256,2048]{1,0:T(8,128)(2,1)}, bf16[256,2048]{1,0:T(8,128)(2,1)}, bf16[256,1024]{1,0:T(8,128)(2,1)}, bf16[256,1024]{1,0:T(8,128)(2,1)}, f32[256,10...) custom-call(s32[18]{0:T(128)} %compare_select_fusion.5.table.core_ref._, ...), custom_call_target="tpu_custom_call" | custom-call | flops 1 | bytes 1 | tf_op jit(solution)/shard_map/mlp/pallas_call | solution.py:174
  95.1 1.6 collective-permute-start.14
  96.6 1.5 collective-permute-done.8.refs_1_
  99.9 3.1 ring_add.5
  103.4 1.7 collective-permute-start.11
  105.1 1.7 halves.2
  107.3 1.5 collective-permute-start.13
  110.0 4.3 %middle.1 = (f32[256,1024]{1,0:T(8,128)}, bf16[256,1024]{1,0:T(8,128)(2,1)}, bf16[512,256]{1,0:T(8,128)(2,1)}, f32[4,1024]{1,0:T(4,128)}) custom-call(f32[256,1024]{1,0:T(8,128)} %get-tuple-element.238.hidden_ref, bf16[256,1024]{1,0:T(8,128)(2,1)} %grad_ref.3, bf16[256,1024]{1,0:T(8,128)(2,1)} %get-tuple-element.241.refs_0_, bf16[256,1024]{1,0:T(8,128)(2,1)} %copy-done.33, ...), custom_call_target="tpu_custom_call" | custom-call | flops 1 | bytes 1 | tf_op jit(solution)/shard_map/middle/pallas_call | solution.py:235
  115.9 3.8 %ring_add.6 = (bf16[256,1024]{1,0:T(8,128)(2,1)}, bf16[256,1024]{1,0:T(8,128)(2,1)}) custom-call(s32[18]{0:T(128)} %compare_select_fusion.5.table.core_ref._, bf16[256,1024]{1,0:T(8,128)(2,1)} %get-tuple-element.228.refs_0_, bf16[256,1024]{1,0:T(8,128)(2,1)} %copy-done.9, bf16[256,2048]{1,0:T(8,128)(2,1)} %get-tuple-element.230.refs_2_.refs_5_, ...), custom_call_target="tpu_custom_call" | custom-call | flops 1 | bytes 1 | tf_op jit(solution)/shard_map/ring_add/pallas_call | solution.py:667
  120.3 4.6 %all-to-all-start.2 = ((bf16[8,64,256]{2,1,0:T(8,128)(2,1)}), bf16[8,64,256]{2,1,0:T(8,128)(2,1)S(1)}, u32[]{:S(2)}, u32[]{:S(2)}) async-start(bf16[8,64,256]{2,1,0:T(8,128)(2,1)} %bitcast.9), calls=%async_computation.2 | async-start | bytes 524288 | tf_op jit(solution)/shard_map/all_to_all | solution.py:435
  126.3 7.7 %all-to-all-done.2.grad_ref = bf16[8,64,256]{2,1,0:T(8,128)(2,1)S(1)} async-done(((bf16[8,64,256]{2,1,0:T(8,128)(2,1)}), bf16[8,64,256]{2,1,0:T(8,128)(2,1)S(1)}, u32[]{:S(2)}, u32[]{:S(2)}) %all-to-all-start.2) | async-done | bytes 262176 | tf_op jit(solution)/shard_map/all_to_all | solution.py:435
  134.0 3.6 %all-to-all-start.3 = ((bf16[8,32,1024]{2,1,0:T(8,128)(2,1)}), bf16[8,32,1024]{2,1,0:T(8,128)(2,1)S(1)}, u32[]{:S(2)}, u32[]{:S(2)}) async-start(bf16[8,32,1024]{2,1,0:T(8,128)(2,1)} %bitcast.10), calls=%async_computation.3 | async-start | bytes 1048576 | tf_op jit(solution)/shard_map/all_to_all | solution.py:435
  137.6 2.0 collective-permute-start.15
  139.7 3.0 join.1.refs_0_
  142.6 14.6 %collective-permute-done.15.refs_4_ = bf16[256,1024]{1,0:T(8,128)(2,1)S(1)} collective-permute-done((bf16[256,1024]{1,0:T(8,128)(2,1)}, bf16[256,1024]{1,0:T(8,128)(2,1)S(1)}, u32[]{:S(2)}, u32[]{:S(2)}) %collective-permute-start.15) | collective-permute-done | bytes 524320 | tf_op jit(solution)/shard_map/ppermute | solution.py:621
  157.3 2.2 collective-permute-done.16.refs_7_
  159.5 3.9 %ring_add.7 = (bf16[256,1024]{1,0:T(8,128)(2,1)}, bf16[256,1024]{1,0:T(8,128)(2,1)}) custom-call(s32[18]{0:T(128)} %compare_select_fusion.5.table.core_ref._, bf16[256,1024]{1,0:T(8,128)(2,1)} %get-tuple-element.228.refs_0_, bf16[256,1024]{1,0:T(8,128)(2,1)} %copy-done.9, bf16[256,2048]{1,0:T(8,128)(2,1)} %get-tuple-element.230.refs_2_.refs_5_, ...), custom_call_target="tpu_custom_call" | custom-call | flops 1 | bytes 1 | tf_op jit(solution)/shard_map/ring_add/pallas_call | solution.py:667
  163.4 4.3 %collective-permute-start.19 = (bf16[256,1024]{1,0:T(8,128)(2,1)}, bf16[256,1024]{1,0:T(8,128)(2,1)S(1)}, u32[]{:S(2)}, u32[]{:S(2)}) collective-permute-start(bf16[256,1024]{1,0:T(8,128)(2,1)} %get-tuple-element.265), channel_id=1, source_target_pairs={{0,8},{8,16},{16,24},{24,28},{28,20},{20,12},{12,4},{4,0},{1,9},{9... | collective-permute-start | bytes 1572872 | tf_op jit(solution)/shard_map/ppermute | solution.py:621
  167.6 1.5 collective-permute-start.24
  169.1 11.9 %attention_backward.2 = (f32[8,64,256]{2,1,0:T(8,128)S(1)}, bf16[8,128,256]{2,1,0:T(8,128)(2,1)S(1)}) custom-call(bf16[8,208,256]{2,1,0:T(8,128)(2,1)S(1)} %copy-done.1, bf16[8,64,256]{2,1,0:T(8,128)(2,1)S(1)} %all-to-all-done.2.grad_ref, f32[8,64,256]{2,1,0:T(8,128)S(1)} %copy-done.4, f32[8,1,256]{2,1,0:T(1,128)S(1)} %copy-done.6, ...), custom_call_target="tpu_custom_call" | custom-call | flops 1 | bytes 1 | tf_op jit(solution)/shard_map/attention_backward/pallas_call | solution.py:397
  182.1 4.1 %ring_add.8 = (bf16[256,1024]{1,0:T(8,128)(2,1)}, bf16[256,1024]{1,0:T(8,128)(2,1)}) custom-call(s32[18]{0:T(128)} %compare_select_fusion.5.table.core_ref._, bf16[256,1024]{1,0:T(8,128)(2,1)} %get-tuple-element.228.refs_0_, bf16[256,1024]{1,0:T(8,128)(2,1)} %copy-done.9, bf16[256,2048]{1,0:T(8,128)(2,1)} %get-tuple-element.230.refs_2_.refs_5_, ...), custom_call_target="tpu_custom_call" | custom-call | flops 1 | bytes 1 | tf_op jit(solution)/shard_map/ring_add/pallas_call | solution.py:667
  186.1 2.0 collective-permute-start.21
  188.9 12.1 %attention_backward.3 = (bf16[8,64,256]{2,1,0:T(8,128)(2,1)S(1)}, f32[8,128,256]{2,1,0:T(8,128)S(1)}) custom-call(bf16[8,208,256]{2,1,0:T(8,128)(2,1)S(1)} %copy-done.1, bf16[8,64,256]{2,1,0:T(8,128)(2,1)S(1)} %all-to-all-done.2.grad_ref, f32[8,64,256]{2,1,0:T(8,128)S(1)} %copy-done.4, f32[8,1,256]{2,1,0:T(1,128)S(1)} %copy-done.6, ...), custom_call_target="tpu_custom_call" | custom-call | flops 1 | bytes 1 | tf_op jit(solution)/shard_map/attention_backward/pallas_call | solution.py:397
  201.0 1.2 add_convert_fusion.1.key_value_ref
  203.3 4.5 %all-to-all-start.4 = ((bf16[8,192,256]{2,1,0:T(8,128)(2,1)}), bf16[8,192,256]{2,1,0:T(8,128)(2,1)}, u32[]{:S(2)}, u32[]{:S(2)}) async-start(bf16[8,192,256]{2,1,0:T(8,128)(2,1)} %pad_maximum_fusion.1), calls=%async_computation.4 | async-start | bytes 1572864 | tf_op jit(solution)/shard_map/all_to_all | solution.py:435
  208.0 5.6 %collective-permute-done.24.refs_1_ = bf16[2048,512]{1,0:T(8,128)(2,1)} collective-permute-done((bf16[2048,512]{1,0:T(8,128)(2,1)}, bf16[2048,512]{1,0:T(8,128)(2,1)}, u32[]{:S(2)}, u32[]{:S(2)}) %collective-permute-start.24) | collective-permute-done | bytes 2097184 | tf_op jit(solution)/shard_map/ppermute | solution.py:462
  213.5 5.0 %head_gradient.1 = bf16[192,1024]{1,0:T(8,128)(2,1)} custom-call(s32[18]{0:T(128)} %compare_select_fusion.5.table.core_ref._, bf16[8,64,256]{2,1,0:T(8,128)(2,1)} %copy-done.5, bf16[8,128,256]{2,1,0:T(8,128)(2,1)} %copy-done.10, bf16[2048,512]{1,0:T(8,128)(2,1)} %join.1.refs_0_, bf16[2048,512]{1,0:T(8,128)(2,1)} %collective-permute-done.24.refs_1_), custom_call_target="tpu_custom_call" | custom-call | flops 1 | bytes 1 | tf_op jit(solution)/shard_map/head_gradient/pallas_call | solution.py:804
  219.7 3.7 %ring_add.9 = bf16[256,1024]{1,0:T(8,128)(2,1)} custom-call(s32[18]{0:T(128)} %compare_select_fusion.5.table.core_ref._, bf16[256,1024]{1,0:T(8,128)(2,1)} %get-tuple-element.228.refs_0_, bf16[256,1024]{1,0:T(8,128)(2,1)} %copy-done.9, bf16[256,2048]{1,0:T(8,128)(2,1)} %get-tuple-element.230.refs_2_.refs_5_, bf16[256,2048]{1,0:T(8,128)(2,1)} %copy-done.7, ...), custom_call_target="tpu_custom_call" | custom-call | flops 1 | bytes 1 | tf_op jit(solution)/shard_map/ring_add/pallas_call | solution.py:667
  223.5 1.2 pad_maximum_fusion.refs_0_
  225.3 1.8 collective-permute-start.26
  228.7 1.2 fusion.21
  233.5 2.6 collective-permute-done.29
  236.1 4.5 %place.5 = (f32[2048,1024]{1,0:T(8,128)}, f32[1024,2048]{1,0:T(8,128)}, f32[2,8,32,1024]{3,2,1,0:T(8,128)}, f32[8,2,16,1024]{3,2,1,0:T(8,128)}, f32[1024,512]{1,...) custom-call(s32[18]{0:T(128)} %compare_select_fusion.5.table.core_ref._, bf16[400,1024]{1,0:T(8,128)(2,1)} %copy-done.15, ...), custom_call_target="tpu_custom_call" | custom-call | flops 1 | bytes 1 | tf_op jit(solution)/shard_map/place/pallas_call | solution.py:713
  240.6 6.2 %collective-permute-done.26.refs_7_ = bf16[400,1024]{1,0:T(8,128)(2,1)} collective-permute-done((bf16[400,1024]{1,0:T(8,128)(2,1)S(1)}, bf16[400,1024]{1,0:T(8,128)(2,1)}, u32[]{:S(2)}, u32[]{:S(2)}) %collective-permute-start.26) | collective-permute-done | bytes 819232 | tf_op jit(solution)/shard_map/ppermute | solution.py:566
  247.7 1.7 collective-permute-start.31
  249.7 1.5 collective-permute-start.36
  251.2 1.5 collective-permute-start.35
  253.6 6.9 %place.6 = (f32[2048,1024]{1,0:T(8,128)}, f32[1024,2048]{1,0:T(8,128)}, f32[2,8,32,1024]{3,2,1,0:T(8,128)}, f32[8,2,16,1024]{3,2,1,0:T(8,128)}, f32[1024,512]{1,...) custom-call(s32[18]{0:T(128)} %compare_select_fusion.5.table.core_re, ...), custom_call_target="tpu_custom_call", output_to_operand_aliasing={{0}: (1, {}), {1}: (2, {}), {2}: (3, {}), {3}: (4, {}), {4}... | custom-call | flops 1 | bytes 1 | tf_op jit(solution)/shard_map/place/pallas_call | solution.py:713
  260.5 2.9 collective-permute-done.36
  263.4 5.0 %collective-permute-done.35 = f32[24,128]{1,0:T(8,128)S(1)} collective-permute-done((f32[24,128]{1,0:T(8,128)S(1)}, f32[24,128]{1,0:T(8,128)S(1)}, u32[]{:S(2)}, u32[]{:S(2)}) %collective-permute-start.35) | collective-permute-done | bytes 12320 | tf_op jit(solution)/shard_map/ppermute | solution.py:979
  268.4 1.3 collective-permute-done.32.refs_9_
  270.7 1.5 collective-permute-start.38
  272.2 1.5 collective-permute-start.41
  274.2 2.2 add_convert_fusion
  276.5 7.0 %place.7 = (f32[2048,1024]{1,0:T(8,128)}, f32[1024,2048]{1,0:T(8,128)}, f32[2,8,32,1024]{3,2,1,0:T(8,128)}, f32[8,2,16,1024]{3,2,1,0:T(8,128)}, f32[1024,512]{1,...) custom-call(s32[18]{0:T(128)} %compare_select_fusion.5.table.core_re, ...), custom_call_target="tpu_custom_call", output_to_operand_aliasing={{0}: (1, {}), {1}: (2, {}), {2}: (3, {}), {3}: (4, {}), {4}... | custom-call | flops 1 | bytes 1 | tf_op jit(solution)/shard_map/place/pallas_call | solution.py:713
  283.5 2.1 collective-permute-done.41
  285.6 5.5 %collective-permute-done.42 = f32[24,128]{1,0:T(8,128)S(1)} collective-permute-done((f32[24,128]{1,0:T(8,128)S(1)}, f32[24,128]{1,0:T(8,128)S(1)}, u32[]{:S(2)}, u32[]{:S(2)}) %collective-permute-start.42) | collective-permute-done | bytes 12320 | tf_op jit(solution)/shard_map/ppermute | solution.py:979
  292.2 2.2 halves.3
  294.4 2.8 collective-permute-start.47
  297.7 1.5 collective-permute-start.44
  299.2 1.5 fusion.13
  300.7 2.3 fusion.11
  303.0 6.9 %place.8 = (f32[2048,1024]{1,0:T(8,128)}, f32[1024,2048]{1,0:T(8,128)}, f32[2,8,32,1024]{3,2,1,0:T(8,128)}, f32[8,2,16,1024]{3,2,1,0:T(8,128)}, f32[1024,512]{1,...) custom-call(s32[18]{0:T(128)} %compare_select_fusion.5.table.core_re, ...), custom_call_target="tpu_custom_call", output_to_operand_aliasing={{0}: (1, {}), {1}: (2, {}), {2}: (3, {}), {3}: (4, {}), {4}... | custom-call | flops 1 | bytes 1 | tf_op jit(solution)/shard_map/place/pallas_call | solution.py:713
  313.5 5.0 %place.9 = (f32[2048,1024]{1,0:T(8,128)}, f32[1024,2048]{1,0:T(8,128)}, f32[2,8,32,1024]{3,2,1,0:T(8,128)}, f32[8,2,16,1024]{3,2,1,0:T(8,128)}, f32[1024,512]{1,...) custom-call(s32[18]{0:T(128)} %compare_select_fusion.5.table.core_re, ...), custom_call_target="tpu_custom_call", output_to_operand_aliasing={{0}: (1, {}), {1}: (2, {}), {2}: (3, {}), {3}: (4, {}), {4}... | custom-call | flops 1 | bytes 1 | tf_op jit(solution)/shard_map/place/pallas_call | solution.py:713
  318.5 1.3 reduce_sum.99
  (207 shorter events, 35.0 us)
Async XLA Ops:
  7.8 61.0 %copy-start.12 = (bf16[512,1024]{1,0:T(8,128)(2,1)S(1)}, bf16[512,1024]{1,0:T(8,128)(2,1)}, u32[]{:S(2)}) copy-start(bf16[512,1024]{1,0:T(8,128)(2,1)} %refs_3_.1) | copy-start | bytes 3145732
  37.4 2.4 collective-permute-start.2
  37.5 18.6 %collective-permute-start = (bf16[256,512]{1,0:T(8,128)(2,1)}, bf16[256,512]{1,0:T(8,128)(2,1)S(1)}, u32[]{:S(2)}, u32[]{:S(2)}) collective-permute-start(bf16[256,512]{1,0:T(8,128)(2,1)} %get-tuple-element.212.refs_0_), channel_id=1, source_target_pairs={{0,8},{8,16},{16,24},{24,28},{28,20},{20,12},{12,4},{4,0},{1,9},{9... | collective-permute-start | bytes 786440 | tf_op jit(solution)/shard_map/ppermute | solution.py:566
  38.2 17.9 %collective-permute-start.1 = (bf16[256,512]{1,0:T(8,128)(2,1)}, bf16[256,512]{1,0:T(8,128)(2,1)S(1)}, u32[]{:S(2)}, u32[]{:S(2)}) collective-permute-start(bf16[256,512]{1,0:T(8,128)(2,1)} %get-tuple-element.212.refs_0_), channel_id=1, source_target_pairs={{0,4},{8,0},{16,8},{24,16},{28,24},{20,28},{12,20},{4,12},{1,5},{9... | collective-permute-start | bytes 786440 | tf_op jit(solution)/shard_map/ppermute | solution.py:566
  56.1 38.4 %copy-start.36 = (bf16[256,512]{1,0:T(8,128)(2,1)}, bf16[256,512]{1,0:T(8,128)(2,1)S(1)}, u32[]{:S(2)}) copy-start(bf16[256,512]{1,0:T(8,128)(2,1)S(1)} %collective-permute-done.refs_1_) | copy-start | bytes 786436
  56.1 38.4 %copy-start.37 = (bf16[256,512]{1,0:T(8,128)(2,1)}, bf16[256,512]{1,0:T(8,128)(2,1)S(1)}, u32[]{:S(2)}) copy-start(bf16[256,512]{1,0:T(8,128)(2,1)S(1)} %collective-permute-done.1.refs_2_) | copy-start | bytes 786436
  69.4 12.6 %collective-permute-start.7 = (bf16[256,1024]{1,0:T(8,128)(2,1)S(1)}, bf16[256,1024]{1,0:T(8,128)(2,1)S(1)}, u32[]{:S(2)}, u32[]{:S(2)}) collective-permute-start(bf16[256,1024]{1,0:T(8,128)(2,1)S(1)} %convolution_convert_fusion.refs_0_), channel_id=1, source_target_pairs={{0,1},{1,0},{2,3},{3,2},{4,5},{5,4},{6,7},{7,6},{8,9},{9,8},{10,11... | collective-permute-start | bytes 1572872 | tf_op jit(solution)/shard_map/ppermute | solution.py:462
  70.9 6.7 %collective-permute-start.3 = (bf16[256,512]{1,0:T(8,128)(2,1)S(1)}, bf16[256,512]{1,0:T(8,128)(2,1)S(1)}, u32[]{:S(2)}, u32[]{:S(2)}) collective-permute-start(bf16[256,512]{1,0:T(8,128)(2,1)S(1)} %collective-permute-done.refs_1_), channel_id=1, source_target_pairs={{0,8},{8,16},{16,24},{24,28},{28,20},{20,12},{12,4},{4,0},{1,9},{9... | collective-permute-start | bytes 786440 | tf_op jit(solution)/shard_map/ppermute | solution.py:566
  72.0 6.4 %collective-permute-start.4 = (bf16[256,512]{1,0:T(8,128)(2,1)S(1)}, bf16[256,512]{1,0:T(8,128)(2,1)S(1)}, u32[]{:S(2)}, u32[]{:S(2)}) collective-permute-start(bf16[256,512]{1,0:T(8,128)(2,1)S(1)} %collective-permute-done.1.refs_2_), channel_id=1, source_target_pairs={{0,4},{8,0},{16,8},{24,16},{28,24},{20,28},{12,20},{4,12},{1,5},{9... | collective-permute-start | bytes 786440 | tf_op jit(solution)/shard_map/ppermute | solution.py:566
  77.6 25.5 %copy-start.38 = (bf16[256,512]{1,0:T(8,128)(2,1)}, bf16[256,512]{1,0:T(8,128)(2,1)S(1)}, u32[]{:S(2)}) copy-start(bf16[256,512]{1,0:T(8,128)(2,1)S(1)} %collective-permute-done.3.refs_3_) | copy-start | bytes 786436
  78.4 16.1 %collective-permute-start.5 = (bf16[256,512]{1,0:T(8,128)(2,1)S(1)}, bf16[256,512]{1,0:T(8,128)(2,1)S(1)}, u32[]{:S(2)}, u32[]{:S(2)}) collective-permute-start(bf16[256,512]{1,0:T(8,128)(2,1)S(1)} %collective-permute-done.3.refs_3_), channel_id=1, source_target_pairs={{0,8},{8,16},{16,24},{24,28},{28,20},{20,12},{12,4},{4,0},{1,9},{9... | collective-permute-start | bytes 786440 | tf_op jit(solution)/shard_map/ppermute | solution.py:566
  79.8 14.7 %collective-permute-start.6 = (bf16[256,512]{1,0:T(8,128)(2,1)S(1)}, bf16[256,512]{1,0:T(8,128)(2,1)S(1)}, u32[]{:S(2)}, u32[]{:S(2)}) collective-permute-start(bf16[256,512]{1,0:T(8,128)(2,1)S(1)} %collective-permute-done.4.refs_4_), channel_id=1, source_target_pairs={{0,4},{8,0},{16,8},{24,16},{28,24},{20,28},{12,20},{4,12},{1,5},{9... | collective-permute-start | bytes 786440 | tf_op jit(solution)/shard_map/ppermute | solution.py:566
  94.5 3.7 %collective-permute-start.9 = (bf16[256,2048]{1,0:T(8,128)(2,1)}, bf16[256,2048]{1,0:T(8,128)(2,1)S(1)}, u32[]{:S(2)}, u32[]{:S(2)}) collective-permute-start(bf16[256,2048]{1,0:T(8,128)(2,1)} %get-tuple-element.231), channel_id=1, source_target_pairs={{0,2},{2,0},{1,3},{3,1},{4,6},{6,4},{5,7},{7,5},{8,10},{10,8},{9,1... | collective-permute-start | bytes 3145736 | tf_op jit(solution)/shard_map/ppermute | solution.py:431
  94.6 3.6 %collective-permute-start.8 = (bf16[256,1024]{1,0:T(8,128)(2,1)}, bf16[256,1024]{1,0:T(8,128)(2,1)S(1)}, u32[]{:S(2)}, u32[]{:S(2)}) collective-permute-start(bf16[256,1024]{1,0:T(8,128)(2,1)} %get-tuple-element.229), channel_id=1, source_target_pairs={{0,2},{2,0},{1,3},{3,1},{4,6},{6,4},{5,7},{7,5},{8,10},{10,8},{9,1... | collective-permute-start | bytes 1572872 | tf_op jit(solution)/shard_map/ppermute | solution.py:431
  95.1 14.1 %collective-permute-start.14 = (bf16[256,1024]{1,0:T(8,128)(2,1)}, bf16[256,1024]{1,0:T(8,128)(2,1)S(1)}, u32[]{:S(2)}, u32[]{:S(2)}) collective-permute-start(bf16[256,1024]{1,0:T(8,128)(2,1)} %get-tuple-element.241.refs_0_), channel_id=1, source_target_pairs={{0,1},{1,0},{2,3},{3,2},{4,5},{5,4},{6,7},{7,6},{8,9},{9,8},{10,11... | collective-permute-start | bytes 1572872 | tf_op jit(solution)/shard_map/ppermute | solution.py:462
  103.1 11.9 %collective-permute-start.10 = (bf16[256,512]{1,0:T(8,128)(2,1)}, bf16[256,512]{1,0:T(8,128)(2,1)S(1)}, u32[]{:S(2)}, u32[]{:S(2)}) collective-permute-start(bf16[256,512]{1,0:T(8,128)(2,1)} %get-tuple-element.232), channel_id=1, source_target_pairs={{0,8},{8,16},{16,24},{24,28},{28,20},{20,12},{12,4},{4,0},{1,9},{9... | collective-permute-start | bytes 786440 | tf_op jit(solution)/shard_map/ppermute | solution.py:621
  103.4 11.6 %collective-permute-start.11 = (bf16[256,512]{1,0:T(8,128)(2,1)}, bf16[256,512]{1,0:T(8,128)(2,1)S(1)}, u32[]{:S(2)}, u32[]{:S(2)}) collective-permute-start(bf16[256,512]{1,0:T(8,128)(2,1)} %get-tuple-element.233), channel_id=1, source_target_pairs={{0,4},{8,0},{16,8},{24,16},{28,24},{20,28},{12,20},{4,12},{1,5},{9... | collective-permute-start | bytes 786440 | tf_op jit(solution)/shard_map/ppermute | solution.py:621
  106.8 7.6 %collective-permute-start.12 = (bf16[256,256]{1,0:T(8,128)(2,1)}, bf16[256,256]{1,0:T(8,128)(2,1)S(1)}, u32[]{:S(2)}, u32[]{:S(2)}) collective-permute-start(bf16[256,256]{1,0:T(8,128)(2,1)} %get-tuple-element.236), channel_id=1, source_target_pairs={{0,8},{8,16},{16,24},{24,28},{28,20},{20,12},{12,4},{4,0},{1,9},{9... | collective-permute-start | bytes 393224 | tf_op jit(solution)/shard_map/ppermute | solution.py:566
  107.3 7.6 %collective-permute-start.13 = (bf16[256,256]{1,0:T(8,128)(2,1)}, bf16[256,256]{1,0:T(8,128)(2,1)S(1)}, u32[]{:S(2)}, u32[]{:S(2)}) collective-permute-start(bf16[256,256]{1,0:T(8,128)(2,1)} %get-tuple-element.237), channel_id=1, source_target_pairs={{0,4},{8,0},{16,8},{24,16},{28,24},{20,28},{12,20},{4,12},{1,5},{9... | collective-permute-start | bytes 393224 | tf_op jit(solution)/shard_map/ppermute | solution.py:566
  114.4 25.2 %copy-start.42 = (bf16[256,256]{1,0:T(8,128)(2,1)}, bf16[256,256]{1,0:T(8,128)(2,1)S(1)}, u32[]{:S(2)}) copy-start(bf16[256,256]{1,0:T(8,128)(2,1)S(1)} %collective-permute-done.12.refs_7_) | copy-start | bytes 393220
  119.7 5.5 %collective-permute-start.18 = (bf16[256,1024]{1,0:T(8,128)(2,1)S(1)}, bf16[256,1024]{1,0:T(8,128)(2,1)S(1)}, u32[]{:S(2)}, u32[]{:S(2)}) collective-permute-start(bf16[256,1024]{1,0:T(8,128)(2,1)S(1)} %copy-done.32), channel_id=1, source_target_pairs={{0,2},{2,0},{1,3},{3,1},{4,6},{6,4},{5,7},{7,5},{8,10},{10,8},{9,1... | collective-permute-start | bytes 1572872 | tf_op jit(solution)/shard_map/ppermute | solution.py:431
  119.7 5.5 %collective-permute-start.17 = (bf16[256,256]{1,0:T(8,128)(2,1)S(1)}, bf16[256,256]{1,0:T(8,128)(2,1)S(1)}, u32[]{:S(2)}, u32[]{:S(2)}) collective-permute-start(bf16[256,256]{1,0:T(8,128)(2,1)S(1)} %constant_dynamic-slice_fusion.1), channel_id=1, source_target_pairs={{0,2},{2,0},{1,3},{3,1},{4,6},{6,4},{5,7},{7,5},{8,10},{10,8},{9,1... | collective-permute-start | bytes 393224 | tf_op jit(solution)/shard_map/ppermute | solution.py:431
  120.3 13.7 %all-to-all-start.2 = ((bf16[8,64,256]{2,1,0:T(8,128)(2,1)}), bf16[8,64,256]{2,1,0:T(8,128)(2,1)S(1)}, u32[]{:S(2)}, u32[]{:S(2)}) async-start(bf16[8,64,256]{2,1,0:T(8,128)(2,1)} %bitcast.9), calls=%async_computation.2 | async-start | bytes 524288 | tf_op jit(solution)/shard_map/all_to_all | solution.py:435
  134.0 25.4 %all-to-all-start.3 = ((bf16[8,32,1024]{2,1,0:T(8,128)(2,1)}), bf16[8,32,1024]{2,1,0:T(8,128)(2,1)S(1)}, u32[]{:S(2)}, u32[]{:S(2)}) async-start(bf16[8,32,1024]{2,1,0:T(8,128)(2,1)} %bitcast.10), calls=%async_computation.3 | async-start | bytes 1048576 | tf_op jit(solution)/shard_map/all_to_all | solution.py:435
  137.6 19.7 %collective-permute-start.15 = (bf16[256,1024]{1,0:T(8,128)(2,1)}, bf16[256,1024]{1,0:T(8,128)(2,1)S(1)}, u32[]{:S(2)}, u32[]{:S(2)}) collective-permute-start(bf16[256,1024]{1,0:T(8,128)(2,1)} %get-tuple-element.253), channel_id=1, source_target_pairs={{0,8},{8,16},{16,24},{24,28},{28,20},{20,12},{12,4},{4,0},{1,9},{9... | collective-permute-start | bytes 1572872 | tf_op jit(solution)/shard_map/ppermute | solution.py:621
  139.6 19.8 %collective-permute-start.16 = (bf16[256,1024]{1,0:T(8,128)(2,1)}, bf16[256,1024]{1,0:T(8,128)(2,1)}, u32[]{:S(2)}, u32[]{:S(2)}) collective-permute-start(bf16[256,1024]{1,0:T(8,128)(2,1)} %get-tuple-element.254), channel_id=1, source_target_pairs={{0,4},{8,0},{16,8},{24,16},{28,24},{20,28},{12,20},{4,12},{1,5},{9... | collective-permute-start | bytes 1572872 | tf_op jit(solution)/shard_map/ppermute | solution.py:621
  142.6 26.5 %copy-start.1 = (bf16[8,208,256]{2,1,0:T(8,128)(2,1)S(1)}, bf16[8,208,256]{2,1,0:T(8,128)(2,1)}, u32[]{:S(2)}) copy-start(bf16[8,208,256]{2,1,0:T(8,128)(2,1)} %copy-done) | copy-start | bytes 2555908
  142.6 26.5 %copy-start.3 = (bf16[8,208,256]{2,1,0:T(8,128)(2,1)S(1)}, bf16[8,208,256]{2,1,0:T(8,128)(2,1)}, u32[]{:S(2)}) copy-start(bf16[8,208,256]{2,1,0:T(8,128)(2,1)} %copy-done.2) | copy-start | bytes 2555908
  142.6 26.5 %copy-start.4 = (f32[8,64,256]{2,1,0:T(8,128)S(1)}, f32[8,64,256]{2,1,0:T(8,128)}, u32[]{:S(2)}) copy-start(f32[8,64,256]{2,1,0:T(8,128)} %get-tuple-element.268.raw_ref) | copy-start | bytes 1572868
  142.6 26.5 %copy-start.6 = (f32[8,1,256]{2,1,0:T(1,128)S(1)}, f32[8,1,256]{2,1,0:T(1,128)}, u32[]{:S(2)}) copy-start(f32[8,1,256]{2,1,0:T(1,128)} %get-tuple-element.269.logsum_ref) | copy-start | bytes 24580
  163.4 17.7 %collective-permute-start.19 = (bf16[256,1024]{1,0:T(8,128)(2,1)}, bf16[256,1024]{1,0:T(8,128)(2,1)S(1)}, u32[]{:S(2)}, u32[]{:S(2)}) collective-permute-start(bf16[256,1024]{1,0:T(8,128)(2,1)} %get-tuple-element.265), channel_id=1, source_target_pairs={{0,8},{8,16},{16,24},{24,28},{28,20},{20,12},{12,4},{4,0},{1,9},{9... | collective-permute-start | bytes 1572872 | tf_op jit(solution)/shard_map/ppermute | solution.py:621
  167.6 13.5 %collective-permute-start.20 = (bf16[256,1024]{1,0:T(8,128)(2,1)}, bf16[256,1024]{1,0:T(8,128)(2,1)S(1)}, u32[]{:S(2)}, u32[]{:S(2)}) collective-permute-start(bf16[256,1024]{1,0:T(8,128)(2,1)} %get-tuple-element.266), channel_id=1, source_target_pairs={{0,4},{8,0},{16,8},{24,16},{28,24},{20,28},{12,20},{4,12},{1,5},{9... | collective-permute-start | bytes 1572872 | tf_op jit(solution)/shard_map/ppermute | solution.py:621
  167.6 45.9 %collective-permute-start.24 = (bf16[2048,512]{1,0:T(8,128)(2,1)}, bf16[2048,512]{1,0:T(8,128)(2,1)}, u32[]{:S(2)}, u32[]{:S(2)}) collective-permute-start(bf16[2048,512]{1,0:T(8,128)(2,1)} %join.1.refs_0_), channel_id=1, source_target_pairs={{0,1},{1,0},{2,3},{3,2},{4,5},{5,4},{6,7},{7,6},{8,9},{9,8},{10,11... | collective-permute-start | bytes 6291464 | tf_op jit(solution)/shard_map/ppermute | solution.py:462
  186.1 14.9 %collective-permute-start.21 = (bf16[256,1024]{1,0:T(8,128)(2,1)}, bf16[256,1024]{1,0:T(8,128)(2,1)}, u32[]{:S(2)}, u32[]{:S(2)}) collective-permute-start(bf16[256,1024]{1,0:T(8,128)(2,1)} %get-tuple-element.279), channel_id=1, source_target_pairs={{0,8},{8,16},{16,24},{24,28},{28,20},{20,12},{12,4},{4,0},{1,9},{9... | collective-permute-start | bytes 1572872 | tf_op jit(solution)/shard_map/ppermute | solution.py:621
  188.1 12.9 %collective-permute-start.22 = (bf16[256,1024]{1,0:T(8,128)(2,1)}, bf16[256,1024]{1,0:T(8,128)(2,1)}, u32[]{:S(2)}, u32[]{:S(2)}) collective-permute-start(bf16[256,1024]{1,0:T(8,128)(2,1)} %get-tuple-element.280), channel_id=1, source_target_pairs={{0,4},{8,0},{16,8},{24,16},{28,24},{20,28},{12,20},{4,12},{1,5},{9... | collective-permute-start | bytes 1572872 | tf_op jit(solution)/shard_map/ppermute | solution.py:621
  188.5 12.6 %collective-permute-start.23 = (bf16[8,128,256]{2,1,0:T(8,128)(2,1)S(1)}, bf16[8,128,256]{2,1,0:T(8,128)(2,1)}, u32[]{:S(2)}, u32[]{:S(2)}) collective-permute-start(bf16[8,128,256]{2,1,0:T(8,128)(2,1)S(1)} %get-tuple-element.290), channel_id=1, source_target_pairs={{0,2},{2,0},{1,3},{3,1},{4,6},{6,4},{5,7},{7,5},{8,10},{10,8},{9,1... | collective-permute-start | bytes 1572872 | tf_op jit(solution)/shard_map/ppermute | solution.py:431
  203.3 25.4 %all-to-all-start.4 = ((bf16[8,192,256]{2,1,0:T(8,128)(2,1)}), bf16[8,192,256]{2,1,0:T(8,128)(2,1)}, u32[]{:S(2)}, u32[]{:S(2)}) async-start(bf16[8,192,256]{2,1,0:T(8,128)(2,1)} %pad_maximum_fusion.1), calls=%async_computation.4 | async-start | bytes 1572864 | tf_op jit(solution)/shard_map/all_to_all | solution.py:435
  219.5 3.9 %collective-permute-start.25 = (bf16[96,1024]{1,0:T(8,128)(2,1)S(1)}, bf16[96,1024]{1,0:T(8,128)(2,1)S(1)}, u32[]{:S(2)}, u32[]{:S(2)}) collective-permute-start(bf16[96,1024]{1,0:T(8,128)(2,1)S(1)} %constant_dynamic-slice_fusion), channel_id=1, source_target_pairs={{0,2},{2,0},{1,3},{3,1},{4,6},{6,4},{5,7},{7,5},{8,10},{10,8},{9,1... | collective-permute-start | bytes 589832 | tf_op jit(solution)/shard_map/ppermute | solution.py:431
  224.7 11.4 %collective-permute-start.28 = (bf16[400,1024]{1,0:T(8,128)(2,1)S(1)}, bf16[400,1024]{1,0:T(8,128)(2,1)}, u32[]{:S(2)}, u32[]{:S(2)}) collective-permute-start(bf16[400,1024]{1,0:T(8,128)(2,1)S(1)} %pad_maximum_fusion.refs_0_), channel_id=1, source_target_pairs={{0,2},{2,0},{1,3},{3,1},{4,6},{6,4},{5,7},{7,5},{8,10},{10,8},{9,1... | collective-permute-start | bytes 2457608 | tf_op jit(solution)/shard_map/ppermute | solution.py:431
  225.3 21.6 %collective-permute-start.26 = (bf16[400,1024]{1,0:T(8,128)(2,1)S(1)}, bf16[400,1024]{1,0:T(8,128)(2,1)}, u32[]{:S(2)}, u32[]{:S(2)}) collective-permute-start(bf16[400,1024]{1,0:T(8,128)(2,1)S(1)} %pad_maximum_fusion.refs_0_), channel_id=1, source_target_pairs={{0,8},{8,16},{16,24},{24,28},{28,20},{20,12},{12,4},{4,0},{1,9},{9... | collective-permute-start | bytes 2457608 | tf_op jit(solution)/shard_map/ppermute | solution.py:566
  227.1 20.0 %collective-permute-start.27 = (bf16[400,1024]{1,0:T(8,128)(2,1)S(1)}, bf16[400,1024]{1,0:T(8,128)(2,1)}, u32[]{:S(2)}, u32[]{:S(2)}) collective-permute-start(bf16[400,1024]{1,0:T(8,128)(2,1)S(1)} %pad_maximum_fusion.refs_0_), channel_id=1, source_target_pairs={{0,4},{8,0},{16,8},{24,16},{28,24},{20,28},{12,20},{4,12},{1,5},{9... | collective-permute-start | bytes 2457608 | tf_op jit(solution)/shard_map/ppermute | solution.py:566
  232.4 3.8 %collective-permute-start.29 = (f32[24,128]{1,0:T(8,128)S(1)}, f32[24,128]{1,0:T(8,128)S(1)}, u32[]{:S(2)}, u32[]{:S(2)}) collective-permute-start(f32[24,128]{1,0:T(8,128)S(1)} %reshape.108), channel_id=1, source_target_pairs={{0,1},{1,0},{2,3},{3,2},{4,5},{5,4},{6,7},{7,6},{8,9},{9,8},{10,11... | collective-permute-start | bytes 36872 | tf_op jit(solution)/shard_map/ppermute | solution.py:462
  236.1 4.5 %collective-permute-start.30 = (f32[24,128]{1,0:T(8,128)S(1)}, f32[24,128]{1,0:T(8,128)S(1)}, u32[]{:S(2)}, u32[]{:S(2)}) collective-permute-start(f32[24,128]{1,0:T(8,128)S(1)} %add.111), channel_id=1, source_target_pairs={{0,2},{2,0},{1,3},{3,1},{4,6},{6,4},{5,7},{7,5},{8,10},{10,8},{9,1... | collective-permute-start | bytes 36872 | tf_op jit(solution)/shard_map/ppermute | solution.py:431
  247.2 27.1 %copy-start.11 = (f32[256,1024]{1,0:T(8,128)S(1)}, f32[256,1024]{1,0:T(8,128)}, u32[]{:S(2)}) copy-start(f32[256,1024]{1,0:T(8,128)} %get-tuple-element.238.hidden_ref) | copy-start | bytes 3145732
  247.2 27.1 %copy-start.47 = (f32[1024]{0:T(1024)S(1)}, f32[1024]{0:T(1024)}, u32[]{:S(2)}) copy-start(f32[1024]{0:T(1024)} %param.35) | copy-start | bytes 12292
  247.2 4.0 %collective-permute-start.33 = (bf16[400,1024]{1,0:T(8,128)(2,1)}, bf16[400,1024]{1,0:T(8,128)(2,1)S(1)}, u32[]{:S(2)}, u32[]{:S(2)}) collective-permute-start(bf16[400,1024]{1,0:T(8,128)(2,1)} %collective-permute-done.26.refs_7_), channel_id=1, source_target_pairs={{0,2},{2,0},{1,3},{3,1},{4,6},{6,4},{5,7},{7,5},{8,10},{10,8},{9,1... | collective-permute-start | bytes 2457608 | tf_op jit(solution)/shard_map/ppermute | solution.py:431
  247.2 5.5 %collective-permute-start.34 = (bf16[400,1024]{1,0:T(8,128)(2,1)}, bf16[400,1024]{1,0:T(8,128)(2,1)S(1)}, u32[]{:S(2)}, u32[]{:S(2)}) collective-permute-start(bf16[400,1024]{1,0:T(8,128)(2,1)} %collective-permute-done.27.refs_9_), channel_id=1, source_target_pairs={{0,2},{2,0},{1,3},{3,1},{4,6},{6,4},{5,7},{7,5},{8,10},{10,8},{9,1... | collective-permute-start | bytes 2457608 | tf_op jit(solution)/shard_map/ppermute | solution.py:431
  247.7 20.7 %collective-permute-start.31 = (bf16[400,1024]{1,0:T(8,128)(2,1)}, bf16[400,1024]{1,0:T(8,128)(2,1)}, u32[]{:S(2)}, u32[]{:S(2)}) collective-permute-start(bf16[400,1024]{1,0:T(8,128)(2,1)} %collective-permute-done.26.refs_7_), channel_id=1, source_target_pairs={{0,8},{8,16},{16,24},{24,28},{28,20},{20,12},{12,4},{4,0},{1,9},{9... | collective-permute-start | bytes 2457608 | tf_op jit(solution)/shard_map/ppermute | solution.py:566
  249.4 20.2 %collective-permute-start.32 = (bf16[400,1024]{1,0:T(8,128)(2,1)}, bf16[400,1024]{1,0:T(8,128)(2,1)}, u32[]{:S(2)}, u32[]{:S(2)}) collective-permute-start(bf16[400,1024]{1,0:T(8,128)(2,1)} %collective-permute-done.27.refs_9_), channel_id=1, source_target_pairs={{0,4},{8,0},{16,8},{24,16},{28,24},{20,28},{12,20},{4,12},{1,5},{9... | collective-permute-start | bytes 2457608 | tf_op jit(solution)/shard_map/ppermute | solution.py:566
  249.7 13.6 %collective-permute-start.36 = (bf16[256,1024]{1,0:T(8,128)(2,1)}, bf16[256,1024]{1,0:T(8,128)(2,1)}, u32[]{:S(2)}, u32[]{:S(2)}) collective-permute-start(bf16[256,1024]{1,0:T(8,128)(2,1)} %get-tuple-element.345), channel_id=1, source_target_pairs={{0,1},{1,0},{2,3},{3,2},{4,5},{5,4},{6,7},{7,6},{8,9},{9,8},{10,11... | collective-permute-start | bytes 1572872 | tf_op jit(solution)/shard_map/ppermute | solution.py:462
  251.2 17.2 %collective-permute-start.35 = (f32[24,128]{1,0:T(8,128)S(1)}, f32[24,128]{1,0:T(8,128)S(1)}, u32[]{:S(2)}, u32[]{:S(2)}) collective-permute-start(f32[24,128]{1,0:T(8,128)S(1)} %add.112), channel_id=1, source_target_pairs={{0,4},{4,0},{8,12},{12,8},{16,20},{20,16},{24,28},{28,24},{1,5},{5... | collective-permute-start | bytes 36872 | tf_op jit(solution)/shard_map/ppermute | solution.py:979
  269.7 4.0 %collective-permute-start.39 = (bf16[400,1024]{1,0:T(8,128)(2,1)}, bf16[400,1024]{1,0:T(8,128)(2,1)}, u32[]{:S(2)}, u32[]{:S(2)}) collective-permute-start(bf16[400,1024]{1,0:T(8,128)(2,1)} %collective-permute-done.31.refs_7_), channel_id=1, source_target_pairs={{0,2},{2,0},{1,3},{3,1},{4,6},{6,4},{5,7},{7,5},{8,10},{10,8},{9,1... | collective-permute-start | bytes 2457608 | tf_op jit(solution)/shard_map/ppermute | solution.py:431
  269.7 6.8 %collective-permute-start.40 = (bf16[400,1024]{1,0:T(8,128)(2,1)}, bf16[400,1024]{1,0:T(8,128)(2,1)}, u32[]{:S(2)}, u32[]{:S(2)}) collective-permute-start(bf16[400,1024]{1,0:T(8,128)(2,1)} %collective-permute-done.32.refs_9_), channel_id=1, source_target_pairs={{0,2},{2,0},{1,3},{3,1},{4,6},{6,4},{5,7},{7,5},{8,10},{10,8},{9,1... | collective-permute-start | bytes 2457608 | tf_op jit(solution)/shard_map/ppermute | solution.py:431
  270.2 20.9 %collective-permute-start.37 = (bf16[400,1024]{1,0:T(8,128)(2,1)}, bf16[400,1024]{1,0:T(8,128)(2,1)S(1)}, u32[]{:S(2)}, u32[]{:S(2)}) collective-permute-start(bf16[400,1024]{1,0:T(8,128)(2,1)} %collective-permute-done.31.refs_7_), channel_id=1, source_target_pairs={{0,8},{8,16},{16,24},{24,28},{28,20},{20,12},{12,4},{4,0},{1,9},{9... | collective-permute-start | bytes 2457608 | tf_op jit(solution)/shard_map/ppermute | solution.py:566
  270.7 20.4 %collective-permute-start.38 = (bf16[400,1024]{1,0:T(8,128)(2,1)}, bf16[400,1024]{1,0:T(8,128)(2,1)S(1)}, u32[]{:S(2)}, u32[]{:S(2)}) collective-permute-start(bf16[400,1024]{1,0:T(8,128)(2,1)} %collective-permute-done.32.refs_9_), channel_id=1, source_target_pairs={{0,4},{8,0},{16,8},{24,16},{28,24},{20,28},{12,20},{4,12},{1,5},{9... | collective-permute-start | bytes 2457608 | tf_op jit(solution)/shard_map/ppermute | solution.py:566
  272.2 13.4 %collective-permute-start.41 = (bf16[256,1024]{1,0:T(8,128)(2,1)S(1)}, bf16[256,1024]{1,0:T(8,128)(2,1)}, u32[]{:S(2)}, u32[]{:S(2)}) collective-permute-start(bf16[256,1024]{1,0:T(8,128)(2,1)S(1)} %get-tuple-element.376), channel_id=1, source_target_pairs={{0,1},{1,0},{2,3},{3,2},{4,5},{5,4},{6,7},{7,6},{8,9},{9,8},{10,11... | collective-permute-start | bytes 1572872 | tf_op jit(solution)/shard_map/ppermute | solution.py:462
  273.7 17.3 %collective-permute-start.42 = (f32[24,128]{1,0:T(8,128)S(1)}, f32[24,128]{1,0:T(8,128)S(1)}, u32[]{:S(2)}, u32[]{:S(2)}) collective-permute-start(f32[24,128]{1,0:T(8,128)S(1)} %add.117), channel_id=1, source_target_pairs={{0,8},{4,12},{8,0},{12,4},{16,24},{20,28},{24,16},{28,20},{1,9},{5... | collective-permute-start | bytes 36872 | tf_op jit(solution)/shard_map/ppermute | solution.py:979
  291.1 12.0 %collective-permute-start.45 = (bf16[400,1024]{1,0:T(8,128)(2,1)S(1)}, bf16[400,1024]{1,0:T(8,128)(2,1)}, u32[]{:S(2)}, u32[]{:S(2)}) collective-permute-start(bf16[400,1024]{1,0:T(8,128)(2,1)S(1)} %collective-permute-done.37.left.refs_7_), channel_id=1, source_target_pairs={{0,2},{2,0},{1,3},{3,1},{4,6},{6,4},{5,7},{7,5},{8,10},{10,8},{9,1... | collective-permute-start | bytes 2457608 | tf_op jit(solution)/shard_map/ppermute | solution.py:431
  291.1 11.9 %collective-permute-start.46 = (bf16[400,1024]{1,0:T(8,128)(2,1)S(1)}, bf16[400,1024]{1,0:T(8,128)(2,1)}, u32[]{:S(2)}, u32[]{:S(2)}) collective-permute-start(bf16[400,1024]{1,0:T(8,128)(2,1)S(1)} %collective-permute-done.38.right.refs_9_), channel_id=1, source_target_pairs={{0,2},{2,0},{1,3},{3,1},{4,6},{6,4},{5,7},{7,5},{8,10},{10,8},{9,1... | collective-permute-start | bytes 2457608 | tf_op jit(solution)/shard_map/ppermute | solution.py:431
  294.4 15.6 %collective-permute-start.47 = (f32[24,128]{1,0:T(8,128)S(1)}, f32[24,128]{1,0:T(8,128)S(1)}, u32[]{:S(2)}, u32[]{:S(2)}) collective-permute-start(f32[24,128]{1,0:T(8,128)S(1)} %add.120), channel_id=1, source_target_pairs={{0,16},{4,20},{8,24},{12,28},{16,0},{20,4},{24,8},{28,12},{1,17},{... | collective-permute-start | bytes 36872 | tf_op jit(solution)/shard_map/ppermute | solution.py:979
  297.2 12.8 %collective-permute-start.43 = (bf16[400,512]{1,0:T(8,128)(2,1)}, bf16[400,512]{1,0:T(8,128)(2,1)}, u32[]{:S(2)}, u32[]{:S(2)}) collective-permute-start(bf16[400,512]{1,0:T(8,128)(2,1)} %get-tuple-element.359), channel_id=1, source_target_pairs={{0,8},{8,16},{16,24},{24,28},{28,20},{20,12},{12,4},{4,0},{1,9},{9... | collective-permute-start | bytes 1228808 | tf_op jit(solution)/shard_map/ppermute | solution.py:566
  297.7 12.2 %collective-permute-start.44 = (bf16[400,512]{1,0:T(8,128)(2,1)}, bf16[400,512]{1,0:T(8,128)(2,1)}, u32[]{:S(2)}, u32[]{:S(2)}) collective-permute-start(bf16[400,512]{1,0:T(8,128)(2,1)} %get-tuple-element.360), channel_id=1, source_target_pairs={{0,4},{8,0},{16,8},{24,16},{28,24},{20,28},{12,20},{4,12},{1,5},{9... | collective-permute-start | bytes 1228808 | tf_op jit(solution)/shard_map/ppermute | solution.py:566
  310.0 2.0 collective-permute-start.48
  310.0 2.5 collective-permute-start.49
  (39 other events, 210.9 us)

commit v17 on v16

--- a/solution.py
+++ b/solution.py
@@ -313,15 +313,16 @@
 
 def backward_kernel(
     crops,
-    before,
+    extra,
     query_ref,
     grad_ref,
     raw_ref,
     logsum_ref,
+    piece,
     *refs,
 ):
-    before_refs, refs = refs[:before], refs[before:]
-    piece, (dquery_ref, sums_ref, keys, key_t, value_n, sums) = refs[0], refs[-6:]
+    extras, refs = refs[:extra], refs[extra:]
+    outputs, (keys, key_t, value_n, sums) = refs[:-4], refs[-4:]
     group = pl.program_id(0)
 
     @pl.when(group == 0)
@@ -342,15 +343,25 @@
     dscores = (probs * (dprobs - delta)).astype(BF16)
     sums[...] += product(dscores, query_side) + product(probs.astype(BF16), grad_side)
     dquery = product(key_t[...], dscores) * 0.125
-    for ref in before_refs:
-        dquery = ref[0] + dquery
-    dquery_ref[0] = dquery.astype(dquery_ref.dtype)
+    if extras:
+        dquery += extras[0][0]
+    if len(outputs) == 1:
+        outputs[0][group, pl.ds(0, HD), :] = dquery.astype(BF16)
+    else:
+        outputs[0][0] = dquery.astype(outputs[0].dtype)
 
     @pl.when(group == pl.num_programs(0) - 1)
     def _():
-        chips, _, patches = sums_ref.shape
+        chips, _, patches = piece.shape
         for chip in range(chips):
-            sums_ref[chip] = sums[pl.ds(chip * patches, patches), :].T.astype(sums_ref.dtype)
+            total = sums[pl.ds(chip * patches, patches), :].T
+            if extra > 1:
+                total += extras[1][chip].astype(F32)
+            total = total.astype(BF16)
+            if len(outputs) == 1:
+                outputs[0][chip, pl.ds(HD, 2 * HD), :] = total
+            else:
+                outputs[1][chip] = total
 
 
 def key_step(count):
@@ -389,32 +400,32 @@
     )(queries, own, other)
 
 
-def backward_piece(queries, grads, raw, logsum, before, keys, earlier, index, pieces, crops, dtypes):
+def attention_backward(queries, grads, raw, logsum, keys, extras, crops):
     groups, _, patches = queries.shape
-    chips = keys.shape[0] // pieces
-    count = chips * keys.shape[2]
+    chips, count = keys.shape[0], keys.shape[0] * keys.shape[2]
     sums_shape = (chips, 2 * HD, keys.shape[2])
+    specs = [query_spec(HD, patches), whole_spec(sums_shape)]
+    shapes = [
+        struct((groups, HD, patches), BF16 if extras else F32),
+        struct(sums_shape, BF16),
+    ]
+    outs = specs
+    if extras and (groups, patches) == (chips, keys.shape[2]):
+        shapes = [struct((chips, 3 * HD, patches), BF16)]
+        outs = [whole_spec(shapes[0].shape)]
     return pl.pallas_call(
-        functools.partial(backward_kernel, crops, len(before)),
+        functools.partial(backward_kernel, crops, len(extras)),
         grid=(groups,),
         in_specs=[
             query_spec(payload_rows, patches),
             query_spec(HD, patches),
             query_spec(HD, patches),
             query_spec(1, patches),
+            whole_spec(keys.shape),
         ]
-        + [query_spec(HD, patches)] * len(before)
-        + [pl.BlockSpec((chips,) + keys.shape[1:], lambda group: (index, 0, 0))]
-        + [pl.BlockSpec(memory_space=pl.ANY)] * len(earlier),
-        out_specs=[
-            query_spec(HD, patches),
-            pl.BlockSpec(sums_shape, lambda group: (index, 0, 0)),
-        ],
-        out_shape=[
-            struct((groups, HD, patches), dtypes[0]),
-            struct((keys.shape[0],) + sums_shape[1:], dtypes[1]),
-        ],
-        input_output_aliases={5 + len(before): 1} if earlier else {},
+        + specs[: len(extras)],
+        out_specs=outs,
+        out_shape=shapes,
         scratch_shapes=[
             pltpu.VMEM((count, 2 * HD), BF16),
             pltpu.VMEM((HD, count), BF16),
@@ -424,7 +435,7 @@
         compiler_params=params,
         cost_estimate=light,
         name="attention_backward",
-    )(queries, grads, raw, logsum, *before, keys, *earlier)
+    )(queries, grads, raw, logsum, keys, *extras)
 
 
 def swap_cores(values):
@@ -586,23 +597,26 @@
 def add_kernel(wanted, count, _, *refs):
     outputs, refs = refs[-count:], list(refs[:-count])
     keep_in, far_in = refs.pop(0), refs.pop(0)
-    for starts, output in zip(wanted, outputs):
+    at = pl.program_id(0)
+
+    def put(output, total):
+        output[...] = total.astype(BF16)
+
+    for places, output in zip(wanted, outputs):
         near, far = refs.pop(0), refs.pop(0)
         total = product(near[...], keep_in[...], 0, 0) + product(far[...], far_in[...], 0, 0)
-        if len(outputs) > len(wanted):
-            for at, output in enumerate(outputs):
-                columns = output.shape[1]
-                output[...] = total[:, at * columns : at * columns + columns].astype(BF16)
+        arrived = [(place, refs.pop(0)) for place in places]
+        if count > len(wanted):
+            for place in range(count):
+                pl.when(at == place)(functools.partial(put, outputs[place], total))
             return
-        output[...] = total.astype(BF16)
-        arrived = [refs.pop(0) for _ in starts]
-        for start in sorted(set(starts)):
-            parts = [part for part, at in zip(arrived, starts) if at == start]
-            columns = slice(start, start + parts[0].shape[1])
-            summed = total[:, columns]
-            for part in parts:
-                summed += part[...].astype(F32)
-            output[:, columns] = summed.astype(BF16)
+        for place, part in arrived:
+            if place is None:
+                total += part[...].astype(F32)
+        put(output, total)
+        for place, part in arrived:
+            if place is not None:
+                pl.when(at == place)(lambda: put(output, total + part[...].astype(F32)))
 
 
 class Reduce:
@@ -625,8 +639,10 @@
     def advance(self, state):
         half = self.sides[0].shape[1] // 2
         ahead, behind = state
-        first = 0 if ahead.shape[1] != half else half
-        self.ready = self.add([(self.left, [(ahead, 0)]), (-self.left, [(behind, first)])])
+        places = (0, 1) if ahead.shape[1] == half else (None, None)
+        self.ready = self.add(
+            [(self.left, [(ahead, places[0])]), (-self.left, [(behind, places[1])])]
+        )
 
     def arrive(self, values):
         self.state, values = lax.optimization_barrier((self.state, values))
@@ -634,7 +650,7 @@
 
     def finish(self):
         ahead, behind = self.state
-        return self.add([(0, [(ahead, 0), (behind, 0)])])[0]
+        return self.add([(0, [(ahead, None), (behind, None)])])[0]
 
     def add(self, wanted, split=False):
         (rows, model), units, chips = self.sides[0].shape, self.units, self.chips
@@ -646,31 +662,33 @@
                 for operand, side in zip(self.operands, self.sides):
                     block = lax.dynamic_slice_in_dim(operand, start, units, 1)
                     total += product(block, side, 0, 0)
-                for part, start in parts:
+                for part, place in parts:
+                    start = (place or 0) * part.shape[1]
                     total = total.at[:, start : start + part.shape[1]].add(part.astype(F32))
                 sums.append(total.astype(BF16))
             return sums
-        side = pl.BlockSpec((rows, model), lambda at, table: (0, 0))
-        whole = pl.BlockSpec((units, model), lambda at, table: (0, 0))
+        half = model // 2
+        side = pl.BlockSpec((rows, half), lambda at, table: (0, at))
+        whole = pl.BlockSpec((units, half), lambda at, table: (0, at))
+        fixed = pl.BlockSpec((units, half), lambda at, table: (0, 0))
         specs, arrays = [side] * 2, list(self.sides)
         for step, parts in wanted:
             block = pl.BlockSpec(
                 (rows, units), lambda at, table, step=step % chips: (0, table[step])
             )
-            specs += [block] * 2
-            specs += [pl.BlockSpec(part.shape, lambda at, table: (0, 0)) for part, _ in parts]
+            specs += [block] * 2 + [whole if place is None else fixed for _, place in parts]
             arrays += list(self.operands) + [part for part, _ in parts]
-        starts = [[start for _, start in parts] for _, parts in wanted]
-        shapes = [struct((units, model), BF16)] * len(wanted)
+        places = [[place for _, place in parts] for _, parts in wanted]
+        shapes, outs = [struct((units, model), BF16)] * len(wanted), [whole] * len(wanted)
         if split:
-            shapes = [struct((units, model // 2), BF16)] * 2
+            shapes, outs = [struct((units, half), BF16)] * 2, [fixed] * 2
         return pl.pallas_call(
-            functools.partial(add_kernel, starts, len(shapes)),
+            functools.partial(add_kernel, places, len(shapes)),
             grid_spec=pltpu.PrefetchScalarGridSpec(
                 num_scalar_prefetch=1,
-                grid=(1,),
+                grid=(2,),
                 in_specs=specs,
-                out_specs=[pl.BlockSpec(shape.shape, lambda at, table: (0, 0)) for shape in shapes],
+                out_specs=outs,
             ),
             out_shape=shapes,
             compiler_params=streaming,
@@ -778,9 +796,9 @@
         pl.when(here & (core != 0))(functools.partial(put, far, near, head))
 
 
-def head_gradient_kernel(steps, chips, table, query_ref, key_value_ref, *refs):
+def head_gradient_kernel(steps, chips, table, grads_ref, *refs):
     parts, out_ref = refs[:-1], refs[-1]
-    patches = query_ref.shape[2]
+    patches = grads_ref.shape[2]
     for at, part in enumerate(parts):
 
         @pl.when(pl.program_id(0) == at)
@@ -788,13 +806,12 @@
             total = jnp.zeros(out_ref.shape, F32)
             for index, step in enumerate(steps):
                 chip = table[chips + step % chips]
-                grads = jnp.concatenate([query_ref[chip], key_value_ref[chip]], axis=0)
-                total += product(grads, part[pl.ds(index * patches, patches), :])
+                total += product(grads_ref[chip], part[pl.ds(index * patches, patches), :])
             out_ref[...] = total.astype(BF16)
 
 
-def head_gradient(dquery, key_value, parts, steps, table):
-    chips, rows, _ = dquery.shape
+def head_gradient(grads, parts, steps, table):
+    chips, rows, _ = grads.shape
     columns = parts[0].shape[1]
 
     def column(at, table):
@@ -808,15 +825,15 @@
             grid=(len(parts),),
             in_specs=[
                 pl.BlockSpec(array.shape, lambda at, table, rank=array.ndim: (0,) * rank)
-                for array in (dquery, key_value, *parts)
+                for array in (grads, *parts)
             ],
-            out_specs=pl.BlockSpec((3 * rows, columns), column),
+            out_specs=pl.BlockSpec((rows, columns), column),
         ),
-        out_shape=struct((3 * rows, columns * len(parts)), BF16),
+        out_shape=struct((rows, columns * len(parts)), BF16),
         compiler_params=streaming,
         cost_estimate=light,
         name="head_gradient",
-    )(table, dquery, key_value, *parts)
+    )(table, grads, *parts)
 
 
 def core_half(values, axis, side):
@@ -904,30 +921,27 @@
     out_near, out_far = share_halves(attn_out, 0)
     doutput = product(out_near, d_branch) + product(out_far, swap_cores(d_branch))
     doutput = doutput.astype(BF16).reshape(chips, -1, model)
-    doutput = to_heads(doutput)
     steps, inputs = zip(*inputs.blocks)
     inputs = join(inputs)
     parts = across_heads(inputs) if cut != model else [inputs]
-    grads, doutput, _ = visit([ring], (grads, doutput, inputs))
-    *dquery, far_sums = backward_piece(
-        queries, grads, raw, logsum, [], other, [], 0, 1, crops, (F32, BF16)
-    )
-    grads, dquery, far_sums = visit([ring], (grads, dquery, far_sums))
+    grads, doutput = visit([ring], (grads, doutput))
+    doutput = to_heads(doutput)
+    dquery, far_sums = attention_backward(queries, grads, raw, logsum, other, [], crops)
     far_sums = swap_cores(far_sums)
-    *dquery, near_sums = backward_piece(
-        queries, grads, raw, logsum, dquery, own, [], 0, 1, crops, (BF16, F32)
-    )
-    near_sums, dquery = ring.arrive((near_sums, dquery))
-    (dquery,) = dquery
-    key_value = (near_sums + far_sums.astype(F32)).astype(BF16)
-    doutput, key_value = lax.optimization_barrier((doutput, key_value))
+    grads, dquery = visit([ring], (grads, dquery))
+    head_grads = attention_backward(
+        queries, grads, raw, logsum, own, [dquery, far_sums], crops
+    )
+    head_grads = ring.arrive(head_grads)
+    doutput, head_grads = lax.optimization_barrier((doutput, head_grads))
     doutput = jnp.sum(doutput.astype(F32), axis=0)
     small = jnp.concatenate([sums.reshape(-1), dup_bias[0]])
     small = jnp.pad(small, (0, small_rows * model - small.shape[0])).reshape(small_rows, model)
     doutput = jnp.concatenate([doutput, small], axis=0).astype(BF16)
     if split == 1:
-        moved = to_heads(jnp.concatenate([dquery, key_value], axis=1))
-        projections = head_gradient(dquery, key_value, parts, steps, table)
+        (head_grads,) = head_grads
+        moved = to_heads(head_grads)
+        projections = head_gradient(head_grads, parts, steps, table)
         near, far = share_halves(projections, 0)
         projections = (near.astype(F32) + far.astype(F32)).astype(BF16)
         size = projections.shape[0]
@@ -936,6 +950,7 @@
             moved[:, at * HD : at * HD + HD].reshape(width, rows) for at in range(3)
         )
     else:
+        dquery, key_value = head_grads
         dquery = gather_queries(dquery, heads, split, rows)
         moved = to_heads(key_value).reshape(heads, split, 2 * HD, rows).astype(F32)
         moved = jnp.sum(moved, axis=1).astype(BF16)

time: 322 us -> 307 us (0.953)
  waiting for transfers between devices: 67.8 us -> 49.1 us
    ppermute x24, waiting for transfers between devices: 30.8 us -> 17.6 us  [send(): lax.ppermute(block, 'chip', ring_pairs(direction))]
    ppermute x6, waiting for transfers between devices: 15 us -> 9.19 us  [across_heads(): return [part, lax.ppermute(part, 'head', [(0, 1), (1, 0)])]]
    all_to_all x3, starting transfers between devices: 12.7 us -> 16.5 us  [to_heads(): return lax.all_to_all(blocks, 'chip', 0, 0, tiled=True)]
    unnamed x103 -> x95, local copies, waits for them, and re-layouts: 9.95 us -> 10.6 us
  transfers between devices with their start and end apart: 53 -> 53, of which waited for: 23 -> 22; matrix products, arithmetic and copies ran while one was open for 5% -> 6% of each run, Pallas kernels for 32% -> 35%
where the time goes in v17:
time: 307 us; the launch traced here: 306 us
  Pallas kernels  124 us (40%)
  starting transfers between devices  57.8 us (19%)
  waiting for transfers between devices  49.1 us (16%)
  blocking collectives  42.4 us (14%)
  local copies, waits for them, and re-layouts  14 us (5%)
  other arithmetic  12.9 us (4%)
  matrix products  4.3 us (1%)
    all_to_all x2, blocking collectives, to_heads(): return lax.all_to_all(blocks, 'chip', 0, 0, tiled=True)  42.4 us
    pallas_call x5, Pallas kernels, place(): pl.pallas_call(functools.partial(place_kernel, heads, len(blocks[0]) // 2...  30.2 us
    pallas_call x2, Pallas kernels, attention_backward(): pl.pallas_call(functools.partial(backward_kernel, crops, len(extras)), gr...  24.9 us
    ppermute x24, starting transfers between devices, send(): lax.ppermute(block, 'chip', ring_pairs(direction))  24.8 us
    pallas_call x5, Pallas kernels, add(): pl.pallas_call(functools.partial(add_kernel, places, len(shapes)), grid_s...  19.2 us
    ppermute x24, waiting for transfers between devices, send(): lax.ppermute(block, 'chip', ring_pairs(direction))  17.6 us
    all_to_all x3, starting transfers between devices, to_heads(): return lax.all_to_all(blocks, 'chip', 0, 0, tiled=True)  16.5 us
    pallas_call x1, Pallas kernels, attention_forward(): pl.pallas_call(functools.partial(forward_kernel, crops, key_step(count)),...  15.3 us
  transfers between devices with their start and end apart: 53, of which 22 were waited for; matrix products, arithmetic and copies ran while one was open for 6% of the time, Pallas kernels for 35%

profile of v17, /device:TPU:0, one launch (start us, length us, event | category | flops | bytes accessed | tf_op | source)
XLA Modules:
  0.0 305.7 jit_solution(4536018932646377780)
XLA Ops:
  1.2 6.6 %project.1 = (bf16[8,208,256]{2,1,0:T(8,128)(2,1)}, bf16[256,1024]{1,0:T(8,128)(2,1)}, bf16[256,512]{1,0:T(8,128)(2,1)}) custom-call(s32[18]{0:T(128)} %compare_select_fusion.5.table.core_ref._, bf16[256,1024]{1,0:T(8,128)(2,1)} %input_ref.3, s32[1,256]{1,0:T(1,128)} %bitcast.73, s32[32]{0:T(128)} %steps_ref.1, f32[1,1024]{1,0:T(1,128)} %bitcast.56, ...), custom_call_target="tpu_custom_call" | custom-call | flops 1 | bytes 1 | tf_op jit(solution)/shard_map/project/pallas_call | solution.py:94
  7.8 29.6 %all_to_all.25.query_ref.own.piece = bf16[8,208,256]{2,1,0:T(8,128)(2,1)S(1)} all-to-all(bf16[8,208,256]{2,1,0:T(8,128)(2,1)} %get-tuple-element.205), channel_id=1, replica_groups=mesh['chip'=8,'core'=2,'head'=2] {'chip'}, dimensions={0} | all-to-all | bytes 1703936 | tf_op jit(solution)/shard_map/all_to_all | solution.py:446
  38.2 1.3 collective-permute-start.1
  40.7 15.3 %attention_forward.1 = (f32[8,64,256]{2,1,0:T(8,128)}, bf16[8,64,256]{2,1,0:T(8,128)(2,1)}, f32[8,1,256]{2,1,0:T(1,128)}) custom-call(bf16[8,208,256]{2,1,0:T(8,128)(2,1)} %copy-done, bf16[8,208,256]{2,1,0:T(8,128)(2,1)} %copy-done, bf16[8,208,256]{2,1,0:T(8,128)(2,1)} %copy-done.2), custom_call_target="tpu_custom_call" | custom-call | flops 1 | bytes 1 | tf_op jit(solution)/shard_map/attention_forward/pallas_call | solution.py:378
  56.1 12.8 %all_to_all.26 = bf16[8,64,256]{2,1,0:T(8,128)(2,1)S(1)} all-to-all(bf16[8,64,256]{2,1,0:T(8,128)(2,1)} %get-tuple-element.212), channel_id=1, replica_groups=mesh['chip'=8,'core'=2,'head'=2] {'chip'}, dimensions={0} | all-to-all | bytes 524288 | tf_op jit(solution)/shard_map/all_to_all | solution.py:446
  69.4 1.6 collective-permute-start.7
  72.9 4.6 %collective-permute-done.3.refs_3_ = bf16[256,512]{1,0:T(8,128)(2,1)S(1)} collective-permute-done((bf16[256,512]{1,0:T(8,128)(2,1)S(1)}, bf16[256,512]{1,0:T(8,128)(2,1)S(1)}, u32[]{:S(2)}, u32[]{:S(2)}) %collective-permute-start.3) | collective-permute-done | bytes 262176 | tf_op jit(solution)/shard_map/ppermute | solution.py:577
  78.4 1.4 collective-permute-start.5
  80.4 1.5 collective-permute-done.7.refs_1_
  82.7 11.7 %mlp.1 = (bf16[256,2048]{1,0:T(8,128)(2,1)}, bf16[256,2048]{1,0:T(8,128)(2,1)}, bf16[256,1024]{1,0:T(8,128)(2,1)}, bf16[256,1024]{1,0:T(8,128)(2,1)}, f32[256,10...) custom-call(s32[18]{0:T(128)} %compare_select_fusion.5.table.core_ref._, ...), custom_call_target="tpu_custom_call" | custom-call | flops 1 | bytes 1 | tf_op jit(solution)/shard_map/mlp/pallas_call | solution.py:174
  95.1 1.6 collective-permute-start.14
  96.6 1.5 collective-permute-done.8.refs_1_
  99.9 3.3 %ring_add.5 = (bf16[256,512]{1,0:T(8,128)(2,1)}, bf16[256,512]{1,0:T(8,128)(2,1)}) custom-call(s32[18]{0:T(128)} %compare_select_fusion.5.table.core_ref._, bf16[256,1024]{1,0:T(8,128)(2,1)} %get-tuple-element.223.refs_0_, bf16[256,1024]{1,0:T(8,128)(2,1)} %copy-done.8, bf16[256,2048]{1,0:T(8,128)(2,1)} %get-tuple-element.225.refs_2_.refs_5_, ...), custom_call_target="tpu_custom_call" | custom-call | flops 1 | bytes 1 | tf_op jit(solution)/shard_map/ring_add/pallas_call | solution.py:685
  103.6 1.7 collective-permute-start.11
  105.3 1.7 halves.2
  107.5 1.5 collective-permute-start.13
  110.0 4.3 %middle.1 = (f32[256,1024]{1,0:T(8,128)}, bf16[256,1024]{1,0:T(8,128)(2,1)}, bf16[512,256]{1,0:T(8,128)(2,1)}, f32[4,1024]{1,0:T(4,128)}) custom-call(f32[256,1024]{1,0:T(8,128)} %get-tuple-element.233.hidden_ref, bf16[256,1024]{1,0:T(8,128)(2,1)} %grad_ref.3, bf16[256,1024]{1,0:T(8,128)(2,1)} %get-tuple-element.236.refs_0_, bf16[256,1024]{1,0:T(8,128)(2,1)} %copy-done.29, ...), custom_call_target="tpu_custom_call" | custom-call | flops 1 | bytes 1 | tf_op jit(solution)/shard_map/middle/pallas_call | solution.py:235
  116.0 4.5 %ring_add.6 = (bf16[256,1024]{1,0:T(8,128)(2,1)}, bf16[256,1024]{1,0:T(8,128)(2,1)}) custom-call(s32[18]{0:T(128)} %compare_select_fusion.5.table.core_ref._, bf16[256,1024]{1,0:T(8,128)(2,1)} %get-tuple-element.223.refs_0_, bf16[256,1024]{1,0:T(8,128)(2,1)} %copy-done.8, bf16[256,2048]{1,0:T(8,128)(2,1)} %get-tuple-element.225.refs_2_.refs_5_, ...), custom_call_target="tpu_custom_call" | custom-call | flops 1 | bytes 1 | tf_op jit(solution)/shard_map/ring_add/pallas_call | solution.py:685
  121.2 4.6 %all-to-all-start.2 = ((bf16[8,64,256]{2,1,0:T(8,128)(2,1)}), bf16[8,64,256]{2,1,0:T(8,128)(2,1)S(1)}, u32[]{:S(2)}, u32[]{:S(2)}) async-start(bf16[8,64,256]{2,1,0:T(8,128)(2,1)} %bitcast.9), calls=%async_computation.2 | async-start | bytes 524288 | tf_op jit(solution)/shard_map/all_to_all | solution.py:446
  125.8 2.0 collective-permute-start.15
  127.8 3.0 join.1.refs_0_
  130.8 1.5 collective-permute-start.24
  133.7 2.4 all-to-all-done.2.grad_ref
  136.1 6.3 %collective-permute-done.15.refs_4_ = bf16[256,1024]{1,0:T(8,128)(2,1)S(1)} collective-permute-done((bf16[256,1024]{1,0:T(8,128)(2,1)}, bf16[256,1024]{1,0:T(8,128)(2,1)S(1)}, u32[]{:S(2)}, u32[]{:S(2)}) %collective-permute-start.15) | collective-permute-done | bytes 524320 | tf_op jit(solution)/shard_map/ppermute | solution.py:635
  142.4 1.9 collective-permute-done.16.refs_7_
  145.1 4.0 %ring_add.7 = (bf16[256,1024]{1,0:T(8,128)(2,1)}, bf16[256,1024]{1,0:T(8,128)(2,1)}) custom-call(s32[18]{0:T(128)} %compare_select_fusion.5.table.core_ref._, bf16[256,1024]{1,0:T(8,128)(2,1)} %get-tuple-element.223.refs_0_, bf16[256,1024]{1,0:T(8,128)(2,1)} %copy-done.8, bf16[256,2048]{1,0:T(8,128)(2,1)} %get-tuple-element.225.refs_2_.refs_5_, ...), custom_call_target="tpu_custom_call" | custom-call | flops 1 | bytes 1 | tf_op jit(solution)/shard_map/ring_add/pallas_call | solution.py:685
  149.1 2.3 collective-permute-start.19
  151.4 4.4 %all-to-all-start.3 = ((bf16[8,32,1024]{2,1,0:T(8,128)(2,1)}), bf16[8,32,1024]{2,1,0:T(8,128)(2,1)}, u32[]{:S(2)}, u32[]{:S(2)}) async-start(bf16[8,32,1024]{2,1,0:T(8,128)(2,1)} %bitcast.10), calls=%async_computation.3 | async-start | bytes 1048576 | tf_op jit(solution)/shard_map/all_to_all | solution.py:446
  155.9 11.9 %attention_backward.2 = (f32[8,64,256]{2,1,0:T(8,128)S(1)}, bf16[8,128,256]{2,1,0:T(8,128)(2,1)S(1)}) custom-call(bf16[8,208,256]{2,1,0:T(8,128)(2,1)S(1)} %copy-done.1, bf16[8,64,256]{2,1,0:T(8,128)(2,1)S(1)} %all-to-all-done.2.grad_ref, f32[8,64,256]{2,1,0:T(8,128)S(1)} %copy-done.4, f32[8,1,256]{2,1,0:T(1,128)S(1)} %copy-done.5, ...), custom_call_target="tpu_custom_call" | custom-call | flops 1 | bytes 1 | tf_op jit(solution)/shard_map/attention_backward/pallas_call | solution.py:416
  167.9 3.8 %ring_add.8 = (bf16[256,1024]{1,0:T(8,128)(2,1)}, bf16[256,1024]{1,0:T(8,128)(2,1)}) custom-call(s32[18]{0:T(128)} %compare_select_fusion.5.table.core_ref._, bf16[256,1024]{1,0:T(8,128)(2,1)} %get-tuple-element.223.refs_0_, bf16[256,1024]{1,0:T(8,128)(2,1)} %copy-done.8, bf16[256,2048]{1,0:T(8,128)(2,1)} %get-tuple-element.225.refs_2_.refs_5_, ...), custom_call_target="tpu_custom_call" | custom-call | flops 1 | bytes 1 | tf_op jit(solution)/shard_map/ring_add/pallas_call | solution.py:685
  171.7 2.0 collective-permute-start.21
  173.8 1.2 convert_reduce_fusion
  175.0 1.3 fusion.12
  176.4 13.0 %attention_backward.3.grads_ref = bf16[8,192,256]{2,1,0:T(8,128)(2,1)} custom-call(bf16[8,208,256]{2,1,0:T(8,128)(2,1)S(1)} %copy-done.1, bf16[8,64,256]{2,1,0:T(8,128)(2,1)S(1)} %all-to-all-done.2.grad_ref, f32[8,64,256]{2,1,0:T(8,128)S(1)} %copy-done.4, f32[8,1,256]{2,1,0:T(1,128)S(1)} %copy-done.5, bf16[8,208,256]{2,1,0:T(8,128)(2,1)S(1)} %copy-done.1, ...), custom_call_target="tpu_custom_call" | custom-call | flops 1 | bytes 1 | tf_op jit(solution)/shard_map/attention_backward/pallas_call | solution.py:416
  189.3 7.5 %all-to-all-start.4 = ((bf16[8,192,256]{2,1,0:T(8,128)(2,1)}), bf16[8,192,256]{2,1,0:T(8,128)(2,1)}, u32[]{:S(2)}, u32[]{:S(2)}) async-start(bf16[8,192,256]{2,1,0:T(8,128)(2,1)} %attention_backward.3.grads_ref), calls=%async_computation.4 | async-start | bytes 1572864 | tf_op jit(solution)/shard_map/all_to_all | solution.py:446
  197.1 5.0 %head_gradient.1 = bf16[192,1024]{1,0:T(8,128)(2,1)} custom-call(s32[18]{0:T(128)} %compare_select_fusion.5.table.core_ref._, bf16[8,192,256]{2,1,0:T(8,128)(2,1)} %attention_backward.3.grads_ref, bf16[2048,512]{1,0:T(8,128)(2,1)} %join.1.refs_0_, bf16[2048,512]{1,0:T(8,128)(2,1)} %collective-permute-done.24.refs_1_), custom_call_target="tpu_custom_call" | custom-call | flops 1 | bytes 1 | tf_op jit(solution)/shard_map/head_gradient/pallas_call | solution.py:821
  203.1 3.6 %ring_add.9 = bf16[256,1024]{1,0:T(8,128)(2,1)} custom-call(s32[18]{0:T(128)} %compare_select_fusion.5.table.core_ref._, bf16[256,1024]{1,0:T(8,128)(2,1)} %get-tuple-element.223.refs_0_, bf16[256,1024]{1,0:T(8,128)(2,1)} %copy-done.8, bf16[256,2048]{1,0:T(8,128)(2,1)} %get-tuple-element.225.refs_2_.refs_5_, bf16[256,2048]{1,0:T(8,128)(2,1)} %copy-done.6, ...), custom_call_target="tpu_custom_call" | custom-call | flops 1 | bytes 1 | tf_op jit(solution)/shard_map/ring_add/pallas_call | solution.py:685
  206.7 1.2 reduce
  209.7 2.0 collective-permute-start.26
  211.7 4.8 %all-to-all-done.4 = bf16[8,192,256]{2,1,0:T(8,128)(2,1)} async-done(((bf16[8,192,256]{2,1,0:T(8,128)(2,1)}), bf16[8,192,256]{2,1,0:T(8,128)(2,1)}, u32[]{:S(2)}, u32[]{:S(2)}) %all-to-all-start.4) | async-done | bytes 786464 | tf_op jit(solution)/shard_map/all_to_all | solution.py:446
  219.6 1.5 fusion.6
  221.1 1.6 collective-permute-start.29
  222.7 2.2 collective-permute-done.29
  226.1 4.5 %place.5 = (f32[2048,1024]{1,0:T(8,128)}, f32[1024,2048]{1,0:T(8,128)}, f32[2,8,32,1024]{3,2,1,0:T(8,128)}, f32[8,2,16,1024]{3,2,1,0:T(8,128)}, f32[1024,512]{1,...) custom-call(s32[18]{0:T(128)} %compare_select_fusion.5.table.core_ref._, bf16[400,1024]{1,0:T(8,128)(2,1)} %copy-done.13, ...), custom_call_target="tpu_custom_call" | custom-call | flops 1 | bytes 1 | tf_op jit(solution)/shard_map/place/pallas_call | solution.py:731
  230.5 2.9 collective-permute-done.27.refs_9_
  234.5 1.5 collective-permute-start.32
  236.0 1.5 collective-permute-start.36
  239.3 6.9 %place.6 = (f32[2048,1024]{1,0:T(8,128)}, f32[1024,2048]{1,0:T(8,128)}, f32[2,8,32,1024]{3,2,1,0:T(8,128)}, f32[8,2,16,1024]{3,2,1,0:T(8,128)}, f32[1024,512]{1,...) custom-call(s32[18]{0:T(128)} %compare_select_fusion.5.table.core_re, ...), custom_call_target="tpu_custom_call", output_to_operand_aliasing={{0}: (1, {}), {1}: (2, {}), {2}: (3, {}), {3}: (4, {}), {4}... | custom-call | flops 1 | bytes 1 | tf_op jit(solution)/shard_map/place/pallas_call | solution.py:731
  246.2 3.4 %collective-permute-done.36 = bf16[256,1024]{1,0:T(8,128)(2,1)} collective-permute-done((bf16[256,1024]{1,0:T(8,128)(2,1)}, bf16[256,1024]{1,0:T(8,128)(2,1)}, u32[]{:S(2)}, u32[]{:S(2)}) %collective-permute-start.36) | collective-permute-done | bytes 524320 | tf_op jit(solution)/shard_map/ppermute | solution.py:473
  249.6 5.0 %collective-permute-done.35 = f32[24,128]{1,0:T(8,128)S(1)} collective-permute-done((f32[24,128]{1,0:T(8,128)S(1)}, f32[24,128]{1,0:T(8,128)S(1)}, u32[]{:S(2)}, u32[]{:S(2)}) %collective-permute-start.35) | collective-permute-done | bytes 12320 | tf_op jit(solution)/shard_map/ppermute | solution.py:994
  256.0 1.3 collective-permute-start.38
  257.3 1.5 collective-permute-start.41
  259.5 2.2 add_convert_fusion
  261.8 7.0 %place.7 = (f32[2048,1024]{1,0:T(8,128)}, f32[1024,2048]{1,0:T(8,128)}, f32[2,8,32,1024]{3,2,1,0:T(8,128)}, f32[8,2,16,1024]{3,2,1,0:T(8,128)}, f32[1024,512]{1,...) custom-call(s32[18]{0:T(128)} %compare_select_fusion.5.table.core_re, ...), custom_call_target="tpu_custom_call", output_to_operand_aliasing={{0}: (1, {}), {1}: (2, {}), {2}: (3, {}), {3}: (4, {}), {4}... | custom-call | flops 1 | bytes 1 | tf_op jit(solution)/shard_map/place/pallas_call | solution.py:731
  268.8 1.9 collective-permute-done.41
  270.7 5.7 %collective-permute-done.42 = f32[24,128]{1,0:T(8,128)S(1)} collective-permute-done((f32[24,128]{1,0:T(8,128)S(1)}, f32[24,128]{1,0:T(8,128)S(1)}, u32[]{:S(2)}, u32[]{:S(2)}) %collective-permute-start.42) | collective-permute-done | bytes 12320 | tf_op jit(solution)/shard_map/ppermute | solution.py:994
  277.5 2.1 halves.3
  279.6 2.4 collective-permute-start.47
  282.2 1.7 collective-permute-start.44
  284.0 1.5 fusion.13
  285.5 2.3 fusion.11
  287.8 6.9 %place.8 = (f32[2048,1024]{1,0:T(8,128)}, f32[1024,2048]{1,0:T(8,128)}, f32[2,8,32,1024]{3,2,1,0:T(8,128)}, f32[8,2,16,1024]{3,2,1,0:T(8,128)}, f32[1024,512]{1,...) custom-call(s32[18]{0:T(128)} %compare_select_fusion.5.table.core_re, ...), custom_call_target="tpu_custom_call", output_to_operand_aliasing={{0}: (1, {}), {1}: (2, {}), {2}: (3, {}), {3}: (4, {}), {4}... | custom-call | flops 1 | bytes 1 | tf_op jit(solution)/shard_map/place/pallas_call | solution.py:731
  298.3 5.0 %place.9 = (f32[2048,1024]{1,0:T(8,128)}, f32[1024,2048]{1,0:T(8,128)}, f32[2,8,32,1024]{3,2,1,0:T(8,128)}, f32[8,2,16,1024]{3,2,1,0:T(8,128)}, f32[1024,512]{1,...) custom-call(s32[18]{0:T(128)} %compare_select_fusion.5.table.core_re, ...), custom_call_target="tpu_custom_call", output_to_operand_aliasing={{0}: (1, {}), {1}: (2, {}), {2}: (3, {}), {3}: (4, {}), {4}... | custom-call | flops 1 | bytes 1 | tf_op jit(solution)/shard_map/place/pallas_call | solution.py:731
  303.2 1.3 reduce_sum.99
  (197 shorter events, 34.6 us)
Async XLA Ops:
  7.8 61.0 %copy-start.10 = (bf16[512,1024]{1,0:T(8,128)(2,1)S(1)}, bf16[512,1024]{1,0:T(8,128)(2,1)}, u32[]{:S(2)}) copy-start(bf16[512,1024]{1,0:T(8,128)(2,1)} %refs_3_.1) | copy-start | bytes 3145732
  37.4 2.4 collective-permute-start.2
  37.5 18.6 %collective-permute-start = (bf16[256,512]{1,0:T(8,128)(2,1)}, bf16[256,512]{1,0:T(8,128)(2,1)S(1)}, u32[]{:S(2)}, u32[]{:S(2)}) collective-permute-start(bf16[256,512]{1,0:T(8,128)(2,1)} %get-tuple-element.207.refs_0_), channel_id=1, source_target_pairs={{0,8},{8,16},{16,24},{24,28},{28,20},{20,12},{12,4},{4,0},{1,9},{9... | collective-permute-start | bytes 786440 | tf_op jit(solution)/shard_map/ppermute | solution.py:577
  38.2 17.9 %collective-permute-start.1 = (bf16[256,512]{1,0:T(8,128)(2,1)}, bf16[256,512]{1,0:T(8,128)(2,1)S(1)}, u32[]{:S(2)}, u32[]{:S(2)}) collective-permute-start(bf16[256,512]{1,0:T(8,128)(2,1)} %get-tuple-element.207.refs_0_), channel_id=1, source_target_pairs={{0,4},{8,0},{16,8},{24,16},{28,24},{20,28},{12,20},{4,12},{1,5},{9... | collective-permute-start | bytes 786440 | tf_op jit(solution)/shard_map/ppermute | solution.py:577
  56.1 38.4 %copy-start.32 = (bf16[256,512]{1,0:T(8,128)(2,1)}, bf16[256,512]{1,0:T(8,128)(2,1)S(1)}, u32[]{:S(2)}) copy-start(bf16[256,512]{1,0:T(8,128)(2,1)S(1)} %collective-permute-done.refs_1_) | copy-start | bytes 786436
  56.1 38.4 %copy-start.33 = (bf16[256,512]{1,0:T(8,128)(2,1)}, bf16[256,512]{1,0:T(8,128)(2,1)S(1)}, u32[]{:S(2)}) copy-start(bf16[256,512]{1,0:T(8,128)(2,1)S(1)} %collective-permute-done.1.refs_2_) | copy-start | bytes 786436
  69.4 12.6 %collective-permute-start.7 = (bf16[256,1024]{1,0:T(8,128)(2,1)S(1)}, bf16[256,1024]{1,0:T(8,128)(2,1)S(1)}, u32[]{:S(2)}, u32[]{:S(2)}) collective-permute-start(bf16[256,1024]{1,0:T(8,128)(2,1)S(1)} %convolution_convert_fusion.refs_0_), channel_id=1, source_target_pairs={{0,1},{1,0},{2,3},{3,2},{4,5},{5,4},{6,7},{7,6},{8,9},{9,8},{10,11... | collective-permute-start | bytes 1572872 | tf_op jit(solution)/shard_map/ppermute | solution.py:473
  70.9 6.7 %collective-permute-start.3 = (bf16[256,512]{1,0:T(8,128)(2,1)S(1)}, bf16[256,512]{1,0:T(8,128)(2,1)S(1)}, u32[]{:S(2)}, u32[]{:S(2)}) collective-permute-start(bf16[256,512]{1,0:T(8,128)(2,1)S(1)} %collective-permute-done.refs_1_), channel_id=1, source_target_pairs={{0,8},{8,16},{16,24},{24,28},{28,20},{20,12},{12,4},{4,0},{1,9},{9... | collective-permute-start | bytes 786440 | tf_op jit(solution)/shard_map/ppermute | solution.py:577
  72.0 6.4 %collective-permute-start.4 = (bf16[256,512]{1,0:T(8,128)(2,1)S(1)}, bf16[256,512]{1,0:T(8,128)(2,1)S(1)}, u32[]{:S(2)}, u32[]{:S(2)}) collective-permute-start(bf16[256,512]{1,0:T(8,128)(2,1)S(1)} %collective-permute-done.1.refs_2_), channel_id=1, source_target_pairs={{0,4},{8,0},{16,8},{24,16},{28,24},{20,28},{12,20},{4,12},{1,5},{9... | collective-permute-start | bytes 786440 | tf_op jit(solution)/shard_map/ppermute | solution.py:577
  77.6 25.6 %copy-start.34 = (bf16[256,512]{1,0:T(8,128)(2,1)}, bf16[256,512]{1,0:T(8,128)(2,1)S(1)}, u32[]{:S(2)}) copy-start(bf16[256,512]{1,0:T(8,128)(2,1)S(1)} %collective-permute-done.3.refs_3_) | copy-start | bytes 786436
  78.4 24.9 %copy-start.35 = (bf16[256,512]{1,0:T(8,128)(2,1)}, bf16[256,512]{1,0:T(8,128)(2,1)S(1)}, u32[]{:S(2)}) copy-start(bf16[256,512]{1,0:T(8,128)(2,1)S(1)} %collective-permute-done.4.refs_4_) | copy-start | bytes 786436
  78.4 16.1 %collective-permute-start.5 = (bf16[256,512]{1,0:T(8,128)(2,1)S(1)}, bf16[256,512]{1,0:T(8,128)(2,1)S(1)}, u32[]{:S(2)}, u32[]{:S(2)}) collective-permute-start(bf16[256,512]{1,0:T(8,128)(2,1)S(1)} %collective-permute-done.3.refs_3_), channel_id=1, source_target_pairs={{0,8},{8,16},{16,24},{24,28},{28,20},{20,12},{12,4},{4,0},{1,9},{9... | collective-permute-start | bytes 786440 | tf_op jit(solution)/shard_map/ppermute | solution.py:577
  79.8 14.7 %collective-permute-start.6 = (bf16[256,512]{1,0:T(8,128)(2,1)S(1)}, bf16[256,512]{1,0:T(8,128)(2,1)S(1)}, u32[]{:S(2)}, u32[]{:S(2)}) collective-permute-start(bf16[256,512]{1,0:T(8,128)(2,1)S(1)} %collective-permute-done.4.refs_4_), channel_id=1, source_target_pairs={{0,4},{8,0},{16,8},{24,16},{28,24},{20,28},{12,20},{4,12},{1,5},{9... | collective-permute-start | bytes 786440 | tf_op jit(solution)/shard_map/ppermute | solution.py:577
  94.5 3.7 %collective-permute-start.9 = (bf16[256,2048]{1,0:T(8,128)(2,1)}, bf16[256,2048]{1,0:T(8,128)(2,1)S(1)}, u32[]{:S(2)}, u32[]{:S(2)}) collective-permute-start(bf16[256,2048]{1,0:T(8,128)(2,1)} %get-tuple-element.226), channel_id=1, source_target_pairs={{0,2},{2,0},{1,3},{3,1},{4,6},{6,4},{5,7},{7,5},{8,10},{10,8},{9,1... | collective-permute-start | bytes 3145736 | tf_op jit(solution)/shard_map/ppermute | solution.py:442
  94.6 3.6 %collective-permute-start.8 = (bf16[256,1024]{1,0:T(8,128)(2,1)}, bf16[256,1024]{1,0:T(8,128)(2,1)S(1)}, u32[]{:S(2)}, u32[]{:S(2)}) collective-permute-start(bf16[256,1024]{1,0:T(8,128)(2,1)} %get-tuple-element.224), channel_id=1, source_target_pairs={{0,2},{2,0},{1,3},{3,1},{4,6},{6,4},{5,7},{7,5},{8,10},{10,8},{9,1... | collective-permute-start | bytes 1572872 | tf_op jit(solution)/shard_map/ppermute | solution.py:442
  95.1 14.1 %collective-permute-start.14 = (bf16[256,1024]{1,0:T(8,128)(2,1)}, bf16[256,1024]{1,0:T(8,128)(2,1)S(1)}, u32[]{:S(2)}, u32[]{:S(2)}) collective-permute-start(bf16[256,1024]{1,0:T(8,128)(2,1)} %get-tuple-element.236.refs_0_), channel_id=1, source_target_pairs={{0,1},{1,0},{2,3},{3,2},{4,5},{5,4},{6,7},{7,6},{8,9},{9,8},{10,11... | collective-permute-start | bytes 1572872 | tf_op jit(solution)/shard_map/ppermute | solution.py:473
  103.2 11.9 %collective-permute-start.10 = (bf16[256,512]{1,0:T(8,128)(2,1)}, bf16[256,512]{1,0:T(8,128)(2,1)S(1)}, u32[]{:S(2)}, u32[]{:S(2)}) collective-permute-start(bf16[256,512]{1,0:T(8,128)(2,1)} %get-tuple-element.227), channel_id=1, source_target_pairs={{0,8},{8,16},{16,24},{24,28},{28,20},{20,12},{12,4},{4,0},{1,9},{9... | collective-permute-start | bytes 786440 | tf_op jit(solution)/shard_map/ppermute | solution.py:635
  103.6 11.6 %collective-permute-start.11 = (bf16[256,512]{1,0:T(8,128)(2,1)}, bf16[256,512]{1,0:T(8,128)(2,1)S(1)}, u32[]{:S(2)}, u32[]{:S(2)}) collective-permute-start(bf16[256,512]{1,0:T(8,128)(2,1)} %get-tuple-element.228), channel_id=1, source_target_pairs={{0,4},{8,0},{16,8},{24,16},{28,24},{20,28},{12,20},{4,12},{1,5},{9... | collective-permute-start | bytes 786440 | tf_op jit(solution)/shard_map/ppermute | solution.py:635
  107.0 7.7 %collective-permute-start.12 = (bf16[256,256]{1,0:T(8,128)(2,1)}, bf16[256,256]{1,0:T(8,128)(2,1)S(1)}, u32[]{:S(2)}, u32[]{:S(2)}) collective-permute-start(bf16[256,256]{1,0:T(8,128)(2,1)} %get-tuple-element.231), channel_id=1, source_target_pairs={{0,8},{8,16},{16,24},{24,28},{28,20},{20,12},{12,4},{4,0},{1,9},{9... | collective-permute-start | bytes 393224 | tf_op jit(solution)/shard_map/ppermute | solution.py:577
  107.5 7.7 %collective-permute-start.13 = (bf16[256,256]{1,0:T(8,128)(2,1)}, bf16[256,256]{1,0:T(8,128)(2,1)S(1)}, u32[]{:S(2)}, u32[]{:S(2)}) collective-permute-start(bf16[256,256]{1,0:T(8,128)(2,1)} %get-tuple-element.232), channel_id=1, source_target_pairs={{0,4},{8,0},{16,8},{24,16},{28,24},{20,28},{12,20},{4,12},{1,5},{9... | collective-permute-start | bytes 393224 | tf_op jit(solution)/shard_map/ppermute | solution.py:577
  120.5 12.1 %collective-permute-start.18 = (bf16[256,1024]{1,0:T(8,128)(2,1)S(1)}, bf16[256,1024]{1,0:T(8,128)(2,1)S(1)}, u32[]{:S(2)}, u32[]{:S(2)}) collective-permute-start(bf16[256,1024]{1,0:T(8,128)(2,1)S(1)} %copy-done.28), channel_id=1, source_target_pairs={{0,2},{2,0},{1,3},{3,1},{4,6},{6,4},{5,7},{7,5},{8,10},{10,8},{9,1... | collective-permute-start | bytes 1572872 | tf_op jit(solution)/shard_map/ppermute | solution.py:442
  120.6 12.0 %collective-permute-start.17 = (bf16[256,256]{1,0:T(8,128)(2,1)S(1)}, bf16[256,256]{1,0:T(8,128)(2,1)S(1)}, u32[]{:S(2)}, u32[]{:S(2)}) collective-permute-start(bf16[256,256]{1,0:T(8,128)(2,1)S(1)} %constant_dynamic-slice_fusion.1), channel_id=1, source_target_pairs={{0,2},{2,0},{1,3},{3,1},{4,6},{6,4},{5,7},{7,5},{8,10},{10,8},{9,1... | collective-permute-start | bytes 393224 | tf_op jit(solution)/shard_map/ppermute | solution.py:442
  121.2 14.9 %all-to-all-start.2 = ((bf16[8,64,256]{2,1,0:T(8,128)(2,1)}), bf16[8,64,256]{2,1,0:T(8,128)(2,1)S(1)}, u32[]{:S(2)}, u32[]{:S(2)}) async-start(bf16[8,64,256]{2,1,0:T(8,128)(2,1)} %bitcast.9), calls=%async_computation.2 | async-start | bytes 524288 | tf_op jit(solution)/shard_map/all_to_all | solution.py:446
  125.8 16.6 %collective-permute-start.15 = (bf16[256,1024]{1,0:T(8,128)(2,1)}, bf16[256,1024]{1,0:T(8,128)(2,1)S(1)}, u32[]{:S(2)}, u32[]{:S(2)}) collective-permute-start(bf16[256,1024]{1,0:T(8,128)(2,1)} %get-tuple-element.248), channel_id=1, source_target_pairs={{0,8},{8,16},{16,24},{24,28},{28,20},{20,12},{12,4},{4,0},{1,9},{9... | collective-permute-start | bytes 1572872 | tf_op jit(solution)/shard_map/ppermute | solution.py:635
  127.8 16.5 %collective-permute-start.16 = (bf16[256,1024]{1,0:T(8,128)(2,1)}, bf16[256,1024]{1,0:T(8,128)(2,1)S(1)}, u32[]{:S(2)}, u32[]{:S(2)}) collective-permute-start(bf16[256,1024]{1,0:T(8,128)(2,1)} %get-tuple-element.249), channel_id=1, source_target_pairs={{0,4},{8,0},{16,8},{24,16},{28,24},{20,28},{12,20},{4,12},{1,5},{9... | collective-permute-start | bytes 1572872 | tf_op jit(solution)/shard_map/ppermute | solution.py:635
  130.8 66.3 %collective-permute-start.24 = (bf16[2048,512]{1,0:T(8,128)(2,1)}, bf16[2048,512]{1,0:T(8,128)(2,1)}, u32[]{:S(2)}, u32[]{:S(2)}) collective-permute-start(bf16[2048,512]{1,0:T(8,128)(2,1)} %join.1.refs_0_), channel_id=1, source_target_pairs={{0,1},{1,0},{2,3},{3,2},{4,5},{5,4},{6,7},{7,6},{8,9},{9,8},{10,11... | collective-permute-start | bytes 6291464 | tf_op jit(solution)/shard_map/ppermute | solution.py:473
  149.1 18.8 %collective-permute-start.19 = (bf16[256,1024]{1,0:T(8,128)(2,1)}, bf16[256,1024]{1,0:T(8,128)(2,1)}, u32[]{:S(2)}, u32[]{:S(2)}) collective-permute-start(bf16[256,1024]{1,0:T(8,128)(2,1)} %get-tuple-element.258), channel_id=1, source_target_pairs={{0,8},{8,16},{16,24},{24,28},{28,20},{20,12},{12,4},{4,0},{1,9},{9... | collective-permute-start | bytes 1572872 | tf_op jit(solution)/shard_map/ppermute | solution.py:635
  151.4 16.4 %collective-permute-start.20 = (bf16[256,1024]{1,0:T(8,128)(2,1)}, bf16[256,1024]{1,0:T(8,128)(2,1)}, u32[]{:S(2)}, u32[]{:S(2)}) collective-permute-start(bf16[256,1024]{1,0:T(8,128)(2,1)} %get-tuple-element.259), channel_id=1, source_target_pairs={{0,4},{8,0},{16,8},{24,16},{28,24},{20,28},{12,20},{4,12},{1,5},{9... | collective-permute-start | bytes 1572872 | tf_op jit(solution)/shard_map/ppermute | solution.py:635
  151.4 37.9 %all-to-all-start.3 = ((bf16[8,32,1024]{2,1,0:T(8,128)(2,1)}), bf16[8,32,1024]{2,1,0:T(8,128)(2,1)}, u32[]{:S(2)}, u32[]{:S(2)}) async-start(bf16[8,32,1024]{2,1,0:T(8,128)(2,1)} %bitcast.10), calls=%async_computation.3 | async-start | bytes 1048576 | tf_op jit(solution)/shard_map/all_to_all | solution.py:446
  167.8 8.6 %collective-permute-start.23 = (bf16[8,128,256]{2,1,0:T(8,128)(2,1)S(1)}, bf16[8,128,256]{2,1,0:T(8,128)(2,1)S(1)}, u32[]{:S(2)}, u32[]{:S(2)}) collective-permute-start(bf16[8,128,256]{2,1,0:T(8,128)(2,1)S(1)} %get-tuple-element.274), channel_id=1, source_target_pairs={{0,2},{2,0},{1,3},{3,1},{4,6},{6,4},{5,7},{7,5},{8,10},{10,8},{9,1... | collective-permute-start | bytes 1572872 | tf_op jit(solution)/shard_map/ppermute | solution.py:442
  171.7 17.6 %collective-permute-start.21 = (bf16[256,1024]{1,0:T(8,128)(2,1)}, bf16[256,1024]{1,0:T(8,128)(2,1)}, u32[]{:S(2)}, u32[]{:S(2)}) collective-permute-start(bf16[256,1024]{1,0:T(8,128)(2,1)} %get-tuple-element.270), channel_id=1, source_target_pairs={{0,8},{8,16},{16,24},{24,28},{28,20},{20,12},{12,4},{4,0},{1,9},{9... | collective-permute-start | bytes 1572872 | tf_op jit(solution)/shard_map/ppermute | solution.py:635
  173.7 15.6 %collective-permute-start.22 = (bf16[256,1024]{1,0:T(8,128)(2,1)}, bf16[256,1024]{1,0:T(8,128)(2,1)}, u32[]{:S(2)}, u32[]{:S(2)}) collective-permute-start(bf16[256,1024]{1,0:T(8,128)(2,1)} %get-tuple-element.271), channel_id=1, source_target_pairs={{0,4},{8,0},{16,8},{24,16},{28,24},{20,28},{12,20},{4,12},{1,5},{9... | collective-permute-start | bytes 1572872 | tf_op jit(solution)/shard_map/ppermute | solution.py:635
  176.3 20.6 %copy-start.42 = (f32[1,2048]{1,0:T(1,128)S(1)}, f32[1,2048]{1,0:T(1,128)}, u32[]{:S(2)}) copy-start(f32[1,2048]{1,0:T(1,128)} %get-tuple-element.284) | copy-start | bytes 24580
  176.3 20.7 %copy-start.41 = (f32[4,1024]{1,0:T(4,128)S(1)}, f32[4,1024]{1,0:T(4,128)}, u32[]{:S(2)}) copy-start(f32[4,1024]{1,0:T(4,128)} %get-tuple-element.283) | copy-start | bytes 49156
  189.3 27.2 %all-to-all-start.4 = ((bf16[8,192,256]{2,1,0:T(8,128)(2,1)}), bf16[8,192,256]{2,1,0:T(8,128)(2,1)}, u32[]{:S(2)}, u32[]{:S(2)}) async-start(bf16[8,192,256]{2,1,0:T(8,128)(2,1)} %attention_backward.3.grads_ref), calls=%async_computation.4 | async-start | bytes 1572864 | tf_op jit(solution)/shard_map/all_to_all | solution.py:446
  203.0 4.9 %collective-permute-start.25 = (bf16[96,1024]{1,0:T(8,128)(2,1)S(1)}, bf16[96,1024]{1,0:T(8,128)(2,1)S(1)}, u32[]{:S(2)}, u32[]{:S(2)}) collective-permute-start(bf16[96,1024]{1,0:T(8,128)(2,1)S(1)} %constant_dynamic-slice_fusion), channel_id=1, source_target_pairs={{0,2},{2,0},{1,3},{3,1},{4,6},{6,4},{5,7},{7,5},{8,10},{10,8},{9,1... | collective-permute-start | bytes 589832 | tf_op jit(solution)/shard_map/ppermute | solution.py:442
  209.2 16.9 %collective-permute-start.28 = (bf16[400,1024]{1,0:T(8,128)(2,1)S(1)}, bf16[400,1024]{1,0:T(8,128)(2,1)}, u32[]{:S(2)}, u32[]{:S(2)}) collective-permute-start(bf16[400,1024]{1,0:T(8,128)(2,1)S(1)} %pad_maximum_fusion.refs_0_), channel_id=1, source_target_pairs={{0,2},{2,0},{1,3},{3,1},{4,6},{6,4},{5,7},{7,5},{8,10},{10,8},{9,1... | collective-permute-start | bytes 2457608 | tf_op jit(solution)/shard_map/ppermute | solution.py:442
  209.7 20.8 %collective-permute-start.26 = (bf16[400,1024]{1,0:T(8,128)(2,1)S(1)}, bf16[400,1024]{1,0:T(8,128)(2,1)}, u32[]{:S(2)}, u32[]{:S(2)}) collective-permute-start(bf16[400,1024]{1,0:T(8,128)(2,1)S(1)} %pad_maximum_fusion.refs_0_), channel_id=1, source_target_pairs={{0,8},{8,16},{16,24},{24,28},{28,20},{20,12},{12,4},{4,0},{1,9},{9... | collective-permute-start | bytes 2457608 | tf_op jit(solution)/shard_map/ppermute | solution.py:577
  211.7 21.7 %collective-permute-start.27 = (bf16[400,1024]{1,0:T(8,128)(2,1)S(1)}, bf16[400,1024]{1,0:T(8,128)(2,1)}, u32[]{:S(2)}, u32[]{:S(2)}) collective-permute-start(bf16[400,1024]{1,0:T(8,128)(2,1)S(1)} %pad_maximum_fusion.refs_0_), channel_id=1, source_target_pairs={{0,4},{8,0},{16,8},{24,16},{28,24},{20,28},{12,20},{4,12},{1,5},{9... | collective-permute-start | bytes 2457608 | tf_op jit(solution)/shard_map/ppermute | solution.py:577
  221.1 3.8 %collective-permute-start.29 = (f32[24,128]{1,0:T(8,128)S(1)}, f32[24,128]{1,0:T(8,128)S(1)}, u32[]{:S(2)}, u32[]{:S(2)}) collective-permute-start(f32[24,128]{1,0:T(8,128)S(1)} %reshape.108), channel_id=1, source_target_pairs={{0,1},{1,0},{2,3},{3,2},{4,5},{5,4},{6,7},{7,6},{8,9},{9,8},{10,11... | collective-permute-start | bytes 36872 | tf_op jit(solution)/shard_map/ppermute | solution.py:473
  224.9 1.2 collective-permute-start.30
  233.4 23.9 %copy-start.17 = (bf16[256,1024]{1,0:T(8,128)(2,1)S(1)}, bf16[256,1024]{1,0:T(8,128)(2,1)}, u32[]{:S(2)}) copy-start(bf16[256,1024]{1,0:T(8,128)(2,1)} %get-tuple-element.366) | copy-start | bytes 1572868
  233.4 26.1 %copy-start.9 = (f32[256,1024]{1,0:T(8,128)S(1)}, f32[256,1024]{1,0:T(8,128)}, u32[]{:S(2)}) copy-start(f32[256,1024]{1,0:T(8,128)} %get-tuple-element.233.hidden_ref) | copy-start | bytes 3145732
  233.4 26.1 %copy-start.43 = (f32[1024]{0:T(1024)S(1)}, f32[1024]{0:T(1024)}, u32[]{:S(2)}) copy-start(f32[1024]{0:T(1024)} %param.35) | copy-start | bytes 12292
  233.4 4.0 %collective-permute-start.33 = (bf16[400,1024]{1,0:T(8,128)(2,1)}, bf16[400,1024]{1,0:T(8,128)(2,1)S(1)}, u32[]{:S(2)}, u32[]{:S(2)}) collective-permute-start(bf16[400,1024]{1,0:T(8,128)(2,1)} %collective-permute-done.26.refs_7_), channel_id=1, source_target_pairs={{0,2},{2,0},{1,3},{3,1},{4,6},{6,4},{5,7},{7,5},{8,10},{10,8},{9,1... | collective-permute-start | bytes 2457608 | tf_op jit(solution)/shard_map/ppermute | solution.py:442
  233.4 4.3 %collective-permute-start.34 = (bf16[400,1024]{1,0:T(8,128)(2,1)}, bf16[400,1024]{1,0:T(8,128)(2,1)S(1)}, u32[]{:S(2)}, u32[]{:S(2)}) collective-permute-start(bf16[400,1024]{1,0:T(8,128)(2,1)} %collective-permute-done.27.refs_9_), channel_id=1, source_target_pairs={{0,2},{2,0},{1,3},{3,1},{4,6},{6,4},{5,7},{7,5},{8,10},{10,8},{9,1... | collective-permute-start | bytes 2457608 | tf_op jit(solution)/shard_map/ppermute | solution.py:442
  233.9 20.7 %collective-permute-start.31 = (bf16[400,1024]{1,0:T(8,128)(2,1)}, bf16[400,1024]{1,0:T(8,128)(2,1)}, u32[]{:S(2)}, u32[]{:S(2)}) collective-permute-start(bf16[400,1024]{1,0:T(8,128)(2,1)} %collective-permute-done.26.refs_7_), channel_id=1, source_target_pairs={{0,8},{8,16},{16,24},{24,28},{28,20},{20,12},{12,4},{4,0},{1,9},{9... | collective-permute-start | bytes 2457608 | tf_op jit(solution)/shard_map/ppermute | solution.py:577
  234.5 20.3 %collective-permute-start.32 = (bf16[400,1024]{1,0:T(8,128)(2,1)}, bf16[400,1024]{1,0:T(8,128)(2,1)}, u32[]{:S(2)}, u32[]{:S(2)}) collective-permute-start(bf16[400,1024]{1,0:T(8,128)(2,1)} %collective-permute-done.27.refs_9_), channel_id=1, source_target_pairs={{0,4},{8,0},{16,8},{24,16},{28,24},{20,28},{12,20},{4,12},{1,5},{9... | collective-permute-start | bytes 2457608 | tf_op jit(solution)/shard_map/ppermute | solution.py:577
  236.0 13.7 %collective-permute-start.36 = (bf16[256,1024]{1,0:T(8,128)(2,1)}, bf16[256,1024]{1,0:T(8,128)(2,1)}, u32[]{:S(2)}, u32[]{:S(2)}) collective-permute-start(bf16[256,1024]{1,0:T(8,128)(2,1)} %get-tuple-element.335), channel_id=1, source_target_pairs={{0,1},{1,0},{2,3},{3,2},{4,5},{5,4},{6,7},{7,6},{8,9},{9,8},{10,11... | collective-permute-start | bytes 1572872 | tf_op jit(solution)/shard_map/ppermute | solution.py:473
  237.5 17.2 %collective-permute-start.35 = (f32[24,128]{1,0:T(8,128)S(1)}, f32[24,128]{1,0:T(8,128)S(1)}, u32[]{:S(2)}, u32[]{:S(2)}) collective-permute-start(f32[24,128]{1,0:T(8,128)S(1)} %add.108), channel_id=1, source_target_pairs={{0,4},{4,0},{8,12},{12,8},{16,20},{20,16},{24,28},{28,24},{1,5},{5... | collective-permute-start | bytes 36872 | tf_op jit(solution)/shard_map/ppermute | solution.py:994
  254.7 4.1 %collective-permute-start.39 = (bf16[400,1024]{1,0:T(8,128)(2,1)}, bf16[400,1024]{1,0:T(8,128)(2,1)}, u32[]{:S(2)}, u32[]{:S(2)}) collective-permute-start(bf16[400,1024]{1,0:T(8,128)(2,1)} %collective-permute-done.31.refs_7_), channel_id=1, source_target_pairs={{0,2},{2,0},{1,3},{3,1},{4,6},{6,4},{5,7},{7,5},{8,10},{10,8},{9,1... | collective-permute-start | bytes 2457608 | tf_op jit(solution)/shard_map/ppermute | solution.py:442
  254.8 7.0 %collective-permute-start.40 = (bf16[400,1024]{1,0:T(8,128)(2,1)}, bf16[400,1024]{1,0:T(8,128)(2,1)}, u32[]{:S(2)}, u32[]{:S(2)}) collective-permute-start(bf16[400,1024]{1,0:T(8,128)(2,1)} %collective-permute-done.32.refs_9_), channel_id=1, source_target_pairs={{0,2},{2,0},{1,3},{3,1},{4,6},{6,4},{5,7},{7,5},{8,10},{10,8},{9,1... | collective-permute-start | bytes 2457608 | tf_op jit(solution)/shard_map/ppermute | solution.py:442
  255.3 21.1 %collective-permute-start.37 = (bf16[400,1024]{1,0:T(8,128)(2,1)}, bf16[400,1024]{1,0:T(8,128)(2,1)S(1)}, u32[]{:S(2)}, u32[]{:S(2)}) collective-permute-start(bf16[400,1024]{1,0:T(8,128)(2,1)} %collective-permute-done.31.refs_7_), channel_id=1, source_target_pairs={{0,8},{8,16},{16,24},{24,28},{28,20},{20,12},{12,4},{4,0},{1,9},{9... | collective-permute-start | bytes 2457608 | tf_op jit(solution)/shard_map/ppermute | solution.py:577
  256.0 20.4 %collective-permute-start.38 = (bf16[400,1024]{1,0:T(8,128)(2,1)}, bf16[400,1024]{1,0:T(8,128)(2,1)S(1)}, u32[]{:S(2)}, u32[]{:S(2)}) collective-permute-start(bf16[400,1024]{1,0:T(8,128)(2,1)} %collective-permute-done.32.refs_9_), channel_id=1, source_target_pairs={{0,4},{8,0},{16,8},{24,16},{28,24},{20,28},{12,20},{4,12},{1,5},{9... | collective-permute-start | bytes 2457608 | tf_op jit(solution)/shard_map/ppermute | solution.py:577
  257.3 13.4 %collective-permute-start.41 = (bf16[256,1024]{1,0:T(8,128)(2,1)S(1)}, bf16[256,1024]{1,0:T(8,128)(2,1)}, u32[]{:S(2)}, u32[]{:S(2)}) collective-permute-start(bf16[256,1024]{1,0:T(8,128)(2,1)S(1)} %copy-done.17), channel_id=1, source_target_pairs={{0,1},{1,0},{2,3},{3,2},{4,5},{5,4},{6,7},{7,6},{8,9},{9,8},{10,11... | collective-permute-start | bytes 1572872 | tf_op jit(solution)/shard_map/ppermute | solution.py:473
  258.8 17.5 %collective-permute-start.42 = (f32[24,128]{1,0:T(8,128)S(1)}, f32[24,128]{1,0:T(8,128)S(1)}, u32[]{:S(2)}, u32[]{:S(2)}) collective-permute-start(f32[24,128]{1,0:T(8,128)S(1)} %add.113), channel_id=1, source_target_pairs={{0,8},{4,12},{8,0},{12,4},{16,24},{20,28},{24,16},{28,20},{1,9},{5... | collective-permute-start | bytes 36872 | tf_op jit(solution)/shard_map/ppermute | solution.py:994
  261.8 22.2 %copy-start.40 = (f32[1024]{0:T(1024)S(1)}, f32[1024]{0:T(1024)}, u32[]{:S(2)}) copy-start(f32[1024]{0:T(1024)} %param.22) | copy-start | bytes 12292
  276.3 11.5 %collective-permute-start.45 = (bf16[400,1024]{1,0:T(8,128)(2,1)S(1)}, bf16[400,1024]{1,0:T(8,128)(2,1)}, u32[]{:S(2)}, u32[]{:S(2)}) collective-permute-start(bf16[400,1024]{1,0:T(8,128)(2,1)S(1)} %collective-permute-done.37.left.refs_7_), channel_id=1, source_target_pairs={{0,2},{2,0},{1,3},{3,1},{4,6},{6,4},{5,7},{7,5},{8,10},{10,8},{9,1... | collective-permute-start | bytes 2457608 | tf_op jit(solution)/shard_map/ppermute | solution.py:442
  276.4 11.4 %collective-permute-start.46 = (bf16[400,1024]{1,0:T(8,128)(2,1)S(1)}, bf16[400,1024]{1,0:T(8,128)(2,1)}, u32[]{:S(2)}, u32[]{:S(2)}) collective-permute-start(bf16[400,1024]{1,0:T(8,128)(2,1)S(1)} %collective-permute-done.38.right.refs_9_), channel_id=1, source_target_pairs={{0,2},{2,0},{1,3},{3,1},{4,6},{6,4},{5,7},{7,5},{8,10},{10,8},{9,1... | collective-permute-start | bytes 2457608 | tf_op jit(solution)/shard_map/ppermute | solution.py:442
  279.6 15.1 %collective-permute-start.47 = (f32[24,128]{1,0:T(8,128)S(1)}, f32[24,128]{1,0:T(8,128)S(1)}, u32[]{:S(2)}, u32[]{:S(2)}) collective-permute-start(f32[24,128]{1,0:T(8,128)S(1)} %add.116), channel_id=1, source_target_pairs={{0,16},{4,20},{8,24},{12,28},{16,0},{20,4},{24,8},{28,12},{1,17},{... | collective-permute-start | bytes 36872 | tf_op jit(solution)/shard_map/ppermute | solution.py:994
  282.0 12.8 %collective-permute-start.43 = (bf16[400,512]{1,0:T(8,128)(2,1)}, bf16[400,512]{1,0:T(8,128)(2,1)}, u32[]{:S(2)}, u32[]{:S(2)}) collective-permute-start(bf16[400,512]{1,0:T(8,128)(2,1)} %get-tuple-element.349), channel_id=1, source_target_pairs={{0,8},{8,16},{16,24},{24,28},{28,20},{20,12},{12,4},{4,0},{1,9},{9... | collective-permute-start | bytes 1228808 | tf_op jit(solution)/shard_map/ppermute | solution.py:577
  282.2 12.5 %collective-permute-start.44 = (bf16[400,512]{1,0:T(8,128)(2,1)}, bf16[400,512]{1,0:T(8,128)(2,1)}, u32[]{:S(2)}, u32[]{:S(2)}) collective-permute-start(bf16[400,512]{1,0:T(8,128)(2,1)} %get-tuple-element.350), channel_id=1, source_target_pairs={{0,4},{8,0},{16,8},{24,16},{28,24},{20,28},{12,20},{4,12},{1,5},{9... | collective-permute-start | bytes 1228808 | tf_op jit(solution)/shard_map/ppermute | solution.py:577
  294.7 2.0 collective-permute-start.48
  294.8 2.5 collective-permute-start.49
  (35 other events, 204.8 us)

commit v18 on v17

--- a/solution.py
+++ b/solution.py
@@ -17,7 +17,7 @@
 payload_rows = 3 * HD + 16
 small_rows = 16
 params = pltpu.CompilerParams(vmem_limit_bytes=48 * 2**20)
-streaming = pltpu.CompilerParams(vmem_limit_bytes=60 * 2**20)
+streaming = pltpu.CompilerParams(vmem_limit_bytes=63_400_000)
 
 
 def normalize(values):
@@ -619,6 +619,21 @@
                 pl.when(at == place)(lambda: put(output, total + part[...].astype(F32)))
 
 
+def finish_kernel(counts, _, keep_in, far_in, near, far, ahead, behind, *refs):
+    refs, output = list(refs[:-1]), refs[-1]
+    total = product(near[...], keep_in[...], 0, 0) + product(far[...], far_in[...], 0, 0)
+    total += ahead[...].astype(F32) + behind[...].astype(F32)
+    start = total.shape[0]
+    output[pl.ds(0, start), :] = total.astype(BF16)
+    for count in counts:
+        total = 0.0
+        for _ in range(count):
+            part = refs.pop(0)[...].astype(F32)
+            total += part if part.ndim == 2 else jnp.sum(part, axis=0)
+        output[pl.ds(start, total.shape[0]), :] = total.astype(BF16)
+        start += total.shape[0]
+
+
 class Reduce:
     def __init__(self, keep, far, keep_in, far_in, table):
         self.chips, self.table = lax.axis_size("chip"), table
@@ -648,9 +663,41 @@
         self.state, values = lax.optimization_barrier((self.state, values))
         return values
 
-    def finish(self):
+    def finish(self, below):
         ahead, behind = self.state
-        return self.add([(0, [(ahead, None), (behind, None)])])[0]
+        if not self.tiled:
+            rows = self.add([(0, [(ahead, None), (behind, None)])])
+            for parts in below:
+                total = jnp.zeros(parts[0].shape[-2:], F32)
+                for part in parts:
+                    part = part.astype(F32)
+                    total += part if part.ndim == 2 else jnp.sum(part, axis=0)
+                rows.append(total.astype(BF16))
+            return jnp.concatenate(rows, axis=0)
+        (rows, model), units, chips = self.sides[0].shape, self.units, self.chips
+        half = model // 2
+        arrays = [ahead, behind] + [part for parts in below for part in parts]
+        specs = [pl.BlockSpec((rows, half), lambda at, table: (0, at))] * 2
+        specs += [pl.BlockSpec((rows, units), lambda at, table: (0, table[0]))] * 2
+        for array in arrays:
+            shape = array.shape[:-1] + (half,)
+            specs.append(
+                pl.BlockSpec(shape, lambda at, table, rank=array.ndim: (0,) * (rank - 1) + (at,))
+            )
+        height = units + sum(parts[0].shape[-2] for parts in below)
+        return pl.pallas_call(
+            functools.partial(finish_kernel, [len(parts) for parts in below]),
+            grid_spec=pltpu.PrefetchScalarGridSpec(
+                num_scalar_prefetch=1,
+                grid=(2,),
+                in_specs=specs,
+                out_specs=pl.BlockSpec((height, half), lambda at, table: (0, at)),
+            ),
+            out_shape=struct((height, model), BF16),
+            compiler_params=streaming,
+            cost_estimate=light,
+            name="ring_finish",
+        )(self.table, *self.sides, *self.operands, *arrays)
 
     def add(self, wanted, split=False):
         (rows, model), units, chips = self.sides[0].shape, self.units, self.chips
@@ -798,15 +845,12 @@
 
 def head_gradient_kernel(steps, chips, table, grads_ref, *refs):
     parts, out_ref = refs[:-1], refs[-1]
-    patches = grads_ref.shape[2]
     for at, part in enumerate(parts):
 
         @pl.when(pl.program_id(0) == at)
         def _(part=part):
-            total = jnp.zeros(out_ref.shape, F32)
-            for index, step in enumerate(steps):
-                chip = table[chips + step % chips]
-                total += product(grads_ref[chip], part[pl.ds(index * patches, patches), :])
+            chosen = [grads_ref[table[chips + step % chips]] for step in steps]
+            total = product(jnp.concatenate(chosen, axis=1), part[...])
             out_ref[...] = total.astype(BF16)
 
 
@@ -893,7 +937,11 @@
     attn_out = gather_queries(out, heads, split, rows)
     attn_out = visit([inputs], attn_out)
     branches = across_heads(product(attn_out, output_weight, 0, 0).astype(BF16))
-    visit([inputs], ())
+    wide = block_input.astype(F32)
+    mean_attn = jnp.mean(wide, axis=-1, keepdims=True)
+    centred = wide - mean_attn
+    inverse_attn = lax.rsqrt(jnp.mean(centred * centred, axis=-1, keepdims=True) + eps)
+    mean_attn, inverse_attn = visit([inputs], (mean_attn, inverse_attn))
     keep, give, keep_in, give_in, hidden, dup_bias, mlp_part, d_mlp_part = mlp(
         table,
         block_input,
@@ -934,18 +982,15 @@
     )
     head_grads = ring.arrive(head_grads)
     doutput, head_grads = lax.optimization_barrier((doutput, head_grads))
-    doutput = jnp.sum(doutput.astype(F32), axis=0)
     small = jnp.concatenate([sums.reshape(-1), dup_bias[0]])
     small = jnp.pad(small, (0, small_rows * model - small.shape[0])).reshape(small_rows, model)
-    doutput = jnp.concatenate([doutput, small], axis=0).astype(BF16)
+    below = [[doutput], [small]]
     if split == 1:
         (head_grads,) = head_grads
         moved = to_heads(head_grads)
         projections = head_gradient(head_grads, parts, steps, table)
         near, far = share_halves(projections, 0)
-        projections = (near.astype(F32) + far.astype(F32)).astype(BF16)
-        size = projections.shape[0]
-        blocks = jnp.concatenate([projections, doutput], axis=0)
+        size, below = near.shape[0], [[near, far]] + below
         dquery, dkey, dvalue = (
             moved[:, at * HD : at * HD + HD].reshape(width, rows) for at in range(3)
         )
@@ -955,15 +1000,13 @@
         moved = to_heads(key_value).reshape(heads, split, 2 * HD, rows).astype(F32)
         moved = jnp.sum(moved, axis=1).astype(BF16)
         dkey, dvalue = (moved[:, at * HD : at * HD + HD].reshape(width, rows) for at in range(2))
-        size, blocks = 0, doutput
+        size = 0
         projections = [
             lax.psum(product(attn_in, grad, 0, 1).astype(BF16), ("chip", "core")).astype(F32)
             for grad in (dquery, dkey, dvalue)
         ]
-    total = ring.finish()
-    start = total.shape[0]
-    ring.size, ring.extra = size, blocks.shape[0] - size - small_rows
-    gathered = Gather(jnp.concatenate([total, blocks], axis=0), True, ring.place)
+    start, ring.size, ring.extra = ring.units, size, doutput.shape[1]
+    gathered = Gather(ring.finish(below), True, ring.place)
     gathered.send(gathered.ready)
     d_part = (
         product(dquery, query_weight, 0, 1)
@@ -971,7 +1014,7 @@
         + product(dvalue, value_weight, 0, 1)
     )
     d_in = across_heads(d_part.astype(BF16))
-    unit_attn, inverse_attn = normalize(block_input.astype(F32))
+    unit_attn = (block_input.astype(F32) - mean_attn) * inverse_attn
     onehot = (segments[:, None] == jnp.arange(crops, dtype=jnp.int32)[None, :]).astype(F32)
     lead = jnp.sum(onehot * lead_steps.astype(F32)[None, :], axis=1) / 12.0
     ends = jnp.stack(
@@ -1015,7 +1058,7 @@
         doutput_weight, small, *projections = rest
         doutput_weight = doutput_weight.reshape(width, model)
     if split != 1:
-        blocks = jnp.zeros((2, chips) + blocks.shape, F32)
+        blocks = jnp.zeros((2, chips, ring.extra + small_rows, model), F32)
         for step, near, far in gathered.pairs:
             for side, block in ((core, near), (1 - core, far)):
                 at = (side, table[chips + step % chips], 0, 0)

time: 307 us -> 305 us (level)
  blocking collectives: 42.4 us -> 29.6 us
  waiting for transfers between devices: 49.1 us -> 59.8 us
  other arithmetic: 12.9 us -> 8.44 us
    all_to_all x2 -> x1, blocking collectives: 42.4 us -> 29.6 us  [to_heads(): return lax.all_to_all(blocks, 'chip', 0, 0, tiled=True)]
    all_to_all x3 -> x4, waiting for transfers between devices: 7.18 us -> 14.3 us  [to_heads(): return lax.all_to_all(blocks, 'chip', 0, 0, tiled=True)]
    pallas_call x0 -> x1, Pallas kernels: none -> 3.91 us  [finish(): pl.pallas_call(functools.partial(finish_kernel, [len(parts) for parts in...]
    pallas_call x5 -> x4, Pallas kernels: 19.2 us -> 15.4 us  [add(): pl.pallas_call(functools.partial(add_kernel, places, len(shapes)), grid_s...]
    reduce_sum x3 -> x2, other arithmetic: 3.72 us -> 0.43 us  [the longest x1 0.28 us: local(): jnp.mean(centred * centred, axis=-1, keepdims=True) + eps]
    all_to_all x3 -> x4, starting transfers between devices: 16.5 us -> 19.1 us  [to_heads(): return lax.all_to_all(blocks, 'chip', 0, 0, tiled=True)]
    unnamed x95 -> x93, local copies, waits for them, and re-layouts: 10.6 us -> 10.7 us
  transfers between devices with their start and end apart: 53 -> 54, of which waited for: 22 -> 26; matrix products, arithmetic and copies ran while one was open for 6% -> 5% of each run, Pallas kernels for 35% -> 36%
where the time goes in v18:
time: 305 us; the launch traced here: 304 us
  Pallas kernels  124 us (41%)
  starting transfers between devices  60.5 us (20%)
  waiting for transfers between devices  59.8 us (20%)
  blocking collectives  29.6 us (10%)
  local copies, waits for them, and re-layouts  15 us (5%)
  other arithmetic  8.44 us (3%)
  matrix products  5.35 us (2%)
    pallas_call x5, Pallas kernels, place(): pl.pallas_call(functools.partial(place_kernel, heads, len(blocks[0]) // 2...  30.2 us
    all_to_all x1, blocking collectives, to_heads(): return lax.all_to_all(blocks, 'chip', 0, 0, tiled=True)  29.6 us
    pallas_call x2, Pallas kernels, attention_backward(): pl.pallas_call(functools.partial(backward_kernel, crops, len(extras)), gr...  24.9 us
    ppermute x24, starting transfers between devices, send(): lax.ppermute(block, 'chip', ring_pairs(direction))  24.8 us
    ppermute x24, waiting for transfers between devices, send(): lax.ppermute(block, 'chip', ring_pairs(direction))  20.6 us
    all_to_all x4, starting transfers between devices, to_heads(): return lax.all_to_all(blocks, 'chip', 0, 0, tiled=True)  19.1 us
    pallas_call x4, Pallas kernels, add(): pl.pallas_call(functools.partial(add_kernel, places, len(shapes)), grid_s...  15.4 us
    pallas_call x1, Pallas kernels, attention_forward(): pl.pallas_call(functools.partial(forward_kernel, crops, key_step(count)),...  15.3 us
  transfers between devices with their start and end apart: 54, of which 26 were waited for; matrix products, arithmetic and copies ran while one was open for 5% of the time, Pallas kernels for 36%

profile of v18, /device:TPU:0, one launch (start us, length us, event | category | flops | bytes accessed | tf_op | source)
XLA Modules:
  0.0 304.0 jit_solution(4242647575179261140)
XLA Ops:
  1.2 6.6 %project.1 = (bf16[8,208,256]{2,1,0:T(8,128)(2,1)}, bf16[256,1024]{1,0:T(8,128)(2,1)}, bf16[256,512]{1,0:T(8,128)(2,1)}) custom-call(s32[18]{0:T(128)} %compare_select_fusion.5.table.core_ref._, bf16[256,1024]{1,0:T(8,128)(2,1)} %input_ref.3, s32[1,256]{1,0:T(1,128)} %bitcast.79, s32[32]{0:T(128)} %steps_ref.1, f32[1,1024]{1,0:T(1,128)} %bitcast.61, ...), custom_call_target="tpu_custom_call" | custom-call | flops 1 | bytes 1 | tf_op jit(solution)/shard_map/project/pallas_call | solution.py:94
  7.8 29.6 %all_to_all.25.query_ref.own.piece = bf16[8,208,256]{2,1,0:T(8,128)(2,1)S(1)} all-to-all(bf16[8,208,256]{2,1,0:T(8,128)(2,1)} %get-tuple-element.207), channel_id=1, replica_groups=mesh['chip'=8,'core'=2,'head'=2] {'chip'}, dimensions={0} | all-to-all | bytes 1703936 | tf_op jit(solution)/shard_map/all_to_all | solution.py:446
  40.7 15.3 %attention_forward.1 = (f32[8,64,256]{2,1,0:T(8,128)}, bf16[8,64,256]{2,1,0:T(8,128)(2,1)}, f32[8,1,256]{2,1,0:T(1,128)}) custom-call(bf16[8,208,256]{2,1,0:T(8,128)(2,1)} %copy-done, bf16[8,208,256]{2,1,0:T(8,128)(2,1)} %copy-done, bf16[8,208,256]{2,1,0:T(8,128)(2,1)} %copy-done.2), custom_call_target="tpu_custom_call" | custom-call | flops 1 | bytes 1 | tf_op jit(solution)/shard_map/attention_forward/pallas_call | solution.py:378
  56.1 3.4 %all-to-all-start.1 = ((bf16[8,64,256]{2,1,0:T(8,128)(2,1)}), bf16[8,64,256]{2,1,0:T(8,128)(2,1)S(1)}, u32[]{:S(2)}, u32[]{:S(2)}) async-start(bf16[8,64,256]{2,1,0:T(8,128)(2,1)} %get-tuple-element.214), calls=%async_computation.1 | async-start | bytes 524288 | tf_op jit(solution)/shard_map/all_to_all | solution.py:446
  59.7 9.3 %all-to-all-done.1 = bf16[8,64,256]{2,1,0:T(8,128)(2,1)S(1)} async-done(((bf16[8,64,256]{2,1,0:T(8,128)(2,1)}), bf16[8,64,256]{2,1,0:T(8,128)(2,1)S(1)}, u32[]{:S(2)}, u32[]{:S(2)}) %all-to-all-start.1) | async-done | bytes 262176 | tf_op jit(solution)/shard_map/all_to_all | solution.py:446
  69.4 1.6 collective-permute-start.7
  73.3 4.4 %collective-permute-done.3.refs_3_ = bf16[256,512]{1,0:T(8,128)(2,1)S(1)} collective-permute-done((bf16[256,512]{1,0:T(8,128)(2,1)S(1)}, bf16[256,512]{1,0:T(8,128)(2,1)S(1)}, u32[]{:S(2)}, u32[]{:S(2)}) %collective-permute-start.3) | collective-permute-done | bytes 262176 | tf_op jit(solution)/shard_map/ppermute | solution.py:577
  78.6 1.4 collective-permute-start.5
  80.6 1.4 collective-permute-done.7.refs_1_
  82.8 11.7 %mlp.1 = (bf16[256,2048]{1,0:T(8,128)(2,1)}, bf16[256,2048]{1,0:T(8,128)(2,1)}, bf16[256,1024]{1,0:T(8,128)(2,1)}, bf16[256,1024]{1,0:T(8,128)(2,1)}, f32[256,10...) custom-call(s32[18]{0:T(128)} %compare_select_fusion.5.table.core_ref._, ...), custom_call_target="tpu_custom_call" | custom-call | flops 1 | bytes 1 | tf_op jit(solution)/shard_map/mlp/pallas_call | solution.py:174
  95.2 1.5 collective-permute-start.14
  96.7 1.6 collective-permute-done.8.refs_1_.far_in
  100.1 3.3 %ring_add.4 = (bf16[256,512]{1,0:T(8,128)(2,1)}, bf16[256,512]{1,0:T(8,128)(2,1)}) custom-call(s32[18]{0:T(128)} %compare_select_fusion.5.table.core_ref._, bf16[256,1024]{1,0:T(8,128)(2,1)} %get-tuple-element.225.refs_0_.keep_in, bf16[256,1024]{1,0:T(8,128)(2,1)} %copy-done.9, bf16[256,2048]{1,0:T(8,128)(2,1)} %get-tuple-element.227.refs_2_.refs_5_.near, ...), custom_call_target="tpu_custom_call" | custom-call | flops 1 | bytes 1 | tf_op jit(solution)/shard_map/ring_add/pallas_call | solution.py:732
  103.6 1.8 collective-permute-start.11
  105.4 1.7 halves.2
  107.6 1.6 collective-permute-start.13
  110.1 4.3 %middle.1 = (f32[256,1024]{1,0:T(8,128)}, bf16[256,1024]{1,0:T(8,128)(2,1)}, bf16[512,256]{1,0:T(8,128)(2,1)}, f32[4,1024]{1,0:T(4,128)}) custom-call(f32[256,1024]{1,0:T(8,128)} %get-tuple-element.235.hidden_ref, bf16[256,1024]{1,0:T(8,128)(2,1)} %grad_ref.3, bf16[256,1024]{1,0:T(8,128)(2,1)} %get-tuple-element.238.refs_0_, bf16[256,1024]{1,0:T(8,128)(2,1)} %copy-done.27, ...), custom_call_target="tpu_custom_call" | custom-call | flops 1 | bytes 1 | tf_op jit(solution)/shard_map/middle/pallas_call | solution.py:235
  116.0 4.3 %ring_add.5 = (bf16[256,1024]{1,0:T(8,128)(2,1)}, bf16[256,1024]{1,0:T(8,128)(2,1)}) custom-call(s32[18]{0:T(128)} %compare_select_fusion.5.table.core_ref._, bf16[256,1024]{1,0:T(8,128)(2,1)} %get-tuple-element.225.refs_0_.keep_in, bf16[256,1024]{1,0:T(8,128)(2,1)} %copy-done.9, bf16[256,2048]{1,0:T(8,128)(2,1)} %get-tuple-element.227.refs_2_.refs_5_.near, ...), custom_call_target="tpu_custom_call" | custom-call | flops 1 | bytes 1 | tf_op jit(solution)/shard_map/ring_add/pallas_call | solution.py:732
  121.5 4.6 %all-to-all-start.2 = ((bf16[8,64,256]{2,1,0:T(8,128)(2,1)}), bf16[8,64,256]{2,1,0:T(8,128)(2,1)S(1)}, u32[]{:S(2)}, u32[]{:S(2)}) async-start(bf16[8,64,256]{2,1,0:T(8,128)(2,1)} %bitcast.11), calls=%async_computation.2 | async-start | bytes 524288 | tf_op jit(solution)/shard_map/all_to_all | solution.py:446
  126.1 2.0 collective-permute-start.15
  128.1 1.3 fusion.14
  129.5 3.0 join.1.refs_0_
  132.5 1.5 collective-permute-start.24
  136.4 6.3 %collective-permute-done.15.refs_4_ = bf16[256,1024]{1,0:T(8,128)(2,1)S(1)} collective-permute-done((bf16[256,1024]{1,0:T(8,128)(2,1)}, bf16[256,1024]{1,0:T(8,128)(2,1)S(1)}, u32[]{:S(2)}, u32[]{:S(2)}) %collective-permute-start.15) | collective-permute-done | bytes 524320 | tf_op jit(solution)/shard_map/ppermute | solution.py:650
  142.7 1.9 collective-permute-done.16.refs_7_
  145.4 4.0 %ring_add.6 = (bf16[256,1024]{1,0:T(8,128)(2,1)}, bf16[256,1024]{1,0:T(8,128)(2,1)}) custom-call(s32[18]{0:T(128)} %compare_select_fusion.5.table.core_ref._, bf16[256,1024]{1,0:T(8,128)(2,1)} %get-tuple-element.225.refs_0_.keep_in, bf16[256,1024]{1,0:T(8,128)(2,1)} %copy-done.9, bf16[256,2048]{1,0:T(8,128)(2,1)} %get-tuple-element.227.refs_2_.refs_5_.near, ...), custom_call_target="tpu_custom_call" | custom-call | flops 1 | bytes 1 | tf_op jit(solution)/shard_map/ring_add/pallas_call | solution.py:732
  149.4 2.3 collective-permute-start.19
  151.7 5.0 %all-to-all-start.3 = ((bf16[8,32,1024]{2,1,0:T(8,128)(2,1)}), bf16[8,32,1024]{2,1,0:T(8,128)(2,1)}, u32[]{:S(2)}, u32[]{:S(2)}) async-start(bf16[8,32,1024]{2,1,0:T(8,128)(2,1)} %bitcast.12), calls=%async_computation.3 | async-start | bytes 1048576 | tf_op jit(solution)/shard_map/all_to_all | solution.py:446
  156.7 11.9 %attention_backward.2 = (f32[8,64,256]{2,1,0:T(8,128)S(1)}, bf16[8,128,256]{2,1,0:T(8,128)(2,1)S(1)}) custom-call(bf16[8,208,256]{2,1,0:T(8,128)(2,1)S(1)} %copy-done.1, bf16[8,64,256]{2,1,0:T(8,128)(2,1)S(1)} %all-to-all-done.2.grad_ref, f32[8,64,256]{2,1,0:T(8,128)S(1)} %copy-done.4, f32[8,1,256]{2,1,0:T(1,128)S(1)} %copy-done.5, ...), custom_call_target="tpu_custom_call" | custom-call | flops 1 | bytes 1 | tf_op jit(solution)/shard_map/attention_backward/pallas_call | solution.py:416
  168.8 3.8 %ring_add.7 = (bf16[256,1024]{1,0:T(8,128)(2,1)}, bf16[256,1024]{1,0:T(8,128)(2,1)}) custom-call(s32[18]{0:T(128)} %compare_select_fusion.5.table.core_ref._, bf16[256,1024]{1,0:T(8,128)(2,1)} %get-tuple-element.225.refs_0_.keep_in, bf16[256,1024]{1,0:T(8,128)(2,1)} %copy-done.9, bf16[256,2048]{1,0:T(8,128)(2,1)} %get-tuple-element.227.refs_2_.refs_5_.near, ...), custom_call_target="tpu_custom_call" | custom-call | flops 1 | bytes 1 | tf_op jit(solution)/shard_map/ring_add/pallas_call | solution.py:732
  172.6 2.1 collective-permute-start.21
  174.8 12.9 %attention_backward.3.grads_ref = bf16[8,192,256]{2,1,0:T(8,128)(2,1)} custom-call(bf16[8,208,256]{2,1,0:T(8,128)(2,1)S(1)} %copy-done.1, bf16[8,64,256]{2,1,0:T(8,128)(2,1)S(1)} %all-to-all-done.2.grad_ref, f32[8,64,256]{2,1,0:T(8,128)S(1)} %copy-done.4, f32[8,1,256]{2,1,0:T(1,128)S(1)} %copy-done.5, bf16[8,208,256]{2,1,0:T(8,128)(2,1)S(1)} %copy-done.1, ...), custom_call_target="tpu_custom_call" | custom-call | flops 1 | bytes 1 | tf_op jit(solution)/shard_map/attention_backward/pallas_call | solution.py:416
  187.7 1.3 collective-permute-done.22.behind
  189.0 6.1 %all-to-all-start.4 = ((bf16[8,192,256]{2,1,0:T(8,128)(2,1)}), bf16[8,192,256]{2,1,0:T(8,128)(2,1)S(1)}, u32[]{:S(2)}, u32[]{:S(2)}) async-start(bf16[8,192,256]{2,1,0:T(8,128)(2,1)} %attention_backward.3.grads_ref), calls=%async_computation.4 | async-start | bytes 1572864 | tf_op jit(solution)/shard_map/all_to_all | solution.py:446
  195.3 5.0 %head_gradient.1 = bf16[192,1024]{1,0:T(8,128)(2,1)} custom-call(s32[18]{0:T(128)} %compare_select_fusion.5.table.core_ref._, bf16[8,192,256]{2,1,0:T(8,128)(2,1)} %attention_backward.3.grads_ref, bf16[2048,512]{1,0:T(8,128)(2,1)} %join.1.refs_0_, bf16[2048,512]{1,0:T(8,128)(2,1)} %collective-permute-done.24.refs_1_), custom_call_target="tpu_custom_call" | custom-call | flops 1 | bytes 1 | tf_op jit(solution)/shard_map/head_gradient/pallas_call | solution.py:865
  200.3 1.7 constant_dynamic-slice_fusion
  204.1 3.9 %ring_finish.1.refs_0_ = bf16[400,1024]{1,0:T(8,128)(2,1)} custom-call(s32[18]{0:T(128)} %compare_select_fusion.5.table.core_ref._, bf16[256,1024]{1,0:T(8,128)(2,1)} %get-tuple-element.225.refs_0_.keep_in, bf16[256,1024]{1,0:T(8,128)(2,1)} %copy-done.9, bf16[256,2048]{1,0:T(8,128)(2,1)} %get-tuple-element.227.refs_2_.refs_5_.near, ...), custom_call_target="tpu_custom_call" | custom-call | flops 1 | bytes 1 | tf_op jit(solution)/shard_map/ring_finish/pallas_call | solution.py:688
  208.3 2.0 collective-permute-start.26
  210.3 3.8 %all-to-all-done.4 = bf16[8,192,256]{2,1,0:T(8,128)(2,1)S(1)} async-done(((bf16[8,192,256]{2,1,0:T(8,128)(2,1)}), bf16[8,192,256]{2,1,0:T(8,128)(2,1)S(1)}, u32[]{:S(2)}, u32[]{:S(2)}) %all-to-all-start.4) | async-done | bytes 786464 | tf_op jit(solution)/shard_map/all_to_all | solution.py:446
  216.0 1.5 fusion.7
  217.6 1.6 collective-permute-start.29
  219.1 2.2 collective-permute-done.29
  222.5 4.5 %place.5 = (f32[2048,1024]{1,0:T(8,128)}, f32[1024,2048]{1,0:T(8,128)}, f32[2,8,32,1024]{3,2,1,0:T(8,128)}, f32[8,2,16,1024]{3,2,1,0:T(8,128)}, f32[1024,512]{1,...) custom-call(s32[18]{0:T(128)} %compare_select_fusion.5.table.core_ref._, bf16[400,1024]{1,0:T(8,128)(2,1)} %ring_finish.1.refs_0_, ...), custom_call_target="tpu_custom_call" | custom-call | flops 1 | bytes 1 | tf_op jit(solution)/shard_map/place/pallas_call | solution.py:778
  227.0 2.4 collective-permute-done.26.refs_7_
  229.4 2.3 collective-permute-done.27.refs_9_
  232.8 1.4 collective-permute-start.32
  234.2 1.5 collective-permute-start.36
  237.5 6.9 %place.6 = (f32[2048,1024]{1,0:T(8,128)}, f32[1024,2048]{1,0:T(8,128)}, f32[2,8,32,1024]{3,2,1,0:T(8,128)}, f32[8,2,16,1024]{3,2,1,0:T(8,128)}, f32[1024,512]{1,...) custom-call(s32[18]{0:T(128)} %compare_select_fusion.5.table.core_re, ...), custom_call_target="tpu_custom_call", output_to_operand_aliasing={{0}: (1, {}), {1}: (2, {}), {2}: (3, {}), {3}: (4, {}), {4}... | custom-call | flops 1 | bytes 1 | tf_op jit(solution)/shard_map/place/pallas_call | solution.py:778
  244.4 3.4 %collective-permute-done.36 = bf16[256,1024]{1,0:T(8,128)(2,1)} collective-permute-done((bf16[256,1024]{1,0:T(8,128)(2,1)}, bf16[256,1024]{1,0:T(8,128)(2,1)}, u32[]{:S(2)}, u32[]{:S(2)}) %collective-permute-start.36) | collective-permute-done | bytes 524320 | tf_op jit(solution)/shard_map/ppermute | solution.py:473
  247.8 5.0 %collective-permute-done.35 = f32[24,128]{1,0:T(8,128)S(1)} collective-permute-done((f32[24,128]{1,0:T(8,128)S(1)}, f32[24,128]{1,0:T(8,128)S(1)}, u32[]{:S(2)}, u32[]{:S(2)}) %collective-permute-start.35) | collective-permute-done | bytes 12320 | tf_op jit(solution)/shard_map/ppermute | solution.py:1037
  253.6 1.5 collective-permute-start.37
  255.6 1.5 collective-permute-start.41
  257.1 1.5 collective-permute-start.42
  258.6 2.2 add_convert_fusion
  260.9 7.0 %place.7 = (f32[2048,1024]{1,0:T(8,128)}, f32[1024,2048]{1,0:T(8,128)}, f32[2,8,32,1024]{3,2,1,0:T(8,128)}, f32[8,2,16,1024]{3,2,1,0:T(8,128)}, f32[1024,512]{1,...) custom-call(s32[18]{0:T(128)} %compare_select_fusion.5.table.core_re, ...), custom_call_target="tpu_custom_call", output_to_operand_aliasing={{0}: (1, {}), {1}: (2, {}), {2}: (3, {}), {3}: (4, {}), {4}... | custom-call | flops 1 | bytes 1 | tf_op jit(solution)/shard_map/place/pallas_call | solution.py:778
  267.9 1.3 collective-permute-done.41
  269.2 6.2 %collective-permute-done.42 = f32[24,128]{1,0:T(8,128)S(1)} collective-permute-done((f32[24,128]{1,0:T(8,128)S(1)}, f32[24,128]{1,0:T(8,128)S(1)}, u32[]{:S(2)}, u32[]{:S(2)}) %collective-permute-start.42) | collective-permute-done | bytes 12320 | tf_op jit(solution)/shard_map/ppermute | solution.py:1037
  276.6 2.1 halves.3
  278.6 1.7 collective-permute-start.47
  280.6 1.7 collective-permute-start.44
  282.4 1.5 fusion.13
  283.9 2.3 fusion.12
  286.2 6.9 %place.8 = (f32[2048,1024]{1,0:T(8,128)}, f32[1024,2048]{1,0:T(8,128)}, f32[2,8,32,1024]{3,2,1,0:T(8,128)}, f32[8,2,16,1024]{3,2,1,0:T(8,128)}, f32[1024,512]{1,...) custom-call(s32[18]{0:T(128)} %compare_select_fusion.5.table.core_re, ...), custom_call_target="tpu_custom_call", output_to_operand_aliasing={{0}: (1, {}), {1}: (2, {}), {2}: (3, {}), {3}: (4, {}), {4}... | custom-call | flops 1 | bytes 1 | tf_op jit(solution)/shard_map/place/pallas_call | solution.py:778
  296.5 5.0 %place.9 = (f32[2048,1024]{1,0:T(8,128)}, f32[1024,2048]{1,0:T(8,128)}, f32[2,8,32,1024]{3,2,1,0:T(8,128)}, f32[8,2,16,1024]{3,2,1,0:T(8,128)}, f32[1024,512]{1,...) custom-call(s32[18]{0:T(128)} %compare_select_fusion.5.table.core_re, ...), custom_call_target="tpu_custom_call", output_to_operand_aliasing={{0}: (1, {}), {1}: (2, {}), {2}: (3, {}), {3}: (4, {}), {4}... | custom-call | flops 1 | bytes 1 | tf_op jit(solution)/shard_map/place/pallas_call | solution.py:778
  (191 shorter events, 36.5 us)
Async XLA Ops:
  7.8 51.7 %copy-start.7 = (bf16[256,1024]{1,0:T(8,128)(2,1)S(1)}, bf16[256,1024]{1,0:T(8,128)(2,1)}, u32[]{:S(2)}) copy-start(bf16[256,1024]{1,0:T(8,128)(2,1)} %input_ref.3) | copy-start | bytes 1572868
  37.4 31.5 %copy-start.11 = (bf16[512,1024]{1,0:T(8,128)(2,1)S(1)}, bf16[512,1024]{1,0:T(8,128)(2,1)}, u32[]{:S(2)}) copy-start(bf16[512,1024]{1,0:T(8,128)(2,1)} %refs_3_.1) | copy-start | bytes 3145732
  37.5 2.4 collective-permute-start.2
  37.5 18.6 %collective-permute-start = (bf16[256,512]{1,0:T(8,128)(2,1)}, bf16[256,512]{1,0:T(8,128)(2,1)S(1)}, u32[]{:S(2)}, u32[]{:S(2)}) collective-permute-start(bf16[256,512]{1,0:T(8,128)(2,1)} %get-tuple-element.209.refs_0_), channel_id=1, source_target_pairs={{0,8},{8,16},{16,24},{24,28},{28,20},{20,12},{12,4},{4,0},{1,9},{9... | collective-permute-start | bytes 786440 | tf_op jit(solution)/shard_map/ppermute | solution.py:577
  38.2 17.8 %collective-permute-start.1 = (bf16[256,512]{1,0:T(8,128)(2,1)}, bf16[256,512]{1,0:T(8,128)(2,1)}, u32[]{:S(2)}, u32[]{:S(2)}) collective-permute-start(bf16[256,512]{1,0:T(8,128)(2,1)} %get-tuple-element.209.refs_0_), channel_id=1, source_target_pairs={{0,4},{8,0},{16,8},{24,16},{28,24},{20,28},{12,20},{4,12},{1,5},{9... | collective-permute-start | bytes 786440 | tf_op jit(solution)/shard_map/ppermute | solution.py:577
  56.0 38.5 %copy-start.31 = (bf16[256,512]{1,0:T(8,128)(2,1)}, bf16[256,512]{1,0:T(8,128)(2,1)S(1)}, u32[]{:S(2)}) copy-start(bf16[256,512]{1,0:T(8,128)(2,1)S(1)} %collective-permute-done.refs_1_) | copy-start | bytes 786436
  56.1 12.9 %all-to-all-start.1 = ((bf16[8,64,256]{2,1,0:T(8,128)(2,1)}), bf16[8,64,256]{2,1,0:T(8,128)(2,1)S(1)}, u32[]{:S(2)}, u32[]{:S(2)}) async-start(bf16[8,64,256]{2,1,0:T(8,128)(2,1)} %get-tuple-element.214), calls=%async_computation.1 | async-start | bytes 524288 | tf_op jit(solution)/shard_map/all_to_all | solution.py:446
  69.4 12.6 %collective-permute-start.7 = (bf16[256,1024]{1,0:T(8,128)(2,1)S(1)}, bf16[256,1024]{1,0:T(8,128)(2,1)S(1)}, u32[]{:S(2)}, u32[]{:S(2)}) collective-permute-start(bf16[256,1024]{1,0:T(8,128)(2,1)S(1)} %convolution_convert_fusion.refs_0_), channel_id=1, source_target_pairs={{0,1},{1,0},{2,3},{3,2},{4,5},{5,4},{6,7},{7,6},{8,9},{9,8},{10,11... | collective-permute-start | bytes 1572872 | tf_op jit(solution)/shard_map/ppermute | solution.py:473
  71.0 6.7 %collective-permute-start.3 = (bf16[256,512]{1,0:T(8,128)(2,1)S(1)}, bf16[256,512]{1,0:T(8,128)(2,1)S(1)}, u32[]{:S(2)}, u32[]{:S(2)}) collective-permute-start(bf16[256,512]{1,0:T(8,128)(2,1)S(1)} %collective-permute-done.refs_1_), channel_id=1, source_target_pairs={{0,8},{8,16},{16,24},{24,28},{28,20},{20,12},{12,4},{4,0},{1,9},{9... | collective-permute-start | bytes 786440 | tf_op jit(solution)/shard_map/ppermute | solution.py:577
  72.0 6.6 %collective-permute-start.4 = (bf16[256,512]{1,0:T(8,128)(2,1)}, bf16[256,512]{1,0:T(8,128)(2,1)S(1)}, u32[]{:S(2)}, u32[]{:S(2)}) collective-permute-start(bf16[256,512]{1,0:T(8,128)(2,1)} %collective-permute-done.1.refs_2_), channel_id=1, source_target_pairs={{0,4},{8,0},{16,8},{24,16},{28,24},{20,28},{12,20},{4,12},{1,5},{9... | collective-permute-start | bytes 786440 | tf_op jit(solution)/shard_map/ppermute | solution.py:577
  77.7 25.7 %copy-start.32 = (bf16[256,512]{1,0:T(8,128)(2,1)}, bf16[256,512]{1,0:T(8,128)(2,1)S(1)}, u32[]{:S(2)}) copy-start(bf16[256,512]{1,0:T(8,128)(2,1)S(1)} %collective-permute-done.3.refs_3_) | copy-start | bytes 786436
  78.6 15.9 %collective-permute-start.5 = (bf16[256,512]{1,0:T(8,128)(2,1)S(1)}, bf16[256,512]{1,0:T(8,128)(2,1)S(1)}, u32[]{:S(2)}, u32[]{:S(2)}) collective-permute-start(bf16[256,512]{1,0:T(8,128)(2,1)S(1)} %collective-permute-done.3.refs_3_), channel_id=1, source_target_pairs={{0,8},{8,16},{16,24},{24,28},{28,20},{20,12},{12,4},{4,0},{1,9},{9... | collective-permute-start | bytes 786440 | tf_op jit(solution)/shard_map/ppermute | solution.py:577
  80.1 14.5 %collective-permute-start.6 = (bf16[256,512]{1,0:T(8,128)(2,1)S(1)}, bf16[256,512]{1,0:T(8,128)(2,1)S(1)}, u32[]{:S(2)}, u32[]{:S(2)}) collective-permute-start(bf16[256,512]{1,0:T(8,128)(2,1)S(1)} %collective-permute-done.4.refs_4_), channel_id=1, source_target_pairs={{0,4},{8,0},{16,8},{24,16},{28,24},{20,28},{12,20},{4,12},{1,5},{9... | collective-permute-start | bytes 786440 | tf_op jit(solution)/shard_map/ppermute | solution.py:577
  94.6 3.7 %collective-permute-start.9 = (bf16[256,2048]{1,0:T(8,128)(2,1)}, bf16[256,2048]{1,0:T(8,128)(2,1)S(1)}, u32[]{:S(2)}, u32[]{:S(2)}) collective-permute-start(bf16[256,2048]{1,0:T(8,128)(2,1)} %get-tuple-element.228), channel_id=1, source_target_pairs={{0,2},{2,0},{1,3},{3,1},{4,6},{6,4},{5,7},{7,5},{8,10},{10,8},{9,1... | collective-permute-start | bytes 3145736 | tf_op jit(solution)/shard_map/ppermute | solution.py:442
  94.7 3.6 %collective-permute-start.8 = (bf16[256,1024]{1,0:T(8,128)(2,1)}, bf16[256,1024]{1,0:T(8,128)(2,1)S(1)}, u32[]{:S(2)}, u32[]{:S(2)}) collective-permute-start(bf16[256,1024]{1,0:T(8,128)(2,1)} %get-tuple-element.226), channel_id=1, source_target_pairs={{0,2},{2,0},{1,3},{3,1},{4,6},{6,4},{5,7},{7,5},{8,10},{10,8},{9,1... | collective-permute-start | bytes 1572872 | tf_op jit(solution)/shard_map/ppermute | solution.py:442
  95.2 14.1 %collective-permute-start.14 = (bf16[256,1024]{1,0:T(8,128)(2,1)}, bf16[256,1024]{1,0:T(8,128)(2,1)S(1)}, u32[]{:S(2)}, u32[]{:S(2)}) collective-permute-start(bf16[256,1024]{1,0:T(8,128)(2,1)} %get-tuple-element.238.refs_0_), channel_id=1, source_target_pairs={{0,1},{1,0},{2,3},{3,2},{4,5},{5,4},{6,7},{7,6},{8,9},{9,8},{10,11... | collective-permute-start | bytes 1572872 | tf_op jit(solution)/shard_map/ppermute | solution.py:473
  103.4 11.8 %collective-permute-start.10 = (bf16[256,512]{1,0:T(8,128)(2,1)}, bf16[256,512]{1,0:T(8,128)(2,1)S(1)}, u32[]{:S(2)}, u32[]{:S(2)}) collective-permute-start(bf16[256,512]{1,0:T(8,128)(2,1)} %get-tuple-element.229), channel_id=1, source_target_pairs={{0,8},{8,16},{16,24},{24,28},{28,20},{20,12},{12,4},{4,0},{1,9},{9... | collective-permute-start | bytes 786440 | tf_op jit(solution)/shard_map/ppermute | solution.py:650
  103.6 11.5 %collective-permute-start.11 = (bf16[256,512]{1,0:T(8,128)(2,1)}, bf16[256,512]{1,0:T(8,128)(2,1)S(1)}, u32[]{:S(2)}, u32[]{:S(2)}) collective-permute-start(bf16[256,512]{1,0:T(8,128)(2,1)} %get-tuple-element.230), channel_id=1, source_target_pairs={{0,4},{8,0},{16,8},{24,16},{28,24},{20,28},{12,20},{4,12},{1,5},{9... | collective-permute-start | bytes 786440 | tf_op jit(solution)/shard_map/ppermute | solution.py:650
  107.1 7.6 %collective-permute-start.12 = (bf16[256,256]{1,0:T(8,128)(2,1)}, bf16[256,256]{1,0:T(8,128)(2,1)S(1)}, u32[]{:S(2)}, u32[]{:S(2)}) collective-permute-start(bf16[256,256]{1,0:T(8,128)(2,1)} %get-tuple-element.233), channel_id=1, source_target_pairs={{0,8},{8,16},{16,24},{24,28},{28,20},{20,12},{12,4},{4,0},{1,9},{9... | collective-permute-start | bytes 393224 | tf_op jit(solution)/shard_map/ppermute | solution.py:577
  107.6 7.6 %collective-permute-start.13 = (bf16[256,256]{1,0:T(8,128)(2,1)}, bf16[256,256]{1,0:T(8,128)(2,1)S(1)}, u32[]{:S(2)}, u32[]{:S(2)}) collective-permute-start(bf16[256,256]{1,0:T(8,128)(2,1)} %get-tuple-element.234), channel_id=1, source_target_pairs={{0,4},{8,0},{16,8},{24,16},{28,24},{20,28},{12,20},{4,12},{1,5},{9... | collective-permute-start | bytes 393224 | tf_op jit(solution)/shard_map/ppermute | solution.py:577
  120.3 13.7 %collective-permute-start.18 = (bf16[256,1024]{1,0:T(8,128)(2,1)}, bf16[256,1024]{1,0:T(8,128)(2,1)S(1)}, u32[]{:S(2)}, u32[]{:S(2)}) collective-permute-start(bf16[256,1024]{1,0:T(8,128)(2,1)} %get-tuple-element.253), channel_id=1, source_target_pairs={{0,2},{2,0},{1,3},{3,1},{4,6},{6,4},{5,7},{7,5},{8,10},{10,8},{9,1... | collective-permute-start | bytes 1572872 | tf_op jit(solution)/shard_map/ppermute | solution.py:442
  121.0 13.0 %collective-permute-start.17 = (bf16[256,256]{1,0:T(8,128)(2,1)}, bf16[256,256]{1,0:T(8,128)(2,1)S(1)}, u32[]{:S(2)}, u32[]{:S(2)}) collective-permute-start(bf16[256,256]{1,0:T(8,128)(2,1)} %constant_dynamic-slice_fusion.2), channel_id=1, source_target_pairs={{0,2},{2,0},{1,3},{3,1},{4,6},{6,4},{5,7},{7,5},{8,10},{10,8},{9,1... | collective-permute-start | bytes 393224 | tf_op jit(solution)/shard_map/ppermute | solution.py:442
  121.5 14.9 %all-to-all-start.2 = ((bf16[8,64,256]{2,1,0:T(8,128)(2,1)}), bf16[8,64,256]{2,1,0:T(8,128)(2,1)S(1)}, u32[]{:S(2)}, u32[]{:S(2)}) async-start(bf16[8,64,256]{2,1,0:T(8,128)(2,1)} %bitcast.11), calls=%async_computation.2 | async-start | bytes 524288 | tf_op jit(solution)/shard_map/all_to_all | solution.py:446
  126.1 16.6 %collective-permute-start.15 = (bf16[256,1024]{1,0:T(8,128)(2,1)}, bf16[256,1024]{1,0:T(8,128)(2,1)S(1)}, u32[]{:S(2)}, u32[]{:S(2)}) collective-permute-start(bf16[256,1024]{1,0:T(8,128)(2,1)} %get-tuple-element.250), channel_id=1, source_target_pairs={{0,8},{8,16},{16,24},{24,28},{28,20},{20,12},{12,4},{4,0},{1,9},{9... | collective-permute-start | bytes 1572872 | tf_op jit(solution)/shard_map/ppermute | solution.py:650
  128.1 16.5 %collective-permute-start.16 = (bf16[256,1024]{1,0:T(8,128)(2,1)}, bf16[256,1024]{1,0:T(8,128)(2,1)S(1)}, u32[]{:S(2)}, u32[]{:S(2)}) collective-permute-start(bf16[256,1024]{1,0:T(8,128)(2,1)} %get-tuple-element.251), channel_id=1, source_target_pairs={{0,4},{8,0},{16,8},{24,16},{28,24},{20,28},{12,20},{4,12},{1,5},{9... | collective-permute-start | bytes 1572872 | tf_op jit(solution)/shard_map/ppermute | solution.py:650
  132.5 62.8 %collective-permute-start.24 = (bf16[2048,512]{1,0:T(8,128)(2,1)}, bf16[2048,512]{1,0:T(8,128)(2,1)}, u32[]{:S(2)}, u32[]{:S(2)}) collective-permute-start(bf16[2048,512]{1,0:T(8,128)(2,1)} %join.1.refs_0_), channel_id=1, source_target_pairs={{0,1},{1,0},{2,3},{3,2},{4,5},{5,4},{6,7},{7,6},{8,9},{9,8},{10,11... | collective-permute-start | bytes 6291464 | tf_op jit(solution)/shard_map/ppermute | solution.py:473
  149.4 19.3 %collective-permute-start.19 = (bf16[256,1024]{1,0:T(8,128)(2,1)}, bf16[256,1024]{1,0:T(8,128)(2,1)}, u32[]{:S(2)}, u32[]{:S(2)}) collective-permute-start(bf16[256,1024]{1,0:T(8,128)(2,1)} %get-tuple-element.260), channel_id=1, source_target_pairs={{0,8},{8,16},{16,24},{24,28},{28,20},{20,12},{12,4},{4,0},{1,9},{9... | collective-permute-start | bytes 1572872 | tf_op jit(solution)/shard_map/ppermute | solution.py:650
  151.7 17.1 %collective-permute-start.20 = (bf16[256,1024]{1,0:T(8,128)(2,1)}, bf16[256,1024]{1,0:T(8,128)(2,1)}, u32[]{:S(2)}, u32[]{:S(2)}) collective-permute-start(bf16[256,1024]{1,0:T(8,128)(2,1)} %get-tuple-element.261), channel_id=1, source_target_pairs={{0,4},{8,0},{16,8},{24,16},{28,24},{20,28},{12,20},{4,12},{1,5},{9... | collective-permute-start | bytes 1572872 | tf_op jit(solution)/shard_map/ppermute | solution.py:650
  151.7 37.3 %all-to-all-start.3 = ((bf16[8,32,1024]{2,1,0:T(8,128)(2,1)}), bf16[8,32,1024]{2,1,0:T(8,128)(2,1)}, u32[]{:S(2)}, u32[]{:S(2)}) async-start(bf16[8,32,1024]{2,1,0:T(8,128)(2,1)} %bitcast.12), calls=%async_computation.3 | async-start | bytes 1048576 | tf_op jit(solution)/shard_map/all_to_all | solution.py:446
  168.7 6.1 %collective-permute-start.23 = (bf16[8,128,256]{2,1,0:T(8,128)(2,1)S(1)}, bf16[8,128,256]{2,1,0:T(8,128)(2,1)S(1)}, u32[]{:S(2)}, u32[]{:S(2)}) collective-permute-start(bf16[8,128,256]{2,1,0:T(8,128)(2,1)S(1)} %get-tuple-element.276), channel_id=1, source_target_pairs={{0,2},{2,0},{1,3},{3,1},{4,6},{6,4},{5,7},{7,5},{8,10},{10,8},{9,1... | collective-permute-start | bytes 1572872 | tf_op jit(solution)/shard_map/ppermute | solution.py:442
  172.6 22.5 %copy-start.44 = (s32[32]{0:T(128)S(1)}, s32[32]{0:T(128)}, u32[]{:S(2)}) copy-start(s32[32]{0:T(128)} %steps_ref.1) | copy-start | bytes 388
  172.6 22.5 %copy-start.43 = (s32[256]{0:T(256)S(1)}, s32[256]{0:T(256)}, u32[]{:S(2)}) copy-start(s32[256]{0:T(256)} %param.20) | copy-start | bytes 3076
  172.6 22.6 %copy-start.40 = (f32[4,1024]{1,0:T(4,128)S(1)}, f32[4,1024]{1,0:T(4,128)}, u32[]{:S(2)}) copy-start(f32[4,1024]{1,0:T(4,128)} %get-tuple-element.285) | copy-start | bytes 49156
  172.6 15.1 %collective-permute-start.21 = (bf16[256,1024]{1,0:T(8,128)(2,1)}, bf16[256,1024]{1,0:T(8,128)(2,1)}, u32[]{:S(2)}, u32[]{:S(2)}) collective-permute-start(bf16[256,1024]{1,0:T(8,128)(2,1)} %get-tuple-element.272), channel_id=1, source_target_pairs={{0,8},{8,16},{16,24},{24,28},{28,20},{20,12},{12,4},{4,0},{1,9},{9... | collective-permute-start | bytes 1572872 | tf_op jit(solution)/shard_map/ppermute | solution.py:650
  174.7 14.3 %collective-permute-start.22 = (bf16[256,1024]{1,0:T(8,128)(2,1)}, bf16[256,1024]{1,0:T(8,128)(2,1)}, u32[]{:S(2)}, u32[]{:S(2)}) collective-permute-start(bf16[256,1024]{1,0:T(8,128)(2,1)} %get-tuple-element.273), channel_id=1, source_target_pairs={{0,4},{8,0},{16,8},{24,16},{28,24},{20,28},{12,20},{4,12},{1,5},{9... | collective-permute-start | bytes 1572872 | tf_op jit(solution)/shard_map/ppermute | solution.py:650
  189.0 25.0 %all-to-all-start.4 = ((bf16[8,192,256]{2,1,0:T(8,128)(2,1)}), bf16[8,192,256]{2,1,0:T(8,128)(2,1)S(1)}, u32[]{:S(2)}, u32[]{:S(2)}) async-start(bf16[8,192,256]{2,1,0:T(8,128)(2,1)} %attention_backward.3.grads_ref), calls=%async_computation.4 | async-start | bytes 1572864 | tf_op jit(solution)/shard_map/all_to_all | solution.py:446
  202.0 1.4 collective-permute-start.25
  208.1 14.4 %collective-permute-start.28 = (bf16[400,1024]{1,0:T(8,128)(2,1)}, bf16[400,1024]{1,0:T(8,128)(2,1)}, u32[]{:S(2)}, u32[]{:S(2)}) collective-permute-start(bf16[400,1024]{1,0:T(8,128)(2,1)} %ring_finish.1.refs_0_), channel_id=1, source_target_pairs={{0,2},{2,0},{1,3},{3,1},{4,6},{6,4},{5,7},{7,5},{8,10},{10,8},{9,1... | collective-permute-start | bytes 2457608 | tf_op jit(solution)/shard_map/ppermute | solution.py:442
  208.3 21.1 %collective-permute-start.26 = (bf16[400,1024]{1,0:T(8,128)(2,1)}, bf16[400,1024]{1,0:T(8,128)(2,1)}, u32[]{:S(2)}, u32[]{:S(2)}) collective-permute-start(bf16[400,1024]{1,0:T(8,128)(2,1)} %ring_finish.1.refs_0_), channel_id=1, source_target_pairs={{0,8},{8,16},{16,24},{24,28},{28,20},{20,12},{12,4},{4,0},{1,9},{9... | collective-permute-start | bytes 2457608 | tf_op jit(solution)/shard_map/ppermute | solution.py:577
  210.3 21.3 %collective-permute-start.27 = (bf16[400,1024]{1,0:T(8,128)(2,1)}, bf16[400,1024]{1,0:T(8,128)(2,1)}, u32[]{:S(2)}, u32[]{:S(2)}) collective-permute-start(bf16[400,1024]{1,0:T(8,128)(2,1)} %ring_finish.1.refs_0_), channel_id=1, source_target_pairs={{0,4},{8,0},{16,8},{24,16},{28,24},{20,28},{12,20},{4,12},{1,5},{9... | collective-permute-start | bytes 2457608 | tf_op jit(solution)/shard_map/ppermute | solution.py:577
  217.6 3.8 %collective-permute-start.29 = (f32[24,128]{1,0:T(8,128)S(1)}, f32[24,128]{1,0:T(8,128)S(1)}, u32[]{:S(2)}, u32[]{:S(2)}) collective-permute-start(f32[24,128]{1,0:T(8,128)S(1)} %reshape.125), channel_id=1, source_target_pairs={{0,1},{1,0},{2,3},{3,2},{4,5},{5,4},{6,7},{7,6},{8,9},{9,8},{10,11... | collective-permute-start | bytes 36872 | tf_op jit(solution)/shard_map/ppermute | solution.py:473
  221.3 1.2 collective-permute-start.30
  231.7 27.0 %copy-start.10 = (f32[256,1024]{1,0:T(8,128)S(1)}, f32[256,1024]{1,0:T(8,128)}, u32[]{:S(2)}) copy-start(f32[256,1024]{1,0:T(8,128)} %get-tuple-element.235.hidden_ref) | copy-start | bytes 3145732
  231.7 27.0 %copy-start.42 = (f32[1024]{0:T(1024)S(1)}, f32[1024]{0:T(1024)}, u32[]{:S(2)}) copy-start(f32[1024]{0:T(1024)} %param.35) | copy-start | bytes 12292
  231.7 4.1 %collective-permute-start.33 = (bf16[400,1024]{1,0:T(8,128)(2,1)}, bf16[400,1024]{1,0:T(8,128)(2,1)S(1)}, u32[]{:S(2)}, u32[]{:S(2)}) collective-permute-start(bf16[400,1024]{1,0:T(8,128)(2,1)} %collective-permute-done.26.refs_7_), channel_id=1, source_target_pairs={{0,2},{2,0},{1,3},{3,1},{4,6},{6,4},{5,7},{7,5},{8,10},{10,8},{9,1... | collective-permute-start | bytes 2457608 | tf_op jit(solution)/shard_map/ppermute | solution.py:442
  231.7 4.7 %collective-permute-start.34 = (bf16[400,1024]{1,0:T(8,128)(2,1)}, bf16[400,1024]{1,0:T(8,128)(2,1)S(1)}, u32[]{:S(2)}, u32[]{:S(2)}) collective-permute-start(bf16[400,1024]{1,0:T(8,128)(2,1)} %collective-permute-done.27.refs_9_), channel_id=1, source_target_pairs={{0,2},{2,0},{1,3},{3,1},{4,6},{6,4},{5,7},{7,5},{8,10},{10,8},{9,1... | collective-permute-start | bytes 2457608 | tf_op jit(solution)/shard_map/ppermute | solution.py:442
  232.2 20.7 %collective-permute-start.31 = (bf16[400,1024]{1,0:T(8,128)(2,1)}, bf16[400,1024]{1,0:T(8,128)(2,1)}, u32[]{:S(2)}, u32[]{:S(2)}) collective-permute-start(bf16[400,1024]{1,0:T(8,128)(2,1)} %collective-permute-done.26.refs_7_), channel_id=1, source_target_pairs={{0,8},{8,16},{16,24},{24,28},{28,20},{20,12},{12,4},{4,0},{1,9},{9... | collective-permute-start | bytes 2457608 | tf_op jit(solution)/shard_map/ppermute | solution.py:577
  232.8 20.2 %collective-permute-start.32 = (bf16[400,1024]{1,0:T(8,128)(2,1)}, bf16[400,1024]{1,0:T(8,128)(2,1)}, u32[]{:S(2)}, u32[]{:S(2)}) collective-permute-start(bf16[400,1024]{1,0:T(8,128)(2,1)} %collective-permute-done.27.refs_9_), channel_id=1, source_target_pairs={{0,4},{8,0},{16,8},{24,16},{28,24},{20,28},{12,20},{4,12},{1,5},{9... | collective-permute-start | bytes 2457608 | tf_op jit(solution)/shard_map/ppermute | solution.py:577
  234.2 13.6 %collective-permute-start.36 = (bf16[256,1024]{1,0:T(8,128)(2,1)}, bf16[256,1024]{1,0:T(8,128)(2,1)}, u32[]{:S(2)}, u32[]{:S(2)}) collective-permute-start(bf16[256,1024]{1,0:T(8,128)(2,1)} %get-tuple-element.339), channel_id=1, source_target_pairs={{0,1},{1,0},{2,3},{3,2},{4,5},{5,4},{6,7},{7,6},{8,9},{9,8},{10,11... | collective-permute-start | bytes 1572872 | tf_op jit(solution)/shard_map/ppermute | solution.py:473
  235.7 17.1 %collective-permute-start.35 = (f32[24,128]{1,0:T(8,128)S(1)}, f32[24,128]{1,0:T(8,128)S(1)}, u32[]{:S(2)}, u32[]{:S(2)}) collective-permute-start(f32[24,128]{1,0:T(8,128)S(1)} %add.108), channel_id=1, source_target_pairs={{0,4},{4,0},{8,12},{12,8},{16,20},{20,16},{24,28},{28,24},{1,5},{5... | collective-permute-start | bytes 36872 | tf_op jit(solution)/shard_map/ppermute | solution.py:1037
  253.1 4.1 %collective-permute-start.39 = (bf16[400,1024]{1,0:T(8,128)(2,1)}, bf16[400,1024]{1,0:T(8,128)(2,1)}, u32[]{:S(2)}, u32[]{:S(2)}) collective-permute-start(bf16[400,1024]{1,0:T(8,128)(2,1)} %collective-permute-done.31.refs_7_), channel_id=1, source_target_pairs={{0,2},{2,0},{1,3},{3,1},{4,6},{6,4},{5,7},{7,5},{8,10},{10,8},{9,1... | collective-permute-start | bytes 2457608 | tf_op jit(solution)/shard_map/ppermute | solution.py:442
  253.1 7.8 %collective-permute-start.40 = (bf16[400,1024]{1,0:T(8,128)(2,1)}, bf16[400,1024]{1,0:T(8,128)(2,1)}, u32[]{:S(2)}, u32[]{:S(2)}) collective-permute-start(bf16[400,1024]{1,0:T(8,128)(2,1)} %collective-permute-done.32.refs_9_), channel_id=1, source_target_pairs={{0,2},{2,0},{1,3},{3,1},{4,6},{6,4},{5,7},{7,5},{8,10},{10,8},{9,1... | collective-permute-start | bytes 2457608 | tf_op jit(solution)/shard_map/ppermute | solution.py:442
  253.6 21.8 %collective-permute-start.37 = (bf16[400,1024]{1,0:T(8,128)(2,1)}, bf16[400,1024]{1,0:T(8,128)(2,1)S(1)}, u32[]{:S(2)}, u32[]{:S(2)}) collective-permute-start(bf16[400,1024]{1,0:T(8,128)(2,1)} %collective-permute-done.31.refs_7_), channel_id=1, source_target_pairs={{0,8},{8,16},{16,24},{24,28},{28,20},{20,12},{12,4},{4,0},{1,9},{9... | collective-permute-start | bytes 2457608 | tf_op jit(solution)/shard_map/ppermute | solution.py:577
  255.1 20.4 %collective-permute-start.38 = (bf16[400,1024]{1,0:T(8,128)(2,1)}, bf16[400,1024]{1,0:T(8,128)(2,1)S(1)}, u32[]{:S(2)}, u32[]{:S(2)}) collective-permute-start(bf16[400,1024]{1,0:T(8,128)(2,1)} %collective-permute-done.32.refs_9_), channel_id=1, source_target_pairs={{0,4},{8,0},{16,8},{24,16},{28,24},{20,28},{12,20},{4,12},{1,5},{9... | collective-permute-start | bytes 2457608 | tf_op jit(solution)/shard_map/ppermute | solution.py:577
  255.6 13.6 %collective-permute-start.41 = (bf16[256,1024]{1,0:T(8,128)(2,1)}, bf16[256,1024]{1,0:T(8,128)(2,1)}, u32[]{:S(2)}, u32[]{:S(2)}) collective-permute-start(bf16[256,1024]{1,0:T(8,128)(2,1)} %get-tuple-element.370), channel_id=1, source_target_pairs={{0,1},{1,0},{2,3},{3,2},{4,5},{5,4},{6,7},{7,6},{8,9},{9,8},{10,11... | collective-permute-start | bytes 1572872 | tf_op jit(solution)/shard_map/ppermute | solution.py:473
  257.1 18.3 %collective-permute-start.42 = (f32[24,128]{1,0:T(8,128)S(1)}, f32[24,128]{1,0:T(8,128)S(1)}, u32[]{:S(2)}, u32[]{:S(2)}) collective-permute-start(f32[24,128]{1,0:T(8,128)S(1)} %add.113), channel_id=1, source_target_pairs={{0,8},{4,12},{8,0},{12,4},{16,24},{20,28},{24,16},{28,20},{1,9},{5... | collective-permute-start | bytes 36872 | tf_op jit(solution)/shard_map/ppermute | solution.py:1037
  260.9 21.5 %copy-start.39 = (f32[1024]{0:T(1024)S(1)}, f32[1024]{0:T(1024)}, u32[]{:S(2)}) copy-start(f32[1024]{0:T(1024)} %param.22) | copy-start | bytes 12292
  275.4 10.8 %collective-permute-start.45 = (bf16[400,1024]{1,0:T(8,128)(2,1)S(1)}, bf16[400,1024]{1,0:T(8,128)(2,1)}, u32[]{:S(2)}, u32[]{:S(2)}) collective-permute-start(bf16[400,1024]{1,0:T(8,128)(2,1)S(1)} %collective-permute-done.37.left.refs_7_), channel_id=1, source_target_pairs={{0,2},{2,0},{1,3},{3,1},{4,6},{6,4},{5,7},{7,5},{8,10},{10,8},{9,1... | collective-permute-start | bytes 2457608 | tf_op jit(solution)/shard_map/ppermute | solution.py:442
  275.5 10.7 %collective-permute-start.46 = (bf16[400,1024]{1,0:T(8,128)(2,1)S(1)}, bf16[400,1024]{1,0:T(8,128)(2,1)}, u32[]{:S(2)}, u32[]{:S(2)}) collective-permute-start(bf16[400,1024]{1,0:T(8,128)(2,1)S(1)} %collective-permute-done.38.right.refs_9_), channel_id=1, source_target_pairs={{0,2},{2,0},{1,3},{3,1},{4,6},{6,4},{5,7},{7,5},{8,10},{10,8},{9,1... | collective-permute-start | bytes 2457608 | tf_op jit(solution)/shard_map/ppermute | solution.py:442
  278.6 14.5 %collective-permute-start.47 = (f32[24,128]{1,0:T(8,128)S(1)}, f32[24,128]{1,0:T(8,128)S(1)}, u32[]{:S(2)}, u32[]{:S(2)}) collective-permute-start(f32[24,128]{1,0:T(8,128)S(1)} %add.116), channel_id=1, source_target_pairs={{0,16},{4,20},{8,24},{12,28},{16,0},{20,4},{24,8},{28,12},{1,17},{... | collective-permute-start | bytes 36872 | tf_op jit(solution)/shard_map/ppermute | solution.py:1037
  280.4 12.8 %collective-permute-start.43 = (bf16[400,512]{1,0:T(8,128)(2,1)}, bf16[400,512]{1,0:T(8,128)(2,1)S(1)}, u32[]{:S(2)}, u32[]{:S(2)}) collective-permute-start(bf16[400,512]{1,0:T(8,128)(2,1)} %get-tuple-element.353), channel_id=1, source_target_pairs={{0,8},{8,16},{16,24},{24,28},{28,20},{20,12},{12,4},{4,0},{1,9},{9... | collective-permute-start | bytes 1228808 | tf_op jit(solution)/shard_map/ppermute | solution.py:577
  280.6 12.5 %collective-permute-start.44 = (bf16[400,512]{1,0:T(8,128)(2,1)}, bf16[400,512]{1,0:T(8,128)(2,1)}, u32[]{:S(2)}, u32[]{:S(2)}) collective-permute-start(bf16[400,512]{1,0:T(8,128)(2,1)} %get-tuple-element.354), channel_id=1, source_target_pairs={{0,4},{8,0},{16,8},{24,16},{28,24},{20,28},{12,20},{4,12},{1,5},{9... | collective-permute-start | bytes 1228808 | tf_op jit(solution)/shard_map/ppermute | solution.py:577
  293.2 1.8 collective-permute-start.48
  293.2 2.5 collective-permute-start.49
  (35 other events, 193.2 us)

commit v19 on v18

--- a/solution.py
+++ b/solution.py
@@ -961,18 +961,19 @@
     ring = Reduce(keep, swap_cores(give), keep_in, swap_cores(give_in), table)
     mlp_part, d_mlp = lax.optimization_barrier((mlp_part, d_mlp))
     d_hidden, d_branch, d_attn, sums = middle(hidden, out_grad, d_mlp, gain_mlp, output_weight)
-    grads = scatter_queries(d_attn, heads, split)
     d_branch, mlp_part = visit([ring, inputs], (d_branch, mlp_part))
     while inputs.busy():
         visit([inputs], ())
     mlp_out = across_heads(mlp_part)
     out_near, out_far = share_halves(attn_out, 0)
-    doutput = product(out_near, d_branch) + product(out_far, swap_cores(d_branch))
+    d_attn, d_branch_far = lax.optimization_barrier((d_attn, swap_cores(d_branch)))
+    grads = scatter_queries(d_attn, heads, split)
+    doutput = product(out_near, d_branch) + product(out_far, d_branch_far)
     doutput = doutput.astype(BF16).reshape(chips, -1, model)
     steps, inputs = zip(*inputs.blocks)
     inputs = join(inputs)
     parts = across_heads(inputs) if cut != model else [inputs]
-    grads, doutput = visit([ring], (grads, doutput))
+    doutput = visit([ring], doutput)
     doutput = to_heads(doutput)
     dquery, far_sums = attention_backward(queries, grads, raw, logsum, other, [], crops)
     far_sums = swap_cores(far_sums)

time: 305 us -> 299 us (0.980)
  waiting for transfers between devices: 59.8 us -> 52.5 us
    ppermute x24, waiting for transfers between devices: 20.6 us -> 15.9 us  [send(): lax.ppermute(block, 'chip', ring_pairs(direction))]
    unnamed x93 -> x89, local copies, waits for them, and re-layouts: 10.7 us -> 11.1 us
  transfers between devices with their start and end apart: 54 -> 54, of which waited for: 26 -> 25; matrix products, arithmetic and copies ran while one was open for 5% -> 6% of each run, Pallas kernels for 36% -> 36%
where the time goes in v19:
time: 299 us; the launch traced here: 297 us
  Pallas kernels  124 us (41%)
  starting transfers between devices  59.3 us (20%)
  waiting for transfers between devices  52.5 us (18%)
  blocking collectives  29.6 us (10%)
  local copies, waits for them, and re-layouts  15.4 us (5%)
  other arithmetic  9.77 us (3%)
  matrix products  5.35 us (2%)
    pallas_call x5, Pallas kernels, place(): pl.pallas_call(functools.partial(place_kernel, heads, len(blocks[0]) // 2...  30.2 us
    all_to_all x1, blocking collectives, to_heads(): return lax.all_to_all(blocks, 'chip', 0, 0, tiled=True)  29.6 us
    pallas_call x2, Pallas kernels, attention_backward(): pl.pallas_call(functools.partial(backward_kernel, crops, len(extras)), gr...  24.9 us
    ppermute x24, starting transfers between devices, send(): lax.ppermute(block, 'chip', ring_pairs(direction))  24.5 us
    all_to_all x4, starting transfers between devices, to_heads(): return lax.all_to_all(blocks, 'chip', 0, 0, tiled=True)  17.3 us
    ppermute x24, waiting for transfers between devices, send(): lax.ppermute(block, 'chip', ring_pairs(direction))  15.9 us
    pallas_call x4, Pallas kernels, add(): pl.pallas_call(functools.partial(add_kernel, places, len(shapes)), grid_s...  15.6 us
    pallas_call x1, Pallas kernels, attention_forward(): pl.pallas_call(functools.partial(forward_kernel, crops, key_step(count)),...  15.3 us
  transfers between devices with their start and end apart: 54, of which 25 were waited for; matrix products, arithmetic and copies ran while one was open for 6% of the time, Pallas kernels for 36%

profile of v19, /device:TPU:0, one launch (start us, length us, event | category | flops | bytes accessed | tf_op | source)
XLA Modules:
  0.0 297.5 jit_solution(16599760760710126317)
XLA Ops:
  1.2 6.6 %project.1 = (bf16[8,208,256]{2,1,0:T(8,128)(2,1)}, bf16[256,1024]{1,0:T(8,128)(2,1)}, bf16[256,512]{1,0:T(8,128)(2,1)}) custom-call(s32[18]{0:T(128)} %compare_select_fusion.5.table.core_ref._, bf16[256,1024]{1,0:T(8,128)(2,1)} %input_ref.3, s32[1,256]{1,0:T(1,128)} %bitcast.79, s32[32]{0:T(128)} %steps_ref.1, f32[1,1024]{1,0:T(1,128)} %bitcast.61, ...), custom_call_target="tpu_custom_call" | custom-call | flops 1 | bytes 1 | tf_op jit(solution)/shard_map/project/pallas_call | solution.py:94
  7.8 29.6 %all_to_all.25.query_ref.own.piece = bf16[8,208,256]{2,1,0:T(8,128)(2,1)S(1)} all-to-all(bf16[8,208,256]{2,1,0:T(8,128)(2,1)} %get-tuple-element.207), channel_id=1, replica_groups=mesh['chip'=8,'core'=2,'head'=2] {'chip'}, dimensions={0} | all-to-all | bytes 1703936 | tf_op jit(solution)/shard_map/all_to_all | solution.py:446
  38.2 1.3 collective-permute-start.1
  40.7 15.3 %attention_forward.1 = (f32[8,64,256]{2,1,0:T(8,128)}, bf16[8,64,256]{2,1,0:T(8,128)(2,1)}, f32[8,1,256]{2,1,0:T(1,128)}) custom-call(bf16[8,208,256]{2,1,0:T(8,128)(2,1)} %copy-done, bf16[8,208,256]{2,1,0:T(8,128)(2,1)} %copy-done, bf16[8,208,256]{2,1,0:T(8,128)(2,1)} %copy-done.2), custom_call_target="tpu_custom_call" | custom-call | flops 1 | bytes 1 | tf_op jit(solution)/shard_map/attention_forward/pallas_call | solution.py:378
  56.1 3.4 %all-to-all-start.1 = ((bf16[8,64,256]{2,1,0:T(8,128)(2,1)}), bf16[8,64,256]{2,1,0:T(8,128)(2,1)S(1)}, u32[]{:S(2)}, u32[]{:S(2)}) async-start(bf16[8,64,256]{2,1,0:T(8,128)(2,1)} %get-tuple-element.214), calls=%async_computation.1 | async-start | bytes 524288 | tf_op jit(solution)/shard_map/all_to_all | solution.py:446
  59.7 9.3 %all-to-all-done.1 = bf16[8,64,256]{2,1,0:T(8,128)(2,1)S(1)} async-done(((bf16[8,64,256]{2,1,0:T(8,128)(2,1)}), bf16[8,64,256]{2,1,0:T(8,128)(2,1)S(1)}, u32[]{:S(2)}, u32[]{:S(2)}) %all-to-all-start.1) | async-done | bytes 262176 | tf_op jit(solution)/shard_map/all_to_all | solution.py:446
  69.4 1.6 collective-permute-start.7
  73.3 4.4 %collective-permute-done.3.refs_3_ = bf16[256,512]{1,0:T(8,128)(2,1)S(1)} collective-permute-done((bf16[256,512]{1,0:T(8,128)(2,1)S(1)}, bf16[256,512]{1,0:T(8,128)(2,1)S(1)}, u32[]{:S(2)}, u32[]{:S(2)}) %collective-permute-start.3) | collective-permute-done | bytes 262176 | tf_op jit(solution)/shard_map/ppermute | solution.py:577
  78.6 1.4 collective-permute-start.5
  80.6 1.4 collective-permute-done.7.refs_1_
  82.8 11.7 %mlp.1 = (bf16[256,2048]{1,0:T(8,128)(2,1)}, bf16[256,2048]{1,0:T(8,128)(2,1)}, bf16[256,1024]{1,0:T(8,128)(2,1)}, bf16[256,1024]{1,0:T(8,128)(2,1)}, f32[256,10...) custom-call(s32[18]{0:T(128)} %compare_select_fusion.5.table.core_ref._, ...), custom_call_target="tpu_custom_call" | custom-call | flops 1 | bytes 1 | tf_op jit(solution)/shard_map/mlp/pallas_call | solution.py:174
  95.2 1.5 collective-permute-start.14
  96.7 1.6 collective-permute-done.8.refs_1_.far_in
  100.0 3.3 %ring_add.4 = (bf16[256,512]{1,0:T(8,128)(2,1)}, bf16[256,512]{1,0:T(8,128)(2,1)}) custom-call(s32[18]{0:T(128)} %compare_select_fusion.5.table.core_ref._, bf16[256,1024]{1,0:T(8,128)(2,1)} %get-tuple-element.225.refs_0_.keep_in, bf16[256,1024]{1,0:T(8,128)(2,1)} %copy-done.9, bf16[256,2048]{1,0:T(8,128)(2,1)} %get-tuple-element.227.refs_2_.refs_5_.near, ...), custom_call_target="tpu_custom_call" | custom-call | flops 1 | bytes 1 | tf_op jit(solution)/shard_map/ring_add/pallas_call | solution.py:732
  103.6 1.8 collective-permute-start.11
  105.3 1.7 halves.2
  107.5 1.6 collective-permute-start.13
  110.1 4.3 %middle.1 = (f32[256,1024]{1,0:T(8,128)}, bf16[256,1024]{1,0:T(8,128)(2,1)}, bf16[512,256]{1,0:T(8,128)(2,1)}, f32[4,1024]{1,0:T(4,128)}) custom-call(f32[256,1024]{1,0:T(8,128)} %get-tuple-element.235.hidden_ref, bf16[256,1024]{1,0:T(8,128)(2,1)} %grad_ref.3, bf16[256,1024]{1,0:T(8,128)(2,1)} %get-tuple-element.238.refs_0_, bf16[256,1024]{1,0:T(8,128)(2,1)} %copy-done.28, ...), custom_call_target="tpu_custom_call" | custom-call | flops 1 | bytes 1 | tf_op jit(solution)/shard_map/middle/pallas_call | solution.py:235
  116.0 4.4 %ring_add.5 = (bf16[256,1024]{1,0:T(8,128)(2,1)}, bf16[256,1024]{1,0:T(8,128)(2,1)}) custom-call(s32[18]{0:T(128)} %compare_select_fusion.5.table.core_ref._, bf16[256,1024]{1,0:T(8,128)(2,1)} %get-tuple-element.225.refs_0_.keep_in, bf16[256,1024]{1,0:T(8,128)(2,1)} %copy-done.9, bf16[256,2048]{1,0:T(8,128)(2,1)} %get-tuple-element.227.refs_2_.refs_5_.near, ...), custom_call_target="tpu_custom_call" | custom-call | flops 1 | bytes 1 | tf_op jit(solution)/shard_map/ring_add/pallas_call | solution.py:732
  121.6 1.7 collective-permute-start.15
  123.7 4.6 %all-to-all-start.2 = ((bf16[8,64,256]{2,1,0:T(8,128)(2,1)}), bf16[8,64,256]{2,1,0:T(8,128)(2,1)S(1)}, u32[]{:S(2)}, u32[]{:S(2)}) async-start(bf16[8,64,256]{2,1,0:T(8,128)(2,1)} %bitcast.12), calls=%async_computation.2 | async-start | bytes 524288 | tf_op jit(solution)/shard_map/all_to_all | solution.py:446
  128.3 1.3 fusion.14
  129.6 3.0 join.1.refs_0_
  132.6 1.5 collective-permute-start.24
  136.4 1.6 collective-permute-done.16.refs_7_
  138.8 4.1 %ring_add.6 = (bf16[256,1024]{1,0:T(8,128)(2,1)}, bf16[256,1024]{1,0:T(8,128)(2,1)}) custom-call(s32[18]{0:T(128)} %compare_select_fusion.5.table.core_ref._, bf16[256,1024]{1,0:T(8,128)(2,1)} %get-tuple-element.225.refs_0_.keep_in, bf16[256,1024]{1,0:T(8,128)(2,1)} %copy-done.9, bf16[256,2048]{1,0:T(8,128)(2,1)} %get-tuple-element.227.refs_2_.refs_5_.near, ...), custom_call_target="tpu_custom_call" | custom-call | flops 1 | bytes 1 | tf_op jit(solution)/shard_map/ring_add/pallas_call | solution.py:732
  142.9 1.7 collective-permute-start.19
  144.9 4.7 %all-to-all-start.3 = ((bf16[8,32,1024]{2,1,0:T(8,128)(2,1)}), bf16[8,32,1024]{2,1,0:T(8,128)(2,1)}, u32[]{:S(2)}, u32[]{:S(2)}) async-start(bf16[8,32,1024]{2,1,0:T(8,128)(2,1)} %bitcast.11), calls=%async_computation.3 | async-start | bytes 1048576 | tf_op jit(solution)/shard_map/all_to_all | solution.py:446
  149.6 11.9 %attention_backward.2 = (f32[8,64,256]{2,1,0:T(8,128)S(1)}, bf16[8,128,256]{2,1,0:T(8,128)(2,1)S(1)}) custom-call(bf16[8,208,256]{2,1,0:T(8,128)(2,1)S(1)} %copy-done.1, bf16[8,64,256]{2,1,0:T(8,128)(2,1)S(1)} %all-to-all-done.2.grad_ref, f32[8,64,256]{2,1,0:T(8,128)S(1)} %copy-done.4, f32[8,1,256]{2,1,0:T(1,128)S(1)} %copy-done.5, ...), custom_call_target="tpu_custom_call" | custom-call | flops 1 | bytes 1 | tf_op jit(solution)/shard_map/attention_backward/pallas_call | solution.py:416
  161.6 3.8 %ring_add.7 = (bf16[256,1024]{1,0:T(8,128)(2,1)}, bf16[256,1024]{1,0:T(8,128)(2,1)}) custom-call(s32[18]{0:T(128)} %compare_select_fusion.5.table.core_ref._, bf16[256,1024]{1,0:T(8,128)(2,1)} %get-tuple-element.225.refs_0_.keep_in, bf16[256,1024]{1,0:T(8,128)(2,1)} %copy-done.9, bf16[256,2048]{1,0:T(8,128)(2,1)} %get-tuple-element.227.refs_2_.refs_5_.near, ...), custom_call_target="tpu_custom_call" | custom-call | flops 1 | bytes 1 | tf_op jit(solution)/shard_map/ring_add/pallas_call | solution.py:732
  165.4 2.1 collective-permute-start.21
  167.6 12.9 %attention_backward.3.grads_ref = bf16[8,192,256]{2,1,0:T(8,128)(2,1)} custom-call(bf16[8,208,256]{2,1,0:T(8,128)(2,1)S(1)} %copy-done.1, bf16[8,64,256]{2,1,0:T(8,128)(2,1)S(1)} %all-to-all-done.2.grad_ref, f32[8,64,256]{2,1,0:T(8,128)S(1)} %copy-done.4, f32[8,1,256]{2,1,0:T(1,128)S(1)} %copy-done.5, bf16[8,208,256]{2,1,0:T(8,128)(2,1)S(1)} %copy-done.1, ...), custom_call_target="tpu_custom_call" | custom-call | flops 1 | bytes 1 | tf_op jit(solution)/shard_map/attention_backward/pallas_call | solution.py:416
  181.8 4.6 %all-to-all-start.4 = ((bf16[8,192,256]{2,1,0:T(8,128)(2,1)}), bf16[8,192,256]{2,1,0:T(8,128)(2,1)S(1)}, u32[]{:S(2)}, u32[]{:S(2)}) async-start(bf16[8,192,256]{2,1,0:T(8,128)(2,1)} %attention_backward.3.grads_ref), calls=%async_computation.4 | async-start | bytes 1572864 | tf_op jit(solution)/shard_map/all_to_all | solution.py:446
  188.6 5.2 %head_gradient.1 = bf16[192,1024]{1,0:T(8,128)(2,1)} custom-call(s32[18]{0:T(128)} %compare_select_fusion.5.table.core_ref._, bf16[8,192,256]{2,1,0:T(8,128)(2,1)} %attention_backward.3.grads_ref, bf16[2048,512]{1,0:T(8,128)(2,1)} %join.1.refs_0_, bf16[2048,512]{1,0:T(8,128)(2,1)} %collective-permute-done.24.refs_1_), custom_call_target="tpu_custom_call" | custom-call | flops 1 | bytes 1 | tf_op jit(solution)/shard_map/head_gradient/pallas_call | solution.py:865
  193.7 1.7 constant_dynamic-slice_fusion
  197.6 3.9 %ring_finish.1.refs_0_ = bf16[400,1024]{1,0:T(8,128)(2,1)} custom-call(s32[18]{0:T(128)} %compare_select_fusion.5.table.core_ref._, bf16[256,1024]{1,0:T(8,128)(2,1)} %get-tuple-element.225.refs_0_.keep_in, bf16[256,1024]{1,0:T(8,128)(2,1)} %copy-done.9, bf16[256,2048]{1,0:T(8,128)(2,1)} %get-tuple-element.227.refs_2_.refs_5_.near, ...), custom_call_target="tpu_custom_call" | custom-call | flops 1 | bytes 1 | tf_op jit(solution)/shard_map/ring_finish/pallas_call | solution.py:688
  201.7 2.0 collective-permute-start.26
  203.8 2.9 all-to-all-done.4
  208.6 1.5 fusion.7
  210.1 1.6 collective-permute-start.29
  211.7 2.2 collective-permute-done.29
  215.1 4.5 %place.5 = (f32[2048,1024]{1,0:T(8,128)}, f32[1024,2048]{1,0:T(8,128)}, f32[2,8,32,1024]{3,2,1,0:T(8,128)}, f32[8,2,16,1024]{3,2,1,0:T(8,128)}, f32[1024,512]{1,...) custom-call(s32[18]{0:T(128)} %compare_select_fusion.5.table.core_ref._, bf16[400,1024]{1,0:T(8,128)(2,1)} %ring_finish.1.refs_0_, ...), custom_call_target="tpu_custom_call" | custom-call | flops 1 | bytes 1 | tf_op jit(solution)/shard_map/place/pallas_call | solution.py:778
  219.6 3.3 %collective-permute-done.26.refs_7_ = bf16[400,1024]{1,0:T(8,128)(2,1)} collective-permute-done((bf16[400,1024]{1,0:T(8,128)(2,1)}, bf16[400,1024]{1,0:T(8,128)(2,1)}, u32[]{:S(2)}, u32[]{:S(2)}) %collective-permute-start.26) | collective-permute-done | bytes 819232 | tf_op jit(solution)/shard_map/ppermute | solution.py:577
  222.8 1.5 collective-permute-done.27.refs_9_
  224.8 1.5 collective-permute-start.31
  226.9 1.5 collective-permute-start.36
  228.4 1.4 collective-permute-start.35
  230.7 6.9 %place.6 = (f32[2048,1024]{1,0:T(8,128)}, f32[1024,2048]{1,0:T(8,128)}, f32[2,8,32,1024]{3,2,1,0:T(8,128)}, f32[8,2,16,1024]{3,2,1,0:T(8,128)}, f32[1024,512]{1,...) custom-call(s32[18]{0:T(128)} %compare_select_fusion.5.table.core_re, ...), custom_call_target="tpu_custom_call", output_to_operand_aliasing={{0}: (1, {}), {1}: (2, {}), {2}: (3, {}), {3}: (4, {}), {4}... | custom-call | flops 1 | bytes 1 | tf_op jit(solution)/shard_map/place/pallas_call | solution.py:778
  237.6 2.9 collective-permute-done.36
  240.5 5.0 %collective-permute-done.35 = f32[24,128]{1,0:T(8,128)S(1)} collective-permute-done((f32[24,128]{1,0:T(8,128)S(1)}, f32[24,128]{1,0:T(8,128)S(1)}, u32[]{:S(2)}, u32[]{:S(2)}) %collective-permute-start.35) | collective-permute-done | bytes 12320 | tf_op jit(solution)/shard_map/ppermute | solution.py:1038
  247.0 1.5 collective-permute-start.37
  249.1 1.5 collective-permute-start.41
  250.6 1.5 collective-permute-start.42
  252.1 2.2 add_convert_fusion
  254.3 7.0 %place.7 = (f32[2048,1024]{1,0:T(8,128)}, f32[1024,2048]{1,0:T(8,128)}, f32[2,8,32,1024]{3,2,1,0:T(8,128)}, f32[8,2,16,1024]{3,2,1,0:T(8,128)}, f32[1024,512]{1,...) custom-call(s32[18]{0:T(128)} %compare_select_fusion.5.table.core_re, ...), custom_call_target="tpu_custom_call", output_to_operand_aliasing={{0}: (1, {}), {1}: (2, {}), {2}: (3, {}), {3}: (4, {}), {4}... | custom-call | flops 1 | bytes 1 | tf_op jit(solution)/shard_map/place/pallas_call | solution.py:778
  261.3 1.3 collective-permute-done.41
  262.7 6.2 %collective-permute-done.42 = f32[24,128]{1,0:T(8,128)S(1)} collective-permute-done((f32[24,128]{1,0:T(8,128)S(1)}, f32[24,128]{1,0:T(8,128)S(1)}, u32[]{:S(2)}, u32[]{:S(2)}) %collective-permute-start.42) | collective-permute-done | bytes 12320 | tf_op jit(solution)/shard_map/ppermute | solution.py:1038
  270.0 2.1 halves.3
  272.1 1.7 collective-permute-start.47
  274.1 1.7 collective-permute-start.44
  275.8 1.5 fusion.13
  277.3 2.3 fusion.12
  279.7 6.9 %place.8 = (f32[2048,1024]{1,0:T(8,128)}, f32[1024,2048]{1,0:T(8,128)}, f32[2,8,32,1024]{3,2,1,0:T(8,128)}, f32[8,2,16,1024]{3,2,1,0:T(8,128)}, f32[1024,512]{1,...) custom-call(s32[18]{0:T(128)} %compare_select_fusion.5.table.core_re, ...), custom_call_target="tpu_custom_call", output_to_operand_aliasing={{0}: (1, {}), {1}: (2, {}), {2}: (3, {}), {3}: (4, {}), {4}... | custom-call | flops 1 | bytes 1 | tf_op jit(solution)/shard_map/place/pallas_call | solution.py:778
  290.0 5.0 %place.9 = (f32[2048,1024]{1,0:T(8,128)}, f32[1024,2048]{1,0:T(8,128)}, f32[2,8,32,1024]{3,2,1,0:T(8,128)}, f32[8,2,16,1024]{3,2,1,0:T(8,128)}, f32[1024,512]{1,...) custom-call(s32[18]{0:T(128)} %compare_select_fusion.5.table.core_re, ...), custom_call_target="tpu_custom_call", output_to_operand_aliasing={{0}: (1, {}), {1}: (2, {}), {2}: (3, {}), {3}: (4, {}), {4}... | custom-call | flops 1 | bytes 1 | tf_op jit(solution)/shard_map/place/pallas_call | solution.py:778
  (187 shorter events, 38.7 us)
Async XLA Ops:
  7.8 51.7 %copy-start.7 = (bf16[256,1024]{1,0:T(8,128)(2,1)S(1)}, bf16[256,1024]{1,0:T(8,128)(2,1)}, u32[]{:S(2)}) copy-start(bf16[256,1024]{1,0:T(8,128)(2,1)} %input_ref.3) | copy-start | bytes 1572868
  37.4 31.5 %copy-start.11 = (bf16[512,1024]{1,0:T(8,128)(2,1)S(1)}, bf16[512,1024]{1,0:T(8,128)(2,1)}, u32[]{:S(2)}) copy-start(bf16[512,1024]{1,0:T(8,128)(2,1)} %refs_3_.1) | copy-start | bytes 3145732
  37.5 2.4 collective-permute-start.2
  37.5 18.6 %collective-permute-start = (bf16[256,512]{1,0:T(8,128)(2,1)}, bf16[256,512]{1,0:T(8,128)(2,1)S(1)}, u32[]{:S(2)}, u32[]{:S(2)}) collective-permute-start(bf16[256,512]{1,0:T(8,128)(2,1)} %get-tuple-element.209.refs_0_), channel_id=1, source_target_pairs={{0,8},{8,16},{16,24},{24,28},{28,20},{20,12},{12,4},{4,0},{1,9},{9... | collective-permute-start | bytes 786440 | tf_op jit(solution)/shard_map/ppermute | solution.py:577
  38.2 17.8 %collective-permute-start.1 = (bf16[256,512]{1,0:T(8,128)(2,1)}, bf16[256,512]{1,0:T(8,128)(2,1)}, u32[]{:S(2)}, u32[]{:S(2)}) collective-permute-start(bf16[256,512]{1,0:T(8,128)(2,1)} %get-tuple-element.209.refs_0_), channel_id=1, source_target_pairs={{0,4},{8,0},{16,8},{24,16},{28,24},{20,28},{12,20},{4,12},{1,5},{9... | collective-permute-start | bytes 786440 | tf_op jit(solution)/shard_map/ppermute | solution.py:577
  56.0 38.5 %copy-start.32 = (bf16[256,512]{1,0:T(8,128)(2,1)}, bf16[256,512]{1,0:T(8,128)(2,1)S(1)}, u32[]{:S(2)}) copy-start(bf16[256,512]{1,0:T(8,128)(2,1)S(1)} %collective-permute-done.refs_1_) | copy-start | bytes 786436
  56.1 12.9 %all-to-all-start.1 = ((bf16[8,64,256]{2,1,0:T(8,128)(2,1)}), bf16[8,64,256]{2,1,0:T(8,128)(2,1)S(1)}, u32[]{:S(2)}, u32[]{:S(2)}) async-start(bf16[8,64,256]{2,1,0:T(8,128)(2,1)} %get-tuple-element.214), calls=%async_computation.1 | async-start | bytes 524288 | tf_op jit(solution)/shard_map/all_to_all | solution.py:446
  69.4 12.6 %collective-permute-start.7 = (bf16[256,1024]{1,0:T(8,128)(2,1)S(1)}, bf16[256,1024]{1,0:T(8,128)(2,1)S(1)}, u32[]{:S(2)}, u32[]{:S(2)}) collective-permute-start(bf16[256,1024]{1,0:T(8,128)(2,1)S(1)} %convolution_convert_fusion.refs_0_), channel_id=1, source_target_pairs={{0,1},{1,0},{2,3},{3,2},{4,5},{5,4},{6,7},{7,6},{8,9},{9,8},{10,11... | collective-permute-start | bytes 1572872 | tf_op jit(solution)/shard_map/ppermute | solution.py:473
  71.0 6.7 %collective-permute-start.3 = (bf16[256,512]{1,0:T(8,128)(2,1)S(1)}, bf16[256,512]{1,0:T(8,128)(2,1)S(1)}, u32[]{:S(2)}, u32[]{:S(2)}) collective-permute-start(bf16[256,512]{1,0:T(8,128)(2,1)S(1)} %collective-permute-done.refs_1_), channel_id=1, source_target_pairs={{0,8},{8,16},{16,24},{24,28},{28,20},{20,12},{12,4},{4,0},{1,9},{9... | collective-permute-start | bytes 786440 | tf_op jit(solution)/shard_map/ppermute | solution.py:577
  72.0 6.6 %collective-permute-start.4 = (bf16[256,512]{1,0:T(8,128)(2,1)}, bf16[256,512]{1,0:T(8,128)(2,1)S(1)}, u32[]{:S(2)}, u32[]{:S(2)}) collective-permute-start(bf16[256,512]{1,0:T(8,128)(2,1)} %collective-permute-done.1.refs_2_), channel_id=1, source_target_pairs={{0,4},{8,0},{16,8},{24,16},{28,24},{20,28},{12,20},{4,12},{1,5},{9... | collective-permute-start | bytes 786440 | tf_op jit(solution)/shard_map/ppermute | solution.py:577
  77.7 25.7 %copy-start.33 = (bf16[256,512]{1,0:T(8,128)(2,1)}, bf16[256,512]{1,0:T(8,128)(2,1)S(1)}, u32[]{:S(2)}) copy-start(bf16[256,512]{1,0:T(8,128)(2,1)S(1)} %collective-permute-done.3.refs_3_) | copy-start | bytes 786436
  78.6 16.0 %copy-start.34 = (bf16[256,512]{1,0:T(8,128)(2,1)}, bf16[256,512]{1,0:T(8,128)(2,1)S(1)}, u32[]{:S(2)}) copy-start(bf16[256,512]{1,0:T(8,128)(2,1)S(1)} %collective-permute-done.4.refs_4_) | copy-start | bytes 786436
  78.6 15.9 %collective-permute-start.5 = (bf16[256,512]{1,0:T(8,128)(2,1)S(1)}, bf16[256,512]{1,0:T(8,128)(2,1)S(1)}, u32[]{:S(2)}, u32[]{:S(2)}) collective-permute-start(bf16[256,512]{1,0:T(8,128)(2,1)S(1)} %collective-permute-done.3.refs_3_), channel_id=1, source_target_pairs={{0,8},{8,16},{16,24},{24,28},{28,20},{20,12},{12,4},{4,0},{1,9},{9... | collective-permute-start | bytes 786440 | tf_op jit(solution)/shard_map/ppermute | solution.py:577
  80.1 14.5 %collective-permute-start.6 = (bf16[256,512]{1,0:T(8,128)(2,1)S(1)}, bf16[256,512]{1,0:T(8,128)(2,1)S(1)}, u32[]{:S(2)}, u32[]{:S(2)}) collective-permute-start(bf16[256,512]{1,0:T(8,128)(2,1)S(1)} %collective-permute-done.4.refs_4_), channel_id=1, source_target_pairs={{0,4},{8,0},{16,8},{24,16},{28,24},{20,28},{12,20},{4,12},{1,5},{9... | collective-permute-start | bytes 786440 | tf_op jit(solution)/shard_map/ppermute | solution.py:577
  94.6 3.7 %collective-permute-start.9 = (bf16[256,2048]{1,0:T(8,128)(2,1)}, bf16[256,2048]{1,0:T(8,128)(2,1)S(1)}, u32[]{:S(2)}, u32[]{:S(2)}) collective-permute-start(bf16[256,2048]{1,0:T(8,128)(2,1)} %get-tuple-element.228), channel_id=1, source_target_pairs={{0,2},{2,0},{1,3},{3,1},{4,6},{6,4},{5,7},{7,5},{8,10},{10,8},{9,1... | collective-permute-start | bytes 3145736 | tf_op jit(solution)/shard_map/ppermute | solution.py:442
  94.7 3.6 %collective-permute-start.8 = (bf16[256,1024]{1,0:T(8,128)(2,1)}, bf16[256,1024]{1,0:T(8,128)(2,1)S(1)}, u32[]{:S(2)}, u32[]{:S(2)}) collective-permute-start(bf16[256,1024]{1,0:T(8,128)(2,1)} %get-tuple-element.226), channel_id=1, source_target_pairs={{0,2},{2,0},{1,3},{3,1},{4,6},{6,4},{5,7},{7,5},{8,10},{10,8},{9,1... | collective-permute-start | bytes 1572872 | tf_op jit(solution)/shard_map/ppermute | solution.py:442
  95.2 14.1 %collective-permute-start.14 = (bf16[256,1024]{1,0:T(8,128)(2,1)}, bf16[256,1024]{1,0:T(8,128)(2,1)S(1)}, u32[]{:S(2)}, u32[]{:S(2)}) collective-permute-start(bf16[256,1024]{1,0:T(8,128)(2,1)} %get-tuple-element.238.refs_0_), channel_id=1, source_target_pairs={{0,1},{1,0},{2,3},{3,2},{4,5},{5,4},{6,7},{7,6},{8,9},{9,8},{10,11... | collective-permute-start | bytes 1572872 | tf_op jit(solution)/shard_map/ppermute | solution.py:473
  103.3 11.8 %collective-permute-start.10 = (bf16[256,512]{1,0:T(8,128)(2,1)}, bf16[256,512]{1,0:T(8,128)(2,1)S(1)}, u32[]{:S(2)}, u32[]{:S(2)}) collective-permute-start(bf16[256,512]{1,0:T(8,128)(2,1)} %get-tuple-element.229), channel_id=1, source_target_pairs={{0,8},{8,16},{16,24},{24,28},{28,20},{20,12},{12,4},{4,0},{1,9},{9... | collective-permute-start | bytes 786440 | tf_op jit(solution)/shard_map/ppermute | solution.py:650
  103.6 11.5 %collective-permute-start.11 = (bf16[256,512]{1,0:T(8,128)(2,1)}, bf16[256,512]{1,0:T(8,128)(2,1)S(1)}, u32[]{:S(2)}, u32[]{:S(2)}) collective-permute-start(bf16[256,512]{1,0:T(8,128)(2,1)} %get-tuple-element.230), channel_id=1, source_target_pairs={{0,4},{8,0},{16,8},{24,16},{28,24},{20,28},{12,20},{4,12},{1,5},{9... | collective-permute-start | bytes 786440 | tf_op jit(solution)/shard_map/ppermute | solution.py:650
  107.0 7.6 %collective-permute-start.12 = (bf16[256,256]{1,0:T(8,128)(2,1)}, bf16[256,256]{1,0:T(8,128)(2,1)S(1)}, u32[]{:S(2)}, u32[]{:S(2)}) collective-permute-start(bf16[256,256]{1,0:T(8,128)(2,1)} %get-tuple-element.233), channel_id=1, source_target_pairs={{0,8},{8,16},{16,24},{24,28},{28,20},{20,12},{12,4},{4,0},{1,9},{9... | collective-permute-start | bytes 393224 | tf_op jit(solution)/shard_map/ppermute | solution.py:577
  107.5 7.6 %collective-permute-start.13 = (bf16[256,256]{1,0:T(8,128)(2,1)}, bf16[256,256]{1,0:T(8,128)(2,1)S(1)}, u32[]{:S(2)}, u32[]{:S(2)}) collective-permute-start(bf16[256,256]{1,0:T(8,128)(2,1)} %get-tuple-element.234), channel_id=1, source_target_pairs={{0,4},{8,0},{16,8},{24,16},{28,24},{20,28},{12,20},{4,12},{1,5},{9... | collective-permute-start | bytes 393224 | tf_op jit(solution)/shard_map/ppermute | solution.py:577
  114.7 14.9 %copy-start.38 = (bf16[256,256]{1,0:T(8,128)(2,1)}, bf16[256,256]{1,0:T(8,128)(2,1)S(1)}, u32[]{:S(2)}) copy-start(bf16[256,256]{1,0:T(8,128)(2,1)S(1)} %collective-permute-done.12.refs_7_) | copy-start | bytes 393220
  120.4 3.3 %collective-permute-start.18 = (bf16[256,1024]{1,0:T(8,128)(2,1)S(1)}, bf16[256,1024]{1,0:T(8,128)(2,1)S(1)}, u32[]{:S(2)}, u32[]{:S(2)}) collective-permute-start(bf16[256,1024]{1,0:T(8,128)(2,1)S(1)} %copy-done.27), channel_id=1, source_target_pairs={{0,2},{2,0},{1,3},{3,1},{4,6},{6,4},{5,7},{7,5},{8,10},{10,8},{9,1... | collective-permute-start | bytes 1572872 | tf_op jit(solution)/shard_map/ppermute | solution.py:442
  121.1 13.0 %collective-permute-start.17 = (bf16[256,256]{1,0:T(8,128)(2,1)}, bf16[256,256]{1,0:T(8,128)(2,1)S(1)}, u32[]{:S(2)}, u32[]{:S(2)}) collective-permute-start(bf16[256,256]{1,0:T(8,128)(2,1)} %constant_dynamic-slice_fusion.2), channel_id=1, source_target_pairs={{0,2},{2,0},{1,3},{3,1},{4,6},{6,4},{5,7},{7,5},{8,10},{10,8},{9,1... | collective-permute-start | bytes 393224 | tf_op jit(solution)/shard_map/ppermute | solution.py:442
  121.6 14.8 %collective-permute-start.15 = (bf16[256,1024]{1,0:T(8,128)(2,1)}, bf16[256,1024]{1,0:T(8,128)(2,1)S(1)}, u32[]{:S(2)}, u32[]{:S(2)}) collective-permute-start(bf16[256,1024]{1,0:T(8,128)(2,1)} %get-tuple-element.250), channel_id=1, source_target_pairs={{0,8},{8,16},{16,24},{24,28},{28,20},{20,12},{12,4},{4,0},{1,9},{9... | collective-permute-start | bytes 1572872 | tf_op jit(solution)/shard_map/ppermute | solution.py:650
  123.4 14.6 %collective-permute-start.16 = (bf16[256,1024]{1,0:T(8,128)(2,1)}, bf16[256,1024]{1,0:T(8,128)(2,1)S(1)}, u32[]{:S(2)}, u32[]{:S(2)}) collective-permute-start(bf16[256,1024]{1,0:T(8,128)(2,1)} %get-tuple-element.251), channel_id=1, source_target_pairs={{0,4},{8,0},{16,8},{24,16},{28,24},{20,28},{12,20},{4,12},{1,5},{9... | collective-permute-start | bytes 1572872 | tf_op jit(solution)/shard_map/ppermute | solution.py:650
  123.7 21.2 %all-to-all-start.2 = ((bf16[8,64,256]{2,1,0:T(8,128)(2,1)}), bf16[8,64,256]{2,1,0:T(8,128)(2,1)S(1)}, u32[]{:S(2)}, u32[]{:S(2)}) async-start(bf16[8,64,256]{2,1,0:T(8,128)(2,1)} %bitcast.12), calls=%async_computation.2 | async-start | bytes 524288 | tf_op jit(solution)/shard_map/all_to_all | solution.py:446
  132.6 56.0 %collective-permute-start.24 = (bf16[2048,512]{1,0:T(8,128)(2,1)}, bf16[2048,512]{1,0:T(8,128)(2,1)}, u32[]{:S(2)}, u32[]{:S(2)}) collective-permute-start(bf16[2048,512]{1,0:T(8,128)(2,1)} %join.1.refs_0_), channel_id=1, source_target_pairs={{0,1},{1,0},{2,3},{3,2},{4,5},{5,4},{6,7},{7,6},{8,9},{9,8},{10,11... | collective-permute-start | bytes 6291464 | tf_op jit(solution)/shard_map/ppermute | solution.py:473
  142.9 18.7 %collective-permute-start.19 = (bf16[256,1024]{1,0:T(8,128)(2,1)}, bf16[256,1024]{1,0:T(8,128)(2,1)}, u32[]{:S(2)}, u32[]{:S(2)}) collective-permute-start(bf16[256,1024]{1,0:T(8,128)(2,1)} %get-tuple-element.260), channel_id=1, source_target_pairs={{0,8},{8,16},{16,24},{24,28},{28,20},{20,12},{12,4},{4,0},{1,9},{9... | collective-permute-start | bytes 1572872 | tf_op jit(solution)/shard_map/ppermute | solution.py:650
  144.6 17.0 %collective-permute-start.20 = (bf16[256,1024]{1,0:T(8,128)(2,1)}, bf16[256,1024]{1,0:T(8,128)(2,1)}, u32[]{:S(2)}, u32[]{:S(2)}) collective-permute-start(bf16[256,1024]{1,0:T(8,128)(2,1)} %get-tuple-element.261), channel_id=1, source_target_pairs={{0,4},{8,0},{16,8},{24,16},{28,24},{20,28},{12,20},{4,12},{1,5},{9... | collective-permute-start | bytes 1572872 | tf_op jit(solution)/shard_map/ppermute | solution.py:650
  144.9 36.9 %all-to-all-start.3 = ((bf16[8,32,1024]{2,1,0:T(8,128)(2,1)}), bf16[8,32,1024]{2,1,0:T(8,128)(2,1)}, u32[]{:S(2)}, u32[]{:S(2)}) async-start(bf16[8,32,1024]{2,1,0:T(8,128)(2,1)} %bitcast.11), calls=%async_computation.3 | async-start | bytes 1048576 | tf_op jit(solution)/shard_map/all_to_all | solution.py:446
  161.5 6.1 %collective-permute-start.23 = (bf16[8,128,256]{2,1,0:T(8,128)(2,1)S(1)}, bf16[8,128,256]{2,1,0:T(8,128)(2,1)S(1)}, u32[]{:S(2)}, u32[]{:S(2)}) collective-permute-start(bf16[8,128,256]{2,1,0:T(8,128)(2,1)S(1)} %get-tuple-element.276), channel_id=1, source_target_pairs={{0,2},{2,0},{1,3},{3,1},{4,6},{6,4},{5,7},{7,5},{8,10},{10,8},{9,1... | collective-permute-start | bytes 1572872 | tf_op jit(solution)/shard_map/ppermute | solution.py:442
  165.4 15.1 %collective-permute-start.21 = (bf16[256,1024]{1,0:T(8,128)(2,1)}, bf16[256,1024]{1,0:T(8,128)(2,1)}, u32[]{:S(2)}, u32[]{:S(2)}) collective-permute-start(bf16[256,1024]{1,0:T(8,128)(2,1)} %get-tuple-element.272), channel_id=1, source_target_pairs={{0,8},{8,16},{16,24},{24,28},{28,20},{20,12},{12,4},{4,0},{1,9},{9... | collective-permute-start | bytes 1572872 | tf_op jit(solution)/shard_map/ppermute | solution.py:650
  167.6 14.2 %collective-permute-start.22 = (bf16[256,1024]{1,0:T(8,128)(2,1)}, bf16[256,1024]{1,0:T(8,128)(2,1)}, u32[]{:S(2)}, u32[]{:S(2)}) collective-permute-start(bf16[256,1024]{1,0:T(8,128)(2,1)} %get-tuple-element.273), channel_id=1, source_target_pairs={{0,4},{8,0},{16,8},{24,16},{28,24},{20,28},{12,20},{4,12},{1,5},{9... | collective-permute-start | bytes 1572872 | tf_op jit(solution)/shard_map/ppermute | solution.py:650
  181.8 24.8 %all-to-all-start.4 = ((bf16[8,192,256]{2,1,0:T(8,128)(2,1)}), bf16[8,192,256]{2,1,0:T(8,128)(2,1)S(1)}, u32[]{:S(2)}, u32[]{:S(2)}) async-start(bf16[8,192,256]{2,1,0:T(8,128)(2,1)} %attention_backward.3.grads_ref), calls=%async_computation.4 | async-start | bytes 1572864 | tf_op jit(solution)/shard_map/all_to_all | solution.py:446
  195.5 1.4 collective-permute-start.25
  201.5 13.6 %collective-permute-start.28 = (bf16[400,1024]{1,0:T(8,128)(2,1)}, bf16[400,1024]{1,0:T(8,128)(2,1)}, u32[]{:S(2)}, u32[]{:S(2)}) collective-permute-start(bf16[400,1024]{1,0:T(8,128)(2,1)} %ring_finish.1.refs_0_), channel_id=1, source_target_pairs={{0,2},{2,0},{1,3},{3,1},{4,6},{6,4},{5,7},{7,5},{8,10},{10,8},{9,1... | collective-permute-start | bytes 2457608 | tf_op jit(solution)/shard_map/ppermute | solution.py:442
  201.7 21.1 %collective-permute-start.26 = (bf16[400,1024]{1,0:T(8,128)(2,1)}, bf16[400,1024]{1,0:T(8,128)(2,1)}, u32[]{:S(2)}, u32[]{:S(2)}) collective-permute-start(bf16[400,1024]{1,0:T(8,128)(2,1)} %ring_finish.1.refs_0_), channel_id=1, source_target_pairs={{0,8},{8,16},{16,24},{24,28},{28,20},{20,12},{12,4},{4,0},{1,9},{9... | collective-permute-start | bytes 2457608 | tf_op jit(solution)/shard_map/ppermute | solution.py:577
  203.8 20.6 %collective-permute-start.27 = (bf16[400,1024]{1,0:T(8,128)(2,1)}, bf16[400,1024]{1,0:T(8,128)(2,1)}, u32[]{:S(2)}, u32[]{:S(2)}) collective-permute-start(bf16[400,1024]{1,0:T(8,128)(2,1)} %ring_finish.1.refs_0_), channel_id=1, source_target_pairs={{0,4},{8,0},{16,8},{24,16},{28,24},{20,28},{12,20},{4,12},{1,5},{9... | collective-permute-start | bytes 2457608 | tf_op jit(solution)/shard_map/ppermute | solution.py:577
  210.1 3.8 %collective-permute-start.29 = (f32[24,128]{1,0:T(8,128)S(1)}, f32[24,128]{1,0:T(8,128)S(1)}, u32[]{:S(2)}, u32[]{:S(2)}) collective-permute-start(f32[24,128]{1,0:T(8,128)S(1)} %reshape.125), channel_id=1, source_target_pairs={{0,1},{1,0},{2,3},{3,2},{4,5},{5,4},{6,7},{7,6},{8,9},{9,8},{10,11... | collective-permute-start | bytes 36872 | tf_op jit(solution)/shard_map/ppermute | solution.py:473
  213.9 1.2 collective-permute-start.30
  224.3 27.7 %copy-start.10 = (f32[256,1024]{1,0:T(8,128)S(1)}, f32[256,1024]{1,0:T(8,128)}, u32[]{:S(2)}) copy-start(f32[256,1024]{1,0:T(8,128)} %get-tuple-element.235.hidden_ref) | copy-start | bytes 3145732
  224.3 27.7 %copy-start.42 = (f32[1024]{0:T(1024)S(1)}, f32[1024]{0:T(1024)}, u32[]{:S(2)}) copy-start(f32[1024]{0:T(1024)} %param.35) | copy-start | bytes 12292
  224.3 4.1 %collective-permute-start.33 = (bf16[400,1024]{1,0:T(8,128)(2,1)}, bf16[400,1024]{1,0:T(8,128)(2,1)S(1)}, u32[]{:S(2)}, u32[]{:S(2)}) collective-permute-start(bf16[400,1024]{1,0:T(8,128)(2,1)} %collective-permute-done.26.refs_7_), channel_id=1, source_target_pairs={{0,2},{2,0},{1,3},{3,1},{4,6},{6,4},{5,7},{7,5},{8,10},{10,8},{9,1... | collective-permute-start | bytes 2457608 | tf_op jit(solution)/shard_map/ppermute | solution.py:442
  224.3 5.5 %collective-permute-start.34 = (bf16[400,1024]{1,0:T(8,128)(2,1)}, bf16[400,1024]{1,0:T(8,128)(2,1)S(1)}, u32[]{:S(2)}, u32[]{:S(2)}) collective-permute-start(bf16[400,1024]{1,0:T(8,128)(2,1)} %collective-permute-done.27.refs_9_), channel_id=1, source_target_pairs={{0,2},{2,0},{1,3},{3,1},{4,6},{6,4},{5,7},{7,5},{8,10},{10,8},{9,1... | collective-permute-start | bytes 2457608 | tf_op jit(solution)/shard_map/ppermute | solution.py:442
  224.8 20.7 %collective-permute-start.31 = (bf16[400,1024]{1,0:T(8,128)(2,1)}, bf16[400,1024]{1,0:T(8,128)(2,1)}, u32[]{:S(2)}, u32[]{:S(2)}) collective-permute-start(bf16[400,1024]{1,0:T(8,128)(2,1)} %collective-permute-done.26.refs_7_), channel_id=1, source_target_pairs={{0,8},{8,16},{16,24},{24,28},{28,20},{20,12},{12,4},{4,0},{1,9},{9... | collective-permute-start | bytes 2457608 | tf_op jit(solution)/shard_map/ppermute | solution.py:577
  226.3 20.2 %collective-permute-start.32 = (bf16[400,1024]{1,0:T(8,128)(2,1)}, bf16[400,1024]{1,0:T(8,128)(2,1)}, u32[]{:S(2)}, u32[]{:S(2)}) collective-permute-start(bf16[400,1024]{1,0:T(8,128)(2,1)} %collective-permute-done.27.refs_9_), channel_id=1, source_target_pairs={{0,4},{8,0},{16,8},{24,16},{28,24},{20,28},{12,20},{4,12},{1,5},{9... | collective-permute-start | bytes 2457608 | tf_op jit(solution)/shard_map/ppermute | solution.py:577
  226.9 13.6 %collective-permute-start.36 = (bf16[256,1024]{1,0:T(8,128)(2,1)}, bf16[256,1024]{1,0:T(8,128)(2,1)}, u32[]{:S(2)}, u32[]{:S(2)}) collective-permute-start(bf16[256,1024]{1,0:T(8,128)(2,1)} %get-tuple-element.339), channel_id=1, source_target_pairs={{0,1},{1,0},{2,3},{3,2},{4,5},{5,4},{6,7},{7,6},{8,9},{9,8},{10,11... | collective-permute-start | bytes 1572872 | tf_op jit(solution)/shard_map/ppermute | solution.py:473
  228.4 17.1 %collective-permute-start.35 = (f32[24,128]{1,0:T(8,128)S(1)}, f32[24,128]{1,0:T(8,128)S(1)}, u32[]{:S(2)}, u32[]{:S(2)}) collective-permute-start(f32[24,128]{1,0:T(8,128)S(1)} %add.108), channel_id=1, source_target_pairs={{0,4},{4,0},{8,12},{12,8},{16,20},{20,16},{24,28},{28,24},{1,5},{5... | collective-permute-start | bytes 36872 | tf_op jit(solution)/shard_map/ppermute | solution.py:1038
  246.5 4.1 %collective-permute-start.39 = (bf16[400,1024]{1,0:T(8,128)(2,1)}, bf16[400,1024]{1,0:T(8,128)(2,1)}, u32[]{:S(2)}, u32[]{:S(2)}) collective-permute-start(bf16[400,1024]{1,0:T(8,128)(2,1)} %collective-permute-done.31.refs_7_), channel_id=1, source_target_pairs={{0,2},{2,0},{1,3},{3,1},{4,6},{6,4},{5,7},{7,5},{8,10},{10,8},{9,1... | collective-permute-start | bytes 2457608 | tf_op jit(solution)/shard_map/ppermute | solution.py:442
  246.5 7.8 %collective-permute-start.40 = (bf16[400,1024]{1,0:T(8,128)(2,1)}, bf16[400,1024]{1,0:T(8,128)(2,1)}, u32[]{:S(2)}, u32[]{:S(2)}) collective-permute-start(bf16[400,1024]{1,0:T(8,128)(2,1)} %collective-permute-done.32.refs_9_), channel_id=1, source_target_pairs={{0,2},{2,0},{1,3},{3,1},{4,6},{6,4},{5,7},{7,5},{8,10},{10,8},{9,1... | collective-permute-start | bytes 2457608 | tf_op jit(solution)/shard_map/ppermute | solution.py:442
  247.0 21.8 %collective-permute-start.37 = (bf16[400,1024]{1,0:T(8,128)(2,1)}, bf16[400,1024]{1,0:T(8,128)(2,1)S(1)}, u32[]{:S(2)}, u32[]{:S(2)}) collective-permute-start(bf16[400,1024]{1,0:T(8,128)(2,1)} %collective-permute-done.31.refs_7_), channel_id=1, source_target_pairs={{0,8},{8,16},{16,24},{24,28},{28,20},{20,12},{12,4},{4,0},{1,9},{9... | collective-permute-start | bytes 2457608 | tf_op jit(solution)/shard_map/ppermute | solution.py:577
  248.5 20.4 %collective-permute-start.38 = (bf16[400,1024]{1,0:T(8,128)(2,1)}, bf16[400,1024]{1,0:T(8,128)(2,1)S(1)}, u32[]{:S(2)}, u32[]{:S(2)}) collective-permute-start(bf16[400,1024]{1,0:T(8,128)(2,1)} %collective-permute-done.32.refs_9_), channel_id=1, source_target_pairs={{0,4},{8,0},{16,8},{24,16},{28,24},{20,28},{12,20},{4,12},{1,5},{9... | collective-permute-start | bytes 2457608 | tf_op jit(solution)/shard_map/ppermute | solution.py:577
  249.1 13.6 %collective-permute-start.41 = (bf16[256,1024]{1,0:T(8,128)(2,1)}, bf16[256,1024]{1,0:T(8,128)(2,1)}, u32[]{:S(2)}, u32[]{:S(2)}) collective-permute-start(bf16[256,1024]{1,0:T(8,128)(2,1)} %get-tuple-element.370), channel_id=1, source_target_pairs={{0,1},{1,0},{2,3},{3,2},{4,5},{5,4},{6,7},{7,6},{8,9},{9,8},{10,11... | collective-permute-start | bytes 1572872 | tf_op jit(solution)/shard_map/ppermute | solution.py:473
  250.6 18.2 %collective-permute-start.42 = (f32[24,128]{1,0:T(8,128)S(1)}, f32[24,128]{1,0:T(8,128)S(1)}, u32[]{:S(2)}, u32[]{:S(2)}) collective-permute-start(f32[24,128]{1,0:T(8,128)S(1)} %add.113), channel_id=1, source_target_pairs={{0,8},{4,12},{8,0},{12,4},{16,24},{20,28},{24,16},{28,20},{1,9},{5... | collective-permute-start | bytes 36872 | tf_op jit(solution)/shard_map/ppermute | solution.py:1038
  254.3 21.5 %copy-start.17 = (bf16[256,1024]{1,0:T(8,128)(2,1)S(1)}, bf16[256,1024]{1,0:T(8,128)(2,1)}, u32[]{:S(2)}) copy-start(bf16[256,1024]{1,0:T(8,128)(2,1)} %get-tuple-element.370) | copy-start | bytes 1572868
  254.3 21.5 %copy-start.40 = (f32[1024]{0:T(1024)S(1)}, f32[1024]{0:T(1024)}, u32[]{:S(2)}) copy-start(f32[1024]{0:T(1024)} %param.22) | copy-start | bytes 12292
  268.9 10.8 %collective-permute-start.45 = (bf16[400,1024]{1,0:T(8,128)(2,1)S(1)}, bf16[400,1024]{1,0:T(8,128)(2,1)}, u32[]{:S(2)}, u32[]{:S(2)}) collective-permute-start(bf16[400,1024]{1,0:T(8,128)(2,1)S(1)} %collective-permute-done.37.left.refs_7_), channel_id=1, source_target_pairs={{0,2},{2,0},{1,3},{3,1},{4,6},{6,4},{5,7},{7,5},{8,10},{10,8},{9,1... | collective-permute-start | bytes 2457608 | tf_op jit(solution)/shard_map/ppermute | solution.py:442
  268.9 10.7 %collective-permute-start.46 = (bf16[400,1024]{1,0:T(8,128)(2,1)S(1)}, bf16[400,1024]{1,0:T(8,128)(2,1)}, u32[]{:S(2)}, u32[]{:S(2)}) collective-permute-start(bf16[400,1024]{1,0:T(8,128)(2,1)S(1)} %collective-permute-done.38.right.refs_9_), channel_id=1, source_target_pairs={{0,2},{2,0},{1,3},{3,1},{4,6},{6,4},{5,7},{7,5},{8,10},{10,8},{9,1... | collective-permute-start | bytes 2457608 | tf_op jit(solution)/shard_map/ppermute | solution.py:442
  272.1 14.5 %collective-permute-start.47 = (f32[24,128]{1,0:T(8,128)S(1)}, f32[24,128]{1,0:T(8,128)S(1)}, u32[]{:S(2)}, u32[]{:S(2)}) collective-permute-start(f32[24,128]{1,0:T(8,128)S(1)} %add.116), channel_id=1, source_target_pairs={{0,16},{4,20},{8,24},{12,28},{16,0},{20,4},{24,8},{28,12},{1,17},{... | collective-permute-start | bytes 36872 | tf_op jit(solution)/shard_map/ppermute | solution.py:1038
  273.8 12.8 %collective-permute-start.43 = (bf16[400,512]{1,0:T(8,128)(2,1)}, bf16[400,512]{1,0:T(8,128)(2,1)S(1)}, u32[]{:S(2)}, u32[]{:S(2)}) collective-permute-start(bf16[400,512]{1,0:T(8,128)(2,1)} %get-tuple-element.353), channel_id=1, source_target_pairs={{0,8},{8,16},{16,24},{24,28},{28,20},{20,12},{12,4},{4,0},{1,9},{9... | collective-permute-start | bytes 1228808 | tf_op jit(solution)/shard_map/ppermute | solution.py:577
  274.1 12.5 %collective-permute-start.44 = (bf16[400,512]{1,0:T(8,128)(2,1)}, bf16[400,512]{1,0:T(8,128)(2,1)}, u32[]{:S(2)}, u32[]{:S(2)}) collective-permute-start(bf16[400,512]{1,0:T(8,128)(2,1)} %get-tuple-element.354), channel_id=1, source_target_pairs={{0,4},{8,0},{16,8},{24,16},{28,24},{20,28},{12,20},{4,12},{1,5},{9... | collective-permute-start | bytes 1228808 | tf_op jit(solution)/shard_map/ppermute | solution.py:577
  286.6 1.8 collective-permute-start.48
  286.7 2.5 collective-permute-start.49
  (33 other events, 142.5 us)

commit v20 on v19

--- a/solution.py
+++ b/solution.py
@@ -167,7 +167,7 @@
 ):
     rows, model = block_input.shape
     units = up_weight.shape[1]
-    step = math.gcd(units, 512)
+    step = math.gcd(units, 1024)
     tile, line = whole_spec((rows, model)), whole_spec((1, model))
     wide = pl.BlockSpec((rows, step), lambda at, table: (0, at))
     bias = pl.BlockSpec((1, step), lambda at, table: (0, at))

time: 299 us -> 299 us (level)
  no operation moved by 1% of the time
where the time goes in v20:
time: 299 us; the launch traced here: 297 us
  Pallas kernels  124 us (41%)
  starting transfers between devices  59.3 us (20%)
  waiting for transfers between devices  52.5 us (18%)
  blocking collectives  29.6 us (10%)
  local copies, waits for them, and re-layouts  15.4 us (5%)
  other arithmetic  9.77 us (3%)
  matrix products  5.35 us (2%)
    pallas_call x5, Pallas kernels, place(): pl.pallas_call(functools.partial(place_kernel, heads, len(blocks[0]) // 2...  30.2 us
    all_to_all x1, blocking collectives, to_heads(): return lax.all_to_all(blocks, 'chip', 0, 0, tiled=True)  29.6 us
    pallas_call x2, Pallas kernels, attention_backward(): pl.pallas_call(functools.partial(backward_kernel, crops, len(extras)), gr...  24.9 us
    ppermute x24, starting transfers between devices, send(): lax.ppermute(block, 'chip', ring_pairs(direction))  24.5 us
    all_to_all x4, starting transfers between devices, to_heads(): return lax.all_to_all(blocks, 'chip', 0, 0, tiled=True)  17.3 us
    ppermute x24, waiting for transfers between devices, send(): lax.ppermute(block, 'chip', ring_pairs(direction))  15.9 us
    pallas_call x4, Pallas kernels, add(): pl.pallas_call(functools.partial(add_kernel, places, len(shapes)), grid_s...  15.6 us
    pallas_call x1, Pallas kernels, attention_forward(): pl.pallas_call(functools.partial(forward_kernel, crops, key_step(count)),...  15.3 us
  transfers between devices with their start and end apart: 54, of which 25 were waited for; matrix products, arithmetic and copies ran while one was open for 6% of the time, Pallas kernels for 36%

profile of v20, /device:TPU:0, one launch (start us, length us, event | category | flops | bytes accessed | tf_op | source)
XLA Modules:
  0.0 297.1 jit_solution(8364812125258885713)
XLA Ops:
  1.2 6.6 %project.1 = (bf16[8,208,256]{2,1,0:T(8,128)(2,1)}, bf16[256,1024]{1,0:T(8,128)(2,1)}, bf16[256,512]{1,0:T(8,128)(2,1)}) custom-call(s32[18]{0:T(128)} %compare_select_fusion.5.table.core_ref._, bf16[256,1024]{1,0:T(8,128)(2,1)} %input_ref.3, s32[1,256]{1,0:T(1,128)} %bitcast.79, s32[32]{0:T(128)} %steps_ref.1, f32[1,1024]{1,0:T(1,128)} %bitcast.61, ...), custom_call_target="tpu_custom_call" | custom-call | flops 1 | bytes 1 | tf_op jit(solution)/shard_map/project/pallas_call | solution.py:94
  7.8 29.6 %all_to_all.25.query_ref.own.piece = bf16[8,208,256]{2,1,0:T(8,128)(2,1)S(1)} all-to-all(bf16[8,208,256]{2,1,0:T(8,128)(2,1)} %get-tuple-element.207), channel_id=1, replica_groups=mesh['chip'=8,'core'=2,'head'=2] {'chip'}, dimensions={0} | all-to-all | bytes 1703936 | tf_op jit(solution)/shard_map/all_to_all | solution.py:446
  38.2 1.3 collective-permute-start.1
  40.7 15.3 %attention_forward.1 = (f32[8,64,256]{2,1,0:T(8,128)}, bf16[8,64,256]{2,1,0:T(8,128)(2,1)}, f32[8,1,256]{2,1,0:T(1,128)}) custom-call(bf16[8,208,256]{2,1,0:T(8,128)(2,1)} %copy-done, bf16[8,208,256]{2,1,0:T(8,128)(2,1)} %copy-done, bf16[8,208,256]{2,1,0:T(8,128)(2,1)} %copy-done.2), custom_call_target="tpu_custom_call" | custom-call | flops 1 | bytes 1 | tf_op jit(solution)/shard_map/attention_forward/pallas_call | solution.py:378
  56.1 3.4 %all-to-all-start.1 = ((bf16[8,64,256]{2,1,0:T(8,128)(2,1)}), bf16[8,64,256]{2,1,0:T(8,128)(2,1)S(1)}, u32[]{:S(2)}, u32[]{:S(2)}) async-start(bf16[8,64,256]{2,1,0:T(8,128)(2,1)} %get-tuple-element.214), calls=%async_computation.1 | async-start | bytes 524288 | tf_op jit(solution)/shard_map/all_to_all | solution.py:446
  59.7 9.3 %all-to-all-done.1 = bf16[8,64,256]{2,1,0:T(8,128)(2,1)S(1)} async-done(((bf16[8,64,256]{2,1,0:T(8,128)(2,1)}), bf16[8,64,256]{2,1,0:T(8,128)(2,1)S(1)}, u32[]{:S(2)}, u32[]{:S(2)}) %all-to-all-start.1) | async-done | bytes 262176 | tf_op jit(solution)/shard_map/all_to_all | solution.py:446
  69.4 1.6 collective-permute-start.7
  73.3 4.4 %collective-permute-done.3.refs_3_ = bf16[256,512]{1,0:T(8,128)(2,1)S(1)} collective-permute-done((bf16[256,512]{1,0:T(8,128)(2,1)S(1)}, bf16[256,512]{1,0:T(8,128)(2,1)S(1)}, u32[]{:S(2)}, u32[]{:S(2)}) %collective-permute-start.3) | collective-permute-done | bytes 262176 | tf_op jit(solution)/shard_map/ppermute | solution.py:577
  78.6 1.4 collective-permute-start.5
  80.6 1.4 collective-permute-done.7.refs_1_
  82.8 11.4 %mlp.1 = (bf16[256,2048]{1,0:T(8,128)(2,1)}, bf16[256,2048]{1,0:T(8,128)(2,1)}, bf16[256,1024]{1,0:T(8,128)(2,1)}, bf16[256,1024]{1,0:T(8,128)(2,1)}, f32[256,10...) custom-call(s32[18]{0:T(128)} %compare_select_fusion.5.table.core_ref._, ...), custom_call_target="tpu_custom_call" | custom-call | flops 1 | bytes 1 | tf_op jit(solution)/shard_map/mlp/pallas_call | solution.py:174
  94.8 1.5 collective-permute-start.14
  96.4 1.6 collective-permute-done.8.refs_1_.far_in
  99.7 3.3 %ring_add.4 = (bf16[256,512]{1,0:T(8,128)(2,1)}, bf16[256,512]{1,0:T(8,128)(2,1)}) custom-call(s32[18]{0:T(128)} %compare_select_fusion.5.table.core_ref._, bf16[256,1024]{1,0:T(8,128)(2,1)} %get-tuple-element.225.refs_0_.keep_in, bf16[256,1024]{1,0:T(8,128)(2,1)} %copy-done.9, bf16[256,2048]{1,0:T(8,128)(2,1)} %get-tuple-element.227.refs_2_.refs_5_.near, ...), custom_call_target="tpu_custom_call" | custom-call | flops 1 | bytes 1 | tf_op jit(solution)/shard_map/ring_add/pallas_call | solution.py:732
  103.2 1.8 collective-permute-start.11
  105.0 1.7 halves.2
  107.1 1.6 collective-permute-start.13
  109.7 4.3 %middle.1 = (f32[256,1024]{1,0:T(8,128)}, bf16[256,1024]{1,0:T(8,128)(2,1)}, bf16[512,256]{1,0:T(8,128)(2,1)}, f32[4,1024]{1,0:T(4,128)}) custom-call(f32[256,1024]{1,0:T(8,128)} %get-tuple-element.235.hidden_ref, bf16[256,1024]{1,0:T(8,128)(2,1)} %grad_ref.3, bf16[256,1024]{1,0:T(8,128)(2,1)} %get-tuple-element.238.refs_0_, bf16[256,1024]{1,0:T(8,128)(2,1)} %copy-done.28, ...), custom_call_target="tpu_custom_call" | custom-call | flops 1 | bytes 1 | tf_op jit(solution)/shard_map/middle/pallas_call | solution.py:235
  115.6 4.4 %ring_add.5 = (bf16[256,1024]{1,0:T(8,128)(2,1)}, bf16[256,1024]{1,0:T(8,128)(2,1)}) custom-call(s32[18]{0:T(128)} %compare_select_fusion.5.table.core_ref._, bf16[256,1024]{1,0:T(8,128)(2,1)} %get-tuple-element.225.refs_0_.keep_in, bf16[256,1024]{1,0:T(8,128)(2,1)} %copy-done.9, bf16[256,2048]{1,0:T(8,128)(2,1)} %get-tuple-element.227.refs_2_.refs_5_.near, ...), custom_call_target="tpu_custom_call" | custom-call | flops 1 | bytes 1 | tf_op jit(solution)/shard_map/ring_add/pallas_call | solution.py:732
  121.3 1.7 collective-permute-start.15
  123.3 4.6 %all-to-all-start.2 = ((bf16[8,64,256]{2,1,0:T(8,128)(2,1)}), bf16[8,64,256]{2,1,0:T(8,128)(2,1)S(1)}, u32[]{:S(2)}, u32[]{:S(2)}) async-start(bf16[8,64,256]{2,1,0:T(8,128)(2,1)} %bitcast.12), calls=%async_computation.2 | async-start | bytes 524288 | tf_op jit(solution)/shard_map/all_to_all | solution.py:446
  127.9 1.3 fusion.14
  129.3 3.0 join.1.refs_0_
  132.3 1.5 collective-permute-start.24
  136.1 1.6 collective-permute-done.16.refs_7_
  138.5 4.1 %ring_add.6 = (bf16[256,1024]{1,0:T(8,128)(2,1)}, bf16[256,1024]{1,0:T(8,128)(2,1)}) custom-call(s32[18]{0:T(128)} %compare_select_fusion.5.table.core_ref._, bf16[256,1024]{1,0:T(8,128)(2,1)} %get-tuple-element.225.refs_0_.keep_in, bf16[256,1024]{1,0:T(8,128)(2,1)} %copy-done.9, bf16[256,2048]{1,0:T(8,128)(2,1)} %get-tuple-element.227.refs_2_.refs_5_.near, ...), custom_call_target="tpu_custom_call" | custom-call | flops 1 | bytes 1 | tf_op jit(solution)/shard_map/ring_add/pallas_call | solution.py:732
  142.5 1.7 collective-permute-start.19
  144.5 4.7 %all-to-all-start.3 = ((bf16[8,32,1024]{2,1,0:T(8,128)(2,1)}), bf16[8,32,1024]{2,1,0:T(8,128)(2,1)}, u32[]{:S(2)}, u32[]{:S(2)}) async-start(bf16[8,32,1024]{2,1,0:T(8,128)(2,1)} %bitcast.11), calls=%async_computation.3 | async-start | bytes 1048576 | tf_op jit(solution)/shard_map/all_to_all | solution.py:446
  149.2 11.9 %attention_backward.2 = (f32[8,64,256]{2,1,0:T(8,128)S(1)}, bf16[8,128,256]{2,1,0:T(8,128)(2,1)S(1)}) custom-call(bf16[8,208,256]{2,1,0:T(8,128)(2,1)S(1)} %copy-done.1, bf16[8,64,256]{2,1,0:T(8,128)(2,1)S(1)} %all-to-all-done.2.grad_ref, f32[8,64,256]{2,1,0:T(8,128)S(1)} %copy-done.4, f32[8,1,256]{2,1,0:T(1,128)S(1)} %copy-done.5, ...), custom_call_target="tpu_custom_call" | custom-call | flops 1 | bytes 1 | tf_op jit(solution)/shard_map/attention_backward/pallas_call | solution.py:416
  161.3 3.8 %ring_add.7 = (bf16[256,1024]{1,0:T(8,128)(2,1)}, bf16[256,1024]{1,0:T(8,128)(2,1)}) custom-call(s32[18]{0:T(128)} %compare_select_fusion.5.table.core_ref._, bf16[256,1024]{1,0:T(8,128)(2,1)} %get-tuple-element.225.refs_0_.keep_in, bf16[256,1024]{1,0:T(8,128)(2,1)} %copy-done.9, bf16[256,2048]{1,0:T(8,128)(2,1)} %get-tuple-element.227.refs_2_.refs_5_.near, ...), custom_call_target="tpu_custom_call" | custom-call | flops 1 | bytes 1 | tf_op jit(solution)/shard_map/ring_add/pallas_call | solution.py:732
  165.1 2.1 collective-permute-start.21
  167.3 12.9 %attention_backward.3.grads_ref = bf16[8,192,256]{2,1,0:T(8,128)(2,1)} custom-call(bf16[8,208,256]{2,1,0:T(8,128)(2,1)S(1)} %copy-done.1, bf16[8,64,256]{2,1,0:T(8,128)(2,1)S(1)} %all-to-all-done.2.grad_ref, f32[8,64,256]{2,1,0:T(8,128)S(1)} %copy-done.4, f32[8,1,256]{2,1,0:T(1,128)S(1)} %copy-done.5, bf16[8,208,256]{2,1,0:T(8,128)(2,1)S(1)} %copy-done.1, ...), custom_call_target="tpu_custom_call" | custom-call | flops 1 | bytes 1 | tf_op jit(solution)/shard_map/attention_backward/pallas_call | solution.py:416
  181.5 4.6 %all-to-all-start.4 = ((bf16[8,192,256]{2,1,0:T(8,128)(2,1)}), bf16[8,192,256]{2,1,0:T(8,128)(2,1)S(1)}, u32[]{:S(2)}, u32[]{:S(2)}) async-start(bf16[8,192,256]{2,1,0:T(8,128)(2,1)} %attention_backward.3.grads_ref), calls=%async_computation.4 | async-start | bytes 1572864 | tf_op jit(solution)/shard_map/all_to_all | solution.py:446
  188.3 5.2 %head_gradient.1 = bf16[192,1024]{1,0:T(8,128)(2,1)} custom-call(s32[18]{0:T(128)} %compare_select_fusion.5.table.core_ref._, bf16[8,192,256]{2,1,0:T(8,128)(2,1)} %attention_backward.3.grads_ref, bf16[2048,512]{1,0:T(8,128)(2,1)} %join.1.refs_0_, bf16[2048,512]{1,0:T(8,128)(2,1)} %collective-permute-done.24.refs_1_), custom_call_target="tpu_custom_call" | custom-call | flops 1 | bytes 1 | tf_op jit(solution)/shard_map/head_gradient/pallas_call | solution.py:865
  193.4 1.7 constant_dynamic-slice_fusion
  197.2 3.9 %ring_finish.1.refs_0_ = bf16[400,1024]{1,0:T(8,128)(2,1)} custom-call(s32[18]{0:T(128)} %compare_select_fusion.5.table.core_ref._, bf16[256,1024]{1,0:T(8,128)(2,1)} %get-tuple-element.225.refs_0_.keep_in, bf16[256,1024]{1,0:T(8,128)(2,1)} %copy-done.9, bf16[256,2048]{1,0:T(8,128)(2,1)} %get-tuple-element.227.refs_2_.refs_5_.near, ...), custom_call_target="tpu_custom_call" | custom-call | flops 1 | bytes 1 | tf_op jit(solution)/shard_map/ring_finish/pallas_call | solution.py:688
  201.4 2.0 collective-permute-start.26
  203.4 2.9 all-to-all-done.4
  208.3 1.5 fusion.7
  209.8 1.6 collective-permute-start.29
  211.4 2.2 collective-permute-done.29
  214.7 4.5 %place.5 = (f32[2048,1024]{1,0:T(8,128)}, f32[1024,2048]{1,0:T(8,128)}, f32[2,8,32,1024]{3,2,1,0:T(8,128)}, f32[8,2,16,1024]{3,2,1,0:T(8,128)}, f32[1024,512]{1,...) custom-call(s32[18]{0:T(128)} %compare_select_fusion.5.table.core_ref._, bf16[400,1024]{1,0:T(8,128)(2,1)} %ring_finish.1.refs_0_, ...), custom_call_target="tpu_custom_call" | custom-call | flops 1 | bytes 1 | tf_op jit(solution)/shard_map/place/pallas_call | solution.py:778
  219.2 3.3 %collective-permute-done.26.refs_7_ = bf16[400,1024]{1,0:T(8,128)(2,1)} collective-permute-done((bf16[400,1024]{1,0:T(8,128)(2,1)}, bf16[400,1024]{1,0:T(8,128)(2,1)}, u32[]{:S(2)}, u32[]{:S(2)}) %collective-permute-start.26) | collective-permute-done | bytes 819232 | tf_op jit(solution)/shard_map/ppermute | solution.py:577
  222.5 1.5 collective-permute-done.27.refs_9_
  224.5 1.5 collective-permute-start.31
  226.5 1.5 collective-permute-start.36
  228.0 1.4 collective-permute-start.35
  230.4 6.9 %place.6 = (f32[2048,1024]{1,0:T(8,128)}, f32[1024,2048]{1,0:T(8,128)}, f32[2,8,32,1024]{3,2,1,0:T(8,128)}, f32[8,2,16,1024]{3,2,1,0:T(8,128)}, f32[1024,512]{1,...) custom-call(s32[18]{0:T(128)} %compare_select_fusion.5.table.core_re, ...), custom_call_target="tpu_custom_call", output_to_operand_aliasing={{0}: (1, {}), {1}: (2, {}), {2}: (3, {}), {3}: (4, {}), {4}... | custom-call | flops 1 | bytes 1 | tf_op jit(solution)/shard_map/place/pallas_call | solution.py:778
  237.3 2.9 collective-permute-done.36
  240.2 5.0 %collective-permute-done.35 = f32[24,128]{1,0:T(8,128)S(1)} collective-permute-done((f32[24,128]{1,0:T(8,128)S(1)}, f32[24,128]{1,0:T(8,128)S(1)}, u32[]{:S(2)}, u32[]{:S(2)}) %collective-permute-start.35) | collective-permute-done | bytes 12320 | tf_op jit(solution)/shard_map/ppermute | solution.py:1038
  246.7 1.5 collective-permute-start.37
  248.7 1.5 collective-permute-start.41
  250.3 1.5 collective-permute-start.42
  251.7 2.2 add_convert_fusion
  254.0 7.0 %place.7 = (f32[2048,1024]{1,0:T(8,128)}, f32[1024,2048]{1,0:T(8,128)}, f32[2,8,32,1024]{3,2,1,0:T(8,128)}, f32[8,2,16,1024]{3,2,1,0:T(8,128)}, f32[1024,512]{1,...) custom-call(s32[18]{0:T(128)} %compare_select_fusion.5.table.core_re, ...), custom_call_target="tpu_custom_call", output_to_operand_aliasing={{0}: (1, {}), {1}: (2, {}), {2}: (3, {}), {3}: (4, {}), {4}... | custom-call | flops 1 | bytes 1 | tf_op jit(solution)/shard_map/place/pallas_call | solution.py:778
  261.0 1.3 collective-permute-done.41
  262.3 6.2 %collective-permute-done.42 = f32[24,128]{1,0:T(8,128)S(1)} collective-permute-done((f32[24,128]{1,0:T(8,128)S(1)}, f32[24,128]{1,0:T(8,128)S(1)}, u32[]{:S(2)}, u32[]{:S(2)}) %collective-permute-start.42) | collective-permute-done | bytes 12320 | tf_op jit(solution)/shard_map/ppermute | solution.py:1038
  269.7 2.1 halves.3
  271.7 1.7 collective-permute-start.47
  273.8 1.7 collective-permute-start.44
  275.5 1.5 fusion.13
  277.0 2.3 fusion.12
  279.3 6.9 %place.8 = (f32[2048,1024]{1,0:T(8,128)}, f32[1024,2048]{1,0:T(8,128)}, f32[2,8,32,1024]{3,2,1,0:T(8,128)}, f32[8,2,16,1024]{3,2,1,0:T(8,128)}, f32[1024,512]{1,...) custom-call(s32[18]{0:T(128)} %compare_select_fusion.5.table.core_re, ...), custom_call_target="tpu_custom_call", output_to_operand_aliasing={{0}: (1, {}), {1}: (2, {}), {2}: (3, {}), {3}: (4, {}), {4}... | custom-call | flops 1 | bytes 1 | tf_op jit(solution)/shard_map/place/pallas_call | solution.py:778
  289.6 5.0 %place.9 = (f32[2048,1024]{1,0:T(8,128)}, f32[1024,2048]{1,0:T(8,128)}, f32[2,8,32,1024]{3,2,1,0:T(8,128)}, f32[8,2,16,1024]{3,2,1,0:T(8,128)}, f32[1024,512]{1,...) custom-call(s32[18]{0:T(128)} %compare_select_fusion.5.table.core_re, ...), custom_call_target="tpu_custom_call", output_to_operand_aliasing={{0}: (1, {}), {1}: (2, {}), {2}: (3, {}), {3}: (4, {}), {4}... | custom-call | flops 1 | bytes 1 | tf_op jit(solution)/shard_map/place/pallas_call | solution.py:778
  (187 shorter events, 38.7 us)
Async XLA Ops:
  7.8 51.7 %copy-start.7 = (bf16[256,1024]{1,0:T(8,128)(2,1)S(1)}, bf16[256,1024]{1,0:T(8,128)(2,1)}, u32[]{:S(2)}) copy-start(bf16[256,1024]{1,0:T(8,128)(2,1)} %input_ref.3) | copy-start | bytes 1572868
  37.4 31.5 %copy-start.11 = (bf16[512,1024]{1,0:T(8,128)(2,1)S(1)}, bf16[512,1024]{1,0:T(8,128)(2,1)}, u32[]{:S(2)}) copy-start(bf16[512,1024]{1,0:T(8,128)(2,1)} %refs_3_.1) | copy-start | bytes 3145732
  37.5 2.4 collective-permute-start.2
  37.5 18.6 %collective-permute-start = (bf16[256,512]{1,0:T(8,128)(2,1)}, bf16[256,512]{1,0:T(8,128)(2,1)S(1)}, u32[]{:S(2)}, u32[]{:S(2)}) collective-permute-start(bf16[256,512]{1,0:T(8,128)(2,1)} %get-tuple-element.209.refs_0_), channel_id=1, source_target_pairs={{0,8},{8,16},{16,24},{24,28},{28,20},{20,12},{12,4},{4,0},{1,9},{9... | collective-permute-start | bytes 786440 | tf_op jit(solution)/shard_map/ppermute | solution.py:577
  38.2 17.8 %collective-permute-start.1 = (bf16[256,512]{1,0:T(8,128)(2,1)}, bf16[256,512]{1,0:T(8,128)(2,1)}, u32[]{:S(2)}, u32[]{:S(2)}) collective-permute-start(bf16[256,512]{1,0:T(8,128)(2,1)} %get-tuple-element.209.refs_0_), channel_id=1, source_target_pairs={{0,4},{8,0},{16,8},{24,16},{28,24},{20,28},{12,20},{4,12},{1,5},{9... | collective-permute-start | bytes 786440 | tf_op jit(solution)/shard_map/ppermute | solution.py:577
  56.0 38.1 %copy-start.32 = (bf16[256,512]{1,0:T(8,128)(2,1)}, bf16[256,512]{1,0:T(8,128)(2,1)S(1)}, u32[]{:S(2)}) copy-start(bf16[256,512]{1,0:T(8,128)(2,1)S(1)} %collective-permute-done.refs_1_) | copy-start | bytes 786436
  56.1 12.9 %all-to-all-start.1 = ((bf16[8,64,256]{2,1,0:T(8,128)(2,1)}), bf16[8,64,256]{2,1,0:T(8,128)(2,1)S(1)}, u32[]{:S(2)}, u32[]{:S(2)}) async-start(bf16[8,64,256]{2,1,0:T(8,128)(2,1)} %get-tuple-element.214), calls=%async_computation.1 | async-start | bytes 524288 | tf_op jit(solution)/shard_map/all_to_all | solution.py:446
  69.4 12.6 %collective-permute-start.7 = (bf16[256,1024]{1,0:T(8,128)(2,1)S(1)}, bf16[256,1024]{1,0:T(8,128)(2,1)S(1)}, u32[]{:S(2)}, u32[]{:S(2)}) collective-permute-start(bf16[256,1024]{1,0:T(8,128)(2,1)S(1)} %convolution_convert_fusion.refs_0_), channel_id=1, source_target_pairs={{0,1},{1,0},{2,3},{3,2},{4,5},{5,4},{6,7},{7,6},{8,9},{9,8},{10,11... | collective-permute-start | bytes 1572872 | tf_op jit(solution)/shard_map/ppermute | solution.py:473
  71.0 6.7 %collective-permute-start.3 = (bf16[256,512]{1,0:T(8,128)(2,1)S(1)}, bf16[256,512]{1,0:T(8,128)(2,1)S(1)}, u32[]{:S(2)}, u32[]{:S(2)}) collective-permute-start(bf16[256,512]{1,0:T(8,128)(2,1)S(1)} %collective-permute-done.refs_1_), channel_id=1, source_target_pairs={{0,8},{8,16},{16,24},{24,28},{28,20},{20,12},{12,4},{4,0},{1,9},{9... | collective-permute-start | bytes 786440 | tf_op jit(solution)/shard_map/ppermute | solution.py:577
  72.0 6.6 %collective-permute-start.4 = (bf16[256,512]{1,0:T(8,128)(2,1)}, bf16[256,512]{1,0:T(8,128)(2,1)S(1)}, u32[]{:S(2)}, u32[]{:S(2)}) collective-permute-start(bf16[256,512]{1,0:T(8,128)(2,1)} %collective-permute-done.1.refs_2_), channel_id=1, source_target_pairs={{0,4},{8,0},{16,8},{24,16},{28,24},{20,28},{12,20},{4,12},{1,5},{9... | collective-permute-start | bytes 786440 | tf_op jit(solution)/shard_map/ppermute | solution.py:577
  77.7 25.3 %copy-start.33 = (bf16[256,512]{1,0:T(8,128)(2,1)}, bf16[256,512]{1,0:T(8,128)(2,1)S(1)}, u32[]{:S(2)}) copy-start(bf16[256,512]{1,0:T(8,128)(2,1)S(1)} %collective-permute-done.3.refs_3_) | copy-start | bytes 786436
  78.6 15.6 %copy-start.34 = (bf16[256,512]{1,0:T(8,128)(2,1)}, bf16[256,512]{1,0:T(8,128)(2,1)S(1)}, u32[]{:S(2)}) copy-start(bf16[256,512]{1,0:T(8,128)(2,1)S(1)} %collective-permute-done.4.refs_4_) | copy-start | bytes 786436
  78.6 15.6 %collective-permute-start.5 = (bf16[256,512]{1,0:T(8,128)(2,1)S(1)}, bf16[256,512]{1,0:T(8,128)(2,1)S(1)}, u32[]{:S(2)}, u32[]{:S(2)}) collective-permute-start(bf16[256,512]{1,0:T(8,128)(2,1)S(1)} %collective-permute-done.3.refs_3_), channel_id=1, source_target_pairs={{0,8},{8,16},{16,24},{24,28},{28,20},{20,12},{12,4},{4,0},{1,9},{9... | collective-permute-start | bytes 786440 | tf_op jit(solution)/shard_map/ppermute | solution.py:577
  80.1 14.2 %collective-permute-start.6 = (bf16[256,512]{1,0:T(8,128)(2,1)S(1)}, bf16[256,512]{1,0:T(8,128)(2,1)S(1)}, u32[]{:S(2)}, u32[]{:S(2)}) collective-permute-start(bf16[256,512]{1,0:T(8,128)(2,1)S(1)} %collective-permute-done.4.refs_4_), channel_id=1, source_target_pairs={{0,4},{8,0},{16,8},{24,16},{28,24},{20,28},{12,20},{4,12},{1,5},{9... | collective-permute-start | bytes 786440 | tf_op jit(solution)/shard_map/ppermute | solution.py:577
  94.2 3.7 %collective-permute-start.9 = (bf16[256,2048]{1,0:T(8,128)(2,1)}, bf16[256,2048]{1,0:T(8,128)(2,1)S(1)}, u32[]{:S(2)}, u32[]{:S(2)}) collective-permute-start(bf16[256,2048]{1,0:T(8,128)(2,1)} %get-tuple-element.228), channel_id=1, source_target_pairs={{0,2},{2,0},{1,3},{3,1},{4,6},{6,4},{5,7},{7,5},{8,10},{10,8},{9,1... | collective-permute-start | bytes 3145736 | tf_op jit(solution)/shard_map/ppermute | solution.py:442
  94.3 3.6 %collective-permute-start.8 = (bf16[256,1024]{1,0:T(8,128)(2,1)}, bf16[256,1024]{1,0:T(8,128)(2,1)S(1)}, u32[]{:S(2)}, u32[]{:S(2)}) collective-permute-start(bf16[256,1024]{1,0:T(8,128)(2,1)} %get-tuple-element.226), channel_id=1, source_target_pairs={{0,2},{2,0},{1,3},{3,1},{4,6},{6,4},{5,7},{7,5},{8,10},{10,8},{9,1... | collective-permute-start | bytes 1572872 | tf_op jit(solution)/shard_map/ppermute | solution.py:442
  94.8 14.1 %collective-permute-start.14 = (bf16[256,1024]{1,0:T(8,128)(2,1)}, bf16[256,1024]{1,0:T(8,128)(2,1)S(1)}, u32[]{:S(2)}, u32[]{:S(2)}) collective-permute-start(bf16[256,1024]{1,0:T(8,128)(2,1)} %get-tuple-element.238.refs_0_), channel_id=1, source_target_pairs={{0,1},{1,0},{2,3},{3,2},{4,5},{5,4},{6,7},{7,6},{8,9},{9,8},{10,11... | collective-permute-start | bytes 1572872 | tf_op jit(solution)/shard_map/ppermute | solution.py:473
  103.0 11.8 %collective-permute-start.10 = (bf16[256,512]{1,0:T(8,128)(2,1)}, bf16[256,512]{1,0:T(8,128)(2,1)S(1)}, u32[]{:S(2)}, u32[]{:S(2)}) collective-permute-start(bf16[256,512]{1,0:T(8,128)(2,1)} %get-tuple-element.229), channel_id=1, source_target_pairs={{0,8},{8,16},{16,24},{24,28},{28,20},{20,12},{12,4},{4,0},{1,9},{9... | collective-permute-start | bytes 786440 | tf_op jit(solution)/shard_map/ppermute | solution.py:650
  103.2 11.6 %collective-permute-start.11 = (bf16[256,512]{1,0:T(8,128)(2,1)}, bf16[256,512]{1,0:T(8,128)(2,1)S(1)}, u32[]{:S(2)}, u32[]{:S(2)}) collective-permute-start(bf16[256,512]{1,0:T(8,128)(2,1)} %get-tuple-element.230), channel_id=1, source_target_pairs={{0,4},{8,0},{16,8},{24,16},{28,24},{20,28},{12,20},{4,12},{1,5},{9... | collective-permute-start | bytes 786440 | tf_op jit(solution)/shard_map/ppermute | solution.py:650
  106.7 7.6 %collective-permute-start.12 = (bf16[256,256]{1,0:T(8,128)(2,1)}, bf16[256,256]{1,0:T(8,128)(2,1)S(1)}, u32[]{:S(2)}, u32[]{:S(2)}) collective-permute-start(bf16[256,256]{1,0:T(8,128)(2,1)} %get-tuple-element.233), channel_id=1, source_target_pairs={{0,8},{8,16},{16,24},{24,28},{28,20},{20,12},{12,4},{4,0},{1,9},{9... | collective-permute-start | bytes 393224 | tf_op jit(solution)/shard_map/ppermute | solution.py:577
  107.1 7.6 %collective-permute-start.13 = (bf16[256,256]{1,0:T(8,128)(2,1)}, bf16[256,256]{1,0:T(8,128)(2,1)S(1)}, u32[]{:S(2)}, u32[]{:S(2)}) collective-permute-start(bf16[256,256]{1,0:T(8,128)(2,1)} %get-tuple-element.234), channel_id=1, source_target_pairs={{0,4},{8,0},{16,8},{24,16},{28,24},{20,28},{12,20},{4,12},{1,5},{9... | collective-permute-start | bytes 393224 | tf_op jit(solution)/shard_map/ppermute | solution.py:577
  114.3 14.9 %copy-start.38 = (bf16[256,256]{1,0:T(8,128)(2,1)}, bf16[256,256]{1,0:T(8,128)(2,1)S(1)}, u32[]{:S(2)}) copy-start(bf16[256,256]{1,0:T(8,128)(2,1)S(1)} %collective-permute-done.12.refs_7_) | copy-start | bytes 393220
  120.1 3.3 %collective-permute-start.18 = (bf16[256,1024]{1,0:T(8,128)(2,1)S(1)}, bf16[256,1024]{1,0:T(8,128)(2,1)S(1)}, u32[]{:S(2)}, u32[]{:S(2)}) collective-permute-start(bf16[256,1024]{1,0:T(8,128)(2,1)S(1)} %copy-done.27), channel_id=1, source_target_pairs={{0,2},{2,0},{1,3},{3,1},{4,6},{6,4},{5,7},{7,5},{8,10},{10,8},{9,1... | collective-permute-start | bytes 1572872 | tf_op jit(solution)/shard_map/ppermute | solution.py:442
  120.8 13.0 %collective-permute-start.17 = (bf16[256,256]{1,0:T(8,128)(2,1)}, bf16[256,256]{1,0:T(8,128)(2,1)S(1)}, u32[]{:S(2)}, u32[]{:S(2)}) collective-permute-start(bf16[256,256]{1,0:T(8,128)(2,1)} %constant_dynamic-slice_fusion.2), channel_id=1, source_target_pairs={{0,2},{2,0},{1,3},{3,1},{4,6},{6,4},{5,7},{7,5},{8,10},{10,8},{9,1... | collective-permute-start | bytes 393224 | tf_op jit(solution)/shard_map/ppermute | solution.py:442
  121.3 14.8 %collective-permute-start.15 = (bf16[256,1024]{1,0:T(8,128)(2,1)}, bf16[256,1024]{1,0:T(8,128)(2,1)S(1)}, u32[]{:S(2)}, u32[]{:S(2)}) collective-permute-start(bf16[256,1024]{1,0:T(8,128)(2,1)} %get-tuple-element.250), channel_id=1, source_target_pairs={{0,8},{8,16},{16,24},{24,28},{28,20},{20,12},{12,4},{4,0},{1,9},{9... | collective-permute-start | bytes 1572872 | tf_op jit(solution)/shard_map/ppermute | solution.py:650
  123.0 14.6 %collective-permute-start.16 = (bf16[256,1024]{1,0:T(8,128)(2,1)}, bf16[256,1024]{1,0:T(8,128)(2,1)S(1)}, u32[]{:S(2)}, u32[]{:S(2)}) collective-permute-start(bf16[256,1024]{1,0:T(8,128)(2,1)} %get-tuple-element.251), channel_id=1, source_target_pairs={{0,4},{8,0},{16,8},{24,16},{28,24},{20,28},{12,20},{4,12},{1,5},{9... | collective-permute-start | bytes 1572872 | tf_op jit(solution)/shard_map/ppermute | solution.py:650
  123.3 21.2 %all-to-all-start.2 = ((bf16[8,64,256]{2,1,0:T(8,128)(2,1)}), bf16[8,64,256]{2,1,0:T(8,128)(2,1)S(1)}, u32[]{:S(2)}, u32[]{:S(2)}) async-start(bf16[8,64,256]{2,1,0:T(8,128)(2,1)} %bitcast.12), calls=%async_computation.2 | async-start | bytes 524288 | tf_op jit(solution)/shard_map/all_to_all | solution.py:446
  132.3 56.0 %collective-permute-start.24 = (bf16[2048,512]{1,0:T(8,128)(2,1)}, bf16[2048,512]{1,0:T(8,128)(2,1)}, u32[]{:S(2)}, u32[]{:S(2)}) collective-permute-start(bf16[2048,512]{1,0:T(8,128)(2,1)} %join.1.refs_0_), channel_id=1, source_target_pairs={{0,1},{1,0},{2,3},{3,2},{4,5},{5,4},{6,7},{7,6},{8,9},{9,8},{10,11... | collective-permute-start | bytes 6291464 | tf_op jit(solution)/shard_map/ppermute | solution.py:473
  142.5 18.7 %collective-permute-start.19 = (bf16[256,1024]{1,0:T(8,128)(2,1)}, bf16[256,1024]{1,0:T(8,128)(2,1)}, u32[]{:S(2)}, u32[]{:S(2)}) collective-permute-start(bf16[256,1024]{1,0:T(8,128)(2,1)} %get-tuple-element.260), channel_id=1, source_target_pairs={{0,8},{8,16},{16,24},{24,28},{28,20},{20,12},{12,4},{4,0},{1,9},{9... | collective-permute-start | bytes 1572872 | tf_op jit(solution)/shard_map/ppermute | solution.py:650
  144.2 17.0 %collective-permute-start.20 = (bf16[256,1024]{1,0:T(8,128)(2,1)}, bf16[256,1024]{1,0:T(8,128)(2,1)}, u32[]{:S(2)}, u32[]{:S(2)}) collective-permute-start(bf16[256,1024]{1,0:T(8,128)(2,1)} %get-tuple-element.261), channel_id=1, source_target_pairs={{0,4},{8,0},{16,8},{24,16},{28,24},{20,28},{12,20},{4,12},{1,5},{9... | collective-permute-start | bytes 1572872 | tf_op jit(solution)/shard_map/ppermute | solution.py:650
  144.5 36.9 %all-to-all-start.3 = ((bf16[8,32,1024]{2,1,0:T(8,128)(2,1)}), bf16[8,32,1024]{2,1,0:T(8,128)(2,1)}, u32[]{:S(2)}, u32[]{:S(2)}) async-start(bf16[8,32,1024]{2,1,0:T(8,128)(2,1)} %bitcast.11), calls=%async_computation.3 | async-start | bytes 1048576 | tf_op jit(solution)/shard_map/all_to_all | solution.py:446
  161.2 6.1 %collective-permute-start.23 = (bf16[8,128,256]{2,1,0:T(8,128)(2,1)S(1)}, bf16[8,128,256]{2,1,0:T(8,128)(2,1)S(1)}, u32[]{:S(2)}, u32[]{:S(2)}) collective-permute-start(bf16[8,128,256]{2,1,0:T(8,128)(2,1)S(1)} %get-tuple-element.276), channel_id=1, source_target_pairs={{0,2},{2,0},{1,3},{3,1},{4,6},{6,4},{5,7},{7,5},{8,10},{10,8},{9,1... | collective-permute-start | bytes 1572872 | tf_op jit(solution)/shard_map/ppermute | solution.py:442
  165.1 15.1 %collective-permute-start.21 = (bf16[256,1024]{1,0:T(8,128)(2,1)}, bf16[256,1024]{1,0:T(8,128)(2,1)}, u32[]{:S(2)}, u32[]{:S(2)}) collective-permute-start(bf16[256,1024]{1,0:T(8,128)(2,1)} %get-tuple-element.272), channel_id=1, source_target_pairs={{0,8},{8,16},{16,24},{24,28},{28,20},{20,12},{12,4},{4,0},{1,9},{9... | collective-permute-start | bytes 1572872 | tf_op jit(solution)/shard_map/ppermute | solution.py:650
  167.2 14.2 %collective-permute-start.22 = (bf16[256,1024]{1,0:T(8,128)(2,1)}, bf16[256,1024]{1,0:T(8,128)(2,1)}, u32[]{:S(2)}, u32[]{:S(2)}) collective-permute-start(bf16[256,1024]{1,0:T(8,128)(2,1)} %get-tuple-element.273), channel_id=1, source_target_pairs={{0,4},{8,0},{16,8},{24,16},{28,24},{20,28},{12,20},{4,12},{1,5},{9... | collective-permute-start | bytes 1572872 | tf_op jit(solution)/shard_map/ppermute | solution.py:650
  181.5 24.8 %all-to-all-start.4 = ((bf16[8,192,256]{2,1,0:T(8,128)(2,1)}), bf16[8,192,256]{2,1,0:T(8,128)(2,1)S(1)}, u32[]{:S(2)}, u32[]{:S(2)}) async-start(bf16[8,192,256]{2,1,0:T(8,128)(2,1)} %attention_backward.3.grads_ref), calls=%async_computation.4 | async-start | bytes 1572864 | tf_op jit(solution)/shard_map/all_to_all | solution.py:446
  195.1 1.4 collective-permute-start.25
  201.2 13.6 %collective-permute-start.28 = (bf16[400,1024]{1,0:T(8,128)(2,1)}, bf16[400,1024]{1,0:T(8,128)(2,1)}, u32[]{:S(2)}, u32[]{:S(2)}) collective-permute-start(bf16[400,1024]{1,0:T(8,128)(2,1)} %ring_finish.1.refs_0_), channel_id=1, source_target_pairs={{0,2},{2,0},{1,3},{3,1},{4,6},{6,4},{5,7},{7,5},{8,10},{10,8},{9,1... | collective-permute-start | bytes 2457608 | tf_op jit(solution)/shard_map/ppermute | solution.py:442
  201.4 21.1 %collective-permute-start.26 = (bf16[400,1024]{1,0:T(8,128)(2,1)}, bf16[400,1024]{1,0:T(8,128)(2,1)}, u32[]{:S(2)}, u32[]{:S(2)}) collective-permute-start(bf16[400,1024]{1,0:T(8,128)(2,1)} %ring_finish.1.refs_0_), channel_id=1, source_target_pairs={{0,8},{8,16},{16,24},{24,28},{28,20},{20,12},{12,4},{4,0},{1,9},{9... | collective-permute-start | bytes 2457608 | tf_op jit(solution)/shard_map/ppermute | solution.py:577
  203.4 20.6 %collective-permute-start.27 = (bf16[400,1024]{1,0:T(8,128)(2,1)}, bf16[400,1024]{1,0:T(8,128)(2,1)}, u32[]{:S(2)}, u32[]{:S(2)}) collective-permute-start(bf16[400,1024]{1,0:T(8,128)(2,1)} %ring_finish.1.refs_0_), channel_id=1, source_target_pairs={{0,4},{8,0},{16,8},{24,16},{28,24},{20,28},{12,20},{4,12},{1,5},{9... | collective-permute-start | bytes 2457608 | tf_op jit(solution)/shard_map/ppermute | solution.py:577
  209.8 3.8 %collective-permute-start.29 = (f32[24,128]{1,0:T(8,128)S(1)}, f32[24,128]{1,0:T(8,128)S(1)}, u32[]{:S(2)}, u32[]{:S(2)}) collective-permute-start(f32[24,128]{1,0:T(8,128)S(1)} %reshape.125), channel_id=1, source_target_pairs={{0,1},{1,0},{2,3},{3,2},{4,5},{5,4},{6,7},{7,6},{8,9},{9,8},{10,11... | collective-permute-start | bytes 36872 | tf_op jit(solution)/shard_map/ppermute | solution.py:473
  213.6 1.2 collective-permute-start.30
  224.0 27.7 %copy-start.10 = (f32[256,1024]{1,0:T(8,128)S(1)}, f32[256,1024]{1,0:T(8,128)}, u32[]{:S(2)}) copy-start(f32[256,1024]{1,0:T(8,128)} %get-tuple-element.235.hidden_ref) | copy-start | bytes 3145732
  224.0 27.7 %copy-start.42 = (f32[1024]{0:T(1024)S(1)}, f32[1024]{0:T(1024)}, u32[]{:S(2)}) copy-start(f32[1024]{0:T(1024)} %param.35) | copy-start | bytes 12292
  224.0 4.1 %collective-permute-start.33 = (bf16[400,1024]{1,0:T(8,128)(2,1)}, bf16[400,1024]{1,0:T(8,128)(2,1)S(1)}, u32[]{:S(2)}, u32[]{:S(2)}) collective-permute-start(bf16[400,1024]{1,0:T(8,128)(2,1)} %collective-permute-done.26.refs_7_), channel_id=1, source_target_pairs={{0,2},{2,0},{1,3},{3,1},{4,6},{6,4},{5,7},{7,5},{8,10},{10,8},{9,1... | collective-permute-start | bytes 2457608 | tf_op jit(solution)/shard_map/ppermute | solution.py:442
  224.0 5.5 %collective-permute-start.34 = (bf16[400,1024]{1,0:T(8,128)(2,1)}, bf16[400,1024]{1,0:T(8,128)(2,1)S(1)}, u32[]{:S(2)}, u32[]{:S(2)}) collective-permute-start(bf16[400,1024]{1,0:T(8,128)(2,1)} %collective-permute-done.27.refs_9_), channel_id=1, source_target_pairs={{0,2},{2,0},{1,3},{3,1},{4,6},{6,4},{5,7},{7,5},{8,10},{10,8},{9,1... | collective-permute-start | bytes 2457608 | tf_op jit(solution)/shard_map/ppermute | solution.py:442
  224.5 20.7 %collective-permute-start.31 = (bf16[400,1024]{1,0:T(8,128)(2,1)}, bf16[400,1024]{1,0:T(8,128)(2,1)}, u32[]{:S(2)}, u32[]{:S(2)}) collective-permute-start(bf16[400,1024]{1,0:T(8,128)(2,1)} %collective-permute-done.26.refs_7_), channel_id=1, source_target_pairs={{0,8},{8,16},{16,24},{24,28},{28,20},{20,12},{12,4},{4,0},{1,9},{9... | collective-permute-start | bytes 2457608 | tf_op jit(solution)/shard_map/ppermute | solution.py:577
  225.9 20.2 %collective-permute-start.32 = (bf16[400,1024]{1,0:T(8,128)(2,1)}, bf16[400,1024]{1,0:T(8,128)(2,1)}, u32[]{:S(2)}, u32[]{:S(2)}) collective-permute-start(bf16[400,1024]{1,0:T(8,128)(2,1)} %collective-permute-done.27.refs_9_), channel_id=1, source_target_pairs={{0,4},{8,0},{16,8},{24,16},{28,24},{20,28},{12,20},{4,12},{1,5},{9... | collective-permute-start | bytes 2457608 | tf_op jit(solution)/shard_map/ppermute | solution.py:577
  226.5 13.6 %collective-permute-start.36 = (bf16[256,1024]{1,0:T(8,128)(2,1)}, bf16[256,1024]{1,0:T(8,128)(2,1)}, u32[]{:S(2)}, u32[]{:S(2)}) collective-permute-start(bf16[256,1024]{1,0:T(8,128)(2,1)} %get-tuple-element.339), channel_id=1, source_target_pairs={{0,1},{1,0},{2,3},{3,2},{4,5},{5,4},{6,7},{7,6},{8,9},{9,8},{10,11... | collective-permute-start | bytes 1572872 | tf_op jit(solution)/shard_map/ppermute | solution.py:473
  228.0 17.1 %collective-permute-start.35 = (f32[24,128]{1,0:T(8,128)S(1)}, f32[24,128]{1,0:T(8,128)S(1)}, u32[]{:S(2)}, u32[]{:S(2)}) collective-permute-start(f32[24,128]{1,0:T(8,128)S(1)} %add.108), channel_id=1, source_target_pairs={{0,4},{4,0},{8,12},{12,8},{16,20},{20,16},{24,28},{28,24},{1,5},{5... | collective-permute-start | bytes 36872 | tf_op jit(solution)/shard_map/ppermute | solution.py:1038
  246.2 4.1 %collective-permute-start.39 = (bf16[400,1024]{1,0:T(8,128)(2,1)}, bf16[400,1024]{1,0:T(8,128)(2,1)}, u32[]{:S(2)}, u32[]{:S(2)}) collective-permute-start(bf16[400,1024]{1,0:T(8,128)(2,1)} %collective-permute-done.31.refs_7_), channel_id=1, source_target_pairs={{0,2},{2,0},{1,3},{3,1},{4,6},{6,4},{5,7},{7,5},{8,10},{10,8},{9,1... | collective-permute-start | bytes 2457608 | tf_op jit(solution)/shard_map/ppermute | solution.py:442
  246.2 7.8 %collective-permute-start.40 = (bf16[400,1024]{1,0:T(8,128)(2,1)}, bf16[400,1024]{1,0:T(8,128)(2,1)}, u32[]{:S(2)}, u32[]{:S(2)}) collective-permute-start(bf16[400,1024]{1,0:T(8,128)(2,1)} %collective-permute-done.32.refs_9_), channel_id=1, source_target_pairs={{0,2},{2,0},{1,3},{3,1},{4,6},{6,4},{5,7},{7,5},{8,10},{10,8},{9,1... | collective-permute-start | bytes 2457608 | tf_op jit(solution)/shard_map/ppermute | solution.py:442
  246.7 21.8 %collective-permute-start.37 = (bf16[400,1024]{1,0:T(8,128)(2,1)}, bf16[400,1024]{1,0:T(8,128)(2,1)S(1)}, u32[]{:S(2)}, u32[]{:S(2)}) collective-permute-start(bf16[400,1024]{1,0:T(8,128)(2,1)} %collective-permute-done.31.refs_7_), channel_id=1, source_target_pairs={{0,8},{8,16},{16,24},{24,28},{28,20},{20,12},{12,4},{4,0},{1,9},{9... | collective-permute-start | bytes 2457608 | tf_op jit(solution)/shard_map/ppermute | solution.py:577
  248.2 20.4 %collective-permute-start.38 = (bf16[400,1024]{1,0:T(8,128)(2,1)}, bf16[400,1024]{1,0:T(8,128)(2,1)S(1)}, u32[]{:S(2)}, u32[]{:S(2)}) collective-permute-start(bf16[400,1024]{1,0:T(8,128)(2,1)} %collective-permute-done.32.refs_9_), channel_id=1, source_target_pairs={{0,4},{8,0},{16,8},{24,16},{28,24},{20,28},{12,20},{4,12},{1,5},{9... | collective-permute-start | bytes 2457608 | tf_op jit(solution)/shard_map/ppermute | solution.py:577
  248.7 13.6 %collective-permute-start.41 = (bf16[256,1024]{1,0:T(8,128)(2,1)}, bf16[256,1024]{1,0:T(8,128)(2,1)}, u32[]{:S(2)}, u32[]{:S(2)}) collective-permute-start(bf16[256,1024]{1,0:T(8,128)(2,1)} %get-tuple-element.370), channel_id=1, source_target_pairs={{0,1},{1,0},{2,3},{3,2},{4,5},{5,4},{6,7},{7,6},{8,9},{9,8},{10,11... | collective-permute-start | bytes 1572872 | tf_op jit(solution)/shard_map/ppermute | solution.py:473
  250.3 18.2 %collective-permute-start.42 = (f32[24,128]{1,0:T(8,128)S(1)}, f32[24,128]{1,0:T(8,128)S(1)}, u32[]{:S(2)}, u32[]{:S(2)}) collective-permute-start(f32[24,128]{1,0:T(8,128)S(1)} %add.113), channel_id=1, source_target_pairs={{0,8},{4,12},{8,0},{12,4},{16,24},{20,28},{24,16},{28,20},{1,9},{5... | collective-permute-start | bytes 36872 | tf_op jit(solution)/shard_map/ppermute | solution.py:1038
  254.0 21.5 %copy-start.17 = (bf16[256,1024]{1,0:T(8,128)(2,1)S(1)}, bf16[256,1024]{1,0:T(8,128)(2,1)}, u32[]{:S(2)}) copy-start(bf16[256,1024]{1,0:T(8,128)(2,1)} %get-tuple-element.370) | copy-start | bytes 1572868
  254.0 21.5 %copy-start.40 = (f32[1024]{0:T(1024)S(1)}, f32[1024]{0:T(1024)}, u32[]{:S(2)}) copy-start(f32[1024]{0:T(1024)} %param.22) | copy-start | bytes 12292
  268.5 10.8 %collective-permute-start.45 = (bf16[400,1024]{1,0:T(8,128)(2,1)S(1)}, bf16[400,1024]{1,0:T(8,128)(2,1)}, u32[]{:S(2)}, u32[]{:S(2)}) collective-permute-start(bf16[400,1024]{1,0:T(8,128)(2,1)S(1)} %collective-permute-done.37.left.refs_7_), channel_id=1, source_target_pairs={{0,2},{2,0},{1,3},{3,1},{4,6},{6,4},{5,7},{7,5},{8,10},{10,8},{9,1... | collective-permute-start | bytes 2457608 | tf_op jit(solution)/shard_map/ppermute | solution.py:442
  268.6 10.7 %collective-permute-start.46 = (bf16[400,1024]{1,0:T(8,128)(2,1)S(1)}, bf16[400,1024]{1,0:T(8,128)(2,1)}, u32[]{:S(2)}, u32[]{:S(2)}) collective-permute-start(bf16[400,1024]{1,0:T(8,128)(2,1)S(1)} %collective-permute-done.38.right.refs_9_), channel_id=1, source_target_pairs={{0,2},{2,0},{1,3},{3,1},{4,6},{6,4},{5,7},{7,5},{8,10},{10,8},{9,1... | collective-permute-start | bytes 2457608 | tf_op jit(solution)/shard_map/ppermute | solution.py:442
  271.7 14.5 %collective-permute-start.47 = (f32[24,128]{1,0:T(8,128)S(1)}, f32[24,128]{1,0:T(8,128)S(1)}, u32[]{:S(2)}, u32[]{:S(2)}) collective-permute-start(f32[24,128]{1,0:T(8,128)S(1)} %add.116), channel_id=1, source_target_pairs={{0,16},{4,20},{8,24},{12,28},{16,0},{20,4},{24,8},{28,12},{1,17},{... | collective-permute-start | bytes 36872 | tf_op jit(solution)/shard_map/ppermute | solution.py:1038
  273.5 12.8 %collective-permute-start.43 = (bf16[400,512]{1,0:T(8,128)(2,1)}, bf16[400,512]{1,0:T(8,128)(2,1)S(1)}, u32[]{:S(2)}, u32[]{:S(2)}) collective-permute-start(bf16[400,512]{1,0:T(8,128)(2,1)} %get-tuple-element.353), channel_id=1, source_target_pairs={{0,8},{8,16},{16,24},{24,28},{28,20},{20,12},{12,4},{4,0},{1,9},{9... | collective-permute-start | bytes 1228808 | tf_op jit(solution)/shard_map/ppermute | solution.py:577
  273.8 12.5 %collective-permute-start.44 = (bf16[400,512]{1,0:T(8,128)(2,1)}, bf16[400,512]{1,0:T(8,128)(2,1)}, u32[]{:S(2)}, u32[]{:S(2)}) collective-permute-start(bf16[400,512]{1,0:T(8,128)(2,1)} %get-tuple-element.354), channel_id=1, source_target_pairs={{0,4},{8,0},{16,8},{24,16},{28,24},{20,28},{12,20},{4,12},{1,5},{9... | collective-permute-start | bytes 1228808 | tf_op jit(solution)/shard_map/ppermute | solution.py:577
  286.3 1.8 collective-permute-start.48
  286.3 2.5 collective-permute-start.49
  (33 other events, 142.5 us)

commit v21 on v19

--- a/solution.py
+++ b/solution.py
@@ -1037,7 +1037,8 @@
         pairs = [(chip, chip ^ reach) for chip in range(chips)]
         return [ends, lax.ppermute(ends, "chip", pairs)]
 
-    ends = step_ends(visit([gathered], ends))
+    ends = visit([gathered], step_ends(ends))
+    ends = step_ends(functools.reduce(jnp.add, ends))
     ends, mlp_out = visit([gathered], (ends, mlp_out))
     ends = step_ends(functools.reduce(jnp.add, ends))
     block_output = hidden + down_bias
@@ -1067,7 +1068,8 @@
                 blocks = lax.dynamic_update_slice(blocks, block, at)
         doutput_weight = blocks[:, :, :-small_rows].reshape(width, model)
         small = blocks[:, :, -small_rows:]
-    small = jnp.sum(small, axis=(0, 1))
+    lines = 4 - (-dup_bias.shape[1] // model)
+    small = jnp.sum(small[:, :, :lines], axis=(0, 1))
     dup_bias = small[4:].reshape(-1)[: dup_bias.shape[1]]
     return (
         block_output,

time: 299 us -> 299 us (level)
    ppermute x24, waiting for transfers between devices: 15.9 us -> 11.4 us  [send(): lax.ppermute(block, 'chip', ring_pairs(direction))]
    ppermute x3, waiting for transfers between devices: 11.2 us -> 15.6 us  [step_ends(): return [ends, lax.ppermute(ends, 'chip', pairs)]]
  transfers between devices with their start and end apart: 54 -> 54, of which waited for: 25 -> 24; matrix products, arithmetic and copies ran while one was open for 6% -> 6% of each run, Pallas kernels for 36% -> 36%
where the time goes in v21:
time: 299 us; the launch traced here: 297 us
  Pallas kernels  124 us (41%)
  starting transfers between devices  60.4 us (20%)
  waiting for transfers between devices  51.2 us (17%)
  blocking collectives  29.6 us (10%)
  local copies, waits for them, and re-layouts  15.4 us (5%)
  other arithmetic  9.57 us (3%)
  matrix products  5.35 us (2%)
    pallas_call x5, Pallas kernels, place(): pl.pallas_call(functools.partial(place_kernel, heads, len(blocks[0]) // 2...  30.2 us
    all_to_all x1, blocking collectives, to_heads(): return lax.all_to_all(blocks, 'chip', 0, 0, tiled=True)  29.6 us
    pallas_call x2, Pallas kernels, attention_backward(): pl.pallas_call(functools.partial(backward_kernel, crops, len(extras)), gr...  24.9 us
    ppermute x24, starting transfers between devices, send(): lax.ppermute(block, 'chip', ring_pairs(direction))  24.5 us
    all_to_all x4, starting transfers between devices, to_heads(): return lax.all_to_all(blocks, 'chip', 0, 0, tiled=True)  17.3 us
    ppermute x3, waiting for transfers between devices, step_ends(): return [ends, lax.ppermute(ends, 'chip', pairs)]  15.6 us
    pallas_call x4, Pallas kernels, add(): pl.pallas_call(functools.partial(add_kernel, places, len(shapes)), grid_s...  15.6 us
    pallas_call x1, Pallas kernels, attention_forward(): pl.pallas_call(functools.partial(forward_kernel, crops, key_step(count)),...  15.3 us
  transfers between devices with their start and end apart: 54, of which 24 were waited for; matrix products, arithmetic and copies ran while one was open for 6% of the time, Pallas kernels for 36%

profile of v21, /device:TPU:0, one launch (start us, length us, event | category | flops | bytes accessed | tf_op | source)
XLA Modules:
  0.0 297.1 jit_solution(13113597654692195325)
XLA Ops:
  1.2 6.6 %project.1 = (bf16[8,208,256]{2,1,0:T(8,128)(2,1)}, bf16[256,1024]{1,0:T(8,128)(2,1)}, bf16[256,512]{1,0:T(8,128)(2,1)}) custom-call(s32[18]{0:T(128)} %compare_select_fusion.5.table.core_ref._, bf16[256,1024]{1,0:T(8,128)(2,1)} %input_ref.3, s32[1,256]{1,0:T(1,128)} %bitcast.79, s32[32]{0:T(128)} %steps_ref.1, f32[1,1024]{1,0:T(1,128)} %bitcast.61, ...), custom_call_target="tpu_custom_call" | custom-call | flops 1 | bytes 1 | tf_op jit(solution)/shard_map/project/pallas_call | solution.py:94
  7.8 29.6 %all_to_all.25.query_ref.own.piece = bf16[8,208,256]{2,1,0:T(8,128)(2,1)S(1)} all-to-all(bf16[8,208,256]{2,1,0:T(8,128)(2,1)} %get-tuple-element.207), channel_id=1, replica_groups=mesh['chip'=8,'core'=2,'head'=2] {'chip'}, dimensions={0} | all-to-all | bytes 1703936 | tf_op jit(solution)/shard_map/all_to_all | solution.py:446
  38.2 1.3 collective-permute-start.1
  40.7 15.3 %attention_forward.1 = (f32[8,64,256]{2,1,0:T(8,128)}, bf16[8,64,256]{2,1,0:T(8,128)(2,1)}, f32[8,1,256]{2,1,0:T(1,128)}) custom-call(bf16[8,208,256]{2,1,0:T(8,128)(2,1)} %copy-done, bf16[8,208,256]{2,1,0:T(8,128)(2,1)} %copy-done, bf16[8,208,256]{2,1,0:T(8,128)(2,1)} %copy-done.2), custom_call_target="tpu_custom_call" | custom-call | flops 1 | bytes 1 | tf_op jit(solution)/shard_map/attention_forward/pallas_call | solution.py:378
  56.1 3.4 %all-to-all-start.1 = ((bf16[8,64,256]{2,1,0:T(8,128)(2,1)}), bf16[8,64,256]{2,1,0:T(8,128)(2,1)S(1)}, u32[]{:S(2)}, u32[]{:S(2)}) async-start(bf16[8,64,256]{2,1,0:T(8,128)(2,1)} %get-tuple-element.214), calls=%async_computation.1 | async-start | bytes 524288 | tf_op jit(solution)/shard_map/all_to_all | solution.py:446
  59.7 9.3 %all-to-all-done.1 = bf16[8,64,256]{2,1,0:T(8,128)(2,1)S(1)} async-done(((bf16[8,64,256]{2,1,0:T(8,128)(2,1)}), bf16[8,64,256]{2,1,0:T(8,128)(2,1)S(1)}, u32[]{:S(2)}, u32[]{:S(2)}) %all-to-all-start.1) | async-done | bytes 262176 | tf_op jit(solution)/shard_map/all_to_all | solution.py:446
  69.4 1.6 collective-permute-start.7
  73.3 4.4 %collective-permute-done.3.refs_3_ = bf16[256,512]{1,0:T(8,128)(2,1)S(1)} collective-permute-done((bf16[256,512]{1,0:T(8,128)(2,1)S(1)}, bf16[256,512]{1,0:T(8,128)(2,1)S(1)}, u32[]{:S(2)}, u32[]{:S(2)}) %collective-permute-start.3) | collective-permute-done | bytes 262176 | tf_op jit(solution)/shard_map/ppermute | solution.py:577
  78.6 1.4 collective-permute-start.5
  80.6 1.4 collective-permute-done.7.refs_1_
  82.8 11.7 %mlp.1 = (bf16[256,2048]{1,0:T(8,128)(2,1)}, bf16[256,2048]{1,0:T(8,128)(2,1)}, bf16[256,1024]{1,0:T(8,128)(2,1)}, bf16[256,1024]{1,0:T(8,128)(2,1)}, f32[256,10...) custom-call(s32[18]{0:T(128)} %compare_select_fusion.5.table.core_ref._, ...), custom_call_target="tpu_custom_call" | custom-call | flops 1 | bytes 1 | tf_op jit(solution)/shard_map/mlp/pallas_call | solution.py:174
  95.2 1.5 collective-permute-start.14
  96.7 1.6 collective-permute-done.8.refs_1_.far_in
  100.0 3.3 %ring_add.4 = (bf16[256,512]{1,0:T(8,128)(2,1)}, bf16[256,512]{1,0:T(8,128)(2,1)}) custom-call(s32[18]{0:T(128)} %compare_select_fusion.5.table.core_ref._, bf16[256,1024]{1,0:T(8,128)(2,1)} %get-tuple-element.225.refs_0_.keep_in, bf16[256,1024]{1,0:T(8,128)(2,1)} %copy-done.9, bf16[256,2048]{1,0:T(8,128)(2,1)} %get-tuple-element.227.refs_2_.refs_5_.near, ...), custom_call_target="tpu_custom_call" | custom-call | flops 1 | bytes 1 | tf_op jit(solution)/shard_map/ring_add/pallas_call | solution.py:732
  103.6 1.8 collective-permute-start.11
  105.3 1.7 halves.2
  107.5 1.6 collective-permute-start.13
  110.1 4.3 %middle.1 = (f32[256,1024]{1,0:T(8,128)}, bf16[256,1024]{1,0:T(8,128)(2,1)}, bf16[512,256]{1,0:T(8,128)(2,1)}, f32[4,1024]{1,0:T(4,128)}) custom-call(f32[256,1024]{1,0:T(8,128)} %get-tuple-element.235.hidden_ref, bf16[256,1024]{1,0:T(8,128)(2,1)} %grad_ref.3, bf16[256,1024]{1,0:T(8,128)(2,1)} %get-tuple-element.238.refs_0_, bf16[256,1024]{1,0:T(8,128)(2,1)} %copy-done.28, ...), custom_call_target="tpu_custom_call" | custom-call | flops 1 | bytes 1 | tf_op jit(solution)/shard_map/middle/pallas_call | solution.py:235
  116.0 4.4 %ring_add.5 = (bf16[256,1024]{1,0:T(8,128)(2,1)}, bf16[256,1024]{1,0:T(8,128)(2,1)}) custom-call(s32[18]{0:T(128)} %compare_select_fusion.5.table.core_ref._, bf16[256,1024]{1,0:T(8,128)(2,1)} %get-tuple-element.225.refs_0_.keep_in, bf16[256,1024]{1,0:T(8,128)(2,1)} %copy-done.9, bf16[256,2048]{1,0:T(8,128)(2,1)} %get-tuple-element.227.refs_2_.refs_5_.near, ...), custom_call_target="tpu_custom_call" | custom-call | flops 1 | bytes 1 | tf_op jit(solution)/shard_map/ring_add/pallas_call | solution.py:732
  121.6 1.7 collective-permute-start.15
  123.7 4.6 %all-to-all-start.2 = ((bf16[8,64,256]{2,1,0:T(8,128)(2,1)}), bf16[8,64,256]{2,1,0:T(8,128)(2,1)S(1)}, u32[]{:S(2)}, u32[]{:S(2)}) async-start(bf16[8,64,256]{2,1,0:T(8,128)(2,1)} %bitcast.12), calls=%async_computation.2 | async-start | bytes 524288 | tf_op jit(solution)/shard_map/all_to_all | solution.py:446
  128.3 1.3 fusion.14
  129.6 3.0 join.1.refs_0_
  132.6 1.5 collective-permute-start.24
  136.4 1.6 collective-permute-done.16.refs_7_
  138.8 4.1 %ring_add.6 = (bf16[256,1024]{1,0:T(8,128)(2,1)}, bf16[256,1024]{1,0:T(8,128)(2,1)}) custom-call(s32[18]{0:T(128)} %compare_select_fusion.5.table.core_ref._, bf16[256,1024]{1,0:T(8,128)(2,1)} %get-tuple-element.225.refs_0_.keep_in, bf16[256,1024]{1,0:T(8,128)(2,1)} %copy-done.9, bf16[256,2048]{1,0:T(8,128)(2,1)} %get-tuple-element.227.refs_2_.refs_5_.near, ...), custom_call_target="tpu_custom_call" | custom-call | flops 1 | bytes 1 | tf_op jit(solution)/shard_map/ring_add/pallas_call | solution.py:732
  142.9 1.7 collective-permute-start.19
  144.9 4.7 %all-to-all-start.3 = ((bf16[8,32,1024]{2,1,0:T(8,128)(2,1)}), bf16[8,32,1024]{2,1,0:T(8,128)(2,1)}, u32[]{:S(2)}, u32[]{:S(2)}) async-start(bf16[8,32,1024]{2,1,0:T(8,128)(2,1)} %bitcast.11), calls=%async_computation.3 | async-start | bytes 1048576 | tf_op jit(solution)/shard_map/all_to_all | solution.py:446
  149.6 11.9 %attention_backward.2 = (f32[8,64,256]{2,1,0:T(8,128)S(1)}, bf16[8,128,256]{2,1,0:T(8,128)(2,1)S(1)}) custom-call(bf16[8,208,256]{2,1,0:T(8,128)(2,1)S(1)} %copy-done.1, bf16[8,64,256]{2,1,0:T(8,128)(2,1)S(1)} %all-to-all-done.2.grad_ref, f32[8,64,256]{2,1,0:T(8,128)S(1)} %copy-done.4, f32[8,1,256]{2,1,0:T(1,128)S(1)} %copy-done.5, ...), custom_call_target="tpu_custom_call" | custom-call | flops 1 | bytes 1 | tf_op jit(solution)/shard_map/attention_backward/pallas_call | solution.py:416
  161.6 3.8 %ring_add.7 = (bf16[256,1024]{1,0:T(8,128)(2,1)}, bf16[256,1024]{1,0:T(8,128)(2,1)}) custom-call(s32[18]{0:T(128)} %compare_select_fusion.5.table.core_ref._, bf16[256,1024]{1,0:T(8,128)(2,1)} %get-tuple-element.225.refs_0_.keep_in, bf16[256,1024]{1,0:T(8,128)(2,1)} %copy-done.9, bf16[256,2048]{1,0:T(8,128)(2,1)} %get-tuple-element.227.refs_2_.refs_5_.near, ...), custom_call_target="tpu_custom_call" | custom-call | flops 1 | bytes 1 | tf_op jit(solution)/shard_map/ring_add/pallas_call | solution.py:732
  165.4 2.1 collective-permute-start.21
  167.6 12.9 %attention_backward.3.grads_ref = bf16[8,192,256]{2,1,0:T(8,128)(2,1)} custom-call(bf16[8,208,256]{2,1,0:T(8,128)(2,1)S(1)} %copy-done.1, bf16[8,64,256]{2,1,0:T(8,128)(2,1)S(1)} %all-to-all-done.2.grad_ref, f32[8,64,256]{2,1,0:T(8,128)S(1)} %copy-done.4, f32[8,1,256]{2,1,0:T(1,128)S(1)} %copy-done.5, bf16[8,208,256]{2,1,0:T(8,128)(2,1)S(1)} %copy-done.1, ...), custom_call_target="tpu_custom_call" | custom-call | flops 1 | bytes 1 | tf_op jit(solution)/shard_map/attention_backward/pallas_call | solution.py:416
  180.5 1.3 collective-permute-done.22.behind
  181.8 4.6 %all-to-all-start.4 = ((bf16[8,192,256]{2,1,0:T(8,128)(2,1)}), bf16[8,192,256]{2,1,0:T(8,128)(2,1)S(1)}, u32[]{:S(2)}, u32[]{:S(2)}) async-start(bf16[8,192,256]{2,1,0:T(8,128)(2,1)} %attention_backward.3.grads_ref), calls=%async_computation.4 | async-start | bytes 1572864 | tf_op jit(solution)/shard_map/all_to_all | solution.py:446
  188.6 5.2 %head_gradient.1 = bf16[192,1024]{1,0:T(8,128)(2,1)} custom-call(s32[18]{0:T(128)} %compare_select_fusion.5.table.core_ref._, bf16[8,192,256]{2,1,0:T(8,128)(2,1)} %attention_backward.3.grads_ref, bf16[2048,512]{1,0:T(8,128)(2,1)} %join.1.refs_0_, bf16[2048,512]{1,0:T(8,128)(2,1)} %collective-permute-done.24.refs_1_), custom_call_target="tpu_custom_call" | custom-call | flops 1 | bytes 1 | tf_op jit(solution)/shard_map/head_gradient/pallas_call | solution.py:865
  193.7 1.7 constant_dynamic-slice_fusion
  197.6 3.9 %ring_finish.1.refs_0_ = bf16[400,1024]{1,0:T(8,128)(2,1)} custom-call(s32[18]{0:T(128)} %compare_select_fusion.5.table.core_ref._, bf16[256,1024]{1,0:T(8,128)(2,1)} %get-tuple-element.225.refs_0_.keep_in, bf16[256,1024]{1,0:T(8,128)(2,1)} %copy-done.9, bf16[256,2048]{1,0:T(8,128)(2,1)} %get-tuple-element.227.refs_2_.refs_5_.near, ...), custom_call_target="tpu_custom_call" | custom-call | flops 1 | bytes 1 | tf_op jit(solution)/shard_map/ring_finish/pallas_call | solution.py:688
  201.7 2.0 collective-permute-start.26
  203.8 2.9 all-to-all-done.4
  208.6 1.5 fusion.7
  210.1 1.6 collective-permute-start.29
  211.7 2.2 collective-permute-done.29
  215.1 1.6 collective-permute-start.31
  216.7 4.5 %place.5 = (f32[2048,1024]{1,0:T(8,128)}, f32[1024,2048]{1,0:T(8,128)}, f32[2,8,32,1024]{3,2,1,0:T(8,128)}, f32[8,2,16,1024]{3,2,1,0:T(8,128)}, f32[1024,512]{1,...) custom-call(s32[18]{0:T(128)} %compare_select_fusion.5.table.core_ref._, bf16[400,1024]{1,0:T(8,128)(2,1)} %ring_finish.1.refs_0_, ...), custom_call_target="tpu_custom_call" | custom-call | flops 1 | bytes 1 | tf_op jit(solution)/shard_map/place/pallas_call | solution.py:778
  221.2 1.8 collective-permute-done.31
  223.0 1.3 collective-permute-done.27.refs_9_
  224.8 1.5 collective-permute-start.32
  226.8 1.5 collective-permute-start.37
  228.4 1.5 collective-permute-start.36
  230.8 6.9 %place.6 = (f32[2048,1024]{1,0:T(8,128)}, f32[1024,2048]{1,0:T(8,128)}, f32[2,8,32,1024]{3,2,1,0:T(8,128)}, f32[8,2,16,1024]{3,2,1,0:T(8,128)}, f32[1024,512]{1,...) custom-call(s32[18]{0:T(128)} %compare_select_fusion.5.table.core_re, ...), custom_call_target="tpu_custom_call", output_to_operand_aliasing={{0}: (1, {}), {1}: (2, {}), {2}: (3, {}), {3}: (4, {}), {4}... | custom-call | flops 1 | bytes 1 | tf_op jit(solution)/shard_map/place/pallas_call | solution.py:778
  237.7 2.7 collective-permute-done.37
  240.4 6.2 %collective-permute-done.36 = f32[24,128]{1,0:T(8,128)S(1)} collective-permute-done((f32[24,128]{1,0:T(8,128)S(1)}, f32[24,128]{1,0:T(8,128)S(1)}, u32[]{:S(2)}, u32[]{:S(2)}) %collective-permute-start.36) | collective-permute-done | bytes 12320 | tf_op jit(solution)/shard_map/ppermute | solution.py:1038
  247.1 1.3 collective-permute-start.38
  249.2 1.5 collective-permute-start.42
  250.7 2.6 collective-permute-start.43
  253.3 2.2 add_convert_fusion
  255.5 7.0 %place.7 = (f32[2048,1024]{1,0:T(8,128)}, f32[1024,2048]{1,0:T(8,128)}, f32[2,8,32,1024]{3,2,1,0:T(8,128)}, f32[8,2,16,1024]{3,2,1,0:T(8,128)}, f32[1024,512]{1,...) custom-call(s32[18]{0:T(128)} %compare_select_fusion.5.table.core_re, ...), custom_call_target="tpu_custom_call", output_to_operand_aliasing={{0}: (1, {}), {1}: (2, {}), {2}: (3, {}), {3}: (4, {}), {4}... | custom-call | flops 1 | bytes 1 | tf_op jit(solution)/shard_map/place/pallas_call | solution.py:778
  262.8 7.6 %collective-permute-done.43 = f32[24,128]{1,0:T(8,128)S(1)} collective-permute-done((f32[24,128]{1,0:T(8,128)S(1)}, f32[24,128]{1,0:T(8,128)S(1)}, u32[]{:S(2)}, u32[]{:S(2)}) %collective-permute-start.43) | collective-permute-done | bytes 12320 | tf_op jit(solution)/shard_map/ppermute | solution.py:1038
  271.6 2.1 halves.3
  273.8 1.9 collective-permute-start.45
  275.7 1.5 fusion.13
  277.2 2.3 fusion.12
  279.5 6.9 %place.8 = (f32[2048,1024]{1,0:T(8,128)}, f32[1024,2048]{1,0:T(8,128)}, f32[2,8,32,1024]{3,2,1,0:T(8,128)}, f32[8,2,16,1024]{3,2,1,0:T(8,128)}, f32[1024,512]{1,...) custom-call(s32[18]{0:T(128)} %compare_select_fusion.5.table.core_re, ...), custom_call_target="tpu_custom_call", output_to_operand_aliasing={{0}: (1, {}), {1}: (2, {}), {2}: (3, {}), {3}: (4, {}), {4}... | custom-call | flops 1 | bytes 1 | tf_op jit(solution)/shard_map/place/pallas_call | solution.py:778
  289.8 5.0 %place.9 = (f32[2048,1024]{1,0:T(8,128)}, f32[1024,2048]{1,0:T(8,128)}, f32[2,8,32,1024]{3,2,1,0:T(8,128)}, f32[8,2,16,1024]{3,2,1,0:T(8,128)}, f32[1024,512]{1,...) custom-call(s32[18]{0:T(128)} %compare_select_fusion.5.table.core_re, ...), custom_call_target="tpu_custom_call", output_to_operand_aliasing={{0}: (1, {}), {1}: (2, {}), {2}: (3, {}), {3}: (4, {}), {4}... | custom-call | flops 1 | bytes 1 | tf_op jit(solution)/shard_map/place/pallas_call | solution.py:778
  (187 shorter events, 36.5 us)
Async XLA Ops:
  7.8 51.7 %copy-start.7 = (bf16[256,1024]{1,0:T(8,128)(2,1)S(1)}, bf16[256,1024]{1,0:T(8,128)(2,1)}, u32[]{:S(2)}) copy-start(bf16[256,1024]{1,0:T(8,128)(2,1)} %input_ref.3) | copy-start | bytes 1572868
  37.4 31.5 %copy-start.11 = (bf16[512,1024]{1,0:T(8,128)(2,1)S(1)}, bf16[512,1024]{1,0:T(8,128)(2,1)}, u32[]{:S(2)}) copy-start(bf16[512,1024]{1,0:T(8,128)(2,1)} %refs_3_.1) | copy-start | bytes 3145732
  37.5 2.4 collective-permute-start.2
  37.5 18.6 %collective-permute-start = (bf16[256,512]{1,0:T(8,128)(2,1)}, bf16[256,512]{1,0:T(8,128)(2,1)S(1)}, u32[]{:S(2)}, u32[]{:S(2)}) collective-permute-start(bf16[256,512]{1,0:T(8,128)(2,1)} %get-tuple-element.209.refs_0_), channel_id=1, source_target_pairs={{0,8},{8,16},{16,24},{24,28},{28,20},{20,12},{12,4},{4,0},{1,9},{9... | collective-permute-start | bytes 786440 | tf_op jit(solution)/shard_map/ppermute | solution.py:577
  38.2 17.8 %collective-permute-start.1 = (bf16[256,512]{1,0:T(8,128)(2,1)}, bf16[256,512]{1,0:T(8,128)(2,1)}, u32[]{:S(2)}, u32[]{:S(2)}) collective-permute-start(bf16[256,512]{1,0:T(8,128)(2,1)} %get-tuple-element.209.refs_0_), channel_id=1, source_target_pairs={{0,4},{8,0},{16,8},{24,16},{28,24},{20,28},{12,20},{4,12},{1,5},{9... | collective-permute-start | bytes 786440 | tf_op jit(solution)/shard_map/ppermute | solution.py:577
  56.0 38.5 %copy-start.32 = (bf16[256,512]{1,0:T(8,128)(2,1)}, bf16[256,512]{1,0:T(8,128)(2,1)S(1)}, u32[]{:S(2)}) copy-start(bf16[256,512]{1,0:T(8,128)(2,1)S(1)} %collective-permute-done.refs_1_) | copy-start | bytes 786436
  56.1 12.9 %all-to-all-start.1 = ((bf16[8,64,256]{2,1,0:T(8,128)(2,1)}), bf16[8,64,256]{2,1,0:T(8,128)(2,1)S(1)}, u32[]{:S(2)}, u32[]{:S(2)}) async-start(bf16[8,64,256]{2,1,0:T(8,128)(2,1)} %get-tuple-element.214), calls=%async_computation.1 | async-start | bytes 524288 | tf_op jit(solution)/shard_map/all_to_all | solution.py:446
  69.4 12.6 %collective-permute-start.7 = (bf16[256,1024]{1,0:T(8,128)(2,1)S(1)}, bf16[256,1024]{1,0:T(8,128)(2,1)S(1)}, u32[]{:S(2)}, u32[]{:S(2)}) collective-permute-start(bf16[256,1024]{1,0:T(8,128)(2,1)S(1)} %convolution_convert_fusion.refs_0_), channel_id=1, source_target_pairs={{0,1},{1,0},{2,3},{3,2},{4,5},{5,4},{6,7},{7,6},{8,9},{9,8},{10,11... | collective-permute-start | bytes 1572872 | tf_op jit(solution)/shard_map/ppermute | solution.py:473
  71.0 6.7 %collective-permute-start.3 = (bf16[256,512]{1,0:T(8,128)(2,1)S(1)}, bf16[256,512]{1,0:T(8,128)(2,1)S(1)}, u32[]{:S(2)}, u32[]{:S(2)}) collective-permute-start(bf16[256,512]{1,0:T(8,128)(2,1)S(1)} %collective-permute-done.refs_1_), channel_id=1, source_target_pairs={{0,8},{8,16},{16,24},{24,28},{28,20},{20,12},{12,4},{4,0},{1,9},{9... | collective-permute-start | bytes 786440 | tf_op jit(solution)/shard_map/ppermute | solution.py:577
  72.0 6.6 %collective-permute-start.4 = (bf16[256,512]{1,0:T(8,128)(2,1)}, bf16[256,512]{1,0:T(8,128)(2,1)S(1)}, u32[]{:S(2)}, u32[]{:S(2)}) collective-permute-start(bf16[256,512]{1,0:T(8,128)(2,1)} %collective-permute-done.1.refs_2_), channel_id=1, source_target_pairs={{0,4},{8,0},{16,8},{24,16},{28,24},{20,28},{12,20},{4,12},{1,5},{9... | collective-permute-start | bytes 786440 | tf_op jit(solution)/shard_map/ppermute | solution.py:577
  77.7 25.7 %copy-start.33 = (bf16[256,512]{1,0:T(8,128)(2,1)}, bf16[256,512]{1,0:T(8,128)(2,1)S(1)}, u32[]{:S(2)}) copy-start(bf16[256,512]{1,0:T(8,128)(2,1)S(1)} %collective-permute-done.3.refs_3_) | copy-start | bytes 786436
  78.6 16.0 %copy-start.34 = (bf16[256,512]{1,0:T(8,128)(2,1)}, bf16[256,512]{1,0:T(8,128)(2,1)S(1)}, u32[]{:S(2)}) copy-start(bf16[256,512]{1,0:T(8,128)(2,1)S(1)} %collective-permute-done.4.refs_4_) | copy-start | bytes 786436
  78.6 15.9 %collective-permute-start.5 = (bf16[256,512]{1,0:T(8,128)(2,1)S(1)}, bf16[256,512]{1,0:T(8,128)(2,1)S(1)}, u32[]{:S(2)}, u32[]{:S(2)}) collective-permute-start(bf16[256,512]{1,0:T(8,128)(2,1)S(1)} %collective-permute-done.3.refs_3_), channel_id=1, source_target_pairs={{0,8},{8,16},{16,24},{24,28},{28,20},{20,12},{12,4},{4,0},{1,9},{9... | collective-permute-start | bytes 786440 | tf_op jit(solution)/shard_map/ppermute | solution.py:577
  80.1 14.5 %collective-permute-start.6 = (bf16[256,512]{1,0:T(8,128)(2,1)S(1)}, bf16[256,512]{1,0:T(8,128)(2,1)S(1)}, u32[]{:S(2)}, u32[]{:S(2)}) collective-permute-start(bf16[256,512]{1,0:T(8,128)(2,1)S(1)} %collective-permute-done.4.refs_4_), channel_id=1, source_target_pairs={{0,4},{8,0},{16,8},{24,16},{28,24},{20,28},{12,20},{4,12},{1,5},{9... | collective-permute-start | bytes 786440 | tf_op jit(solution)/shard_map/ppermute | solution.py:577
  94.6 3.7 %collective-permute-start.9 = (bf16[256,2048]{1,0:T(8,128)(2,1)}, bf16[256,2048]{1,0:T(8,128)(2,1)S(1)}, u32[]{:S(2)}, u32[]{:S(2)}) collective-permute-start(bf16[256,2048]{1,0:T(8,128)(2,1)} %get-tuple-element.228), channel_id=1, source_target_pairs={{0,2},{2,0},{1,3},{3,1},{4,6},{6,4},{5,7},{7,5},{8,10},{10,8},{9,1... | collective-permute-start | bytes 3145736 | tf_op jit(solution)/shard_map/ppermute | solution.py:442
  94.7 3.6 %collective-permute-start.8 = (bf16[256,1024]{1,0:T(8,128)(2,1)}, bf16[256,1024]{1,0:T(8,128)(2,1)S(1)}, u32[]{:S(2)}, u32[]{:S(2)}) collective-permute-start(bf16[256,1024]{1,0:T(8,128)(2,1)} %get-tuple-element.226), channel_id=1, source_target_pairs={{0,2},{2,0},{1,3},{3,1},{4,6},{6,4},{5,7},{7,5},{8,10},{10,8},{9,1... | collective-permute-start | bytes 1572872 | tf_op jit(solution)/shard_map/ppermute | solution.py:442
  95.2 14.1 %collective-permute-start.14 = (bf16[256,1024]{1,0:T(8,128)(2,1)}, bf16[256,1024]{1,0:T(8,128)(2,1)S(1)}, u32[]{:S(2)}, u32[]{:S(2)}) collective-permute-start(bf16[256,1024]{1,0:T(8,128)(2,1)} %get-tuple-element.238.refs_0_), channel_id=1, source_target_pairs={{0,1},{1,0},{2,3},{3,2},{4,5},{5,4},{6,7},{7,6},{8,9},{9,8},{10,11... | collective-permute-start | bytes 1572872 | tf_op jit(solution)/shard_map/ppermute | solution.py:473
  103.3 11.8 %collective-permute-start.10 = (bf16[256,512]{1,0:T(8,128)(2,1)}, bf16[256,512]{1,0:T(8,128)(2,1)S(1)}, u32[]{:S(2)}, u32[]{:S(2)}) collective-permute-start(bf16[256,512]{1,0:T(8,128)(2,1)} %get-tuple-element.229), channel_id=1, source_target_pairs={{0,8},{8,16},{16,24},{24,28},{28,20},{20,12},{12,4},{4,0},{1,9},{9... | collective-permute-start | bytes 786440 | tf_op jit(solution)/shard_map/ppermute | solution.py:650
  103.6 11.5 %collective-permute-start.11 = (bf16[256,512]{1,0:T(8,128)(2,1)}, bf16[256,512]{1,0:T(8,128)(2,1)S(1)}, u32[]{:S(2)}, u32[]{:S(2)}) collective-permute-start(bf16[256,512]{1,0:T(8,128)(2,1)} %get-tuple-element.230), channel_id=1, source_target_pairs={{0,4},{8,0},{16,8},{24,16},{28,24},{20,28},{12,20},{4,12},{1,5},{9... | collective-permute-start | bytes 786440 | tf_op jit(solution)/shard_map/ppermute | solution.py:650
  107.0 7.6 %collective-permute-start.12 = (bf16[256,256]{1,0:T(8,128)(2,1)}, bf16[256,256]{1,0:T(8,128)(2,1)S(1)}, u32[]{:S(2)}, u32[]{:S(2)}) collective-permute-start(bf16[256,256]{1,0:T(8,128)(2,1)} %get-tuple-element.233), channel_id=1, source_target_pairs={{0,8},{8,16},{16,24},{24,28},{28,20},{20,12},{12,4},{4,0},{1,9},{9... | collective-permute-start | bytes 393224 | tf_op jit(solution)/shard_map/ppermute | solution.py:577
  107.5 7.6 %collective-permute-start.13 = (bf16[256,256]{1,0:T(8,128)(2,1)}, bf16[256,256]{1,0:T(8,128)(2,1)S(1)}, u32[]{:S(2)}, u32[]{:S(2)}) collective-permute-start(bf16[256,256]{1,0:T(8,128)(2,1)} %get-tuple-element.234), channel_id=1, source_target_pairs={{0,4},{8,0},{16,8},{24,16},{28,24},{20,28},{12,20},{4,12},{1,5},{9... | collective-permute-start | bytes 393224 | tf_op jit(solution)/shard_map/ppermute | solution.py:577
  114.7 14.9 %copy-start.38 = (bf16[256,256]{1,0:T(8,128)(2,1)}, bf16[256,256]{1,0:T(8,128)(2,1)S(1)}, u32[]{:S(2)}) copy-start(bf16[256,256]{1,0:T(8,128)(2,1)S(1)} %collective-permute-done.12.refs_7_) | copy-start | bytes 393220
  120.4 3.3 %collective-permute-start.18 = (bf16[256,1024]{1,0:T(8,128)(2,1)S(1)}, bf16[256,1024]{1,0:T(8,128)(2,1)S(1)}, u32[]{:S(2)}, u32[]{:S(2)}) collective-permute-start(bf16[256,1024]{1,0:T(8,128)(2,1)S(1)} %copy-done.27), channel_id=1, source_target_pairs={{0,2},{2,0},{1,3},{3,1},{4,6},{6,4},{5,7},{7,5},{8,10},{10,8},{9,1... | collective-permute-start | bytes 1572872 | tf_op jit(solution)/shard_map/ppermute | solution.py:442
  121.1 13.0 %collective-permute-start.17 = (bf16[256,256]{1,0:T(8,128)(2,1)}, bf16[256,256]{1,0:T(8,128)(2,1)S(1)}, u32[]{:S(2)}, u32[]{:S(2)}) collective-permute-start(bf16[256,256]{1,0:T(8,128)(2,1)} %constant_dynamic-slice_fusion.2), channel_id=1, source_target_pairs={{0,2},{2,0},{1,3},{3,1},{4,6},{6,4},{5,7},{7,5},{8,10},{10,8},{9,1... | collective-permute-start | bytes 393224 | tf_op jit(solution)/shard_map/ppermute | solution.py:442
  121.6 14.8 %collective-permute-start.15 = (bf16[256,1024]{1,0:T(8,128)(2,1)}, bf16[256,1024]{1,0:T(8,128)(2,1)S(1)}, u32[]{:S(2)}, u32[]{:S(2)}) collective-permute-start(bf16[256,1024]{1,0:T(8,128)(2,1)} %get-tuple-element.250), channel_id=1, source_target_pairs={{0,8},{8,16},{16,24},{24,28},{28,20},{20,12},{12,4},{4,0},{1,9},{9... | collective-permute-start | bytes 1572872 | tf_op jit(solution)/shard_map/ppermute | solution.py:650
  123.4 14.6 %collective-permute-start.16 = (bf16[256,1024]{1,0:T(8,128)(2,1)}, bf16[256,1024]{1,0:T(8,128)(2,1)S(1)}, u32[]{:S(2)}, u32[]{:S(2)}) collective-permute-start(bf16[256,1024]{1,0:T(8,128)(2,1)} %get-tuple-element.251), channel_id=1, source_target_pairs={{0,4},{8,0},{16,8},{24,16},{28,24},{20,28},{12,20},{4,12},{1,5},{9... | collective-permute-start | bytes 1572872 | tf_op jit(solution)/shard_map/ppermute | solution.py:650
  123.7 21.2 %all-to-all-start.2 = ((bf16[8,64,256]{2,1,0:T(8,128)(2,1)}), bf16[8,64,256]{2,1,0:T(8,128)(2,1)S(1)}, u32[]{:S(2)}, u32[]{:S(2)}) async-start(bf16[8,64,256]{2,1,0:T(8,128)(2,1)} %bitcast.12), calls=%async_computation.2 | async-start | bytes 524288 | tf_op jit(solution)/shard_map/all_to_all | solution.py:446
  132.6 56.0 %collective-permute-start.24 = (bf16[2048,512]{1,0:T(8,128)(2,1)}, bf16[2048,512]{1,0:T(8,128)(2,1)}, u32[]{:S(2)}, u32[]{:S(2)}) collective-permute-start(bf16[2048,512]{1,0:T(8,128)(2,1)} %join.1.refs_0_), channel_id=1, source_target_pairs={{0,1},{1,0},{2,3},{3,2},{4,5},{5,4},{6,7},{7,6},{8,9},{9,8},{10,11... | collective-permute-start | bytes 6291464 | tf_op jit(solution)/shard_map/ppermute | solution.py:473
  142.9 18.7 %collective-permute-start.19 = (bf16[256,1024]{1,0:T(8,128)(2,1)}, bf16[256,1024]{1,0:T(8,128)(2,1)}, u32[]{:S(2)}, u32[]{:S(2)}) collective-permute-start(bf16[256,1024]{1,0:T(8,128)(2,1)} %get-tuple-element.260), channel_id=1, source_target_pairs={{0,8},{8,16},{16,24},{24,28},{28,20},{20,12},{12,4},{4,0},{1,9},{9... | collective-permute-start | bytes 1572872 | tf_op jit(solution)/shard_map/ppermute | solution.py:650
  144.6 17.0 %collective-permute-start.20 = (bf16[256,1024]{1,0:T(8,128)(2,1)}, bf16[256,1024]{1,0:T(8,128)(2,1)}, u32[]{:S(2)}, u32[]{:S(2)}) collective-permute-start(bf16[256,1024]{1,0:T(8,128)(2,1)} %get-tuple-element.261), channel_id=1, source_target_pairs={{0,4},{8,0},{16,8},{24,16},{28,24},{20,28},{12,20},{4,12},{1,5},{9... | collective-permute-start | bytes 1572872 | tf_op jit(solution)/shard_map/ppermute | solution.py:650
  144.9 36.9 %all-to-all-start.3 = ((bf16[8,32,1024]{2,1,0:T(8,128)(2,1)}), bf16[8,32,1024]{2,1,0:T(8,128)(2,1)}, u32[]{:S(2)}, u32[]{:S(2)}) async-start(bf16[8,32,1024]{2,1,0:T(8,128)(2,1)} %bitcast.11), calls=%async_computation.3 | async-start | bytes 1048576 | tf_op jit(solution)/shard_map/all_to_all | solution.py:446
  161.5 6.1 %collective-permute-start.23 = (bf16[8,128,256]{2,1,0:T(8,128)(2,1)S(1)}, bf16[8,128,256]{2,1,0:T(8,128)(2,1)S(1)}, u32[]{:S(2)}, u32[]{:S(2)}) collective-permute-start(bf16[8,128,256]{2,1,0:T(8,128)(2,1)S(1)} %get-tuple-element.276), channel_id=1, source_target_pairs={{0,2},{2,0},{1,3},{3,1},{4,6},{6,4},{5,7},{7,5},{8,10},{10,8},{9,1... | collective-permute-start | bytes 1572872 | tf_op jit(solution)/shard_map/ppermute | solution.py:442
  165.4 15.1 %collective-permute-start.21 = (bf16[256,1024]{1,0:T(8,128)(2,1)}, bf16[256,1024]{1,0:T(8,128)(2,1)}, u32[]{:S(2)}, u32[]{:S(2)}) collective-permute-start(bf16[256,1024]{1,0:T(8,128)(2,1)} %get-tuple-element.272), channel_id=1, source_target_pairs={{0,8},{8,16},{16,24},{24,28},{28,20},{20,12},{12,4},{4,0},{1,9},{9... | collective-permute-start | bytes 1572872 | tf_op jit(solution)/shard_map/ppermute | solution.py:650
  167.6 14.2 %collective-permute-start.22 = (bf16[256,1024]{1,0:T(8,128)(2,1)}, bf16[256,1024]{1,0:T(8,128)(2,1)}, u32[]{:S(2)}, u32[]{:S(2)}) collective-permute-start(bf16[256,1024]{1,0:T(8,128)(2,1)} %get-tuple-element.273), channel_id=1, source_target_pairs={{0,4},{8,0},{16,8},{24,16},{28,24},{20,28},{12,20},{4,12},{1,5},{9... | collective-permute-start | bytes 1572872 | tf_op jit(solution)/shard_map/ppermute | solution.py:650
  181.8 24.8 %all-to-all-start.4 = ((bf16[8,192,256]{2,1,0:T(8,128)(2,1)}), bf16[8,192,256]{2,1,0:T(8,128)(2,1)S(1)}, u32[]{:S(2)}, u32[]{:S(2)}) async-start(bf16[8,192,256]{2,1,0:T(8,128)(2,1)} %attention_backward.3.grads_ref), calls=%async_computation.4 | async-start | bytes 1572864 | tf_op jit(solution)/shard_map/all_to_all | solution.py:446
  195.5 1.4 collective-permute-start.25
  201.5 15.2 %collective-permute-start.28 = (bf16[400,1024]{1,0:T(8,128)(2,1)}, bf16[400,1024]{1,0:T(8,128)(2,1)}, u32[]{:S(2)}, u32[]{:S(2)}) collective-permute-start(bf16[400,1024]{1,0:T(8,128)(2,1)} %ring_finish.1.refs_0_), channel_id=1, source_target_pairs={{0,2},{2,0},{1,3},{3,1},{4,6},{6,4},{5,7},{7,5},{8,10},{10,8},{9,1... | collective-permute-start | bytes 2457608 | tf_op jit(solution)/shard_map/ppermute | solution.py:442
  201.7 21.3 %collective-permute-start.26 = (bf16[400,1024]{1,0:T(8,128)(2,1)}, bf16[400,1024]{1,0:T(8,128)(2,1)}, u32[]{:S(2)}, u32[]{:S(2)}) collective-permute-start(bf16[400,1024]{1,0:T(8,128)(2,1)} %ring_finish.1.refs_0_), channel_id=1, source_target_pairs={{0,8},{8,16},{16,24},{24,28},{28,20},{20,12},{12,4},{4,0},{1,9},{9... | collective-permute-start | bytes 2457608 | tf_op jit(solution)/shard_map/ppermute | solution.py:577
  203.8 20.6 %collective-permute-start.27 = (bf16[400,1024]{1,0:T(8,128)(2,1)}, bf16[400,1024]{1,0:T(8,128)(2,1)}, u32[]{:S(2)}, u32[]{:S(2)}) collective-permute-start(bf16[400,1024]{1,0:T(8,128)(2,1)} %ring_finish.1.refs_0_), channel_id=1, source_target_pairs={{0,4},{8,0},{16,8},{24,16},{28,24},{20,28},{12,20},{4,12},{1,5},{9... | collective-permute-start | bytes 2457608 | tf_op jit(solution)/shard_map/ppermute | solution.py:577
  210.1 3.8 %collective-permute-start.29 = (f32[24,128]{1,0:T(8,128)S(1)}, f32[24,128]{1,0:T(8,128)S(1)}, u32[]{:S(2)}, u32[]{:S(2)}) collective-permute-start(f32[24,128]{1,0:T(8,128)S(1)} %reshape.126), channel_id=1, source_target_pairs={{0,1},{1,0},{2,3},{3,2},{4,5},{5,4},{6,7},{7,6},{8,9},{9,8},{10,11... | collective-permute-start | bytes 36872 | tf_op jit(solution)/shard_map/ppermute | solution.py:473
  213.9 1.2 collective-permute-start.30
  215.1 7.9 %collective-permute-start.31 = (f32[24,128]{1,0:T(8,128)S(1)}, f32[24,128]{1,0:T(8,128)S(1)}, u32[]{:S(2)}, u32[]{:S(2)}) collective-permute-start(f32[24,128]{1,0:T(8,128)S(1)} %add.108), channel_id=1, source_target_pairs={{0,4},{4,0},{8,12},{12,8},{16,20},{20,16},{24,28},{28,24},{1,5},{5... | collective-permute-start | bytes 36872 | tf_op jit(solution)/shard_map/ppermute | solution.py:1038
  224.3 4.1 %collective-permute-start.34 = (bf16[400,1024]{1,0:T(8,128)(2,1)}, bf16[400,1024]{1,0:T(8,128)(2,1)S(1)}, u32[]{:S(2)}, u32[]{:S(2)}) collective-permute-start(bf16[400,1024]{1,0:T(8,128)(2,1)} %collective-permute-done.26.refs_7_), channel_id=1, source_target_pairs={{0,2},{2,0},{1,3},{3,1},{4,6},{6,4},{5,7},{7,5},{8,10},{10,8},{9,1... | collective-permute-start | bytes 2457608 | tf_op jit(solution)/shard_map/ppermute | solution.py:442
  224.3 5.6 %collective-permute-start.35 = (bf16[400,1024]{1,0:T(8,128)(2,1)}, bf16[400,1024]{1,0:T(8,128)(2,1)S(1)}, u32[]{:S(2)}, u32[]{:S(2)}) collective-permute-start(bf16[400,1024]{1,0:T(8,128)(2,1)} %collective-permute-done.27.refs_9_), channel_id=1, source_target_pairs={{0,2},{2,0},{1,3},{3,1},{4,6},{6,4},{5,7},{7,5},{8,10},{10,8},{9,1... | collective-permute-start | bytes 2457608 | tf_op jit(solution)/shard_map/ppermute | solution.py:442
  224.8 21.8 %collective-permute-start.32 = (bf16[400,1024]{1,0:T(8,128)(2,1)}, bf16[400,1024]{1,0:T(8,128)(2,1)}, u32[]{:S(2)}, u32[]{:S(2)}) collective-permute-start(bf16[400,1024]{1,0:T(8,128)(2,1)} %collective-permute-done.26.refs_7_), channel_id=1, source_target_pairs={{0,8},{8,16},{16,24},{24,28},{28,20},{20,12},{12,4},{4,0},{1,9},{9... | collective-permute-start | bytes 2457608 | tf_op jit(solution)/shard_map/ppermute | solution.py:577
  226.3 20.4 %collective-permute-start.33 = (bf16[400,1024]{1,0:T(8,128)(2,1)}, bf16[400,1024]{1,0:T(8,128)(2,1)}, u32[]{:S(2)}, u32[]{:S(2)}) collective-permute-start(bf16[400,1024]{1,0:T(8,128)(2,1)} %collective-permute-done.27.refs_9_), channel_id=1, source_target_pairs={{0,4},{8,0},{16,8},{24,16},{28,24},{20,28},{12,20},{4,12},{1,5},{9... | collective-permute-start | bytes 2457608 | tf_op jit(solution)/shard_map/ppermute | solution.py:577
  226.8 13.6 %collective-permute-start.37 = (bf16[256,1024]{1,0:T(8,128)(2,1)}, bf16[256,1024]{1,0:T(8,128)(2,1)}, u32[]{:S(2)}, u32[]{:S(2)}) collective-permute-start(bf16[256,1024]{1,0:T(8,128)(2,1)} %get-tuple-element.341), channel_id=1, source_target_pairs={{0,1},{1,0},{2,3},{3,2},{4,5},{5,4},{6,7},{7,6},{8,9},{9,8},{10,11... | collective-permute-start | bytes 1572872 | tf_op jit(solution)/shard_map/ppermute | solution.py:473
  228.4 24.9 %copy-start.10 = (f32[256,1024]{1,0:T(8,128)S(1)}, f32[256,1024]{1,0:T(8,128)}, u32[]{:S(2)}) copy-start(f32[256,1024]{1,0:T(8,128)} %get-tuple-element.235.hidden_ref) | copy-start | bytes 3145732
  228.4 24.9 %copy-start.42 = (f32[1024]{0:T(1024)S(1)}, f32[1024]{0:T(1024)}, u32[]{:S(2)}) copy-start(f32[1024]{0:T(1024)} %param.35) | copy-start | bytes 12292
  228.4 18.2 %collective-permute-start.36 = (f32[24,128]{1,0:T(8,128)S(1)}, f32[24,128]{1,0:T(8,128)S(1)}, u32[]{:S(2)}, u32[]{:S(2)}) collective-permute-start(f32[24,128]{1,0:T(8,128)S(1)} %add.109), channel_id=1, source_target_pairs={{0,8},{4,12},{8,0},{12,4},{16,24},{20,28},{24,16},{28,20},{1,9},{5... | collective-permute-start | bytes 36872 | tf_op jit(solution)/shard_map/ppermute | solution.py:1038
  246.6 4.1 %collective-permute-start.40 = (bf16[400,1024]{1,0:T(8,128)(2,1)}, bf16[400,1024]{1,0:T(8,128)(2,1)}, u32[]{:S(2)}, u32[]{:S(2)}) collective-permute-start(bf16[400,1024]{1,0:T(8,128)(2,1)} %collective-permute-done.32.refs_7_), channel_id=1, source_target_pairs={{0,2},{2,0},{1,3},{3,1},{4,6},{6,4},{5,7},{7,5},{8,10},{10,8},{9,1... | collective-permute-start | bytes 2457608 | tf_op jit(solution)/shard_map/ppermute | solution.py:442
  246.6 8.9 %collective-permute-start.41 = (bf16[400,1024]{1,0:T(8,128)(2,1)}, bf16[400,1024]{1,0:T(8,128)(2,1)}, u32[]{:S(2)}, u32[]{:S(2)}) collective-permute-start(bf16[400,1024]{1,0:T(8,128)(2,1)} %collective-permute-done.33.refs_9_), channel_id=1, source_target_pairs={{0,2},{2,0},{1,3},{3,1},{4,6},{6,4},{5,7},{7,5},{8,10},{10,8},{9,1... | collective-permute-start | bytes 2457608 | tf_op jit(solution)/shard_map/ppermute | solution.py:442
  247.1 23.3 %collective-permute-start.38 = (bf16[400,1024]{1,0:T(8,128)(2,1)}, bf16[400,1024]{1,0:T(8,128)(2,1)S(1)}, u32[]{:S(2)}, u32[]{:S(2)}) collective-permute-start(bf16[400,1024]{1,0:T(8,128)(2,1)} %collective-permute-done.32.refs_7_), channel_id=1, source_target_pairs={{0,8},{8,16},{16,24},{24,28},{28,20},{20,12},{12,4},{4,0},{1,9},{9... | collective-permute-start | bytes 2457608 | tf_op jit(solution)/shard_map/ppermute | solution.py:577
  248.4 22.0 %collective-permute-start.39 = (bf16[400,1024]{1,0:T(8,128)(2,1)}, bf16[400,1024]{1,0:T(8,128)(2,1)S(1)}, u32[]{:S(2)}, u32[]{:S(2)}) collective-permute-start(bf16[400,1024]{1,0:T(8,128)(2,1)} %collective-permute-done.33.refs_9_), channel_id=1, source_target_pairs={{0,4},{8,0},{16,8},{24,16},{28,24},{20,28},{12,20},{4,12},{1,5},{9... | collective-permute-start | bytes 2457608 | tf_op jit(solution)/shard_map/ppermute | solution.py:577
  249.2 13.7 %collective-permute-start.42 = (bf16[256,1024]{1,0:T(8,128)(2,1)}, bf16[256,1024]{1,0:T(8,128)(2,1)}, u32[]{:S(2)}, u32[]{:S(2)}) collective-permute-start(bf16[256,1024]{1,0:T(8,128)(2,1)} %get-tuple-element.372), channel_id=1, source_target_pairs={{0,1},{1,0},{2,3},{3,2},{4,5},{5,4},{6,7},{7,6},{8,9},{9,8},{10,11... | collective-permute-start | bytes 1572872 | tf_op jit(solution)/shard_map/ppermute | solution.py:473
  250.7 19.7 %collective-permute-start.43 = (f32[24,128]{1,0:T(8,128)S(1)}, f32[24,128]{1,0:T(8,128)S(1)}, u32[]{:S(2)}, u32[]{:S(2)}) collective-permute-start(f32[24,128]{1,0:T(8,128)S(1)} %add.114), channel_id=1, source_target_pairs={{0,16},{4,20},{8,24},{12,28},{16,0},{20,4},{24,8},{28,12},{1,17},{... | collective-permute-start | bytes 36872 | tf_op jit(solution)/shard_map/ppermute | solution.py:1038
  255.5 20.1 %copy-start.17 = (bf16[256,1024]{1,0:T(8,128)(2,1)S(1)}, bf16[256,1024]{1,0:T(8,128)(2,1)}, u32[]{:S(2)}) copy-start(bf16[256,1024]{1,0:T(8,128)(2,1)} %get-tuple-element.372) | copy-start | bytes 1572868
  255.5 20.1 %copy-start.40 = (f32[1024]{0:T(1024)S(1)}, f32[1024]{0:T(1024)}, u32[]{:S(2)}) copy-start(f32[1024]{0:T(1024)} %param.22) | copy-start | bytes 12292
  270.4 9.1 %collective-permute-start.46 = (bf16[400,1024]{1,0:T(8,128)(2,1)S(1)}, bf16[400,1024]{1,0:T(8,128)(2,1)}, u32[]{:S(2)}, u32[]{:S(2)}) collective-permute-start(bf16[400,1024]{1,0:T(8,128)(2,1)S(1)} %collective-permute-done.38.left.refs_7_), channel_id=1, source_target_pairs={{0,2},{2,0},{1,3},{3,1},{4,6},{6,4},{5,7},{7,5},{8,10},{10,8},{9,1... | collective-permute-start | bytes 2457608 | tf_op jit(solution)/shard_map/ppermute | solution.py:442
  270.5 9.0 %collective-permute-start.47 = (bf16[400,1024]{1,0:T(8,128)(2,1)S(1)}, bf16[400,1024]{1,0:T(8,128)(2,1)}, u32[]{:S(2)}, u32[]{:S(2)}) collective-permute-start(bf16[400,1024]{1,0:T(8,128)(2,1)S(1)} %collective-permute-done.39.right.refs_9_), channel_id=1, source_target_pairs={{0,2},{2,0},{1,3},{3,1},{4,6},{6,4},{5,7},{7,5},{8,10},{10,8},{9,1... | collective-permute-start | bytes 2457608 | tf_op jit(solution)/shard_map/ppermute | solution.py:442
  273.6 12.8 %collective-permute-start.44 = (bf16[400,512]{1,0:T(8,128)(2,1)}, bf16[400,512]{1,0:T(8,128)(2,1)S(1)}, u32[]{:S(2)}, u32[]{:S(2)}) collective-permute-start(bf16[400,512]{1,0:T(8,128)(2,1)} %get-tuple-element.355), channel_id=1, source_target_pairs={{0,8},{8,16},{16,24},{24,28},{28,20},{20,12},{12,4},{4,0},{1,9},{9... | collective-permute-start | bytes 1228808 | tf_op jit(solution)/shard_map/ppermute | solution.py:577
  273.8 12.6 %collective-permute-start.45 = (bf16[400,512]{1,0:T(8,128)(2,1)}, bf16[400,512]{1,0:T(8,128)(2,1)}, u32[]{:S(2)}, u32[]{:S(2)}) collective-permute-start(bf16[400,512]{1,0:T(8,128)(2,1)} %get-tuple-element.356), channel_id=1, source_target_pairs={{0,4},{8,0},{16,8},{24,16},{28,24},{20,28},{12,20},{4,12},{1,5},{9... | collective-permute-start | bytes 1228808 | tf_op jit(solution)/shard_map/ppermute | solution.py:577
  286.4 1.8 collective-permute-start.48
  286.5 2.5 collective-permute-start.49
  (33 other events, 140.9 us)

commit v22 on v19

--- a/solution.py
+++ b/solution.py
@@ -1028,7 +1028,7 @@
     ends = ends.reshape(-1, 128)
     ends = functools.reduce(jnp.add, across_heads(ends))
     ends = ends + swap_cores(ends)
-    moves = [chips >> (at + 1) for at in range(chips.bit_length() - 1)][::-1]
+    moves = [chips >> (at + 1) for at in range(chips.bit_length() - 1)]
 
     def step_ends(ends):
         if not moves:

time: 299 us -> 299 us (level)
  transfers between devices with their start and end apart: 54 -> 54, of which waited for: 25 -> 24; matrix products, arithmetic and copies ran while one was open for 6% -> 6% of each run, Pallas kernels for 36% -> 36%
where the time goes in v22:
time: 299 us; the launch traced here: 297 us
  Pallas kernels  124 us (41%)
  starting transfers between devices  58.5 us (20%)
  waiting for transfers between devices  52.9 us (18%)
  blocking collectives  29.6 us (10%)
  local copies, waits for them, and re-layouts  15.4 us (5%)
  other arithmetic  9.77 us (3%)
  matrix products  5.35 us (2%)
    pallas_call x5, Pallas kernels, place(): pl.pallas_call(functools.partial(place_kernel, heads, len(blocks[0]) // 2...  30.2 us
    all_to_all x1, blocking collectives, to_heads(): return lax.all_to_all(blocks, 'chip', 0, 0, tiled=True)  29.6 us
    pallas_call x2, Pallas kernels, attention_backward(): pl.pallas_call(functools.partial(backward_kernel, crops, len(extras)), gr...  24.9 us
    ppermute x24, starting transfers between devices, send(): lax.ppermute(block, 'chip', ring_pairs(direction))  24.5 us
    all_to_all x4, starting transfers between devices, to_heads(): return lax.all_to_all(blocks, 'chip', 0, 0, tiled=True)  17.3 us
    pallas_call x4, Pallas kernels, add(): pl.pallas_call(functools.partial(add_kernel, places, len(shapes)), grid_s...  15.6 us
    pallas_call x1, Pallas kernels, attention_forward(): pl.pallas_call(functools.partial(forward_kernel, crops, key_step(count)),...  15.3 us
    ppermute x24, waiting for transfers between devices, send(): lax.ppermute(block, 'chip', ring_pairs(direction))  14.9 us
  transfers between devices with their start and end apart: 54, of which 24 were waited for; matrix products, arithmetic and copies ran while one was open for 6% of the time, Pallas kernels for 36%

profile of v22, /device:TPU:0, one launch (start us, length us, event | category | flops | bytes accessed | tf_op | source)
XLA Modules:
  0.0 297.0 jit_solution(5260850960383278212)
XLA Ops:
  1.2 6.6 %project.1 = (bf16[8,208,256]{2,1,0:T(8,128)(2,1)}, bf16[256,1024]{1,0:T(8,128)(2,1)}, bf16[256,512]{1,0:T(8,128)(2,1)}) custom-call(s32[18]{0:T(128)} %compare_select_fusion.5.table.core_ref._, bf16[256,1024]{1,0:T(8,128)(2,1)} %input_ref.3, s32[1,256]{1,0:T(1,128)} %bitcast.79, s32[32]{0:T(128)} %steps_ref.1, f32[1,1024]{1,0:T(1,128)} %bitcast.61, ...), custom_call_target="tpu_custom_call" | custom-call | flops 1 | bytes 1 | tf_op jit(solution)/shard_map/project/pallas_call | solution.py:94
  7.8 29.6 %all_to_all.25.query_ref.own.piece = bf16[8,208,256]{2,1,0:T(8,128)(2,1)S(1)} all-to-all(bf16[8,208,256]{2,1,0:T(8,128)(2,1)} %get-tuple-element.207), channel_id=1, replica_groups=mesh['chip'=8,'core'=2,'head'=2] {'chip'}, dimensions={0} | all-to-all | bytes 1703936 | tf_op jit(solution)/shard_map/all_to_all | solution.py:446
  38.2 1.3 collective-permute-start.1
  40.7 15.3 %attention_forward.1 = (f32[8,64,256]{2,1,0:T(8,128)}, bf16[8,64,256]{2,1,0:T(8,128)(2,1)}, f32[8,1,256]{2,1,0:T(1,128)}) custom-call(bf16[8,208,256]{2,1,0:T(8,128)(2,1)} %copy-done, bf16[8,208,256]{2,1,0:T(8,128)(2,1)} %copy-done, bf16[8,208,256]{2,1,0:T(8,128)(2,1)} %copy-done.2), custom_call_target="tpu_custom_call" | custom-call | flops 1 | bytes 1 | tf_op jit(solution)/shard_map/attention_forward/pallas_call | solution.py:378
  56.1 3.4 %all-to-all-start.1 = ((bf16[8,64,256]{2,1,0:T(8,128)(2,1)}), bf16[8,64,256]{2,1,0:T(8,128)(2,1)S(1)}, u32[]{:S(2)}, u32[]{:S(2)}) async-start(bf16[8,64,256]{2,1,0:T(8,128)(2,1)} %get-tuple-element.214), calls=%async_computation.1 | async-start | bytes 524288 | tf_op jit(solution)/shard_map/all_to_all | solution.py:446
  59.7 9.3 %all-to-all-done.1 = bf16[8,64,256]{2,1,0:T(8,128)(2,1)S(1)} async-done(((bf16[8,64,256]{2,1,0:T(8,128)(2,1)}), bf16[8,64,256]{2,1,0:T(8,128)(2,1)S(1)}, u32[]{:S(2)}, u32[]{:S(2)}) %all-to-all-start.1) | async-done | bytes 262176 | tf_op jit(solution)/shard_map/all_to_all | solution.py:446
  69.4 1.6 collective-permute-start.7
  73.3 4.4 %collective-permute-done.3.refs_3_ = bf16[256,512]{1,0:T(8,128)(2,1)S(1)} collective-permute-done((bf16[256,512]{1,0:T(8,128)(2,1)S(1)}, bf16[256,512]{1,0:T(8,128)(2,1)S(1)}, u32[]{:S(2)}, u32[]{:S(2)}) %collective-permute-start.3) | collective-permute-done | bytes 262176 | tf_op jit(solution)/shard_map/ppermute | solution.py:577
  78.6 1.4 collective-permute-start.5
  80.6 1.4 collective-permute-done.7.refs_1_
  82.8 11.7 %mlp.1 = (bf16[256,2048]{1,0:T(8,128)(2,1)}, bf16[256,2048]{1,0:T(8,128)(2,1)}, bf16[256,1024]{1,0:T(8,128)(2,1)}, bf16[256,1024]{1,0:T(8,128)(2,1)}, f32[256,10...) custom-call(s32[18]{0:T(128)} %compare_select_fusion.5.table.core_ref._, ...), custom_call_target="tpu_custom_call" | custom-call | flops 1 | bytes 1 | tf_op jit(solution)/shard_map/mlp/pallas_call | solution.py:174
  95.2 1.5 collective-permute-start.14
  96.7 1.6 collective-permute-done.8.refs_1_.far_in
  100.0 3.3 %ring_add.4 = (bf16[256,512]{1,0:T(8,128)(2,1)}, bf16[256,512]{1,0:T(8,128)(2,1)}) custom-call(s32[18]{0:T(128)} %compare_select_fusion.5.table.core_ref._, bf16[256,1024]{1,0:T(8,128)(2,1)} %get-tuple-element.225.refs_0_.keep_in, bf16[256,1024]{1,0:T(8,128)(2,1)} %copy-done.9, bf16[256,2048]{1,0:T(8,128)(2,1)} %get-tuple-element.227.refs_2_.refs_5_.near, ...), custom_call_target="tpu_custom_call" | custom-call | flops 1 | bytes 1 | tf_op jit(solution)/shard_map/ring_add/pallas_call | solution.py:732
  103.6 1.8 collective-permute-start.11
  105.3 1.7 halves.2
  107.5 1.6 collective-permute-start.13
  110.1 4.3 %middle.1 = (f32[256,1024]{1,0:T(8,128)}, bf16[256,1024]{1,0:T(8,128)(2,1)}, bf16[512,256]{1,0:T(8,128)(2,1)}, f32[4,1024]{1,0:T(4,128)}) custom-call(f32[256,1024]{1,0:T(8,128)} %get-tuple-element.235.hidden_ref, bf16[256,1024]{1,0:T(8,128)(2,1)} %grad_ref.3, bf16[256,1024]{1,0:T(8,128)(2,1)} %get-tuple-element.238.refs_0_, bf16[256,1024]{1,0:T(8,128)(2,1)} %copy-done.28, ...), custom_call_target="tpu_custom_call" | custom-call | flops 1 | bytes 1 | tf_op jit(solution)/shard_map/middle/pallas_call | solution.py:235
  116.0 4.4 %ring_add.5 = (bf16[256,1024]{1,0:T(8,128)(2,1)}, bf16[256,1024]{1,0:T(8,128)(2,1)}) custom-call(s32[18]{0:T(128)} %compare_select_fusion.5.table.core_ref._, bf16[256,1024]{1,0:T(8,128)(2,1)} %get-tuple-element.225.refs_0_.keep_in, bf16[256,1024]{1,0:T(8,128)(2,1)} %copy-done.9, bf16[256,2048]{1,0:T(8,128)(2,1)} %get-tuple-element.227.refs_2_.refs_5_.near, ...), custom_call_target="tpu_custom_call" | custom-call | flops 1 | bytes 1 | tf_op jit(solution)/shard_map/ring_add/pallas_call | solution.py:732
  121.6 1.7 collective-permute-start.15
  123.7 4.6 %all-to-all-start.2 = ((bf16[8,64,256]{2,1,0:T(8,128)(2,1)}), bf16[8,64,256]{2,1,0:T(8,128)(2,1)S(1)}, u32[]{:S(2)}, u32[]{:S(2)}) async-start(bf16[8,64,256]{2,1,0:T(8,128)(2,1)} %bitcast.12), calls=%async_computation.2 | async-start | bytes 524288 | tf_op jit(solution)/shard_map/all_to_all | solution.py:446
  128.3 1.3 fusion.14
  129.6 3.0 join.1.refs_0_
  132.6 1.5 collective-permute-start.24
  136.4 1.6 collective-permute-done.16.refs_7_
  138.8 4.1 %ring_add.6 = (bf16[256,1024]{1,0:T(8,128)(2,1)}, bf16[256,1024]{1,0:T(8,128)(2,1)}) custom-call(s32[18]{0:T(128)} %compare_select_fusion.5.table.core_ref._, bf16[256,1024]{1,0:T(8,128)(2,1)} %get-tuple-element.225.refs_0_.keep_in, bf16[256,1024]{1,0:T(8,128)(2,1)} %copy-done.9, bf16[256,2048]{1,0:T(8,128)(2,1)} %get-tuple-element.227.refs_2_.refs_5_.near, ...), custom_call_target="tpu_custom_call" | custom-call | flops 1 | bytes 1 | tf_op jit(solution)/shard_map/ring_add/pallas_call | solution.py:732
  142.9 1.7 collective-permute-start.19
  144.9 4.7 %all-to-all-start.3 = ((bf16[8,32,1024]{2,1,0:T(8,128)(2,1)}), bf16[8,32,1024]{2,1,0:T(8,128)(2,1)}, u32[]{:S(2)}, u32[]{:S(2)}) async-start(bf16[8,32,1024]{2,1,0:T(8,128)(2,1)} %bitcast.11), calls=%async_computation.3 | async-start | bytes 1048576 | tf_op jit(solution)/shard_map/all_to_all | solution.py:446
  149.6 11.9 %attention_backward.2 = (f32[8,64,256]{2,1,0:T(8,128)S(1)}, bf16[8,128,256]{2,1,0:T(8,128)(2,1)S(1)}) custom-call(bf16[8,208,256]{2,1,0:T(8,128)(2,1)S(1)} %copy-done.1, bf16[8,64,256]{2,1,0:T(8,128)(2,1)S(1)} %all-to-all-done.2.grad_ref, f32[8,64,256]{2,1,0:T(8,128)S(1)} %copy-done.4, f32[8,1,256]{2,1,0:T(1,128)S(1)} %copy-done.5, ...), custom_call_target="tpu_custom_call" | custom-call | flops 1 | bytes 1 | tf_op jit(solution)/shard_map/attention_backward/pallas_call | solution.py:416
  161.6 3.8 %ring_add.7 = (bf16[256,1024]{1,0:T(8,128)(2,1)}, bf16[256,1024]{1,0:T(8,128)(2,1)}) custom-call(s32[18]{0:T(128)} %compare_select_fusion.5.table.core_ref._, bf16[256,1024]{1,0:T(8,128)(2,1)} %get-tuple-element.225.refs_0_.keep_in, bf16[256,1024]{1,0:T(8,128)(2,1)} %copy-done.9, bf16[256,2048]{1,0:T(8,128)(2,1)} %get-tuple-element.227.refs_2_.refs_5_.near, ...), custom_call_target="tpu_custom_call" | custom-call | flops 1 | bytes 1 | tf_op jit(solution)/shard_map/ring_add/pallas_call | solution.py:732
  165.4 2.1 collective-permute-start.21
  167.6 12.9 %attention_backward.3.grads_ref = bf16[8,192,256]{2,1,0:T(8,128)(2,1)} custom-call(bf16[8,208,256]{2,1,0:T(8,128)(2,1)S(1)} %copy-done.1, bf16[8,64,256]{2,1,0:T(8,128)(2,1)S(1)} %all-to-all-done.2.grad_ref, f32[8,64,256]{2,1,0:T(8,128)S(1)} %copy-done.4, f32[8,1,256]{2,1,0:T(1,128)S(1)} %copy-done.5, bf16[8,208,256]{2,1,0:T(8,128)(2,1)S(1)} %copy-done.1, ...), custom_call_target="tpu_custom_call" | custom-call | flops 1 | bytes 1 | tf_op jit(solution)/shard_map/attention_backward/pallas_call | solution.py:416
  180.5 1.3 collective-permute-done.22.behind
  181.8 4.6 %all-to-all-start.4 = ((bf16[8,192,256]{2,1,0:T(8,128)(2,1)}), bf16[8,192,256]{2,1,0:T(8,128)(2,1)S(1)}, u32[]{:S(2)}, u32[]{:S(2)}) async-start(bf16[8,192,256]{2,1,0:T(8,128)(2,1)} %attention_backward.3.grads_ref), calls=%async_computation.4 | async-start | bytes 1572864 | tf_op jit(solution)/shard_map/all_to_all | solution.py:446
  188.6 5.2 %head_gradient.1 = bf16[192,1024]{1,0:T(8,128)(2,1)} custom-call(s32[18]{0:T(128)} %compare_select_fusion.5.table.core_ref._, bf16[8,192,256]{2,1,0:T(8,128)(2,1)} %attention_backward.3.grads_ref, bf16[2048,512]{1,0:T(8,128)(2,1)} %join.1.refs_0_, bf16[2048,512]{1,0:T(8,128)(2,1)} %collective-permute-done.24.refs_1_), custom_call_target="tpu_custom_call" | custom-call | flops 1 | bytes 1 | tf_op jit(solution)/shard_map/head_gradient/pallas_call | solution.py:865
  193.7 1.7 constant_dynamic-slice_fusion
  197.6 3.9 %ring_finish.1.refs_0_ = bf16[400,1024]{1,0:T(8,128)(2,1)} custom-call(s32[18]{0:T(128)} %compare_select_fusion.5.table.core_ref._, bf16[256,1024]{1,0:T(8,128)(2,1)} %get-tuple-element.225.refs_0_.keep_in, bf16[256,1024]{1,0:T(8,128)(2,1)} %copy-done.9, bf16[256,2048]{1,0:T(8,128)(2,1)} %get-tuple-element.227.refs_2_.refs_5_.near, ...), custom_call_target="tpu_custom_call" | custom-call | flops 1 | bytes 1 | tf_op jit(solution)/shard_map/ring_finish/pallas_call | solution.py:688
  201.7 2.0 collective-permute-start.26
  203.8 2.9 all-to-all-done.4
  208.6 1.5 fusion.7
  210.1 1.6 collective-permute-start.29
  211.7 2.2 collective-permute-done.29
  215.1 4.5 %place.5 = (f32[2048,1024]{1,0:T(8,128)}, f32[1024,2048]{1,0:T(8,128)}, f32[2,8,32,1024]{3,2,1,0:T(8,128)}, f32[8,2,16,1024]{3,2,1,0:T(8,128)}, f32[1024,512]{1,...) custom-call(s32[18]{0:T(128)} %compare_select_fusion.5.table.core_ref._, bf16[400,1024]{1,0:T(8,128)(2,1)} %ring_finish.1.refs_0_, ...), custom_call_target="tpu_custom_call" | custom-call | flops 1 | bytes 1 | tf_op jit(solution)/shard_map/place/pallas_call | solution.py:778
  219.6 3.3 %collective-permute-done.26.refs_7_ = bf16[400,1024]{1,0:T(8,128)(2,1)} collective-permute-done((bf16[400,1024]{1,0:T(8,128)(2,1)}, bf16[400,1024]{1,0:T(8,128)(2,1)}, u32[]{:S(2)}, u32[]{:S(2)}) %collective-permute-start.26) | collective-permute-done | bytes 819232 | tf_op jit(solution)/shard_map/ppermute | solution.py:577
  222.8 1.5 collective-permute-done.27.refs_9_
  224.8 1.5 collective-permute-start.31
  226.9 1.5 collective-permute-start.36
  228.4 2.3 collective-permute-start.35
  231.6 6.9 %place.6 = (f32[2048,1024]{1,0:T(8,128)}, f32[1024,2048]{1,0:T(8,128)}, f32[2,8,32,1024]{3,2,1,0:T(8,128)}, f32[8,2,16,1024]{3,2,1,0:T(8,128)}, f32[1024,512]{1,...) custom-call(s32[18]{0:T(128)} %compare_select_fusion.5.table.core_re, ...), custom_call_target="tpu_custom_call", output_to_operand_aliasing={{0}: (1, {}), {1}: (2, {}), {2}: (3, {}), {3}: (4, {}), {4}... | custom-call | flops 1 | bytes 1 | tf_op jit(solution)/shard_map/place/pallas_call | solution.py:778
  238.5 2.0 collective-permute-done.36
  240.5 7.2 %collective-permute-done.35 = f32[24,128]{1,0:T(8,128)S(1)} collective-permute-done((f32[24,128]{1,0:T(8,128)S(1)}, f32[24,128]{1,0:T(8,128)S(1)}, u32[]{:S(2)}, u32[]{:S(2)}) %collective-permute-start.35) | collective-permute-done | bytes 12320 | tf_op jit(solution)/shard_map/ppermute | solution.py:1038
  248.2 1.3 collective-permute-start.37
  250.3 1.5 collective-permute-start.41
  251.8 1.3 collective-permute-start.42
  253.1 2.2 add_convert_fusion
  255.4 7.0 %place.7 = (f32[2048,1024]{1,0:T(8,128)}, f32[1024,2048]{1,0:T(8,128)}, f32[2,8,32,1024]{3,2,1,0:T(8,128)}, f32[8,2,16,1024]{3,2,1,0:T(8,128)}, f32[1024,512]{1,...) custom-call(s32[18]{0:T(128)} %compare_select_fusion.5.table.core_re, ...), custom_call_target="tpu_custom_call", output_to_operand_aliasing={{0}: (1, {}), {1}: (2, {}), {2}: (3, {}), {3}: (4, {}), {4}... | custom-call | flops 1 | bytes 1 | tf_op jit(solution)/shard_map/place/pallas_call | solution.py:778
  262.4 1.5 collective-permute-done.41
  263.9 6.1 %collective-permute-done.42 = f32[24,128]{1,0:T(8,128)S(1)} collective-permute-done((f32[24,128]{1,0:T(8,128)S(1)}, f32[24,128]{1,0:T(8,128)S(1)}, u32[]{:S(2)}, u32[]{:S(2)}) %collective-permute-start.42) | collective-permute-done | bytes 12320 | tf_op jit(solution)/shard_map/ppermute | solution.py:1038
  271.2 2.1 halves.3
  275.4 1.5 fusion.13
  276.9 2.3 fusion.12
  279.3 6.9 %place.8 = (f32[2048,1024]{1,0:T(8,128)}, f32[1024,2048]{1,0:T(8,128)}, f32[2,8,32,1024]{3,2,1,0:T(8,128)}, f32[8,2,16,1024]{3,2,1,0:T(8,128)}, f32[1024,512]{1,...) custom-call(s32[18]{0:T(128)} %compare_select_fusion.5.table.core_re, ...), custom_call_target="tpu_custom_call", output_to_operand_aliasing={{0}: (1, {}), {1}: (2, {}), {2}: (3, {}), {3}: (4, {}), {4}... | custom-call | flops 1 | bytes 1 | tf_op jit(solution)/shard_map/place/pallas_call | solution.py:778
  289.6 5.0 %place.9 = (f32[2048,1024]{1,0:T(8,128)}, f32[1024,2048]{1,0:T(8,128)}, f32[2,8,32,1024]{3,2,1,0:T(8,128)}, f32[8,2,16,1024]{3,2,1,0:T(8,128)}, f32[1024,512]{1,...) custom-call(s32[18]{0:T(128)} %compare_select_fusion.5.table.core_re, ...), custom_call_target="tpu_custom_call", output_to_operand_aliasing={{0}: (1, {}), {1}: (2, {}), {2}: (3, {}), {3}: (4, {}), {4}... | custom-call | flops 1 | bytes 1 | tf_op jit(solution)/shard_map/place/pallas_call | solution.py:778
  294.5 1.3 reduce_sum.89
  (187 shorter events, 37.2 us)
Async XLA Ops:
  7.8 51.7 %copy-start.7 = (bf16[256,1024]{1,0:T(8,128)(2,1)S(1)}, bf16[256,1024]{1,0:T(8,128)(2,1)}, u32[]{:S(2)}) copy-start(bf16[256,1024]{1,0:T(8,128)(2,1)} %input_ref.3) | copy-start | bytes 1572868
  37.4 31.5 %copy-start.11 = (bf16[512,1024]{1,0:T(8,128)(2,1)S(1)}, bf16[512,1024]{1,0:T(8,128)(2,1)}, u32[]{:S(2)}) copy-start(bf16[512,1024]{1,0:T(8,128)(2,1)} %refs_3_.1) | copy-start | bytes 3145732
  37.5 2.4 collective-permute-start.2
  37.5 18.6 %collective-permute-start = (bf16[256,512]{1,0:T(8,128)(2,1)}, bf16[256,512]{1,0:T(8,128)(2,1)S(1)}, u32[]{:S(2)}, u32[]{:S(2)}) collective-permute-start(bf16[256,512]{1,0:T(8,128)(2,1)} %get-tuple-element.209.refs_0_), channel_id=1, source_target_pairs={{0,8},{8,16},{16,24},{24,28},{28,20},{20,12},{12,4},{4,0},{1,9},{9... | collective-permute-start | bytes 786440 | tf_op jit(solution)/shard_map/ppermute | solution.py:577
  38.2 17.8 %collective-permute-start.1 = (bf16[256,512]{1,0:T(8,128)(2,1)}, bf16[256,512]{1,0:T(8,128)(2,1)}, u32[]{:S(2)}, u32[]{:S(2)}) collective-permute-start(bf16[256,512]{1,0:T(8,128)(2,1)} %get-tuple-element.209.refs_0_), channel_id=1, source_target_pairs={{0,4},{8,0},{16,8},{24,16},{28,24},{20,28},{12,20},{4,12},{1,5},{9... | collective-permute-start | bytes 786440 | tf_op jit(solution)/shard_map/ppermute | solution.py:577
  56.0 38.5 %copy-start.32 = (bf16[256,512]{1,0:T(8,128)(2,1)}, bf16[256,512]{1,0:T(8,128)(2,1)S(1)}, u32[]{:S(2)}) copy-start(bf16[256,512]{1,0:T(8,128)(2,1)S(1)} %collective-permute-done.refs_1_) | copy-start | bytes 786436
  56.1 12.9 %all-to-all-start.1 = ((bf16[8,64,256]{2,1,0:T(8,128)(2,1)}), bf16[8,64,256]{2,1,0:T(8,128)(2,1)S(1)}, u32[]{:S(2)}, u32[]{:S(2)}) async-start(bf16[8,64,256]{2,1,0:T(8,128)(2,1)} %get-tuple-element.214), calls=%async_computation.1 | async-start | bytes 524288 | tf_op jit(solution)/shard_map/all_to_all | solution.py:446
  69.4 12.6 %collective-permute-start.7 = (bf16[256,1024]{1,0:T(8,128)(2,1)S(1)}, bf16[256,1024]{1,0:T(8,128)(2,1)S(1)}, u32[]{:S(2)}, u32[]{:S(2)}) collective-permute-start(bf16[256,1024]{1,0:T(8,128)(2,1)S(1)} %convolution_convert_fusion.refs_0_), channel_id=1, source_target_pairs={{0,1},{1,0},{2,3},{3,2},{4,5},{5,4},{6,7},{7,6},{8,9},{9,8},{10,11... | collective-permute-start | bytes 1572872 | tf_op jit(solution)/shard_map/ppermute | solution.py:473
  71.0 6.7 %collective-permute-start.3 = (bf16[256,512]{1,0:T(8,128)(2,1)S(1)}, bf16[256,512]{1,0:T(8,128)(2,1)S(1)}, u32[]{:S(2)}, u32[]{:S(2)}) collective-permute-start(bf16[256,512]{1,0:T(8,128)(2,1)S(1)} %collective-permute-done.refs_1_), channel_id=1, source_target_pairs={{0,8},{8,16},{16,24},{24,28},{28,20},{20,12},{12,4},{4,0},{1,9},{9... | collective-permute-start | bytes 786440 | tf_op jit(solution)/shard_map/ppermute | solution.py:577
  72.0 6.6 %collective-permute-start.4 = (bf16[256,512]{1,0:T(8,128)(2,1)}, bf16[256,512]{1,0:T(8,128)(2,1)S(1)}, u32[]{:S(2)}, u32[]{:S(2)}) collective-permute-start(bf16[256,512]{1,0:T(8,128)(2,1)} %collective-permute-done.1.refs_2_), channel_id=1, source_target_pairs={{0,4},{8,0},{16,8},{24,16},{28,24},{20,28},{12,20},{4,12},{1,5},{9... | collective-permute-start | bytes 786440 | tf_op jit(solution)/shard_map/ppermute | solution.py:577
  77.7 25.7 %copy-start.33 = (bf16[256,512]{1,0:T(8,128)(2,1)}, bf16[256,512]{1,0:T(8,128)(2,1)S(1)}, u32[]{:S(2)}) copy-start(bf16[256,512]{1,0:T(8,128)(2,1)S(1)} %collective-permute-done.3.refs_3_) | copy-start | bytes 786436
  78.6 16.0 %copy-start.34 = (bf16[256,512]{1,0:T(8,128)(2,1)}, bf16[256,512]{1,0:T(8,128)(2,1)S(1)}, u32[]{:S(2)}) copy-start(bf16[256,512]{1,0:T(8,128)(2,1)S(1)} %collective-permute-done.4.refs_4_) | copy-start | bytes 786436
  78.6 15.9 %collective-permute-start.5 = (bf16[256,512]{1,0:T(8,128)(2,1)S(1)}, bf16[256,512]{1,0:T(8,128)(2,1)S(1)}, u32[]{:S(2)}, u32[]{:S(2)}) collective-permute-start(bf16[256,512]{1,0:T(8,128)(2,1)S(1)} %collective-permute-done.3.refs_3_), channel_id=1, source_target_pairs={{0,8},{8,16},{16,24},{24,28},{28,20},{20,12},{12,4},{4,0},{1,9},{9... | collective-permute-start | bytes 786440 | tf_op jit(solution)/shard_map/ppermute | solution.py:577
  80.1 14.5 %collective-permute-start.6 = (bf16[256,512]{1,0:T(8,128)(2,1)S(1)}, bf16[256,512]{1,0:T(8,128)(2,1)S(1)}, u32[]{:S(2)}, u32[]{:S(2)}) collective-permute-start(bf16[256,512]{1,0:T(8,128)(2,1)S(1)} %collective-permute-done.4.refs_4_), channel_id=1, source_target_pairs={{0,4},{8,0},{16,8},{24,16},{28,24},{20,28},{12,20},{4,12},{1,5},{9... | collective-permute-start | bytes 786440 | tf_op jit(solution)/shard_map/ppermute | solution.py:577
  94.6 3.7 %collective-permute-start.9 = (bf16[256,2048]{1,0:T(8,128)(2,1)}, bf16[256,2048]{1,0:T(8,128)(2,1)S(1)}, u32[]{:S(2)}, u32[]{:S(2)}) collective-permute-start(bf16[256,2048]{1,0:T(8,128)(2,1)} %get-tuple-element.228), channel_id=1, source_target_pairs={{0,2},{2,0},{1,3},{3,1},{4,6},{6,4},{5,7},{7,5},{8,10},{10,8},{9,1... | collective-permute-start | bytes 3145736 | tf_op jit(solution)/shard_map/ppermute | solution.py:442
  94.7 3.6 %collective-permute-start.8 = (bf16[256,1024]{1,0:T(8,128)(2,1)}, bf16[256,1024]{1,0:T(8,128)(2,1)S(1)}, u32[]{:S(2)}, u32[]{:S(2)}) collective-permute-start(bf16[256,1024]{1,0:T(8,128)(2,1)} %get-tuple-element.226), channel_id=1, source_target_pairs={{0,2},{2,0},{1,3},{3,1},{4,6},{6,4},{5,7},{7,5},{8,10},{10,8},{9,1... | collective-permute-start | bytes 1572872 | tf_op jit(solution)/shard_map/ppermute | solution.py:442
  95.2 14.1 %collective-permute-start.14 = (bf16[256,1024]{1,0:T(8,128)(2,1)}, bf16[256,1024]{1,0:T(8,128)(2,1)S(1)}, u32[]{:S(2)}, u32[]{:S(2)}) collective-permute-start(bf16[256,1024]{1,0:T(8,128)(2,1)} %get-tuple-element.238.refs_0_), channel_id=1, source_target_pairs={{0,1},{1,0},{2,3},{3,2},{4,5},{5,4},{6,7},{7,6},{8,9},{9,8},{10,11... | collective-permute-start | bytes 1572872 | tf_op jit(solution)/shard_map/ppermute | solution.py:473
  103.3 11.8 %collective-permute-start.10 = (bf16[256,512]{1,0:T(8,128)(2,1)}, bf16[256,512]{1,0:T(8,128)(2,1)S(1)}, u32[]{:S(2)}, u32[]{:S(2)}) collective-permute-start(bf16[256,512]{1,0:T(8,128)(2,1)} %get-tuple-element.229), channel_id=1, source_target_pairs={{0,8},{8,16},{16,24},{24,28},{28,20},{20,12},{12,4},{4,0},{1,9},{9... | collective-permute-start | bytes 786440 | tf_op jit(solution)/shard_map/ppermute | solution.py:650
  103.6 11.5 %collective-permute-start.11 = (bf16[256,512]{1,0:T(8,128)(2,1)}, bf16[256,512]{1,0:T(8,128)(2,1)S(1)}, u32[]{:S(2)}, u32[]{:S(2)}) collective-permute-start(bf16[256,512]{1,0:T(8,128)(2,1)} %get-tuple-element.230), channel_id=1, source_target_pairs={{0,4},{8,0},{16,8},{24,16},{28,24},{20,28},{12,20},{4,12},{1,5},{9... | collective-permute-start | bytes 786440 | tf_op jit(solution)/shard_map/ppermute | solution.py:650
  107.0 7.6 %collective-permute-start.12 = (bf16[256,256]{1,0:T(8,128)(2,1)}, bf16[256,256]{1,0:T(8,128)(2,1)S(1)}, u32[]{:S(2)}, u32[]{:S(2)}) collective-permute-start(bf16[256,256]{1,0:T(8,128)(2,1)} %get-tuple-element.233), channel_id=1, source_target_pairs={{0,8},{8,16},{16,24},{24,28},{28,20},{20,12},{12,4},{4,0},{1,9},{9... | collective-permute-start | bytes 393224 | tf_op jit(solution)/shard_map/ppermute | solution.py:577
  107.5 7.6 %collective-permute-start.13 = (bf16[256,256]{1,0:T(8,128)(2,1)}, bf16[256,256]{1,0:T(8,128)(2,1)S(1)}, u32[]{:S(2)}, u32[]{:S(2)}) collective-permute-start(bf16[256,256]{1,0:T(8,128)(2,1)} %get-tuple-element.234), channel_id=1, source_target_pairs={{0,4},{8,0},{16,8},{24,16},{28,24},{20,28},{12,20},{4,12},{1,5},{9... | collective-permute-start | bytes 393224 | tf_op jit(solution)/shard_map/ppermute | solution.py:577
  114.7 14.9 %copy-start.38 = (bf16[256,256]{1,0:T(8,128)(2,1)}, bf16[256,256]{1,0:T(8,128)(2,1)S(1)}, u32[]{:S(2)}) copy-start(bf16[256,256]{1,0:T(8,128)(2,1)S(1)} %collective-permute-done.12.refs_7_) | copy-start | bytes 393220
  120.4 3.3 %collective-permute-start.18 = (bf16[256,1024]{1,0:T(8,128)(2,1)S(1)}, bf16[256,1024]{1,0:T(8,128)(2,1)S(1)}, u32[]{:S(2)}, u32[]{:S(2)}) collective-permute-start(bf16[256,1024]{1,0:T(8,128)(2,1)S(1)} %copy-done.27), channel_id=1, source_target_pairs={{0,2},{2,0},{1,3},{3,1},{4,6},{6,4},{5,7},{7,5},{8,10},{10,8},{9,1... | collective-permute-start | bytes 1572872 | tf_op jit(solution)/shard_map/ppermute | solution.py:442
  121.1 13.0 %collective-permute-start.17 = (bf16[256,256]{1,0:T(8,128)(2,1)}, bf16[256,256]{1,0:T(8,128)(2,1)S(1)}, u32[]{:S(2)}, u32[]{:S(2)}) collective-permute-start(bf16[256,256]{1,0:T(8,128)(2,1)} %constant_dynamic-slice_fusion.2), channel_id=1, source_target_pairs={{0,2},{2,0},{1,3},{3,1},{4,6},{6,4},{5,7},{7,5},{8,10},{10,8},{9,1... | collective-permute-start | bytes 393224 | tf_op jit(solution)/shard_map/ppermute | solution.py:442
  121.6 14.8 %collective-permute-start.15 = (bf16[256,1024]{1,0:T(8,128)(2,1)}, bf16[256,1024]{1,0:T(8,128)(2,1)S(1)}, u32[]{:S(2)}, u32[]{:S(2)}) collective-permute-start(bf16[256,1024]{1,0:T(8,128)(2,1)} %get-tuple-element.250), channel_id=1, source_target_pairs={{0,8},{8,16},{16,24},{24,28},{28,20},{20,12},{12,4},{4,0},{1,9},{9... | collective-permute-start | bytes 1572872 | tf_op jit(solution)/shard_map/ppermute | solution.py:650
  123.4 14.6 %collective-permute-start.16 = (bf16[256,1024]{1,0:T(8,128)(2,1)}, bf16[256,1024]{1,0:T(8,128)(2,1)S(1)}, u32[]{:S(2)}, u32[]{:S(2)}) collective-permute-start(bf16[256,1024]{1,0:T(8,128)(2,1)} %get-tuple-element.251), channel_id=1, source_target_pairs={{0,4},{8,0},{16,8},{24,16},{28,24},{20,28},{12,20},{4,12},{1,5},{9... | collective-permute-start | bytes 1572872 | tf_op jit(solution)/shard_map/ppermute | solution.py:650
  123.7 21.2 %all-to-all-start.2 = ((bf16[8,64,256]{2,1,0:T(8,128)(2,1)}), bf16[8,64,256]{2,1,0:T(8,128)(2,1)S(1)}, u32[]{:S(2)}, u32[]{:S(2)}) async-start(bf16[8,64,256]{2,1,0:T(8,128)(2,1)} %bitcast.12), calls=%async_computation.2 | async-start | bytes 524288 | tf_op jit(solution)/shard_map/all_to_all | solution.py:446
  132.6 56.0 %collective-permute-start.24 = (bf16[2048,512]{1,0:T(8,128)(2,1)}, bf16[2048,512]{1,0:T(8,128)(2,1)}, u32[]{:S(2)}, u32[]{:S(2)}) collective-permute-start(bf16[2048,512]{1,0:T(8,128)(2,1)} %join.1.refs_0_), channel_id=1, source_target_pairs={{0,1},{1,0},{2,3},{3,2},{4,5},{5,4},{6,7},{7,6},{8,9},{9,8},{10,11... | collective-permute-start | bytes 6291464 | tf_op jit(solution)/shard_map/ppermute | solution.py:473
  142.9 18.7 %collective-permute-start.19 = (bf16[256,1024]{1,0:T(8,128)(2,1)}, bf16[256,1024]{1,0:T(8,128)(2,1)}, u32[]{:S(2)}, u32[]{:S(2)}) collective-permute-start(bf16[256,1024]{1,0:T(8,128)(2,1)} %get-tuple-element.260), channel_id=1, source_target_pairs={{0,8},{8,16},{16,24},{24,28},{28,20},{20,12},{12,4},{4,0},{1,9},{9... | collective-permute-start | bytes 1572872 | tf_op jit(solution)/shard_map/ppermute | solution.py:650
  144.6 17.0 %collective-permute-start.20 = (bf16[256,1024]{1,0:T(8,128)(2,1)}, bf16[256,1024]{1,0:T(8,128)(2,1)}, u32[]{:S(2)}, u32[]{:S(2)}) collective-permute-start(bf16[256,1024]{1,0:T(8,128)(2,1)} %get-tuple-element.261), channel_id=1, source_target_pairs={{0,4},{8,0},{16,8},{24,16},{28,24},{20,28},{12,20},{4,12},{1,5},{9... | collective-permute-start | bytes 1572872 | tf_op jit(solution)/shard_map/ppermute | solution.py:650
  144.9 36.9 %all-to-all-start.3 = ((bf16[8,32,1024]{2,1,0:T(8,128)(2,1)}), bf16[8,32,1024]{2,1,0:T(8,128)(2,1)}, u32[]{:S(2)}, u32[]{:S(2)}) async-start(bf16[8,32,1024]{2,1,0:T(8,128)(2,1)} %bitcast.11), calls=%async_computation.3 | async-start | bytes 1048576 | tf_op jit(solution)/shard_map/all_to_all | solution.py:446
  161.5 6.1 %collective-permute-start.23 = (bf16[8,128,256]{2,1,0:T(8,128)(2,1)S(1)}, bf16[8,128,256]{2,1,0:T(8,128)(2,1)S(1)}, u32[]{:S(2)}, u32[]{:S(2)}) collective-permute-start(bf16[8,128,256]{2,1,0:T(8,128)(2,1)S(1)} %get-tuple-element.276), channel_id=1, source_target_pairs={{0,2},{2,0},{1,3},{3,1},{4,6},{6,4},{5,7},{7,5},{8,10},{10,8},{9,1... | collective-permute-start | bytes 1572872 | tf_op jit(solution)/shard_map/ppermute | solution.py:442
  165.4 15.1 %collective-permute-start.21 = (bf16[256,1024]{1,0:T(8,128)(2,1)}, bf16[256,1024]{1,0:T(8,128)(2,1)}, u32[]{:S(2)}, u32[]{:S(2)}) collective-permute-start(bf16[256,1024]{1,0:T(8,128)(2,1)} %get-tuple-element.272), channel_id=1, source_target_pairs={{0,8},{8,16},{16,24},{24,28},{28,20},{20,12},{12,4},{4,0},{1,9},{9... | collective-permute-start | bytes 1572872 | tf_op jit(solution)/shard_map/ppermute | solution.py:650
  167.6 14.2 %collective-permute-start.22 = (bf16[256,1024]{1,0:T(8,128)(2,1)}, bf16[256,1024]{1,0:T(8,128)(2,1)}, u32[]{:S(2)}, u32[]{:S(2)}) collective-permute-start(bf16[256,1024]{1,0:T(8,128)(2,1)} %get-tuple-element.273), channel_id=1, source_target_pairs={{0,4},{8,0},{16,8},{24,16},{28,24},{20,28},{12,20},{4,12},{1,5},{9... | collective-permute-start | bytes 1572872 | tf_op jit(solution)/shard_map/ppermute | solution.py:650
  181.8 24.8 %all-to-all-start.4 = ((bf16[8,192,256]{2,1,0:T(8,128)(2,1)}), bf16[8,192,256]{2,1,0:T(8,128)(2,1)S(1)}, u32[]{:S(2)}, u32[]{:S(2)}) async-start(bf16[8,192,256]{2,1,0:T(8,128)(2,1)} %attention_backward.3.grads_ref), calls=%async_computation.4 | async-start | bytes 1572864 | tf_op jit(solution)/shard_map/all_to_all | solution.py:446
  195.5 1.4 collective-permute-start.25
  201.5 13.6 %collective-permute-start.28 = (bf16[400,1024]{1,0:T(8,128)(2,1)}, bf16[400,1024]{1,0:T(8,128)(2,1)}, u32[]{:S(2)}, u32[]{:S(2)}) collective-permute-start(bf16[400,1024]{1,0:T(8,128)(2,1)} %ring_finish.1.refs_0_), channel_id=1, source_target_pairs={{0,2},{2,0},{1,3},{3,1},{4,6},{6,4},{5,7},{7,5},{8,10},{10,8},{9,1... | collective-permute-start | bytes 2457608 | tf_op jit(solution)/shard_map/ppermute | solution.py:442
  201.7 21.1 %collective-permute-start.26 = (bf16[400,1024]{1,0:T(8,128)(2,1)}, bf16[400,1024]{1,0:T(8,128)(2,1)}, u32[]{:S(2)}, u32[]{:S(2)}) collective-permute-start(bf16[400,1024]{1,0:T(8,128)(2,1)} %ring_finish.1.refs_0_), channel_id=1, source_target_pairs={{0,8},{8,16},{16,24},{24,28},{28,20},{20,12},{12,4},{4,0},{1,9},{9... | collective-permute-start | bytes 2457608 | tf_op jit(solution)/shard_map/ppermute | solution.py:577
  203.8 20.6 %collective-permute-start.27 = (bf16[400,1024]{1,0:T(8,128)(2,1)}, bf16[400,1024]{1,0:T(8,128)(2,1)}, u32[]{:S(2)}, u32[]{:S(2)}) collective-permute-start(bf16[400,1024]{1,0:T(8,128)(2,1)} %ring_finish.1.refs_0_), channel_id=1, source_target_pairs={{0,4},{8,0},{16,8},{24,16},{28,24},{20,28},{12,20},{4,12},{1,5},{9... | collective-permute-start | bytes 2457608 | tf_op jit(solution)/shard_map/ppermute | solution.py:577
  210.1 3.8 %collective-permute-start.29 = (f32[24,128]{1,0:T(8,128)S(1)}, f32[24,128]{1,0:T(8,128)S(1)}, u32[]{:S(2)}, u32[]{:S(2)}) collective-permute-start(f32[24,128]{1,0:T(8,128)S(1)} %reshape.125), channel_id=1, source_target_pairs={{0,1},{1,0},{2,3},{3,2},{4,5},{5,4},{6,7},{7,6},{8,9},{9,8},{10,11... | collective-permute-start | bytes 36872 | tf_op jit(solution)/shard_map/ppermute | solution.py:473
  213.9 1.2 collective-permute-start.30
  224.3 28.8 %copy-start.10 = (f32[256,1024]{1,0:T(8,128)S(1)}, f32[256,1024]{1,0:T(8,128)}, u32[]{:S(2)}) copy-start(f32[256,1024]{1,0:T(8,128)} %get-tuple-element.235.hidden_ref) | copy-start | bytes 3145732
  224.3 28.8 %copy-start.42 = (f32[1024]{0:T(1024)S(1)}, f32[1024]{0:T(1024)}, u32[]{:S(2)}) copy-start(f32[1024]{0:T(1024)} %param.35) | copy-start | bytes 12292
  224.3 4.1 %collective-permute-start.33 = (bf16[400,1024]{1,0:T(8,128)(2,1)}, bf16[400,1024]{1,0:T(8,128)(2,1)S(1)}, u32[]{:S(2)}, u32[]{:S(2)}) collective-permute-start(bf16[400,1024]{1,0:T(8,128)(2,1)} %collective-permute-done.26.refs_7_), channel_id=1, source_target_pairs={{0,2},{2,0},{1,3},{3,1},{4,6},{6,4},{5,7},{7,5},{8,10},{10,8},{9,1... | collective-permute-start | bytes 2457608 | tf_op jit(solution)/shard_map/ppermute | solution.py:442
  224.3 6.4 %collective-permute-start.34 = (bf16[400,1024]{1,0:T(8,128)(2,1)}, bf16[400,1024]{1,0:T(8,128)(2,1)S(1)}, u32[]{:S(2)}, u32[]{:S(2)}) collective-permute-start(bf16[400,1024]{1,0:T(8,128)(2,1)} %collective-permute-done.27.refs_9_), channel_id=1, source_target_pairs={{0,2},{2,0},{1,3},{3,1},{4,6},{6,4},{5,7},{7,5},{8,10},{10,8},{9,1... | collective-permute-start | bytes 2457608 | tf_op jit(solution)/shard_map/ppermute | solution.py:442
  224.8 22.9 %collective-permute-start.31 = (bf16[400,1024]{1,0:T(8,128)(2,1)}, bf16[400,1024]{1,0:T(8,128)(2,1)}, u32[]{:S(2)}, u32[]{:S(2)}) collective-permute-start(bf16[400,1024]{1,0:T(8,128)(2,1)} %collective-permute-done.26.refs_7_), channel_id=1, source_target_pairs={{0,8},{8,16},{16,24},{24,28},{28,20},{20,12},{12,4},{4,0},{1,9},{9... | collective-permute-start | bytes 2457608 | tf_op jit(solution)/shard_map/ppermute | solution.py:577
  226.3 21.4 %collective-permute-start.32 = (bf16[400,1024]{1,0:T(8,128)(2,1)}, bf16[400,1024]{1,0:T(8,128)(2,1)}, u32[]{:S(2)}, u32[]{:S(2)}) collective-permute-start(bf16[400,1024]{1,0:T(8,128)(2,1)} %collective-permute-done.27.refs_9_), channel_id=1, source_target_pairs={{0,4},{8,0},{16,8},{24,16},{28,24},{20,28},{12,20},{4,12},{1,5},{9... | collective-permute-start | bytes 2457608 | tf_op jit(solution)/shard_map/ppermute | solution.py:577
  226.9 13.6 %collective-permute-start.36 = (bf16[256,1024]{1,0:T(8,128)(2,1)}, bf16[256,1024]{1,0:T(8,128)(2,1)}, u32[]{:S(2)}, u32[]{:S(2)}) collective-permute-start(bf16[256,1024]{1,0:T(8,128)(2,1)} %get-tuple-element.339), channel_id=1, source_target_pairs={{0,1},{1,0},{2,3},{3,2},{4,5},{5,4},{6,7},{7,6},{8,9},{9,8},{10,11... | collective-permute-start | bytes 1572872 | tf_op jit(solution)/shard_map/ppermute | solution.py:473
  228.4 19.3 %collective-permute-start.35 = (f32[24,128]{1,0:T(8,128)S(1)}, f32[24,128]{1,0:T(8,128)S(1)}, u32[]{:S(2)}, u32[]{:S(2)}) collective-permute-start(f32[24,128]{1,0:T(8,128)S(1)} %add.108), channel_id=1, source_target_pairs={{0,16},{4,20},{8,24},{12,28},{16,0},{20,4},{24,8},{28,12},{1,17},{... | collective-permute-start | bytes 36872 | tf_op jit(solution)/shard_map/ppermute | solution.py:1038
  247.7 4.1 %collective-permute-start.39 = (bf16[400,1024]{1,0:T(8,128)(2,1)}, bf16[400,1024]{1,0:T(8,128)(2,1)}, u32[]{:S(2)}, u32[]{:S(2)}) collective-permute-start(bf16[400,1024]{1,0:T(8,128)(2,1)} %collective-permute-done.31.refs_7_), channel_id=1, source_target_pairs={{0,2},{2,0},{1,3},{3,1},{4,6},{6,4},{5,7},{7,5},{8,10},{10,8},{9,1... | collective-permute-start | bytes 2457608 | tf_op jit(solution)/shard_map/ppermute | solution.py:442
  247.7 7.6 %collective-permute-start.40 = (bf16[400,1024]{1,0:T(8,128)(2,1)}, bf16[400,1024]{1,0:T(8,128)(2,1)}, u32[]{:S(2)}, u32[]{:S(2)}) collective-permute-start(bf16[400,1024]{1,0:T(8,128)(2,1)} %collective-permute-done.32.refs_9_), channel_id=1, source_target_pairs={{0,2},{2,0},{1,3},{3,1},{4,6},{6,4},{5,7},{7,5},{8,10},{10,8},{9,1... | collective-permute-start | bytes 2457608 | tf_op jit(solution)/shard_map/ppermute | solution.py:442
  248.2 21.8 %collective-permute-start.37 = (bf16[400,1024]{1,0:T(8,128)(2,1)}, bf16[400,1024]{1,0:T(8,128)(2,1)S(1)}, u32[]{:S(2)}, u32[]{:S(2)}) collective-permute-start(bf16[400,1024]{1,0:T(8,128)(2,1)} %collective-permute-done.31.refs_7_), channel_id=1, source_target_pairs={{0,8},{8,16},{16,24},{24,28},{28,20},{20,12},{12,4},{4,0},{1,9},{9... | collective-permute-start | bytes 2457608 | tf_op jit(solution)/shard_map/ppermute | solution.py:577
  249.6 20.4 %collective-permute-start.38 = (bf16[400,1024]{1,0:T(8,128)(2,1)}, bf16[400,1024]{1,0:T(8,128)(2,1)S(1)}, u32[]{:S(2)}, u32[]{:S(2)}) collective-permute-start(bf16[400,1024]{1,0:T(8,128)(2,1)} %collective-permute-done.32.refs_9_), channel_id=1, source_target_pairs={{0,4},{8,0},{16,8},{24,16},{28,24},{20,28},{12,20},{4,12},{1,5},{9... | collective-permute-start | bytes 2457608 | tf_op jit(solution)/shard_map/ppermute | solution.py:577
  250.3 13.7 %collective-permute-start.41 = (bf16[256,1024]{1,0:T(8,128)(2,1)}, bf16[256,1024]{1,0:T(8,128)(2,1)}, u32[]{:S(2)}, u32[]{:S(2)}) collective-permute-start(bf16[256,1024]{1,0:T(8,128)(2,1)} %get-tuple-element.370), channel_id=1, source_target_pairs={{0,1},{1,0},{2,3},{3,2},{4,5},{5,4},{6,7},{7,6},{8,9},{9,8},{10,11... | collective-permute-start | bytes 1572872 | tf_op jit(solution)/shard_map/ppermute | solution.py:473
  251.8 18.2 %collective-permute-start.42 = (f32[24,128]{1,0:T(8,128)S(1)}, f32[24,128]{1,0:T(8,128)S(1)}, u32[]{:S(2)}, u32[]{:S(2)}) collective-permute-start(f32[24,128]{1,0:T(8,128)S(1)} %add.113), channel_id=1, source_target_pairs={{0,8},{4,12},{8,0},{12,4},{16,24},{20,28},{24,16},{28,20},{1,9},{5... | collective-permute-start | bytes 36872 | tf_op jit(solution)/shard_map/ppermute | solution.py:1038
  255.4 20.1 %copy-start.17 = (bf16[256,1024]{1,0:T(8,128)(2,1)S(1)}, bf16[256,1024]{1,0:T(8,128)(2,1)}, u32[]{:S(2)}) copy-start(bf16[256,1024]{1,0:T(8,128)(2,1)} %get-tuple-element.370) | copy-start | bytes 1572868
  255.4 20.1 %copy-start.40 = (f32[1024]{0:T(1024)S(1)}, f32[1024]{0:T(1024)}, u32[]{:S(2)}) copy-start(f32[1024]{0:T(1024)} %param.22) | copy-start | bytes 12292
  270.0 9.3 %collective-permute-start.45 = (bf16[400,1024]{1,0:T(8,128)(2,1)S(1)}, bf16[400,1024]{1,0:T(8,128)(2,1)}, u32[]{:S(2)}, u32[]{:S(2)}) collective-permute-start(bf16[400,1024]{1,0:T(8,128)(2,1)S(1)} %collective-permute-done.37.left.refs_7_), channel_id=1, source_target_pairs={{0,2},{2,0},{1,3},{3,1},{4,6},{6,4},{5,7},{7,5},{8,10},{10,8},{9,1... | collective-permute-start | bytes 2457608 | tf_op jit(solution)/shard_map/ppermute | solution.py:442
  270.1 9.2 %collective-permute-start.46 = (bf16[400,1024]{1,0:T(8,128)(2,1)S(1)}, bf16[400,1024]{1,0:T(8,128)(2,1)}, u32[]{:S(2)}, u32[]{:S(2)}) collective-permute-start(bf16[400,1024]{1,0:T(8,128)(2,1)S(1)} %collective-permute-done.38.right.refs_9_), channel_id=1, source_target_pairs={{0,2},{2,0},{1,3},{3,1},{4,6},{6,4},{5,7},{7,5},{8,10},{10,8},{9,1... | collective-permute-start | bytes 2457608 | tf_op jit(solution)/shard_map/ppermute | solution.py:442
  273.2 12.9 %collective-permute-start.47 = (f32[24,128]{1,0:T(8,128)S(1)}, f32[24,128]{1,0:T(8,128)S(1)}, u32[]{:S(2)}, u32[]{:S(2)}) collective-permute-start(f32[24,128]{1,0:T(8,128)S(1)} %add.116), channel_id=1, source_target_pairs={{0,4},{4,0},{8,12},{12,8},{16,20},{20,16},{24,28},{28,24},{1,5},{5... | collective-permute-start | bytes 36872 | tf_op jit(solution)/shard_map/ppermute | solution.py:1038
  273.4 12.8 %collective-permute-start.43 = (bf16[400,512]{1,0:T(8,128)(2,1)}, bf16[400,512]{1,0:T(8,128)(2,1)S(1)}, u32[]{:S(2)}, u32[]{:S(2)}) collective-permute-start(bf16[400,512]{1,0:T(8,128)(2,1)} %get-tuple-element.353), channel_id=1, source_target_pairs={{0,8},{8,16},{16,24},{24,28},{28,20},{20,12},{12,4},{4,0},{1,9},{9... | collective-permute-start | bytes 1228808 | tf_op jit(solution)/shard_map/ppermute | solution.py:577
  274.2 12.0 %collective-permute-start.44 = (bf16[400,512]{1,0:T(8,128)(2,1)}, bf16[400,512]{1,0:T(8,128)(2,1)}, u32[]{:S(2)}, u32[]{:S(2)}) collective-permute-start(bf16[400,512]{1,0:T(8,128)(2,1)} %get-tuple-element.354), channel_id=1, source_target_pairs={{0,4},{8,0},{16,8},{24,16},{28,24},{20,28},{12,20},{4,12},{1,5},{9... | collective-permute-start | bytes 1228808 | tf_op jit(solution)/shard_map/ppermute | solution.py:577
  286.2 1.8 collective-permute-start.48
  286.3 2.5 collective-permute-start.49
  (33 other events, 141.9 us)
